TPU v7x, 32 devices: a whole 2x2x4 slice. The times are simulated.
32 devices in a mesh: seq: 8 (over y, x, core), dp: 4 (over z).
Axes of the slice: x: 2, y: 2, z: 4, core: 2. Of those that a mesh axis runs over, the one named last changes fastest.
Arguments:
- inputs: bfloat16 [4, 8, 512, 512], P('dp', 'seq'), may hold values from -6 to 6
- norm_gain: float32 [512], replicated, may hold values from 0.25 to 1.75
- qkv_weight: bfloat16 [512, 1536], replicated, may hold values from -2 to 2
- out_weight: bfloat16 [512, 512], replicated, may hold values from -0.25 to 0.25
- out_cotan: bfloat16 [4, 8, 512, 512], P('dp', 'seq'), may hold values from -6 to 6
Outputs:
- input_grad: bfloat16 [4, 8, 512, 512], P('dp', 'seq')
- qkv_weight_grad: float32 [512, 1536], P('seq')
- out_weight_grad: float32 [512, 512], P('seq')
- gain_grad: float32 [512], P('seq')
All inputs are finite; a program needn't handle non-finite values.
Results may differ from a plain program's by a relative error of at most 0.0091.
Values may be sent and summed in bfloat16 or wider, within the bound.
No kernel may reach another device: no remote copies, remote signals or barrier semaphores. Data moves between devices by JAX's collectives and lax.ppermute only.
A program may use at most 64 MiB of HBM per device.

v0:
```python
import math

import jax
import jax.numpy as jnp
from jax import lax
from jax.sharding import PartitionSpec as P

H = 8
HD = 64


def blocked(kernel, arrays, group_size):
    block_count = arrays[0].shape[0] // group_size
    split_arrays = tuple(
        (member.reshape((block_count, group_size) + member.shape[1:]) for member in arrays)
    )
    result = lax.map(lambda pieces: kernel(*pieces), split_arrays)
    return jax.tree.map(
        lambda member: member.reshape((block_count * group_size,) + member.shape[2:]), result
    )


def attend_probs(queries, key_vals):
    score_scale = HD ** (-0.5)
    scores = (
        jnp.einsum("glhd,gmhd->ghlm", queries, key_vals, preferred_element_type=jnp.float32)
        * score_scale
    )
    length = queries.shape[1]
    causal = lax.broadcasted_iota(jnp.int32, (length, length), 0) >= lax.broadcasted_iota(
        jnp.int32, (length, length), 1
    )
    scores = jnp.where(causal, scores, -1e30)
    row_max = jnp.max(scores, -1, keepdims=True)
    exponent = jnp.exp(scores - row_max)
    return exponent / jnp.sum(exponent, -1, keepdims=True)


def forward_block(queries, key_vals, values):
    weights = attend_probs(queries, key_vals).astype(jnp.bfloat16)
    return jnp.einsum(
        "ghlm,gmhd->glhd", weights, values, preferred_element_type=jnp.float32
    ).astype(jnp.bfloat16)


def backward_block(queries, key_vals, values, attended, cotangent):
    score_scale = HD ** (-0.5)
    softmax_probs = attend_probs(queries, key_vals)
    weights = softmax_probs.astype(jnp.bfloat16)
    prob_grad = jnp.einsum("glhd,gmhd->ghlm", cotangent, values, preferred_element_type=jnp.float32)
    row_delta = jnp.sum(cotangent.astype(jnp.float32) * attended.astype(jnp.float32), -1)
    row_delta = jnp.transpose(row_delta, (0, 2, 1))[..., None]
    score_grad = (softmax_probs * (prob_grad - row_delta)).astype(jnp.bfloat16)
    grad_query = (
        jnp.einsum("ghlm,gmhd->glhd", score_grad, key_vals, preferred_element_type=jnp.float32)
        * score_scale
    ).astype(jnp.bfloat16)
    grad_keys = (
        jnp.einsum("ghlm,glhd->gmhd", score_grad, queries, preferred_element_type=jnp.float32)
        * score_scale
    ).astype(jnp.bfloat16)
    grad_values = jnp.einsum(
        "ghlm,glhd->gmhd", weights, cotangent, preferred_element_type=jnp.float32
    ).astype(jnp.bfloat16)
    return (grad_query, grad_keys, grad_values)


def column_work(cols_in, cotangent, col_group):
    col_att = blocked(forward_block, cols_in, col_group)
    col_grads = blocked(backward_block, cols_in + (col_att, cotangent), col_group)
    return (col_att, col_grads)


def body(inputs, norm_gain, qkv_weight, out_weight, out_cotan):
    band_rows = inputs.shape[1]
    columns = inputs.shape[2]
    feature_width = inputs.shape[3]
    seq_count = lax.axis_size("seq")
    all_rows = band_rows * seq_count
    col_share = columns // seq_count
    half_heads = H // 2
    half_width = half_heads * HD
    tokens = band_rows * columns
    flat_input = inputs.reshape(tokens, feature_width).astype(jnp.float32)
    inverse_rms = lax.rsqrt(jnp.mean(flat_input * flat_input, -1, keepdims=True) + 1e-05)
    normed = flat_input * inverse_rms
    hidden = (normed * norm_gain).astype(jnp.bfloat16)
    weight_parts = qkv_weight.reshape(feature_width, 3, H, HD)
    weight_rows = weight_parts[:, :, :half_heads].reshape(feature_width, 3 * half_width)
    weight_cols = weight_parts[:, :, half_heads:].reshape(feature_width, 3 * half_width)
    row_proj = jnp.dot(hidden, weight_rows, preferred_element_type=jnp.float32).astype(jnp.bfloat16)
    row_grid = row_proj.reshape(band_rows, columns, 3, half_heads, HD)
    flat_cotan = out_cotan.reshape(tokens, feature_width)
    grad_att = jnp.dot(flat_cotan, out_weight.T, preferred_element_type=jnp.float32).astype(
        jnp.bfloat16
    )
    att_cot_grid = grad_att.reshape(band_rows, columns, H, HD)
    col_cot = att_cot_grid[:, :, half_heads:].reshape(band_rows, columns, half_width)
    col_group = math.gcd(col_share, max(1, 512 // all_rows))
    outgoing = jnp.concatenate([hidden.reshape(band_rows, columns, feature_width), col_cot], -1)
    received = jnp.swapaxes(
        lax.all_to_all(outgoing, "seq", split_axis=1, concat_axis=0, tiled=True), 0, 1
    )
    hidden_cols = received[:, :, :feature_width].reshape(col_share * all_rows, feature_width)
    col_proj = jnp.dot(hidden_cols, weight_cols, preferred_element_type=jnp.float32).astype(
        jnp.bfloat16
    )
    col_grid = col_proj.reshape(col_share, all_rows, 3, half_heads, HD)
    cot_grid = received[:, :, feature_width:].reshape(col_share, all_rows, half_heads, HD)
    cols_in = (col_grid[:, :, 0], col_grid[:, :, 1], col_grid[:, :, 2])
    col_att, col_grads = column_work(cols_in, cot_grid, col_group)
    joined = jnp.stack((col_att,) + tuple(col_grads), 2)
    joined = jnp.swapaxes(joined, 0, 1).reshape(all_rows, col_share, 4 * half_width)
    returned = lax.all_to_all(joined, "seq", split_axis=0, concat_axis=1, tiled=True)
    col_out = returned[:, :, :half_width]
    col_dqkv = returned[:, :, half_width:]
    row_group = math.gcd(band_rows, max(1, 512 // columns))
    rows_in = (row_grid[:, :, 0], row_grid[:, :, 1], row_grid[:, :, 2])
    row_att = blocked(forward_block, rows_in, row_group)
    row_grads = blocked(
        backward_block, rows_in + (row_att, att_cot_grid[:, :, :half_heads]), row_group
    )
    attended = jnp.concatenate(
        [row_att, col_out.reshape(band_rows, columns, half_heads, HD)], 2
    ).reshape(tokens, feature_width)
    row_dqkv = jnp.stack(row_grads, 2)
    grad_qkv = jnp.concatenate(
        [row_dqkv, col_dqkv.reshape(band_rows, columns, 3, half_heads, HD)], 3
    ).reshape(tokens, 3 * feature_width)
    term_out = jnp.dot(attended.T, flat_cotan, preferred_element_type=jnp.float32)
    term_qkv = jnp.dot(hidden.T, grad_qkv, preferred_element_type=jnp.float32)
    grad_hidden = jnp.dot(grad_qkv, qkv_weight.T, preferred_element_type=jnp.float32)
    term_gain = jnp.sum(grad_hidden * normed, 0)
    grad_normed = grad_hidden * norm_gain
    grad_input = inverse_rms * (
        grad_normed - normed * jnp.mean(grad_normed * normed, -1, keepdims=True)
    )
    input_grad = (
        (flat_cotan.astype(jnp.float32) + grad_input).astype(jnp.bfloat16).reshape(inputs.shape)
    )
    full_qkv, full_out, full_gain = lax.psum((term_qkv, term_out, term_gain), ("seq", "dp"))
    row_share = feature_width // seq_count
    first_row = lax.axis_index("seq") * row_share
    sum_qkv = lax.dynamic_slice_in_dim(full_qkv, first_row, row_share, 0)
    sum_out = lax.dynamic_slice_in_dim(full_out, first_row, row_share, 0)
    sum_gain = lax.dynamic_slice_in_dim(full_gain, first_row, row_share, 0)
    return (input_grad, sum_qkv, sum_out, sum_gain)


def solution(mesh):
    return jax.shard_map(
        body,
        mesh=mesh,
        in_specs=(P("dp", "seq", None, None), P(), P(), P(), P("dp", "seq", None, None)),
        out_specs=(P("dp", "seq", None, None), P("seq", None), P("seq", None), P("seq")),
        check_vma=False,
    )
```

profile of v0, /device:TPU:0, one launch (start us, length us, event | category | flops | bytes accessed | tf_op | source)
XLA Modules:
  0.0 241.7 jit_solution(10994994406863088898)
XLA Ops:
  7.2 1.3 fusion.34
  8.5 1.5 convolution_convert_fusion.4
  10.5 1.2 copy.132
  11.7 0.5 broadcast.143
  12.2 6.3 %reduce.5 = bf16[512,768]{1,0:T(8,128)(2,1)} reduce(bf16[512,1,768]{2,1,0:T(2,128)(2,1)S(1)} %bitcast.187, bf16[]{:T(256)} %broadcast.143), dimensions={1}, to_apply=%bitcast.186.reduce_sub_computation | reduce | bytes 1572866
  18.5 3.0 %reshape.280 = bf16[8,2,24576]{2,1,0:T(2,128)(2,1)} reshape(bf16[512,768]{1,0:T(8,128)(2,1)} %reduce.5) | data formatting | bytes 1572864
  21.5 5.2 %all-to-all-start = ((bf16[8,2,24576]{2,1,0:T(2,128)(2,1)}), bf16[8,2,24576]{2,1,0:T(2,128)(2,1)}, u32[]{:S(2)}, u32[]{:S(2)}) async-start(bf16[8,2,24576]{2,1,0:T(2,128)(2,1)} %reshape.280), calls=%async_computation | async-start | bytes 1572864 | tf_op jit(solution)/shard_map/all_to_all | solution.py:102
  26.7 1.7 copy.66
  28.5 1.0 fusion.64
  29.5 0.6 convolution_convert_fusion.1
  30.4 3.6 %fusion.67 = (f32[4,512]{1,0:T(4,128)S(1)}, f32[4,512,512]{1,2,0:T(8,128)}) fusion(pred[512,512]{0,1:T(8,128)(4,1)S(1)} %iota_compare_fusion, bf16[1,512,3,4,64]{1,4,3,2,0:T(8,128)(2,1)S(1)} %bitcast.198), kind=kOutput, calls=%fused_computation.101 | convolution fusion | flops 138412544 | bytes 4988928 | tf_op jit(solution)/shard_map/while/body/eval_jaxpr/sub | solution.py:35
  34.0 2.8 %fusion.6 = bf16[4,512,512]{1,2,0:T(8,128)(2,1)S(1)} fusion(f32[4,512,512]{1,2,0:T(8,128)} %get-tuple-element.84, f32[4,512]{1,0:T(4,128)S(1)} %get-tuple-element.83), kind=kLoop, calls=%fused_computation.11 | loop fusion | flops 2097152 | bytes 6299648 | tf_op jit(solution)/shard_map/while/body/eval_jaxpr/convert_element_type | solution.py:40
  36.8 1.5 fusion.27
  38.3 1.2 multiply_reduce_fusion.1
  39.5 4.1 %reshape.281 = bf16[512,1,768]{2,1,0:T(2,128)(2,1)S(1)} reshape(bf16[8,2,24576]{2,1,0:T(2,128)(2,1)} %all-to-all-done) | data formatting | bytes 1572864
  43.8 1.0 reshape.279
  44.8 1.6 convolution_convert_fusion
  46.5 2.8 %reshape.270 = bf16[64,8,3,4,64]{4,3,2,1,0:T(4,128)(2,1)S(1)} reshape(bf16[512,768]{1,0:T(8,128)(2,1)} %convolution_convert_fusion) | data formatting | bytes 1572864 | tf_op jit(solution)/shard_map/reshape | solution.py:108
  49.2 1.5 fusion.65
  50.8 2.0 fusion.66
  52.8 0.5 fusion.21
  53.3 0.5 copy-done.14
  53.8 0.8 multiply_reduce_fusion
  54.6 0.6 fusion.16
  55.2 0.5 copy-done.8
  55.7 0.4 fusion.19
  56.1 0.5 fusion.20
  56.6 0.5 maximum_bitcast_fusion
  57.2 0.8 copy.86
  58.0 2.5 %reshape.271 = bf16[8,64,1024]{2,1,0:T(8,128)(2,1)} reshape(bf16[8,64,4,4,64]{4,3,2,1,0:T(4,128)(2,1)S(1)} %copy.86) | data formatting | bytes 2097152 | tf_op jit(solution)/shard_map/reshape | solution.py:113
  60.5 4.5 %all-to-all-start.1 = ((bf16[8,64,1024]{2,1,0:T(8,128)(2,1)}), bf16[8,64,1024]{2,1,0:T(8,128)(2,1)S(1)}, u32[]{:S(2)}, u32[]{:S(2)}) async-start(bf16[8,64,1024]{2,1,0:T(8,128)(2,1)} %reshape.271), calls=%async_computation.1 | async-start | bytes 2097152 | tf_op jit(solution)/shard_map/all_to_all | solution.py:114
  65.1 2.9 %multiply_convert_fusion = bf16[4,512,512]{1,2,0:T(8,128)(2,1)S(1)} fusion(f32[4,512]{1,0:T(4,128)S(1)} %bitcast.212, f32[4,512,512]{1,2,0:T(8,128)} %get-tuple-element.84, f32[4,512]{1,0:T(4,128)S(1)} %get-tuple-element.83, bf16[1,512,3,4,64]{1,4,3,2,0:T(8,128)(2,1)S(1)} %bitcast.200, bf16[1,512,8,64]{1,3,2,0:T(8,128)(2,1)S(1)} %bitcast.197), kind=kOutput, calls=%fused_computation.2 | convolution fusion | flops 138412032 | bytes 6832128 | tf_op jit(solution)/shard_map/while/body/eval_jaxpr/glhd,gmhd->ghlm/dot_general | solution.py:50
  68.0 1.5 fusion.24
  69.5 1.2 fusion.25
  70.7 9.8 %all-to-all-done.1 = bf16[8,64,1024]{2,1,0:T(8,128)(2,1)S(1)} async-done(((bf16[8,64,1024]{2,1,0:T(8,128)(2,1)}), bf16[8,64,1024]{2,1,0:T(8,128)(2,1)S(1)}, u32[]{:S(2)}, u32[]{:S(2)}) %all-to-all-start.1) | async-done | bytes 1048608 | tf_op jit(solution)/shard_map/all_to_all | solution.py:114
  80.4 0.7 slice.69
  81.2 1.2 copy.87
  82.4 1.1 copy.88
  83.5 1.1 pad_maximum_fusion.2
  84.6 1.4 fusion.43
  86.3 2.9 %fusion.57 = f32[512,1536]{1,0:T(8,128)} fusion(bf16[512,1536]{0,1:T(8,128)(2,1)S(1)} %bitcast.190, bf16[1,1,512,512]{3,2,1,0:T(8,128)(2,1)S(1)} %copy-done.1, f32[512]{0:T(512)S(1)} %copy-done.15, f32[512]{0:T(512)S(1)} %add_rsqrt_fusion), kind=kOutput, calls=%fused_computation.90 | convolution fusion | flops 806354944 | bytes 5246976 | tf_op jit(solution)/shard_map/dot_general | solution.py:131
  89.2 3.6 %fusion.33 = (f32[512]{0:T(512)S(1)}, f32[512]{0:T(512)S(1)}, f32[512,512]{1,0:T(8,128)}) fusion(bf16[1,1,512,512]{3,2,1,0:T(8,128)(2,1)S(1)} %copy-done.1, f32[512]{0:T(512)S(1)} %add_rsqrt_fusion, f32[512]{0:T(512)S(1)} %copy-done.15, bf16[512,1536]{0,1:T(8,128)(2,1)S(1)} %bitcast.191, bf16[512,1536]{1,0:T(8,128)(2,1)} %param.7), kind=kOutput, calls=%fused_computation.55 | convolution fusion | flops 807140352 | bytes 4726784 | tf_op jit(solution)/shard_map/dot_general | solution.py:132
  92.8 40.0 %psum.23 = f32[512]{0:T(512)S(1)} all-reduce(f32[512]{0:T(512)S(1)} %get-tuple-element.60), channel_id=1, replica_groups=mesh['seq'=8,'dp'=4] {'seq','dp'}, use_global_device_ids=true, to_apply=%region_11.12 | all-reduce | flops 512 | bytes 4096 | tf_op jit(solution)/shard_map/psum | solution.py:141
  132.9 0.6 dynamic_slice.45
  133.5 2.4 fusion.41
  135.8 95.7 %all-reduce.3.cloned.1.call-done = (f32[512,1536]{1,0:T(8,128)}, f32[512,512]{1,0:T(8,128)}) async-done(((f32[512,1536]{1,0:T(8,128)}, f32[512,512]{1,0:T(8,128)}), (f32[512,1536]{1,0:T(8,128)}, f32[512,512]{1,0:T(8,128)})) %all-reduce.3.cloned.1.call-update) | async-done | bytes 4194320 | tf_op jit(solution)/shard_map/psum | solution.py:141
  231.6 1.8 constant_dynamic-slice_fusion.1
  233.3 1.6 constant_dynamic-slice_fusion
  (47 shorter events, 1.3 us)
Async XLA Ops:
  7.2 1.4 copy-start
  7.2 3.0 %copy-start.1 = (bf16[1,1,512,512]{3,2,1,0:T(8,128)(2,1)S(1)}, bf16[1,1,512,512]{3,2,1,0:T(8,128)(2,1)}, u32[]{:S(2)}) copy-start(bf16[1,1,512,512]{3,2,1,0:T(8,128)(2,1)} %param.5) | copy-start | bytes 1572868
  7.2 3.0 %copy-start.15 = (f32[512]{0:T(512)S(1)}, f32[512]{0:T(512)}, u32[]{:S(2)}) copy-start(f32[512]{0:T(512)} %param.6) | copy-start | bytes 6148
  10.0 28.3 %copy-start.3 = (bf16[512,512]{0,1:T(8,128)(2,1)}, bf16[512,512]{0,1:T(8,128)(2,1)S(1)}, u32[]{:S(2)}) copy-start(bf16[512,512]{0,1:T(8,128)(2,1)S(1)} %convolution_convert_fusion.4) | copy-start | bytes 1572868
  21.5 18.0 %all-to-all-start = ((bf16[8,2,24576]{2,1,0:T(2,128)(2,1)}), bf16[8,2,24576]{2,1,0:T(2,128)(2,1)}, u32[]{:S(2)}, u32[]{:S(2)}) async-start(bf16[8,2,24576]{2,1,0:T(2,128)(2,1)} %reshape.280), calls=%async_computation | async-start | bytes 1572864 | tf_op jit(solution)/shard_map/all_to_all | solution.py:102
  30.4 7.9 %copy-start.5 = (bf16[512,768]{0,1:T(8,128)(2,1)}, bf16[512,768]{0,1:T(8,128)(2,1)S(1)}, u32[]{:S(2)}) copy-start(bf16[512,768]{0,1:T(8,128)(2,1)S(1)} %copy.67) | copy-start | bytes 2359300
  43.6 1.2 copy-start.12
  50.8 2.0 copy-start.13
  52.8 1.0 copy-start.14
  54.6 1.0 copy-start.8
  60.5 4.5 %copy-start.4 = (bf16[512,512]{0,1:T(8,128)(2,1)S(1)}, bf16[512,512]{0,1:T(8,128)(2,1)}, u32[]{:S(2)}) copy-start(bf16[512,512]{0,1:T(8,128)(2,1)} %copy-done.3) | copy-start | bytes 1572868
  60.5 4.5 %copy-start.6 = (bf16[512,768]{0,1:T(8,128)(2,1)S(1)}, bf16[512,768]{0,1:T(8,128)(2,1)}, u32[]{:S(2)}) copy-start(bf16[512,768]{0,1:T(8,128)(2,1)} %copy-done.5) | copy-start | bytes 2359300
  60.5 19.9 %all-to-all-start.1 = ((bf16[8,64,1024]{2,1,0:T(8,128)(2,1)}), bf16[8,64,1024]{2,1,0:T(8,128)(2,1)S(1)}, u32[]{:S(2)}, u32[]{:S(2)}) async-start(bf16[8,64,1024]{2,1,0:T(8,128)(2,1)} %reshape.271), calls=%async_computation.1 | async-start | bytes 2097152 | tf_op jit(solution)/shard_map/all_to_all | solution.py:114
  65.0 166.5 %all-reduce.3.cloned.1.call-start = ((), (), s32[]{:S(2)}) async-start(), calls=%async_computation.2 | async-start | bytes 8388608 | tf_op jit(solution)/shard_map/psum | solution.py:141
  81.1 3.5 %copy-start.2 = (bf16[1,1,512,512]{3,2,1,0:T(8,128)(2,1)S(1)}, bf16[1,1,512,512]{3,2,1,0:T(8,128)(2,1)}, u32[]{:S(2)}) copy-start(bf16[1,1,512,512]{3,2,1,0:T(8,128)(2,1)} %param.9) | copy-start | bytes 1572868
  82.4 3.7 %copy-start.9 = (bf16[1,512,1,4,64]{1,4,3,2,0:T(8,128)(2,1)S(1)}, bf16[1,512,1,4,64]{1,4,3,2,0:T(8,128)(2,1)}, u32[]{:S(2)}) copy-start(bf16[1,512,1,4,64]{1,4,3,2,0:T(8,128)(2,1)} %fusion.27) | copy-start | bytes 786436
  83.5 2.6 %copy-start.7 = (bf16[1,512,768]{1,2,0:T(8,128)(2,1)S(1)}, bf16[1,512,768]{1,2,0:T(8,128)(2,1)}, u32[]{:S(2)}) copy-start(bf16[1,512,768]{1,2,0:T(8,128)(2,1)} %copy.87) | copy-start | bytes 2359300
  83.5 2.6 %copy-start.10 = (bf16[1,512,1,4,64]{1,4,3,2,0:T(8,128)(2,1)S(1)}, bf16[1,512,1,4,64]{1,4,3,2,0:T(8,128)(2,1)}, u32[]{:S(2)}) copy-start(bf16[1,512,1,4,64]{1,4,3,2,0:T(8,128)(2,1)} %fusion.24) | copy-start | bytes 786436
  83.5 2.6 %copy-start.11 = (bf16[1,512,1,4,64]{1,4,3,2,0:T(8,128)(2,1)S(1)}, bf16[1,512,1,4,64]{1,4,3,2,0:T(8,128)(2,1)}, u32[]{:S(2)}) copy-start(bf16[1,512,1,4,64]{1,4,3,2,0:T(8,128)(2,1)} %fusion.25) | copy-start | bytes 786436
Sparse Core Ops, SparseCore 0:
  89.3 142.1 all-reduce.2
where the time goes:
time: 243 us; the launch traced here: 242 us
  waiting for transfers between devices  105 us (43%)
  blocking collectives  40 us (16%)
  local copies, waits for them, and re-layouts  28.8 us (12%)
  matrix products  28.4 us (12%)
  other arithmetic  14.9 us (6%)
  between operations  14.4 us (6%)
  starting transfers between devices  9.69 us (4%)
    psum x1, waiting for transfers between devices, body(): lax.psum((term_qkv, term_out, term_gain), ('seq', 'dp'))  95.7 us
    psum x1, blocking collectives, body(): lax.psum((term_qkv, term_out, term_gain), ('seq', 'dp'))  40 us
    unnamed x37, local copies, waits for them, and re-layouts  10.4 us
    all_to_all x1, waiting for transfers between devices, body(): lax.all_to_all(joined, 'seq', split_axis=0, concat_axis=1, tiled=True)  9.76 us
    unnamed x1, other arithmetic  6.3 us
    sub x2, matrix products, attend_probs(): exponent = jnp.exp(scores - row_max)  5.62 us
    all_to_all x1, starting transfers between devices, body(): lax.all_to_all(outgoing, 'seq', split_axis=1, concat_axis=0, tiled=True)  5.17 us
  transfers between devices with their start and end apart: 3, of which 2 were waited for; matrix products, arithmetic and copies ran while one was open for 10% of the time, Pallas kernels for 0%

commit v1 on v0

v1 whole, which is shorter than its diff:
```python
import functools
import math

import jax
import jax.numpy as jnp
from jax import lax
from jax.experimental import pallas as pl
from jax.experimental.pallas import tpu as pltpu
from jax.sharding import PartitionSpec as P

H = 8
HD = 64
HH = H // 2
HW = HH * HD
SCALE = HD ** (-0.5)
F32 = jnp.float32
BF16 = jnp.bfloat16
GAIN_LANES = 128
QUERY_BLOCK = 128
VMEM_BYTES = 40 * 1024 * 1024


def dot_nn(a, b):
    return lax.dot_general(a, b, (((1,), (0,)), ((), ())), preferred_element_type=F32)


def dot_nt(a, b):
    return lax.dot_general(a, b, (((1,), (1,)), ((), ())), preferred_element_type=F32)


def rms_parts(x):
    inverse_rms = lax.rsqrt(jnp.mean(x * x, -1, keepdims=True) + 1e-05)
    return inverse_rms, x * inverse_rms


def head_step(q, k, v, g, qt, kt, vt, gt, mask):
    scores = jnp.where(mask, dot_nn(q, kt), -1e30)
    exponent = jnp.exp(scores - jnp.max(scores, -1, keepdims=True))
    probs = exponent * (1.0 / jnp.sum(exponent, -1, keepdims=True))
    weights = probs.astype(BF16)
    attended = dot_nn(weights, v).astype(BF16)
    delta = jnp.sum(g.astype(F32) * attended.astype(F32), -1, keepdims=True)
    score_grad = (probs * (dot_nn(g, vt) - delta)).astype(BF16)
    grad_q = (dot_nn(score_grad, k) * SCALE).astype(BF16)
    return attended, grad_q, dot_nn(qt, score_grad), dot_nn(gt, weights)


def part_columns(width, second):
    return [slice(i * width + second * HW, i * width + (second + 1) * HW) for i in range(3)]


def project(hidden, cot, wqkv_ref, wout_ref, second):
    parts = part_columns(wqkv_ref.shape[0], second)
    q, k, v = [dot_nn(hidden, wqkv_ref[:, cols]).astype(BF16) for cols in parts]
    g = dot_nt(cot, wout_ref[second * HW : (second + 1) * HW, :]).astype(BF16)
    return q * jnp.asarray(SCALE, BF16), k, v, g


def weight_terms(hidden, normed, cot, attended, grads, wqkv_ref, second):
    hidden_t = hidden.T
    parts = part_columns(wqkv_ref.shape[0], second)
    term_qkv = [dot_nn(hidden_t, grad) for grad in grads]
    term_out = dot_nn(attended.T, cot)
    grad_hidden = dot_nt(grads[0], wqkv_ref[:, parts[0]])
    grad_hidden += dot_nt(grads[1], wqkv_ref[:, parts[1]])
    grad_hidden += dot_nt(grads[2], wqkv_ref[:, parts[2]])
    term_gain = jnp.sum(grad_hidden * normed, 0, keepdims=True)
    return term_qkv, term_out, grad_hidden, term_gain


def row_kernel(
    x_ref, cot_ref, gain_ref, wqkv_ref, wout_ref,
    qkv_ref, out_ref, hidden_ref, gain_term_ref,
    dkt_ref, dvt_ref,
):
    tokens = x_ref.shape[0]
    _, normed = rms_parts(x_ref[...].astype(F32))
    hidden = (normed * gain_ref[...]).astype(BF16)
    cot = cot_ref[...]
    q, k, v, g = project(hidden, cot, wqkv_ref, wout_ref, 0)
    qt, kt, vt, gt = q.T, k.T, v.T, g.T
    dkt_ref[...] = jnp.zeros_like(dkt_ref)
    dvt_ref[...] = jnp.zeros_like(dvt_ref)
    step = math.gcd(tokens, QUERY_BLOCK)
    att_blocks, dq_blocks = [], []
    for start in range(0, tokens, step):
        rows, keys = slice(start, start + step), slice(0, start + step)
        shape = (step, start + step)
        mask = (
            lax.broadcasted_iota(jnp.int32, shape, 0) + start
            >= lax.broadcasted_iota(jnp.int32, shape, 1)
        )
        atts, dqs = [], []
        for head in range(HH):
            lanes = slice(head * HD, (head + 1) * HD)
            attended, dq, dkt, dvt = head_step(
                q[rows, lanes], k[keys, lanes], v[keys, lanes], g[rows, lanes],
                qt[lanes, rows], kt[lanes, keys], vt[lanes, keys], gt[lanes, rows], mask,
            )
            dkt_ref[lanes, keys] += dkt
            dvt_ref[lanes, keys] += dvt
            atts.append(attended)
            dqs.append(dq)
        att_blocks.append(jnp.concatenate(atts, 1))
        dq_blocks.append(jnp.concatenate(dqs, 1))
    attended = jnp.concatenate(att_blocks, 0)
    grads = (
        jnp.concatenate(dq_blocks, 0),
        dkt_ref[...].astype(BF16).T,
        dvt_ref[...].astype(BF16).T,
    )
    term_qkv, term_out, grad_hidden, term_gain = weight_terms(
        hidden, normed, cot, attended, grads, wqkv_ref, 0
    )
    for i in range(3):
        qkv_ref[:, i * HW : (i + 1) * HW] = term_qkv[i].astype(BF16)
    out_ref[...] = term_out.astype(BF16)
    hidden_ref[...] = grad_hidden
    gain_term_ref[...] = term_gain


def column_kernel(
    moved_ref, gain_ref, wqkv_ref, wout_ref, row_out_ref, row_gain_ref,
    back_ref, terms_ref,
):
    all_rows, _, share, width = moved_ref.shape
    group = math.gcd(share, 16)
    block = all_rows * group
    starts = range(0, share, group)

    def gathered(which):
        pieces = []
        for start in starts:
            piece = moved_ref[:, which, start : start + group, :]
            pieces.append(piece.astype(F32).reshape(block, width))
        return jnp.concatenate(pieces, 0)

    _, normed = rms_parts(gathered(0))
    hidden = (normed * gain_ref[...]).astype(BF16)
    cot = gathered(1).astype(BF16)
    q, k, v, g = project(hidden, cot, wqkv_ref, wout_ref, 1)
    qt, kt, vt, gt = q.T, k.T, v.T, g.T
    query = lax.broadcasted_iota(jnp.int32, (block, block), 0)
    key = lax.broadcasted_iota(jnp.int32, (block, block), 1)
    mask = (query >= key) & (query % group == key % group)
    att_blocks, dq_blocks, dkt_blocks, dvt_blocks = [], [], [], []
    for start in range(0, all_rows * share, block):
        rows = slice(start, start + block)
        results = []
        for head in range(HH):
            lanes = slice(head * HD, (head + 1) * HD)
            results.append(
                head_step(
                    q[rows, lanes], k[rows, lanes], v[rows, lanes], g[rows, lanes],
                    qt[lanes, rows], kt[lanes, rows], vt[lanes, rows], gt[lanes, rows], mask,
                )
            )
        att_blocks.append(jnp.concatenate([r[0] for r in results], 1))
        dq_blocks.append(jnp.concatenate([r[1] for r in results], 1))
        dkt_blocks.append(jnp.concatenate([r[2] for r in results], 0))
        dvt_blocks.append(jnp.concatenate([r[3] for r in results], 0))
    attended = jnp.concatenate(att_blocks, 0)
    grads = (
        jnp.concatenate(dq_blocks, 0),
        jnp.concatenate(dkt_blocks, 1).astype(BF16).T,
        jnp.concatenate(dvt_blocks, 1).astype(BF16).T,
    )
    term_qkv, term_out, grad_hidden, term_gain = weight_terms(
        hidden, normed, cot, attended, grads, wqkv_ref, 1
    )
    for i, start in enumerate(starts):
        piece = grad_hidden[i * block : (i + 1) * block].reshape(all_rows, group, width)
        back_ref[:, start : start + group, :] = piece.astype(BF16)
    for i in range(3):
        terms_ref[:, i * HW : (i + 1) * HW] = term_qkv[i].astype(BF16)
    out_lanes = slice(3 * HW, 3 * HW + width)
    terms_ref[:HW, out_lanes] = row_out_ref[...]
    terms_ref[HW:, out_lanes] = term_out.astype(BF16)
    gain = jnp.broadcast_to(term_gain + row_gain_ref[...], (GAIN_LANES, width)).T
    terms_ref[:, 3 * HW + width :] = split_gain(gain)


def split_gain(gain):
    lane = lax.broadcasted_iota(jnp.int32, gain.shape, 1)
    rounded = gain.astype(BF16).astype(F32)
    return jnp.where(lane < GAIN_LANES // 2, rounded, gain - rounded).astype(BF16)


def joined_gain(pairs):
    return pairs[:, :1] + pairs[:, GAIN_LANES // 2 : GAIN_LANES // 2 + 1]


def input_kernel(x_ref, cot_ref, gain_ref, row_ref, col_ref, grad_ref):
    inverse_rms, normed = rms_parts(x_ref[...].astype(F32))
    grad_normed = (row_ref[...] + col_ref[...].astype(F32)) * gain_ref[...]
    projected = jnp.mean(grad_normed * normed, -1, keepdims=True)
    grad = inverse_rms * (grad_normed - normed * projected)
    grad_ref[...] = (cot_ref[...].astype(F32) + grad).astype(BF16)


def call(kernel, name, outs, scratch=(), flops=0, args=()):
    size = sum(math.prod(a.shape) * a.dtype.itemsize for a in (*args, *outs))
    return pl.pallas_call(
        kernel,
        out_shape=outs,
        in_specs=[pl.BlockSpec(memory_space=pltpu.VMEM)] * len(args),
        out_specs=[pl.BlockSpec(memory_space=pltpu.VMEM)] * len(outs),
        scratch_shapes=scratch,
        name=name,
        cost_estimate=pl.CostEstimate(flops=flops, bytes_accessed=size, transcendentals=0),
        compiler_params=pltpu.CompilerParams(vmem_limit_bytes=VMEM_BYTES),
    )(*args)


def body(inputs, norm_gain, qkv_weight, out_weight, out_cotan):
    columns, width = inputs.shape[2:]
    n = lax.axis_size("seq")
    m = lax.axis_size("dp")
    share = columns // n
    row_share = width // n
    x = inputs.reshape(columns, width)
    cot = out_cotan.reshape(columns, width)
    gain = norm_gain.reshape(1, width)

    outgoing = jnp.stack([x.reshape(n, share, width), cot.reshape(n, share, width)], 1)
    moved = lax.all_to_all(outgoing, "seq", split_axis=0, concat_axis=0, tiled=True)

    shaped = jax.ShapeDtypeStruct
    row_qkv, row_out, row_hidden, row_gain = call(
        row_kernel,
        "row_heads",
        [
            shaped((width, 3 * HW), BF16),
            shaped((HW, width), BF16),
            shaped((columns, width), F32),
            shaped((1, width), F32),
        ],
        [pltpu.VMEM((HW, columns), F32), pltpu.VMEM((HW, columns), F32)],
        6_000_000_000,
        (x, cot, gain, qkv_weight, out_weight),
    )
    row_terms = lax.all_to_all(
        row_qkv.reshape(n, row_share, 3 * HW), "seq", split_axis=0, concat_axis=0, tiled=True
    )
    term_width = 3 * HW + width + GAIN_LANES
    back, col_terms = call(
        column_kernel,
        "column_heads",
        [shaped((n, share, width), BF16), shaped((width, term_width), BF16)],
        (),
        4_000_000_000,
        (moved, gain, qkv_weight, out_weight, row_out, row_gain),
    )
    returned = lax.all_to_all(back, "seq", split_axis=0, concat_axis=0, tiled=True)
    col_terms = lax.all_to_all(
        col_terms.reshape(n, row_share, term_width), "seq", split_axis=0, concat_axis=0, tiled=True
    )
    (input_grad,) = call(
        input_kernel,
        "input_grad",
        [shaped((columns, width), BF16)],
        (),
        10_000_000,
        (x, cot, gain, row_hidden, returned.reshape(columns, width)),
    )

    row_sum = jnp.sum(row_terms.astype(F32), 0)
    col_sum = jnp.sum(col_terms.astype(F32), 0)

    def over_dp(total, has_gain):
        for distance in (1, 2):
            sent = total.astype(BF16)
            if has_gain:
                sent = jnp.concatenate(
                    [sent[:, :-GAIN_LANES], split_gain(jnp.broadcast_to(joined_gain(total[:, -GAIN_LANES:]), (row_share, GAIN_LANES)))], 1
                )
            got = lax.ppermute(sent, "dp", [(i, i ^ distance) for i in range(m)])
            total = sent.astype(F32) + got.astype(F32)
        return total

    row_sum = over_dp(row_sum, False)
    col_sum = over_dp(col_sum, True)
    sum_qkv = jnp.concatenate(
        [part for i in range(3) for part in (row_sum[:, i * HW : (i + 1) * HW], col_sum[:, i * HW : (i + 1) * HW])], 1
    )
    sum_out = col_sum[:, 3 * HW : 3 * HW + width]
    sum_gain = joined_gain(col_sum[:, -GAIN_LANES:]).reshape(row_share)
    return (input_grad.reshape(inputs.shape), sum_qkv, sum_out, sum_gain)


def solution(mesh):
    return jax.shard_map(
        body,
        mesh=mesh,
        in_specs=(P("dp", "seq", None, None), P(), P(), P(), P("dp", "seq", None, None)),
        out_specs=(P("dp", "seq", None, None), P("seq", None), P("seq", None), P("seq")),
        check_vma=False,
    )
```

time: 243 us -> 88.7 us (0.37)
  waiting for transfers between devices: 105 us -> 21 us
  blocking collectives: 40 us -> 0 us
  matrix products: 28.4 us -> 0 us
  Pallas kernels: 0 us -> 27.8 us
  local copies, waits for them, and re-layouts: 28.8 us -> 5.93 us
  starting transfers between devices: 9.69 us -> 26.1 us
  between operations: 14.4 us -> 0.86 us
  other arithmetic: 14.9 us -> 6.48 us
    psum x1 -> x0, waiting for transfers between devices: 95.7 us -> none  [body(): lax.psum((term_qkv, term_out, term_gain), ('seq', 'dp'))]
    psum x1 -> x0, blocking collectives: 40 us -> none  [body(): lax.psum((term_qkv, term_out, term_gain), ('seq', 'dp'))]
    pallas_call x0 -> x3, Pallas kernels: none -> 27.8 us  [call(): pl.pallas_call(kernel, out_shape=outs, in_specs=[pl.BlockSpec(memory_spac...]
    dot_general x16 -> x0, matrix products: 22.8 us -> none  [the longest x1 3.62 us: body(): jnp.dot(grad_qkv, qkv_weight.T, preferred_element_type=jnp.float32)]
    ppermute x0 -> x4, starting transfers between devices: none -> 8.6 us  [over_dp(): got = lax.ppermute(sent, 'dp', [(i, i ^ distance) for i in range(m)])]
    all_to_all x2 -> x4, starting transfers between devices: 9.66 us -> 17.5 us  [the longest x1 5.31 us: body(): lax.all_to_all(outgoing, 'seq', split_axis=0, concat_axis=0, tiled=True)]
    all_to_all x2 -> x4, waiting for transfers between devices: 9.76 us -> 16.2 us  [the longest x1 10.5 us: body(): lax.all_to_all(col_terms.reshape(n, row_share, term_width), 'seq', split_...]
    unnamed x1 -> x0, other arithmetic: 6.3 us -> none
  transfers between devices with their start and end apart: 3 -> 8, of which waited for: 2 -> 5; matrix products, arithmetic and copies ran while one was open for 10% -> 5% of each run, Pallas kernels for 0% -> 32%
where the time goes in v1:
time: 88.7 us; the launch traced here: 88.2 us
  Pallas kernels  27.8 us (31%)
  starting transfers between devices  26.1 us (29%)
  waiting for transfers between devices  21 us (24%)
  other arithmetic  6.48 us (7%)
  local copies, waits for them, and re-layouts  5.93 us (7%)
    pallas_call x3, Pallas kernels, call(): pl.pallas_call(kernel, out_shape=outs, in_specs=[pl.BlockSpec(memory_spac...  27.8 us
    all_to_all x1, waiting for transfers between devices, body(): lax.all_to_all(col_terms.reshape(n, row_share, term_width), 'seq', split_...  10.5 us
    ppermute x4, starting transfers between devices, over_dp(): got = lax.ppermute(sent, 'dp', [(i, i ^ distance) for i in range(m)])  8.6 us
    all_to_all x1, waiting for transfers between devices, body(): lax.all_to_all(back, 'seq', split_axis=0, concat_axis=0, tiled=True)  5.63 us
    all_to_all x1, starting transfers between devices, body(): lax.all_to_all(outgoing, 'seq', split_axis=0, concat_axis=0, tiled=True)  5.31 us
    unnamed x25, local copies, waits for them, and re-layouts  5.21 us
    ppermute x4, waiting for transfers between devices, over_dp(): got = lax.ppermute(sent, 'dp', [(i, i ^ distance) for i in range(m)])  4.84 us
    all_to_all x1, starting transfers between devices, body(): lax.all_to_all(row_qkv.reshape(n, row_share, 3 * HW), 'seq', split_axis=0...  4.4 us
  transfers between devices with their start and end apart: 8, of which 5 were waited for; matrix products, arithmetic and copies ran while one was open for 5% of the time, Pallas kernels for 32%

profile of v1, /device:TPU:0, one launch (start us, length us, event | category | flops | bytes accessed | tf_op | source)
XLA Modules:
  0.0 88.2 jit_solution(16039010843859921766)
XLA Ops:
  0.6 2.3 %pad_maximum_fusion = bf16[8,2,64,512]{3,2,1,0:T(8,128)(2,1)} fusion(bf16[8,1,64,512]{3,2,1,0:T(8,128)(2,1)} %bitcast.13, bf16[8,1,64,512]{3,2,1,0:T(8,128)(2,1)} %bitcast.10), kind=kLoop, calls=%fused_computation.1 | loop fusion | flops 524288 | bytes 2097152 | tf_op jit(solution)/shard_map/stack | solution.py:225
  2.9 0.0 copy-start.1
  2.9 0.0 copy-start.4
  2.9 0.0 copy-start.7
  2.9 5.3 %all-to-all-start = ((bf16[8,2,64,512]{3,2,1,0:T(8,128)(2,1)}), bf16[8,2,64,512]{3,2,1,0:T(8,128)(2,1)S(1)}, u32[]{:S(2)}, u32[]{:S(2)}) async-start(bf16[8,2,64,512]{3,2,1,0:T(8,128)(2,1)} %pad_maximum_fusion), calls=%async_computation | async-start | bytes 2097152 | tf_op jit(solution)/shard_map/all_to_all | solution.py:226
  8.2 0.0 copy-done
  8.2 0.0 copy-done.1
  8.2 0.0 copy-done.4
  8.2 0.0 copy-done.7
  8.3 0.0 copy-start.5
  8.3 1.4 %copy-done.5 = bf16[512,1536]{1,0:T(8,128)(2,1)S(1)} copy-done((bf16[512,1536]{1,0:T(8,128)(2,1)S(1)}, bf16[512,1536]{1,0:T(8,128)(2,1)}, u32[]{:S(2)}) %copy-start.5) | copy-done | bytes 1572888
  9.7 13.3 %row_heads.1 = (bf16[512,768]{1,0:T(8,128)(2,1)}, bf16[256,512]{1,0:T(8,128)(2,1)S(1)}, f32[512,512]{1,0:T(8,128)S(1)}, f32[1,512]{1,0:T(1,128)S(1)}) custom-call(bf16[512,512]{1,0:T(8,128)(2,1)S(1)} %bitcast.11, bf16[512,512]{1,0:T(8,128)(2,1)S(1)} %bitcast.14, f32[1,512]{1,0:T(1,128)S(1)} %bitcast.16, bf16[512,1536]{1,0:T(8,128)(2,1)S(1)} %copy-done.5, ...), custom_call_target="tpu_custom_call" | custom-call | flops 6000000000 | bytes 5246976 | tf_op jit(solution)/shard_map/row_heads/pallas_call | solution.py:203
  23.0 0.0 copy-start.2
  23.0 1.0 %copy-done.2 = f32[512,512]{1,0:T(8,128)} copy-done((f32[512,512]{1,0:T(8,128)}, f32[512,512]{1,0:T(8,128)S(1)}, u32[]{:S(2)}) %copy-start.2) | copy-done | bytes 1048600
  24.0 0.0 all-to-all-done.moved_ref
  24.0 4.4 %all-to-all-start.2 = ((bf16[8,64,768]{2,1,0:T(8,128)(2,1)}), bf16[8,64,768]{2,1,0:T(8,128)(2,1)}, u32[]{:S(2)}, u32[]{:S(2)}) async-start(bf16[8,64,768]{2,1,0:T(8,128)(2,1)} %bitcast.7), calls=%async_computation.2 | async-start | bytes 1572864 | tf_op jit(solution)/shard_map/all_to_all | solution.py:242
  28.4 0.0 copy-start.6
  28.4 1.4 %copy-done.6 = bf16[512,1536]{1,0:T(8,128)(2,1)S(1)} copy-done((bf16[512,1536]{1,0:T(8,128)(2,1)S(1)}, bf16[512,1536]{1,0:T(8,128)(2,1)}, u32[]{:S(2)}) %copy-start.6) | copy-done | bytes 1572888
  29.8 13.2 %column_heads.1 = (bf16[8,64,512]{2,1,0:T(8,128)(2,1)}, bf16[512,1408]{1,0:T(8,128)(2,1)}) custom-call(bf16[8,2,64,512]{3,2,1,0:T(8,128)(2,1)S(1)} %all-to-all-done.moved_ref, f32[1,512]{1,0:T(1,128)S(1)} %bitcast.17, bf16[512,1536]{1,0:T(8,128)(2,1)S(1)} %copy-done.6, bf16[512,512]{1,0:T(8,128)(2,1)S(1)} %copy-done.7, ...), custom_call_target="tpu_custom_call" | custom-call | flops 4000000000 | bytes 5378048 | tf_op jit(solution)/shard_map/column_heads/pallas_call | solution.py:203
  43.0 0.0 all-to-all-done.2
  43.0 4.3 %all-to-all-start.3 = ((bf16[8,64,1408]{2,1,0:T(8,128)(2,1)}), bf16[8,64,1408]{2,1,0:T(8,128)(2,1)}, u32[]{:S(2)}, u32[]{:S(2)}) async-start(bf16[8,64,1408]{2,1,0:T(8,128)(2,1)} %bitcast.8), calls=%async_computation.3 | async-start | bytes 2883584 | tf_op jit(solution)/shard_map/all_to_all | solution.py:255
  47.3 1.2 %reduce_sum.21 = bf16[64,768]{1,0:T(8,128)(2,1)S(1)} reduce(bf16[8,64,768]{2,1,0:T(8,128)(2,1)} %all-to-all-done.2, bf16[]{:T(256)} %constant.1.clone.1), dimensions={0}, to_apply=%region_0.0 | reduce | flops 344064 | bytes 884738 | tf_op jit(solution)/shard_map/reduce_sum | solution.py:267
  48.5 1.7 %collective-permute-start = (bf16[64,768]{1,0:T(8,128)(2,1)S(1)}, bf16[64,768]{1,0:T(8,128)(2,1)S(1)}, u32[]{:S(2)}, u32[]{:S(2)}) collective-permute-start(bf16[64,768]{1,0:T(8,128)(2,1)S(1)} %reduce_sum.21), channel_id=1, source_target_pairs={{0,1},{1,0},{2,3},{3,2},{4,5},{5,4},{6,7},{7,6},{8,9},{9,8},{10,11... | collective-permute-start | bytes 294920 | tf_op jit(solution)/shard_map/ppermute | solution.py:277
  50.2 3.5 %collective-permute-done = bf16[64,768]{1,0:T(8,128)(2,1)S(1)} collective-permute-done((bf16[64,768]{1,0:T(8,128)(2,1)S(1)}, bf16[64,768]{1,0:T(8,128)(2,1)S(1)}, u32[]{:S(2)}, u32[]{:S(2)}) %collective-permute-start) | collective-permute-done | bytes 98336 | tf_op jit(solution)/shard_map/ppermute | solution.py:277
  53.7 2.6 %collective-permute-start.1 = (bf16[64,768]{1,0:T(8,128)(2,1)S(1)}, bf16[64,768]{1,0:T(8,128)(2,1)S(1)}, u32[]{:S(2)}, u32[]{:S(2)}) collective-permute-start(bf16[64,768]{1,0:T(8,128)(2,1)S(1)} %add_convert_fusion), channel_id=1, source_target_pairs={{0,2},{1,3},{2,0},{3,1},{4,6},{5,7},{6,4},{7,5},{8,10},{9,11},{10,... | collective-permute-start | bytes 294920 | tf_op jit(solution)/shard_map/ppermute | solution.py:277
  56.4 10.5 %all-to-all-done.3 = bf16[8,64,1408]{2,1,0:T(8,128)(2,1)} async-done(((bf16[8,64,1408]{2,1,0:T(8,128)(2,1)}), bf16[8,64,1408]{2,1,0:T(8,128)(2,1)}, u32[]{:S(2)}, u32[]{:S(2)}) %all-to-all-start.3) | async-done | bytes 1441824 | tf_op jit(solution)/shard_map/all_to_all | solution.py:255
  66.9 1.6 %convert_reduce_fusion = f32[64,1408]{1,0:T(8,128)S(1)} fusion(bf16[8,64,1408]{2,1,0:T(8,128)(2,1)} %all-to-all-done.3), kind=kLoop, calls=%fused_computation | loop fusion | flops 1351680 | bytes 1802240 | tf_op jit(solution)/shard_map/reduce_sum | solution.py:268
  68.5 0.2 fusion.2
  68.7 0.1 select_convert_fusion.1
  68.8 0.0 copy-start.3
  68.8 1.7 %collective-permute-start.2 = (bf16[64,1408]{1,0:T(8,128)(2,1)S(1)}, bf16[64,1408]{1,0:T(8,128)(2,1)S(1)}, u32[]{:S(2)}, u32[]{:S(2)}) collective-permute-start(bf16[64,1408]{1,0:T(8,128)(2,1)S(1)} %pad_maximum_fusion.1), channel_id=1, source_target_pairs={{0,1},{1,0},{2,3},{3,2},{4,5},{5,4},{6,7},{7,6},{8,9},{9,8},{10,11... | collective-permute-start | bytes 540680 | tf_op jit(solution)/shard_map/ppermute | solution.py:277
  70.5 0.0 collective-permute-done.1
  70.5 3.5 %all-to-all-start.1 = ((bf16[8,64,512]{2,1,0:T(8,128)(2,1)}), bf16[8,64,512]{2,1,0:T(8,128)(2,1)S(1)}, u32[]{:S(2)}, u32[]{:S(2)}) async-start(bf16[8,64,512]{2,1,0:T(8,128)(2,1)} %get-tuple-element.13), calls=%async_computation.1 | async-start | bytes 1048576 | tf_op jit(solution)/shard_map/all_to_all | solution.py:254
  74.0 0.4 collective-permute-done.2
  74.4 0.2 fusion.1
  74.6 0.1 select_convert_fusion
  74.8 2.7 %collective-permute-start.3 = (bf16[64,1408]{1,0:T(8,128)(2,1)S(1)}, bf16[64,1408]{1,0:T(8,128)(2,1)S(1)}, u32[]{:S(2)}, u32[]{:S(2)}) collective-permute-start(bf16[64,1408]{1,0:T(8,128)(2,1)S(1)} %pad_maximum_fusion.2), channel_id=1, source_target_pairs={{0,2},{1,3},{2,0},{3,1},{4,6},{5,7},{6,4},{7,5},{8,10},{9,11},{10,... | collective-permute-start | bytes 540680 | tf_op jit(solution)/shard_map/ppermute | solution.py:277
  77.5 0.6 slice_dynamic-update-slice_fusion.5
  78.1 5.6 %all-to-all-done.1 = bf16[8,64,512]{2,1,0:T(8,128)(2,1)S(1)} async-done(((bf16[8,64,512]{2,1,0:T(8,128)(2,1)}), bf16[8,64,512]{2,1,0:T(8,128)(2,1)S(1)}, u32[]{:S(2)}, u32[]{:S(2)}) %all-to-all-start.1) | async-done | bytes 524320 | tf_op jit(solution)/shard_map/all_to_all | solution.py:254
  83.7 0.0 copy-done.3
  83.7 0.0 copy-start.8
  83.7 1.3 %input_grad.1 = bf16[512,512]{1,0:T(8,128)(2,1)} custom-call(bf16[512,512]{1,0:T(8,128)(2,1)S(1)} %bitcast.12, bf16[512,512]{1,0:T(8,128)(2,1)S(1)} %bitcast.15, f32[1,512]{1,0:T(1,128)S(1)} %bitcast.18, f32[512,512]{1,0:T(8,128)S(1)} %copy-done.3, bf16[512,512]{1,0:T(8,128)(2,1)S(1)} %bitcast.9), custom_call_target="tpu_custom_call" | custom-call | flops 10000000 | bytes 3147776 | tf_op jit(solution)/shard_map/input_grad/pallas_call | solution.py:203
  85.0 0.9 %collective-permute-done.3 = bf16[64,1408]{1,0:T(8,128)(2,1)S(1)} collective-permute-done((bf16[64,1408]{1,0:T(8,128)(2,1)S(1)}, bf16[64,1408]{1,0:T(8,128)(2,1)S(1)}, u32[]{:S(2)}, u32[]{:S(2)}) %collective-permute-start.3) | collective-permute-done | bytes 180256 | tf_op jit(solution)/shard_map/ppermute | solution.py:277
  86.0 0.7 fusion
  86.7 0.7 slice.81
  87.4 0.0 copy-done.8
  87.5 0.0 copy-start.9
  87.5 0.7 copy-done.9
  (19 shorter events, 0.3 us)
Async XLA Ops:
  2.9 5.3 %copy-start = (bf16[1,1,512,512]{3,2,1,0:T(8,128)(2,1)S(1)}, bf16[1,1,512,512]{3,2,1,0:T(8,128)(2,1)}, u32[]{:S(2)}) copy-start(bf16[1,1,512,512]{3,2,1,0:T(8,128)(2,1)} %param.5) | copy-start | bytes 1572868
  2.9 5.3 %copy-start.1 = (bf16[1,1,512,512]{3,2,1,0:T(8,128)(2,1)S(1)}, bf16[1,1,512,512]{3,2,1,0:T(8,128)(2,1)}, u32[]{:S(2)}) copy-start(bf16[1,1,512,512]{3,2,1,0:T(8,128)(2,1)} %param.9) | copy-start | bytes 1572868
  2.9 5.3 %copy-start.4 = (f32[512]{0:T(512)S(1)}, f32[512]{0:T(512)}, u32[]{:S(2)}) copy-start(f32[512]{0:T(512)} %param.6) | copy-start | bytes 6148
  2.9 5.3 %copy-start.7 = (bf16[512,512]{1,0:T(8,128)(2,1)S(1)}, bf16[512,512]{1,0:T(8,128)(2,1)}, u32[]{:S(2)}) copy-start(bf16[512,512]{1,0:T(8,128)(2,1)} %wout_ref.3) | copy-start | bytes 1572868
  2.9 21.1 %all-to-all-start = ((bf16[8,2,64,512]{3,2,1,0:T(8,128)(2,1)}), bf16[8,2,64,512]{3,2,1,0:T(8,128)(2,1)S(1)}, u32[]{:S(2)}, u32[]{:S(2)}) async-start(bf16[8,2,64,512]{3,2,1,0:T(8,128)(2,1)} %pad_maximum_fusion), calls=%async_computation | async-start | bytes 2097152 | tf_op jit(solution)/shard_map/all_to_all | solution.py:226
  8.3 1.4 %copy-start.5 = (bf16[512,1536]{1,0:T(8,128)(2,1)S(1)}, bf16[512,1536]{1,0:T(8,128)(2,1)}, u32[]{:S(2)}) copy-start(bf16[512,1536]{1,0:T(8,128)(2,1)} %wqkv_ref.3) | copy-start | bytes 4718596
  23.0 1.0 %copy-start.2 = (f32[512,512]{1,0:T(8,128)}, f32[512,512]{1,0:T(8,128)S(1)}, u32[]{:S(2)}) copy-start(f32[512,512]{1,0:T(8,128)S(1)} %get-tuple-element.10.row_ref) | copy-start | bytes 3145732
  24.0 19.0 %all-to-all-start.2 = ((bf16[8,64,768]{2,1,0:T(8,128)(2,1)}), bf16[8,64,768]{2,1,0:T(8,128)(2,1)}, u32[]{:S(2)}, u32[]{:S(2)}) async-start(bf16[8,64,768]{2,1,0:T(8,128)(2,1)} %bitcast.7), calls=%async_computation.2 | async-start | bytes 1572864 | tf_op jit(solution)/shard_map/all_to_all | solution.py:242
  28.4 1.4 %copy-start.6 = (bf16[512,1536]{1,0:T(8,128)(2,1)S(1)}, bf16[512,1536]{1,0:T(8,128)(2,1)}, u32[]{:S(2)}) copy-start(bf16[512,1536]{1,0:T(8,128)(2,1)} %wqkv_ref.3) | copy-start | bytes 4718596
  43.0 23.9 %all-to-all-start.3 = ((bf16[8,64,1408]{2,1,0:T(8,128)(2,1)}), bf16[8,64,1408]{2,1,0:T(8,128)(2,1)}, u32[]{:S(2)}, u32[]{:S(2)}) async-start(bf16[8,64,1408]{2,1,0:T(8,128)(2,1)} %bitcast.8), calls=%async_computation.3 | async-start | bytes 2883584 | tf_op jit(solution)/shard_map/all_to_all | solution.py:255
  48.5 5.2 %collective-permute-start = (bf16[64,768]{1,0:T(8,128)(2,1)S(1)}, bf16[64,768]{1,0:T(8,128)(2,1)S(1)}, u32[]{:S(2)}, u32[]{:S(2)}) collective-permute-start(bf16[64,768]{1,0:T(8,128)(2,1)S(1)} %reduce_sum.21), channel_id=1, source_target_pairs={{0,1},{1,0},{2,3},{3,2},{4,5},{5,4},{6,7},{7,6},{8,9},{9,8},{10,11... | collective-permute-start | bytes 294920 | tf_op jit(solution)/shard_map/ppermute | solution.py:277
  53.7 16.8 %collective-permute-start.1 = (bf16[64,768]{1,0:T(8,128)(2,1)S(1)}, bf16[64,768]{1,0:T(8,128)(2,1)S(1)}, u32[]{:S(2)}, u32[]{:S(2)}) collective-permute-start(bf16[64,768]{1,0:T(8,128)(2,1)S(1)} %add_convert_fusion), channel_id=1, source_target_pairs={{0,2},{1,3},{2,0},{3,1},{4,6},{5,7},{6,4},{7,5},{8,10},{9,11},{10,... | collective-permute-start | bytes 294920 | tf_op jit(solution)/shard_map/ppermute | solution.py:277
  68.8 14.9 %copy-start.3 = (f32[512,512]{1,0:T(8,128)S(1)}, f32[512,512]{1,0:T(8,128)}, u32[]{:S(2)}) copy-start(f32[512,512]{1,0:T(8,128)} %copy-done.2) | copy-start | bytes 3145732
  68.8 5.6 %collective-permute-start.2 = (bf16[64,1408]{1,0:T(8,128)(2,1)S(1)}, bf16[64,1408]{1,0:T(8,128)(2,1)S(1)}, u32[]{:S(2)}, u32[]{:S(2)}) collective-permute-start(bf16[64,1408]{1,0:T(8,128)(2,1)S(1)} %pad_maximum_fusion.1), channel_id=1, source_target_pairs={{0,1},{1,0},{2,3},{3,2},{4,5},{5,4},{6,7},{7,6},{8,9},{9,8},{10,11... | collective-permute-start | bytes 540680 | tf_op jit(solution)/shard_map/ppermute | solution.py:277
  70.5 13.2 %all-to-all-start.1 = ((bf16[8,64,512]{2,1,0:T(8,128)(2,1)}), bf16[8,64,512]{2,1,0:T(8,128)(2,1)S(1)}, u32[]{:S(2)}, u32[]{:S(2)}) async-start(bf16[8,64,512]{2,1,0:T(8,128)(2,1)} %get-tuple-element.13), calls=%async_computation.1 | async-start | bytes 1048576 | tf_op jit(solution)/shard_map/all_to_all | solution.py:254
  74.8 11.2 %collective-permute-start.3 = (bf16[64,1408]{1,0:T(8,128)(2,1)S(1)}, bf16[64,1408]{1,0:T(8,128)(2,1)S(1)}, u32[]{:S(2)}, u32[]{:S(2)}) collective-permute-start(bf16[64,1408]{1,0:T(8,128)(2,1)S(1)} %pad_maximum_fusion.2), channel_id=1, source_target_pairs={{0,2},{1,3},{2,0},{3,1},{4,6},{5,7},{6,4},{7,5},{8,10},{9,11},{10,... | collective-permute-start | bytes 540680 | tf_op jit(solution)/shard_map/ppermute | solution.py:277
  83.7 3.7 %copy-start.8 = (f32[64,1536]{1,0:T(8,128)S(1)}, f32[64,1536]{1,0:T(8,128)}, u32[]{:S(2)}) copy-start(f32[64,1536]{1,0:T(8,128)} %slice_dynamic-update-slice_fusion.5) | copy-start | bytes 1179652
  87.5 0.7 copy-start.9

commit v2 on v1

--- a/solution.py
+++ b/solution.py
@@ -33,16 +33,42 @@
     return inverse_rms, x * inverse_rms
 
 
-def head_step(q, k, v, g, qt, kt, vt, gt, mask):
-    scores = jnp.where(mask, dot_nn(q, kt), -1e30)
-    exponent = jnp.exp(scores - jnp.max(scores, -1, keepdims=True))
-    probs = exponent * (1.0 / jnp.sum(exponent, -1, keepdims=True))
+def transposed(x):
+    block = math.gcd(x.shape[1], 256)
+    eye = (
+        lax.broadcasted_iota(jnp.int32, (block, block), 0)
+        == lax.broadcasted_iota(jnp.int32, (block, block), 1)
+    ).astype(F32).astype(BF16)
+    parts = [
+        dot_nt(eye, x[:, at : at + block]).astype(BF16) for at in range(0, x.shape[1], block)
+    ]
+    return parts[0] if len(parts) == 1 else jnp.concatenate(parts, 0)
+
+
+def head_pair(x):
+    lane = lax.broadcasted_iota(jnp.int32, x.shape, 1)
+    zero = jnp.zeros_like(x)
+    return jnp.concatenate([jnp.where(lane < HD, x, zero), jnp.where(lane < HD, zero, x)], 0)
+
+
+def pair_step(q2, g2, gt, k, v, kt, vt, mask_at, mask):
+    count = gt.shape[1]
+    scores = dot_nt(k, q2)
+    tail = jnp.where(mask, scores[mask_at:], -1e30)
+    scores = tail if mask_at == 0 else jnp.concatenate([scores[:mask_at], tail], 0)
+    exponent = jnp.exp(scores - jnp.max(scores, 0, keepdims=True))
+    probs = exponent * (1.0 / jnp.sum(exponent, 0, keepdims=True))
     weights = probs.astype(BF16)
-    attended = dot_nn(weights, v).astype(BF16)
-    delta = jnp.sum(g.astype(F32) * attended.astype(F32), -1, keepdims=True)
-    score_grad = (probs * (dot_nn(g, vt) - delta)).astype(BF16)
-    grad_q = (dot_nn(score_grad, k) * SCALE).astype(BF16)
-    return attended, grad_q, dot_nn(qt, score_grad), dot_nn(gt, weights)
+    both = dot_nn(vt, weights)
+    attended = jnp.concatenate([both[:HD, :count], both[HD:, count:]], 0).astype(BF16)
+    product = gt.astype(F32) * attended.astype(F32)
+    delta = jnp.concatenate(
+        [jnp.sum(product[:HD], 0, keepdims=True), jnp.sum(product[HD:], 0, keepdims=True)], 1
+    )
+    score_grad = (probs * (dot_nt(v, g2) - delta)).astype(BF16)
+    both = dot_nn(kt, score_grad)
+    grad_q = (jnp.concatenate([both[:HD, :count], both[HD:, count:]], 0) * SCALE).astype(BF16)
+    return attended, grad_q, dot_nn(score_grad, q2), dot_nn(weights, g2)
 
 
 def part_columns(width, second):
@@ -56,11 +82,11 @@
     return q * jnp.asarray(SCALE, BF16), k, v, g
 
 
-def weight_terms(hidden, normed, cot, attended, grads, wqkv_ref, second):
-    hidden_t = hidden.T
+def weight_terms(hidden, normed, cot, attended_t, grads, wqkv_ref, second):
+    hidden_t = transposed(hidden)
     parts = part_columns(wqkv_ref.shape[0], second)
     term_qkv = [dot_nn(hidden_t, grad) for grad in grads]
-    term_out = dot_nn(attended.T, cot)
+    term_out = dot_nn(attended_t, cot)
     grad_hidden = dot_nt(grads[0], wqkv_ref[:, parts[0]])
     grad_hidden += dot_nt(grads[1], wqkv_ref[:, parts[1]])
     grad_hidden += dot_nt(grads[2], wqkv_ref[:, parts[2]])
@@ -71,43 +97,40 @@
 def row_kernel(
     x_ref, cot_ref, gain_ref, wqkv_ref, wout_ref,
     qkv_ref, out_ref, hidden_ref, gain_term_ref,
-    dkt_ref, dvt_ref,
+    dk_ref, dv_ref,
 ):
     tokens = x_ref.shape[0]
     _, normed = rms_parts(x_ref[...].astype(F32))
     hidden = (normed * gain_ref[...]).astype(BF16)
     cot = cot_ref[...]
     q, k, v, g = project(hidden, cot, wqkv_ref, wout_ref, 0)
-    qt, kt, vt, gt = q.T, k.T, v.T, g.T
-    dkt_ref[...] = jnp.zeros_like(dkt_ref)
-    dvt_ref[...] = jnp.zeros_like(dvt_ref)
+    kt, vt, gt = transposed(k), transposed(v), transposed(g)
+    dk_ref[...] = jnp.zeros_like(dk_ref)
+    dv_ref[...] = jnp.zeros_like(dv_ref)
     step = math.gcd(tokens, QUERY_BLOCK)
-    att_blocks, dq_blocks = [], []
-    for start in range(0, tokens, step):
-        rows, keys = slice(start, start + step), slice(0, start + step)
-        shape = (step, start + step)
-        mask = (
-            lax.broadcasted_iota(jnp.int32, shape, 0) + start
-            >= lax.broadcasted_iota(jnp.int32, shape, 1)
-        )
+    query = lax.broadcasted_iota(jnp.int32, (step, 2 * step), 1) % step
+    mask = query >= lax.broadcasted_iota(jnp.int32, (step, 2 * step), 0)
+    att_pairs, dq_pairs = [], []
+    for pair in range(HH // 2):
+        lanes = slice(pair * 2 * HD, (pair + 1) * 2 * HD)
         atts, dqs = [], []
-        for head in range(HH):
-            lanes = slice(head * HD, (head + 1) * HD)
-            attended, dq, dkt, dvt = head_step(
-                q[rows, lanes], k[keys, lanes], v[keys, lanes], g[rows, lanes],
-                qt[lanes, rows], kt[lanes, keys], vt[lanes, keys], gt[lanes, rows], mask,
+        for start in range(0, tokens, step):
+            rows, keys = slice(start, start + step), slice(0, start + step)
+            attended, dq, dk, dv = pair_step(
+                head_pair(q[rows, lanes]), head_pair(g[rows, lanes]), gt[lanes, rows],
+                k[keys, lanes], v[keys, lanes], kt[lanes, keys], vt[lanes, keys], start, mask,
             )
-            dkt_ref[lanes, keys] += dkt
-            dvt_ref[lanes, keys] += dvt
+            dk_ref[keys, lanes] += dk
+            dv_ref[keys, lanes] += dv
             atts.append(attended)
             dqs.append(dq)
-        att_blocks.append(jnp.concatenate(atts, 1))
-        dq_blocks.append(jnp.concatenate(dqs, 1))
-    attended = jnp.concatenate(att_blocks, 0)
+        att_pairs.append(jnp.concatenate(atts, 1))
+        dq_pairs.append(jnp.concatenate(dqs, 1))
+    attended = jnp.concatenate(att_pairs, 0)
     grads = (
-        jnp.concatenate(dq_blocks, 0),
-        dkt_ref[...].astype(BF16).T,
-        dvt_ref[...].astype(BF16).T,
+        transposed(jnp.concatenate(dq_pairs, 0)),
+        dk_ref[...].astype(BF16),
+        dv_ref[...].astype(BF16),
     )
     term_qkv, term_out, grad_hidden, term_gain = weight_terms(
         hidden, normed, cot, attended, grads, wqkv_ref, 0
@@ -139,31 +162,31 @@
     hidden = (normed * gain_ref[...]).astype(BF16)
     cot = gathered(1).astype(BF16)
     q, k, v, g = project(hidden, cot, wqkv_ref, wout_ref, 1)
-    qt, kt, vt, gt = q.T, k.T, v.T, g.T
-    query = lax.broadcasted_iota(jnp.int32, (block, block), 0)
-    key = lax.broadcasted_iota(jnp.int32, (block, block), 1)
+    kt, vt, gt = transposed(k), transposed(v), transposed(g)
+    query = lax.broadcasted_iota(jnp.int32, (block, 2 * block), 1) % block
+    key = lax.broadcasted_iota(jnp.int32, (block, 2 * block), 0)
     mask = (query >= key) & (query % group == key % group)
-    att_blocks, dq_blocks, dkt_blocks, dvt_blocks = [], [], [], []
-    for start in range(0, all_rows * share, block):
-        rows = slice(start, start + block)
+    att_pairs, dq_pairs, dk_pairs, dv_pairs = [], [], [], []
+    for pair in range(HH // 2):
+        lanes = slice(pair * 2 * HD, (pair + 1) * 2 * HD)
         results = []
-        for head in range(HH):
-            lanes = slice(head * HD, (head + 1) * HD)
+        for start in range(0, all_rows * share, block):
+            rows = slice(start, start + block)
             results.append(
-                head_step(
-                    q[rows, lanes], k[rows, lanes], v[rows, lanes], g[rows, lanes],
-                    qt[lanes, rows], kt[lanes, rows], vt[lanes, rows], gt[lanes, rows], mask,
+                pair_step(
+                    head_pair(q[rows, lanes]), head_pair(g[rows, lanes]), gt[lanes, rows],
+                    k[rows, lanes], v[rows, lanes], kt[lanes, rows], vt[lanes, rows], 0, mask,
                 )
             )
-        att_blocks.append(jnp.concatenate([r[0] for r in results], 1))
-        dq_blocks.append(jnp.concatenate([r[1] for r in results], 1))
-        dkt_blocks.append(jnp.concatenate([r[2] for r in results], 0))
-        dvt_blocks.append(jnp.concatenate([r[3] for r in results], 0))
-    attended = jnp.concatenate(att_blocks, 0)
+        att_pairs.append(jnp.concatenate([r[0] for r in results], 1))
+        dq_pairs.append(jnp.concatenate([r[1] for r in results], 1))
+        dk_pairs.append(jnp.concatenate([r[2] for r in results], 0))
+        dv_pairs.append(jnp.concatenate([r[3] for r in results], 0))
+    attended = jnp.concatenate(att_pairs, 0)
     grads = (
-        jnp.concatenate(dq_blocks, 0),
-        jnp.concatenate(dkt_blocks, 1).astype(BF16).T,
-        jnp.concatenate(dvt_blocks, 1).astype(BF16).T,
+        transposed(jnp.concatenate(dq_pairs, 0)),
+        jnp.concatenate(dk_pairs, 1).astype(BF16),
+        jnp.concatenate(dv_pairs, 1).astype(BF16),
     )
     term_qkv, term_out, grad_hidden, term_gain = weight_terms(
         hidden, normed, cot, attended, grads, wqkv_ref, 1
@@ -235,7 +258,7 @@
             shaped((columns, width), F32),
             shaped((1, width), F32),
         ],
-        [pltpu.VMEM((HW, columns), F32), pltpu.VMEM((HW, columns), F32)],
+        [pltpu.VMEM((columns, HW), F32), pltpu.VMEM((columns, HW), F32)],
         6_000_000_000,
         (x, cot, gain, qkv_weight, out_weight),
     )

time: 88.7 us -> 86.2 us (0.972)
  Pallas kernels: 27.8 us -> 16.5 us
  waiting for transfers between devices: 21 us -> 30 us
    pallas_call x3, Pallas kernels: 27.8 us -> 16.5 us  [call(): pl.pallas_call(kernel, out_shape=outs, in_specs=[pl.BlockSpec(memory_spac...]
    all_to_all x1, waiting for transfers between devices: 0.01 us -> 4.84 us  [body(): lax.all_to_all(outgoing, 'seq', split_axis=0, concat_axis=0, tiled=True)]
    all_to_all x1, waiting for transfers between devices: 0.01 us -> 4.18 us  [body(): lax.all_to_all(row_qkv.reshape(n, row_share, 3 * HW), 'seq', split_axis=0...]
  transfers between devices with their start and end apart: 8 -> 8, of which waited for: 5 -> 7; matrix products, arithmetic and copies ran while one was open for 5% -> 5% of each run, Pallas kernels for 32% -> 19%
where the time goes in v2:
time: 86.2 us; the launch traced here: 85.7 us
  waiting for transfers between devices  30 us (35%)
  starting transfers between devices  25.9 us (30%)
  Pallas kernels  16.5 us (19%)
  other arithmetic  6.48 us (8%)
  local copies, waits for them, and re-layouts  5.93 us (7%)
    pallas_call x3, Pallas kernels, call(): pl.pallas_call(kernel, out_shape=outs, in_specs=[pl.BlockSpec(memory_spac...  16.5 us
    all_to_all x1, waiting for transfers between devices, body(): lax.all_to_all(col_terms.reshape(n, row_share, term_width), 'seq', split_...  10.6 us
    ppermute x4, starting transfers between devices, over_dp(): got = lax.ppermute(sent, 'dp', [(i, i ^ distance) for i in range(m)])  8.61 us
    all_to_all x1, waiting for transfers between devices, body(): lax.all_to_all(back, 'seq', split_axis=0, concat_axis=0, tiled=True)  5.63 us
    all_to_all x1, starting transfers between devices, body(): lax.all_to_all(outgoing, 'seq', split_axis=0, concat_axis=0, tiled=True)  5.31 us
    unnamed x25, local copies, waits for them, and re-layouts  5.21 us
    all_to_all x1, waiting for transfers between devices, body(): lax.all_to_all(outgoing, 'seq', split_axis=0, concat_axis=0, tiled=True)  4.84 us
    ppermute x4, waiting for transfers between devices, over_dp(): got = lax.ppermute(sent, 'dp', [(i, i ^ distance) for i in range(m)])  4.8 us
  transfers between devices with their start and end apart: 8, of which 7 were waited for; matrix products, arithmetic and copies ran while one was open for 5% of the time, Pallas kernels for 19%

profile of v2, /device:TPU:0, one launch (start us, length us, event | category | flops | bytes accessed | tf_op | source)
XLA Modules:
  0.0 85.7 jit_solution(5180189556403828561)
XLA Ops:
  0.6 2.3 %pad_maximum_fusion = bf16[8,2,64,512]{3,2,1,0:T(8,128)(2,1)} fusion(bf16[8,1,64,512]{3,2,1,0:T(8,128)(2,1)} %bitcast.13, bf16[8,1,64,512]{3,2,1,0:T(8,128)(2,1)} %bitcast.10), kind=kLoop, calls=%fused_computation.1 | loop fusion | flops 524288 | bytes 2097152 | tf_op jit(solution)/shard_map/stack | solution.py:248
  2.9 0.0 copy-start
  2.9 0.0 copy-start.4
  2.9 0.0 copy-start.7
  2.9 5.3 %all-to-all-start = ((bf16[8,2,64,512]{3,2,1,0:T(8,128)(2,1)}), bf16[8,2,64,512]{3,2,1,0:T(8,128)(2,1)S(1)}, u32[]{:S(2)}, u32[]{:S(2)}) async-start(bf16[8,2,64,512]{3,2,1,0:T(8,128)(2,1)} %pad_maximum_fusion), calls=%async_computation | async-start | bytes 2097152 | tf_op jit(solution)/shard_map/all_to_all | solution.py:249
  8.2 0.0 copy-done
  8.2 0.0 copy-done.1
  8.2 0.0 copy-done.4
  8.2 0.0 copy-done.7
  8.3 0.0 copy-start.5
  8.3 1.4 %copy-done.5 = bf16[512,1536]{1,0:T(8,128)(2,1)S(1)} copy-done((bf16[512,1536]{1,0:T(8,128)(2,1)S(1)}, bf16[512,1536]{1,0:T(8,128)(2,1)}, u32[]{:S(2)}) %copy-start.5) | copy-done | bytes 1572888
  9.7 8.1 %row_heads.1 = (bf16[512,768]{1,0:T(8,128)(2,1)}, bf16[256,512]{1,0:T(8,128)(2,1)S(1)}, f32[512,512]{1,0:T(8,128)S(1)}, f32[1,512]{1,0:T(1,128)S(1)}) custom-call(bf16[512,512]{1,0:T(8,128)(2,1)S(1)} %bitcast.11, bf16[512,512]{1,0:T(8,128)(2,1)S(1)} %bitcast.14, f32[1,512]{1,0:T(1,128)S(1)} %bitcast.16, bf16[512,1536]{1,0:T(8,128)(2,1)S(1)} %copy-done.5, ...), custom_call_target="tpu_custom_call" | custom-call | flops 6000000000 | bytes 5246976 | tf_op jit(solution)/shard_map/row_heads/pallas_call | solution.py:226
  17.8 0.0 copy-start.2
  17.8 1.0 %copy-done.2 = f32[512,512]{1,0:T(8,128)} copy-done((f32[512,512]{1,0:T(8,128)}, f32[512,512]{1,0:T(8,128)S(1)}, u32[]{:S(2)}) %copy-start.2) | copy-done | bytes 1048600
  18.8 4.8 %all-to-all-done.moved_ref = bf16[8,2,64,512]{3,2,1,0:T(8,128)(2,1)S(1)} async-done(((bf16[8,2,64,512]{3,2,1,0:T(8,128)(2,1)}), bf16[8,2,64,512]{3,2,1,0:T(8,128)(2,1)S(1)}, u32[]{:S(2)}, u32[]{:S(2)}) %all-to-all-start) | async-done | bytes 1048608 | tf_op jit(solution)/shard_map/all_to_all | solution.py:249
  23.6 4.2 %all-to-all-start.2 = ((bf16[8,64,768]{2,1,0:T(8,128)(2,1)}), bf16[8,64,768]{2,1,0:T(8,128)(2,1)}, u32[]{:S(2)}, u32[]{:S(2)}) async-start(bf16[8,64,768]{2,1,0:T(8,128)(2,1)} %bitcast.7), calls=%async_computation.2 | async-start | bytes 1572864 | tf_op jit(solution)/shard_map/all_to_all | solution.py:265
  27.9 0.0 copy-start.6
  27.9 1.4 %copy-done.6 = bf16[512,1536]{1,0:T(8,128)(2,1)S(1)} copy-done((bf16[512,1536]{1,0:T(8,128)(2,1)S(1)}, bf16[512,1536]{1,0:T(8,128)(2,1)}, u32[]{:S(2)}) %copy-start.6) | copy-done | bytes 1572888
  29.3 7.0 %column_heads.1 = (bf16[8,64,512]{2,1,0:T(8,128)(2,1)}, bf16[512,1408]{1,0:T(8,128)(2,1)}) custom-call(bf16[8,2,64,512]{3,2,1,0:T(8,128)(2,1)S(1)} %all-to-all-done.moved_ref, f32[1,512]{1,0:T(1,128)S(1)} %bitcast.17, bf16[512,1536]{1,0:T(8,128)(2,1)S(1)} %copy-done.6, bf16[512,512]{1,0:T(8,128)(2,1)S(1)} %copy-done.7, ...), custom_call_target="tpu_custom_call" | custom-call | flops 4000000000 | bytes 5378048 | tf_op jit(solution)/shard_map/column_heads/pallas_call | solution.py:226
  36.3 4.2 %all-to-all-done.2 = bf16[8,64,768]{2,1,0:T(8,128)(2,1)} async-done(((bf16[8,64,768]{2,1,0:T(8,128)(2,1)}), bf16[8,64,768]{2,1,0:T(8,128)(2,1)}, u32[]{:S(2)}, u32[]{:S(2)}) %all-to-all-start.2) | async-done | bytes 786464 | tf_op jit(solution)/shard_map/all_to_all | solution.py:265
  40.5 4.3 %all-to-all-start.3 = ((bf16[8,64,1408]{2,1,0:T(8,128)(2,1)}), bf16[8,64,1408]{2,1,0:T(8,128)(2,1)}, u32[]{:S(2)}, u32[]{:S(2)}) async-start(bf16[8,64,1408]{2,1,0:T(8,128)(2,1)} %bitcast.8), calls=%async_computation.3 | async-start | bytes 2883584 | tf_op jit(solution)/shard_map/all_to_all | solution.py:278
  44.8 1.2 %reduce_sum.21 = bf16[64,768]{1,0:T(8,128)(2,1)S(1)} reduce(bf16[8,64,768]{2,1,0:T(8,128)(2,1)} %all-to-all-done.2, bf16[]{:T(256)} %constant.1.clone.1), dimensions={0}, to_apply=%region_0.0 | reduce | flops 344064 | bytes 884738 | tf_op jit(solution)/shard_map/reduce_sum | solution.py:290
  46.0 1.7 %collective-permute-start = (bf16[64,768]{1,0:T(8,128)(2,1)S(1)}, bf16[64,768]{1,0:T(8,128)(2,1)S(1)}, u32[]{:S(2)}, u32[]{:S(2)}) collective-permute-start(bf16[64,768]{1,0:T(8,128)(2,1)S(1)} %reduce_sum.21), channel_id=1, source_target_pairs={{0,1},{1,0},{2,3},{3,2},{4,5},{5,4},{6,7},{7,6},{8,9},{9,8},{10,11... | collective-permute-start | bytes 294920 | tf_op jit(solution)/shard_map/ppermute | solution.py:300
  47.7 3.5 %collective-permute-done = bf16[64,768]{1,0:T(8,128)(2,1)S(1)} collective-permute-done((bf16[64,768]{1,0:T(8,128)(2,1)S(1)}, bf16[64,768]{1,0:T(8,128)(2,1)S(1)}, u32[]{:S(2)}, u32[]{:S(2)}) %collective-permute-start) | collective-permute-done | bytes 98336 | tf_op jit(solution)/shard_map/ppermute | solution.py:300
  51.2 2.7 %collective-permute-start.1 = (bf16[64,768]{1,0:T(8,128)(2,1)S(1)}, bf16[64,768]{1,0:T(8,128)(2,1)S(1)}, u32[]{:S(2)}, u32[]{:S(2)}) collective-permute-start(bf16[64,768]{1,0:T(8,128)(2,1)S(1)} %add_convert_fusion), channel_id=1, source_target_pairs={{0,2},{1,3},{2,0},{3,1},{4,6},{5,7},{6,4},{7,5},{8,10},{9,11},{10,... | collective-permute-start | bytes 294920 | tf_op jit(solution)/shard_map/ppermute | solution.py:300
  53.8 10.6 %all-to-all-done.3 = bf16[8,64,1408]{2,1,0:T(8,128)(2,1)} async-done(((bf16[8,64,1408]{2,1,0:T(8,128)(2,1)}), bf16[8,64,1408]{2,1,0:T(8,128)(2,1)}, u32[]{:S(2)}, u32[]{:S(2)}) %all-to-all-start.3) | async-done | bytes 1441824 | tf_op jit(solution)/shard_map/all_to_all | solution.py:278
  64.4 1.6 %convert_reduce_fusion = f32[64,1408]{1,0:T(8,128)S(1)} fusion(bf16[8,64,1408]{2,1,0:T(8,128)(2,1)} %all-to-all-done.3), kind=kLoop, calls=%fused_computation | loop fusion | flops 1351680 | bytes 1802240 | tf_op jit(solution)/shard_map/reduce_sum | solution.py:291
  66.0 0.2 fusion.2
  66.2 0.1 select_convert_fusion.1
  66.3 0.0 copy-start.3
  66.3 1.6 %collective-permute-start.2 = (bf16[64,1408]{1,0:T(8,128)(2,1)S(1)}, bf16[64,1408]{1,0:T(8,128)(2,1)S(1)}, u32[]{:S(2)}, u32[]{:S(2)}) collective-permute-start(bf16[64,1408]{1,0:T(8,128)(2,1)S(1)} %pad_maximum_fusion.1), channel_id=1, source_target_pairs={{0,1},{1,0},{2,3},{3,2},{4,5},{5,4},{6,7},{7,6},{8,9},{9,8},{10,11... | collective-permute-start | bytes 540680 | tf_op jit(solution)/shard_map/ppermute | solution.py:300
  68.0 0.0 collective-permute-done.1
  68.0 3.5 %all-to-all-start.1 = ((bf16[8,64,512]{2,1,0:T(8,128)(2,1)}), bf16[8,64,512]{2,1,0:T(8,128)(2,1)S(1)}, u32[]{:S(2)}, u32[]{:S(2)}) async-start(bf16[8,64,512]{2,1,0:T(8,128)(2,1)} %get-tuple-element.13), calls=%async_computation.1 | async-start | bytes 1048576 | tf_op jit(solution)/shard_map/all_to_all | solution.py:277
  71.5 0.4 collective-permute-done.2
  71.9 0.2 fusion.1
  72.1 0.1 select_convert_fusion
  72.3 2.7 %collective-permute-start.3 = (bf16[64,1408]{1,0:T(8,128)(2,1)S(1)}, bf16[64,1408]{1,0:T(8,128)(2,1)S(1)}, u32[]{:S(2)}, u32[]{:S(2)}) collective-permute-start(bf16[64,1408]{1,0:T(8,128)(2,1)S(1)} %pad_maximum_fusion.2), channel_id=1, source_target_pairs={{0,2},{1,3},{2,0},{3,1},{4,6},{5,7},{6,4},{7,5},{8,10},{9,11},{10,... | collective-permute-start | bytes 540680 | tf_op jit(solution)/shard_map/ppermute | solution.py:300
  74.9 0.6 slice_dynamic-update-slice_fusion.5
  75.6 5.6 %all-to-all-done.1 = bf16[8,64,512]{2,1,0:T(8,128)(2,1)S(1)} async-done(((bf16[8,64,512]{2,1,0:T(8,128)(2,1)}), bf16[8,64,512]{2,1,0:T(8,128)(2,1)S(1)}, u32[]{:S(2)}, u32[]{:S(2)}) %all-to-all-start.1) | async-done | bytes 524320 | tf_op jit(solution)/shard_map/all_to_all | solution.py:277
  81.2 0.0 copy-done.3
  81.2 0.0 copy-start.8
  81.2 1.3 %input_grad.1 = bf16[512,512]{1,0:T(8,128)(2,1)} custom-call(bf16[512,512]{1,0:T(8,128)(2,1)S(1)} %bitcast.12, bf16[512,512]{1,0:T(8,128)(2,1)S(1)} %bitcast.15, f32[1,512]{1,0:T(1,128)S(1)} %bitcast.18, f32[512,512]{1,0:T(8,128)S(1)} %copy-done.3, bf16[512,512]{1,0:T(8,128)(2,1)S(1)} %bitcast.9), custom_call_target="tpu_custom_call" | custom-call | flops 10000000 | bytes 3147776 | tf_op jit(solution)/shard_map/input_grad/pallas_call | solution.py:226
  82.5 0.9 %collective-permute-done.3 = bf16[64,1408]{1,0:T(8,128)(2,1)S(1)} collective-permute-done((bf16[64,1408]{1,0:T(8,128)(2,1)S(1)}, bf16[64,1408]{1,0:T(8,128)(2,1)S(1)}, u32[]{:S(2)}, u32[]{:S(2)}) %collective-permute-start.3) | collective-permute-done | bytes 180256 | tf_op jit(solution)/shard_map/ppermute | solution.py:300
  83.5 0.7 fusion
  84.2 0.7 slice.81
  84.9 0.0 copy-done.8
  85.0 0.0 copy-start.9
  85.0 0.7 copy-done.9
  (19 shorter events, 0.3 us)
Async XLA Ops:
  2.9 5.3 %copy-start = (bf16[1,1,512,512]{3,2,1,0:T(8,128)(2,1)S(1)}, bf16[1,1,512,512]{3,2,1,0:T(8,128)(2,1)}, u32[]{:S(2)}) copy-start(bf16[1,1,512,512]{3,2,1,0:T(8,128)(2,1)} %param.5) | copy-start | bytes 1572868
  2.9 5.3 %copy-start.1 = (bf16[1,1,512,512]{3,2,1,0:T(8,128)(2,1)S(1)}, bf16[1,1,512,512]{3,2,1,0:T(8,128)(2,1)}, u32[]{:S(2)}) copy-start(bf16[1,1,512,512]{3,2,1,0:T(8,128)(2,1)} %param.9) | copy-start | bytes 1572868
  2.9 5.3 %copy-start.4 = (f32[512]{0:T(512)S(1)}, f32[512]{0:T(512)}, u32[]{:S(2)}) copy-start(f32[512]{0:T(512)} %param.6) | copy-start | bytes 6148
  2.9 5.3 %copy-start.7 = (bf16[512,512]{1,0:T(8,128)(2,1)S(1)}, bf16[512,512]{1,0:T(8,128)(2,1)}, u32[]{:S(2)}) copy-start(bf16[512,512]{1,0:T(8,128)(2,1)} %wout_ref.3) | copy-start | bytes 1572868
  2.9 20.7 %all-to-all-start = ((bf16[8,2,64,512]{3,2,1,0:T(8,128)(2,1)}), bf16[8,2,64,512]{3,2,1,0:T(8,128)(2,1)S(1)}, u32[]{:S(2)}, u32[]{:S(2)}) async-start(bf16[8,2,64,512]{3,2,1,0:T(8,128)(2,1)} %pad_maximum_fusion), calls=%async_computation | async-start | bytes 2097152 | tf_op jit(solution)/shard_map/all_to_all | solution.py:249
  8.3 1.4 %copy-start.5 = (bf16[512,1536]{1,0:T(8,128)(2,1)S(1)}, bf16[512,1536]{1,0:T(8,128)(2,1)}, u32[]{:S(2)}) copy-start(bf16[512,1536]{1,0:T(8,128)(2,1)} %wqkv_ref.3) | copy-start | bytes 4718596
  17.8 1.0 %copy-start.2 = (f32[512,512]{1,0:T(8,128)}, f32[512,512]{1,0:T(8,128)S(1)}, u32[]{:S(2)}) copy-start(f32[512,512]{1,0:T(8,128)S(1)} %get-tuple-element.10.row_ref) | copy-start | bytes 3145732
  23.6 16.8 %all-to-all-start.2 = ((bf16[8,64,768]{2,1,0:T(8,128)(2,1)}), bf16[8,64,768]{2,1,0:T(8,128)(2,1)}, u32[]{:S(2)}, u32[]{:S(2)}) async-start(bf16[8,64,768]{2,1,0:T(8,128)(2,1)} %bitcast.7), calls=%async_computation.2 | async-start | bytes 1572864 | tf_op jit(solution)/shard_map/all_to_all | solution.py:265
  27.9 1.4 %copy-start.6 = (bf16[512,1536]{1,0:T(8,128)(2,1)S(1)}, bf16[512,1536]{1,0:T(8,128)(2,1)}, u32[]{:S(2)}) copy-start(bf16[512,1536]{1,0:T(8,128)(2,1)} %wqkv_ref.3) | copy-start | bytes 4718596
  40.5 23.9 %all-to-all-start.3 = ((bf16[8,64,1408]{2,1,0:T(8,128)(2,1)}), bf16[8,64,1408]{2,1,0:T(8,128)(2,1)}, u32[]{:S(2)}, u32[]{:S(2)}) async-start(bf16[8,64,1408]{2,1,0:T(8,128)(2,1)} %bitcast.8), calls=%async_computation.3 | async-start | bytes 2883584 | tf_op jit(solution)/shard_map/all_to_all | solution.py:278
  46.0 5.1 %collective-permute-start = (bf16[64,768]{1,0:T(8,128)(2,1)S(1)}, bf16[64,768]{1,0:T(8,128)(2,1)S(1)}, u32[]{:S(2)}, u32[]{:S(2)}) collective-permute-start(bf16[64,768]{1,0:T(8,128)(2,1)S(1)} %reduce_sum.21), channel_id=1, source_target_pairs={{0,1},{1,0},{2,3},{3,2},{4,5},{5,4},{6,7},{7,6},{8,9},{9,8},{10,11... | collective-permute-start | bytes 294920 | tf_op jit(solution)/shard_map/ppermute | solution.py:300
  51.2 16.8 %collective-permute-start.1 = (bf16[64,768]{1,0:T(8,128)(2,1)S(1)}, bf16[64,768]{1,0:T(8,128)(2,1)S(1)}, u32[]{:S(2)}, u32[]{:S(2)}) collective-permute-start(bf16[64,768]{1,0:T(8,128)(2,1)S(1)} %add_convert_fusion), channel_id=1, source_target_pairs={{0,2},{1,3},{2,0},{3,1},{4,6},{5,7},{6,4},{7,5},{8,10},{9,11},{10,... | collective-permute-start | bytes 294920 | tf_op jit(solution)/shard_map/ppermute | solution.py:300
  66.3 14.9 %copy-start.3 = (f32[512,512]{1,0:T(8,128)S(1)}, f32[512,512]{1,0:T(8,128)}, u32[]{:S(2)}) copy-start(f32[512,512]{1,0:T(8,128)} %copy-done.2) | copy-start | bytes 3145732
  66.3 5.6 %collective-permute-start.2 = (bf16[64,1408]{1,0:T(8,128)(2,1)S(1)}, bf16[64,1408]{1,0:T(8,128)(2,1)S(1)}, u32[]{:S(2)}, u32[]{:S(2)}) collective-permute-start(bf16[64,1408]{1,0:T(8,128)(2,1)S(1)} %pad_maximum_fusion.1), channel_id=1, source_target_pairs={{0,1},{1,0},{2,3},{3,2},{4,5},{5,4},{6,7},{7,6},{8,9},{9,8},{10,11... | collective-permute-start | bytes 540680 | tf_op jit(solution)/shard_map/ppermute | solution.py:300
  68.0 13.2 %all-to-all-start.1 = ((bf16[8,64,512]{2,1,0:T(8,128)(2,1)}), bf16[8,64,512]{2,1,0:T(8,128)(2,1)S(1)}, u32[]{:S(2)}, u32[]{:S(2)}) async-start(bf16[8,64,512]{2,1,0:T(8,128)(2,1)} %get-tuple-element.13), calls=%async_computation.1 | async-start | bytes 1048576 | tf_op jit(solution)/shard_map/all_to_all | solution.py:277
  72.3 11.2 %collective-permute-start.3 = (bf16[64,1408]{1,0:T(8,128)(2,1)S(1)}, bf16[64,1408]{1,0:T(8,128)(2,1)S(1)}, u32[]{:S(2)}, u32[]{:S(2)}) collective-permute-start(bf16[64,1408]{1,0:T(8,128)(2,1)S(1)} %pad_maximum_fusion.2), channel_id=1, source_target_pairs={{0,2},{1,3},{2,0},{3,1},{4,6},{5,7},{6,4},{7,5},{8,10},{9,11},{10,... | collective-permute-start | bytes 540680 | tf_op jit(solution)/shard_map/ppermute | solution.py:300
  81.2 3.7 %copy-start.8 = (f32[64,1536]{1,0:T(8,128)S(1)}, f32[64,1536]{1,0:T(8,128)}, u32[]{:S(2)}) copy-start(f32[64,1536]{1,0:T(8,128)} %slice_dynamic-update-slice_fusion.5) | copy-start | bytes 1179652
  85.0 0.7 copy-start.9

commit v3 on v2

v3 whole, which is shorter than its diff:
```python
import math

import jax
import jax.numpy as jnp
from jax import lax
from jax.experimental import pallas as pl
from jax.experimental.pallas import tpu as pltpu
from jax.sharding import PartitionSpec as P

H = 8
HD = 64
HH = H // 2
HW = HH * HD
SCALE = HD ** (-0.5)
F32 = jnp.float32
BF16 = jnp.bfloat16
QUERY_BLOCK = 128
BIG_VMEM = 32 * 1024 * 1024
SMALL_VMEM = 12 * 1024 * 1024
ANY = pl.BlockSpec(memory_space=pl.ANY)
VMEM = pl.BlockSpec(memory_space=pltpu.VMEM)
SMEM = pl.BlockSpec(memory_space=pltpu.SMEM)
shaped = jax.ShapeDtypeStruct


def dot_nn(a, b):
    return lax.dot_general(a, b, (((1,), (0,)), ((), ())), preferred_element_type=F32)


def dot_nt(a, b):
    return lax.dot_general(a, b, (((1,), (1,)), ((), ())), preferred_element_type=F32)


def rms_parts(x):
    inverse_rms = lax.rsqrt(jnp.mean(x * x, -1, keepdims=True) + 1e-05)
    return inverse_rms, x * inverse_rms


def transposed(x):
    block = math.gcd(x.shape[1], 256)
    eye = (
        lax.broadcasted_iota(jnp.int32, (block, block), 0)
        == lax.broadcasted_iota(jnp.int32, (block, block), 1)
    ).astype(F32).astype(BF16)
    parts = [
        dot_nt(eye, x[:, at : at + block]).astype(BF16) for at in range(0, x.shape[1], block)
    ]
    return parts[0] if len(parts) == 1 else jnp.concatenate(parts, 0)


def head_pair(x):
    lane = lax.broadcasted_iota(jnp.int32, x.shape, 1)
    zero = jnp.zeros_like(x)
    return jnp.concatenate([jnp.where(lane < HD, x, zero), jnp.where(lane < HD, zero, x)], 0)


def pair_step(q2, g2, gt, k, v, kt, vt, mask_at, mask):
    count = gt.shape[1]
    scores = dot_nt(k, q2)
    tail = jnp.where(mask, scores[mask_at:], -1e30)
    scores = tail if mask_at == 0 else jnp.concatenate([scores[:mask_at], tail], 0)
    exponent = jnp.exp(scores - jnp.max(scores, 0, keepdims=True))
    probs = exponent * (1.0 / jnp.sum(exponent, 0, keepdims=True))
    weights = probs.astype(BF16)
    both = dot_nn(vt, weights)
    attended = jnp.concatenate([both[:HD, :count], both[HD:, count:]], 0).astype(BF16)
    product = gt.astype(F32) * attended.astype(F32)
    delta = jnp.concatenate(
        [jnp.sum(product[:HD], 0, keepdims=True), jnp.sum(product[HD:], 0, keepdims=True)], 1
    )
    score_grad = (probs * (dot_nt(v, g2) - delta)).astype(BF16)
    both = dot_nn(kt, score_grad)
    grad_q = (jnp.concatenate([both[:HD, :count], both[HD:, count:]], 0) * SCALE).astype(BF16)
    return attended, grad_q, dot_nn(score_grad, q2), dot_nn(weights, g2)


def qkv_copies(wqkv_ref, w_ref, sems, second):
    width = wqkv_ref.shape[0]
    return [
        pltpu.make_async_copy(
            wqkv_ref.at[:, pl.ds(i * width + second * HW, HW)],
            w_ref.at[:, pl.ds(i * HW, HW)],
            sems.at[i],
        )
        for i in range(3)
    ]


def weight_copies(wqkv_ref, wout_ref, w_ref, wo_ref, sems, second):
    out_rows = wout_ref.at[pl.ds(second * HW, HW), :]
    return [
        *qkv_copies(wqkv_ref, w_ref, sems, second),
        pltpu.make_async_copy(out_rows, wo_ref, sems.at[3]),
    ]


def project(hidden, cot, w_ref, wo_ref):
    projected = dot_nn(hidden, w_ref[...]).astype(BF16)
    q, k, v = [projected[:, i * HW : (i + 1) * HW] for i in range(3)]
    g = dot_nt(cot, wo_ref[...]).astype(BF16)
    return q * jnp.asarray(SCALE, BF16), k, v, g


def row_kernel(
    x_any, cot_any, gain_ref, wqkv_any, wout_any,
    qkv_ref, out_ref, grads_ref,
    x_ref, cot_ref, w_ref, wo_ref, dk_ref, dv_ref, sems,
):
    copies = [
        pltpu.make_async_copy(x_any, x_ref, sems.at[4]),
        *weight_copies(wqkv_any, wout_any, w_ref, wo_ref, sems, 0),
        pltpu.make_async_copy(cot_any, cot_ref, sems.at[5]),
    ]
    for copy in copies:
        copy.start()
    dk_ref[...] = jnp.zeros_like(dk_ref)
    dv_ref[...] = jnp.zeros_like(dv_ref)
    copies[0].wait()
    tokens = x_ref.shape[0]
    _, normed = rms_parts(x_ref[...].astype(F32))
    hidden = (normed * gain_ref[...]).astype(BF16)
    hidden_t = transposed(hidden)
    for copy in copies[1:]:
        copy.wait()
    cot = cot_ref[...]
    q, k, v, g = project(hidden, cot, w_ref, wo_ref)
    kt, vt, gt = transposed(k), transposed(v), transposed(g)
    step = math.gcd(tokens, QUERY_BLOCK)
    query = lax.broadcasted_iota(jnp.int32, (step, 2 * step), 1) % step
    mask = query >= lax.broadcasted_iota(jnp.int32, (step, 2 * step), 0)
    att_pairs, dq_pairs = [], []
    for pair in range(HH // 2):
        lanes = slice(pair * 2 * HD, (pair + 1) * 2 * HD)
        atts, dqs = [], []
        for start in range(0, tokens, step):
            rows, keys = slice(start, start + step), slice(0, start + step)
            attended, dq, dk, dv = pair_step(
                head_pair(q[rows, lanes]), head_pair(g[rows, lanes]), gt[lanes, rows],
                k[keys, lanes], v[keys, lanes], kt[lanes, keys], vt[lanes, keys], start, mask,
            )
            dk_ref[keys, lanes] += dk
            dv_ref[keys, lanes] += dv
            atts.append(attended)
            dqs.append(dq)
        att_pairs.append(jnp.concatenate(atts, 1))
        dq_pairs.append(jnp.concatenate(dqs, 1))
    grads_ref[:, :HW] = transposed(jnp.concatenate(dq_pairs, 0))
    grads_ref[:, HW : 2 * HW] = dk_ref[...].astype(BF16)
    grads_ref[:, 2 * HW :] = dv_ref[...].astype(BF16)
    qkv_ref[...] = dot_nn(hidden_t, grads_ref[...]).astype(BF16)
    out_ref[...] = dot_nn(jnp.concatenate(att_pairs, 0), cot).astype(BF16)


def column_part(moved_ref, gain_ref, w_ref, wo_ref, weight_waits, grads_ref):
    all_rows, _, share, width = moved_ref.shape
    group = math.gcd(share, 16)
    block = all_rows * group

    def gathered(which):
        pieces = []
        for start in range(0, share, group):
            piece = moved_ref[:, which, start : start + group, :]
            if group % 16 == 0:
                pieces.append(piece.reshape(block, width))
            else:
                pieces.append(piece.astype(F32).reshape(block, width).astype(BF16))
        return jnp.concatenate(pieces, 0)

    _, normed = rms_parts(gathered(0).astype(F32))
    hidden = (normed * gain_ref[...]).astype(BF16)
    hidden_t = transposed(hidden)
    cot = gathered(1)
    for copy in weight_waits:
        copy.wait()
    q, k, v, g = project(hidden, cot, w_ref, wo_ref)
    kt, vt, gt = transposed(k), transposed(v), transposed(g)
    query = lax.broadcasted_iota(jnp.int32, (block, 2 * block), 1) % block
    key = lax.broadcasted_iota(jnp.int32, (block, 2 * block), 0)
    mask = (query >= key) & (query % group == key % group)
    att_pairs, dq_pairs = [], []
    for pair in range(HH // 2):
        lanes = slice(pair * 2 * HD, (pair + 1) * 2 * HD)
        atts, dqs = [], []
        for start in range(0, all_rows * share, block):
            rows = slice(start, start + block)
            attended, dq, dk, dv = pair_step(
                head_pair(q[rows, lanes]), head_pair(g[rows, lanes]), gt[lanes, rows],
                k[rows, lanes], v[rows, lanes], kt[lanes, rows], vt[lanes, rows], 0, mask,
            )
            grads_ref[rows, HW + lanes.start : HW + lanes.stop] = dk.astype(BF16)
            grads_ref[rows, 2 * HW + lanes.start : 2 * HW + lanes.stop] = dv.astype(BF16)
            atts.append(attended)
            dqs.append(dq)
        att_pairs.append(jnp.concatenate(atts, 1))
        dq_pairs.append(jnp.concatenate(dqs, 1))
    grads_ref[:, :HW] = transposed(jnp.concatenate(dq_pairs, 0))
    term_qkv = dot_nn(hidden_t, grads_ref[...]).astype(BF16)
    term_out = dot_nn(jnp.concatenate(att_pairs, 0), cot).astype(BF16)
    return term_qkv, term_out


def column_kernel(
    moved_any, gain_ref, wqkv_any, wout_any, row_qkv_ref, row_out_ref,
    terms_ref, grads_ref,
    moved_ref, w_ref, wo_ref, sems,
):
    copy = pltpu.make_async_copy(moved_any, moved_ref, sems.at[4])
    weights = weight_copies(wqkv_any, wout_any, w_ref, wo_ref, sems, 1)
    for one in (copy, *weights):
        one.start()
    copy.wait()
    term_qkv, term_out = column_part(moved_ref, gain_ref, w_ref, wo_ref, weights, grads_ref)
    width = terms_ref.shape[0]
    for i in range(3):
        at = i * width
        terms_ref[:, at : at + HW] = row_qkv_ref[:, i * HW : (i + 1) * HW]
        terms_ref[:, at + HW : at + 2 * HW] = term_qkv[:, i * HW : (i + 1) * HW]
    terms_ref[:HW, 3 * width :] = row_out_ref[...]
    terms_ref[HW:, 3 * width :] = term_out


def column_chip_kernel(
    place_ref, x_any, cot_any, own_any,
    near_1, near_2, near_3, far_1, far_2, far_3,
    gain_ref, wqkv_any, wout_any, row_qkv_ref, row_out_ref,
    send_ref, keep_ref, grads_ref,
    moved_ref, w_ref, wo_ref, sems,
):
    chip, core = place_ref[0], place_ref[1]
    share = moved_ref.shape[2]
    at = pl.multiple_of((chip * 2 + core) * share, share)
    half = pl.multiple_of(core * share, share)
    me, other = chip * 2 + core, chip * 2 + 1 - core
    copies = [
        pltpu.make_async_copy(x_any.at[pl.ds(at, share), :], moved_ref.at[me, 0], sems.at[4]),
        pltpu.make_async_copy(cot_any.at[pl.ds(at, share), :], moved_ref.at[me, 1], sems.at[5]),
        pltpu.make_async_copy(own_any, moved_ref.at[other], sems.at[6]),
    ]
    for i, (near, far) in enumerate(((near_1, far_1), (near_2, far_2), (near_3, far_3))):
        there = 2 * (chip ^ (i + 1))
        for j, (piece, row) in enumerate(((near, there + core), (far, there + 1 - core))):
            copies.append(
                pltpu.make_async_copy(
                    piece.at[:, pl.ds(half, share), :], moved_ref.at[row], sems.at[7 + 2 * i + j]
                )
            )
    weights = weight_copies(wqkv_any, wout_any, w_ref, wo_ref, sems, 1)
    for copy in (*copies, *weights):
        copy.start()
    for copy in copies:
        copy.wait()
    term_qkv, term_out = column_part(moved_ref, gain_ref, w_ref, wo_ref, weights, grads_ref)
    width = moved_ref.shape[3]
    first = core == 0

    def split(piece, chips, lanes):
        parts = piece.reshape(chips.stop - chips.start, 2, share, piece.shape[1])
        even, odd = parts[:, 0], parts[:, 1]
        send_ref[chips, :, lanes] = jnp.where(first, odd, even)
        keep_ref[chips, :, lanes] = jnp.where(first, even, odd)

    chips = send_ref.shape[0]
    for i in range(3):
        lanes = slice(i * HW, (i + 1) * HW)
        at = i * width
        split(row_qkv_ref[:, lanes], slice(0, chips), slice(at, at + HW))
        split(term_qkv[:, lanes], slice(0, chips), slice(at + HW, at + 2 * HW))
    split(row_out_ref[...], slice(0, chips // 2), slice(3 * width, 4 * width))
    split(term_out, slice(chips // 2, chips), slice(3 * width, 4 * width))


def back_kernel(grads_ref, wqkv_any, back_ref, w_ref, sems):
    copies = qkv_copies(wqkv_any, w_ref, sems, 1)
    for copy in copies:
        copy.start()
    for copy in copies:
        copy.wait()
    grad_hidden = dot_nt(grads_ref[...], w_ref[...])
    all_rows, share, width = back_ref.shape
    group = math.gcd(share, 16)
    block = all_rows * group
    for i in range(share // group):
        piece = grad_hidden[i * block : (i + 1) * block].reshape(all_rows, group, width)
        back_ref[:, i * group : (i + 1) * group, :] = piece.astype(BF16)


def input_kernel(x_ref, cot_ref, gain_ref, grads_ref, wqkv_any, back_ref, grad_ref, w_ref, sems):
    copies = qkv_copies(wqkv_any, w_ref, sems, 0)
    for copy in copies:
        copy.start()
    inverse_rms, normed = rms_parts(x_ref[...].astype(F32))
    for copy in copies:
        copy.wait()
    grad_hidden = dot_nt(grads_ref[...], w_ref[...]) + back_ref[...].astype(F32)
    grad_normed = grad_hidden * gain_ref[...]
    projected = jnp.mean(grad_normed * normed, -1, keepdims=True)
    grad = inverse_rms * (grad_normed - normed * projected)
    grad_ref[...] = (cot_ref[...].astype(F32) + grad).astype(BF16)


def pack_kernel(place_ref, x_any, cot_any, own_ref, off_1, off_2, off_3, sems):
    chip, core = place_ref[0], place_ref[1]
    share = own_ref.shape[1]
    at = pl.multiple_of((chip * 2 + 1 - core) * share, share)
    copies = []
    for which, source in enumerate((x_any, cot_any)):
        copies.append(
            pltpu.make_async_copy(
                source.at[pl.ds(at, share), :], own_ref.at[which], sems.at[which]
            )
        )
        for i, target in enumerate((off_1, off_2, off_3)):
            there = pl.multiple_of((chip ^ (i + 1)) * 2 * share, 2 * share)
            copies.append(
                pltpu.make_async_copy(
                    source.at[pl.ds(there, 2 * share), :],
                    target.at[which],
                    sems.at[2 + 2 * i + which],
                )
            )
    for copy in copies:
        copy.start()
    for copy in copies:
        copy.wait()


def chip_sum_kernel(place_ref, keep_ref, got_ref, own_ref, off_1, off_2, off_3):
    chip = place_ref[0]
    for i, target in enumerate((own_ref, off_1, off_2, off_3)):
        there = chip ^ i
        total = keep_ref[there].astype(F32) + got_ref[there].astype(F32)
        target[...] = total.astype(target.dtype)


def layer_sum_kernel(place_ref, own_ref, got_1, got_2, got_3, send_ref, keep_ref):
    upper = place_ref[2] == 1
    total = own_ref[...] + (
        (got_1[...].astype(F32) + got_2[...].astype(F32)) + got_3[...].astype(F32)
    )
    half = total.shape[0] // 2
    low, high = total[:half], total[half:]
    send_ref[...] = jnp.where(upper, low, high).astype(BF16)
    keep_ref[...] = jnp.where(upper, high, low)


def add_kernel(kept_ref, got_ref, out_ref):
    out_ref[...] = (kept_ref[...].astype(F32) + got_ref[...].astype(F32)).astype(BF16)


def result_kernel(place_ref, held_ref, got_ref, wqkv_any, gain_ref, qkv_ref, out_ref, grad_ref, w_ref, sem):
    rows = qkv_ref.shape[0]
    at = pl.multiple_of((place_ref[0] * 2 + place_ref[1]) * rows, rows)
    copy = pltpu.make_async_copy(wqkv_any.at[pl.ds(at, rows), :], w_ref, sem)
    copy.start()
    upper = place_ref[2] == 1
    held, got = held_ref[...].astype(F32), got_ref[...].astype(F32)
    half = rows // 2
    low, high = jnp.where(upper, got, held), jnp.where(upper, held, got)
    cut = qkv_ref.shape[1]
    qkv_ref[:half], qkv_ref[half:] = low[:, :cut], high[:, :cut]
    out_ref[:half], out_ref[half:] = low[:, cut:], high[:, cut:]
    copy.wait()
    total = jnp.sum(qkv_ref[...] * w_ref[...].astype(F32), -1, keepdims=True)
    grad_ref[...] = total / gain_ref[...]


def call(kernel, name, ins, outs, scratch=(), flops=0, vmem=SMALL_VMEM, out_specs=None):
    outs = [shaped(*out) for out in outs]
    args = [array for _, array in ins]
    size = sum(math.prod(a.shape) * a.dtype.itemsize for a in (*args, *outs))
    return pl.pallas_call(
        kernel,
        out_shape=outs,
        in_specs=[spec for spec, _ in ins],
        out_specs=out_specs or [VMEM] * len(outs),
        scratch_shapes=scratch,
        name=name,
        cost_estimate=pl.CostEstimate(flops=flops, bytes_accessed=size, transcendentals=0),
        compiler_params=pltpu.CompilerParams(vmem_limit_bytes=vmem),
    )(*args)


def body(inputs, norm_gain, qkv_weight, out_weight, out_cotan):
    columns, width = inputs.shape[2:]
    n = lax.axis_size("seq")
    m = lax.axis_size("dp")
    share = columns // n
    row_share = width // n
    term_width = 4 * width
    x = inputs.reshape(columns, width)
    cot = out_cotan.reshape(columns, width)
    gain = norm_gain.reshape(1, width)
    chips = 4
    layered = n == 2 * chips and m == 4 and row_share == share
    here = lax.axis_index("seq")
    place = jnp.stack([here // 2, here % 2, lax.axis_index("dp") % 2]).astype(jnp.int32)
    weight_scratch = [
        pltpu.VMEM((width, 3 * HW), BF16),
        pltpu.VMEM((HW, width), BF16),
    ]
    small_scratch = [pltpu.VMEM((width, 3 * HW), BF16), pltpu.SemaphoreType.DMA((3,))]

    def swap(array, axis, bits):
        count = lax.axis_size(axis)
        return lax.ppermute(array, axis, [(i, i ^ bits) for i in range(count)])

    if layered:
        packed = call(
            pack_kernel,
            "pack_columns",
            [(SMEM, place), (ANY, x), (ANY, cot)],
            [((2, share, width), BF16)] + [((2, 2 * share, width), BF16)] * 3,
            [pltpu.SemaphoreType.DMA((8,))],
            out_specs=[ANY] * 4,
        )
        near_3 = swap(packed[3], "seq", 6)
        near_1 = swap(packed[1], "seq", 2)
        near_2 = swap(packed[2], "seq", 4)
        own = swap(packed[0], "seq", 1)
    else:
        outgoing = jnp.stack([x.reshape(n, share, width), cot.reshape(n, share, width)], 1)
        moved = lax.all_to_all(outgoing, "seq", split_axis=0, concat_axis=0, tiled=True)

    row_qkv, row_out, row_grads = call(
        row_kernel,
        "row_heads",
        [(ANY, x), (ANY, cot), (VMEM, gain), (ANY, qkv_weight), (ANY, out_weight)],
        [((width, 3 * HW), BF16), ((HW, width), BF16), ((columns, 3 * HW), BF16)],
        [
            pltpu.VMEM((columns, width), BF16),
            pltpu.VMEM((columns, width), BF16),
            *weight_scratch,
            pltpu.VMEM((columns, HW), F32),
            pltpu.VMEM((columns, HW), F32),
            pltpu.SemaphoreType.DMA((6,)),
        ],
        5_000_000_000,
        BIG_VMEM,
    )
    moved_scratch = pltpu.VMEM((n, 2, share, width), BF16)
    if layered:
        near_1, near_2, near_3, row_qkv = lax.optimization_barrier((near_1, near_2, near_3, row_qkv))
        far_3, far_1, far_2 = swap(near_3, "seq", 1), swap(near_1, "seq", 1), swap(near_2, "seq", 1)
    shared = [
        (VMEM, gain), (ANY, qkv_weight), (ANY, out_weight), (VMEM, row_qkv), (VMEM, row_out),
    ]
    if layered:
        send, keep, col_grads = call(
            column_chip_kernel,
            "column_heads",
            [
                (SMEM, place), (ANY, x), (ANY, cot), (ANY, own),
                (ANY, near_1), (ANY, near_2), (ANY, near_3),
                (ANY, far_1), (ANY, far_2), (ANY, far_3), *shared,
            ],
            [((chips, row_share, term_width), BF16)] * 2 + [((columns, 3 * HW), BF16)],
            [moved_scratch, *weight_scratch, pltpu.SemaphoreType.DMA((13,))],
            4_000_000_000,
            BIG_VMEM,
        )
        got = swap(send, "seq", 1)
    else:
        terms, col_grads = call(
            column_kernel,
            "column_heads",
            [(ANY, moved), *shared],
            [((width, term_width), BF16), ((columns, 3 * HW), BF16)],
            [moved_scratch, *weight_scratch, pltpu.SemaphoreType.DMA((5,))],
            4_000_000_000,
            BIG_VMEM,
        )
    if layered:
        owned, off_1, off_2, off_3 = call(
            chip_sum_kernel,
            "add_cores",
            [(SMEM, place), (VMEM, keep), (VMEM, got)],
            [((row_share, term_width), F32)] + [((row_share, term_width), BF16)] * 3,
        )
        got_3 = swap(off_3, "seq", 6)
        got_1 = swap(off_1, "seq", 2)
        got_2 = swap(off_2, "seq", 4)
        col_grads, owned = lax.optimization_barrier((col_grads, owned))
    (back,) = call(
        back_kernel,
        "column_grad_hidden",
        [(VMEM, col_grads), (ANY, qkv_weight)],
        [((n, share, width), BF16)],
        small_scratch,
        400_000_000,
    )
    if layered:
        back, owned = lax.optimization_barrier((back, owned))
    returned = lax.all_to_all(back, "seq", split_axis=0, concat_axis=0, tiled=True)
    half_rows = (row_share // 2, term_width)
    if layered:
        to_next, kept = call(
            layer_sum_kernel,
            "add_chips",
            [(SMEM, place), (VMEM, owned), (VMEM, got_1), (VMEM, got_2), (VMEM, got_3)],
            [(half_rows, BF16), (half_rows, F32)],
        )
        from_next = swap(to_next, "dp", 1)
        (pair_sum,) = call(
            add_kernel, "add_pair", [(VMEM, kept), (VMEM, from_next)], [(half_rows, BF16)]
        )
        from_far = swap(pair_sum, "dp", 2)
        (held,) = call(
            add_kernel, "add_pairs", [(VMEM, pair_sum), (VMEM, from_far)], [(half_rows, BF16)]
        )
        other = swap(held, "dp", 1)
    (input_grad,) = call(
        input_kernel,
        "input_grad",
        [
            (VMEM, x), (VMEM, cot), (VMEM, gain), (VMEM, row_grads), (ANY, qkv_weight),
            (VMEM, returned.reshape(columns, width)),
        ],
        [((columns, width), BF16)],
        small_scratch,
        400_000_000,
    )
    own_gain = lax.dynamic_slice_in_dim(norm_gain, here * row_share, row_share, 0)
    if layered:
        sum_qkv, sum_out, sum_gain = call(
            result_kernel,
            "result",
            [
                (SMEM, place), (VMEM, held), (VMEM, other), (ANY, qkv_weight),
                (VMEM, own_gain.reshape(row_share, 1)),
            ],
            [((row_share, 3 * width), F32), ((row_share, width), F32), ((row_share, 1), F32)],
            [pltpu.VMEM((row_share, 3 * width), BF16), pltpu.SemaphoreType.DMA],
        )
        sum_gain = sum_gain.reshape(row_share)
    else:
        terms = lax.all_to_all(
            terms.reshape(n, row_share, term_width), "seq", split_axis=0, concat_axis=0, tiled=True
        )
        total = jnp.sum(terms.astype(F32), 0)
        for step in range(m.bit_length() - 1):
            sent = total.astype(BF16)
            total = sent.astype(F32) + swap(sent, "dp", 1 << step).astype(F32)
        sum_qkv, sum_out = total[:, : 3 * width], total[:, 3 * width :]
        own_weight = lax.dynamic_slice_in_dim(qkv_weight, here * row_share, row_share, 0)
        sum_gain = jnp.sum(sum_qkv * own_weight.astype(F32), -1) / own_gain
    return (input_grad.reshape(inputs.shape), sum_qkv, sum_out, sum_gain)


def solution(mesh):
    return jax.shard_map(
        body,
        mesh=mesh,
        in_specs=(P("dp", "seq", None, None), P(), P(), P(), P("dp", "seq", None, None)),
        out_specs=(P("dp", "seq", None, None), P("seq", None), P("seq", None), P("seq")),
        check_vma=False,
    )
```

time: 86.2 us -> 78.4 us (0.910)
  waiting for transfers between devices: 30 us -> 21.5 us
  Pallas kernels: 16.5 us -> 24.8 us
  starting transfers between devices: 25.9 us -> 18.3 us
  other arithmetic: 6.48 us -> 0.7 us
  local copies, waits for them, and re-layouts: 5.93 us -> 11.4 us
    all_to_all x3 -> x0, waiting for transfers between devices: 19.6 us -> none  [the longest x1 10.6 us: body(): lax.all_to_all(col_terms.reshape(n, row_share, term_width), 'seq', split_...]
    ppermute x4 -> x14, waiting for transfers between devices: 4.8 us -> 21.5 us  [swap(): return lax.ppermute(array, axis, [(i, i ^ bits) for i in range(count)])]
    all_to_all x3 -> x0, starting transfers between devices: 13.8 us -> none  [the longest x1 5.31 us: body(): lax.all_to_all(outgoing, 'seq', split_axis=0, concat_axis=0, tiled=True)]
    pallas_call x3 -> x10, Pallas kernels: 16.5 us -> 24.8 us  [call(): pl.pallas_call(kernel, out_shape=outs, in_specs=[spec for spec, _ in ins]...]
    unnamed x25 -> x30, local copies, waits for them, and re-layouts: 5.21 us -> 11.2 us
    all_to_all x1, waiting for transfers between devices: 5.63 us -> 0.01 us  [body(): lax.all_to_all(back, 'seq', split_axis=0, concat_axis=0, tiled=True)]
    ppermute x4 -> x14, starting transfers between devices: 8.61 us -> 14 us  [swap(): return lax.ppermute(array, axis, [(i, i ^ bits) for i in range(count)])]
    reduce_sum x2 -> x0, other arithmetic: 2.83 us -> none  [the longest x1 1.59 us: body(): col_sum = jnp.sum(col_terms.astype(F32), 0)]
  transfers between devices with their start and end apart: 8 -> 15, of which waited for: 7 -> 6; matrix products, arithmetic and copies ran while one was open for 5% -> 0% of each run, Pallas kernels for 19% -> 16%
where the time goes in v3:
time: 78.4 us; the launch traced here: 77.5 us
  Pallas kernels  24.8 us (32%)
  waiting for transfers between devices  21.5 us (27%)
  starting transfers between devices  18.3 us (23%)
  local copies, waits for them, and re-layouts  11.4 us (15%)
  between operations  0.82 us (1%)
    pallas_call x10, Pallas kernels, call(): pl.pallas_call(kernel, out_shape=outs, in_specs=[spec for spec, _ in ins]...  24.8 us
    ppermute x14, waiting for transfers between devices, swap(): return lax.ppermute(array, axis, [(i, i ^ bits) for i in range(count)])  21.5 us
    ppermute x14, starting transfers between devices, swap(): return lax.ppermute(array, axis, [(i, i ^ bits) for i in range(count)])  14 us
    unnamed x30, local copies, waits for them, and re-layouts  11.2 us
    all_to_all x1, starting transfers between devices, body(): lax.all_to_all(back, 'seq', split_axis=0, concat_axis=0, tiled=True)  4.31 us
  transfers between devices with their start and end apart: 15, of which 6 were waited for; matrix products, arithmetic and copies ran while one was open for 0% of the time, Pallas kernels for 16%

profile of v3, /device:TPU:0, one launch (start us, length us, event | category | flops | bytes accessed | tf_op | source)
XLA Modules:
  0.0 77.5 jit_solution(13676338432064532471)
XLA Ops:
  0.7 0.1 pad_add_fusion.place_ref
  0.7 1.0 %copy-done.2 = bf16[1,1,512,512]{3,2,1,0:T(8,128)(2,1)S(1)} copy-done((bf16[1,1,512,512]{3,2,1,0:T(8,128)(2,1)S(1)}, bf16[1,1,512,512]{3,2,1,0:T(8,128)(2,1)}, u32[]{:S(2)}) %copy-start.2) | copy-done | bytes 524312
  1.8 1.0 %copy-done.5 = bf16[1,1,512,512]{3,2,1,0:T(8,128)(2,1)S(1)} copy-done((bf16[1,1,512,512]{3,2,1,0:T(8,128)(2,1)S(1)}, bf16[1,1,512,512]{3,2,1,0:T(8,128)(2,1)}, u32[]{:S(2)}) %copy-start.5) | copy-done | bytes 524312
  2.8 1.8 %pack_columns.1 = (bf16[2,64,512]{2,1,0:T(8,128)(2,1)S(1)}, bf16[2,128,512]{2,1,0:T(8,128)(2,1)S(1)}, bf16[2,128,512]{2,1,0:T(8,128)(2,1)S(1)}, bf16[2,128,512]{2,1,0:T(8,128)(2,1)S(1)}) custom-call(s32[3]{0:T(128)S(1)} %pad_add_fusion.place_ref, bf16[512,512]{1,0:T(8,128)(2,1)S(1)} %bitcast.11, bf16[512,512]{1,0:T(8,128)(2,1)S(1)} %bitcast.15), custom_call_target="tpu_custom_call" | custom-call | bytes 1966092 | tf_op jit(solution)/shard_map/pack_columns/pallas_call | solution.py:371
  4.6 3.0 %collective-permute-start.1 = (bf16[2,128,512]{2,1,0:T(8,128)(2,1)S(1)}, bf16[2,128,512]{2,1,0:T(8,128)(2,1)S(1)}, u32[]{:S(2)}, u32[]{:S(2)}) collective-permute-start(bf16[2,128,512]{2,1,0:T(8,128)(2,1)S(1)} %get-tuple-element.33), channel_id=1, source_target_pairs={{0,8},{4,12},{8,0},{12,4},{16,24},{20,28},{24,16},{28,20},{1,9},{5... | collective-permute-start | bytes 786440 | tf_op jit(solution)/shard_map/ppermute | solution.py:405
  7.6 1.5 %collective-permute-start.2 = (bf16[2,128,512]{2,1,0:T(8,128)(2,1)S(1)}, bf16[2,128,512]{2,1,0:T(8,128)(2,1)S(1)}, u32[]{:S(2)}, u32[]{:S(2)}) collective-permute-start(bf16[2,128,512]{2,1,0:T(8,128)(2,1)S(1)} %get-tuple-element.34), channel_id=1, source_target_pairs={{0,16},{4,20},{8,24},{12,28},{16,0},{20,4},{24,8},{28,12},{1,17},{... | collective-permute-start | bytes 786440 | tf_op jit(solution)/shard_map/ppermute | solution.py:405
  9.2 0.0 collective-permute-start.3
  9.2 1.4 %copy-done = bf16[512,1536]{1,0:T(8,128)(2,1)S(1)} copy-done((bf16[512,1536]{1,0:T(8,128)(2,1)S(1)}, bf16[512,1536]{1,0:T(8,128)(2,1)}, u32[]{:S(2)}) %copy-start) | copy-done | bytes 1572888
  10.6 1.0 %copy-done.3 = bf16[1,1,512,512]{3,2,1,0:T(8,128)(2,1)S(1)} copy-done((bf16[1,1,512,512]{3,2,1,0:T(8,128)(2,1)S(1)}, bf16[1,1,512,512]{3,2,1,0:T(8,128)(2,1)}, u32[]{:S(2)}) %copy-start.3) | copy-done | bytes 524312
  11.6 1.0 %copy-done.6 = bf16[1,1,512,512]{3,2,1,0:T(8,128)(2,1)S(1)} copy-done((bf16[1,1,512,512]{3,2,1,0:T(8,128)(2,1)S(1)}, bf16[1,1,512,512]{3,2,1,0:T(8,128)(2,1)}, u32[]{:S(2)}) %copy-start.6) | copy-done | bytes 524312
  12.7 0.7 copy-done.12
  13.4 1.0 %copy-done.14 = bf16[512,512]{1,0:T(8,128)(2,1)S(1)} copy-done((bf16[512,512]{1,0:T(8,128)(2,1)S(1)}, bf16[512,512]{1,0:T(8,128)(2,1)}, u32[]{:S(2)}) %copy-start.14) | copy-done | bytes 524312
  14.4 7.8 %row_heads.1 = (bf16[512,768]{1,0:T(8,128)(2,1)S(1)}, bf16[256,512]{1,0:T(8,128)(2,1)S(1)}, bf16[512,768]{1,0:T(8,128)(2,1)S(1)}) custom-call(bf16[512,512]{1,0:T(8,128)(2,1)S(1)} %bitcast.12, bf16[512,512]{1,0:T(8,128)(2,1)S(1)} %bitcast.16, f32[1,512]{1,0:T(1,128)S(1)} %bitcast.19, bf16[512,1536]{1,0:T(8,128)(2,1)S(1)} %copy-done, ...), custom_call_target="tpu_custom_call" | custom-call | flops 5000000000 | bytes 4982784 | tf_op jit(solution)/shard_map/row_heads/pallas_call | solution.py:371
  22.2 0.9 %copy-done.8 = bf16[512,768]{1,0:T(8,128)(2,1)} copy-done((bf16[512,768]{1,0:T(8,128)(2,1)}, bf16[512,768]{1,0:T(8,128)(2,1)S(1)}, u32[]{:S(2)}) %copy-start.8) | copy-done | bytes 786456
  23.1 0.1 collective-permute-start.4
  23.2 0.5 collective-permute-start.5
  23.7 0.1 collective-permute-start.6
  23.8 0.4 collective-permute-start
  24.2 1.5 %collective-permute-done.own_any = bf16[2,64,512]{2,1,0:T(8,128)(2,1)S(1)} collective-permute-done((bf16[2,64,512]{2,1,0:T(8,128)(2,1)S(1)}, bf16[2,64,512]{2,1,0:T(8,128)(2,1)S(1)}, u32[]{:S(2)}, u32[]{:S(2)}) %collective-permute-start) | collective-permute-done | bytes 131104 | tf_op jit(solution)/shard_map/ppermute | solution.py:405
  25.7 7.4 %column_heads.1 = (bf16[4,64,2048]{2,1,0:T(8,128)(2,1)S(1)}, bf16[4,64,2048]{2,1,0:T(8,128)(2,1)S(1)}, bf16[512,768]{1,0:T(8,128)(2,1)S(1)}) custom-call(s32[3]{0:T(128)S(1)} %pad_add_fusion.place_ref, bf16[512,512]{1,0:T(8,128)(2,1)S(1)} %bitcast.13, bf16[512,512]{1,0:T(8,128)(2,1)S(1)} %bitcast.17, bf16[2,64,512]{2,1,0:T(8,128)(2,1)S(1)} %collective-permute-done.own_any, ...), custom_call_target="tpu_custom_call" | custom-call | flops 4000000000 | bytes 8783884 | tf_op jit(solution)/shard_map/column_heads/pallas_call | solution.py:371
  33.1 0.2 collective-permute-start.7
  33.3 2.5 %collective-permute-done.7.got_ref = bf16[4,64,2048]{2,1,0:T(8,128)(2,1)S(1)} collective-permute-done((bf16[4,64,2048]{2,1,0:T(8,128)(2,1)S(1)}, bf16[4,64,2048]{2,1,0:T(8,128)(2,1)S(1)}, u32[]{:S(2)}, u32[]{:S(2)}) %collective-permute-start.7) | collective-permute-done | bytes 1048608 | tf_op jit(solution)/shard_map/ppermute | solution.py:405
  35.8 1.5 %add_cores.1 = (f32[64,2048]{1,0:T(8,128)S(1)}, bf16[64,2048]{1,0:T(8,128)(2,1)}, bf16[64,2048]{1,0:T(8,128)(2,1)}, bf16[64,2048]{1,0:T(8,128)(2,1)}) custom-call(s32[3]{0:T(128)S(1)} %pad_add_fusion.place_ref, bf16[4,64,2048]{2,1,0:T(8,128)(2,1)S(1)} %get-tuple-element.43.keep_ref, bf16[4,64,2048]{2,1,0:T(8,128)(2,1)S(1)} %collective-permute-done.7.got_ref), custom_call_target="tpu_custom_call" | custom-call | bytes 3407884 | tf_op jit(solution)/shard_map/add_cores/pallas_call | solution.py:371
  37.3 0.8 %copy-done.10 = f32[64,2048]{1,0:T(8,128)} copy-done((f32[64,2048]{1,0:T(8,128)}, f32[64,2048]{1,0:T(8,128)S(1)}, u32[]{:S(2)}) %copy-start.10) | copy-done | bytes 524312
  38.2 1.9 %collective-permute-start.8 = (bf16[64,2048]{1,0:T(8,128)(2,1)}, bf16[64,2048]{1,0:T(8,128)(2,1)S(1)}, u32[]{:S(2)}, u32[]{:S(2)}) collective-permute-start(bf16[64,2048]{1,0:T(8,128)(2,1)} %get-tuple-element.50), channel_id=1, source_target_pairs={{0,8},{4,12},{8,0},{12,4},{16,24},{20,28},{24,16},{28,20},{1,9},{5... | collective-permute-start | bytes 786440 | tf_op jit(solution)/shard_map/ppermute | solution.py:405
  40.1 1.5 %collective-permute-start.9 = (bf16[64,2048]{1,0:T(8,128)(2,1)}, bf16[64,2048]{1,0:T(8,128)(2,1)}, u32[]{:S(2)}, u32[]{:S(2)}) collective-permute-start(bf16[64,2048]{1,0:T(8,128)(2,1)} %get-tuple-element.51), channel_id=1, source_target_pairs={{0,16},{4,20},{8,24},{12,28},{16,0},{20,4},{24,8},{28,12},{1,17},{... | collective-permute-start | bytes 786440 | tf_op jit(solution)/shard_map/ppermute | solution.py:405
  41.6 0.0 collective-permute-start.10
  41.6 1.5 %column_grad_hidden.1 = bf16[8,64,512]{2,1,0:T(8,128)(2,1)} custom-call(bf16[512,768]{1,0:T(8,128)(2,1)S(1)} %get-tuple-element.46.grads_ref, bf16[512,1536]{1,0:T(8,128)(2,1)S(1)} %copy-done), custom_call_target="tpu_custom_call" | custom-call | flops 400000000 | bytes 2883584 | tf_op jit(solution)/shard_map/column_grad_hidden/pallas_call | solution.py:371
  43.1 0.0 copy-start.1
  43.2 0.0 copy-start.4
  43.2 0.0 copy-start.7
  43.2 4.3 %all-to-all-start = ((bf16[8,64,512]{2,1,0:T(8,128)(2,1)}), bf16[8,64,512]{2,1,0:T(8,128)(2,1)S(1)}, u32[]{:S(2)}, u32[]{:S(2)}) async-start(bf16[8,64,512]{2,1,0:T(8,128)(2,1)} %column_grad_hidden.1), calls=%async_computation | async-start | bytes 1048576 | tf_op jit(solution)/shard_map/all_to_all | solution.py:493
  47.5 0.0 collective-permute-done.8.got_1
  47.5 8.0 %collective-permute-done.9.got_2 = bf16[64,2048]{1,0:T(8,128)(2,1)} collective-permute-done((bf16[64,2048]{1,0:T(8,128)(2,1)}, bf16[64,2048]{1,0:T(8,128)(2,1)}, u32[]{:S(2)}, u32[]{:S(2)}) %collective-permute-start.9) | collective-permute-done | bytes 262176 | tf_op jit(solution)/shard_map/ppermute | solution.py:405
  55.5 1.0 %copy-done.11 = f32[64,2048]{1,0:T(8,128)S(1)} copy-done((f32[64,2048]{1,0:T(8,128)S(1)}, f32[64,2048]{1,0:T(8,128)}, u32[]{:S(2)}) %copy-start.11) | copy-done | bytes 524312
  56.6 1.2 %add_chips.1 = (bf16[32,2048]{1,0:T(8,128)(2,1)S(1)}, f32[32,2048]{1,0:T(8,128)S(1)}) custom-call(s32[3]{0:T(128)S(1)} %pad_add_fusion.place_ref, f32[64,2048]{1,0:T(8,128)S(1)} %copy-done.11, bf16[64,2048]{1,0:T(8,128)(2,1)S(1)} %collective-permute-done.8.got_1, bf16[64,2048]{1,0:T(8,128)(2,1)} %collective-permute-done.9.got_2, ...), custom_call_target="tpu_custom_call" | custom-call | bytes 1703948 | tf_op jit(solution)/shard_map/add_chips/pallas_call | solution.py:371
  57.8 1.4 %collective-permute-start.11 = (bf16[32,2048]{1,0:T(8,128)(2,1)S(1)}, bf16[32,2048]{1,0:T(8,128)(2,1)S(1)}, u32[]{:S(2)}, u32[]{:S(2)}) collective-permute-start(bf16[32,2048]{1,0:T(8,128)(2,1)S(1)} %get-tuple-element.54), channel_id=1, source_target_pairs={{0,1},{1,0},{2,3},{3,2},{4,5},{5,4},{6,7},{7,6},{8,9},{9,8},{10,11... | collective-permute-start | bytes 393224 | tf_op jit(solution)/shard_map/ppermute | solution.py:405
  59.2 3.6 %collective-permute-done.11.got_ref = bf16[32,2048]{1,0:T(8,128)(2,1)S(1)} collective-permute-done((bf16[32,2048]{1,0:T(8,128)(2,1)S(1)}, bf16[32,2048]{1,0:T(8,128)(2,1)S(1)}, u32[]{:S(2)}, u32[]{:S(2)}) %collective-permute-start.11) | collective-permute-done | bytes 131104 | tf_op jit(solution)/shard_map/ppermute | solution.py:405
  62.8 2.8 %collective-permute-start.12 = (bf16[32,2048]{1,0:T(8,128)(2,1)S(1)}, bf16[32,2048]{1,0:T(8,128)(2,1)S(1)}, u32[]{:S(2)}, u32[]{:S(2)}) collective-permute-start(bf16[32,2048]{1,0:T(8,128)(2,1)S(1)} %add_pair.1.kept_ref), channel_id=1, source_target_pairs={{0,2},{1,3},{2,0},{3,1},{4,6},{5,7},{6,4},{7,5},{8,10},{9,11},{10,... | collective-permute-start | bytes 393224 | tf_op jit(solution)/shard_map/ppermute | solution.py:405
  65.7 4.5 %collective-permute-done.12.got_ref = bf16[32,2048]{1,0:T(8,128)(2,1)S(1)} collective-permute-done((bf16[32,2048]{1,0:T(8,128)(2,1)S(1)}, bf16[32,2048]{1,0:T(8,128)(2,1)S(1)}, u32[]{:S(2)}, u32[]{:S(2)}) %collective-permute-start.12) | collective-permute-done | bytes 131104 | tf_op jit(solution)/shard_map/ppermute | solution.py:405
  70.2 0.5 collective-permute-start.13
  70.7 0.1 dynamic-slice_bitcast_fusion
  70.8 0.1 copy.10.gain_ref
  70.9 1.1 %copy-done.9 = bf16[512,768]{1,0:T(8,128)(2,1)S(1)} copy-done((bf16[512,768]{1,0:T(8,128)(2,1)S(1)}, bf16[512,768]{1,0:T(8,128)(2,1)}, u32[]{:S(2)}) %copy-start.9) | copy-done | bytes 786456
  72.0 1.9 %input_grad.1 = bf16[512,512]{1,0:T(8,128)(2,1)} custom-call(bf16[512,512]{1,0:T(8,128)(2,1)S(1)} %bitcast.14, bf16[512,512]{1,0:T(8,128)(2,1)S(1)} %bitcast.18, f32[1,512]{1,0:T(1,128)S(1)} %bitcast.21, bf16[512,768]{1,0:T(8,128)(2,1)S(1)} %copy-done.9, bf16[512,1536]{1,0:T(8,128)(2,1)S(1)} %copy-done.1, bf16[512,512]{1,0:T(8,128)(2,1)S(1)} %bitcast.10), custom_call_target="tpu_custom_call" | custom-call | flops 400000000 | bytes 4458496 | tf_op jit(solution)/shard_map/input_grad/pallas_call | solution.py:371
  74.0 1.3 %collective-permute-done.13.got_ref = bf16[32,2048]{1,0:T(8,128)(2,1)S(1)} collective-permute-done((bf16[32,2048]{1,0:T(8,128)(2,1)S(1)}, bf16[32,2048]{1,0:T(8,128)(2,1)S(1)}, u32[]{:S(2)}, u32[]{:S(2)}) %collective-permute-start.13) | collective-permute-done | bytes 131104 | tf_op jit(solution)/shard_map/ppermute | solution.py:405
  75.2 1.6 %result.1 = (f32[64,1536]{1,0:T(8,128)}, f32[64,512]{1,0:T(8,128)}, f32[64,1]{1,0:T(8,128)S(1)}) custom-call(s32[3]{0:T(128)S(1)} %pad_add_fusion.place_ref, bf16[32,2048]{1,0:T(8,128)(2,1)S(1)} %add_pairs.1.held_ref, bf16[32,2048]{1,0:T(8,128)(2,1)S(1)} %collective-permute-done.13.got_ref, bf16[512,1536]{1,0:T(8,128)(2,1)S(1)} %copy-done.1, ...), custom_call_target="tpu_custom_call" | custom-call | bytes 2359820 | tf_op jit(solution)/shard_map/result/pallas_call | solution.py:371
  76.9 0.6 reduce
  (26 shorter events, 0.1 us)
Async XLA Ops:
  0.7 1.0 %copy-start.2 = (bf16[1,1,512,512]{3,2,1,0:T(8,128)(2,1)S(1)}, bf16[1,1,512,512]{3,2,1,0:T(8,128)(2,1)}, u32[]{:S(2)}) copy-start(bf16[1,1,512,512]{3,2,1,0:T(8,128)(2,1)} %param.5) | copy-start | bytes 1572868
  1.8 1.0 %copy-start.5 = (bf16[1,1,512,512]{3,2,1,0:T(8,128)(2,1)S(1)}, bf16[1,1,512,512]{3,2,1,0:T(8,128)(2,1)}, u32[]{:S(2)}) copy-start(bf16[1,1,512,512]{3,2,1,0:T(8,128)(2,1)} %param.9) | copy-start | bytes 1572868
  4.6 18.5 %collective-permute-start.1 = (bf16[2,128,512]{2,1,0:T(8,128)(2,1)S(1)}, bf16[2,128,512]{2,1,0:T(8,128)(2,1)S(1)}, u32[]{:S(2)}, u32[]{:S(2)}) collective-permute-start(bf16[2,128,512]{2,1,0:T(8,128)(2,1)S(1)} %get-tuple-element.33), channel_id=1, source_target_pairs={{0,8},{4,12},{8,0},{12,4},{16,24},{20,28},{24,16},{28,20},{1,9},{5... | collective-permute-start | bytes 786440 | tf_op jit(solution)/shard_map/ppermute | solution.py:405
  7.6 15.5 %collective-permute-start.2 = (bf16[2,128,512]{2,1,0:T(8,128)(2,1)S(1)}, bf16[2,128,512]{2,1,0:T(8,128)(2,1)S(1)}, u32[]{:S(2)}, u32[]{:S(2)}) collective-permute-start(bf16[2,128,512]{2,1,0:T(8,128)(2,1)S(1)} %get-tuple-element.34), channel_id=1, source_target_pairs={{0,16},{4,20},{8,24},{12,28},{16,0},{20,4},{24,8},{28,12},{1,17},{... | collective-permute-start | bytes 786440 | tf_op jit(solution)/shard_map/ppermute | solution.py:405
  9.2 14.0 %collective-permute-start.3 = (bf16[2,128,512]{2,1,0:T(8,128)(2,1)S(1)}, bf16[2,128,512]{2,1,0:T(8,128)(2,1)S(1)}, u32[]{:S(2)}, u32[]{:S(2)}) collective-permute-start(bf16[2,128,512]{2,1,0:T(8,128)(2,1)S(1)} %get-tuple-element.35), channel_id=1, source_target_pairs={{0,24},{4,28},{8,16},{12,20},{16,8},{20,12},{24,0},{28,4},{1,25},{... | collective-permute-start | bytes 786440 | tf_op jit(solution)/shard_map/ppermute | solution.py:405
  9.2 1.4 %copy-start = (bf16[512,1536]{1,0:T(8,128)(2,1)S(1)}, bf16[512,1536]{1,0:T(8,128)(2,1)}, u32[]{:S(2)}) copy-start(bf16[512,1536]{1,0:T(8,128)(2,1)} %wqkv_any.9) | copy-start | bytes 4718596
  10.6 1.0 %copy-start.3 = (bf16[1,1,512,512]{3,2,1,0:T(8,128)(2,1)S(1)}, bf16[1,1,512,512]{3,2,1,0:T(8,128)(2,1)}, u32[]{:S(2)}) copy-start(bf16[1,1,512,512]{3,2,1,0:T(8,128)(2,1)} %param.5) | copy-start | bytes 1572868
  11.6 1.0 %copy-start.6 = (bf16[1,1,512,512]{3,2,1,0:T(8,128)(2,1)S(1)}, bf16[1,1,512,512]{3,2,1,0:T(8,128)(2,1)}, u32[]{:S(2)}) copy-start(bf16[1,1,512,512]{3,2,1,0:T(8,128)(2,1)} %param.9) | copy-start | bytes 1572868
  12.7 0.7 copy-start.12
  13.4 1.0 %copy-start.14 = (bf16[512,512]{1,0:T(8,128)(2,1)S(1)}, bf16[512,512]{1,0:T(8,128)(2,1)}, u32[]{:S(2)}) copy-start(bf16[512,512]{1,0:T(8,128)(2,1)} %wout_any.3) | copy-start | bytes 1572868
  22.2 0.9 %copy-start.8 = (bf16[512,768]{1,0:T(8,128)(2,1)}, bf16[512,768]{1,0:T(8,128)(2,1)S(1)}, u32[]{:S(2)}) copy-start(bf16[512,768]{1,0:T(8,128)(2,1)S(1)} %get-tuple-element.31.grads_ref) | copy-start | bytes 2359300
  23.1 2.5 %collective-permute-start.4 = (bf16[2,128,512]{2,1,0:T(8,128)(2,1)S(1)}, bf16[2,128,512]{2,1,0:T(8,128)(2,1)S(1)}, u32[]{:S(2)}, u32[]{:S(2)}) collective-permute-start(bf16[2,128,512]{2,1,0:T(8,128)(2,1)S(1)} %collective-permute-done.1.near_1), channel_id=1, source_target_pairs={{0,4},{4,0},{8,12},{12,8},{16,20},{20,16},{24,28},{28,24},{1,5},{5... | collective-permute-start | bytes 786440 | tf_op jit(solution)/shard_map/ppermute | solution.py:405
  23.2 2.5 %collective-permute-start.5 = (bf16[2,128,512]{2,1,0:T(8,128)(2,1)S(1)}, bf16[2,128,512]{2,1,0:T(8,128)(2,1)S(1)}, u32[]{:S(2)}, u32[]{:S(2)}) collective-permute-start(bf16[2,128,512]{2,1,0:T(8,128)(2,1)S(1)} %collective-permute-done.2.near_2), channel_id=1, source_target_pairs={{0,4},{4,0},{8,12},{12,8},{16,20},{20,16},{24,28},{28,24},{1,5},{5... | collective-permute-start | bytes 786440 | tf_op jit(solution)/shard_map/ppermute | solution.py:405
  23.7 2.0 %collective-permute-start.6 = (bf16[2,128,512]{2,1,0:T(8,128)(2,1)S(1)}, bf16[2,128,512]{2,1,0:T(8,128)(2,1)S(1)}, u32[]{:S(2)}, u32[]{:S(2)}) collective-permute-start(bf16[2,128,512]{2,1,0:T(8,128)(2,1)S(1)} %collective-permute-done.3.near_3), channel_id=1, source_target_pairs={{0,4},{4,0},{8,12},{12,8},{16,20},{20,16},{24,28},{28,24},{1,5},{5... | collective-permute-start | bytes 786440 | tf_op jit(solution)/shard_map/ppermute | solution.py:405
  23.8 1.9 %collective-permute-start = (bf16[2,64,512]{2,1,0:T(8,128)(2,1)S(1)}, bf16[2,64,512]{2,1,0:T(8,128)(2,1)S(1)}, u32[]{:S(2)}, u32[]{:S(2)}) collective-permute-start(bf16[2,64,512]{2,1,0:T(8,128)(2,1)S(1)} %get-tuple-element.32), channel_id=1, source_target_pairs={{0,4},{4,0},{8,12},{12,8},{16,20},{20,16},{24,28},{28,24},{1,5},{5... | collective-permute-start | bytes 393224 | tf_op jit(solution)/shard_map/ppermute | solution.py:405
  33.1 2.7 %collective-permute-start.7 = (bf16[4,64,2048]{2,1,0:T(8,128)(2,1)S(1)}, bf16[4,64,2048]{2,1,0:T(8,128)(2,1)S(1)}, u32[]{:S(2)}, u32[]{:S(2)}) collective-permute-start(bf16[4,64,2048]{2,1,0:T(8,128)(2,1)S(1)} %get-tuple-element.44), channel_id=1, source_target_pairs={{0,4},{4,0},{8,12},{12,8},{16,20},{20,16},{24,28},{28,24},{1,5},{5... | collective-permute-start | bytes 3145736 | tf_op jit(solution)/shard_map/ppermute | solution.py:405
  37.3 0.8 %copy-start.10 = (f32[64,2048]{1,0:T(8,128)}, f32[64,2048]{1,0:T(8,128)S(1)}, u32[]{:S(2)}) copy-start(f32[64,2048]{1,0:T(8,128)S(1)} %get-tuple-element.49.own_ref) | copy-start | bytes 1572868
  38.2 9.3 %collective-permute-start.8 = (bf16[64,2048]{1,0:T(8,128)(2,1)}, bf16[64,2048]{1,0:T(8,128)(2,1)S(1)}, u32[]{:S(2)}, u32[]{:S(2)}) collective-permute-start(bf16[64,2048]{1,0:T(8,128)(2,1)} %get-tuple-element.50), channel_id=1, source_target_pairs={{0,8},{4,12},{8,0},{12,4},{16,24},{20,28},{24,16},{28,20},{1,9},{5... | collective-permute-start | bytes 786440 | tf_op jit(solution)/shard_map/ppermute | solution.py:405
  40.1 15.4 %collective-permute-start.9 = (bf16[64,2048]{1,0:T(8,128)(2,1)}, bf16[64,2048]{1,0:T(8,128)(2,1)}, u32[]{:S(2)}, u32[]{:S(2)}) collective-permute-start(bf16[64,2048]{1,0:T(8,128)(2,1)} %get-tuple-element.51), channel_id=1, source_target_pairs={{0,16},{4,20},{8,24},{12,28},{16,0},{20,4},{24,8},{28,12},{1,17},{... | collective-permute-start | bytes 786440 | tf_op jit(solution)/shard_map/ppermute | solution.py:405
  41.6 13.9 %collective-permute-start.10 = (bf16[64,2048]{1,0:T(8,128)(2,1)}, bf16[64,2048]{1,0:T(8,128)(2,1)}, u32[]{:S(2)}, u32[]{:S(2)}) collective-permute-start(bf16[64,2048]{1,0:T(8,128)(2,1)} %get-tuple-element.52), channel_id=1, source_target_pairs={{0,24},{4,28},{8,16},{12,20},{16,8},{20,12},{24,0},{28,4},{1,25},{... | collective-permute-start | bytes 786440 | tf_op jit(solution)/shard_map/ppermute | solution.py:405
  41.6 29.1 %copy-start.13 = (f32[512]{0:T(512)S(1)}, f32[512]{0:T(512)}, u32[]{:S(2)}) copy-start(f32[512]{0:T(512)} %param.6) | copy-start | bytes 6148
  43.1 27.7 %copy-start.1 = (bf16[512,1536]{1,0:T(8,128)(2,1)S(1)}, bf16[512,1536]{1,0:T(8,128)(2,1)}, u32[]{:S(2)}) copy-start(bf16[512,1536]{1,0:T(8,128)(2,1)} %wqkv_any.9) | copy-start | bytes 4718596
  43.2 27.7 %copy-start.4 = (bf16[1,1,512,512]{3,2,1,0:T(8,128)(2,1)S(1)}, bf16[1,1,512,512]{3,2,1,0:T(8,128)(2,1)}, u32[]{:S(2)}) copy-start(bf16[1,1,512,512]{3,2,1,0:T(8,128)(2,1)} %param.5) | copy-start | bytes 1572868
  43.2 27.7 %copy-start.7 = (bf16[1,1,512,512]{3,2,1,0:T(8,128)(2,1)S(1)}, bf16[1,1,512,512]{3,2,1,0:T(8,128)(2,1)}, u32[]{:S(2)}) copy-start(bf16[1,1,512,512]{3,2,1,0:T(8,128)(2,1)} %param.9) | copy-start | bytes 1572868
  43.2 27.7 %all-to-all-start = ((bf16[8,64,512]{2,1,0:T(8,128)(2,1)}), bf16[8,64,512]{2,1,0:T(8,128)(2,1)S(1)}, u32[]{:S(2)}, u32[]{:S(2)}) async-start(bf16[8,64,512]{2,1,0:T(8,128)(2,1)} %column_grad_hidden.1), calls=%async_computation | async-start | bytes 1048576 | tf_op jit(solution)/shard_map/all_to_all | solution.py:493
  55.5 1.0 %copy-start.11 = (f32[64,2048]{1,0:T(8,128)S(1)}, f32[64,2048]{1,0:T(8,128)}, u32[]{:S(2)}) copy-start(f32[64,2048]{1,0:T(8,128)} %copy-done.10) | copy-start | bytes 1572868
  57.8 5.0 %collective-permute-start.11 = (bf16[32,2048]{1,0:T(8,128)(2,1)S(1)}, bf16[32,2048]{1,0:T(8,128)(2,1)S(1)}, u32[]{:S(2)}, u32[]{:S(2)}) collective-permute-start(bf16[32,2048]{1,0:T(8,128)(2,1)S(1)} %get-tuple-element.54), channel_id=1, source_target_pairs={{0,1},{1,0},{2,3},{3,2},{4,5},{5,4},{6,7},{7,6},{8,9},{9,8},{10,11... | collective-permute-start | bytes 393224 | tf_op jit(solution)/shard_map/ppermute | solution.py:405
  62.8 7.3 %collective-permute-start.12 = (bf16[32,2048]{1,0:T(8,128)(2,1)S(1)}, bf16[32,2048]{1,0:T(8,128)(2,1)S(1)}, u32[]{:S(2)}, u32[]{:S(2)}) collective-permute-start(bf16[32,2048]{1,0:T(8,128)(2,1)S(1)} %add_pair.1.kept_ref), channel_id=1, source_target_pairs={{0,2},{1,3},{2,0},{3,1},{4,6},{5,7},{6,4},{7,5},{8,10},{9,11},{10,... | collective-permute-start | bytes 393224 | tf_op jit(solution)/shard_map/ppermute | solution.py:405
  70.2 5.0 %collective-permute-start.13 = (bf16[32,2048]{1,0:T(8,128)(2,1)S(1)}, bf16[32,2048]{1,0:T(8,128)(2,1)S(1)}, u32[]{:S(2)}, u32[]{:S(2)}) collective-permute-start(bf16[32,2048]{1,0:T(8,128)(2,1)S(1)} %add_pairs.1.held_ref), channel_id=1, source_target_pairs={{0,1},{1,0},{2,3},{3,2},{4,5},{5,4},{6,7},{7,6},{8,9},{9,8},{10,11... | collective-permute-start | bytes 393224 | tf_op jit(solution)/shard_map/ppermute | solution.py:405
  70.9 1.1 %copy-start.9 = (bf16[512,768]{1,0:T(8,128)(2,1)S(1)}, bf16[512,768]{1,0:T(8,128)(2,1)}, u32[]{:S(2)}) copy-start(bf16[512,768]{1,0:T(8,128)(2,1)} %copy-done.8) | copy-start | bytes 2359300

commit v4 on v3

--- a/solution.py
+++ b/solution.py
@@ -15,11 +15,12 @@
 F32 = jnp.float32
 BF16 = jnp.bfloat16
 QUERY_BLOCK = 128
-BIG_VMEM = 32 * 1024 * 1024
-SMALL_VMEM = 12 * 1024 * 1024
+BIG_VMEM = 20 * 1024 * 1024
+SMALL_VMEM = 8 * 1024 * 1024
 ANY = pl.BlockSpec(memory_space=pl.ANY)
 VMEM = pl.BlockSpec(memory_space=pltpu.VMEM)
 SMEM = pl.BlockSpec(memory_space=pltpu.SMEM)
+HBM = pl.BlockSpec(memory_space=pltpu.HBM)
 shaped = jax.ShapeDtypeStruct
 
 
@@ -94,6 +95,17 @@
     ]
 
 
+def started(*copies):
+    for copy in copies:
+        copy.start()
+    return copies
+
+
+def finished(*copies):
+    for copy in copies:
+        copy.wait()
+
+
 def project(hidden, cot, w_ref, wo_ref):
     projected = dot_nn(hidden, w_ref[...]).astype(BF16)
     q, k, v = [projected[:, i * HW : (i + 1) * HW] for i in range(3)]
@@ -102,26 +114,26 @@
 
 
 def row_kernel(
-    x_any, cot_any, gain_ref, wqkv_any, wout_any,
-    qkv_ref, out_ref, grads_ref,
-    x_ref, cot_ref, w_ref, wo_ref, dk_ref, dv_ref, sems,
+    x_any, cot_any, gain_any, wqkv_any, wout_any,
+    qkv_ref, out_ref, grads_any,
+    x_ref, cot_ref, gain_ref, w_ref, wo_ref, dk_ref, dv_ref, grads_ref, sems,
 ):
-    copies = [
+    first = started(
         pltpu.make_async_copy(x_any, x_ref, sems.at[4]),
+        pltpu.make_async_copy(gain_any, gain_ref, sems.at[5]),
+    )
+    later = started(
         *weight_copies(wqkv_any, wout_any, w_ref, wo_ref, sems, 0),
-        pltpu.make_async_copy(cot_any, cot_ref, sems.at[5]),
-    ]
-    for copy in copies:
-        copy.start()
+        pltpu.make_async_copy(cot_any, cot_ref, sems.at[6]),
+    )
     dk_ref[...] = jnp.zeros_like(dk_ref)
     dv_ref[...] = jnp.zeros_like(dv_ref)
-    copies[0].wait()
+    finished(*first)
     tokens = x_ref.shape[0]
     _, normed = rms_parts(x_ref[...].astype(F32))
     hidden = (normed * gain_ref[...]).astype(BF16)
     hidden_t = transposed(hidden)
-    for copy in copies[1:]:
-        copy.wait()
+    finished(*later)
     cot = cot_ref[...]
     q, k, v, g = project(hidden, cot, w_ref, wo_ref)
     kt, vt, gt = transposed(k), transposed(v), transposed(g)
@@ -147,8 +159,10 @@
     grads_ref[:, :HW] = transposed(jnp.concatenate(dq_pairs, 0))
     grads_ref[:, HW : 2 * HW] = dk_ref[...].astype(BF16)
     grads_ref[:, 2 * HW :] = dv_ref[...].astype(BF16)
+    handed = started(pltpu.make_async_copy(grads_ref, grads_any, sems.at[4]))
     qkv_ref[...] = dot_nn(hidden_t, grads_ref[...]).astype(BF16)
     out_ref[...] = dot_nn(jnp.concatenate(att_pairs, 0), cot).astype(BF16)
+    finished(*handed)
 
 
 def column_part(moved_ref, gain_ref, w_ref, wo_ref, weight_waits, grads_ref):
@@ -170,8 +184,7 @@
     hidden = (normed * gain_ref[...]).astype(BF16)
     hidden_t = transposed(hidden)
     cot = gathered(1)
-    for copy in weight_waits:
-        copy.wait()
+    finished(*weight_waits)
     q, k, v, g = project(hidden, cot, w_ref, wo_ref)
     kt, vt, gt = transposed(k), transposed(v), transposed(g)
     query = lax.broadcasted_iota(jnp.int32, (block, 2 * block), 1) % block
@@ -200,15 +213,16 @@
 
 
 def column_kernel(
-    moved_any, gain_ref, wqkv_any, wout_any, row_qkv_ref, row_out_ref,
+    moved_any, gain_any, wqkv_any, wout_any, row_qkv_ref, row_out_ref,
     terms_ref, grads_ref,
-    moved_ref, w_ref, wo_ref, sems,
+    moved_ref, gain_ref, w_ref, wo_ref, sems,
 ):
-    copy = pltpu.make_async_copy(moved_any, moved_ref, sems.at[4])
-    weights = weight_copies(wqkv_any, wout_any, w_ref, wo_ref, sems, 1)
-    for one in (copy, *weights):
-        one.start()
-    copy.wait()
+    copies = started(
+        pltpu.make_async_copy(moved_any, moved_ref, sems.at[4]),
+        pltpu.make_async_copy(gain_any, gain_ref, sems.at[5]),
+    )
+    weights = started(*weight_copies(wqkv_any, wout_any, w_ref, wo_ref, sems, 1))
+    finished(*copies)
     term_qkv, term_out = column_part(moved_ref, gain_ref, w_ref, wo_ref, weights, grads_ref)
     width = terms_ref.shape[0]
     for i in range(3):
@@ -222,9 +236,9 @@
 def column_chip_kernel(
     place_ref, x_any, cot_any, own_any,
     near_1, near_2, near_3, far_1, far_2, far_3,
-    gain_ref, wqkv_any, wout_any, row_qkv_ref, row_out_ref,
+    gain_any, wqkv_any, wout_any, row_qkv_ref, row_out_ref,
     send_ref, keep_ref, grads_ref,
-    moved_ref, w_ref, wo_ref, sems,
+    moved_ref, gain_ref, w_ref, wo_ref, sems,
 ):
     chip, core = place_ref[0], place_ref[1]
     share = moved_ref.shape[2]
@@ -235,6 +249,7 @@
         pltpu.make_async_copy(x_any.at[pl.ds(at, share), :], moved_ref.at[me, 0], sems.at[4]),
         pltpu.make_async_copy(cot_any.at[pl.ds(at, share), :], moved_ref.at[me, 1], sems.at[5]),
         pltpu.make_async_copy(own_any, moved_ref.at[other], sems.at[6]),
+        pltpu.make_async_copy(gain_any, gain_ref, sems.at[13]),
     ]
     for i, (near, far) in enumerate(((near_1, far_1), (near_2, far_2), (near_3, far_3))):
         there = 2 * (chip ^ (i + 1))
@@ -244,11 +259,9 @@
                     piece.at[:, pl.ds(half, share), :], moved_ref.at[row], sems.at[7 + 2 * i + j]
                 )
             )
-    weights = weight_copies(wqkv_any, wout_any, w_ref, wo_ref, sems, 1)
-    for copy in (*copies, *weights):
-        copy.start()
-    for copy in copies:
-        copy.wait()
+    started(*copies)
+    weights = started(*weight_copies(wqkv_any, wout_any, w_ref, wo_ref, sems, 1))
+    finished(*copies)
     term_qkv, term_out = column_part(moved_ref, gain_ref, w_ref, wo_ref, weights, grads_ref)
     width = moved_ref.shape[3]
     first = core == 0
@@ -270,11 +283,7 @@
 
 
 def back_kernel(grads_ref, wqkv_any, back_ref, w_ref, sems):
-    copies = qkv_copies(wqkv_any, w_ref, sems, 1)
-    for copy in copies:
-        copy.start()
-    for copy in copies:
-        copy.wait()
+    finished(*started(*qkv_copies(wqkv_any, w_ref, sems, 1)))
     grad_hidden = dot_nt(grads_ref[...], w_ref[...])
     all_rows, share, width = back_ref.shape
     group = math.gcd(share, 16)
@@ -284,14 +293,23 @@
         back_ref[:, i * group : (i + 1) * group, :] = piece.astype(BF16)
 
 
-def input_kernel(x_ref, cot_ref, gain_ref, grads_ref, wqkv_any, back_ref, grad_ref, w_ref, sems):
-    copies = qkv_copies(wqkv_any, w_ref, sems, 0)
-    for copy in copies:
-        copy.start()
+def input_kernel(
+    x_any, cot_any, gain_any, grads_any, wqkv_any, back_ref, grad_ref,
+    x_ref, cot_ref, gain_ref, grads_ref, w_ref, sems,
+):
+    products = started(
+        pltpu.make_async_copy(grads_any, grads_ref, sems.at[3]),
+        *qkv_copies(wqkv_any, w_ref, sems, 0),
+    )
+    others = started(
+        pltpu.make_async_copy(x_any, x_ref, sems.at[4]),
+        pltpu.make_async_copy(gain_any, gain_ref, sems.at[5]),
+        pltpu.make_async_copy(cot_any, cot_ref, sems.at[6]),
+    )
+    finished(*products)
+    grad_hidden = dot_nt(grads_ref[...], w_ref[...]) + back_ref[...].astype(F32)
+    finished(*others)
     inverse_rms, normed = rms_parts(x_ref[...].astype(F32))
-    for copy in copies:
-        copy.wait()
-    grad_hidden = dot_nt(grads_ref[...], w_ref[...]) + back_ref[...].astype(F32)
     grad_normed = grad_hidden * gain_ref[...]
     projected = jnp.mean(grad_normed * normed, -1, keepdims=True)
     grad = inverse_rms * (grad_normed - normed * projected)
@@ -318,25 +336,27 @@
                     sems.at[2 + 2 * i + which],
                 )
             )
-    for copy in copies:
-        copy.start()
-    for copy in copies:
-        copy.wait()
-
-
-def chip_sum_kernel(place_ref, keep_ref, got_ref, own_ref, off_1, off_2, off_3):
+    finished(*started(*copies))
+
+
+def chip_sum_kernel(place_ref, keep_ref, got_ref, own_any, off_1, off_2, off_3, own_ref, sem):
     chip = place_ref[0]
+    handed = None
     for i, target in enumerate((own_ref, off_1, off_2, off_3)):
         there = chip ^ i
         total = keep_ref[there].astype(F32) + got_ref[there].astype(F32)
         target[...] = total.astype(target.dtype)
-
-
-def layer_sum_kernel(place_ref, own_ref, got_1, got_2, got_3, send_ref, keep_ref):
+        if handed is None:
+            handed = started(pltpu.make_async_copy(own_ref, own_any, sem))
+    finished(*handed)
+
+
+def layer_sum_kernel(place_ref, own_any, got_1, got_2, got_3, send_ref, keep_ref, own_ref, sem):
+    own = started(pltpu.make_async_copy(own_any, own_ref, sem))
     upper = place_ref[2] == 1
-    total = own_ref[...] + (
-        (got_1[...].astype(F32) + got_2[...].astype(F32)) + got_3[...].astype(F32)
-    )
+    total = (got_1[...].astype(F32) + got_2[...].astype(F32)) + got_3[...].astype(F32)
+    finished(*own)
+    total += own_ref[...]
     half = total.shape[0] // 2
     low, high = total[:half], total[half:]
     send_ref[...] = jnp.where(upper, low, high).astype(BF16)
@@ -347,11 +367,16 @@
     out_ref[...] = (kept_ref[...].astype(F32) + got_ref[...].astype(F32)).astype(BF16)
 
 
-def result_kernel(place_ref, held_ref, got_ref, wqkv_any, gain_ref, qkv_ref, out_ref, grad_ref, w_ref, sem):
+def result_kernel(
+    place_ref, held_ref, got_ref, wqkv_any, gain_any, qkv_ref, out_ref, grad_ref,
+    w_ref, gain_ref, sems,
+):
     rows = qkv_ref.shape[0]
     at = pl.multiple_of((place_ref[0] * 2 + place_ref[1]) * rows, rows)
-    copy = pltpu.make_async_copy(wqkv_any.at[pl.ds(at, rows), :], w_ref, sem)
-    copy.start()
+    copies = started(
+        pltpu.make_async_copy(wqkv_any.at[pl.ds(at, rows), :], w_ref, sems.at[0]),
+        pltpu.make_async_copy(gain_any, gain_ref, sems.at[1]),
+    )
     upper = place_ref[2] == 1
     held, got = held_ref[...].astype(F32), got_ref[...].astype(F32)
     half = rows // 2
@@ -359,20 +384,31 @@
     cut = qkv_ref.shape[1]
     qkv_ref[:half], qkv_ref[half:] = low[:, :cut], high[:, :cut]
     out_ref[:half], out_ref[half:] = low[:, cut:], high[:, cut:]
-    copy.wait()
+    finished(*copies)
     total = jnp.sum(qkv_ref[...] * w_ref[...].astype(F32), -1, keepdims=True)
-    grad_ref[...] = total / gain_ref[...]
+    shape = (rows, gain_ref.shape[1])
+    row = lax.broadcasted_iota(jnp.int32, shape, 0)
+    feature = lax.broadcasted_iota(jnp.int32, shape, 1)
+    gain = jnp.sum(jnp.where(feature == row + at, gain_ref[...], 0.0), -1, keepdims=True)
+    shape = (rows, grad_ref.shape[1])
+    same = lax.broadcasted_iota(jnp.int32, shape, 0) == lax.broadcasted_iota(jnp.int32, shape, 1)
+    grad_ref[...] = jnp.sum(jnp.where(same, total / gain, 0.0), 0, keepdims=True)
 
 
 def call(kernel, name, ins, outs, scratch=(), flops=0, vmem=SMALL_VMEM, out_specs=None):
-    outs = [shaped(*out) for out in outs]
-    args = [array for _, array in ins]
+    out_specs = out_specs or [VMEM] * len(outs)
+    places = [pltpu.HBM if spec is HBM else None for spec in out_specs]
+    outs = [place(*out) if place else shaped(*out) for place, out in zip(places, outs)]
+    args = [
+        pltpu.with_memory_space_constraint(array, pltpu.HBM) if spec is HBM else array
+        for spec, array in ins
+    ]
     size = sum(math.prod(a.shape) * a.dtype.itemsize for a in (*args, *outs))
     return pl.pallas_call(
         kernel,
         out_shape=outs,
         in_specs=[spec for spec, _ in ins],
-        out_specs=out_specs or [VMEM] * len(outs),
+        out_specs=out_specs,
         scratch_shapes=scratch,
         name=name,
         cost_estimate=pl.CostEstimate(flops=flops, bytes_accessed=size, transcendentals=0),
@@ -395,6 +431,7 @@
     here = lax.axis_index("seq")
     place = jnp.stack([here // 2, here % 2, lax.axis_index("dp") % 2]).astype(jnp.int32)
     weight_scratch = [
+        pltpu.VMEM((1, width), F32),
         pltpu.VMEM((width, 3 * HW), BF16),
         pltpu.VMEM((HW, width), BF16),
     ]
@@ -408,7 +445,7 @@
         packed = call(
             pack_kernel,
             "pack_columns",
-            [(SMEM, place), (ANY, x), (ANY, cot)],
+            [(SMEM, place), (HBM, x), (HBM, cot)],
             [((2, share, width), BF16)] + [((2, 2 * share, width), BF16)] * 3,
             [pltpu.SemaphoreType.DMA((8,))],
             out_specs=[ANY] * 4,
@@ -424,7 +461,7 @@
     row_qkv, row_out, row_grads = call(
         row_kernel,
         "row_heads",
-        [(ANY, x), (ANY, cot), (VMEM, gain), (ANY, qkv_weight), (ANY, out_weight)],
+        [(HBM, x), (HBM, cot), (HBM, gain), (HBM, qkv_weight), (HBM, out_weight)],
         [((width, 3 * HW), BF16), ((HW, width), BF16), ((columns, 3 * HW), BF16)],
         [
             pltpu.VMEM((columns, width), BF16),
@@ -432,29 +469,31 @@
             *weight_scratch,
             pltpu.VMEM((columns, HW), F32),
             pltpu.VMEM((columns, HW), F32),
-            pltpu.SemaphoreType.DMA((6,)),
+            pltpu.VMEM((columns, 3 * HW), BF16),
+            pltpu.SemaphoreType.DMA((7,)),
         ],
         5_000_000_000,
         BIG_VMEM,
+        [VMEM, VMEM, HBM],
     )
     moved_scratch = pltpu.VMEM((n, 2, share, width), BF16)
     if layered:
         near_1, near_2, near_3, row_qkv = lax.optimization_barrier((near_1, near_2, near_3, row_qkv))
         far_3, far_1, far_2 = swap(near_3, "seq", 1), swap(near_1, "seq", 1), swap(near_2, "seq", 1)
     shared = [
-        (VMEM, gain), (ANY, qkv_weight), (ANY, out_weight), (VMEM, row_qkv), (VMEM, row_out),
+        (HBM, gain), (HBM, qkv_weight), (HBM, out_weight), (VMEM, row_qkv), (VMEM, row_out),
     ]
     if layered:
         send, keep, col_grads = call(
             column_chip_kernel,
             "column_heads",
             [
-                (SMEM, place), (ANY, x), (ANY, cot), (ANY, own),
+                (SMEM, place), (HBM, x), (HBM, cot), (ANY, own),
                 (ANY, near_1), (ANY, near_2), (ANY, near_3),
                 (ANY, far_1), (ANY, far_2), (ANY, far_3), *shared,
             ],
             [((chips, row_share, term_width), BF16)] * 2 + [((columns, 3 * HW), BF16)],
-            [moved_scratch, *weight_scratch, pltpu.SemaphoreType.DMA((13,))],
+            [moved_scratch, *weight_scratch, pltpu.SemaphoreType.DMA((14,))],
             4_000_000_000,
             BIG_VMEM,
         )
@@ -465,7 +504,7 @@
             "column_heads",
             [(ANY, moved), *shared],
             [((width, term_width), BF16), ((columns, 3 * HW), BF16)],
-            [moved_scratch, *weight_scratch, pltpu.SemaphoreType.DMA((5,))],
+            [moved_scratch, *weight_scratch, pltpu.SemaphoreType.DMA((6,))],
             4_000_000_000,
             BIG_VMEM,
         )
@@ -475,6 +514,8 @@
             "add_cores",
             [(SMEM, place), (VMEM, keep), (VMEM, got)],
             [((row_share, term_width), F32)] + [((row_share, term_width), BF16)] * 3,
+            [pltpu.VMEM((row_share, term_width), F32), pltpu.SemaphoreType.DMA],
+            out_specs=[HBM, VMEM, VMEM, VMEM],
         )
         got_3 = swap(off_3, "seq", 6)
         got_1 = swap(off_1, "seq", 2)
@@ -483,23 +524,25 @@
     (back,) = call(
         back_kernel,
         "column_grad_hidden",
-        [(VMEM, col_grads), (ANY, qkv_weight)],
+        [(VMEM, col_grads), (HBM, qkv_weight)],
         [((n, share, width), BF16)],
         small_scratch,
         400_000_000,
     )
+    half_rows = (row_share // 2, term_width)
     if layered:
         back, owned = lax.optimization_barrier((back, owned))
-    returned = lax.all_to_all(back, "seq", split_axis=0, concat_axis=0, tiled=True)
-    half_rows = (row_share // 2, term_width)
-    if layered:
         to_next, kept = call(
             layer_sum_kernel,
             "add_chips",
-            [(SMEM, place), (VMEM, owned), (VMEM, got_1), (VMEM, got_2), (VMEM, got_3)],
+            [(SMEM, place), (HBM, owned), (VMEM, got_1), (VMEM, got_2), (VMEM, got_3)],
             [(half_rows, BF16), (half_rows, F32)],
+            [pltpu.VMEM((row_share, term_width), F32), pltpu.SemaphoreType.DMA],
         )
         from_next = swap(to_next, "dp", 1)
+        back, to_next = lax.optimization_barrier((back, to_next))
+    returned = lax.all_to_all(back, "seq", split_axis=0, concat_axis=0, tiled=True)
+    if layered:
         (pair_sum,) = call(
             add_kernel, "add_pair", [(VMEM, kept), (VMEM, from_next)], [(half_rows, BF16)]
         )
@@ -512,24 +555,33 @@
         input_kernel,
         "input_grad",
         [
-            (VMEM, x), (VMEM, cot), (VMEM, gain), (VMEM, row_grads), (ANY, qkv_weight),
+            (HBM, x), (HBM, cot), (HBM, gain), (HBM, row_grads), (HBM, qkv_weight),
             (VMEM, returned.reshape(columns, width)),
         ],
         [((columns, width), BF16)],
-        small_scratch,
+        [
+            pltpu.VMEM((columns, width), BF16),
+            pltpu.VMEM((columns, width), BF16),
+            pltpu.VMEM((1, width), F32),
+            pltpu.VMEM((columns, 3 * HW), BF16),
+            pltpu.VMEM((width, 3 * HW), BF16),
+            pltpu.SemaphoreType.DMA((7,)),
+        ],
         400_000_000,
     )
-    own_gain = lax.dynamic_slice_in_dim(norm_gain, here * row_share, row_share, 0)
     if layered:
         sum_qkv, sum_out, sum_gain = call(
             result_kernel,
             "result",
             [
-                (SMEM, place), (VMEM, held), (VMEM, other), (ANY, qkv_weight),
-                (VMEM, own_gain.reshape(row_share, 1)),
+                (SMEM, place), (VMEM, held), (VMEM, other), (HBM, qkv_weight), (HBM, gain),
             ],
-            [((row_share, 3 * width), F32), ((row_share, width), F32), ((row_share, 1), F32)],
-            [pltpu.VMEM((row_share, 3 * width), BF16), pltpu.SemaphoreType.DMA],
+            [((row_share, 3 * width), F32), ((row_share, width), F32), ((1, row_share), F32)],
+            [
+                pltpu.VMEM((row_share, 3 * width), BF16),
+                pltpu.VMEM((1, width), F32),
+                pltpu.SemaphoreType.DMA((2,)),
+            ],
         )
         sum_gain = sum_gain.reshape(row_share)
     else:
@@ -541,6 +593,7 @@
             sent = total.astype(BF16)
             total = sent.astype(F32) + swap(sent, "dp", 1 << step).astype(F32)
         sum_qkv, sum_out = total[:, : 3 * width], total[:, 3 * width :]
+        own_gain = lax.dynamic_slice_in_dim(norm_gain, here * row_share, row_share, 0)
         own_weight = lax.dynamic_slice_in_dim(qkv_weight, here * row_share, row_share, 0)
         sum_gain = jnp.sum(sum_qkv * own_weight.astype(F32), -1) / own_gain
     return (input_grad.reshape(inputs.shape), sum_qkv, sum_out, sum_gain)

time: 78.4 us -> 79.3 us (1.011)
  local copies, waits for them, and re-layouts: 11.4 us -> 0 us
  waiting for transfers between devices: 21.5 us -> 30.3 us
  Pallas kernels: 24.8 us -> 29.9 us
    unnamed x30 -> x0, local copies, waits for them, and re-layouts: 11.2 us -> none
    ppermute x14, waiting for transfers between devices: 21.5 us -> 30.3 us  [swap(): return lax.ppermute(array, axis, [(i, i ^ bits) for i in range(count)])]
    pallas_call x10, Pallas kernels: 24.8 us -> 29.9 us  [call(): pl.pallas_call(kernel, out_shape=outs, in_specs=[spec for spec, _ in ins]...]
    all_to_all x1, starting transfers between devices: 4.31 us -> 3.51 us  [body(): lax.all_to_all(back, 'seq', split_axis=0, concat_axis=0, tiled=True)]
  transfers between devices with their start and end apart: 15 -> 15, of which waited for: 6 -> 9; matrix products, arithmetic and copies ran while one was open for 0% -> 0% of each run, Pallas kernels for 16% -> 18%
where the time goes in v4:
time: 79.3 us; the launch traced here: 78.8 us
  waiting for transfers between devices  30.3 us (38%)
  Pallas kernels  29.9 us (38%)
  starting transfers between devices  17.9 us (23%)
    ppermute x14, waiting for transfers between devices, swap(): return lax.ppermute(array, axis, [(i, i ^ bits) for i in range(count)])  30.3 us
    pallas_call x10, Pallas kernels, call(): pl.pallas_call(kernel, out_shape=outs, in_specs=[spec for spec, _ in ins]...  29.9 us
    ppermute x14, starting transfers between devices, swap(): return lax.ppermute(array, axis, [(i, i ^ bits) for i in range(count)])  14.3 us
    all_to_all x1, starting transfers between devices, body(): lax.all_to_all(back, 'seq', split_axis=0, concat_axis=0, tiled=True)  3.51 us
  transfers between devices with their start and end apart: 15, of which 9 were waited for; matrix products, arithmetic and copies ran while one was open for 0% of the time, Pallas kernels for 18%

profile of v4, /device:TPU:0, one launch (start us, length us, event | category | flops | bytes accessed | tf_op | source)
XLA Modules:
  0.0 78.8 jit_solution(3348343784957827634)
XLA Ops:
  0.7 0.1 pad_add_fusion.place_ref
  0.7 1.9 %pack_columns.1 = (bf16[2,64,512]{2,1,0:T(8,128)(2,1)S(1)}, bf16[2,128,512]{2,1,0:T(8,128)(2,1)S(1)}, bf16[2,128,512]{2,1,0:T(8,128)(2,1)S(1)}, bf16[2,128,512]{2,1,0:T(8,128)(2,1)S(1)}) custom-call(s32[3]{0:T(128)S(1)} %pad_add_fusion.place_ref, bf16[512,512]{1,0:T(8,128)(2,1)} %bitcast.10, bf16[512,512]{1,0:T(8,128)(2,1)} %bitcast.14), custom_call_target="tpu_custom_call" | custom-call | bytes 1966092 | tf_op jit(solution)/shard_map/pack_columns/pallas_call | solution.py:407
  2.6 3.0 %collective-permute-start.1 = (bf16[2,128,512]{2,1,0:T(8,128)(2,1)S(1)}, bf16[2,128,512]{2,1,0:T(8,128)(2,1)S(1)}, u32[]{:S(2)}, u32[]{:S(2)}) collective-permute-start(bf16[2,128,512]{2,1,0:T(8,128)(2,1)S(1)} %get-tuple-element.34), channel_id=1, source_target_pairs={{0,8},{4,12},{8,0},{12,4},{16,24},{20,28},{24,16},{28,20},{1,9},{5... | collective-permute-start | bytes 786440 | tf_op jit(solution)/shard_map/ppermute | solution.py:442
  5.6 1.5 %collective-permute-start.2 = (bf16[2,128,512]{2,1,0:T(8,128)(2,1)S(1)}, bf16[2,128,512]{2,1,0:T(8,128)(2,1)S(1)}, u32[]{:S(2)}, u32[]{:S(2)}) collective-permute-start(bf16[2,128,512]{2,1,0:T(8,128)(2,1)S(1)} %get-tuple-element.35), channel_id=1, source_target_pairs={{0,16},{4,20},{8,24},{12,28},{16,0},{20,4},{24,8},{28,12},{1,17},{... | collective-permute-start | bytes 786440 | tf_op jit(solution)/shard_map/ppermute | solution.py:442
  7.1 0.0 collective-permute-start.3
  7.1 8.9 %row_heads.1 = (bf16[512,768]{1,0:T(8,128)(2,1)S(1)}, bf16[256,512]{1,0:T(8,128)(2,1)S(1)}, bf16[512,768]{1,0:T(8,128)(2,1)}) custom-call(bf16[512,512]{1,0:T(8,128)(2,1)} %bitcast.11, bf16[512,512]{1,0:T(8,128)(2,1)} %bitcast.15, f32[1,512]{1,0:T(1,128)} %bitcast.19, bf16[512,1536]{1,0:T(8,128)(2,1)} %wqkv_any.9, bf16[512,512]{1,0:T(8,128)(2,1)} %wout_any.3), custom_call_target="tpu_custom_call" | custom-call | flops 5000000000 | bytes 4982784 | tf_op jit(solution)/shard_map/row_heads/pallas_call | solution.py:407
  16.1 0.0 collective-permute-done.1.near_1
  16.1 2.9 %collective-permute-done.2.near_2 = bf16[2,128,512]{2,1,0:T(8,128)(2,1)S(1)} collective-permute-done((bf16[2,128,512]{2,1,0:T(8,128)(2,1)S(1)}, bf16[2,128,512]{2,1,0:T(8,128)(2,1)S(1)}, u32[]{:S(2)}, u32[]{:S(2)}) %collective-permute-start.2) | collective-permute-done | bytes 262176 | tf_op jit(solution)/shard_map/ppermute | solution.py:442
  19.0 0.0 collective-permute-done.3.near_3
  19.0 0.0 collective-permute-start.4
  19.0 0.5 collective-permute-start.5
  19.5 0.0 collective-permute-start.6
  19.5 0.5 collective-permute-start
  20.0 1.5 %collective-permute-done.own_any = bf16[2,64,512]{2,1,0:T(8,128)(2,1)S(1)} collective-permute-done((bf16[2,64,512]{2,1,0:T(8,128)(2,1)S(1)}, bf16[2,64,512]{2,1,0:T(8,128)(2,1)S(1)}, u32[]{:S(2)}, u32[]{:S(2)}) %collective-permute-start) | collective-permute-done | bytes 131104 | tf_op jit(solution)/shard_map/ppermute | solution.py:442
  21.5 0.0 collective-permute-done.4.far_1
  21.5 0.0 collective-permute-done.5.far_2
  21.5 0.0 collective-permute-done.6.far_3
  21.5 7.8 %column_heads.1 = (bf16[4,64,2048]{2,1,0:T(8,128)(2,1)S(1)}, bf16[4,64,2048]{2,1,0:T(8,128)(2,1)S(1)}, bf16[512,768]{1,0:T(8,128)(2,1)S(1)}) custom-call(s32[3]{0:T(128)S(1)} %pad_add_fusion.place_ref, bf16[512,512]{1,0:T(8,128)(2,1)} %bitcast.12, bf16[512,512]{1,0:T(8,128)(2,1)} %bitcast.16, bf16[2,64,512]{2,1,0:T(8,128)(2,1)S(1)} %collective-permute-done.own_any, ...), custom_call_target="tpu_custom_call" | custom-call | flops 4000000000 | bytes 8783884 | tf_op jit(solution)/shard_map/column_heads/pallas_call | solution.py:407
  29.3 0.2 collective-permute-start.7
  29.5 2.5 %collective-permute-done.7.got_ref = bf16[4,64,2048]{2,1,0:T(8,128)(2,1)S(1)} collective-permute-done((bf16[4,64,2048]{2,1,0:T(8,128)(2,1)S(1)}, bf16[4,64,2048]{2,1,0:T(8,128)(2,1)S(1)}, u32[]{:S(2)}, u32[]{:S(2)}) %collective-permute-start.7) | collective-permute-done | bytes 1048608 | tf_op jit(solution)/shard_map/ppermute | solution.py:442
  32.0 1.4 %add_cores.1 = (f32[64,2048]{1,0:T(8,128)}, bf16[64,2048]{1,0:T(8,128)(2,1)S(1)}, bf16[64,2048]{1,0:T(8,128)(2,1)S(1)}, bf16[64,2048]{1,0:T(8,128)(2,1)S(1)}) custom-call(s32[3]{0:T(128)S(1)} %pad_add_fusion.place_ref, bf16[4,64,2048]{2,1,0:T(8,128)(2,1)S(1)} %get-tuple-element.44.keep_ref, bf16[4,64,2048]{2,1,0:T(8,128)(2,1)S(1)} %collective-permute-done.7.got_ref), custom_call_target="tpu_custom_call" | custom-call | bytes 3407884 | tf_op jit(solution)/shard_map/add_cores/pallas_call | solution.py:407
  33.5 1.3 %collective-permute-start.8 = (bf16[64,2048]{1,0:T(8,128)(2,1)S(1)}, bf16[64,2048]{1,0:T(8,128)(2,1)S(1)}, u32[]{:S(2)}, u32[]{:S(2)}) collective-permute-start(bf16[64,2048]{1,0:T(8,128)(2,1)S(1)} %get-tuple-element.51), channel_id=1, source_target_pairs={{0,8},{4,12},{8,0},{12,4},{16,24},{20,28},{24,16},{28,20},{1,9},{5... | collective-permute-start | bytes 786440 | tf_op jit(solution)/shard_map/ppermute | solution.py:442
  34.8 0.8 %collective-permute-start.9 = (bf16[64,2048]{1,0:T(8,128)(2,1)S(1)}, bf16[64,2048]{1,0:T(8,128)(2,1)S(1)}, u32[]{:S(2)}, u32[]{:S(2)}) collective-permute-start(bf16[64,2048]{1,0:T(8,128)(2,1)S(1)} %get-tuple-element.52), channel_id=1, source_target_pairs={{0,16},{4,20},{8,24},{12,28},{16,0},{20,4},{24,8},{28,12},{1,17},{... | collective-permute-start | bytes 786440 | tf_op jit(solution)/shard_map/ppermute | solution.py:442
  35.6 1.4 %collective-permute-start.10 = (bf16[64,2048]{1,0:T(8,128)(2,1)S(1)}, bf16[64,2048]{1,0:T(8,128)(2,1)S(1)}, u32[]{:S(2)}, u32[]{:S(2)}) collective-permute-start(bf16[64,2048]{1,0:T(8,128)(2,1)S(1)} %get-tuple-element.53), channel_id=1, source_target_pairs={{0,24},{4,28},{8,16},{12,20},{16,8},{20,12},{24,0},{28,4},{1,25},{... | collective-permute-start | bytes 786440 | tf_op jit(solution)/shard_map/ppermute | solution.py:442
  37.0 2.5 %column_grad_hidden.1 = bf16[8,64,512]{2,1,0:T(8,128)(2,1)} custom-call(bf16[512,768]{1,0:T(8,128)(2,1)S(1)} %get-tuple-element.47.grads_ref, bf16[512,1536]{1,0:T(8,128)(2,1)} %wqkv_any.9), custom_call_target="tpu_custom_call" | custom-call | flops 400000000 | bytes 2883584 | tf_op jit(solution)/shard_map/column_grad_hidden/pallas_call | solution.py:407
  39.6 3.1 %collective-permute-done.8.got_1 = bf16[64,2048]{1,0:T(8,128)(2,1)S(1)} collective-permute-done((bf16[64,2048]{1,0:T(8,128)(2,1)S(1)}, bf16[64,2048]{1,0:T(8,128)(2,1)S(1)}, u32[]{:S(2)}, u32[]{:S(2)}) %collective-permute-start.8) | collective-permute-done | bytes 262176 | tf_op jit(solution)/shard_map/ppermute | solution.py:442
  42.7 4.1 %collective-permute-done.9.got_2 = bf16[64,2048]{1,0:T(8,128)(2,1)S(1)} collective-permute-done((bf16[64,2048]{1,0:T(8,128)(2,1)S(1)}, bf16[64,2048]{1,0:T(8,128)(2,1)S(1)}, u32[]{:S(2)}, u32[]{:S(2)}) %collective-permute-start.9) | collective-permute-done | bytes 262176 | tf_op jit(solution)/shard_map/ppermute | solution.py:442
  46.8 1.6 %collective-permute-done.10.got_3 = bf16[64,2048]{1,0:T(8,128)(2,1)S(1)} collective-permute-done((bf16[64,2048]{1,0:T(8,128)(2,1)S(1)}, bf16[64,2048]{1,0:T(8,128)(2,1)S(1)}, u32[]{:S(2)}, u32[]{:S(2)}) %collective-permute-start.10) | collective-permute-done | bytes 262176 | tf_op jit(solution)/shard_map/ppermute | solution.py:442
  48.4 1.7 %add_chips.1 = (bf16[32,2048]{1,0:T(8,128)(2,1)S(1)}, f32[32,2048]{1,0:T(8,128)S(1)}) custom-call(s32[3]{0:T(128)S(1)} %pad_add_fusion.place_ref, f32[64,2048]{1,0:T(8,128)} %get-tuple-element.50.own_any, bf16[64,2048]{1,0:T(8,128)(2,1)S(1)} %collective-permute-done.8.got_1, bf16[64,2048]{1,0:T(8,128)(2,1)S(1)} %collective-permute-done.9.got_2, ...), custom_call_target="tpu_custom_call" | custom-call | bytes 1703948 | tf_op jit(solution)/shard_map/add_chips/pallas_call | solution.py:407
  50.1 3.5 %all-to-all-start = ((bf16[8,64,512]{2,1,0:T(8,128)(2,1)}), bf16[8,64,512]{2,1,0:T(8,128)(2,1)S(1)}, u32[]{:S(2)}, u32[]{:S(2)}) async-start(bf16[8,64,512]{2,1,0:T(8,128)(2,1)} %column_grad_hidden.1), calls=%async_computation | async-start | bytes 1048576 | tf_op jit(solution)/shard_map/all_to_all | solution.py:544
  53.6 1.6 %collective-permute-start.11 = (bf16[32,2048]{1,0:T(8,128)(2,1)S(1)}, bf16[32,2048]{1,0:T(8,128)(2,1)S(1)}, u32[]{:S(2)}, u32[]{:S(2)}) collective-permute-start(bf16[32,2048]{1,0:T(8,128)(2,1)S(1)} %get-tuple-element.54), channel_id=1, source_target_pairs={{0,1},{1,0},{2,3},{3,2},{4,5},{5,4},{6,7},{7,6},{8,9},{9,8},{10,11... | collective-permute-start | bytes 393224 | tf_op jit(solution)/shard_map/ppermute | solution.py:442
  55.3 4.2 %collective-permute-done.11.got_ref = bf16[32,2048]{1,0:T(8,128)(2,1)S(1)} collective-permute-done((bf16[32,2048]{1,0:T(8,128)(2,1)S(1)}, bf16[32,2048]{1,0:T(8,128)(2,1)S(1)}, u32[]{:S(2)}, u32[]{:S(2)}) %collective-permute-start.11) | collective-permute-done | bytes 131104 | tf_op jit(solution)/shard_map/ppermute | solution.py:442
  59.5 2.7 %collective-permute-start.12 = (bf16[32,2048]{1,0:T(8,128)(2,1)S(1)}, bf16[32,2048]{1,0:T(8,128)(2,1)S(1)}, u32[]{:S(2)}, u32[]{:S(2)}) collective-permute-start(bf16[32,2048]{1,0:T(8,128)(2,1)S(1)} %add_pair.1.kept_ref), channel_id=1, source_target_pairs={{0,2},{1,3},{2,0},{3,1},{4,6},{5,7},{6,4},{7,5},{8,10},{9,11},{10,... | collective-permute-start | bytes 393224 | tf_op jit(solution)/shard_map/ppermute | solution.py:442
  62.1 6.1 %collective-permute-done.12.got_ref = bf16[32,2048]{1,0:T(8,128)(2,1)S(1)} collective-permute-done((bf16[32,2048]{1,0:T(8,128)(2,1)S(1)}, bf16[32,2048]{1,0:T(8,128)(2,1)S(1)}, u32[]{:S(2)}, u32[]{:S(2)}) %collective-permute-start.12) | collective-permute-done | bytes 131104 | tf_op jit(solution)/shard_map/ppermute | solution.py:442
  68.2 0.7 collective-permute-start.13
  68.9 4.3 %collective-permute-done.13.got_ref = bf16[32,2048]{1,0:T(8,128)(2,1)S(1)} collective-permute-done((bf16[32,2048]{1,0:T(8,128)(2,1)S(1)}, bf16[32,2048]{1,0:T(8,128)(2,1)S(1)}, u32[]{:S(2)}, u32[]{:S(2)}) %collective-permute-start.13) | collective-permute-done | bytes 131104 | tf_op jit(solution)/shard_map/ppermute | solution.py:442
  73.2 2.3 %result.1 = (f32[64,1536]{1,0:T(8,128)}, f32[64,512]{1,0:T(8,128)}, f32[1,64]{1,0:T(1,128)}) custom-call(s32[3]{0:T(128)S(1)} %pad_add_fusion.place_ref, bf16[32,2048]{1,0:T(8,128)(2,1)S(1)} %add_pairs.1.held_ref, bf16[32,2048]{1,0:T(8,128)(2,1)S(1)} %collective-permute-done.13.got_ref, bf16[512,1536]{1,0:T(8,128)(2,1)} %wqkv_any.9, f32[1,512]{1,0:T(1,128)} %bitcast.21), custom_call_target="tpu_custom_call" | custom-call | bytes 2361612 | tf_op jit(solution)/shard_map/result/pallas_call | solution.py:407
  75.5 0.0 all-to-all-done
  75.5 3.3 %input_grad.1 = bf16[512,512]{1,0:T(8,128)(2,1)} custom-call(bf16[512,512]{1,0:T(8,128)(2,1)} %bitcast.13, bf16[512,512]{1,0:T(8,128)(2,1)} %bitcast.17, f32[1,512]{1,0:T(1,128)} %bitcast.22, bf16[512,768]{1,0:T(8,128)(2,1)} %get-tuple-element.32.grads_any, bf16[512,1536]{1,0:T(8,128)(2,1)} %wqkv_any.9, bf16[512,512]{1,0:T(8,128)(2,1)S(1)} %bitcast.9), custom_call_target="tpu_custom_call" | custom-call | flops 400000000 | bytes 4458496 | tf_op jit(solution)/shard_map/input_grad/pallas_call | solution.py:407
  (2 shorter events, 0.1 us)
Async XLA Ops:
  2.6 13.5 %collective-permute-start.1 = (bf16[2,128,512]{2,1,0:T(8,128)(2,1)S(1)}, bf16[2,128,512]{2,1,0:T(8,128)(2,1)S(1)}, u32[]{:S(2)}, u32[]{:S(2)}) collective-permute-start(bf16[2,128,512]{2,1,0:T(8,128)(2,1)S(1)} %get-tuple-element.34), channel_id=1, source_target_pairs={{0,8},{4,12},{8,0},{12,4},{16,24},{20,28},{24,16},{28,20},{1,9},{5... | collective-permute-start | bytes 786440 | tf_op jit(solution)/shard_map/ppermute | solution.py:442
  5.6 13.4 %collective-permute-start.2 = (bf16[2,128,512]{2,1,0:T(8,128)(2,1)S(1)}, bf16[2,128,512]{2,1,0:T(8,128)(2,1)S(1)}, u32[]{:S(2)}, u32[]{:S(2)}) collective-permute-start(bf16[2,128,512]{2,1,0:T(8,128)(2,1)S(1)} %get-tuple-element.35), channel_id=1, source_target_pairs={{0,16},{4,20},{8,24},{12,28},{16,0},{20,4},{24,8},{28,12},{1,17},{... | collective-permute-start | bytes 786440 | tf_op jit(solution)/shard_map/ppermute | solution.py:442
  7.1 11.9 %collective-permute-start.3 = (bf16[2,128,512]{2,1,0:T(8,128)(2,1)S(1)}, bf16[2,128,512]{2,1,0:T(8,128)(2,1)S(1)}, u32[]{:S(2)}, u32[]{:S(2)}) collective-permute-start(bf16[2,128,512]{2,1,0:T(8,128)(2,1)S(1)} %get-tuple-element.36), channel_id=1, source_target_pairs={{0,24},{4,28},{8,16},{12,20},{16,8},{20,12},{24,0},{28,4},{1,25},{... | collective-permute-start | bytes 786440 | tf_op jit(solution)/shard_map/ppermute | solution.py:442
  19.0 2.5 %collective-permute-start.4 = (bf16[2,128,512]{2,1,0:T(8,128)(2,1)S(1)}, bf16[2,128,512]{2,1,0:T(8,128)(2,1)S(1)}, u32[]{:S(2)}, u32[]{:S(2)}) collective-permute-start(bf16[2,128,512]{2,1,0:T(8,128)(2,1)S(1)} %collective-permute-done.1.near_1), channel_id=1, source_target_pairs={{0,4},{4,0},{8,12},{12,8},{16,20},{20,16},{24,28},{28,24},{1,5},{5... | collective-permute-start | bytes 786440 | tf_op jit(solution)/shard_map/ppermute | solution.py:442
  19.0 2.5 %collective-permute-start.5 = (bf16[2,128,512]{2,1,0:T(8,128)(2,1)S(1)}, bf16[2,128,512]{2,1,0:T(8,128)(2,1)S(1)}, u32[]{:S(2)}, u32[]{:S(2)}) collective-permute-start(bf16[2,128,512]{2,1,0:T(8,128)(2,1)S(1)} %collective-permute-done.2.near_2), channel_id=1, source_target_pairs={{0,4},{4,0},{8,12},{12,8},{16,20},{20,16},{24,28},{28,24},{1,5},{5... | collective-permute-start | bytes 786440 | tf_op jit(solution)/shard_map/ppermute | solution.py:442
  19.5 2.0 %collective-permute-start.6 = (bf16[2,128,512]{2,1,0:T(8,128)(2,1)S(1)}, bf16[2,128,512]{2,1,0:T(8,128)(2,1)S(1)}, u32[]{:S(2)}, u32[]{:S(2)}) collective-permute-start(bf16[2,128,512]{2,1,0:T(8,128)(2,1)S(1)} %collective-permute-done.3.near_3), channel_id=1, source_target_pairs={{0,4},{4,0},{8,12},{12,8},{16,20},{20,16},{24,28},{28,24},{1,5},{5... | collective-permute-start | bytes 786440 | tf_op jit(solution)/shard_map/ppermute | solution.py:442
  19.5 2.0 %collective-permute-start = (bf16[2,64,512]{2,1,0:T(8,128)(2,1)S(1)}, bf16[2,64,512]{2,1,0:T(8,128)(2,1)S(1)}, u32[]{:S(2)}, u32[]{:S(2)}) collective-permute-start(bf16[2,64,512]{2,1,0:T(8,128)(2,1)S(1)} %get-tuple-element.33), channel_id=1, source_target_pairs={{0,4},{4,0},{8,12},{12,8},{16,20},{20,16},{24,28},{28,24},{1,5},{5... | collective-permute-start | bytes 393224 | tf_op jit(solution)/shard_map/ppermute | solution.py:442
  29.3 2.7 %collective-permute-start.7 = (bf16[4,64,2048]{2,1,0:T(8,128)(2,1)S(1)}, bf16[4,64,2048]{2,1,0:T(8,128)(2,1)S(1)}, u32[]{:S(2)}, u32[]{:S(2)}) collective-permute-start(bf16[4,64,2048]{2,1,0:T(8,128)(2,1)S(1)} %get-tuple-element.45), channel_id=1, source_target_pairs={{0,4},{4,0},{8,12},{12,8},{16,20},{20,16},{24,28},{28,24},{1,5},{5... | collective-permute-start | bytes 3145736 | tf_op jit(solution)/shard_map/ppermute | solution.py:442
  33.5 9.2 %collective-permute-start.8 = (bf16[64,2048]{1,0:T(8,128)(2,1)S(1)}, bf16[64,2048]{1,0:T(8,128)(2,1)S(1)}, u32[]{:S(2)}, u32[]{:S(2)}) collective-permute-start(bf16[64,2048]{1,0:T(8,128)(2,1)S(1)} %get-tuple-element.51), channel_id=1, source_target_pairs={{0,8},{4,12},{8,0},{12,4},{16,24},{20,28},{24,16},{28,20},{1,9},{5... | collective-permute-start | bytes 786440 | tf_op jit(solution)/shard_map/ppermute | solution.py:442
  34.8 12.1 %collective-permute-start.9 = (bf16[64,2048]{1,0:T(8,128)(2,1)S(1)}, bf16[64,2048]{1,0:T(8,128)(2,1)S(1)}, u32[]{:S(2)}, u32[]{:S(2)}) collective-permute-start(bf16[64,2048]{1,0:T(8,128)(2,1)S(1)} %get-tuple-element.52), channel_id=1, source_target_pairs={{0,16},{4,20},{8,24},{12,28},{16,0},{20,4},{24,8},{28,12},{1,17},{... | collective-permute-start | bytes 786440 | tf_op jit(solution)/shard_map/ppermute | solution.py:442
  35.6 12.9 %collective-permute-start.10 = (bf16[64,2048]{1,0:T(8,128)(2,1)S(1)}, bf16[64,2048]{1,0:T(8,128)(2,1)S(1)}, u32[]{:S(2)}, u32[]{:S(2)}) collective-permute-start(bf16[64,2048]{1,0:T(8,128)(2,1)S(1)} %get-tuple-element.53), channel_id=1, source_target_pairs={{0,24},{4,28},{8,16},{12,20},{16,8},{20,12},{24,0},{28,4},{1,25},{... | collective-permute-start | bytes 786440 | tf_op jit(solution)/shard_map/ppermute | solution.py:442
  50.1 25.4 %all-to-all-start = ((bf16[8,64,512]{2,1,0:T(8,128)(2,1)}), bf16[8,64,512]{2,1,0:T(8,128)(2,1)S(1)}, u32[]{:S(2)}, u32[]{:S(2)}) async-start(bf16[8,64,512]{2,1,0:T(8,128)(2,1)} %column_grad_hidden.1), calls=%async_computation | async-start | bytes 1048576 | tf_op jit(solution)/shard_map/all_to_all | solution.py:544
  53.6 5.8 %collective-permute-start.11 = (bf16[32,2048]{1,0:T(8,128)(2,1)S(1)}, bf16[32,2048]{1,0:T(8,128)(2,1)S(1)}, u32[]{:S(2)}, u32[]{:S(2)}) collective-permute-start(bf16[32,2048]{1,0:T(8,128)(2,1)S(1)} %get-tuple-element.54), channel_id=1, source_target_pairs={{0,1},{1,0},{2,3},{3,2},{4,5},{5,4},{6,7},{7,6},{8,9},{9,8},{10,11... | collective-permute-start | bytes 393224 | tf_op jit(solution)/shard_map/ppermute | solution.py:442
  59.5 8.7 %collective-permute-start.12 = (bf16[32,2048]{1,0:T(8,128)(2,1)S(1)}, bf16[32,2048]{1,0:T(8,128)(2,1)S(1)}, u32[]{:S(2)}, u32[]{:S(2)}) collective-permute-start(bf16[32,2048]{1,0:T(8,128)(2,1)S(1)} %add_pair.1.kept_ref), channel_id=1, source_target_pairs={{0,2},{1,3},{2,0},{3,1},{4,6},{5,7},{6,4},{7,5},{8,10},{9,11},{10,... | collective-permute-start | bytes 393224 | tf_op jit(solution)/shard_map/ppermute | solution.py:442
  68.2 5.0 %collective-permute-start.13 = (bf16[32,2048]{1,0:T(8,128)(2,1)S(1)}, bf16[32,2048]{1,0:T(8,128)(2,1)S(1)}, u32[]{:S(2)}, u32[]{:S(2)}) collective-permute-start(bf16[32,2048]{1,0:T(8,128)(2,1)S(1)} %add_pairs.1.held_ref), channel_id=1, source_target_pairs={{0,1},{1,0},{2,3},{3,2},{4,5},{5,4},{6,7},{7,6},{8,9},{9,8},{10,11... | collective-permute-start | bytes 393224 | tf_op jit(solution)/shard_map/ppermute | solution.py:442

commit v5 on v4

--- a/solution.py
+++ b/solution.py
@@ -55,24 +55,47 @@
     return jnp.concatenate([jnp.where(lane < HD, x, zero), jnp.where(lane < HD, zero, x)], 0)
 
 
-def pair_step(q2, g2, gt, k, v, kt, vt, mask_at, mask):
-    count = gt.shape[1]
-    scores = dot_nt(k, q2)
-    tail = jnp.where(mask, scores[mask_at:], -1e30)
-    scores = tail if mask_at == 0 else jnp.concatenate([scores[:mask_at], tail], 0)
-    exponent = jnp.exp(scores - jnp.max(scores, 0, keepdims=True))
-    probs = exponent * (1.0 / jnp.sum(exponent, 0, keepdims=True))
-    weights = probs.astype(BF16)
-    both = dot_nn(vt, weights)
-    attended = jnp.concatenate([both[:HD, :count], both[HD:, count:]], 0).astype(BF16)
-    product = gt.astype(F32) * attended.astype(F32)
-    delta = jnp.concatenate(
-        [jnp.sum(product[:HD], 0, keepdims=True), jnp.sum(product[HD:], 0, keepdims=True)], 1
-    )
-    score_grad = (probs * (dot_nt(v, g2) - delta)).astype(BF16)
-    both = dot_nn(kt, score_grad)
-    grad_q = (jnp.concatenate([both[:HD, :count], both[HD:, count:]], 0) * SCALE).astype(BF16)
-    return attended, grad_q, dot_nn(score_grad, q2), dot_nn(weights, g2)
+def both_heads(both, count):
+    return jnp.concatenate([both[:HD, :count], both[HD:, count:]], 0)
+
+
+def pair_steps(items, mask_rows, mask):
+    count = items[0][2].shape[1]
+    scores = [dot_nt(k, q2) for q2, _, _, k, _, _, _ in items]
+    prob_grads = [dot_nt(v, g2) for _, g2, _, _, v, _, _ in items]
+    probs = []
+    for score in scores:
+        first = score.shape[0] - mask_rows
+        tail = jnp.where(mask, score[first:], -1e30)
+        score = tail if first == 0 else jnp.concatenate([score[:first], tail], 0)
+        exponent = jnp.exp(score - jnp.max(score, 0, keepdims=True))
+        probs.append(exponent * (1.0 / jnp.sum(exponent, 0, keepdims=True)))
+    weights = [prob.astype(BF16) for prob in probs]
+    attended = [
+        both_heads(dot_nn(item[6], weight), count).astype(BF16)
+        for item, weight in zip(items, weights)
+    ]
+    score_grads = []
+    for item, att, prob, prob_grad in zip(items, attended, probs, prob_grads):
+        product = item[2].astype(F32) * att.astype(F32)
+        delta = [jnp.sum(part, 0, keepdims=True) for part in (product[:HD], product[HD:])]
+        score_grads.append((prob * (prob_grad - jnp.concatenate(delta, 1))).astype(BF16))
+    grad_q = [
+        (both_heads(dot_nn(item[5], score_grad), count) * SCALE).astype(BF16)
+        for item, score_grad in zip(items, score_grads)
+    ]
+    grad_k = [dot_nn(score_grad, item[0]) for item, score_grad in zip(items, score_grads)]
+    grad_v = [dot_nn(weight, item[1]) for item, weight in zip(items, weights)]
+    return list(zip(attended, grad_q, grad_k, grad_v))
+
+
+def split_cores(piece, core, send_ref, keep_ref, chips, lanes):
+    rows = send_ref.shape[1]
+    parts = piece.reshape(chips.stop - chips.start, 2, rows, piece.shape[1])
+    even, odd = parts[:, 0], parts[:, 1]
+    first = core == 0
+    send_ref[chips, :, lanes] = jnp.where(first, odd, even)
+    keep_ref[chips, :, lanes] = jnp.where(first, even, odd)
 
 
 def qkv_copies(wqkv_ref, w_ref, sems, second):
@@ -113,9 +136,8 @@
     return q * jnp.asarray(SCALE, BF16), k, v, g
 
 
-def row_kernel(
-    x_any, cot_any, gain_any, wqkv_any, wout_any,
-    qkv_ref, out_ref, grads_any,
+def row_part(
+    x_any, cot_any, gain_any, wqkv_any, wout_any, out_ref, grads_any,
     x_ref, cot_ref, gain_ref, w_ref, wo_ref, dk_ref, dv_ref, grads_ref, sems,
 ):
     first = started(
@@ -140,29 +162,43 @@
     step = math.gcd(tokens, QUERY_BLOCK)
     query = lax.broadcasted_iota(jnp.int32, (step, 2 * step), 1) % step
     mask = query >= lax.broadcasted_iota(jnp.int32, (step, 2 * step), 0)
-    att_pairs, dq_pairs = [], []
-    for pair in range(HH // 2):
-        lanes = slice(pair * 2 * HD, (pair + 1) * 2 * HD)
-        atts, dqs = [], []
-        for start in range(0, tokens, step):
-            rows, keys = slice(start, start + step), slice(0, start + step)
-            attended, dq, dk, dv = pair_step(
+    pairs = [slice(i * 2 * HD, (i + 1) * 2 * HD) for i in range(HH // 2)]
+    att_blocks, dq_blocks = [], []
+    for start in range(0, tokens, step):
+        rows, keys = slice(start, start + step), slice(0, start + step)
+        items = [
+            (
                 head_pair(q[rows, lanes]), head_pair(g[rows, lanes]), gt[lanes, rows],
-                k[keys, lanes], v[keys, lanes], kt[lanes, keys], vt[lanes, keys], start, mask,
+                k[keys, lanes], v[keys, lanes], kt[lanes, keys], vt[lanes, keys],
             )
+            for lanes in pairs
+        ]
+        results = pair_steps(items, step, mask)
+        for lanes, (_, _, dk, dv) in zip(pairs, results):
             dk_ref[keys, lanes] += dk
             dv_ref[keys, lanes] += dv
-            atts.append(attended)
-            dqs.append(dq)
-        att_pairs.append(jnp.concatenate(atts, 1))
-        dq_pairs.append(jnp.concatenate(dqs, 1))
-    grads_ref[:, :HW] = transposed(jnp.concatenate(dq_pairs, 0))
+        att_blocks.append(jnp.concatenate([result[0] for result in results], 0))
+        dq_blocks.append(jnp.concatenate([result[1] for result in results], 0))
+    grads_ref[:, :HW] = transposed(jnp.concatenate(dq_blocks, 1))
     grads_ref[:, HW : 2 * HW] = dk_ref[...].astype(BF16)
     grads_ref[:, 2 * HW :] = dv_ref[...].astype(BF16)
     handed = started(pltpu.make_async_copy(grads_ref, grads_any, sems.at[4]))
-    qkv_ref[...] = dot_nn(hidden_t, grads_ref[...]).astype(BF16)
-    out_ref[...] = dot_nn(jnp.concatenate(att_pairs, 0), cot).astype(BF16)
+    term_qkv = dot_nn(hidden_t, grads_ref[...]).astype(BF16)
+    out_ref[...] = dot_nn(jnp.concatenate(att_blocks, 1), cot).astype(BF16)
     finished(*handed)
+    return term_qkv
+
+
+def row_kernel(x_any, cot_any, gain_any, wqkv_any, wout_any, qkv_ref, *refs):
+    qkv_ref[...] = row_part(x_any, cot_any, gain_any, wqkv_any, wout_any, *refs)
+
+
+def row_chip_kernel(
+    place_ref, x_any, cot_any, gain_any, wqkv_any, wout_any, send_ref, keep_ref, *refs
+):
+    term_qkv = row_part(x_any, cot_any, gain_any, wqkv_any, wout_any, *refs)
+    whole = slice(0, send_ref.shape[0]), slice(0, send_ref.shape[2])
+    split_cores(term_qkv, place_ref[1], send_ref, keep_ref, *whole)
 
 
 def column_part(moved_ref, gain_ref, w_ref, wo_ref, weight_waits, grads_ref):
@@ -183,32 +219,36 @@
     _, normed = rms_parts(gathered(0).astype(F32))
     hidden = (normed * gain_ref[...]).astype(BF16)
     hidden_t = transposed(hidden)
+    finished(*weight_waits)
     cot = gathered(1)
-    finished(*weight_waits)
     q, k, v, g = project(hidden, cot, w_ref, wo_ref)
     kt, vt, gt = transposed(k), transposed(v), transposed(g)
     query = lax.broadcasted_iota(jnp.int32, (block, 2 * block), 1) % block
     key = lax.broadcasted_iota(jnp.int32, (block, 2 * block), 0)
     mask = (query >= key) & (query % group == key % group)
-    att_pairs, dq_pairs = [], []
-    for pair in range(HH // 2):
-        lanes = slice(pair * 2 * HD, (pair + 1) * 2 * HD)
-        atts, dqs = [], []
-        for start in range(0, all_rows * share, block):
-            rows = slice(start, start + block)
-            attended, dq, dk, dv = pair_step(
-                head_pair(q[rows, lanes]), head_pair(g[rows, lanes]), gt[lanes, rows],
-                k[rows, lanes], v[rows, lanes], kt[lanes, rows], vt[lanes, rows], 0, mask,
-            )
-            grads_ref[rows, HW + lanes.start : HW + lanes.stop] = dk.astype(BF16)
-            grads_ref[rows, 2 * HW + lanes.start : 2 * HW + lanes.stop] = dv.astype(BF16)
-            atts.append(attended)
-            dqs.append(dq)
-        att_pairs.append(jnp.concatenate(atts, 1))
-        dq_pairs.append(jnp.concatenate(dqs, 1))
-    grads_ref[:, :HW] = transposed(jnp.concatenate(dq_pairs, 0))
+    pairs = [slice(i * 2 * HD, (i + 1) * 2 * HD) for i in range(HH // 2)]
+    blocks = [slice(at, at + block) for at in range(0, all_rows * share, block)]
+    items = [
+        (
+            head_pair(q[rows, lanes]), head_pair(g[rows, lanes]), gt[lanes, rows],
+            k[rows, lanes], v[rows, lanes], kt[lanes, rows], vt[lanes, rows],
+        )
+        for lanes in pairs
+        for rows in blocks
+    ]
+    results = pair_steps(items, block, mask)
+    places = [(lanes, rows) for lanes in pairs for rows in blocks]
+    for (lanes, rows), (_, _, dk, dv) in zip(places, results):
+        grads_ref[rows, HW + lanes.start : HW + lanes.stop] = dk.astype(BF16)
+        grads_ref[rows, 2 * HW + lanes.start : 2 * HW + lanes.stop] = dv.astype(BF16)
+    by_pair = [results[i * len(blocks) : (i + 1) * len(blocks)] for i in range(len(pairs))]
+    attended, grad_q = [
+        jnp.concatenate([jnp.concatenate([r[i] for r in some], 1) for some in by_pair], 0)
+        for i in range(2)
+    ]
+    grads_ref[:, :HW] = transposed(grad_q)
     term_qkv = dot_nn(hidden_t, grads_ref[...]).astype(BF16)
-    term_out = dot_nn(jnp.concatenate(att_pairs, 0), cot).astype(BF16)
+    term_out = dot_nn(attended, cot).astype(BF16)
     return term_qkv, term_out
 
 
@@ -236,7 +276,7 @@
 def column_chip_kernel(
     place_ref, x_any, cot_any, own_any,
     near_1, near_2, near_3, far_1, far_2, far_3,
-    gain_any, wqkv_any, wout_any, row_qkv_ref, row_out_ref,
+    gain_any, wqkv_any, wout_any, row_out_ref,
     send_ref, keep_ref, grads_ref,
     moved_ref, gain_ref, w_ref, wo_ref, sems,
 ):
@@ -245,41 +285,31 @@
     at = pl.multiple_of((chip * 2 + core) * share, share)
     half = pl.multiple_of(core * share, share)
     me, other = chip * 2 + core, chip * 2 + 1 - core
-    copies = [
-        pltpu.make_async_copy(x_any.at[pl.ds(at, share), :], moved_ref.at[me, 0], sems.at[4]),
-        pltpu.make_async_copy(cot_any.at[pl.ds(at, share), :], moved_ref.at[me, 1], sems.at[5]),
-        pltpu.make_async_copy(own_any, moved_ref.at[other], sems.at[6]),
-        pltpu.make_async_copy(gain_any, gain_ref, sems.at[13]),
-    ]
-    for i, (near, far) in enumerate(((near_1, far_1), (near_2, far_2), (near_3, far_3))):
-        there = 2 * (chip ^ (i + 1))
-        for j, (piece, row) in enumerate(((near, there + core), (far, there + 1 - core))):
-            copies.append(
-                pltpu.make_async_copy(
-                    piece.at[:, pl.ds(half, share), :], moved_ref.at[row], sems.at[7 + 2 * i + j]
-                )
-            )
-    started(*copies)
-    weights = started(*weight_copies(wqkv_any, wout_any, w_ref, wo_ref, sems, 1))
-    finished(*copies)
-    term_qkv, term_out = column_part(moved_ref, gain_ref, w_ref, wo_ref, weights, grads_ref)
-    width = moved_ref.shape[3]
-    first = core == 0
-
-    def split(piece, chips, lanes):
-        parts = piece.reshape(chips.stop - chips.start, 2, share, piece.shape[1])
-        even, odd = parts[:, 0], parts[:, 1]
-        send_ref[chips, :, lanes] = jnp.where(first, odd, even)
-        keep_ref[chips, :, lanes] = jnp.where(first, even, odd)
-
+    groups = []
+    for which, source in enumerate((x_any, cot_any)):
+        group = [
+            (source.at[pl.ds(at, share), :], me),
+            (own_any.at[which], other),
+        ]
+        for i, (near, far) in enumerate(((near_1, far_1), (near_2, far_2), (near_3, far_3))):
+            there = 2 * (chip ^ (i + 1))
+            group.append((near.at[which, pl.ds(half, share), :], there + core))
+            group.append((far.at[which, pl.ds(half, share), :], there + 1 - core))
+        base = 5 + which * len(group)
+        groups.append([
+            pltpu.make_async_copy(piece, moved_ref.at[row, which], sems.at[base + i])
+            for i, (piece, row) in enumerate(group)
+        ])
+    first = started(*groups[0], pltpu.make_async_copy(gain_any, gain_ref, sems.at[4]))
+    later = started(*weight_copies(wqkv_any, wout_any, w_ref, wo_ref, sems, 1), *groups[1])
+    finished(*first)
+    term_qkv, term_out = column_part(moved_ref, gain_ref, w_ref, wo_ref, later, grads_ref)
     chips = send_ref.shape[0]
-    for i in range(3):
-        lanes = slice(i * HW, (i + 1) * HW)
-        at = i * width
-        split(row_qkv_ref[:, lanes], slice(0, chips), slice(at, at + HW))
-        split(term_qkv[:, lanes], slice(0, chips), slice(at + HW, at + 2 * HW))
-    split(row_out_ref[...], slice(0, chips // 2), slice(3 * width, 4 * width))
-    split(term_out, slice(chips // 2, chips), slice(3 * width, 4 * width))
+    refs = core, send_ref, keep_ref
+    out_lanes = slice(3 * HW, send_ref.shape[2])
+    split_cores(term_qkv, *refs, slice(0, chips), slice(0, 3 * HW))
+    split_cores(row_out_ref[...], *refs, slice(0, chips // 2), out_lanes)
+    split_cores(term_out, *refs, slice(chips // 2, chips), out_lanes)
 
 
 def back_kernel(grads_ref, wqkv_any, back_ref, w_ref, sems):
@@ -363,12 +393,17 @@
     keep_ref[...] = jnp.where(upper, high, low)
 
 
+def pass_kernel(any_ref, same_ref):
+    pass
+
+
 def add_kernel(kept_ref, got_ref, out_ref):
     out_ref[...] = (kept_ref[...].astype(F32) + got_ref[...].astype(F32)).astype(BF16)
 
 
 def result_kernel(
-    place_ref, held_ref, got_ref, wqkv_any, gain_any, qkv_ref, out_ref, grad_ref,
+    place_ref, row_held, row_got, held_ref, got_ref, wqkv_any, gain_any,
+    qkv_ref, out_ref, grad_ref,
     w_ref, gain_ref, sems,
 ):
     rows = qkv_ref.shape[0]
@@ -378,12 +413,21 @@
         pltpu.make_async_copy(gain_any, gain_ref, sems.at[1]),
     )
     upper = place_ref[2] == 1
-    held, got = held_ref[...].astype(F32), got_ref[...].astype(F32)
     half = rows // 2
-    low, high = jnp.where(upper, got, held), jnp.where(upper, held, got)
-    cut = qkv_ref.shape[1]
-    qkv_ref[:half], qkv_ref[half:] = low[:, :cut], high[:, :cut]
-    out_ref[:half], out_ref[half:] = low[:, cut:], high[:, cut:]
+    width = out_ref.shape[1]
+
+    def ordered(held_ref, got_ref, lanes):
+        held, got = held_ref[:, lanes].astype(F32), got_ref[:, lanes].astype(F32)
+        return (jnp.where(upper, got, held), jnp.where(upper, held, got))
+
+    for i in range(3):
+        lanes = slice(i * HW, (i + 1) * HW)
+        at_row, at_col = i * width, i * width + HW
+        low, high = ordered(row_held, row_got, lanes)
+        qkv_ref[:half, at_row : at_row + HW], qkv_ref[half:, at_row : at_row + HW] = low, high
+        low, high = ordered(held_ref, got_ref, lanes)
+        qkv_ref[:half, at_col : at_col + HW], qkv_ref[half:, at_col : at_col + HW] = low, high
+    out_ref[:half], out_ref[half:] = ordered(held_ref, got_ref, slice(3 * HW, 3 * HW + width))
     finished(*copies)
     total = jnp.sum(qkv_ref[...] * w_ref[...].astype(F32), -1, keepdims=True)
     shape = (rows, gain_ref.shape[1])
@@ -395,7 +439,7 @@
     grad_ref[...] = jnp.sum(jnp.where(same, total / gain, 0.0), 0, keepdims=True)
 
 
-def call(kernel, name, ins, outs, scratch=(), flops=0, vmem=SMALL_VMEM, out_specs=None):
+def call(kernel, name, ins, outs, scratch=(), flops=0, vmem=SMALL_VMEM, out_specs=None, aliases=None):
     out_specs = out_specs or [VMEM] * len(outs)
     places = [pltpu.HBM if spec is HBM else None for spec in out_specs]
     outs = [place(*out) if place else shaped(*out) for place, out in zip(places, outs)]
@@ -410,10 +454,51 @@
         in_specs=[spec for spec, _ in ins],
         out_specs=out_specs,
         scratch_shapes=scratch,
+        input_output_aliases=aliases or {},
         name=name,
         cost_estimate=pl.CostEstimate(flops=flops, bytes_accessed=size, transcendentals=0),
         compiler_params=pltpu.CompilerParams(vmem_limit_bytes=vmem),
     )(*args)
+
+
+def swap(array, axis, bits):
+    count = lax.axis_size(axis)
+    return lax.ppermute(array, axis, [(i, i ^ bits) for i in range(count)])
+
+
+def add_cores(place, keep, got, name):
+    _, rows, wide = keep.shape
+    return call(
+        chip_sum_kernel,
+        name + "_add_cores",
+        [(SMEM, place), (VMEM, keep), (VMEM, got)],
+        [((rows, wide), F32)] + [((rows, wide), BF16)] * 3,
+        [pltpu.VMEM((rows, wide), F32), pltpu.SemaphoreType.DMA],
+        out_specs=[HBM, VMEM, VMEM, VMEM],
+    )
+
+
+def cross_chips(off_1, off_2, off_3):
+    got_3 = swap(off_3, "seq", 6)
+    got_1 = swap(off_1, "seq", 2)
+    got_2 = swap(off_2, "seq", 4)
+    return got_1, got_2, got_3
+
+
+def add_chips(place, owned, got, name):
+    rows, wide = owned.shape
+    return call(
+        layer_sum_kernel,
+        name + "_add_chips",
+        [(SMEM, place), (HBM, owned), *[(VMEM, one) for one in got]],
+        [((rows // 2, wide), BF16), ((rows // 2, wide), F32)],
+        [pltpu.VMEM((rows, wide), F32), pltpu.SemaphoreType.DMA],
+    )
+
+
+def add_two(kept, got, name):
+    (total,) = call(add_kernel, name, [(VMEM, kept), (VMEM, got)], [(kept.shape, BF16)])
+    return total
 
 
 def body(inputs, norm_gain, qkv_weight, out_weight, out_cotan):
@@ -422,7 +507,7 @@
     m = lax.axis_size("dp")
     share = columns // n
     row_share = width // n
-    term_width = 4 * width
+    row_width, col_width = 3 * HW, 3 * HW + width
     x = inputs.reshape(columns, width)
     cot = out_cotan.reshape(columns, width)
     gain = norm_gain.reshape(1, width)
@@ -435,11 +520,8 @@
         pltpu.VMEM((width, 3 * HW), BF16),
         pltpu.VMEM((HW, width), BF16),
     ]
-    small_scratch = [pltpu.VMEM((width, 3 * HW), BF16), pltpu.SemaphoreType.DMA((3,))]
-
-    def swap(array, axis, bits):
-        count = lax.axis_size(axis)
-        return lax.ppermute(array, axis, [(i, i ^ bits) for i in range(count)])
+    weights = [(HBM, gain), (HBM, qkv_weight), (HBM, out_weight)]
+    grads_out = ((columns, 3 * HW), BF16)
 
     if layered:
         packed = call(
@@ -450,19 +532,19 @@
             [pltpu.SemaphoreType.DMA((8,))],
             out_specs=[ANY] * 4,
         )
-        near_3 = swap(packed[3], "seq", 6)
-        near_1 = swap(packed[1], "seq", 2)
-        near_2 = swap(packed[2], "seq", 4)
+        near_1, near_2, near_3 = cross_chips(*packed[1:])
         own = swap(packed[0], "seq", 1)
     else:
         outgoing = jnp.stack([x.reshape(n, share, width), cot.reshape(n, share, width)], 1)
         moved = lax.all_to_all(outgoing, "seq", split_axis=0, concat_axis=0, tiled=True)
 
-    row_qkv, row_out, row_grads = call(
-        row_kernel,
+    split_out = ((chips, row_share, row_width), BF16)
+    term_outs = [split_out] * 2 if layered else [((width, row_width), BF16)]
+    *row_terms, row_out, row_grads = call(
+        row_chip_kernel if layered else row_kernel,
         "row_heads",
-        [(HBM, x), (HBM, cot), (HBM, gain), (HBM, qkv_weight), (HBM, out_weight)],
-        [((width, 3 * HW), BF16), ((HW, width), BF16), ((columns, 3 * HW), BF16)],
+        [(SMEM, place)] * layered + [(HBM, x), (HBM, cot), *weights],
+        [*term_outs, ((HW, width), BF16), grads_out],
         [
             pltpu.VMEM((columns, width), BF16),
             pltpu.VMEM((columns, width), BF16),
@@ -474,83 +556,70 @@
         ],
         5_000_000_000,
         BIG_VMEM,
-        [VMEM, VMEM, HBM],
+        [VMEM] * len(term_outs) + [VMEM, HBM],
     )
     moved_scratch = pltpu.VMEM((n, 2, share, width), BF16)
     if layered:
-        near_1, near_2, near_3, row_qkv = lax.optimization_barrier((near_1, near_2, near_3, row_qkv))
+        row_send, row_keep = row_terms
+        near_1, near_2, near_3, row_send = lax.optimization_barrier(
+            (near_1, near_2, near_3, row_send)
+        )
         far_3, far_1, far_2 = swap(near_3, "seq", 1), swap(near_1, "seq", 1), swap(near_2, "seq", 1)
-    shared = [
-        (HBM, gain), (HBM, qkv_weight), (HBM, out_weight), (VMEM, row_qkv), (VMEM, row_out),
-    ]
-    if layered:
+        row_owned, *row_off = add_cores(place, row_keep, swap(row_send, "seq", 1), "row")
+        row_got = cross_chips(*row_off)
+        own, row_owned = lax.optimization_barrier((own, row_owned))
         send, keep, col_grads = call(
             column_chip_kernel,
             "column_heads",
             [
                 (SMEM, place), (HBM, x), (HBM, cot), (ANY, own),
                 (ANY, near_1), (ANY, near_2), (ANY, near_3),
-                (ANY, far_1), (ANY, far_2), (ANY, far_3), *shared,
+                (ANY, far_1), (ANY, far_2), (ANY, far_3), *weights, (VMEM, row_out),
             ],
-            [((chips, row_share, term_width), BF16)] * 2 + [((columns, 3 * HW), BF16)],
-            [moved_scratch, *weight_scratch, pltpu.SemaphoreType.DMA((14,))],
+            [((chips, row_share, col_width), BF16)] * 2 + [grads_out],
+            [moved_scratch, *weight_scratch, pltpu.SemaphoreType.DMA((21,))],
             4_000_000_000,
             BIG_VMEM,
         )
-        got = swap(send, "seq", 1)
+        send, row_got = lax.optimization_barrier((send, row_got))
+        row_next, row_kept = add_chips(place, row_owned, row_got, "row")
+        row_pair = add_two(row_kept, swap(row_next, "dp", 1), "row_add_pair")
+        keep, row_kept = lax.optimization_barrier((keep, row_kept))
+        owned, *off = add_cores(place, keep, swap(send, "seq", 1), "column")
+        got = cross_chips(*off)
+        col_grads, owned, row_pair = lax.optimization_barrier((col_grads, owned, row_pair))
+        row_held = add_two(row_pair, swap(row_pair, "dp", 2), "row_add_pairs")
     else:
         terms, col_grads = call(
             column_kernel,
             "column_heads",
-            [(ANY, moved), *shared],
-            [((width, term_width), BF16), ((columns, 3 * HW), BF16)],
+            [(ANY, moved), *weights, (VMEM, row_terms[0]), (VMEM, row_out)],
+            [((width, 4 * width), BF16), grads_out],
             [moved_scratch, *weight_scratch, pltpu.SemaphoreType.DMA((6,))],
             4_000_000_000,
             BIG_VMEM,
         )
-    if layered:
-        owned, off_1, off_2, off_3 = call(
-            chip_sum_kernel,
-            "add_cores",
-            [(SMEM, place), (VMEM, keep), (VMEM, got)],
-            [((row_share, term_width), F32)] + [((row_share, term_width), BF16)] * 3,
-            [pltpu.VMEM((row_share, term_width), F32), pltpu.SemaphoreType.DMA],
-            out_specs=[HBM, VMEM, VMEM, VMEM],
-        )
-        got_3 = swap(off_3, "seq", 6)
-        got_1 = swap(off_1, "seq", 2)
-        got_2 = swap(off_2, "seq", 4)
-        col_grads, owned = lax.optimization_barrier((col_grads, owned))
     (back,) = call(
         back_kernel,
         "column_grad_hidden",
         [(VMEM, col_grads), (HBM, qkv_weight)],
         [((n, share, width), BF16)],
-        small_scratch,
+        [pltpu.VMEM((width, 3 * HW), BF16), pltpu.SemaphoreType.DMA((3,))],
         400_000_000,
     )
-    half_rows = (row_share // 2, term_width)
     if layered:
         back, owned = lax.optimization_barrier((back, owned))
-        to_next, kept = call(
-            layer_sum_kernel,
-            "add_chips",
-            [(SMEM, place), (HBM, owned), (VMEM, got_1), (VMEM, got_2), (VMEM, got_3)],
-            [(half_rows, BF16), (half_rows, F32)],
-            [pltpu.VMEM((row_share, term_width), F32), pltpu.SemaphoreType.DMA],
-        )
-        from_next = swap(to_next, "dp", 1)
-        back, to_next = lax.optimization_barrier((back, to_next))
+        to_next, kept = add_chips(place, owned, got, "column")
+        back, kept = lax.optimization_barrier((back, kept))
+        (back,) = call(
+            pass_kernel, "pass_on", [(ANY, back)], [(back.shape, BF16)],
+            out_specs=[ANY], aliases={0: 0},
+        )
+        kept, row_held = lax.optimization_barrier((kept, row_held))
+        pair_sum = add_two(kept, swap(to_next, "dp", 1), "column_add_pair")
+        row_other = swap(row_held, "dp", 1)
+        held = add_two(pair_sum, swap(pair_sum, "dp", 2), "column_add_pairs")
     returned = lax.all_to_all(back, "seq", split_axis=0, concat_axis=0, tiled=True)
-    if layered:
-        (pair_sum,) = call(
-            add_kernel, "add_pair", [(VMEM, kept), (VMEM, from_next)], [(half_rows, BF16)]
-        )
-        from_far = swap(pair_sum, "dp", 2)
-        (held,) = call(
-            add_kernel, "add_pairs", [(VMEM, pair_sum), (VMEM, from_far)], [(half_rows, BF16)]
-        )
-        other = swap(held, "dp", 1)
     (input_grad,) = call(
         input_kernel,
         "input_grad",
@@ -570,11 +639,14 @@
         400_000_000,
     )
     if layered:
+        other = swap(held, "dp", 1)
+        held, input_grad = lax.optimization_barrier((held, input_grad))
         sum_qkv, sum_out, sum_gain = call(
             result_kernel,
             "result",
             [
-                (SMEM, place), (VMEM, held), (VMEM, other), (HBM, qkv_weight), (HBM, gain),
+                (SMEM, place), (VMEM, row_held), (VMEM, row_other), (VMEM, held), (VMEM, other),
+                (HBM, qkv_weight), (HBM, gain),
             ],
             [((row_share, 3 * width), F32), ((row_share, width), F32), ((1, row_share), F32)],
             [
@@ -586,7 +658,7 @@
         sum_gain = sum_gain.reshape(row_share)
     else:
         terms = lax.all_to_all(
-            terms.reshape(n, row_share, term_width), "seq", split_axis=0, concat_axis=0, tiled=True
+            terms.reshape(n, row_share, 4 * width), "seq", split_axis=0, concat_axis=0, tiled=True
         )
         total = jnp.sum(terms.astype(F32), 0)
         for step in range(m.bit_length() - 1):

time: 79.3 us -> 71.8 us (0.905)
  waiting for transfers between devices: 30.3 us -> 15.7 us
  starting transfers between devices: 17.9 us -> 26.3 us
  Pallas kernels: 29.9 us -> 28.4 us
    ppermute x14 -> x21, waiting for transfers between devices: 30.3 us -> 15.7 us  [swap(): return lax.ppermute(array, axis, [(i, i ^ bits) for i in range(count)])]
    ppermute x14 -> x21, starting transfers between devices: 14.3 us -> 22.8 us  [swap(): return lax.ppermute(array, axis, [(i, i ^ bits) for i in range(count)])]
    pallas_call x10 -> x15, Pallas kernels: 29.9 us -> 28.4 us  [call(): pl.pallas_call(kernel, out_shape=outs, in_specs=[spec for spec, _ in ins]...]
  transfers between devices with their start and end apart: 15 -> 22, of which waited for: 9 -> 8; matrix products, arithmetic and copies ran while one was open for 0% -> 0% of each run, Pallas kernels for 18% -> 30%
where the time goes in v5:
time: 71.8 us; the launch traced here: 71.4 us
  Pallas kernels  28.4 us (40%)
  starting transfers between devices  26.3 us (37%)
  waiting for transfers between devices  15.7 us (22%)
  between operations  0.86 us (1%)
    pallas_call x15, Pallas kernels, call(): pl.pallas_call(kernel, out_shape=outs, in_specs=[spec for spec, _ in ins]...  28.4 us
    ppermute x21, starting transfers between devices, swap(): return lax.ppermute(array, axis, [(i, i ^ bits) for i in range(count)])  22.8 us
    ppermute x21, waiting for transfers between devices, swap(): return lax.ppermute(array, axis, [(i, i ^ bits) for i in range(count)])  15.7 us
    all_to_all x1, starting transfers between devices, body(): lax.all_to_all(back, 'seq', split_axis=0, concat_axis=0, tiled=True)  3.51 us
  transfers between devices with their start and end apart: 22, of which 8 were waited for; matrix products, arithmetic and copies ran while one was open for 0% of the time, Pallas kernels for 30%

profile of v5, /device:TPU:0, one launch (start us, length us, event | category | flops | bytes accessed | tf_op | source)
XLA Modules:
  0.0 71.4 jit_solution(683156816760751199)
XLA Ops:
  0.7 0.1 pad_add_fusion.place_ref
  0.7 1.9 %pack_columns.1 = (bf16[2,64,512]{2,1,0:T(8,128)(2,1)S(1)}, bf16[2,128,512]{2,1,0:T(8,128)(2,1)S(1)}, bf16[2,128,512]{2,1,0:T(8,128)(2,1)S(1)}, bf16[2,128,512]{2,1,0:T(8,128)(2,1)S(1)}) custom-call(s32[3]{0:T(128)S(1)} %pad_add_fusion.place_ref, bf16[512,512]{1,0:T(8,128)(2,1)} %bitcast.10, bf16[512,512]{1,0:T(8,128)(2,1)} %bitcast.14), custom_call_target="tpu_custom_call" | custom-call | bytes 1966092 | tf_op jit(solution)/shard_map/pack_columns/pallas_call | solution.py:451
  2.6 3.0 %collective-permute-start.1 = (bf16[2,128,512]{2,1,0:T(8,128)(2,1)S(1)}, bf16[2,128,512]{2,1,0:T(8,128)(2,1)S(1)}, u32[]{:S(2)}, u32[]{:S(2)}) collective-permute-start(bf16[2,128,512]{2,1,0:T(8,128)(2,1)S(1)} %get-tuple-element.54), channel_id=1, source_target_pairs={{0,8},{4,12},{8,0},{12,4},{16,24},{20,28},{24,16},{28,20},{1,9},{5... | collective-permute-start | bytes 786440 | tf_op jit(solution)/shard_map/ppermute | solution.py:466
  5.6 1.5 %collective-permute-start.2 = (bf16[2,128,512]{2,1,0:T(8,128)(2,1)S(1)}, bf16[2,128,512]{2,1,0:T(8,128)(2,1)S(1)}, u32[]{:S(2)}, u32[]{:S(2)}) collective-permute-start(bf16[2,128,512]{2,1,0:T(8,128)(2,1)S(1)} %get-tuple-element.55), channel_id=1, source_target_pairs={{0,16},{4,20},{8,24},{12,28},{16,0},{20,4},{24,8},{28,12},{1,17},{... | collective-permute-start | bytes 786440 | tf_op jit(solution)/shard_map/ppermute | solution.py:466
  7.1 0.0 collective-permute-start.3
  7.1 7.4 %row_heads.1 = (bf16[4,64,768]{2,1,0:T(8,128)(2,1)S(1)}, bf16[4,64,768]{2,1,0:T(8,128)(2,1)S(1)}, bf16[256,512]{1,0:T(8,128)(2,1)S(1)}, bf16[512,768]{1,0:T(8,128)(2,1)}) custom-call(s32[3]{0:T(128)S(1)} %pad_add_fusion.place_ref, bf16[512,512]{1,0:T(8,128)(2,1)} %bitcast.11, bf16[512,512]{1,0:T(8,128)(2,1)} %bitcast.15, f32[1,512]{1,0:T(1,128)} %bitcast.19, ...), custom_call_target="tpu_custom_call" | custom-call | flops 5000000000 | bytes 4982796 | tf_op jit(solution)/shard_map/row_heads/pallas_call | solution.py:451
  14.6 4.4 %collective-permute-done.2.near_2 = bf16[2,128,512]{2,1,0:T(8,128)(2,1)S(1)} collective-permute-done((bf16[2,128,512]{2,1,0:T(8,128)(2,1)S(1)}, bf16[2,128,512]{2,1,0:T(8,128)(2,1)S(1)}, u32[]{:S(2)}, u32[]{:S(2)}) %collective-permute-start.2) | collective-permute-done | bytes 262176 | tf_op jit(solution)/shard_map/ppermute | solution.py:466
  19.0 0.0 collective-permute-start.4
  19.0 0.5 collective-permute-start.5
  19.5 0.0 collective-permute-start.6
  19.5 0.5 collective-permute-start.7
  20.0 0.0 collective-permute-start
  20.0 0.7 collective-permute-done.4.got_ref
  20.7 1.2 %row_add_cores.1 = (f32[64,768]{1,0:T(8,128)}, bf16[64,768]{1,0:T(8,128)(2,1)S(1)}, bf16[64,768]{1,0:T(8,128)(2,1)S(1)}, bf16[64,768]{1,0:T(8,128)(2,1)S(1)}) custom-call(s32[3]{0:T(128)S(1)} %pad_add_fusion.place_ref, bf16[4,64,768]{2,1,0:T(8,128)(2,1)S(1)} %get-tuple-element.53.keep_ref, bf16[4,64,768]{2,1,0:T(8,128)(2,1)S(1)} %collective-permute-done.4.got_ref), custom_call_target="tpu_custom_call" | custom-call | bytes 1277964 | tf_op jit(solution)/shard_map/row_add_cores/pallas_call | solution.py:451
  22.0 0.1 collective-permute-done.own_any
  22.0 1.3 %collective-permute-start.8 = (bf16[64,768]{1,0:T(8,128)(2,1)S(1)}, bf16[64,768]{1,0:T(8,128)(2,1)S(1)}, u32[]{:S(2)}, u32[]{:S(2)}) collective-permute-start(bf16[64,768]{1,0:T(8,128)(2,1)S(1)} %get-tuple-element.69), channel_id=1, source_target_pairs={{0,8},{4,12},{8,0},{12,4},{16,24},{20,28},{24,16},{28,20},{1,9},{5... | collective-permute-start | bytes 294920 | tf_op jit(solution)/shard_map/ppermute | solution.py:466
  23.3 0.8 %collective-permute-start.9 = (bf16[64,768]{1,0:T(8,128)(2,1)S(1)}, bf16[64,768]{1,0:T(8,128)(2,1)S(1)}, u32[]{:S(2)}, u32[]{:S(2)}) collective-permute-start(bf16[64,768]{1,0:T(8,128)(2,1)S(1)} %get-tuple-element.70), channel_id=1, source_target_pairs={{0,16},{4,20},{8,24},{12,28},{16,0},{20,4},{24,8},{28,12},{1,17},{... | collective-permute-start | bytes 294920 | tf_op jit(solution)/shard_map/ppermute | solution.py:466
  24.1 1.4 %collective-permute-start.10 = (bf16[64,768]{1,0:T(8,128)(2,1)S(1)}, bf16[64,768]{1,0:T(8,128)(2,1)S(1)}, u32[]{:S(2)}, u32[]{:S(2)}) collective-permute-start(bf16[64,768]{1,0:T(8,128)(2,1)S(1)} %get-tuple-element.71), channel_id=1, source_target_pairs={{0,24},{4,28},{8,16},{12,20},{16,8},{20,12},{24,0},{28,4},{1,25},{... | collective-permute-start | bytes 294920 | tf_op jit(solution)/shard_map/ppermute | solution.py:466
  25.5 0.0 collective-permute-done.6.far_2
  25.5 0.0 collective-permute-done.7.far_3
  25.5 5.3 %column_heads.1 = (bf16[4,64,1280]{2,1,0:T(8,128)(2,1)S(1)}, bf16[4,64,1280]{2,1,0:T(8,128)(2,1)S(1)}, bf16[512,768]{1,0:T(8,128)(2,1)S(1)}) custom-call(s32[3]{0:T(128)S(1)} %pad_add_fusion.place_ref, bf16[512,512]{1,0:T(8,128)(2,1)} %bitcast.12, bf16[512,512]{1,0:T(8,128)(2,1)} %bitcast.16, bf16[2,64,512]{2,1,0:T(8,128)(2,1)S(1)} %collective-permute-done.own_any, ...), custom_call_target="tpu_custom_call" | custom-call | flops 4000000000 | bytes 7211020 | tf_op jit(solution)/shard_map/column_heads/pallas_call | solution.py:451
  30.9 0.0 collective-permute-done.9.got_2
  30.9 0.0 collective-permute-done.10.got_3
  30.9 0.1 collective-permute-start.11
  31.0 1.5 %row_add_chips.1 = (bf16[32,768]{1,0:T(8,128)(2,1)S(1)}, f32[32,768]{1,0:T(8,128)S(1)}) custom-call(s32[3]{0:T(128)S(1)} %pad_add_fusion.place_ref, f32[64,768]{1,0:T(8,128)} %get-tuple-element.67.own_any, bf16[64,768]{1,0:T(8,128)(2,1)S(1)} %collective-permute-done.8.got_1, bf16[64,768]{1,0:T(8,128)(2,1)S(1)} %collective-permute-done.9.got_2, ...), custom_call_target="tpu_custom_call" | custom-call | bytes 638988 | tf_op jit(solution)/shard_map/row_add_chips/pallas_call | solution.py:451
  32.5 0.6 collective-permute-done.11.got_ref
  33.1 1.3 %column_add_cores.1 = (f32[64,1280]{1,0:T(8,128)}, bf16[64,1280]{1,0:T(8,128)(2,1)S(1)}, bf16[64,1280]{1,0:T(8,128)(2,1)S(1)}, bf16[64,1280]{1,0:T(8,128)(2,1)S(1)}) custom-call(s32[3]{0:T(128)S(1)} %pad_add_fusion.place_ref, bf16[4,64,1280]{2,1,0:T(8,128)(2,1)S(1)} %get-tuple-element.76.keep_ref, bf16[4,64,1280]{2,1,0:T(8,128)(2,1)S(1)} %collective-permute-done.11.got_ref), custom_call_target="tpu_custom_call" | custom-call | bytes 2129932 | tf_op jit(solution)/shard_map/column_add_cores/pallas_call | solution.py:451
  34.4 1.3 %collective-permute-start.13 = (bf16[64,1280]{1,0:T(8,128)(2,1)S(1)}, bf16[64,1280]{1,0:T(8,128)(2,1)S(1)}, u32[]{:S(2)}, u32[]{:S(2)}) collective-permute-start(bf16[64,1280]{1,0:T(8,128)(2,1)S(1)} %get-tuple-element.84), channel_id=1, source_target_pairs={{0,8},{4,12},{8,0},{12,4},{16,24},{20,28},{24,16},{28,20},{1,9},{5... | collective-permute-start | bytes 491528 | tf_op jit(solution)/shard_map/ppermute | solution.py:466
  35.7 0.8 %collective-permute-start.14 = (bf16[64,1280]{1,0:T(8,128)(2,1)S(1)}, bf16[64,1280]{1,0:T(8,128)(2,1)S(1)}, u32[]{:S(2)}, u32[]{:S(2)}) collective-permute-start(bf16[64,1280]{1,0:T(8,128)(2,1)S(1)} %get-tuple-element.85), channel_id=1, source_target_pairs={{0,16},{4,20},{8,24},{12,28},{16,0},{20,4},{24,8},{28,12},{1,17},{... | collective-permute-start | bytes 491528 | tf_op jit(solution)/shard_map/ppermute | solution.py:466
  36.5 1.4 %collective-permute-start.15 = (bf16[64,1280]{1,0:T(8,128)(2,1)S(1)}, bf16[64,1280]{1,0:T(8,128)(2,1)S(1)}, u32[]{:S(2)}, u32[]{:S(2)}) collective-permute-start(bf16[64,1280]{1,0:T(8,128)(2,1)S(1)} %get-tuple-element.86), channel_id=1, source_target_pairs={{0,24},{4,28},{8,16},{12,20},{16,8},{20,12},{24,0},{28,4},{1,25},{... | collective-permute-start | bytes 491528 | tf_op jit(solution)/shard_map/ppermute | solution.py:466
  38.0 1.6 %collective-permute-start.12 = (bf16[32,768]{1,0:T(8,128)(2,1)S(1)}, bf16[32,768]{1,0:T(8,128)(2,1)S(1)}, u32[]{:S(2)}, u32[]{:S(2)}) collective-permute-start(bf16[32,768]{1,0:T(8,128)(2,1)S(1)} %get-tuple-element.79), channel_id=1, source_target_pairs={{0,1},{1,0},{2,3},{3,2},{4,5},{5,4},{6,7},{7,6},{8,9},{9,8},{10,11... | collective-permute-start | bytes 147464 | tf_op jit(solution)/shard_map/ppermute | solution.py:466
  39.5 2.5 %collective-permute-done.12.got_ref = bf16[32,768]{1,0:T(8,128)(2,1)S(1)} collective-permute-done((bf16[32,768]{1,0:T(8,128)(2,1)S(1)}, bf16[32,768]{1,0:T(8,128)(2,1)S(1)}, u32[]{:S(2)}, u32[]{:S(2)}) %collective-permute-start.12) | collective-permute-done | bytes 49184 | tf_op jit(solution)/shard_map/ppermute | solution.py:466
  42.1 2.5 %column_grad_hidden.1.any_ref = bf16[8,64,512]{2,1,0:T(8,128)(2,1)} custom-call(bf16[512,768]{1,0:T(8,128)(2,1)S(1)} %get-tuple-element.80.grads_ref, bf16[512,1536]{1,0:T(8,128)(2,1)} %wqkv_any.9), custom_call_target="tpu_custom_call" | custom-call | flops 400000000 | bytes 2883584 | tf_op jit(solution)/shard_map/column_grad_hidden/pallas_call | solution.py:451
  44.6 0.0 collective-permute-done.14.got_2
  44.7 0.5 collective-permute-done.15.got_3
  45.2 1.6 %column_add_chips.1 = (bf16[32,1280]{1,0:T(8,128)(2,1)S(1)}, f32[32,1280]{1,0:T(8,128)S(1)}) custom-call(s32[3]{0:T(128)S(1)} %pad_add_fusion.place_ref, f32[64,1280]{1,0:T(8,128)} %get-tuple-element.83.own_any, bf16[64,1280]{1,0:T(8,128)(2,1)S(1)} %collective-permute-done.13.got_1, bf16[64,1280]{1,0:T(8,128)(2,1)S(1)} %collective-permute-done.14.got_2, ...), custom_call_target="tpu_custom_call" | custom-call | bytes 1064972 | tf_op jit(solution)/shard_map/column_add_chips/pallas_call | solution.py:451
  46.8 3.5 %all-to-all-start = ((bf16[8,64,512]{2,1,0:T(8,128)(2,1)}), bf16[8,64,512]{2,1,0:T(8,128)(2,1)S(1)}, u32[]{:S(2)}, u32[]{:S(2)}) async-start(bf16[8,64,512]{2,1,0:T(8,128)(2,1)} %pass_on.1), calls=%async_computation | async-start | bytes 1048576 | tf_op jit(solution)/shard_map/all_to_all | solution.py:622
  50.3 1.6 %collective-permute-start.17 = (bf16[32,1280]{1,0:T(8,128)(2,1)S(1)}, bf16[32,1280]{1,0:T(8,128)(2,1)S(1)}, u32[]{:S(2)}, u32[]{:S(2)}) collective-permute-start(bf16[32,1280]{1,0:T(8,128)(2,1)S(1)} %get-tuple-element.91), channel_id=1, source_target_pairs={{0,1},{1,0},{2,3},{3,2},{4,5},{5,4},{6,7},{7,6},{8,9},{9,8},{10,11... | collective-permute-start | bytes 245768 | tf_op jit(solution)/shard_map/ppermute | solution.py:466
  51.9 2.6 %collective-permute-start.16 = (bf16[32,768]{1,0:T(8,128)(2,1)S(1)}, bf16[32,768]{1,0:T(8,128)(2,1)S(1)}, u32[]{:S(2)}, u32[]{:S(2)}) collective-permute-start(bf16[32,768]{1,0:T(8,128)(2,1)S(1)} %row_add_pair.1.kept_ref), channel_id=1, source_target_pairs={{0,2},{1,3},{2,0},{3,1},{4,6},{5,7},{6,4},{7,5},{8,10},{9,11},{10,... | collective-permute-start | bytes 147464 | tf_op jit(solution)/shard_map/ppermute | solution.py:466
  54.5 2.8 %collective-permute-done.16.got_ref = bf16[32,768]{1,0:T(8,128)(2,1)S(1)} collective-permute-done((bf16[32,768]{1,0:T(8,128)(2,1)S(1)}, bf16[32,768]{1,0:T(8,128)(2,1)S(1)}, u32[]{:S(2)}, u32[]{:S(2)}) %collective-permute-start.16) | collective-permute-done | bytes 49184 | tf_op jit(solution)/shard_map/ppermute | solution.py:466
  57.4 0.0 collective-permute-done.17.got_ref
  57.4 2.2 %collective-permute-start.18 = (bf16[32,1280]{1,0:T(8,128)(2,1)S(1)}, bf16[32,1280]{1,0:T(8,128)(2,1)S(1)}, u32[]{:S(2)}, u32[]{:S(2)}) collective-permute-start(bf16[32,1280]{1,0:T(8,128)(2,1)S(1)} %column_add_pair.1.kept_ref), channel_id=1, source_target_pairs={{0,2},{1,3},{2,0},{3,1},{4,6},{5,7},{6,4},{7,5},{8,10},{9,11},{10,... | collective-permute-start | bytes 245768 | tf_op jit(solution)/shard_map/ppermute | solution.py:466
  59.6 4.1 %collective-permute-done.18.got_ref = bf16[32,1280]{1,0:T(8,128)(2,1)S(1)} collective-permute-done((bf16[32,1280]{1,0:T(8,128)(2,1)S(1)}, bf16[32,1280]{1,0:T(8,128)(2,1)S(1)}, u32[]{:S(2)}, u32[]{:S(2)}) %collective-permute-start.18) | collective-permute-done | bytes 81952 | tf_op jit(solution)/shard_map/ppermute | solution.py:466
  63.7 0.6 collective-permute-start.20
  64.3 1.5 %collective-permute-start.19 = (bf16[32,768]{1,0:T(8,128)(2,1)S(1)}, bf16[32,768]{1,0:T(8,128)(2,1)S(1)}, u32[]{:S(2)}, u32[]{:S(2)}) collective-permute-start(bf16[32,768]{1,0:T(8,128)(2,1)S(1)} %row_add_pairs.1.row_held), channel_id=1, source_target_pairs={{0,1},{1,0},{2,3},{3,2},{4,5},{5,4},{6,7},{7,6},{8,9},{9,8},{10,11... | collective-permute-start | bytes 147464 | tf_op jit(solution)/shard_map/ppermute | solution.py:466
  65.8 0.0 all-to-all-done
  65.8 3.3 %input_grad.1 = bf16[512,512]{1,0:T(8,128)(2,1)} custom-call(bf16[512,512]{1,0:T(8,128)(2,1)} %bitcast.13, bf16[512,512]{1,0:T(8,128)(2,1)} %bitcast.17, f32[1,512]{1,0:T(1,128)} %bitcast.21, bf16[512,768]{1,0:T(8,128)(2,1)} %get-tuple-element.92.grads_any, bf16[512,1536]{1,0:T(8,128)(2,1)} %wqkv_any.9, bf16[512,512]{1,0:T(8,128)(2,1)S(1)} %bitcast.9), custom_call_target="tpu_custom_call" | custom-call | flops 400000000 | bytes 4458496 | tf_op jit(solution)/shard_map/input_grad/pallas_call | solution.py:451
  69.1 2.3 %result.1 = (f32[64,1536]{1,0:T(8,128)}, f32[64,512]{1,0:T(8,128)}, f32[1,64]{1,0:T(1,128)}) custom-call(s32[3]{0:T(128)S(1)} %pad_add_fusion.place_ref, bf16[32,768]{1,0:T(8,128)(2,1)S(1)} %row_add_pairs.1.row_held, bf16[32,768]{1,0:T(8,128)(2,1)S(1)} %collective-permute-done.19.row_got, bf16[32,1280]{1,0:T(8,128)(2,1)S(1)} %column_add_pairs.1.held_ref, ...), custom_call_target="tpu_custom_call" | custom-call | bytes 2361612 | tf_op jit(solution)/shard_map/result/pallas_call | solution.py:451
  (12 shorter events, 0.1 us)
Async XLA Ops:
  2.6 12.0 %collective-permute-start.1 = (bf16[2,128,512]{2,1,0:T(8,128)(2,1)S(1)}, bf16[2,128,512]{2,1,0:T(8,128)(2,1)S(1)}, u32[]{:S(2)}, u32[]{:S(2)}) collective-permute-start(bf16[2,128,512]{2,1,0:T(8,128)(2,1)S(1)} %get-tuple-element.54), channel_id=1, source_target_pairs={{0,8},{4,12},{8,0},{12,4},{16,24},{20,28},{24,16},{28,20},{1,9},{5... | collective-permute-start | bytes 786440 | tf_op jit(solution)/shard_map/ppermute | solution.py:466
  5.6 13.4 %collective-permute-start.2 = (bf16[2,128,512]{2,1,0:T(8,128)(2,1)S(1)}, bf16[2,128,512]{2,1,0:T(8,128)(2,1)S(1)}, u32[]{:S(2)}, u32[]{:S(2)}) collective-permute-start(bf16[2,128,512]{2,1,0:T(8,128)(2,1)S(1)} %get-tuple-element.55), channel_id=1, source_target_pairs={{0,16},{4,20},{8,24},{12,28},{16,0},{20,4},{24,8},{28,12},{1,17},{... | collective-permute-start | bytes 786440 | tf_op jit(solution)/shard_map/ppermute | solution.py:466
  7.1 11.9 %collective-permute-start.3 = (bf16[2,128,512]{2,1,0:T(8,128)(2,1)S(1)}, bf16[2,128,512]{2,1,0:T(8,128)(2,1)S(1)}, u32[]{:S(2)}, u32[]{:S(2)}) collective-permute-start(bf16[2,128,512]{2,1,0:T(8,128)(2,1)S(1)} %get-tuple-element.56), channel_id=1, source_target_pairs={{0,24},{4,28},{8,16},{12,20},{16,8},{20,12},{24,0},{28,4},{1,25},{... | collective-permute-start | bytes 786440 | tf_op jit(solution)/shard_map/ppermute | solution.py:466
  19.0 1.7 %collective-permute-start.4 = (bf16[4,64,768]{2,1,0:T(8,128)(2,1)S(1)}, bf16[4,64,768]{2,1,0:T(8,128)(2,1)S(1)}, u32[]{:S(2)}, u32[]{:S(2)}) collective-permute-start(bf16[4,64,768]{2,1,0:T(8,128)(2,1)S(1)} %get-tuple-element.58), channel_id=1, source_target_pairs={{0,4},{4,0},{8,12},{12,8},{16,20},{20,16},{24,28},{28,24},{1,5},{5... | collective-permute-start | bytes 1179656 | tf_op jit(solution)/shard_map/ppermute | solution.py:466
  19.0 5.1 %collective-permute-start.5 = (bf16[2,128,512]{2,1,0:T(8,128)(2,1)S(1)}, bf16[2,128,512]{2,1,0:T(8,128)(2,1)S(1)}, u32[]{:S(2)}, u32[]{:S(2)}) collective-permute-start(bf16[2,128,512]{2,1,0:T(8,128)(2,1)S(1)} %collective-permute-done.1.near_1), channel_id=1, source_target_pairs={{0,4},{4,0},{8,12},{12,8},{16,20},{20,16},{24,28},{28,24},{1,5},{5... | collective-permute-start | bytes 786440 | tf_op jit(solution)/shard_map/ppermute | solution.py:466
  19.5 6.0 %collective-permute-start.6 = (bf16[2,128,512]{2,1,0:T(8,128)(2,1)S(1)}, bf16[2,128,512]{2,1,0:T(8,128)(2,1)S(1)}, u32[]{:S(2)}, u32[]{:S(2)}) collective-permute-start(bf16[2,128,512]{2,1,0:T(8,128)(2,1)S(1)} %collective-permute-done.2.near_2), channel_id=1, source_target_pairs={{0,4},{4,0},{8,12},{12,8},{16,20},{20,16},{24,28},{28,24},{1,5},{5... | collective-permute-start | bytes 786440 | tf_op jit(solution)/shard_map/ppermute | solution.py:466
  19.5 6.0 %collective-permute-start.7 = (bf16[2,128,512]{2,1,0:T(8,128)(2,1)S(1)}, bf16[2,128,512]{2,1,0:T(8,128)(2,1)S(1)}, u32[]{:S(2)}, u32[]{:S(2)}) collective-permute-start(bf16[2,128,512]{2,1,0:T(8,128)(2,1)S(1)} %collective-permute-done.3.near_3), channel_id=1, source_target_pairs={{0,4},{4,0},{8,12},{12,8},{16,20},{20,16},{24,28},{28,24},{1,5},{5... | collective-permute-start | bytes 786440 | tf_op jit(solution)/shard_map/ppermute | solution.py:466
  20.0 2.0 %collective-permute-start = (bf16[2,64,512]{2,1,0:T(8,128)(2,1)S(1)}, bf16[2,64,512]{2,1,0:T(8,128)(2,1)S(1)}, u32[]{:S(2)}, u32[]{:S(2)}) collective-permute-start(bf16[2,64,512]{2,1,0:T(8,128)(2,1)S(1)} %get-tuple-element.52), channel_id=1, source_target_pairs={{0,4},{4,0},{8,12},{12,8},{16,20},{20,16},{24,28},{28,24},{1,5},{5... | collective-permute-start | bytes 393224 | tf_op jit(solution)/shard_map/ppermute | solution.py:466
  22.0 8.9 %collective-permute-start.8 = (bf16[64,768]{1,0:T(8,128)(2,1)S(1)}, bf16[64,768]{1,0:T(8,128)(2,1)S(1)}, u32[]{:S(2)}, u32[]{:S(2)}) collective-permute-start(bf16[64,768]{1,0:T(8,128)(2,1)S(1)} %get-tuple-element.69), channel_id=1, source_target_pairs={{0,8},{4,12},{8,0},{12,4},{16,24},{20,28},{24,16},{28,20},{1,9},{5... | collective-permute-start | bytes 294920 | tf_op jit(solution)/shard_map/ppermute | solution.py:466
  23.3 7.6 %collective-permute-start.9 = (bf16[64,768]{1,0:T(8,128)(2,1)S(1)}, bf16[64,768]{1,0:T(8,128)(2,1)S(1)}, u32[]{:S(2)}, u32[]{:S(2)}) collective-permute-start(bf16[64,768]{1,0:T(8,128)(2,1)S(1)} %get-tuple-element.70), channel_id=1, source_target_pairs={{0,16},{4,20},{8,24},{12,28},{16,0},{20,4},{24,8},{28,12},{1,17},{... | collective-permute-start | bytes 294920 | tf_op jit(solution)/shard_map/ppermute | solution.py:466
  24.1 6.8 %collective-permute-start.10 = (bf16[64,768]{1,0:T(8,128)(2,1)S(1)}, bf16[64,768]{1,0:T(8,128)(2,1)S(1)}, u32[]{:S(2)}, u32[]{:S(2)}) collective-permute-start(bf16[64,768]{1,0:T(8,128)(2,1)S(1)} %get-tuple-element.71), channel_id=1, source_target_pairs={{0,24},{4,28},{8,16},{12,20},{16,8},{20,12},{24,0},{28,4},{1,25},{... | collective-permute-start | bytes 294920 | tf_op jit(solution)/shard_map/ppermute | solution.py:466
  30.9 2.2 %collective-permute-start.11 = (bf16[4,64,1280]{2,1,0:T(8,128)(2,1)S(1)}, bf16[4,64,1280]{2,1,0:T(8,128)(2,1)S(1)}, u32[]{:S(2)}, u32[]{:S(2)}) collective-permute-start(bf16[4,64,1280]{2,1,0:T(8,128)(2,1)S(1)} %get-tuple-element.77), channel_id=1, source_target_pairs={{0,4},{4,0},{8,12},{12,8},{16,20},{20,16},{24,28},{28,24},{1,5},{5... | collective-permute-start | bytes 1966088 | tf_op jit(solution)/shard_map/ppermute | solution.py:466
  34.4 10.2 %collective-permute-start.13 = (bf16[64,1280]{1,0:T(8,128)(2,1)S(1)}, bf16[64,1280]{1,0:T(8,128)(2,1)S(1)}, u32[]{:S(2)}, u32[]{:S(2)}) collective-permute-start(bf16[64,1280]{1,0:T(8,128)(2,1)S(1)} %get-tuple-element.84), channel_id=1, source_target_pairs={{0,8},{4,12},{8,0},{12,4},{16,24},{20,28},{24,16},{28,20},{1,9},{5... | collective-permute-start | bytes 491528 | tf_op jit(solution)/shard_map/ppermute | solution.py:466
  35.7 8.9 %collective-permute-start.14 = (bf16[64,1280]{1,0:T(8,128)(2,1)S(1)}, bf16[64,1280]{1,0:T(8,128)(2,1)S(1)}, u32[]{:S(2)}, u32[]{:S(2)}) collective-permute-start(bf16[64,1280]{1,0:T(8,128)(2,1)S(1)} %get-tuple-element.85), channel_id=1, source_target_pairs={{0,16},{4,20},{8,24},{12,28},{16,0},{20,4},{24,8},{28,12},{1,17},{... | collective-permute-start | bytes 491528 | tf_op jit(solution)/shard_map/ppermute | solution.py:466
  36.5 8.7 %collective-permute-start.15 = (bf16[64,1280]{1,0:T(8,128)(2,1)S(1)}, bf16[64,1280]{1,0:T(8,128)(2,1)S(1)}, u32[]{:S(2)}, u32[]{:S(2)}) collective-permute-start(bf16[64,1280]{1,0:T(8,128)(2,1)S(1)} %get-tuple-element.86), channel_id=1, source_target_pairs={{0,24},{4,28},{8,16},{12,20},{16,8},{20,12},{24,0},{28,4},{1,25},{... | collective-permute-start | bytes 491528 | tf_op jit(solution)/shard_map/ppermute | solution.py:466
  38.0 4.1 %collective-permute-start.12 = (bf16[32,768]{1,0:T(8,128)(2,1)S(1)}, bf16[32,768]{1,0:T(8,128)(2,1)S(1)}, u32[]{:S(2)}, u32[]{:S(2)}) collective-permute-start(bf16[32,768]{1,0:T(8,128)(2,1)S(1)} %get-tuple-element.79), channel_id=1, source_target_pairs={{0,1},{1,0},{2,3},{3,2},{4,5},{5,4},{6,7},{7,6},{8,9},{9,8},{10,11... | collective-permute-start | bytes 147464 | tf_op jit(solution)/shard_map/ppermute | solution.py:466
  46.8 19.0 %all-to-all-start = ((bf16[8,64,512]{2,1,0:T(8,128)(2,1)}), bf16[8,64,512]{2,1,0:T(8,128)(2,1)S(1)}, u32[]{:S(2)}, u32[]{:S(2)}) async-start(bf16[8,64,512]{2,1,0:T(8,128)(2,1)} %pass_on.1), calls=%async_computation | async-start | bytes 1048576 | tf_op jit(solution)/shard_map/all_to_all | solution.py:622
  50.3 7.1 %collective-permute-start.17 = (bf16[32,1280]{1,0:T(8,128)(2,1)S(1)}, bf16[32,1280]{1,0:T(8,128)(2,1)S(1)}, u32[]{:S(2)}, u32[]{:S(2)}) collective-permute-start(bf16[32,1280]{1,0:T(8,128)(2,1)S(1)} %get-tuple-element.91), channel_id=1, source_target_pairs={{0,1},{1,0},{2,3},{3,2},{4,5},{5,4},{6,7},{7,6},{8,9},{9,8},{10,11... | collective-permute-start | bytes 245768 | tf_op jit(solution)/shard_map/ppermute | solution.py:466
  51.9 5.4 %collective-permute-start.16 = (bf16[32,768]{1,0:T(8,128)(2,1)S(1)}, bf16[32,768]{1,0:T(8,128)(2,1)S(1)}, u32[]{:S(2)}, u32[]{:S(2)}) collective-permute-start(bf16[32,768]{1,0:T(8,128)(2,1)S(1)} %row_add_pair.1.kept_ref), channel_id=1, source_target_pairs={{0,2},{1,3},{2,0},{3,1},{4,6},{5,7},{6,4},{7,5},{8,10},{9,11},{10,... | collective-permute-start | bytes 147464 | tf_op jit(solution)/shard_map/ppermute | solution.py:466
  57.4 6.3 %collective-permute-start.18 = (bf16[32,1280]{1,0:T(8,128)(2,1)S(1)}, bf16[32,1280]{1,0:T(8,128)(2,1)S(1)}, u32[]{:S(2)}, u32[]{:S(2)}) collective-permute-start(bf16[32,1280]{1,0:T(8,128)(2,1)S(1)} %column_add_pair.1.kept_ref), channel_id=1, source_target_pairs={{0,2},{1,3},{2,0},{3,1},{4,6},{5,7},{6,4},{7,5},{8,10},{9,11},{10,... | collective-permute-start | bytes 245768 | tf_op jit(solution)/shard_map/ppermute | solution.py:466
  63.7 5.4 %collective-permute-start.20 = (bf16[32,1280]{1,0:T(8,128)(2,1)S(1)}, bf16[32,1280]{1,0:T(8,128)(2,1)S(1)}, u32[]{:S(2)}, u32[]{:S(2)}) collective-permute-start(bf16[32,1280]{1,0:T(8,128)(2,1)S(1)} %column_add_pairs.1.held_ref), channel_id=1, source_target_pairs={{0,1},{1,0},{2,3},{3,2},{4,5},{5,4},{6,7},{7,6},{8,9},{9,8},{10,11... | collective-permute-start | bytes 245768 | tf_op jit(solution)/shard_map/ppermute | solution.py:466
  64.3 4.8 %collective-permute-start.19 = (bf16[32,768]{1,0:T(8,128)(2,1)S(1)}, bf16[32,768]{1,0:T(8,128)(2,1)S(1)}, u32[]{:S(2)}, u32[]{:S(2)}) collective-permute-start(bf16[32,768]{1,0:T(8,128)(2,1)S(1)} %row_add_pairs.1.row_held), channel_id=1, source_target_pairs={{0,1},{1,0},{2,3},{3,2},{4,5},{5,4},{6,7},{7,6},{8,9},{9,8},{10,11... | collective-permute-start | bytes 147464 | tf_op jit(solution)/shard_map/ppermute | solution.py:466

commit v6 on v5

--- a/solution.py
+++ b/solution.py
@@ -21,6 +21,7 @@
 VMEM = pl.BlockSpec(memory_space=pltpu.VMEM)
 SMEM = pl.BlockSpec(memory_space=pltpu.SMEM)
 HBM = pl.BlockSpec(memory_space=pltpu.HBM)
+PINNED = pl.BlockSpec(memory_space=pltpu.VMEM)
 shaped = jax.ShapeDtypeStruct
 
 
@@ -194,11 +195,13 @@
 
 
 def row_chip_kernel(
-    place_ref, x_any, cot_any, gain_any, wqkv_any, wout_any, send_ref, keep_ref, *refs
+    place_ref, x_any, cot_any, gain_any, wqkv_any, wout_any,
+    send_1, send_2, keep_1, keep_2, *refs,
 ):
     term_qkv = row_part(x_any, cot_any, gain_any, wqkv_any, wout_any, *refs)
-    whole = slice(0, send_ref.shape[0]), slice(0, send_ref.shape[2])
-    split_cores(term_qkv, place_ref[1], send_ref, keep_ref, *whole)
+    chips, lanes = slice(0, send_1.shape[0]), slice(0, send_1.shape[2])
+    split_cores(term_qkv[:, : lanes.stop], place_ref[1], send_1, keep_1, chips, lanes)
+    split_cores(term_qkv[:, lanes.stop :], place_ref[1], send_2, keep_2, chips, lanes)
 
 
 def column_part(moved_ref, gain_ref, w_ref, wo_ref, weight_waits, grads_ref):
@@ -323,6 +326,34 @@
         back_ref[:, i * group : (i + 1) * group, :] = piece.astype(BF16)
 
 
+def back_chip_kernel(place_ref, grads_ref, wqkv_any, send_1, send_2, keep_ref, w_ref, sems):
+    finished(*started(*qkv_copies(wqkv_any, w_ref, sems, 1)))
+    grad_hidden = dot_nt(grads_ref[...], w_ref[...])
+    chips, share, width = keep_ref.shape
+    half = width // 2
+    group = math.gcd(share, 16)
+    block = 2 * chips * group
+    first = place_ref[1] == 0
+    for i in range(share // group):
+        piece = grad_hidden[i * block : (i + 1) * block].reshape(chips, 2, group, width)
+        even, odd = piece[:, 0], piece[:, 1]
+        at = slice(i * group, (i + 1) * group)
+        sent = jnp.where(first, odd, even).astype(BF16)
+        send_1[:, at, :], send_2[:, at, :] = sent[:, :, :half], sent[:, :, half:]
+        keep_ref[:, at, :] = jnp.where(first, even, odd).astype(BF16)
+
+
+def back_pack_kernel(place_ref, keep_ref, got_1, got_2, own_ref, off_1, off_2, off_3):
+    chip, core = place_ref[0], place_ref[1]
+    share, half = keep_ref.shape[1], got_1.shape[2]
+    kept_at = pl.multiple_of(core * share, share)
+    got_at = pl.multiple_of((1 - core) * share, share)
+    for i, target in enumerate((own_ref, off_1, off_2, off_3)):
+        target[pl.ds(kept_at, share), :] = keep_ref[chip ^ i]
+        target[pl.ds(got_at, share), :half] = got_1[chip ^ i]
+        target[pl.ds(got_at, share), half:] = got_2[chip ^ i]
+
+
 def input_kernel(
     x_any, cot_any, gain_any, grads_any, wqkv_any, back_ref, grad_ref,
     x_ref, cot_ref, gain_ref, grads_ref, w_ref, sems,
@@ -340,10 +371,49 @@
     grad_hidden = dot_nt(grads_ref[...], w_ref[...]) + back_ref[...].astype(F32)
     finished(*others)
     inverse_rms, normed = rms_parts(x_ref[...].astype(F32))
-    grad_normed = grad_hidden * gain_ref[...]
+    grad_ref[...] = input_grad(normed, inverse_rms, grad_hidden, gain_ref[...], cot_ref[...])
+
+
+def input_grad(normed, inverse_rms, grad_hidden, gain, cot):
+    grad_normed = grad_hidden * gain
     projected = jnp.mean(grad_normed * normed, -1, keepdims=True)
     grad = inverse_rms * (grad_normed - normed * projected)
-    grad_ref[...] = (cot_ref[...].astype(F32) + grad).astype(BF16)
+    return (cot.astype(F32) + grad).astype(BF16)
+
+
+def ready_kernel(
+    place_ref, grads_any, wqkv_any, x_any, cot_any,
+    hidden_ref, rows_ref, x_ref, cot_ref,
+    grads_ref, w_ref, sems,
+):
+    rows = rows_ref.shape[0]
+    at = pl.multiple_of((place_ref[0] * 2 + place_ref[1]) * rows, rows)
+    products = started(
+        pltpu.make_async_copy(grads_any, grads_ref, sems.at[3]),
+        *qkv_copies(wqkv_any, w_ref, sems, 0),
+    )
+    others = started(
+        pltpu.make_async_copy(wqkv_any.at[pl.ds(at, rows), :], rows_ref, sems.at[4]),
+        pltpu.make_async_copy(x_any, x_ref, sems.at[5]),
+        pltpu.make_async_copy(cot_any, cot_ref, sems.at[6]),
+    )
+    finished(*products)
+    hidden_ref[...] = dot_nt(grads_ref[...], w_ref[...])
+    finished(*others)
+
+
+def input_chip_kernel(
+    place_ref, x_ref, cot_ref, gain_ref, hidden_ref, own_ref, got_1, got_2, got_3, grad_ref
+):
+    chip = place_ref[0]
+    count = own_ref.shape[0]
+    for i, back_ref in enumerate((own_ref, got_1, got_2, got_3)):
+        at = pl.ds(pl.multiple_of((chip ^ i) * count, count), count)
+        inverse_rms, normed = rms_parts(x_ref[at, :].astype(F32))
+        grad_hidden = hidden_ref[at, :] + back_ref[...].astype(F32)
+        grad_ref[at, :] = input_grad(
+            normed, inverse_rms, grad_hidden, gain_ref[...], cot_ref[at, :]
+        )
 
 
 def pack_kernel(place_ref, x_any, cot_any, own_ref, off_1, off_2, off_3, sems):
@@ -369,66 +439,55 @@
     finished(*started(*copies))
 
 
-def chip_sum_kernel(place_ref, keep_ref, got_ref, own_any, off_1, off_2, off_3, own_ref, sem):
+def chip_sum_kernel(place_ref, *refs):
     chip = place_ref[0]
-    handed = None
-    for i, target in enumerate((own_ref, off_1, off_2, off_3)):
-        there = chip ^ i
-        total = keep_ref[there].astype(F32) + got_ref[there].astype(F32)
-        target[...] = total.astype(target.dtype)
-        if handed is None:
-            handed = started(pltpu.make_async_copy(own_ref, own_any, sem))
-    finished(*handed)
-
-
-def layer_sum_kernel(place_ref, own_any, got_1, got_2, got_3, send_ref, keep_ref, own_ref, sem):
-    own = started(pltpu.make_async_copy(own_any, own_ref, sem))
+    pieces, targets = refs[:-4], refs[-4:]
+    count = len(pieces) // 2
+    for i, target in enumerate(targets):
+        at = 0
+        for kept_ref, got_ref in zip(pieces[:count], pieces[count:]):
+            total = kept_ref[chip ^ i].astype(F32) + got_ref[chip ^ i].astype(F32)
+            target[:, at : at + total.shape[1]] = total.astype(target.dtype)
+            at += total.shape[1]
+
+
+def layer_sum_kernel(place_ref, own_ref, got_1, got_2, got_3, send_ref, keep_ref):
     upper = place_ref[2] == 1
-    total = (got_1[...].astype(F32) + got_2[...].astype(F32)) + got_3[...].astype(F32)
-    finished(*own)
-    total += own_ref[...]
+    total = own_ref[...] + (
+        (got_1[...].astype(F32) + got_2[...].astype(F32)) + got_3[...].astype(F32)
+    )
     half = total.shape[0] // 2
     low, high = total[:half], total[half:]
     send_ref[...] = jnp.where(upper, low, high).astype(BF16)
     keep_ref[...] = jnp.where(upper, high, low)
 
 
-def pass_kernel(any_ref, same_ref):
-    pass
-
-
 def add_kernel(kept_ref, got_ref, out_ref):
     out_ref[...] = (kept_ref[...].astype(F32) + got_ref[...].astype(F32)).astype(BF16)
 
 
-def result_kernel(
-    place_ref, row_held, row_got, held_ref, got_ref, wqkv_any, gain_any,
-    qkv_ref, out_ref, grad_ref,
-    w_ref, gain_ref, sems,
-):
+def join_kernel(row_ref, kept_ref, got_ref, out_ref):
+    cut = row_ref.shape[1]
+    out_ref[:, :cut] = row_ref[...]
+    out_ref[:, cut:] = (kept_ref[...] + got_ref[...].astype(F32)).astype(BF16)
+
+
+def result_kernel(place_ref, held_ref, got_ref, w_ref, gain_ref, qkv_ref, out_ref, grad_ref):
     rows = qkv_ref.shape[0]
     at = pl.multiple_of((place_ref[0] * 2 + place_ref[1]) * rows, rows)
-    copies = started(
-        pltpu.make_async_copy(wqkv_any.at[pl.ds(at, rows), :], w_ref, sems.at[0]),
-        pltpu.make_async_copy(gain_any, gain_ref, sems.at[1]),
-    )
     upper = place_ref[2] == 1
     half = rows // 2
     width = out_ref.shape[1]
 
-    def ordered(held_ref, got_ref, lanes):
+    def ordered(lanes):
         held, got = held_ref[:, lanes].astype(F32), got_ref[:, lanes].astype(F32)
         return (jnp.where(upper, got, held), jnp.where(upper, held, got))
 
     for i in range(3):
-        lanes = slice(i * HW, (i + 1) * HW)
-        at_row, at_col = i * width, i * width + HW
-        low, high = ordered(row_held, row_got, lanes)
-        qkv_ref[:half, at_row : at_row + HW], qkv_ref[half:, at_row : at_row + HW] = low, high
-        low, high = ordered(held_ref, got_ref, lanes)
-        qkv_ref[:half, at_col : at_col + HW], qkv_ref[half:, at_col : at_col + HW] = low, high
-    out_ref[:half], out_ref[half:] = ordered(held_ref, got_ref, slice(3 * HW, 3 * HW + width))
-    finished(*copies)
+        for at_from, at_to in ((i * HW, i * width), ((3 + i) * HW, i * width + HW)):
+            to = slice(at_to, at_to + HW)
+            qkv_ref[:half, to], qkv_ref[half:, to] = ordered(slice(at_from, at_from + HW))
+    out_ref[:half], out_ref[half:] = ordered(slice(6 * HW, 6 * HW + width))
     total = jnp.sum(qkv_ref[...] * w_ref[...].astype(F32), -1, keepdims=True)
     shape = (rows, gain_ref.shape[1])
     row = lax.broadcasted_iota(jnp.int32, shape, 0)
@@ -439,24 +498,22 @@
     grad_ref[...] = jnp.sum(jnp.where(same, total / gain, 0.0), 0, keepdims=True)
 
 
-def call(kernel, name, ins, outs, scratch=(), flops=0, vmem=SMALL_VMEM, out_specs=None, aliases=None):
+def call(kernel, name, ins, outs, scratch=(), vmem=SMALL_VMEM, out_specs=None):
     out_specs = out_specs or [VMEM] * len(outs)
-    places = [pltpu.HBM if spec is HBM else None for spec in out_specs]
+    places = [{id(HBM): pltpu.HBM, id(PINNED): pltpu.VMEM}.get(id(spec)) for spec in out_specs]
     outs = [place(*out) if place else shaped(*out) for place, out in zip(places, outs)]
     args = [
         pltpu.with_memory_space_constraint(array, pltpu.HBM) if spec is HBM else array
         for spec, array in ins
     ]
-    size = sum(math.prod(a.shape) * a.dtype.itemsize for a in (*args, *outs))
     return pl.pallas_call(
         kernel,
         out_shape=outs,
         in_specs=[spec for spec, _ in ins],
         out_specs=out_specs,
         scratch_shapes=scratch,
-        input_output_aliases=aliases or {},
         name=name,
-        cost_estimate=pl.CostEstimate(flops=flops, bytes_accessed=size, transcendentals=0),
+        cost_estimate=pl.CostEstimate(flops=0, bytes_accessed=0, transcendentals=0),
         compiler_params=pltpu.CompilerParams(vmem_limit_bytes=vmem),
     )(*args)
 
@@ -467,14 +524,13 @@
 
 
 def add_cores(place, keep, got, name):
-    _, rows, wide = keep.shape
+    rows, wide = keep[0].shape[1], sum(one.shape[2] for one in keep)
     return call(
         chip_sum_kernel,
         name + "_add_cores",
-        [(SMEM, place), (VMEM, keep), (VMEM, got)],
+        [(SMEM, place), *[(VMEM, one) for one in (*keep, *got)]],
         [((rows, wide), F32)] + [((rows, wide), BF16)] * 3,
-        [pltpu.VMEM((rows, wide), F32), pltpu.SemaphoreType.DMA],
-        out_specs=[HBM, VMEM, VMEM, VMEM],
+        out_specs=[PINNED, VMEM, VMEM, VMEM],
     )
 
 
@@ -490,9 +546,9 @@
     return call(
         layer_sum_kernel,
         name + "_add_chips",
-        [(SMEM, place), (HBM, owned), *[(VMEM, one) for one in got]],
+        [(SMEM, place), (VMEM, owned), *[(VMEM, one) for one in got]],
         [((rows // 2, wide), BF16), ((rows // 2, wide), F32)],
-        [pltpu.VMEM((rows, wide), F32), pltpu.SemaphoreType.DMA],
+        out_specs=[VMEM, PINNED],
     )
 
 
@@ -534,16 +590,18 @@
         )
         near_1, near_2, near_3 = cross_chips(*packed[1:])
         own = swap(packed[0], "seq", 1)
+        placed, _ = lax.optimization_barrier((place, packed[0]))
     else:
         outgoing = jnp.stack([x.reshape(n, share, width), cot.reshape(n, share, width)], 1)
         moved = lax.all_to_all(outgoing, "seq", split_axis=0, concat_axis=0, tiled=True)
-
-    split_out = ((chips, row_share, row_width), BF16)
-    term_outs = [split_out] * 2 if layered else [((width, row_width), BF16)]
+        placed = place
+
+    split_out = ((chips, row_share, row_width // 2), BF16)
+    term_outs = [split_out] * 4 if layered else [((width, row_width), BF16)]
     *row_terms, row_out, row_grads = call(
         row_chip_kernel if layered else row_kernel,
         "row_heads",
-        [(SMEM, place)] * layered + [(HBM, x), (HBM, cot), *weights],
+        [(SMEM, placed)] * layered + [(HBM, x), (HBM, cot), *weights],
         [*term_outs, ((HW, width), BF16), grads_out],
         [
             pltpu.VMEM((columns, width), BF16),
@@ -554,20 +612,19 @@
             pltpu.VMEM((columns, 3 * HW), BF16),
             pltpu.SemaphoreType.DMA((7,)),
         ],
-        5_000_000_000,
         BIG_VMEM,
         [VMEM] * len(term_outs) + [VMEM, HBM],
     )
     moved_scratch = pltpu.VMEM((n, 2, share, width), BF16)
     if layered:
-        row_send, row_keep = row_terms
-        near_1, near_2, near_3, row_send = lax.optimization_barrier(
-            (near_1, near_2, near_3, row_send)
+        near_1, *row_terms = lax.optimization_barrier((near_1, *row_terms))
+        row_sent = [swap(one, "seq", 1) for one in row_terms[:2]]
+        row_owned, *row_off = add_cores(place, row_terms[2:], row_sent, "row")
+        near_1, near_2, near_3, row_owned = lax.optimization_barrier(
+            (near_1, near_2, near_3, row_owned)
         )
         far_3, far_1, far_2 = swap(near_3, "seq", 1), swap(near_1, "seq", 1), swap(near_2, "seq", 1)
-        row_owned, *row_off = add_cores(place, row_keep, swap(row_send, "seq", 1), "row")
         row_got = cross_chips(*row_off)
-        own, row_owned = lax.optimization_barrier((own, row_owned))
         send, keep, col_grads = call(
             column_chip_kernel,
             "column_heads",
@@ -578,17 +635,77 @@
             ],
             [((chips, row_share, col_width), BF16)] * 2 + [grads_out],
             [moved_scratch, *weight_scratch, pltpu.SemaphoreType.DMA((21,))],
-            4_000_000_000,
             BIG_VMEM,
         )
         send, row_got = lax.optimization_barrier((send, row_got))
         row_next, row_kept = add_chips(place, row_owned, row_got, "row")
         row_pair = add_two(row_kept, swap(row_next, "dp", 1), "row_add_pair")
         keep, row_kept = lax.optimization_barrier((keep, row_kept))
-        owned, *off = add_cores(place, keep, swap(send, "seq", 1), "column")
+        owned, *off = add_cores(place, [keep], [swap(send, "seq", 1)], "column")
         got = cross_chips(*off)
-        col_grads, owned, row_pair = lax.optimization_barrier((col_grads, owned, row_pair))
-        row_held = add_two(row_pair, swap(row_pair, "dp", 2), "row_add_pairs")
+        col_grads, owned = lax.optimization_barrier((col_grads, owned))
+        *back_parts, back_keep = call(
+            back_chip_kernel,
+            "column_grad_hidden",
+            [(SMEM, place), (VMEM, col_grads), (HBM, qkv_weight)],
+            [((chips, share, width // 2), BF16)] * 2 + [((chips, share, width), BF16)],
+            [pltpu.VMEM((width, 3 * HW), BF16), pltpu.SemaphoreType.DMA((3,))],
+        )
+        back = call(
+            back_pack_kernel,
+            "pack_grad_hidden",
+            [
+                (SMEM, place), (VMEM, back_keep),
+                *[(VMEM, swap(part, "seq", 1)) for part in back_parts],
+            ],
+            [((2 * share, width), BF16)] * 4,
+        )
+        *back, owned, row_pair = lax.optimization_barrier((*back, owned, row_pair))
+        to_next, kept = add_chips(place, owned, got, "column")
+        row_grads, kept = lax.optimization_barrier((row_grads, kept))
+        row_hidden, weight_rows, x_near, cot_near = call(
+            ready_kernel,
+            "row_grad_hidden",
+            [(SMEM, place), (HBM, row_grads), (HBM, qkv_weight), (HBM, x), (HBM, cot)],
+            [
+                ((columns, width), F32), ((row_share, 3 * width), BF16),
+                ((columns, width), BF16), ((columns, width), BF16),
+            ],
+            [
+                pltpu.VMEM((columns, 3 * HW), BF16),
+                pltpu.VMEM((width, 3 * HW), BF16),
+                pltpu.SemaphoreType.DMA((7,)),
+            ],
+            out_specs=[PINNED] * 4,
+        )
+        kept, row_hidden = lax.optimization_barrier((kept, row_hidden))
+        (joined,) = call(
+            join_kernel,
+            "join_terms",
+            [(VMEM, row_pair), (VMEM, kept), (VMEM, swap(to_next, "dp", 1))],
+            [((row_share // 2, row_width + col_width), BF16)],
+        )
+        *back, joined = lax.optimization_barrier((*back, joined))
+        held = add_two(joined, swap(joined, "dp", 2), "add_pairs")
+        other = swap(held, "dp", 1)
+        (grad,) = call(
+            input_chip_kernel,
+            "input_grad",
+            [
+                (SMEM, place), (VMEM, x_near), (VMEM, cot_near), (VMEM, gain), (VMEM, row_hidden),
+                (VMEM, back[0]), *[(VMEM, one) for one in cross_chips(*back[1:])],
+            ],
+            [((columns, width), BF16)],
+        )
+        sum_qkv, sum_out, sum_gain = call(
+            result_kernel,
+            "result",
+            [
+                (SMEM, place), (VMEM, held), (VMEM, other), (VMEM, weight_rows), (VMEM, gain),
+            ],
+            [((row_share, 3 * width), F32), ((row_share, width), F32), ((1, row_share), F32)],
+        )
+        sum_gain = sum_gain.reshape(row_share)
     else:
         terms, col_grads = call(
             column_kernel,
@@ -596,67 +713,33 @@
             [(ANY, moved), *weights, (VMEM, row_terms[0]), (VMEM, row_out)],
             [((width, 4 * width), BF16), grads_out],
             [moved_scratch, *weight_scratch, pltpu.SemaphoreType.DMA((6,))],
-            4_000_000_000,
             BIG_VMEM,
         )
-    (back,) = call(
-        back_kernel,
-        "column_grad_hidden",
-        [(VMEM, col_grads), (HBM, qkv_weight)],
-        [((n, share, width), BF16)],
-        [pltpu.VMEM((width, 3 * HW), BF16), pltpu.SemaphoreType.DMA((3,))],
-        400_000_000,
-    )
-    if layered:
-        back, owned = lax.optimization_barrier((back, owned))
-        to_next, kept = add_chips(place, owned, got, "column")
-        back, kept = lax.optimization_barrier((back, kept))
         (back,) = call(
-            pass_kernel, "pass_on", [(ANY, back)], [(back.shape, BF16)],
-            out_specs=[ANY], aliases={0: 0},
-        )
-        kept, row_held = lax.optimization_barrier((kept, row_held))
-        pair_sum = add_two(kept, swap(to_next, "dp", 1), "column_add_pair")
-        row_other = swap(row_held, "dp", 1)
-        held = add_two(pair_sum, swap(pair_sum, "dp", 2), "column_add_pairs")
-    returned = lax.all_to_all(back, "seq", split_axis=0, concat_axis=0, tiled=True)
-    (input_grad,) = call(
-        input_kernel,
-        "input_grad",
-        [
-            (HBM, x), (HBM, cot), (HBM, gain), (HBM, row_grads), (HBM, qkv_weight),
-            (VMEM, returned.reshape(columns, width)),
-        ],
-        [((columns, width), BF16)],
-        [
-            pltpu.VMEM((columns, width), BF16),
-            pltpu.VMEM((columns, width), BF16),
-            pltpu.VMEM((1, width), F32),
-            pltpu.VMEM((columns, 3 * HW), BF16),
-            pltpu.VMEM((width, 3 * HW), BF16),
-            pltpu.SemaphoreType.DMA((7,)),
-        ],
-        400_000_000,
-    )
-    if layered:
-        other = swap(held, "dp", 1)
-        held, input_grad = lax.optimization_barrier((held, input_grad))
-        sum_qkv, sum_out, sum_gain = call(
-            result_kernel,
-            "result",
+            back_kernel,
+            "column_grad_hidden",
+            [(VMEM, col_grads), (HBM, qkv_weight)],
+            [((n, share, width), BF16)],
+            [pltpu.VMEM((width, 3 * HW), BF16), pltpu.SemaphoreType.DMA((3,))],
+        )
+        returned = lax.all_to_all(back, "seq", split_axis=0, concat_axis=0, tiled=True)
+        (grad,) = call(
+            input_kernel,
+            "input_grad",
             [
-                (SMEM, place), (VMEM, row_held), (VMEM, row_other), (VMEM, held), (VMEM, other),
-                (HBM, qkv_weight), (HBM, gain),
+                (HBM, x), (HBM, cot), (HBM, gain), (HBM, row_grads), (HBM, qkv_weight),
+                (VMEM, returned.reshape(columns, width)),
             ],
-            [((row_share, 3 * width), F32), ((row_share, width), F32), ((1, row_share), F32)],
+            [((columns, width), BF16)],
             [
-                pltpu.VMEM((row_share, 3 * width), BF16),
+                pltpu.VMEM((columns, width), BF16),
+                pltpu.VMEM((columns, width), BF16),
                 pltpu.VMEM((1, width), F32),
-                pltpu.SemaphoreType.DMA((2,)),
+                pltpu.VMEM((columns, 3 * HW), BF16),
+                pltpu.VMEM((width, 3 * HW), BF16),
+                pltpu.SemaphoreType.DMA((7,)),
             ],
         )
-        sum_gain = sum_gain.reshape(row_share)
-    else:
         terms = lax.all_to_all(
             terms.reshape(n, row_share, 4 * width), "seq", split_axis=0, concat_axis=0, tiled=True
         )
@@ -668,7 +751,7 @@
         own_gain = lax.dynamic_slice_in_dim(norm_gain, here * row_share, row_share, 0)
         own_weight = lax.dynamic_slice_in_dim(qkv_weight, here * row_share, row_share, 0)
         sum_gain = jnp.sum(sum_qkv * own_weight.astype(F32), -1) / own_gain
-    return (input_grad.reshape(inputs.shape), sum_qkv, sum_out, sum_gain)
+    return (grad.reshape(inputs.shape), sum_qkv, sum_out, sum_gain)
 
 
 def solution(mesh):

time: 71.8 us -> 62.6 us (0.87)
  waiting for transfers between devices: 15.7 us -> 11.4 us
  starting transfers between devices: 26.3 us -> 23.9 us
  Pallas kernels: 28.4 us -> 26.2 us
    ppermute x21 -> x25, waiting for transfers between devices: 15.7 us -> 11.4 us  [swap(): return lax.ppermute(array, axis, [(i, i ^ bits) for i in range(count)])]
    all_to_all x1 -> x0, starting transfers between devices: 3.51 us -> none  [body(): lax.all_to_all(back, 'seq', split_axis=0, concat_axis=0, tiled=True)]
    pallas_call x15, Pallas kernels: 28.4 us -> 26.2 us  [call(): pl.pallas_call(kernel, out_shape=outs, in_specs=[spec for spec, _ in ins]...]
    ppermute x21 -> x25, starting transfers between devices: 22.8 us -> 23.9 us  [swap(): return lax.ppermute(array, axis, [(i, i ^ bits) for i in range(count)])]
  transfers between devices with their start and end apart: 22 -> 25, of which waited for: 8 -> 13; matrix products, arithmetic and copies ran while one was open for 0% -> 0% of each run, Pallas kernels for 30% -> 36%
where the time goes in v6:
time: 62.6 us; the launch traced here: 62.3 us
  Pallas kernels  26.2 us (42%)
  starting transfers between devices  23.9 us (38%)
  waiting for transfers between devices  11.4 us (18%)
  between operations  0.84 us (1%)
    pallas_call x15, Pallas kernels, call(): pl.pallas_call(kernel, out_shape=outs, in_specs=[spec for spec, _ in ins]...  26.2 us
    ppermute x25, starting transfers between devices, swap(): return lax.ppermute(array, axis, [(i, i ^ bits) for i in range(count)])  23.9 us
    ppermute x25, waiting for transfers between devices, swap(): return lax.ppermute(array, axis, [(i, i ^ bits) for i in range(count)])  11.4 us
  transfers between devices with their start and end apart: 25, of which 13 were waited for; matrix products, arithmetic and copies ran while one was open for 0% of the time, Pallas kernels for 36%

profile of v6, /device:TPU:0, one launch (start us, length us, event | category | flops | bytes accessed | tf_op | source)
XLA Modules:
  0.0 62.3 jit_solution(1823415412656924288)
XLA Ops:
  0.7 0.1 pad_add_fusion.place_ref
  0.7 1.9 %pack_columns.1 = (bf16[2,64,512]{2,1,0:T(8,128)(2,1)S(1)}, bf16[2,128,512]{2,1,0:T(8,128)(2,1)S(1)}, bf16[2,128,512]{2,1,0:T(8,128)(2,1)S(1)}, bf16[2,128,512]{2,1,0:T(8,128)(2,1)S(1)}) custom-call(s32[3]{0:T(128)S(1)} %pad_add_fusion.place_ref, bf16[512,512]{1,0:T(8,128)(2,1)} %bitcast.12, bf16[512,512]{1,0:T(8,128)(2,1)} %bitcast.16), custom_call_target="tpu_custom_call" | custom-call | tf_op jit(solution)/shard_map/pack_columns/pallas_call | solution.py:509
  2.6 3.0 %collective-permute-start.1 = (bf16[2,128,512]{2,1,0:T(8,128)(2,1)S(1)}, bf16[2,128,512]{2,1,0:T(8,128)(2,1)S(1)}, u32[]{:S(2)}, u32[]{:S(2)}) collective-permute-start(bf16[2,128,512]{2,1,0:T(8,128)(2,1)S(1)} %get-tuple-element.78), channel_id=1, source_target_pairs={{0,8},{4,12},{8,0},{12,4},{16,24},{20,28},{24,16},{28,20},{1,9},{5... | collective-permute-start | bytes 786440 | tf_op jit(solution)/shard_map/ppermute | solution.py:523
  5.6 1.5 %collective-permute-start.2 = (bf16[2,128,512]{2,1,0:T(8,128)(2,1)S(1)}, bf16[2,128,512]{2,1,0:T(8,128)(2,1)S(1)}, u32[]{:S(2)}, u32[]{:S(2)}) collective-permute-start(bf16[2,128,512]{2,1,0:T(8,128)(2,1)S(1)} %get-tuple-element.84), channel_id=1, source_target_pairs={{0,16},{4,20},{8,24},{12,28},{16,0},{20,4},{24,8},{28,12},{1,17},{... | collective-permute-start | bytes 786440 | tf_op jit(solution)/shard_map/ppermute | solution.py:523
  7.1 7.4 %row_heads.1 = (bf16[4,64,384]{2,1,0:T(8,128)(2,1)S(1)}, bf16[4,64,384]{2,1,0:T(8,128)(2,1)S(1)}, bf16[4,64,384]{2,1,0:T(8,128)(2,1)S(1)}, bf16[4,64,384]{2,1,0:...) custom-call(s32[3]{0:T(128)S(1)} %pad_add_fusion.place_ref, bf16[512,512]{1,0:T(8,128)(2,1)} %bitcast.13, ...), custom_call_target="tpu_custom_call" | custom-call | tf_op jit(solution)/shard_map/row_heads/pallas_call | solution.py:509
  14.6 0.1 collective-permute-start.4
  14.7 0.5 collective-permute-start.5
  15.2 0.9 %collective-permute-done.4.refs_2_ = bf16[4,64,384]{2,1,0:T(8,128)(2,1)S(1)} collective-permute-done((bf16[4,64,384]{2,1,0:T(8,128)(2,1)S(1)}, bf16[4,64,384]{2,1,0:T(8,128)(2,1)S(1)}, u32[]{:S(2)}, u32[]{:S(2)}) %collective-permute-start.4) | collective-permute-done | bytes 196640 | tf_op jit(solution)/shard_map/ppermute | solution.py:523
  16.1 0.3 collective-permute-done.5.refs_3_
  16.4 0.6 %row_add_cores.1 = (f32[64,768]{1,0:T(8,128)S(1)}, bf16[64,768]{1,0:T(8,128)(2,1)S(1)}, bf16[64,768]{1,0:T(8,128)(2,1)S(1)}, bf16[64,768]{1,0:T(8,128)(2,1)S(1)}) custom-call(s32[3]{0:T(128)S(1)} %pad_add_fusion.place_ref, bf16[4,64,384]{2,1,0:T(8,128)(2,1)S(1)} %get-tuple-element.86.refs_0_, bf16[4,64,384]{2,1,0:T(8,128)(2,1)S(1)} %get-tuple-element.87.refs_1_, ...), custom_call_target="tpu_custom_call" | custom-call | tf_op jit(solution)/shard_map/row_add_cores/pallas_call | solution.py:509
  17.0 2.0 %collective-permute-done.2.near_2 = bf16[2,128,512]{2,1,0:T(8,128)(2,1)S(1)} collective-permute-done((bf16[2,128,512]{2,1,0:T(8,128)(2,1)S(1)}, bf16[2,128,512]{2,1,0:T(8,128)(2,1)S(1)}, u32[]{:S(2)}, u32[]{:S(2)}) %collective-permute-start.2) | collective-permute-done | bytes 262176 | tf_op jit(solution)/shard_map/ppermute | solution.py:523
  19.0 0.5 collective-permute-start.7
  19.5 0.5 collective-permute-start
  20.0 1.2 %collective-permute-start.9 = (bf16[64,768]{1,0:T(8,128)(2,1)S(1)}, bf16[64,768]{1,0:T(8,128)(2,1)S(1)}, u32[]{:S(2)}, u32[]{:S(2)}) collective-permute-start(bf16[64,768]{1,0:T(8,128)(2,1)S(1)} %get-tuple-element.99), channel_id=1, source_target_pairs={{0,8},{4,12},{8,0},{12,4},{16,24},{20,28},{24,16},{28,20},{1,9},{5... | collective-permute-start | bytes 294920 | tf_op jit(solution)/shard_map/ppermute | solution.py:523
  21.2 0.2 collective-permute-done.own_any
  21.5 1.5 %collective-permute-start.10 = (bf16[64,768]{1,0:T(8,128)(2,1)S(1)}, bf16[64,768]{1,0:T(8,128)(2,1)S(1)}, u32[]{:S(2)}, u32[]{:S(2)}) collective-permute-start(bf16[64,768]{1,0:T(8,128)(2,1)S(1)} %get-tuple-element.100), channel_id=1, source_target_pairs={{0,16},{4,20},{8,24},{12,28},{16,0},{20,4},{24,8},{28,12},{1,17},{... | collective-permute-start | bytes 294920 | tf_op jit(solution)/shard_map/ppermute | solution.py:523
  23.0 1.2 %collective-permute-start.11 = (bf16[64,768]{1,0:T(8,128)(2,1)S(1)}, bf16[64,768]{1,0:T(8,128)(2,1)S(1)}, u32[]{:S(2)}, u32[]{:S(2)}) collective-permute-start(bf16[64,768]{1,0:T(8,128)(2,1)S(1)} %get-tuple-element.101), channel_id=1, source_target_pairs={{0,24},{4,28},{8,16},{12,20},{16,8},{20,12},{24,0},{28,4},{1,25},{... | collective-permute-start | bytes 294920 | tf_op jit(solution)/shard_map/ppermute | solution.py:523
  24.2 5.5 %column_heads.1 = (bf16[4,64,1280]{2,1,0:T(8,128)(2,1)S(1)}, bf16[4,64,1280]{2,1,0:T(8,128)(2,1)S(1)}, bf16[512,768]{1,0:T(8,128)(2,1)S(1)}) custom-call(s32[3]{0:T(128)S(1)} %pad_add_fusion.place_ref, bf16[512,512]{1,0:T(8,128)(2,1)} %bitcast.14, bf16[512,512]{1,0:T(8,128)(2,1)} %bitcast.18, bf16[2,64,512]{2,1,0:T(8,128)(2,1)S(1)} %collective-permute-done.own_any, ...), custom_call_target="tpu_custom_call" | custom-call | tf_op jit(solution)/shard_map/column_heads/pallas_call | solution.py:509
  29.7 0.1 collective-permute-start.12
  29.8 0.6 row_add_chips.1
  30.4 1.6 %collective-permute-start.15 = (bf16[32,768]{1,0:T(8,128)(2,1)S(1)}, bf16[32,768]{1,0:T(8,128)(2,1)S(1)}, u32[]{:S(2)}, u32[]{:S(2)}) collective-permute-start(bf16[32,768]{1,0:T(8,128)(2,1)S(1)} %get-tuple-element.118), channel_id=1, source_target_pairs={{0,1},{1,0},{2,3},{3,2},{4,5},{5,4},{6,7},{7,6},{8,9},{9,8},{10,11... | collective-permute-start | bytes 147464 | tf_op jit(solution)/shard_map/ppermute | solution.py:523
  32.1 0.7 %column_add_cores.1 = (f32[64,1280]{1,0:T(8,128)S(1)}, bf16[64,1280]{1,0:T(8,128)(2,1)S(1)}, bf16[64,1280]{1,0:T(8,128)(2,1)S(1)}, bf16[64,1280]{1,0:T(8,128)(2,1)S(1)}) custom-call(s32[3]{0:T(128)S(1)} %pad_add_fusion.place_ref, bf16[4,64,1280]{2,1,0:T(8,128)(2,1)S(1)} %get-tuple-element.106.refs_0_, bf16[4,64,1280]{2,1,0:T(8,128)(2,1)S(1)} %collective-permute-done.12.refs_1_), custom_call_target="tpu_custom_call" | custom-call | tf_op jit(solution)/shard_map/column_add_cores/pallas_call | solution.py:509
  32.8 0.9 %collective-permute-start.16 = (bf16[64,1280]{1,0:T(8,128)(2,1)S(1)}, bf16[64,1280]{1,0:T(8,128)(2,1)S(1)}, u32[]{:S(2)}, u32[]{:S(2)}) collective-permute-start(bf16[64,1280]{1,0:T(8,128)(2,1)S(1)} %get-tuple-element.120), channel_id=1, source_target_pairs={{0,8},{4,12},{8,0},{12,4},{16,24},{20,28},{24,16},{28,20},{1,9},{5... | collective-permute-start | bytes 491528 | tf_op jit(solution)/shard_map/ppermute | solution.py:523
  33.6 1.5 %collective-permute-start.17 = (bf16[64,1280]{1,0:T(8,128)(2,1)S(1)}, bf16[64,1280]{1,0:T(8,128)(2,1)S(1)}, u32[]{:S(2)}, u32[]{:S(2)}) collective-permute-start(bf16[64,1280]{1,0:T(8,128)(2,1)S(1)} %get-tuple-element.121), channel_id=1, source_target_pairs={{0,16},{4,20},{8,24},{12,28},{16,0},{20,4},{24,8},{28,12},{1,17},{... | collective-permute-start | bytes 491528 | tf_op jit(solution)/shard_map/ppermute | solution.py:523
  35.1 1.2 %collective-permute-start.18 = (bf16[64,1280]{1,0:T(8,128)(2,1)S(1)}, bf16[64,1280]{1,0:T(8,128)(2,1)S(1)}, u32[]{:S(2)}, u32[]{:S(2)}) collective-permute-start(bf16[64,1280]{1,0:T(8,128)(2,1)S(1)} %get-tuple-element.122), channel_id=1, source_target_pairs={{0,24},{4,28},{8,16},{12,20},{16,8},{20,12},{24,0},{28,4},{1,25},{... | collective-permute-start | bytes 491528 | tf_op jit(solution)/shard_map/ppermute | solution.py:523
  36.3 2.3 %column_grad_hidden.1 = (bf16[4,64,256]{2,1,0:T(8,128)(2,1)S(1)}, bf16[4,64,256]{2,1,0:T(8,128)(2,1)S(1)}, bf16[4,64,512]{2,1,0:T(8,128)(2,1)S(1)}) custom-call(s32[3]{0:T(128)S(1)} %pad_add_fusion.place_ref, bf16[512,768]{1,0:T(8,128)(2,1)S(1)} %get-tuple-element.109.grads_ref, bf16[512,1536]{1,0:T(8,128)(2,1)} %wqkv_any.7), custom_call_target="tpu_custom_call" | custom-call | tf_op jit(solution)/shard_map/column_grad_hidden/pallas_call | solution.py:509
  38.6 0.1 collective-permute-start.13
  38.7 0.5 collective-permute-start.14
  39.2 0.8 %collective-permute-done.13.got_1 = bf16[4,64,256]{2,1,0:T(8,128)(2,1)S(1)} collective-permute-done((bf16[4,64,256]{2,1,0:T(8,128)(2,1)S(1)}, bf16[4,64,256]{2,1,0:T(8,128)(2,1)S(1)}, u32[]{:S(2)}, u32[]{:S(2)}) %collective-permute-start.13) | collective-permute-done | bytes 131104 | tf_op jit(solution)/shard_map/ppermute | solution.py:523
  40.0 0.2 collective-permute-done.14.got_2
  40.2 0.6 pack_grad_hidden.1
  40.8 2.4 %collective-permute-done.17.got_2 = bf16[64,1280]{1,0:T(8,128)(2,1)S(1)} collective-permute-done((bf16[64,1280]{1,0:T(8,128)(2,1)S(1)}, bf16[64,1280]{1,0:T(8,128)(2,1)S(1)}, u32[]{:S(2)}, u32[]{:S(2)}) %collective-permute-start.17) | collective-permute-done | bytes 163872 | tf_op jit(solution)/shard_map/ppermute | solution.py:523
  43.2 0.6 %column_add_chips.1 = (bf16[32,1280]{1,0:T(8,128)(2,1)S(1)}, f32[32,1280]{1,0:T(8,128)S(1)}) custom-call(s32[3]{0:T(128)S(1)} %pad_add_fusion.place_ref, f32[64,1280]{1,0:T(8,128)S(1)} %get-tuple-element.119.own_ref, bf16[64,1280]{1,0:T(8,128)(2,1)S(1)} %collective-permute-done.16.got_1, bf16[64,1280]{1,0:T(8,128)(2,1)S(1)} %collective-permute-done.17.got_2, ...), custom_call_target="tpu_custom_call" | custom-call | tf_op jit(solution)/shard_map/column_add_chips/pallas_call | solution.py:509
  43.8 1.4 %collective-permute-start.19 = (bf16[32,1280]{1,0:T(8,128)(2,1)S(1)}, bf16[32,1280]{1,0:T(8,128)(2,1)S(1)}, u32[]{:S(2)}, u32[]{:S(2)}) collective-permute-start(bf16[32,1280]{1,0:T(8,128)(2,1)S(1)} %get-tuple-element.136), channel_id=1, source_target_pairs={{0,1},{1,0},{2,3},{3,2},{4,5},{5,4},{6,7},{7,6},{8,9},{9,8},{10,11... | collective-permute-start | bytes 245768 | tf_op jit(solution)/shard_map/ppermute | solution.py:523
  45.2 2.6 %row_grad_hidden.1 = (f32[512,512]{1,0:T(8,128)S(1)}, bf16[64,1536]{1,0:T(8,128)(2,1)S(1)}, bf16[512,512]{1,0:T(8,128)(2,1)S(1)}, bf16[512,512]{1,0:T(8,128)(2,1)S(1)}) custom-call(s32[3]{0:T(128)S(1)} %pad_add_fusion.place_ref, bf16[512,768]{1,0:T(8,128)(2,1)} %get-tuple-element.124.grads_any, bf16[512,1536]{1,0:T(8,128)(2,1)} %wqkv_any.7, ...), custom_call_target="tpu_custom_call" | custom-call | tf_op jit(solution)/shard_map/row_grad_hidden/pallas_call | solution.py:509
  47.8 0.5 collective-permute-done.19.got_ref
  48.3 2.7 %collective-permute-start.23 = (bf16[32,2048]{1,0:T(8,128)(2,1)S(1)}, bf16[32,2048]{1,0:T(8,128)(2,1)S(1)}, u32[]{:S(2)}, u32[]{:S(2)}) collective-permute-start(bf16[32,2048]{1,0:T(8,128)(2,1)S(1)} %join_terms.1.kept_ref), channel_id=1, source_target_pairs={{0,2},{1,3},{2,0},{3,1},{4,6},{5,7},{6,4},{7,5},{8,10},{9,11},{10,... | collective-permute-start | bytes 393224 | tf_op jit(solution)/shard_map/ppermute | solution.py:523
  51.0 1.2 %collective-permute-start.20 = (bf16[128,512]{1,0:T(8,128)(2,1)S(1)}, bf16[128,512]{1,0:T(8,128)(2,1)S(1)}, u32[]{:S(2)}, u32[]{:S(2)}) collective-permute-start(bf16[128,512]{1,0:T(8,128)(2,1)S(1)} %get-tuple-element.138), channel_id=1, source_target_pairs={{0,8},{4,12},{8,0},{12,4},{16,24},{20,28},{24,16},{28,20},{1,9},{5... | collective-permute-start | bytes 393224 | tf_op jit(solution)/shard_map/ppermute | solution.py:523
  52.2 0.9 %collective-permute-start.21 = (bf16[128,512]{1,0:T(8,128)(2,1)S(1)}, bf16[128,512]{1,0:T(8,128)(2,1)S(1)}, u32[]{:S(2)}, u32[]{:S(2)}) collective-permute-start(bf16[128,512]{1,0:T(8,128)(2,1)S(1)} %get-tuple-element.139), channel_id=1, source_target_pairs={{0,16},{4,20},{8,24},{12,28},{16,0},{20,4},{24,8},{28,12},{1,17},{... | collective-permute-start | bytes 393224 | tf_op jit(solution)/shard_map/ppermute | solution.py:523
  53.1 1.4 %collective-permute-start.22 = (bf16[128,512]{1,0:T(8,128)(2,1)S(1)}, bf16[128,512]{1,0:T(8,128)(2,1)S(1)}, u32[]{:S(2)}, u32[]{:S(2)}) collective-permute-start(bf16[128,512]{1,0:T(8,128)(2,1)S(1)} %get-tuple-element.140), channel_id=1, source_target_pairs={{0,24},{4,28},{8,16},{12,20},{16,8},{20,12},{24,0},{28,4},{1,25},{... | collective-permute-start | bytes 393224 | tf_op jit(solution)/shard_map/ppermute | solution.py:523
  54.5 1.4 %collective-permute-done.23.got_ref = bf16[32,2048]{1,0:T(8,128)(2,1)S(1)} collective-permute-done((bf16[32,2048]{1,0:T(8,128)(2,1)S(1)}, bf16[32,2048]{1,0:T(8,128)(2,1)S(1)}, u32[]{:S(2)}, u32[]{:S(2)}) %collective-permute-start.23) | collective-permute-done | bytes 131104 | tf_op jit(solution)/shard_map/ppermute | solution.py:523
  55.9 0.4 collective-permute-start.24
  56.3 0.4 collective-permute-done.20.got_1
  56.8 0.4 collective-permute-done.21.got_2
  57.2 1.8 %collective-permute-done.22.got_3 = bf16[128,512]{1,0:T(8,128)(2,1)S(1)} collective-permute-done((bf16[128,512]{1,0:T(8,128)(2,1)S(1)}, bf16[128,512]{1,0:T(8,128)(2,1)S(1)}, u32[]{:S(2)}, u32[]{:S(2)}) %collective-permute-start.22) | collective-permute-done | bytes 131104 | tf_op jit(solution)/shard_map/ppermute | solution.py:523
  59.0 1.9 %input_grad.1 = bf16[512,512]{1,0:T(8,128)(2,1)} custom-call(s32[3]{0:T(128)S(1)} %pad_add_fusion.place_ref, bf16[512,512]{1,0:T(8,128)(2,1)S(1)} %get-tuple-element.125.x_ref, bf16[512,512]{1,0:T(8,128)(2,1)S(1)} %get-tuple-element.126.cot_ref, f32[1,512]{1,0:T(1,128)S(1)} %bitcast.10, f32[512,512]{1,0:T(8,128)S(1)} %get-tuple-element.129.hidden_ref, ...), custom_call_target="tpu_custom_call" | custom-call | tf_op jit(solution)/shard_map/input_grad/pallas_call | solution.py:509
  60.9 0.1 collective-permute-done.24.got_ref
  60.9 1.4 %result.1 = (f32[64,1536]{1,0:T(8,128)}, f32[64,512]{1,0:T(8,128)}, f32[1,64]{1,0:T(1,128)}) custom-call(s32[3]{0:T(128)S(1)} %pad_add_fusion.place_ref, bf16[32,2048]{1,0:T(8,128)(2,1)S(1)} %add_pairs.1.held_ref, bf16[32,2048]{1,0:T(8,128)(2,1)S(1)} %collective-permute-done.24.got_ref, bf16[64,1536]{1,0:T(8,128)(2,1)S(1)} %get-tuple-element.142.w_ref, ...), custom_call_target="tpu_custom_call" | custom-call | tf_op jit(solution)/shard_map/result/pallas_call | solution.py:509
  (20 shorter events, 0.1 us)
Async XLA Ops:
  2.6 12.0 %collective-permute-start.1 = (bf16[2,128,512]{2,1,0:T(8,128)(2,1)S(1)}, bf16[2,128,512]{2,1,0:T(8,128)(2,1)S(1)}, u32[]{:S(2)}, u32[]{:S(2)}) collective-permute-start(bf16[2,128,512]{2,1,0:T(8,128)(2,1)S(1)} %get-tuple-element.78), channel_id=1, source_target_pairs={{0,8},{4,12},{8,0},{12,4},{16,24},{20,28},{24,16},{28,20},{1,9},{5... | collective-permute-start | bytes 786440 | tf_op jit(solution)/shard_map/ppermute | solution.py:523
  5.6 13.4 %collective-permute-start.2 = (bf16[2,128,512]{2,1,0:T(8,128)(2,1)S(1)}, bf16[2,128,512]{2,1,0:T(8,128)(2,1)S(1)}, u32[]{:S(2)}, u32[]{:S(2)}) collective-permute-start(bf16[2,128,512]{2,1,0:T(8,128)(2,1)S(1)} %get-tuple-element.84), channel_id=1, source_target_pairs={{0,16},{4,20},{8,24},{12,28},{16,0},{20,4},{24,8},{28,12},{1,17},{... | collective-permute-start | bytes 786440 | tf_op jit(solution)/shard_map/ppermute | solution.py:523
  7.1 11.9 %collective-permute-start.3 = (bf16[2,128,512]{2,1,0:T(8,128)(2,1)S(1)}, bf16[2,128,512]{2,1,0:T(8,128)(2,1)S(1)}, u32[]{:S(2)}, u32[]{:S(2)}) collective-permute-start(bf16[2,128,512]{2,1,0:T(8,128)(2,1)S(1)} %get-tuple-element.85), channel_id=1, source_target_pairs={{0,24},{4,28},{8,16},{12,20},{16,8},{20,12},{24,0},{28,4},{1,25},{... | collective-permute-start | bytes 786440 | tf_op jit(solution)/shard_map/ppermute | solution.py:523
  14.6 1.5 %collective-permute-start.4 = (bf16[4,64,384]{2,1,0:T(8,128)(2,1)S(1)}, bf16[4,64,384]{2,1,0:T(8,128)(2,1)S(1)}, u32[]{:S(2)}, u32[]{:S(2)}) collective-permute-start(bf16[4,64,384]{2,1,0:T(8,128)(2,1)S(1)} %get-tuple-element.88), channel_id=1, source_target_pairs={{0,4},{4,0},{8,12},{12,8},{16,20},{20,16},{24,28},{28,24},{1,5},{5... | collective-permute-start | bytes 589832 | tf_op jit(solution)/shard_map/ppermute | solution.py:523
  14.7 1.7 %collective-permute-start.5 = (bf16[4,64,384]{2,1,0:T(8,128)(2,1)S(1)}, bf16[4,64,384]{2,1,0:T(8,128)(2,1)S(1)}, u32[]{:S(2)}, u32[]{:S(2)}) collective-permute-start(bf16[4,64,384]{2,1,0:T(8,128)(2,1)S(1)} %get-tuple-element.89), channel_id=1, source_target_pairs={{0,4},{4,0},{8,12},{12,8},{16,20},{20,16},{24,28},{28,24},{1,5},{5... | collective-permute-start | bytes 589832 | tf_op jit(solution)/shard_map/ppermute | solution.py:523
  19.0 4.0 %collective-permute-start.6 = (bf16[2,128,512]{2,1,0:T(8,128)(2,1)S(1)}, bf16[2,128,512]{2,1,0:T(8,128)(2,1)S(1)}, u32[]{:S(2)}, u32[]{:S(2)}) collective-permute-start(bf16[2,128,512]{2,1,0:T(8,128)(2,1)S(1)} %collective-permute-done.1.near_1), channel_id=1, source_target_pairs={{0,4},{4,0},{8,12},{12,8},{16,20},{20,16},{24,28},{28,24},{1,5},{5... | collective-permute-start | bytes 786440 | tf_op jit(solution)/shard_map/ppermute | solution.py:523
  19.0 5.2 %collective-permute-start.7 = (bf16[2,128,512]{2,1,0:T(8,128)(2,1)S(1)}, bf16[2,128,512]{2,1,0:T(8,128)(2,1)S(1)}, u32[]{:S(2)}, u32[]{:S(2)}) collective-permute-start(bf16[2,128,512]{2,1,0:T(8,128)(2,1)S(1)} %collective-permute-done.2.near_2), channel_id=1, source_target_pairs={{0,4},{4,0},{8,12},{12,8},{16,20},{20,16},{24,28},{28,24},{1,5},{5... | collective-permute-start | bytes 786440 | tf_op jit(solution)/shard_map/ppermute | solution.py:523
  19.5 4.7 %collective-permute-start.8 = (bf16[2,128,512]{2,1,0:T(8,128)(2,1)S(1)}, bf16[2,128,512]{2,1,0:T(8,128)(2,1)S(1)}, u32[]{:S(2)}, u32[]{:S(2)}) collective-permute-start(bf16[2,128,512]{2,1,0:T(8,128)(2,1)S(1)} %collective-permute-done.3.near_3), channel_id=1, source_target_pairs={{0,4},{4,0},{8,12},{12,8},{16,20},{20,16},{24,28},{28,24},{1,5},{5... | collective-permute-start | bytes 786440 | tf_op jit(solution)/shard_map/ppermute | solution.py:523
  19.5 2.0 %collective-permute-start = (bf16[2,64,512]{2,1,0:T(8,128)(2,1)S(1)}, bf16[2,64,512]{2,1,0:T(8,128)(2,1)S(1)}, u32[]{:S(2)}, u32[]{:S(2)}) collective-permute-start(bf16[2,64,512]{2,1,0:T(8,128)(2,1)S(1)} %get-tuple-element.75), channel_id=1, source_target_pairs={{0,4},{4,0},{8,12},{12,8},{16,20},{20,16},{24,28},{28,24},{1,5},{5... | collective-permute-start | bytes 393224 | tf_op jit(solution)/shard_map/ppermute | solution.py:523
  20.0 9.7 %collective-permute-start.9 = (bf16[64,768]{1,0:T(8,128)(2,1)S(1)}, bf16[64,768]{1,0:T(8,128)(2,1)S(1)}, u32[]{:S(2)}, u32[]{:S(2)}) collective-permute-start(bf16[64,768]{1,0:T(8,128)(2,1)S(1)} %get-tuple-element.99), channel_id=1, source_target_pairs={{0,8},{4,12},{8,0},{12,4},{16,24},{20,28},{24,16},{28,20},{1,9},{5... | collective-permute-start | bytes 294920 | tf_op jit(solution)/shard_map/ppermute | solution.py:523
  21.5 8.3 %collective-permute-start.10 = (bf16[64,768]{1,0:T(8,128)(2,1)S(1)}, bf16[64,768]{1,0:T(8,128)(2,1)S(1)}, u32[]{:S(2)}, u32[]{:S(2)}) collective-permute-start(bf16[64,768]{1,0:T(8,128)(2,1)S(1)} %get-tuple-element.100), channel_id=1, source_target_pairs={{0,16},{4,20},{8,24},{12,28},{16,0},{20,4},{24,8},{28,12},{1,17},{... | collective-permute-start | bytes 294920 | tf_op jit(solution)/shard_map/ppermute | solution.py:523
  23.0 6.7 %collective-permute-start.11 = (bf16[64,768]{1,0:T(8,128)(2,1)S(1)}, bf16[64,768]{1,0:T(8,128)(2,1)S(1)}, u32[]{:S(2)}, u32[]{:S(2)}) collective-permute-start(bf16[64,768]{1,0:T(8,128)(2,1)S(1)} %get-tuple-element.101), channel_id=1, source_target_pairs={{0,24},{4,28},{8,16},{12,20},{16,8},{20,12},{24,0},{28,4},{1,25},{... | collective-permute-start | bytes 294920 | tf_op jit(solution)/shard_map/ppermute | solution.py:523
  29.7 2.3 %collective-permute-start.12 = (bf16[4,64,1280]{2,1,0:T(8,128)(2,1)S(1)}, bf16[4,64,1280]{2,1,0:T(8,128)(2,1)S(1)}, u32[]{:S(2)}, u32[]{:S(2)}) collective-permute-start(bf16[4,64,1280]{2,1,0:T(8,128)(2,1)S(1)} %get-tuple-element.107), channel_id=1, source_target_pairs={{0,4},{4,0},{8,12},{12,8},{16,20},{20,16},{24,28},{28,24},{1,5},{5... | collective-permute-start | bytes 1966088 | tf_op jit(solution)/shard_map/ppermute | solution.py:523
  30.4 8.3 %collective-permute-start.15 = (bf16[32,768]{1,0:T(8,128)(2,1)S(1)}, bf16[32,768]{1,0:T(8,128)(2,1)S(1)}, u32[]{:S(2)}, u32[]{:S(2)}) collective-permute-start(bf16[32,768]{1,0:T(8,128)(2,1)S(1)} %get-tuple-element.118), channel_id=1, source_target_pairs={{0,1},{1,0},{2,3},{3,2},{4,5},{5,4},{6,7},{7,6},{8,9},{9,8},{10,11... | collective-permute-start | bytes 147464 | tf_op jit(solution)/shard_map/ppermute | solution.py:523
  32.8 8.0 %collective-permute-start.16 = (bf16[64,1280]{1,0:T(8,128)(2,1)S(1)}, bf16[64,1280]{1,0:T(8,128)(2,1)S(1)}, u32[]{:S(2)}, u32[]{:S(2)}) collective-permute-start(bf16[64,1280]{1,0:T(8,128)(2,1)S(1)} %get-tuple-element.120), channel_id=1, source_target_pairs={{0,8},{4,12},{8,0},{12,4},{16,24},{20,28},{24,16},{28,20},{1,9},{5... | collective-permute-start | bytes 491528 | tf_op jit(solution)/shard_map/ppermute | solution.py:523
  33.6 9.5 %collective-permute-start.17 = (bf16[64,1280]{1,0:T(8,128)(2,1)S(1)}, bf16[64,1280]{1,0:T(8,128)(2,1)S(1)}, u32[]{:S(2)}, u32[]{:S(2)}) collective-permute-start(bf16[64,1280]{1,0:T(8,128)(2,1)S(1)} %get-tuple-element.121), channel_id=1, source_target_pairs={{0,16},{4,20},{8,24},{12,28},{16,0},{20,4},{24,8},{28,12},{1,17},{... | collective-permute-start | bytes 491528 | tf_op jit(solution)/shard_map/ppermute | solution.py:523
  35.1 8.0 %collective-permute-start.18 = (bf16[64,1280]{1,0:T(8,128)(2,1)S(1)}, bf16[64,1280]{1,0:T(8,128)(2,1)S(1)}, u32[]{:S(2)}, u32[]{:S(2)}) collective-permute-start(bf16[64,1280]{1,0:T(8,128)(2,1)S(1)} %get-tuple-element.122), channel_id=1, source_target_pairs={{0,24},{4,28},{8,16},{12,20},{16,8},{20,12},{24,0},{28,4},{1,25},{... | collective-permute-start | bytes 491528 | tf_op jit(solution)/shard_map/ppermute | solution.py:523
  38.6 1.4 %collective-permute-start.13 = (bf16[4,64,256]{2,1,0:T(8,128)(2,1)S(1)}, bf16[4,64,256]{2,1,0:T(8,128)(2,1)S(1)}, u32[]{:S(2)}, u32[]{:S(2)}) collective-permute-start(bf16[4,64,256]{2,1,0:T(8,128)(2,1)S(1)} %get-tuple-element.111), channel_id=1, source_target_pairs={{0,4},{4,0},{8,12},{12,8},{16,20},{20,16},{24,28},{28,24},{1,5},{5... | collective-permute-start | bytes 393224 | tf_op jit(solution)/shard_map/ppermute | solution.py:523
  38.7 1.5 %collective-permute-start.14 = (bf16[4,64,256]{2,1,0:T(8,128)(2,1)S(1)}, bf16[4,64,256]{2,1,0:T(8,128)(2,1)S(1)}, u32[]{:S(2)}, u32[]{:S(2)}) collective-permute-start(bf16[4,64,256]{2,1,0:T(8,128)(2,1)S(1)} %get-tuple-element.112), channel_id=1, source_target_pairs={{0,4},{4,0},{8,12},{12,8},{16,20},{20,16},{24,28},{28,24},{1,5},{5... | collective-permute-start | bytes 393224 | tf_op jit(solution)/shard_map/ppermute | solution.py:523
  43.8 4.5 %collective-permute-start.19 = (bf16[32,1280]{1,0:T(8,128)(2,1)S(1)}, bf16[32,1280]{1,0:T(8,128)(2,1)S(1)}, u32[]{:S(2)}, u32[]{:S(2)}) collective-permute-start(bf16[32,1280]{1,0:T(8,128)(2,1)S(1)} %get-tuple-element.136), channel_id=1, source_target_pairs={{0,1},{1,0},{2,3},{3,2},{4,5},{5,4},{6,7},{7,6},{8,9},{9,8},{10,11... | collective-permute-start | bytes 245768 | tf_op jit(solution)/shard_map/ppermute | solution.py:523
  45.2 13.8 %copy-start = (f32[512]{0:T(512)S(1)}, f32[512]{0:T(512)}, u32[]{:S(2)}) copy-start(f32[512]{0:T(512)} %param.6) | copy-start | bytes 6148
  48.3 7.5 %collective-permute-start.23 = (bf16[32,2048]{1,0:T(8,128)(2,1)S(1)}, bf16[32,2048]{1,0:T(8,128)(2,1)S(1)}, u32[]{:S(2)}, u32[]{:S(2)}) collective-permute-start(bf16[32,2048]{1,0:T(8,128)(2,1)S(1)} %join_terms.1.kept_ref), channel_id=1, source_target_pairs={{0,2},{1,3},{2,0},{3,1},{4,6},{5,7},{6,4},{7,5},{8,10},{9,11},{10,... | collective-permute-start | bytes 393224 | tf_op jit(solution)/shard_map/ppermute | solution.py:523
  51.0 5.8 %collective-permute-start.20 = (bf16[128,512]{1,0:T(8,128)(2,1)S(1)}, bf16[128,512]{1,0:T(8,128)(2,1)S(1)}, u32[]{:S(2)}, u32[]{:S(2)}) collective-permute-start(bf16[128,512]{1,0:T(8,128)(2,1)S(1)} %get-tuple-element.138), channel_id=1, source_target_pairs={{0,8},{4,12},{8,0},{12,4},{16,24},{20,28},{24,16},{28,20},{1,9},{5... | collective-permute-start | bytes 393224 | tf_op jit(solution)/shard_map/ppermute | solution.py:523
  52.2 5.0 %collective-permute-start.21 = (bf16[128,512]{1,0:T(8,128)(2,1)S(1)}, bf16[128,512]{1,0:T(8,128)(2,1)S(1)}, u32[]{:S(2)}, u32[]{:S(2)}) collective-permute-start(bf16[128,512]{1,0:T(8,128)(2,1)S(1)} %get-tuple-element.139), channel_id=1, source_target_pairs={{0,16},{4,20},{8,24},{12,28},{16,0},{20,4},{24,8},{28,12},{1,17},{... | collective-permute-start | bytes 393224 | tf_op jit(solution)/shard_map/ppermute | solution.py:523
  53.1 5.9 %collective-permute-start.22 = (bf16[128,512]{1,0:T(8,128)(2,1)S(1)}, bf16[128,512]{1,0:T(8,128)(2,1)S(1)}, u32[]{:S(2)}, u32[]{:S(2)}) collective-permute-start(bf16[128,512]{1,0:T(8,128)(2,1)S(1)} %get-tuple-element.140), channel_id=1, source_target_pairs={{0,24},{4,28},{8,16},{12,20},{16,8},{20,12},{24,0},{28,4},{1,25},{... | collective-permute-start | bytes 393224 | tf_op jit(solution)/shard_map/ppermute | solution.py:523
  55.9 5.0 %collective-permute-start.24 = (bf16[32,2048]{1,0:T(8,128)(2,1)S(1)}, bf16[32,2048]{1,0:T(8,128)(2,1)S(1)}, u32[]{:S(2)}, u32[]{:S(2)}) collective-permute-start(bf16[32,2048]{1,0:T(8,128)(2,1)S(1)} %add_pairs.1.held_ref), channel_id=1, source_target_pairs={{0,1},{1,0},{2,3},{3,2},{4,5},{5,4},{6,7},{7,6},{8,9},{9,8},{10,11... | collective-permute-start | bytes 393224 | tf_op jit(solution)/shard_map/ppermute | solution.py:523

commit v7 on v6

--- a/solution.py
+++ b/solution.py
@@ -138,8 +138,9 @@
 
 
 def row_part(
-    x_any, cot_any, gain_any, wqkv_any, wout_any, out_ref, grads_any,
-    x_ref, cot_ref, gain_ref, w_ref, wo_ref, dk_ref, dv_ref, grads_ref, sems,
+    x_any, cot_any, gain_any, wqkv_any, wout_any,
+    out_ref, hidden_ref, x_ref, cot_ref,
+    gain_ref, w_ref, wo_ref, dk_ref, dv_ref, grads_ref, sems,
 ):
     first = started(
         pltpu.make_async_copy(x_any, x_ref, sems.at[4]),
@@ -183,10 +184,9 @@
     grads_ref[:, :HW] = transposed(jnp.concatenate(dq_blocks, 1))
     grads_ref[:, HW : 2 * HW] = dk_ref[...].astype(BF16)
     grads_ref[:, 2 * HW :] = dv_ref[...].astype(BF16)
-    handed = started(pltpu.make_async_copy(grads_ref, grads_any, sems.at[4]))
     term_qkv = dot_nn(hidden_t, grads_ref[...]).astype(BF16)
     out_ref[...] = dot_nn(jnp.concatenate(att_blocks, 1), cot).astype(BF16)
-    finished(*handed)
+    hidden_ref[...] = dot_nt(grads_ref[...], w_ref[...])
     return term_qkv
 
 
@@ -196,12 +196,16 @@
 
 def row_chip_kernel(
     place_ref, x_any, cot_any, gain_any, wqkv_any, wout_any,
-    send_1, send_2, keep_1, keep_2, *refs,
+    send_1, send_2, keep_1, keep_2, rows_ref, *refs,
 ):
+    rows = rows_ref.shape[0]
+    at = pl.multiple_of((place_ref[0] * 2 + place_ref[1]) * rows, rows)
+    own = started(pltpu.make_async_copy(wqkv_any.at[pl.ds(at, rows), :], rows_ref, refs[-1].at[7]))
     term_qkv = row_part(x_any, cot_any, gain_any, wqkv_any, wout_any, *refs)
     chips, lanes = slice(0, send_1.shape[0]), slice(0, send_1.shape[2])
     split_cores(term_qkv[:, : lanes.stop], place_ref[1], send_1, keep_1, chips, lanes)
     split_cores(term_qkv[:, lanes.stop :], place_ref[1], send_2, keep_2, chips, lanes)
+    finished(*own)
 
 
 def column_part(moved_ref, gain_ref, w_ref, wo_ref, weight_waits, grads_ref):
@@ -257,8 +261,8 @@
 
 def column_kernel(
     moved_any, gain_any, wqkv_any, wout_any, row_qkv_ref, row_out_ref,
-    terms_ref, grads_ref,
-    moved_ref, gain_ref, w_ref, wo_ref, sems,
+    terms_ref, grads_ref, w_ref,
+    moved_ref, gain_ref, wo_ref, sems,
 ):
     copies = started(
         pltpu.make_async_copy(moved_any, moved_ref, sems.at[4]),
@@ -280,8 +284,8 @@
     place_ref, x_any, cot_any, own_any,
     near_1, near_2, near_3, far_1, far_2, far_3,
     gain_any, wqkv_any, wout_any, row_out_ref,
-    send_ref, keep_ref, grads_ref,
-    moved_ref, gain_ref, w_ref, wo_ref, sems,
+    send_ref, keep_ref, grads_ref, w_ref,
+    moved_ref, gain_ref, wo_ref, sems,
 ):
     chip, core = place_ref[0], place_ref[1]
     share = moved_ref.shape[2]
@@ -315,8 +319,7 @@
     split_cores(term_out, *refs, slice(chips // 2, chips), out_lanes)
 
 
-def back_kernel(grads_ref, wqkv_any, back_ref, w_ref, sems):
-    finished(*started(*qkv_copies(wqkv_any, w_ref, sems, 1)))
+def back_kernel(grads_ref, w_ref, back_ref):
     grad_hidden = dot_nt(grads_ref[...], w_ref[...])
     all_rows, share, width = back_ref.shape
     group = math.gcd(share, 16)
@@ -326,11 +329,9 @@
         back_ref[:, i * group : (i + 1) * group, :] = piece.astype(BF16)
 
 
-def back_chip_kernel(place_ref, grads_ref, wqkv_any, send_1, send_2, keep_ref, w_ref, sems):
-    finished(*started(*qkv_copies(wqkv_any, w_ref, sems, 1)))
+def back_chip_kernel(place_ref, grads_ref, w_ref, send_ref, keep_ref):
     grad_hidden = dot_nt(grads_ref[...], w_ref[...])
     chips, share, width = keep_ref.shape
-    half = width // 2
     group = math.gcd(share, 16)
     block = 2 * chips * group
     first = place_ref[1] == 0
@@ -338,39 +339,23 @@
         piece = grad_hidden[i * block : (i + 1) * block].reshape(chips, 2, group, width)
         even, odd = piece[:, 0], piece[:, 1]
         at = slice(i * group, (i + 1) * group)
-        sent = jnp.where(first, odd, even).astype(BF16)
-        send_1[:, at, :], send_2[:, at, :] = sent[:, :, :half], sent[:, :, half:]
+        send_ref[:, at, :] = jnp.where(first, odd, even).astype(BF16)
         keep_ref[:, at, :] = jnp.where(first, even, odd).astype(BF16)
 
 
-def back_pack_kernel(place_ref, keep_ref, got_1, got_2, own_ref, off_1, off_2, off_3):
+def back_pack_kernel(place_ref, keep_ref, got_ref, own_ref, off_1, off_2, off_3):
     chip, core = place_ref[0], place_ref[1]
-    share, half = keep_ref.shape[1], got_1.shape[2]
+    share = keep_ref.shape[1]
     kept_at = pl.multiple_of(core * share, share)
     got_at = pl.multiple_of((1 - core) * share, share)
     for i, target in enumerate((own_ref, off_1, off_2, off_3)):
         target[pl.ds(kept_at, share), :] = keep_ref[chip ^ i]
-        target[pl.ds(got_at, share), :half] = got_1[chip ^ i]
-        target[pl.ds(got_at, share), half:] = got_2[chip ^ i]
-
-
-def input_kernel(
-    x_any, cot_any, gain_any, grads_any, wqkv_any, back_ref, grad_ref,
-    x_ref, cot_ref, gain_ref, grads_ref, w_ref, sems,
-):
-    products = started(
-        pltpu.make_async_copy(grads_any, grads_ref, sems.at[3]),
-        *qkv_copies(wqkv_any, w_ref, sems, 0),
-    )
-    others = started(
-        pltpu.make_async_copy(x_any, x_ref, sems.at[4]),
-        pltpu.make_async_copy(gain_any, gain_ref, sems.at[5]),
-        pltpu.make_async_copy(cot_any, cot_ref, sems.at[6]),
-    )
-    finished(*products)
-    grad_hidden = dot_nt(grads_ref[...], w_ref[...]) + back_ref[...].astype(F32)
-    finished(*others)
+        target[pl.ds(got_at, share), :] = got_ref[chip ^ i]
+
+
+def input_kernel(x_ref, cot_ref, gain_ref, hidden_ref, back_ref, grad_ref):
     inverse_rms, normed = rms_parts(x_ref[...].astype(F32))
+    grad_hidden = hidden_ref[...] + back_ref[...].astype(F32)
     grad_ref[...] = input_grad(normed, inverse_rms, grad_hidden, gain_ref[...], cot_ref[...])
 
 
@@ -379,27 +364,6 @@
     projected = jnp.mean(grad_normed * normed, -1, keepdims=True)
     grad = inverse_rms * (grad_normed - normed * projected)
     return (cot.astype(F32) + grad).astype(BF16)
-
-
-def ready_kernel(
-    place_ref, grads_any, wqkv_any, x_any, cot_any,
-    hidden_ref, rows_ref, x_ref, cot_ref,
-    grads_ref, w_ref, sems,
-):
-    rows = rows_ref.shape[0]
-    at = pl.multiple_of((place_ref[0] * 2 + place_ref[1]) * rows, rows)
-    products = started(
-        pltpu.make_async_copy(grads_any, grads_ref, sems.at[3]),
-        *qkv_copies(wqkv_any, w_ref, sems, 0),
-    )
-    others = started(
-        pltpu.make_async_copy(wqkv_any.at[pl.ds(at, rows), :], rows_ref, sems.at[4]),
-        pltpu.make_async_copy(x_any, x_ref, sems.at[5]),
-        pltpu.make_async_copy(cot_any, cot_ref, sems.at[6]),
-    )
-    finished(*products)
-    hidden_ref[...] = dot_nt(grads_ref[...], w_ref[...])
-    finished(*others)
 
 
 def input_chip_kernel(
@@ -466,28 +430,25 @@
     out_ref[...] = (kept_ref[...].astype(F32) + got_ref[...].astype(F32)).astype(BF16)
 
 
-def join_kernel(row_ref, kept_ref, got_ref, out_ref):
-    cut = row_ref.shape[1]
-    out_ref[:, :cut] = row_ref[...]
-    out_ref[:, cut:] = (kept_ref[...] + got_ref[...].astype(F32)).astype(BF16)
-
-
-def result_kernel(place_ref, held_ref, got_ref, w_ref, gain_ref, qkv_ref, out_ref, grad_ref):
+def result_kernel(
+    place_ref, row_held, row_got, held_ref, got_ref, w_ref, gain_ref, qkv_ref, out_ref, grad_ref
+):
     rows = qkv_ref.shape[0]
     at = pl.multiple_of((place_ref[0] * 2 + place_ref[1]) * rows, rows)
     upper = place_ref[2] == 1
     half = rows // 2
     width = out_ref.shape[1]
 
-    def ordered(lanes):
+    def ordered(held_ref, got_ref, lanes):
         held, got = held_ref[:, lanes].astype(F32), got_ref[:, lanes].astype(F32)
         return (jnp.where(upper, got, held), jnp.where(upper, held, got))
 
     for i in range(3):
-        for at_from, at_to in ((i * HW, i * width), ((3 + i) * HW, i * width + HW)):
+        lanes = slice(i * HW, (i + 1) * HW)
+        for at_to, pair in ((i * width, (row_held, row_got)), (i * width + HW, (held_ref, got_ref))):
             to = slice(at_to, at_to + HW)
-            qkv_ref[:half, to], qkv_ref[half:, to] = ordered(slice(at_from, at_from + HW))
-    out_ref[:half], out_ref[half:] = ordered(slice(6 * HW, 6 * HW + width))
+            qkv_ref[:half, to], qkv_ref[half:, to] = ordered(*pair, lanes)
+    out_ref[:half], out_ref[half:] = ordered(held_ref, got_ref, slice(3 * HW, 3 * HW + width))
     total = jnp.sum(qkv_ref[...] * w_ref[...].astype(F32), -1, keepdims=True)
     shape = (rows, gain_ref.shape[1])
     row = lax.broadcasted_iota(jnp.int32, shape, 0)
@@ -577,7 +538,7 @@
         pltpu.VMEM((HW, width), BF16),
     ]
     weights = [(HBM, gain), (HBM, qkv_weight), (HBM, out_weight)]
-    grads_out = ((columns, 3 * HW), BF16)
+    col_outs = [((columns, 3 * HW), BF16), ((width, 3 * HW), BF16)]
 
     if layered:
         packed = call(
@@ -598,25 +559,29 @@
 
     split_out = ((chips, row_share, row_width // 2), BF16)
     term_outs = [split_out] * 4 if layered else [((width, row_width), BF16)]
-    *row_terms, row_out, row_grads = call(
+    if layered:
+        term_outs.append(((row_share, 3 * width), BF16))
+    *row_terms, row_out, row_hidden, x_near, cot_near = call(
         row_chip_kernel if layered else row_kernel,
         "row_heads",
         [(SMEM, placed)] * layered + [(HBM, x), (HBM, cot), *weights],
-        [*term_outs, ((HW, width), BF16), grads_out],
         [
-            pltpu.VMEM((columns, width), BF16),
-            pltpu.VMEM((columns, width), BF16),
+            *term_outs, ((HW, width), BF16), ((columns, width), F32),
+            ((columns, width), BF16), ((columns, width), BF16),
+        ],
+        [
             *weight_scratch,
             pltpu.VMEM((columns, HW), F32),
             pltpu.VMEM((columns, HW), F32),
             pltpu.VMEM((columns, 3 * HW), BF16),
-            pltpu.SemaphoreType.DMA((7,)),
+            pltpu.SemaphoreType.DMA((8,)),
         ],
         BIG_VMEM,
-        [VMEM] * len(term_outs) + [VMEM, HBM],
+        [VMEM] * 4 * layered + [PINNED] * 5 if layered else [VMEM] * 5,
     )
     moved_scratch = pltpu.VMEM((n, 2, share, width), BF16)
     if layered:
+        *row_terms, weight_rows = row_terms
         near_1, *row_terms = lax.optimization_barrier((near_1, *row_terms))
         row_sent = [swap(one, "seq", 1) for one in row_terms[:2]]
         row_owned, *row_off = add_cores(place, row_terms[2:], row_sent, "row")
@@ -625,7 +590,7 @@
         )
         far_3, far_1, far_2 = swap(near_3, "seq", 1), swap(near_1, "seq", 1), swap(near_2, "seq", 1)
         row_got = cross_chips(*row_off)
-        send, keep, col_grads = call(
+        send, keep, *col_grads = call(
             column_chip_kernel,
             "column_heads",
             [
@@ -633,61 +598,37 @@
                 (ANY, near_1), (ANY, near_2), (ANY, near_3),
                 (ANY, far_1), (ANY, far_2), (ANY, far_3), *weights, (VMEM, row_out),
             ],
-            [((chips, row_share, col_width), BF16)] * 2 + [grads_out],
-            [moved_scratch, *weight_scratch, pltpu.SemaphoreType.DMA((21,))],
+            [((chips, row_share, col_width), BF16)] * 2 + col_outs,
+            [moved_scratch, weight_scratch[0], weight_scratch[2], pltpu.SemaphoreType.DMA((21,))],
             BIG_VMEM,
+            [VMEM, VMEM, PINNED, PINNED],
         )
         send, row_got = lax.optimization_barrier((send, row_got))
         row_next, row_kept = add_chips(place, row_owned, row_got, "row")
-        row_pair = add_two(row_kept, swap(row_next, "dp", 1), "row_add_pair")
-        keep, row_kept = lax.optimization_barrier((keep, row_kept))
+        back_send, back_keep = call(
+            back_chip_kernel,
+            "column_grad_hidden",
+            [(SMEM, place), *[(VMEM, one) for one in col_grads]],
+            [((chips, share, width), BF16)] * 2,
+        )
+        keep, row_kept, back_keep = lax.optimization_barrier((keep, row_kept, back_keep))
         owned, *off = add_cores(place, [keep], [swap(send, "seq", 1)], "column")
         got = cross_chips(*off)
-        col_grads, owned = lax.optimization_barrier((col_grads, owned))
-        *back_parts, back_keep = call(
-            back_chip_kernel,
-            "column_grad_hidden",
-            [(SMEM, place), (VMEM, col_grads), (HBM, qkv_weight)],
-            [((chips, share, width // 2), BF16)] * 2 + [((chips, share, width), BF16)],
-            [pltpu.VMEM((width, 3 * HW), BF16), pltpu.SemaphoreType.DMA((3,))],
-        )
+        row_pair = add_two(row_kept, swap(row_next, "dp", 1), "row_add_pair")
+        row_pair, _ = lax.optimization_barrier((row_pair, owned))
+        row_held = add_two(row_pair, swap(row_pair, "dp", 2), "row_add_pairs")
         back = call(
             back_pack_kernel,
             "pack_grad_hidden",
-            [
-                (SMEM, place), (VMEM, back_keep),
-                *[(VMEM, swap(part, "seq", 1)) for part in back_parts],
-            ],
+            [(SMEM, place), (VMEM, back_keep), (VMEM, swap(back_send, "seq", 1))],
             [((2 * share, width), BF16)] * 4,
         )
-        *back, owned, row_pair = lax.optimization_barrier((*back, owned, row_pair))
+        *back, owned, row_held = lax.optimization_barrier((*back, owned, row_held))
         to_next, kept = add_chips(place, owned, got, "column")
-        row_grads, kept = lax.optimization_barrier((row_grads, kept))
-        row_hidden, weight_rows, x_near, cot_near = call(
-            ready_kernel,
-            "row_grad_hidden",
-            [(SMEM, place), (HBM, row_grads), (HBM, qkv_weight), (HBM, x), (HBM, cot)],
-            [
-                ((columns, width), F32), ((row_share, 3 * width), BF16),
-                ((columns, width), BF16), ((columns, width), BF16),
-            ],
-            [
-                pltpu.VMEM((columns, 3 * HW), BF16),
-                pltpu.VMEM((width, 3 * HW), BF16),
-                pltpu.SemaphoreType.DMA((7,)),
-            ],
-            out_specs=[PINNED] * 4,
-        )
-        kept, row_hidden = lax.optimization_barrier((kept, row_hidden))
-        (joined,) = call(
-            join_kernel,
-            "join_terms",
-            [(VMEM, row_pair), (VMEM, kept), (VMEM, swap(to_next, "dp", 1))],
-            [((row_share // 2, row_width + col_width), BF16)],
-        )
-        *back, joined = lax.optimization_barrier((*back, joined))
-        held = add_two(joined, swap(joined, "dp", 2), "add_pairs")
-        other = swap(held, "dp", 1)
+        *back, kept = lax.optimization_barrier((*back, kept))
+        row_other = swap(row_held, "dp", 1)
+        pair_sum = add_two(kept, swap(to_next, "dp", 1), "column_add_pair")
+        held = add_two(pair_sum, swap(pair_sum, "dp", 2), "column_add_pairs")
         (grad,) = call(
             input_chip_kernel,
             "input_grad",
@@ -697,48 +638,42 @@
             ],
             [((columns, width), BF16)],
         )
+        held, row_other, grad = lax.optimization_barrier((held, row_other, grad))
+        other = swap(held, "dp", 1)
         sum_qkv, sum_out, sum_gain = call(
             result_kernel,
             "result",
             [
-                (SMEM, place), (VMEM, held), (VMEM, other), (VMEM, weight_rows), (VMEM, gain),
+                (SMEM, place), (VMEM, row_held), (VMEM, row_other), (VMEM, held), (VMEM, other),
+                (VMEM, weight_rows), (VMEM, gain),
             ],
             [((row_share, 3 * width), F32), ((row_share, width), F32), ((1, row_share), F32)],
         )
         sum_gain = sum_gain.reshape(row_share)
     else:
-        terms, col_grads = call(
+        terms, *col_grads = call(
             column_kernel,
             "column_heads",
             [(ANY, moved), *weights, (VMEM, row_terms[0]), (VMEM, row_out)],
-            [((width, 4 * width), BF16), grads_out],
-            [moved_scratch, *weight_scratch, pltpu.SemaphoreType.DMA((6,))],
+            [((width, 4 * width), BF16), *col_outs],
+            [moved_scratch, weight_scratch[0], weight_scratch[2], pltpu.SemaphoreType.DMA((6,))],
             BIG_VMEM,
         )
         (back,) = call(
             back_kernel,
             "column_grad_hidden",
-            [(VMEM, col_grads), (HBM, qkv_weight)],
+            [(VMEM, one) for one in col_grads],
             [((n, share, width), BF16)],
-            [pltpu.VMEM((width, 3 * HW), BF16), pltpu.SemaphoreType.DMA((3,))],
         )
         returned = lax.all_to_all(back, "seq", split_axis=0, concat_axis=0, tiled=True)
         (grad,) = call(
             input_kernel,
             "input_grad",
             [
-                (HBM, x), (HBM, cot), (HBM, gain), (HBM, row_grads), (HBM, qkv_weight),
+                (VMEM, x_near), (VMEM, cot_near), (VMEM, gain), (VMEM, row_hidden),
                 (VMEM, returned.reshape(columns, width)),
             ],
             [((columns, width), BF16)],
-            [
-                pltpu.VMEM((columns, width), BF16),
-                pltpu.VMEM((columns, width), BF16),
-                pltpu.VMEM((1, width), F32),
-                pltpu.VMEM((columns, 3 * HW), BF16),
-                pltpu.VMEM((width, 3 * HW), BF16),
-                pltpu.SemaphoreType.DMA((7,)),
-            ],
         )
         terms = lax.all_to_all(
             terms.reshape(n, row_share, 4 * width), "seq", split_axis=0, concat_axis=0, tiled=True

time: 62.6 us -> 64.4 us (1.029)
  starting transfers between devices: 23.9 us -> 30.2 us
  Pallas kernels: 26.2 us -> 22.5 us
  waiting for transfers between devices: 11.4 us -> 10.6 us
    ppermute x25 -> x26, starting transfers between devices: 23.9 us -> 30.2 us  [swap(): return lax.ppermute(array, axis, [(i, i ^ bits) for i in range(count)])]
    pallas_call x15, Pallas kernels: 26.2 us -> 22.5 us  [call(): pl.pallas_call(kernel, out_shape=outs, in_specs=[spec for spec, _ in ins]...]
    ppermute x25 -> x26, waiting for transfers between devices: 11.4 us -> 10.6 us  [swap(): return lax.ppermute(array, axis, [(i, i ^ bits) for i in range(count)])]
  transfers between devices with their start and end apart: 25 -> 26, of which waited for: 13 -> 8; matrix products, arithmetic and copies ran while one was open for 0% -> 0% of each run, Pallas kernels for 36% -> 29%
where the time goes in v7:
time: 64.4 us; the launch traced here: 64.2 us
  starting transfers between devices  30.2 us (47%)
  Pallas kernels  22.5 us (35%)
  waiting for transfers between devices  10.6 us (16%)
  between operations  0.85 us (1%)
    ppermute x26, starting transfers between devices, swap(): return lax.ppermute(array, axis, [(i, i ^ bits) for i in range(count)])  30.2 us
    pallas_call x15, Pallas kernels, call(): pl.pallas_call(kernel, out_shape=outs, in_specs=[spec for spec, _ in ins]...  22.5 us
    ppermute x26, waiting for transfers between devices, swap(): return lax.ppermute(array, axis, [(i, i ^ bits) for i in range(count)])  10.6 us
  transfers between devices with their start and end apart: 26, of which 8 were waited for; matrix products, arithmetic and copies ran while one was open for 0% of the time, Pallas kernels for 29%

profile of v7, /device:TPU:0, one launch (start us, length us, event | category | flops | bytes accessed | tf_op | source)
XLA Modules:
  0.0 64.2 jit_solution(6112495556674596191)
XLA Ops:
  0.7 0.1 pad_add_fusion.place_ref
  0.7 1.9 %pack_columns.1 = (bf16[2,64,512]{2,1,0:T(8,128)(2,1)S(1)}, bf16[2,128,512]{2,1,0:T(8,128)(2,1)S(1)}, bf16[2,128,512]{2,1,0:T(8,128)(2,1)S(1)}, bf16[2,128,512]{2,1,0:T(8,128)(2,1)S(1)}) custom-call(s32[3]{0:T(128)S(1)} %pad_add_fusion.place_ref, bf16[512,512]{1,0:T(8,128)(2,1)} %bitcast.12, bf16[512,512]{1,0:T(8,128)(2,1)} %bitcast.15), custom_call_target="tpu_custom_call" | custom-call | tf_op jit(solution)/shard_map/pack_columns/pallas_call | solution.py:470
  2.6 3.0 %collective-permute-start.1 = (bf16[2,128,512]{2,1,0:T(8,128)(2,1)S(1)}, bf16[2,128,512]{2,1,0:T(8,128)(2,1)S(1)}, u32[]{:S(2)}, u32[]{:S(2)}) collective-permute-start(bf16[2,128,512]{2,1,0:T(8,128)(2,1)S(1)} %get-tuple-element.75), channel_id=1, source_target_pairs={{0,8},{4,12},{8,0},{12,4},{16,24},{20,28},{24,16},{28,20},{1,9},{5... | collective-permute-start | bytes 786440 | tf_op jit(solution)/shard_map/ppermute | solution.py:484
  5.6 1.5 %collective-permute-start.2 = (bf16[2,128,512]{2,1,0:T(8,128)(2,1)S(1)}, bf16[2,128,512]{2,1,0:T(8,128)(2,1)S(1)}, u32[]{:S(2)}, u32[]{:S(2)}) collective-permute-start(bf16[2,128,512]{2,1,0:T(8,128)(2,1)S(1)} %get-tuple-element.82), channel_id=1, source_target_pairs={{0,16},{4,20},{8,24},{12,28},{16,0},{20,4},{24,8},{28,12},{1,17},{... | collective-permute-start | bytes 786440 | tf_op jit(solution)/shard_map/ppermute | solution.py:484
  7.1 0.0 collective-permute-start.3
  7.1 7.6 %row_heads.1 = (bf16[4,64,384]{2,1,0:T(8,128)(2,1)S(1)}, bf16[4,64,384]{2,1,0:T(8,128)(2,1)S(1)}, bf16[4,64,384]{2,1,0:T(8,128)(2,1)S(1)}, bf16[4,64,384]{2,1,0:...) custom-call(s32[3]{0:T(128)S(1)} %pad_add_fusion.place_ref, ...), custom_call_target="tpu_custom_call" | custom-call | tf_op jit(solution)/shard_map/row_heads/pallas_call | solution.py:470
  14.7 0.0 collective-permute-done.1.near_1
  14.7 0.1 collective-permute-start.4
  14.8 0.5 collective-permute-start.5
  15.3 0.9 %collective-permute-done.4.refs_2_ = bf16[4,64,384]{2,1,0:T(8,128)(2,1)S(1)} collective-permute-done((bf16[4,64,384]{2,1,0:T(8,128)(2,1)S(1)}, bf16[4,64,384]{2,1,0:T(8,128)(2,1)S(1)}, u32[]{:S(2)}, u32[]{:S(2)}) %collective-permute-start.4) | collective-permute-done | bytes 196640 | tf_op jit(solution)/shard_map/ppermute | solution.py:484
  16.3 0.3 collective-permute-done.5.refs_3_
  16.5 0.6 row_add_cores.1
  17.2 1.8 %collective-permute-done.2.near_2 = bf16[2,128,512]{2,1,0:T(8,128)(2,1)S(1)} collective-permute-done((bf16[2,128,512]{2,1,0:T(8,128)(2,1)S(1)}, bf16[2,128,512]{2,1,0:T(8,128)(2,1)S(1)}, u32[]{:S(2)}, u32[]{:S(2)}) %collective-permute-start.2) | collective-permute-done | bytes 262176 | tf_op jit(solution)/shard_map/ppermute | solution.py:484
  19.0 0.5 collective-permute-start.7
  19.5 0.0 collective-permute-start.8
  19.5 0.5 collective-permute-start
  20.0 1.2 %collective-permute-start.9 = (bf16[64,768]{1,0:T(8,128)(2,1)S(1)}, bf16[64,768]{1,0:T(8,128)(2,1)S(1)}, u32[]{:S(2)}, u32[]{:S(2)}) collective-permute-start(bf16[64,768]{1,0:T(8,128)(2,1)S(1)} %get-tuple-element.96), channel_id=1, source_target_pairs={{0,8},{4,12},{8,0},{12,4},{16,24},{20,28},{24,16},{28,20},{1,9},{5... | collective-permute-start | bytes 294920 | tf_op jit(solution)/shard_map/ppermute | solution.py:484
  21.2 0.2 collective-permute-done.own_any
  21.5 1.5 %collective-permute-start.10 = (bf16[64,768]{1,0:T(8,128)(2,1)S(1)}, bf16[64,768]{1,0:T(8,128)(2,1)S(1)}, u32[]{:S(2)}, u32[]{:S(2)}) collective-permute-start(bf16[64,768]{1,0:T(8,128)(2,1)S(1)} %get-tuple-element.97), channel_id=1, source_target_pairs={{0,16},{4,20},{8,24},{12,28},{16,0},{20,4},{24,8},{28,12},{1,17},{... | collective-permute-start | bytes 294920 | tf_op jit(solution)/shard_map/ppermute | solution.py:484
  23.0 1.2 %collective-permute-start.11 = (bf16[64,768]{1,0:T(8,128)(2,1)S(1)}, bf16[64,768]{1,0:T(8,128)(2,1)S(1)}, u32[]{:S(2)}, u32[]{:S(2)}) collective-permute-start(bf16[64,768]{1,0:T(8,128)(2,1)S(1)} %get-tuple-element.98), channel_id=1, source_target_pairs={{0,24},{4,28},{8,16},{12,20},{16,8},{20,12},{24,0},{28,4},{1,25},{... | collective-permute-start | bytes 294920 | tf_op jit(solution)/shard_map/ppermute | solution.py:484
  24.2 5.4 %column_heads.1 = (bf16[4,64,1280]{2,1,0:T(8,128)(2,1)S(1)}, bf16[4,64,1280]{2,1,0:T(8,128)(2,1)S(1)}, bf16[512,768]{1,0:T(8,128)(2,1)S(1)}, bf16[512,768]{1,0:T(8,128)(2,1)S(1)}) custom-call(s32[3]{0:T(128)S(1)} %pad_add_fusion.place_ref, bf16[512,512]{1,0:T(8,128)(2,1)} %bitcast.14, bf16[512,512]{1,0:T(8,128)(2,1)} %bitcast.17, ...), custom_call_target="tpu_custom_call" | custom-call | tf_op jit(solution)/shard_map/column_heads/pallas_call | solution.py:470
  29.5 0.0 collective-permute-done.9.got_1
  29.6 0.1 collective-permute-start.13
  29.6 1.1 %column_grad_hidden.1 = (bf16[4,64,512]{2,1,0:T(8,128)(2,1)S(1)}, bf16[4,64,512]{2,1,0:T(8,128)(2,1)S(1)}) custom-call(s32[3]{0:T(128)S(1)} %pad_add_fusion.place_ref, bf16[512,768]{1,0:T(8,128)(2,1)S(1)} %get-tuple-element.103.grads_ref, bf16[512,768]{1,0:T(8,128)(2,1)S(1)} %get-tuple-element.104.w_ref), custom_call_target="tpu_custom_call" | custom-call | tf_op jit(solution)/shard_map/column_grad_hidden/pallas_call | solution.py:470
  30.8 0.6 collective-permute-start.12
  31.3 0.6 row_add_chips.1
  31.9 0.0 copy-start
  32.0 0.7 %column_add_cores.1 = (f32[64,1280]{1,0:T(8,128)S(1)}, bf16[64,1280]{1,0:T(8,128)(2,1)S(1)}, bf16[64,1280]{1,0:T(8,128)(2,1)S(1)}, bf16[64,1280]{1,0:T(8,128)(2,1)S(1)}) custom-call(s32[3]{0:T(128)S(1)} %pad_add_fusion.place_ref, bf16[4,64,1280]{2,1,0:T(8,128)(2,1)S(1)} %get-tuple-element.112.refs_0_, bf16[4,64,1280]{2,1,0:T(8,128)(2,1)S(1)} %collective-permute-done.13.refs_1_), custom_call_target="tpu_custom_call" | custom-call | tf_op jit(solution)/shard_map/column_add_cores/pallas_call | solution.py:470
  32.7 0.9 %collective-permute-start.16 = (bf16[64,1280]{1,0:T(8,128)(2,1)S(1)}, bf16[64,1280]{1,0:T(8,128)(2,1)S(1)}, u32[]{:S(2)}, u32[]{:S(2)}) collective-permute-start(bf16[64,1280]{1,0:T(8,128)(2,1)S(1)} %get-tuple-element.123), channel_id=1, source_target_pairs={{0,8},{4,12},{8,0},{12,4},{16,24},{20,28},{24,16},{28,20},{1,9},{5... | collective-permute-start | bytes 491528 | tf_op jit(solution)/shard_map/ppermute | solution.py:484
  33.5 1.5 %collective-permute-start.17 = (bf16[64,1280]{1,0:T(8,128)(2,1)S(1)}, bf16[64,1280]{1,0:T(8,128)(2,1)S(1)}, u32[]{:S(2)}, u32[]{:S(2)}) collective-permute-start(bf16[64,1280]{1,0:T(8,128)(2,1)S(1)} %get-tuple-element.124), channel_id=1, source_target_pairs={{0,16},{4,20},{8,24},{12,28},{16,0},{20,4},{24,8},{28,12},{1,17},{... | collective-permute-start | bytes 491528 | tf_op jit(solution)/shard_map/ppermute | solution.py:484
  35.0 1.2 %collective-permute-start.18 = (bf16[64,1280]{1,0:T(8,128)(2,1)S(1)}, bf16[64,1280]{1,0:T(8,128)(2,1)S(1)}, u32[]{:S(2)}, u32[]{:S(2)}) collective-permute-start(bf16[64,1280]{1,0:T(8,128)(2,1)S(1)} %get-tuple-element.125), channel_id=1, source_target_pairs={{0,24},{4,28},{8,16},{12,20},{16,8},{20,12},{24,0},{28,4},{1,25},{... | collective-permute-start | bytes 491528 | tf_op jit(solution)/shard_map/ppermute | solution.py:484
  36.2 1.6 %collective-permute-start.14 = (bf16[32,768]{1,0:T(8,128)(2,1)S(1)}, bf16[32,768]{1,0:T(8,128)(2,1)S(1)}, u32[]{:S(2)}, u32[]{:S(2)}) collective-permute-start(bf16[32,768]{1,0:T(8,128)(2,1)S(1)} %get-tuple-element.116), channel_id=1, source_target_pairs={{0,1},{1,0},{2,3},{3,2},{4,5},{5,4},{6,7},{7,6},{8,9},{9,8},{10,11... | collective-permute-start | bytes 147464 | tf_op jit(solution)/shard_map/ppermute | solution.py:484
  37.8 2.5 %collective-permute-done.14.got_ref = bf16[32,768]{1,0:T(8,128)(2,1)S(1)} collective-permute-done((bf16[32,768]{1,0:T(8,128)(2,1)S(1)}, bf16[32,768]{1,0:T(8,128)(2,1)S(1)}, u32[]{:S(2)}, u32[]{:S(2)}) %collective-permute-start.14) | collective-permute-done | bytes 49184 | tf_op jit(solution)/shard_map/ppermute | solution.py:484
  40.3 2.7 %collective-permute-start.15 = (bf16[32,768]{1,0:T(8,128)(2,1)S(1)}, bf16[32,768]{1,0:T(8,128)(2,1)S(1)}, u32[]{:S(2)}, u32[]{:S(2)}) collective-permute-start(bf16[32,768]{1,0:T(8,128)(2,1)S(1)} %row_add_pair.1.kept_ref), channel_id=1, source_target_pairs={{0,2},{1,3},{2,0},{3,1},{4,6},{5,7},{6,4},{7,5},{8,10},{9,11},{10,... | collective-permute-start | bytes 147464 | tf_op jit(solution)/shard_map/ppermute | solution.py:484
  43.0 0.6 pack_grad_hidden.1
  43.6 1.8 %collective-permute-done.15.got_ref = bf16[32,768]{1,0:T(8,128)(2,1)S(1)} collective-permute-done((bf16[32,768]{1,0:T(8,128)(2,1)S(1)}, bf16[32,768]{1,0:T(8,128)(2,1)S(1)}, u32[]{:S(2)}, u32[]{:S(2)}) %collective-permute-start.15) | collective-permute-done | bytes 49184 | tf_op jit(solution)/shard_map/ppermute | solution.py:484
  45.4 0.6 column_add_chips.1
  46.1 1.6 %collective-permute-start.19 = (bf16[32,1280]{1,0:T(8,128)(2,1)S(1)}, bf16[32,1280]{1,0:T(8,128)(2,1)S(1)}, u32[]{:S(2)}, u32[]{:S(2)}) collective-permute-start(bf16[32,1280]{1,0:T(8,128)(2,1)S(1)} %get-tuple-element.128), channel_id=1, source_target_pairs={{0,1},{1,0},{2,3},{3,2},{4,5},{5,4},{6,7},{7,6},{8,9},{9,8},{10,11... | collective-permute-start | bytes 245768 | tf_op jit(solution)/shard_map/ppermute | solution.py:484
  47.7 0.8 %collective-permute-start.22 = (bf16[128,512]{1,0:T(8,128)(2,1)S(1)}, bf16[128,512]{1,0:T(8,128)(2,1)S(1)}, u32[]{:S(2)}, u32[]{:S(2)}) collective-permute-start(bf16[128,512]{1,0:T(8,128)(2,1)S(1)} %get-tuple-element.134), channel_id=1, source_target_pairs={{0,8},{4,12},{8,0},{12,4},{16,24},{20,28},{24,16},{28,20},{1,9},{5... | collective-permute-start | bytes 393224 | tf_op jit(solution)/shard_map/ppermute | solution.py:484
  48.5 1.5 %collective-permute-start.23 = (bf16[128,512]{1,0:T(8,128)(2,1)S(1)}, bf16[128,512]{1,0:T(8,128)(2,1)S(1)}, u32[]{:S(2)}, u32[]{:S(2)}) collective-permute-start(bf16[128,512]{1,0:T(8,128)(2,1)S(1)} %get-tuple-element.135), channel_id=1, source_target_pairs={{0,16},{4,20},{8,24},{12,28},{16,0},{20,4},{24,8},{28,12},{1,17},{... | collective-permute-start | bytes 393224 | tf_op jit(solution)/shard_map/ppermute | solution.py:484
  50.0 1.2 %collective-permute-start.24 = (bf16[128,512]{1,0:T(8,128)(2,1)S(1)}, bf16[128,512]{1,0:T(8,128)(2,1)S(1)}, u32[]{:S(2)}, u32[]{:S(2)}) collective-permute-start(bf16[128,512]{1,0:T(8,128)(2,1)S(1)} %get-tuple-element.136), channel_id=1, source_target_pairs={{0,24},{4,28},{8,16},{12,20},{16,8},{20,12},{24,0},{28,4},{1,25},{... | collective-permute-start | bytes 393224 | tf_op jit(solution)/shard_map/ppermute | solution.py:484
  51.2 3.1 %collective-permute-start.20 = (bf16[32,1280]{1,0:T(8,128)(2,1)S(1)}, bf16[32,1280]{1,0:T(8,128)(2,1)S(1)}, u32[]{:S(2)}, u32[]{:S(2)}) collective-permute-start(bf16[32,1280]{1,0:T(8,128)(2,1)S(1)} %column_add_pair.1.kept_ref), channel_id=1, source_target_pairs={{0,2},{1,3},{2,0},{3,1},{4,6},{5,7},{6,4},{7,5},{8,10},{9,11},{10,... | collective-permute-start | bytes 245768 | tf_op jit(solution)/shard_map/ppermute | solution.py:484
  54.3 1.8 %collective-permute-start.21 = (bf16[32,768]{1,0:T(8,128)(2,1)S(1)}, bf16[32,768]{1,0:T(8,128)(2,1)S(1)}, u32[]{:S(2)}, u32[]{:S(2)}) collective-permute-start(bf16[32,768]{1,0:T(8,128)(2,1)S(1)} %row_add_pairs.1.row_held), channel_id=1, source_target_pairs={{0,1},{1,0},{2,3},{3,2},{4,5},{5,4},{6,7},{7,6},{8,9},{9,8},{10,11... | collective-permute-start | bytes 147464 | tf_op jit(solution)/shard_map/ppermute | solution.py:484
  56.1 1.9 %input_grad.1 = bf16[512,512]{1,0:T(8,128)(2,1)} custom-call(s32[3]{0:T(128)S(1)} %pad_add_fusion.place_ref, bf16[512,512]{1,0:T(8,128)(2,1)S(1)} %get-tuple-element.130.x_ref, bf16[512,512]{1,0:T(8,128)(2,1)S(1)} %get-tuple-element.131.cot_ref, f32[1,512]{1,0:T(1,128)S(1)} %bitcast.10, f32[512,512]{1,0:T(8,128)S(1)} %get-tuple-element.132.hidden_ref, ...), custom_call_target="tpu_custom_call" | custom-call | tf_op jit(solution)/shard_map/input_grad/pallas_call | solution.py:470
  58.0 0.4 collective-permute-done.21.row_got
  58.4 1.8 %collective-permute-start.25 = (bf16[32,1280]{1,0:T(8,128)(2,1)S(1)}, bf16[32,1280]{1,0:T(8,128)(2,1)S(1)}, u32[]{:S(2)}, u32[]{:S(2)}) collective-permute-start(bf16[32,1280]{1,0:T(8,128)(2,1)S(1)} %column_add_pairs.1.held_ref), channel_id=1, source_target_pairs={{0,1},{1,0},{2,3},{3,2},{4,5},{5,4},{6,7},{7,6},{8,9},{9,8},{10,11... | collective-permute-start | bytes 245768 | tf_op jit(solution)/shard_map/ppermute | solution.py:484
  60.2 2.7 %collective-permute-done.25.got_ref = bf16[32,1280]{1,0:T(8,128)(2,1)S(1)} collective-permute-done((bf16[32,1280]{1,0:T(8,128)(2,1)S(1)}, bf16[32,1280]{1,0:T(8,128)(2,1)S(1)}, u32[]{:S(2)}, u32[]{:S(2)}) %collective-permute-start.25) | collective-permute-done | bytes 81952 | tf_op jit(solution)/shard_map/ppermute | solution.py:484
  62.8 1.4 %result.1 = (f32[64,1536]{1,0:T(8,128)}, f32[64,512]{1,0:T(8,128)}, f32[1,64]{1,0:T(1,128)}) custom-call(s32[3]{0:T(128)S(1)} %pad_add_fusion.place_ref, bf16[32,768]{1,0:T(8,128)(2,1)S(1)} %row_add_pairs.1.row_held, bf16[32,768]{1,0:T(8,128)(2,1)S(1)} %collective-permute-done.21.row_got, bf16[32,1280]{1,0:T(8,128)(2,1)S(1)} %column_add_pairs.1.held_ref, ...), custom_call_target="tpu_custom_call" | custom-call | tf_op jit(solution)/shard_map/result/pallas_call | solution.py:470
  (22 shorter events, 0.1 us)
Async XLA Ops:
  2.6 12.1 %collective-permute-start.1 = (bf16[2,128,512]{2,1,0:T(8,128)(2,1)S(1)}, bf16[2,128,512]{2,1,0:T(8,128)(2,1)S(1)}, u32[]{:S(2)}, u32[]{:S(2)}) collective-permute-start(bf16[2,128,512]{2,1,0:T(8,128)(2,1)S(1)} %get-tuple-element.75), channel_id=1, source_target_pairs={{0,8},{4,12},{8,0},{12,4},{16,24},{20,28},{24,16},{28,20},{1,9},{5... | collective-permute-start | bytes 786440 | tf_op jit(solution)/shard_map/ppermute | solution.py:484
  5.6 13.4 %collective-permute-start.2 = (bf16[2,128,512]{2,1,0:T(8,128)(2,1)S(1)}, bf16[2,128,512]{2,1,0:T(8,128)(2,1)S(1)}, u32[]{:S(2)}, u32[]{:S(2)}) collective-permute-start(bf16[2,128,512]{2,1,0:T(8,128)(2,1)S(1)} %get-tuple-element.82), channel_id=1, source_target_pairs={{0,16},{4,20},{8,24},{12,28},{16,0},{20,4},{24,8},{28,12},{1,17},{... | collective-permute-start | bytes 786440 | tf_op jit(solution)/shard_map/ppermute | solution.py:484
  7.1 11.9 %collective-permute-start.3 = (bf16[2,128,512]{2,1,0:T(8,128)(2,1)S(1)}, bf16[2,128,512]{2,1,0:T(8,128)(2,1)S(1)}, u32[]{:S(2)}, u32[]{:S(2)}) collective-permute-start(bf16[2,128,512]{2,1,0:T(8,128)(2,1)S(1)} %get-tuple-element.83), channel_id=1, source_target_pairs={{0,24},{4,28},{8,16},{12,20},{16,8},{20,12},{24,0},{28,4},{1,25},{... | collective-permute-start | bytes 786440 | tf_op jit(solution)/shard_map/ppermute | solution.py:484
  14.7 1.5 %collective-permute-start.4 = (bf16[4,64,384]{2,1,0:T(8,128)(2,1)S(1)}, bf16[4,64,384]{2,1,0:T(8,128)(2,1)S(1)}, u32[]{:S(2)}, u32[]{:S(2)}) collective-permute-start(bf16[4,64,384]{2,1,0:T(8,128)(2,1)S(1)} %get-tuple-element.86), channel_id=1, source_target_pairs={{0,4},{4,0},{8,12},{12,8},{16,20},{20,16},{24,28},{28,24},{1,5},{5... | collective-permute-start | bytes 589832 | tf_op jit(solution)/shard_map/ppermute | solution.py:484
  14.8 1.7 %collective-permute-start.5 = (bf16[4,64,384]{2,1,0:T(8,128)(2,1)S(1)}, bf16[4,64,384]{2,1,0:T(8,128)(2,1)S(1)}, u32[]{:S(2)}, u32[]{:S(2)}) collective-permute-start(bf16[4,64,384]{2,1,0:T(8,128)(2,1)S(1)} %get-tuple-element.87), channel_id=1, source_target_pairs={{0,4},{4,0},{8,12},{12,8},{16,20},{20,16},{24,28},{28,24},{1,5},{5... | collective-permute-start | bytes 589832 | tf_op jit(solution)/shard_map/ppermute | solution.py:484
  19.0 4.0 %collective-permute-start.6 = (bf16[2,128,512]{2,1,0:T(8,128)(2,1)S(1)}, bf16[2,128,512]{2,1,0:T(8,128)(2,1)S(1)}, u32[]{:S(2)}, u32[]{:S(2)}) collective-permute-start(bf16[2,128,512]{2,1,0:T(8,128)(2,1)S(1)} %collective-permute-done.1.near_1), channel_id=1, source_target_pairs={{0,4},{4,0},{8,12},{12,8},{16,20},{20,16},{24,28},{28,24},{1,5},{5... | collective-permute-start | bytes 786440 | tf_op jit(solution)/shard_map/ppermute | solution.py:484
  19.0 5.2 %collective-permute-start.7 = (bf16[2,128,512]{2,1,0:T(8,128)(2,1)S(1)}, bf16[2,128,512]{2,1,0:T(8,128)(2,1)S(1)}, u32[]{:S(2)}, u32[]{:S(2)}) collective-permute-start(bf16[2,128,512]{2,1,0:T(8,128)(2,1)S(1)} %collective-permute-done.2.near_2), channel_id=1, source_target_pairs={{0,4},{4,0},{8,12},{12,8},{16,20},{20,16},{24,28},{28,24},{1,5},{5... | collective-permute-start | bytes 786440 | tf_op jit(solution)/shard_map/ppermute | solution.py:484
  19.5 4.7 %collective-permute-start.8 = (bf16[2,128,512]{2,1,0:T(8,128)(2,1)S(1)}, bf16[2,128,512]{2,1,0:T(8,128)(2,1)S(1)}, u32[]{:S(2)}, u32[]{:S(2)}) collective-permute-start(bf16[2,128,512]{2,1,0:T(8,128)(2,1)S(1)} %collective-permute-done.3.near_3), channel_id=1, source_target_pairs={{0,4},{4,0},{8,12},{12,8},{16,20},{20,16},{24,28},{28,24},{1,5},{5... | collective-permute-start | bytes 786440 | tf_op jit(solution)/shard_map/ppermute | solution.py:484
  19.5 2.0 %collective-permute-start = (bf16[2,64,512]{2,1,0:T(8,128)(2,1)S(1)}, bf16[2,64,512]{2,1,0:T(8,128)(2,1)S(1)}, u32[]{:S(2)}, u32[]{:S(2)}) collective-permute-start(bf16[2,64,512]{2,1,0:T(8,128)(2,1)S(1)} %get-tuple-element.74), channel_id=1, source_target_pairs={{0,4},{4,0},{8,12},{12,8},{16,20},{20,16},{24,28},{28,24},{1,5},{5... | collective-permute-start | bytes 393224 | tf_op jit(solution)/shard_map/ppermute | solution.py:484
  20.0 9.5 %collective-permute-start.9 = (bf16[64,768]{1,0:T(8,128)(2,1)S(1)}, bf16[64,768]{1,0:T(8,128)(2,1)S(1)}, u32[]{:S(2)}, u32[]{:S(2)}) collective-permute-start(bf16[64,768]{1,0:T(8,128)(2,1)S(1)} %get-tuple-element.96), channel_id=1, source_target_pairs={{0,8},{4,12},{8,0},{12,4},{16,24},{20,28},{24,16},{28,20},{1,9},{5... | collective-permute-start | bytes 294920 | tf_op jit(solution)/shard_map/ppermute | solution.py:484
  21.5 8.1 %collective-permute-start.10 = (bf16[64,768]{1,0:T(8,128)(2,1)S(1)}, bf16[64,768]{1,0:T(8,128)(2,1)S(1)}, u32[]{:S(2)}, u32[]{:S(2)}) collective-permute-start(bf16[64,768]{1,0:T(8,128)(2,1)S(1)} %get-tuple-element.97), channel_id=1, source_target_pairs={{0,16},{4,20},{8,24},{12,28},{16,0},{20,4},{24,8},{28,12},{1,17},{... | collective-permute-start | bytes 294920 | tf_op jit(solution)/shard_map/ppermute | solution.py:484
  23.0 6.6 %collective-permute-start.11 = (bf16[64,768]{1,0:T(8,128)(2,1)S(1)}, bf16[64,768]{1,0:T(8,128)(2,1)S(1)}, u32[]{:S(2)}, u32[]{:S(2)}) collective-permute-start(bf16[64,768]{1,0:T(8,128)(2,1)S(1)} %get-tuple-element.98), channel_id=1, source_target_pairs={{0,24},{4,28},{8,16},{12,20},{16,8},{20,12},{24,0},{28,4},{1,25},{... | collective-permute-start | bytes 294920 | tf_op jit(solution)/shard_map/ppermute | solution.py:484
  29.6 2.4 %collective-permute-start.13 = (bf16[4,64,1280]{2,1,0:T(8,128)(2,1)S(1)}, bf16[4,64,1280]{2,1,0:T(8,128)(2,1)S(1)}, u32[]{:S(2)}, u32[]{:S(2)}) collective-permute-start(bf16[4,64,1280]{2,1,0:T(8,128)(2,1)S(1)} %get-tuple-element.113), channel_id=1, source_target_pairs={{0,4},{4,0},{8,12},{12,8},{16,20},{20,16},{24,28},{28,24},{1,5},{5... | collective-permute-start | bytes 1966088 | tf_op jit(solution)/shard_map/ppermute | solution.py:484
  30.8 12.2 %collective-permute-start.12 = (bf16[4,64,512]{2,1,0:T(8,128)(2,1)S(1)}, bf16[4,64,512]{2,1,0:T(8,128)(2,1)S(1)}, u32[]{:S(2)}, u32[]{:S(2)}) collective-permute-start(bf16[4,64,512]{2,1,0:T(8,128)(2,1)S(1)} %get-tuple-element.107), channel_id=1, source_target_pairs={{0,4},{4,0},{8,12},{12,8},{16,20},{20,16},{24,28},{28,24},{1,5},{5... | collective-permute-start | bytes 786440 | tf_op jit(solution)/shard_map/ppermute | solution.py:484
  31.9 24.2 %copy-start = (f32[512]{0:T(512)S(1)}, f32[512]{0:T(512)}, u32[]{:S(2)}) copy-start(f32[512]{0:T(512)} %param.6) | copy-start | bytes 6148
  32.7 12.7 %collective-permute-start.16 = (bf16[64,1280]{1,0:T(8,128)(2,1)S(1)}, bf16[64,1280]{1,0:T(8,128)(2,1)S(1)}, u32[]{:S(2)}, u32[]{:S(2)}) collective-permute-start(bf16[64,1280]{1,0:T(8,128)(2,1)S(1)} %get-tuple-element.123), channel_id=1, source_target_pairs={{0,8},{4,12},{8,0},{12,4},{16,24},{20,28},{24,16},{28,20},{1,9},{5... | collective-permute-start | bytes 491528 | tf_op jit(solution)/shard_map/ppermute | solution.py:484
  33.5 11.9 %collective-permute-start.17 = (bf16[64,1280]{1,0:T(8,128)(2,1)S(1)}, bf16[64,1280]{1,0:T(8,128)(2,1)S(1)}, u32[]{:S(2)}, u32[]{:S(2)}) collective-permute-start(bf16[64,1280]{1,0:T(8,128)(2,1)S(1)} %get-tuple-element.124), channel_id=1, source_target_pairs={{0,16},{4,20},{8,24},{12,28},{16,0},{20,4},{24,8},{28,12},{1,17},{... | collective-permute-start | bytes 491528 | tf_op jit(solution)/shard_map/ppermute | solution.py:484
  35.0 10.4 %collective-permute-start.18 = (bf16[64,1280]{1,0:T(8,128)(2,1)S(1)}, bf16[64,1280]{1,0:T(8,128)(2,1)S(1)}, u32[]{:S(2)}, u32[]{:S(2)}) collective-permute-start(bf16[64,1280]{1,0:T(8,128)(2,1)S(1)} %get-tuple-element.125), channel_id=1, source_target_pairs={{0,24},{4,28},{8,16},{12,20},{16,8},{20,12},{24,0},{28,4},{1,25},{... | collective-permute-start | bytes 491528 | tf_op jit(solution)/shard_map/ppermute | solution.py:484
  36.2 4.1 %collective-permute-start.14 = (bf16[32,768]{1,0:T(8,128)(2,1)S(1)}, bf16[32,768]{1,0:T(8,128)(2,1)S(1)}, u32[]{:S(2)}, u32[]{:S(2)}) collective-permute-start(bf16[32,768]{1,0:T(8,128)(2,1)S(1)} %get-tuple-element.116), channel_id=1, source_target_pairs={{0,1},{1,0},{2,3},{3,2},{4,5},{5,4},{6,7},{7,6},{8,9},{9,8},{10,11... | collective-permute-start | bytes 147464 | tf_op jit(solution)/shard_map/ppermute | solution.py:484
  40.3 5.1 %collective-permute-start.15 = (bf16[32,768]{1,0:T(8,128)(2,1)S(1)}, bf16[32,768]{1,0:T(8,128)(2,1)S(1)}, u32[]{:S(2)}, u32[]{:S(2)}) collective-permute-start(bf16[32,768]{1,0:T(8,128)(2,1)S(1)} %row_add_pair.1.kept_ref), channel_id=1, source_target_pairs={{0,2},{1,3},{2,0},{3,1},{4,6},{5,7},{6,4},{7,5},{8,10},{9,11},{10,... | collective-permute-start | bytes 147464 | tf_op jit(solution)/shard_map/ppermute | solution.py:484
  46.1 5.1 %collective-permute-start.19 = (bf16[32,1280]{1,0:T(8,128)(2,1)S(1)}, bf16[32,1280]{1,0:T(8,128)(2,1)S(1)}, u32[]{:S(2)}, u32[]{:S(2)}) collective-permute-start(bf16[32,1280]{1,0:T(8,128)(2,1)S(1)} %get-tuple-element.128), channel_id=1, source_target_pairs={{0,1},{1,0},{2,3},{3,2},{4,5},{5,4},{6,7},{7,6},{8,9},{9,8},{10,11... | collective-permute-start | bytes 245768 | tf_op jit(solution)/shard_map/ppermute | solution.py:484
  47.7 8.4 %collective-permute-start.22 = (bf16[128,512]{1,0:T(8,128)(2,1)S(1)}, bf16[128,512]{1,0:T(8,128)(2,1)S(1)}, u32[]{:S(2)}, u32[]{:S(2)}) collective-permute-start(bf16[128,512]{1,0:T(8,128)(2,1)S(1)} %get-tuple-element.134), channel_id=1, source_target_pairs={{0,8},{4,12},{8,0},{12,4},{16,24},{20,28},{24,16},{28,20},{1,9},{5... | collective-permute-start | bytes 393224 | tf_op jit(solution)/shard_map/ppermute | solution.py:484
  48.5 7.6 %collective-permute-start.23 = (bf16[128,512]{1,0:T(8,128)(2,1)S(1)}, bf16[128,512]{1,0:T(8,128)(2,1)S(1)}, u32[]{:S(2)}, u32[]{:S(2)}) collective-permute-start(bf16[128,512]{1,0:T(8,128)(2,1)S(1)} %get-tuple-element.135), channel_id=1, source_target_pairs={{0,16},{4,20},{8,24},{12,28},{16,0},{20,4},{24,8},{28,12},{1,17},{... | collective-permute-start | bytes 393224 | tf_op jit(solution)/shard_map/ppermute | solution.py:484
  50.0 6.1 %collective-permute-start.24 = (bf16[128,512]{1,0:T(8,128)(2,1)S(1)}, bf16[128,512]{1,0:T(8,128)(2,1)S(1)}, u32[]{:S(2)}, u32[]{:S(2)}) collective-permute-start(bf16[128,512]{1,0:T(8,128)(2,1)S(1)} %get-tuple-element.136), channel_id=1, source_target_pairs={{0,24},{4,28},{8,16},{12,20},{16,8},{20,12},{24,0},{28,4},{1,25},{... | collective-permute-start | bytes 393224 | tf_op jit(solution)/shard_map/ppermute | solution.py:484
  51.2 6.8 %collective-permute-start.20 = (bf16[32,1280]{1,0:T(8,128)(2,1)S(1)}, bf16[32,1280]{1,0:T(8,128)(2,1)S(1)}, u32[]{:S(2)}, u32[]{:S(2)}) collective-permute-start(bf16[32,1280]{1,0:T(8,128)(2,1)S(1)} %column_add_pair.1.kept_ref), channel_id=1, source_target_pairs={{0,2},{1,3},{2,0},{3,1},{4,6},{5,7},{6,4},{7,5},{8,10},{9,11},{10,... | collective-permute-start | bytes 245768 | tf_op jit(solution)/shard_map/ppermute | solution.py:484
  54.3 4.1 %collective-permute-start.21 = (bf16[32,768]{1,0:T(8,128)(2,1)S(1)}, bf16[32,768]{1,0:T(8,128)(2,1)S(1)}, u32[]{:S(2)}, u32[]{:S(2)}) collective-permute-start(bf16[32,768]{1,0:T(8,128)(2,1)S(1)} %row_add_pairs.1.row_held), channel_id=1, source_target_pairs={{0,1},{1,0},{2,3},{3,2},{4,5},{5,4},{6,7},{7,6},{8,9},{9,8},{10,11... | collective-permute-start | bytes 147464 | tf_op jit(solution)/shard_map/ppermute | solution.py:484
  58.4 4.4 %collective-permute-start.25 = (bf16[32,1280]{1,0:T(8,128)(2,1)S(1)}, bf16[32,1280]{1,0:T(8,128)(2,1)S(1)}, u32[]{:S(2)}, u32[]{:S(2)}) collective-permute-start(bf16[32,1280]{1,0:T(8,128)(2,1)S(1)} %column_add_pairs.1.held_ref), channel_id=1, source_target_pairs={{0,1},{1,0},{2,3},{3,2},{4,5},{5,4},{6,7},{7,6},{8,9},{9,8},{10,11... | collective-permute-start | bytes 245768 | tf_op jit(solution)/shard_map/ppermute | solution.py:484

commit v8 on v7

--- a/solution.py
+++ b/solution.py
@@ -21,6 +21,7 @@
 VMEM = pl.BlockSpec(memory_space=pltpu.VMEM)
 SMEM = pl.BlockSpec(memory_space=pltpu.SMEM)
 HBM = pl.BlockSpec(memory_space=pltpu.HBM)
+CHIP_STEPS = (3, 2, 1)
 PINNED = pl.BlockSpec(memory_space=pltpu.VMEM)
 shaped = jax.ShapeDtypeStruct
 
@@ -139,8 +140,8 @@
 
 def row_part(
     x_any, cot_any, gain_any, wqkv_any, wout_any,
-    out_ref, hidden_ref, x_ref, cot_ref,
-    gain_ref, w_ref, wo_ref, dk_ref, dv_ref, grads_ref, sems,
+    out_ref, base_ref, normed_ref, inverse_ref,
+    x_ref, cot_ref, gain_ref, w_ref, wo_ref, dk_ref, dv_ref, grads_ref, sems,
 ):
     first = started(
         pltpu.make_async_copy(x_any, x_ref, sems.at[4]),
@@ -154,8 +155,8 @@
     dv_ref[...] = jnp.zeros_like(dv_ref)
     finished(*first)
     tokens = x_ref.shape[0]
-    _, normed = rms_parts(x_ref[...].astype(F32))
-    hidden = (normed * gain_ref[...]).astype(BF16)
+    inverse_ref[...], normed_ref[...] = rms_parts(x_ref[...].astype(F32))
+    hidden = (normed_ref[...] * gain_ref[...]).astype(BF16)
     hidden_t = transposed(hidden)
     finished(*later)
     cot = cot_ref[...]
@@ -186,7 +187,10 @@
     grads_ref[:, 2 * HW :] = dv_ref[...].astype(BF16)
     term_qkv = dot_nn(hidden_t, grads_ref[...]).astype(BF16)
     out_ref[...] = dot_nn(jnp.concatenate(att_blocks, 1), cot).astype(BF16)
-    hidden_ref[...] = dot_nt(grads_ref[...], w_ref[...])
+    grad_normed = dot_nt(grads_ref[...], w_ref[...]) * gain_ref[...]
+    base_ref[...] = input_grad(
+        cot_ref[...].astype(F32), normed_ref[...], inverse_ref[...], grad_normed
+    )
     return term_qkv
 
 
@@ -298,8 +302,8 @@
             (source.at[pl.ds(at, share), :], me),
             (own_any.at[which], other),
         ]
-        for i, (near, far) in enumerate(((near_1, far_1), (near_2, far_2), (near_3, far_3))):
-            there = 2 * (chip ^ (i + 1))
+        for step, near, far in zip(CHIP_STEPS, (near_1, near_2, near_3), (far_1, far_2, far_3)):
+            there = 2 * (chip ^ step)
             group.append((near.at[which, pl.ds(half, share), :], there + core))
             group.append((far.at[which, pl.ds(half, share), :], there + 1 - core))
         base = 5 + which * len(group)
@@ -348,36 +352,36 @@
     share = keep_ref.shape[1]
     kept_at = pl.multiple_of(core * share, share)
     got_at = pl.multiple_of((1 - core) * share, share)
-    for i, target in enumerate((own_ref, off_1, off_2, off_3)):
-        target[pl.ds(kept_at, share), :] = keep_ref[chip ^ i]
-        target[pl.ds(got_at, share), :] = got_ref[chip ^ i]
-
-
-def input_kernel(x_ref, cot_ref, gain_ref, hidden_ref, back_ref, grad_ref):
-    inverse_rms, normed = rms_parts(x_ref[...].astype(F32))
-    grad_hidden = hidden_ref[...] + back_ref[...].astype(F32)
-    grad_ref[...] = input_grad(normed, inverse_rms, grad_hidden, gain_ref[...], cot_ref[...])
-
-
-def input_grad(normed, inverse_rms, grad_hidden, gain, cot):
-    grad_normed = grad_hidden * gain
+    for step, target in zip((0, *CHIP_STEPS), (own_ref, off_1, off_2, off_3)):
+        target[pl.ds(kept_at, share), :] = keep_ref[chip ^ step]
+        target[pl.ds(got_at, share), :] = got_ref[chip ^ step]
+
+
+def input_kernel(base_ref, normed_ref, inverse_ref, gain_ref, back_ref, grad_ref):
+    grad_ref[...] = input_grad(
+        base_ref[...], normed_ref[...], inverse_ref[...], back_ref[...].astype(F32) * gain_ref[...]
+    ).astype(BF16)
+
+
+def input_grad(base, normed, inverse_rms, grad_normed):
     projected = jnp.mean(grad_normed * normed, -1, keepdims=True)
-    grad = inverse_rms * (grad_normed - normed * projected)
-    return (cot.astype(F32) + grad).astype(BF16)
+    return base + inverse_rms * (grad_normed - normed * projected)
 
 
 def input_chip_kernel(
-    place_ref, x_ref, cot_ref, gain_ref, hidden_ref, own_ref, got_1, got_2, got_3, grad_ref
+    place_ref, base_ref, normed_ref, inverse_ref, gain_ref, own_ref, got_1, got_2, got_3,
+    grad_any, grad_ref, sems,
 ):
     chip = place_ref[0]
     count = own_ref.shape[0]
-    for i, back_ref in enumerate((own_ref, got_1, got_2, got_3)):
-        at = pl.ds(pl.multiple_of((chip ^ i) * count, count), count)
-        inverse_rms, normed = rms_parts(x_ref[at, :].astype(F32))
-        grad_hidden = hidden_ref[at, :] + back_ref[...].astype(F32)
-        grad_ref[at, :] = input_grad(
-            normed, inverse_rms, grad_hidden, gain_ref[...], cot_ref[at, :]
-        )
+    copies = []
+    for i, (step, back_ref) in enumerate(zip((0, *CHIP_STEPS), (own_ref, got_1, got_2, got_3))):
+        at = pl.ds(pl.multiple_of((chip ^ step) * count, count), count)
+        grad_normed = back_ref[...].astype(F32) * gain_ref[...]
+        grad = input_grad(base_ref[at, :], normed_ref[at, :], inverse_ref[at, :], grad_normed)
+        grad_ref[i] = grad.astype(BF16)
+        copies += started(pltpu.make_async_copy(grad_ref.at[i], grad_any.at[at, :], sems.at[i]))
+    finished(*copies)
 
 
 def pack_kernel(place_ref, x_any, cot_any, own_ref, off_1, off_2, off_3, sems):
@@ -391,8 +395,8 @@
                 source.at[pl.ds(at, share), :], own_ref.at[which], sems.at[which]
             )
         )
-        for i, target in enumerate((off_1, off_2, off_3)):
-            there = pl.multiple_of((chip ^ (i + 1)) * 2 * share, 2 * share)
+        for i, (step, target) in enumerate(zip(CHIP_STEPS, (off_1, off_2, off_3))):
+            there = pl.multiple_of((chip ^ step) * 2 * share, 2 * share)
             copies.append(
                 pltpu.make_async_copy(
                     source.at[pl.ds(there, 2 * share), :],
@@ -403,52 +407,71 @@
     finished(*started(*copies))
 
 
-def chip_sum_kernel(place_ref, *refs):
+def chip_sum_kernel(
+    place_ref, keep_ref, got_ref, row_kept, row_got, own_ref, off_1, off_2, off_3
+):
     chip = place_ref[0]
-    pieces, targets = refs[:-4], refs[-4:]
-    count = len(pieces) // 2
-    for i, target in enumerate(targets):
-        at = 0
-        for kept_ref, got_ref in zip(pieces[:count], pieces[count:]):
-            total = kept_ref[chip ^ i].astype(F32) + got_ref[chip ^ i].astype(F32)
-            target[:, at : at + total.shape[1]] = total.astype(target.dtype)
-            at += total.shape[1]
-
-
-def layer_sum_kernel(place_ref, own_ref, got_1, got_2, got_3, send_ref, keep_ref):
+    cut, rows, fold = keep_ref.shape[2], row_kept.shape[1], row_kept.shape[2] // 2
+    for step, target in zip((0, *CHIP_STEPS), (own_ref, off_1, off_2, off_3)):
+        there = chip ^ step
+        total = keep_ref[there].astype(F32) + got_ref[there].astype(F32)
+        target[:, :cut] = total.astype(target.dtype)
+        total = (row_kept[there] + row_got[there].astype(F32)).astype(target.dtype)
+        target[:rows, cut:] = total[:, :fold]
+        target[rows:, cut:] = total[:, fold:]
+
+
+def row_cores_kernel(place_ref, keep_1, keep_2, got_1, got_2, send_ref, kept_ref):
+    upper = place_ref[2] == 1
+    half, cut = kept_ref.shape[1], keep_1.shape[2]
+    for i, (keep_ref, got_ref) in enumerate(((keep_1, got_1), (keep_2, got_2))):
+        lanes = slice(i * cut, (i + 1) * cut)
+        total = keep_ref[...].astype(F32) + got_ref[...].astype(F32)
+        low, high = total[:, :half], total[:, half:]
+        send_ref[:, :, lanes] = jnp.where(upper, low, high).astype(BF16)
+        kept_ref[:, :, lanes] = jnp.where(upper, high, low)
+
+
+def layer_sum_kernel(place_ref, own_ref, got_1, got_2, got_3, send_ref, keep_ref, row_ref):
     upper = place_ref[2] == 1
     total = own_ref[...] + (
         (got_1[...].astype(F32) + got_2[...].astype(F32)) + got_3[...].astype(F32)
     )
-    half = total.shape[0] // 2
+    half, cut, fold = keep_ref.shape[0], keep_ref.shape[1], row_ref.shape[1] // 2
     low, high = total[:half], total[half:]
-    send_ref[...] = jnp.where(upper, low, high).astype(BF16)
-    keep_ref[...] = jnp.where(upper, high, low)
+    send_ref[...] = jnp.where(upper, low[:, :cut], high[:, :cut]).astype(BF16)
+    keep_ref[...] = jnp.where(upper, high[:, :cut], low[:, :cut])
+    row_ref[:, :fold] = low[:, cut:].astype(BF16)
+    row_ref[:, fold:] = high[:, cut:].astype(BF16)
+
+
+def join_kernel(kept_ref, got_ref, row_ref, out_ref):
+    cut = kept_ref.shape[1]
+    out_ref[:, :cut] = (kept_ref[...] + got_ref[...].astype(F32)).astype(BF16)
+    out_ref[:, cut:] = row_ref[...]
 
 
 def add_kernel(kept_ref, got_ref, out_ref):
     out_ref[...] = (kept_ref[...].astype(F32) + got_ref[...].astype(F32)).astype(BF16)
 
 
-def result_kernel(
-    place_ref, row_held, row_got, held_ref, got_ref, w_ref, gain_ref, qkv_ref, out_ref, grad_ref
-):
+def result_kernel(place_ref, held_ref, got_ref, w_ref, gain_ref, qkv_ref, out_ref, grad_ref):
     rows = qkv_ref.shape[0]
     at = pl.multiple_of((place_ref[0] * 2 + place_ref[1]) * rows, rows)
     upper = place_ref[2] == 1
     half = rows // 2
     width = out_ref.shape[1]
 
-    def ordered(held_ref, got_ref, lanes):
+    def ordered(lanes):
         held, got = held_ref[:, lanes].astype(F32), got_ref[:, lanes].astype(F32)
         return (jnp.where(upper, got, held), jnp.where(upper, held, got))
 
+    row_at = 3 * HW + width
     for i in range(3):
-        lanes = slice(i * HW, (i + 1) * HW)
-        for at_to, pair in ((i * width, (row_held, row_got)), (i * width + HW, (held_ref, got_ref))):
+        for at_from, at_to in ((row_at + i * HW, i * width), (i * HW, i * width + HW)):
             to = slice(at_to, at_to + HW)
-            qkv_ref[:half, to], qkv_ref[half:, to] = ordered(*pair, lanes)
-    out_ref[:half], out_ref[half:] = ordered(held_ref, got_ref, slice(3 * HW, 3 * HW + width))
+            qkv_ref[:half, to], qkv_ref[half:, to] = ordered(slice(at_from, at_from + HW))
+    out_ref[:half], out_ref[half:] = ordered(slice(3 * HW, row_at))
     total = jnp.sum(qkv_ref[...] * w_ref[...].astype(F32), -1, keepdims=True)
     shape = (rows, gain_ref.shape[1])
     row = lax.broadcasted_iota(jnp.int32, shape, 0)
@@ -484,33 +507,8 @@
     return lax.ppermute(array, axis, [(i, i ^ bits) for i in range(count)])
 
 
-def add_cores(place, keep, got, name):
-    rows, wide = keep[0].shape[1], sum(one.shape[2] for one in keep)
-    return call(
-        chip_sum_kernel,
-        name + "_add_cores",
-        [(SMEM, place), *[(VMEM, one) for one in (*keep, *got)]],
-        [((rows, wide), F32)] + [((rows, wide), BF16)] * 3,
-        out_specs=[PINNED, VMEM, VMEM, VMEM],
-    )
-
-
-def cross_chips(off_1, off_2, off_3):
-    got_3 = swap(off_3, "seq", 6)
-    got_1 = swap(off_1, "seq", 2)
-    got_2 = swap(off_2, "seq", 4)
-    return got_1, got_2, got_3
-
-
-def add_chips(place, owned, got, name):
-    rows, wide = owned.shape
-    return call(
-        layer_sum_kernel,
-        name + "_add_chips",
-        [(SMEM, place), (VMEM, owned), *[(VMEM, one) for one in got]],
-        [((rows // 2, wide), BF16), ((rows // 2, wide), F32)],
-        out_specs=[VMEM, PINNED],
-    )
+def cross_chips(*offs):
+    return [swap(off, "seq", 2 * step) for off, step in zip(offs, CHIP_STEPS)]
 
 
 def add_two(kept, got, name):
@@ -531,7 +529,8 @@
     chips = 4
     layered = n == 2 * chips and m == 4 and row_share == share
     here = lax.axis_index("seq")
-    place = jnp.stack([here // 2, here % 2, lax.axis_index("dp") % 2]).astype(jnp.int32)
+    layer = lax.axis_index("dp")
+    place = jnp.stack([here // 2, here % 2, layer % 2, layer // 2]).astype(jnp.int32)
     weight_scratch = [
         pltpu.VMEM((1, width), F32),
         pltpu.VMEM((width, 3 * HW), BF16),
@@ -551,7 +550,7 @@
         )
         near_1, near_2, near_3 = cross_chips(*packed[1:])
         own = swap(packed[0], "seq", 1)
-        placed, _ = lax.optimization_barrier((place, packed[0]))
+        placed, _ = lax.optimization_barrier((place, own))
     else:
         outgoing = jnp.stack([x.reshape(n, share, width), cot.reshape(n, share, width)], 1)
         moved = lax.all_to_all(outgoing, "seq", split_axis=0, concat_axis=0, tiled=True)
@@ -561,15 +560,17 @@
     term_outs = [split_out] * 4 if layered else [((width, row_width), BF16)]
     if layered:
         term_outs.append(((row_share, 3 * width), BF16))
-    *row_terms, row_out, row_hidden, x_near, cot_near = call(
+    *row_terms, row_out, base, normed, inverse_rms = call(
         row_chip_kernel if layered else row_kernel,
         "row_heads",
         [(SMEM, placed)] * layered + [(HBM, x), (HBM, cot), *weights],
         [
             *term_outs, ((HW, width), BF16), ((columns, width), F32),
-            ((columns, width), BF16), ((columns, width), BF16),
+            ((columns, width), F32), ((columns, 1), F32),
         ],
         [
+            pltpu.VMEM((columns, width), BF16),
+            pltpu.VMEM((columns, width), BF16),
             *weight_scratch,
             pltpu.VMEM((columns, HW), F32),
             pltpu.VMEM((columns, HW), F32),
@@ -582,14 +583,20 @@
     moved_scratch = pltpu.VMEM((n, 2, share, width), BF16)
     if layered:
         *row_terms, weight_rows = row_terms
-        near_1, *row_terms = lax.optimization_barrier((near_1, *row_terms))
         row_sent = [swap(one, "seq", 1) for one in row_terms[:2]]
-        row_owned, *row_off = add_cores(place, row_terms[2:], row_sent, "row")
-        near_1, near_2, near_3, row_owned = lax.optimization_barrier(
-            (near_1, near_2, near_3, row_owned)
+        half_block = (chips, row_share // 2, row_width)
+        row_next, row_kept = call(
+            row_cores_kernel,
+            "row_add_cores",
+            [(SMEM, place), *[(VMEM, one) for one in (*row_terms[2:], *row_sent)]],
+            [(half_block, BF16), (half_block, F32)],
+            out_specs=[VMEM, PINNED],
+        )
+        near_1, near_2, near_3, row_kept = lax.optimization_barrier(
+            (near_1, near_2, near_3, row_kept)
         )
         far_3, far_1, far_2 = swap(near_3, "seq", 1), swap(near_1, "seq", 1), swap(near_2, "seq", 1)
-        row_got = cross_chips(*row_off)
+        row_got = swap(row_next, "dp", 1)
         send, keep, *col_grads = call(
             column_chip_kernel,
             "column_heads",
@@ -604,48 +611,65 @@
             [VMEM, VMEM, PINNED, PINNED],
         )
         send, row_got = lax.optimization_barrier((send, row_got))
-        row_next, row_kept = add_chips(place, row_owned, row_got, "row")
         back_send, back_keep = call(
             back_chip_kernel,
             "column_grad_hidden",
             [(SMEM, place), *[(VMEM, one) for one in col_grads]],
             [((chips, share, width), BF16)] * 2,
         )
-        keep, row_kept, back_keep = lax.optimization_barrier((keep, row_kept, back_keep))
-        owned, *off = add_cores(place, [keep], [swap(send, "seq", 1)], "column")
+        keep, back_keep = lax.optimization_barrier((keep, back_keep))
+        joint_width = col_width + row_width // 2
+        owned, *off = call(
+            chip_sum_kernel,
+            "add_cores",
+            [
+                (SMEM, place), (VMEM, keep), (VMEM, swap(send, "seq", 1)),
+                (VMEM, row_kept), (VMEM, row_got),
+            ],
+            [((row_share, joint_width), F32)] + [((row_share, joint_width), BF16)] * 3,
+            out_specs=[PINNED, VMEM, VMEM, VMEM],
+        )
         got = cross_chips(*off)
-        row_pair = add_two(row_kept, swap(row_next, "dp", 1), "row_add_pair")
-        row_pair, _ = lax.optimization_barrier((row_pair, owned))
-        row_held = add_two(row_pair, swap(row_pair, "dp", 2), "row_add_pairs")
         back = call(
             back_pack_kernel,
             "pack_grad_hidden",
             [(SMEM, place), (VMEM, back_keep), (VMEM, swap(back_send, "seq", 1))],
             [((2 * share, width), BF16)] * 4,
         )
-        *back, owned, row_held = lax.optimization_barrier((*back, owned, row_held))
-        to_next, kept = add_chips(place, owned, got, "column")
-        *back, kept = lax.optimization_barrier((*back, kept))
-        row_other = swap(row_held, "dp", 1)
-        pair_sum = add_two(kept, swap(to_next, "dp", 1), "column_add_pair")
-        held = add_two(pair_sum, swap(pair_sum, "dp", 2), "column_add_pairs")
+        *back, owned = lax.optimization_barrier((*back, owned))
+        half_rows = row_share // 2
+        to_next, kept, row_sum = call(
+            layer_sum_kernel,
+            "add_chips",
+            [(SMEM, place), (VMEM, owned), *[(VMEM, one) for one in got]],
+            [((half_rows, col_width), BF16), ((half_rows, col_width), F32), ((half_rows, row_width), BF16)],
+            out_specs=[VMEM, PINNED, VMEM],
+        )
+        (pair_sum,) = call(
+            join_kernel,
+            "add_pair",
+            [(VMEM, kept), (VMEM, swap(to_next, "dp", 1)), (VMEM, row_sum)],
+            [((half_rows, col_width + row_width), BF16)],
+        )
+        *back, pair_sum = lax.optimization_barrier((*back, pair_sum))
+        held = add_two(pair_sum, swap(pair_sum, "dp", 2), "add_pairs")
+        other = swap(held, "dp", 1)
         (grad,) = call(
             input_chip_kernel,
             "input_grad",
             [
-                (SMEM, place), (VMEM, x_near), (VMEM, cot_near), (VMEM, gain), (VMEM, row_hidden),
+                (SMEM, place), (VMEM, base), (VMEM, normed), (VMEM, inverse_rms), (VMEM, gain),
                 (VMEM, back[0]), *[(VMEM, one) for one in cross_chips(*back[1:])],
             ],
             [((columns, width), BF16)],
-        )
-        held, row_other, grad = lax.optimization_barrier((held, row_other, grad))
-        other = swap(held, "dp", 1)
+            [pltpu.VMEM((chips, 2 * share, width), BF16), pltpu.SemaphoreType.DMA((chips,))],
+            out_specs=[HBM],
+        )
         sum_qkv, sum_out, sum_gain = call(
             result_kernel,
             "result",
             [
-                (SMEM, place), (VMEM, row_held), (VMEM, row_other), (VMEM, held), (VMEM, other),
-                (VMEM, weight_rows), (VMEM, gain),
+                (SMEM, place), (VMEM, held), (VMEM, other), (VMEM, weight_rows), (VMEM, gain),
             ],
             [((row_share, 3 * width), F32), ((row_share, width), F32), ((1, row_share), F32)],
         )
@@ -670,7 +694,7 @@
             input_kernel,
             "input_grad",
             [
-                (VMEM, x_near), (VMEM, cot_near), (VMEM, gain), (VMEM, row_hidden),
+                (VMEM, base), (VMEM, normed), (VMEM, inverse_rms), (VMEM, gain),
                 (VMEM, returned.reshape(columns, width)),
             ],
             [((columns, width), BF16)],

time: 64.4 us -> 62.9 us (0.977)
  starting transfers between devices: 30.2 us -> 20 us
  waiting for transfers between devices: 10.6 us -> 19.9 us
    ppermute x26 -> x21, starting transfers between devices: 30.2 us -> 20 us  [swap(): return lax.ppermute(array, axis, [(i, i ^ bits) for i in range(count)])]
    ppermute x26 -> x21, waiting for transfers between devices: 10.6 us -> 19.9 us  [swap(): return lax.ppermute(array, axis, [(i, i ^ bits) for i in range(count)])]
    pallas_call x15 -> x12, Pallas kernels: 22.5 us -> 21.9 us  [call(): pl.pallas_call(kernel, out_shape=outs, in_specs=[spec for spec, _ in ins]...]
  transfers between devices with their start and end apart: 26 -> 21, of which waited for: 8 -> 15; matrix products, arithmetic and copies ran while one was open for 0% -> 0% of each run, Pallas kernels for 29% -> 29%
where the time goes in v8:
time: 62.9 us; the launch traced here: 62.7 us
  Pallas kernels  21.9 us (35%)
  starting transfers between devices  20 us (32%)
  waiting for transfers between devices  19.9 us (32%)
  between operations  0.78 us (1%)
    pallas_call x12, Pallas kernels, call(): pl.pallas_call(kernel, out_shape=outs, in_specs=[spec for spec, _ in ins]...  21.9 us
    ppermute x21, starting transfers between devices, swap(): return lax.ppermute(array, axis, [(i, i ^ bits) for i in range(count)])  20 us
    ppermute x21, waiting for transfers between devices, swap(): return lax.ppermute(array, axis, [(i, i ^ bits) for i in range(count)])  19.9 us
  transfers between devices with their start and end apart: 21, of which 15 were waited for; matrix products, arithmetic and copies ran while one was open for 0% of the time, Pallas kernels for 29%

profile of v8, /device:TPU:0, one launch (start us, length us, event | category | flops | bytes accessed | tf_op | source)
XLA Modules:
  0.0 62.7 jit_solution(13989201721988447057)
XLA Ops:
  0.7 0.1 pad_add_fusion.place_ref
  0.7 1.9 %pack_columns.1 = (bf16[2,64,512]{2,1,0:T(8,128)(2,1)S(1)}, bf16[2,128,512]{2,1,0:T(8,128)(2,1)S(1)}, bf16[2,128,512]{2,1,0:T(8,128)(2,1)S(1)}, bf16[2,128,512]{2,1,0:T(8,128)(2,1)S(1)}) custom-call(s32[4]{0:T(128)S(1)} %pad_add_fusion.place_ref, bf16[512,512]{1,0:T(8,128)(2,1)} %bitcast.13, bf16[512,512]{1,0:T(8,128)(2,1)} %bitcast.16), custom_call_target="tpu_custom_call" | custom-call | tf_op jit(solution)/shard_map/pack_columns/pallas_call | solution.py:493
  2.6 0.5 collective-permute-start
  3.1 3.5 %collective-permute-start.1 = (bf16[2,128,512]{2,1,0:T(8,128)(2,1)S(1)}, bf16[2,128,512]{2,1,0:T(8,128)(2,1)S(1)}, u32[]{:S(2)}, u32[]{:S(2)}) collective-permute-start(bf16[2,128,512]{2,1,0:T(8,128)(2,1)S(1)} %get-tuple-element.63), channel_id=1, source_target_pairs={{0,24},{4,28},{8,16},{12,20},{16,8},{20,12},{24,0},{28,4},{1,25},{... | collective-permute-start | bytes 786440 | tf_op jit(solution)/shard_map/ppermute | solution.py:507
  6.6 0.5 collective-permute-start.2
  7.2 0.1 collective-permute-start.3
  7.3 7.8 %row_heads.1 = (bf16[4,64,384]{2,1,0:T(8,128)(2,1)S(1)}, bf16[4,64,384]{2,1,0:T(8,128)(2,1)S(1)}, bf16[4,64,384]{2,1,0:T(8,128)(2,1)S(1)}, bf16[4,64,384]{2,1,0:...) custom-call(s32[4]{0:T(128)S(1)} %pad_add_fusion.place_ref, ...), custom_call_target="tpu_custom_call" | custom-call | tf_op jit(solution)/shard_map/row_heads/pallas_call | solution.py:493
  15.1 0.1 collective-permute-start.4
  15.2 0.5 collective-permute-start.5
  15.7 0.9 %collective-permute-done.4.got_1 = bf16[4,64,384]{2,1,0:T(8,128)(2,1)S(1)} collective-permute-done((bf16[4,64,384]{2,1,0:T(8,128)(2,1)S(1)}, bf16[4,64,384]{2,1,0:T(8,128)(2,1)S(1)}, u32[]{:S(2)}, u32[]{:S(2)}) %collective-permute-start.4) | collective-permute-done | bytes 196640 | tf_op jit(solution)/shard_map/ppermute | solution.py:507
  16.6 0.3 collective-permute-done.5.got_2
  16.9 0.7 %row_add_cores.1 = (bf16[4,32,768]{2,1,0:T(8,128)(2,1)S(1)}, f32[4,32,768]{2,1,0:T(8,128)S(1)}) custom-call(s32[4]{0:T(128)S(1)} %pad_add_fusion.place_ref, bf16[4,64,384]{2,1,0:T(8,128)(2,1)S(1)} %get-tuple-element.66.keep_1, bf16[4,64,384]{2,1,0:T(8,128)(2,1)S(1)} %get-tuple-element.67.keep_2, bf16[4,64,384]{2,1,0:T(8,128)(2,1)S(1)} %collective-permute-done.4.got_1, ...), custom_call_target="tpu_custom_call" | custom-call | tf_op jit(solution)/shard_map/row_add_cores/pallas_call | solution.py:493
  17.6 1.6 %collective-permute-done.2.near_2 = bf16[2,128,512]{2,1,0:T(8,128)(2,1)S(1)} collective-permute-done((bf16[2,128,512]{2,1,0:T(8,128)(2,1)S(1)}, bf16[2,128,512]{2,1,0:T(8,128)(2,1)S(1)}, u32[]{:S(2)}, u32[]{:S(2)}) %collective-permute-start.2) | collective-permute-done | bytes 262176 | tf_op jit(solution)/shard_map/ppermute | solution.py:507
  19.2 0.3 collective-permute-done.3.near_3
  19.5 0.5 collective-permute-start.7
  20.0 0.0 collective-permute-start.8
  20.0 1.6 %collective-permute-start.10 = (bf16[4,32,768]{2,1,0:T(8,128)(2,1)S(1)}, bf16[4,32,768]{2,1,0:T(8,128)(2,1)S(1)}, u32[]{:S(2)}, u32[]{:S(2)}) collective-permute-start(bf16[4,32,768]{2,1,0:T(8,128)(2,1)S(1)} %get-tuple-element.87), channel_id=1, source_target_pairs={{0,1},{1,0},{2,3},{3,2},{4,5},{5,4},{6,7},{7,6},{8,9},{9,8},{10,11... | collective-permute-start | bytes 589832 | tf_op jit(solution)/shard_map/ppermute | solution.py:507
  21.6 0.2 collective-permute-done.8.far_3
  21.8 5.4 %column_heads.1 = (bf16[4,64,1280]{2,1,0:T(8,128)(2,1)S(1)}, bf16[4,64,1280]{2,1,0:T(8,128)(2,1)S(1)}, bf16[512,768]{1,0:T(8,128)(2,1)S(1)}, bf16[512,768]{1,0:T(8,128)(2,1)S(1)}) custom-call(s32[4]{0:T(128)S(1)} %pad_add_fusion.place_ref, bf16[512,512]{1,0:T(8,128)(2,1)} %bitcast.15, bf16[512,512]{1,0:T(8,128)(2,1)} %bitcast.18, ...), custom_call_target="tpu_custom_call" | custom-call | tf_op jit(solution)/shard_map/column_heads/pallas_call | solution.py:493
  27.1 0.2 collective-permute-done.10.row_got
  27.3 0.0 collective-permute-start.11
  27.3 1.1 %column_grad_hidden.1 = (bf16[4,64,512]{2,1,0:T(8,128)(2,1)S(1)}, bf16[4,64,512]{2,1,0:T(8,128)(2,1)S(1)}) custom-call(s32[4]{0:T(128)S(1)} %pad_add_fusion.place_ref, bf16[512,768]{1,0:T(8,128)(2,1)S(1)} %get-tuple-element.76.grads_ref, bf16[512,768]{1,0:T(8,128)(2,1)S(1)} %get-tuple-element.77.w_ref), custom_call_target="tpu_custom_call" | custom-call | tf_op jit(solution)/shard_map/column_grad_hidden/pallas_call | solution.py:493
  28.5 0.5 collective-permute-start.9
  29.0 0.4 collective-permute-done.11.got_ref
  29.4 0.7 %add_cores.1 = (f32[64,1664]{1,0:T(8,128)S(1)}, bf16[64,1664]{1,0:T(8,128)(2,1)S(1)}, bf16[64,1664]{1,0:T(8,128)(2,1)S(1)}, bf16[64,1664]{1,0:T(8,128)(2,1)S(1)}) custom-call(s32[4]{0:T(128)S(1)} %pad_add_fusion.place_ref, bf16[4,64,1280]{2,1,0:T(8,128)(2,1)S(1)} %get-tuple-element.85.keep_ref, bf16[4,64,1280]{2,1,0:T(8,128)(2,1)S(1)} %collective-permute-done.11.got_ref, ...), custom_call_target="tpu_custom_call" | custom-call | tf_op jit(solution)/shard_map/add_cores/pallas_call | solution.py:493
  30.1 0.0 copy-start
  30.1 1.5 %collective-permute-start.12 = (bf16[64,1664]{1,0:T(8,128)(2,1)S(1)}, bf16[64,1664]{1,0:T(8,128)(2,1)S(1)}, u32[]{:S(2)}, u32[]{:S(2)}) collective-permute-start(bf16[64,1664]{1,0:T(8,128)(2,1)S(1)} %get-tuple-element.97), channel_id=1, source_target_pairs={{0,24},{4,28},{8,16},{12,20},{16,8},{20,12},{24,0},{28,4},{1,25},{... | collective-permute-start | bytes 638984 | tf_op jit(solution)/shard_map/ppermute | solution.py:507
  31.7 1.5 %collective-permute-start.13 = (bf16[64,1664]{1,0:T(8,128)(2,1)S(1)}, bf16[64,1664]{1,0:T(8,128)(2,1)S(1)}, u32[]{:S(2)}, u32[]{:S(2)}) collective-permute-start(bf16[64,1664]{1,0:T(8,128)(2,1)S(1)} %get-tuple-element.98), channel_id=1, source_target_pairs={{0,16},{4,20},{8,24},{12,28},{16,0},{20,4},{24,8},{28,12},{1,17},{... | collective-permute-start | bytes 638984 | tf_op jit(solution)/shard_map/ppermute | solution.py:507
  33.2 0.5 collective-permute-start.14
  33.7 0.6 pack_grad_hidden.1
  34.3 5.0 %collective-permute-done.12.got_1 = bf16[64,1664]{1,0:T(8,128)(2,1)S(1)} collective-permute-done((bf16[64,1664]{1,0:T(8,128)(2,1)S(1)}, bf16[64,1664]{1,0:T(8,128)(2,1)S(1)}, u32[]{:S(2)}, u32[]{:S(2)}) %collective-permute-start.12) | collective-permute-done | bytes 213024 | tf_op jit(solution)/shard_map/ppermute | solution.py:507
  39.2 3.7 %collective-permute-done.13.got_2 = bf16[64,1664]{1,0:T(8,128)(2,1)S(1)} collective-permute-done((bf16[64,1664]{1,0:T(8,128)(2,1)S(1)}, bf16[64,1664]{1,0:T(8,128)(2,1)S(1)}, u32[]{:S(2)}, u32[]{:S(2)}) %collective-permute-start.13) | collective-permute-done | bytes 213024 | tf_op jit(solution)/shard_map/ppermute | solution.py:507
  43.0 0.0 collective-permute-done.14.got_3
  43.0 0.6 %add_chips.1 = (bf16[32,1280]{1,0:T(8,128)(2,1)S(1)}, f32[32,1280]{1,0:T(8,128)S(1)}, bf16[32,768]{1,0:T(8,128)(2,1)S(1)}) custom-call(s32[4]{0:T(128)S(1)} %pad_add_fusion.place_ref, f32[64,1664]{1,0:T(8,128)S(1)} %get-tuple-element.96.own_ref, bf16[64,1664]{1,0:T(8,128)(2,1)S(1)} %collective-permute-done.12.got_1, ...), custom_call_target="tpu_custom_call" | custom-call | tf_op jit(solution)/shard_map/add_chips/pallas_call | solution.py:493
  43.6 1.6 %collective-permute-start.15 = (bf16[32,1280]{1,0:T(8,128)(2,1)S(1)}, bf16[32,1280]{1,0:T(8,128)(2,1)S(1)}, u32[]{:S(2)}, u32[]{:S(2)}) collective-permute-start(bf16[32,1280]{1,0:T(8,128)(2,1)S(1)} %get-tuple-element.101), channel_id=1, source_target_pairs={{0,1},{1,0},{2,3},{3,2},{4,5},{5,4},{6,7},{7,6},{8,9},{9,8},{10,11... | collective-permute-start | bytes 245768 | tf_op jit(solution)/shard_map/ppermute | solution.py:507
  45.3 2.9 %collective-permute-done.15.got_ref = bf16[32,1280]{1,0:T(8,128)(2,1)S(1)} collective-permute-done((bf16[32,1280]{1,0:T(8,128)(2,1)S(1)}, bf16[32,1280]{1,0:T(8,128)(2,1)S(1)}, u32[]{:S(2)}, u32[]{:S(2)}) %collective-permute-start.15) | collective-permute-done | bytes 81952 | tf_op jit(solution)/shard_map/ppermute | solution.py:507
  48.2 2.7 %collective-permute-start.19 = (bf16[32,2048]{1,0:T(8,128)(2,1)S(1)}, bf16[32,2048]{1,0:T(8,128)(2,1)S(1)}, u32[]{:S(2)}, u32[]{:S(2)}) collective-permute-start(bf16[32,2048]{1,0:T(8,128)(2,1)S(1)} %add_pair.1.kept_ref), channel_id=1, source_target_pairs={{0,2},{1,3},{2,0},{3,1},{4,6},{5,7},{6,4},{7,5},{8,10},{9,11},{10,... | collective-permute-start | bytes 393224 | tf_op jit(solution)/shard_map/ppermute | solution.py:507
  50.8 1.6 %collective-permute-start.16 = (bf16[128,512]{1,0:T(8,128)(2,1)S(1)}, bf16[128,512]{1,0:T(8,128)(2,1)S(1)}, u32[]{:S(2)}, u32[]{:S(2)}) collective-permute-start(bf16[128,512]{1,0:T(8,128)(2,1)S(1)} %get-tuple-element.104), channel_id=1, source_target_pairs={{0,24},{4,28},{8,16},{12,20},{16,8},{20,12},{24,0},{28,4},{1,25},{... | collective-permute-start | bytes 393224 | tf_op jit(solution)/shard_map/ppermute | solution.py:507
  52.5 1.3 %collective-permute-start.17 = (bf16[128,512]{1,0:T(8,128)(2,1)S(1)}, bf16[128,512]{1,0:T(8,128)(2,1)S(1)}, u32[]{:S(2)}, u32[]{:S(2)}) collective-permute-start(bf16[128,512]{1,0:T(8,128)(2,1)S(1)} %get-tuple-element.105), channel_id=1, source_target_pairs={{0,16},{4,20},{8,24},{12,28},{16,0},{20,4},{24,8},{28,12},{1,17},{... | collective-permute-start | bytes 393224 | tf_op jit(solution)/shard_map/ppermute | solution.py:507
  53.8 0.5 collective-permute-start.18
  54.3 1.9 %collective-permute-done.19.got_ref = bf16[32,2048]{1,0:T(8,128)(2,1)S(1)} collective-permute-done((bf16[32,2048]{1,0:T(8,128)(2,1)S(1)}, bf16[32,2048]{1,0:T(8,128)(2,1)S(1)}, u32[]{:S(2)}, u32[]{:S(2)}) %collective-permute-start.19) | collective-permute-done | bytes 131104 | tf_op jit(solution)/shard_map/ppermute | solution.py:507
  56.2 0.7 %collective-permute-start.20 = (bf16[32,2048]{1,0:T(8,128)(2,1)S(1)}, bf16[32,2048]{1,0:T(8,128)(2,1)S(1)}, u32[]{:S(2)}, u32[]{:S(2)}) collective-permute-start(bf16[32,2048]{1,0:T(8,128)(2,1)S(1)} %add_pairs.1.held_ref), channel_id=1, source_target_pairs={{0,1},{1,0},{2,3},{3,2},{4,5},{5,4},{6,7},{7,6},{8,9},{9,8},{10,11... | collective-permute-start | bytes 393224 | tf_op jit(solution)/shard_map/ppermute | solution.py:507
  57.0 0.4 collective-permute-done.16.got_1
  57.4 1.1 %collective-permute-done.17.got_2 = bf16[128,512]{1,0:T(8,128)(2,1)S(1)} collective-permute-done((bf16[128,512]{1,0:T(8,128)(2,1)S(1)}, bf16[128,512]{1,0:T(8,128)(2,1)S(1)}, u32[]{:S(2)}, u32[]{:S(2)}) %collective-permute-start.17) | collective-permute-done | bytes 131104 | tf_op jit(solution)/shard_map/ppermute | solution.py:507
  58.5 0.2 collective-permute-done.18.got_3
  58.7 1.7 %input_grad.1 = bf16[512,512]{1,0:T(8,128)(2,1)} custom-call(s32[4]{0:T(128)S(1)} %pad_add_fusion.place_ref, f32[512,512]{1,0:T(8,128)S(1)} %get-tuple-element.60.base_ref, f32[512,512]{1,0:T(8,128)S(1)} %get-tuple-element.61.normed_ref, f32[512,1]{1,0:T(8,128)S(1)} %get-tuple-element.62.inverse_ref, f32[1,512]{1,0:T(1,128)S(1)} %bitcast.11, ...), custom_call_target="tpu_custom_call" | custom-call | tf_op jit(solution)/shard_map/input_grad/pallas_call | solution.py:493
  60.4 0.8 %collective-permute-done.20.got_ref = bf16[32,2048]{1,0:T(8,128)(2,1)S(1)} collective-permute-done((bf16[32,2048]{1,0:T(8,128)(2,1)S(1)}, bf16[32,2048]{1,0:T(8,128)(2,1)S(1)}, u32[]{:S(2)}, u32[]{:S(2)}) %collective-permute-start.20) | collective-permute-done | bytes 131104 | tf_op jit(solution)/shard_map/ppermute | solution.py:507
  61.3 1.4 %result.1 = (f32[64,1536]{1,0:T(8,128)}, f32[64,512]{1,0:T(8,128)}, f32[1,64]{1,0:T(1,128)}) custom-call(s32[4]{0:T(128)S(1)} %pad_add_fusion.place_ref, bf16[32,2048]{1,0:T(8,128)(2,1)S(1)} %add_pairs.1.held_ref, bf16[32,2048]{1,0:T(8,128)(2,1)S(1)} %collective-permute-done.20.got_ref, bf16[64,1536]{1,0:T(8,128)(2,1)S(1)} %get-tuple-element.108.w_ref, ...), custom_call_target="tpu_custom_call" | custom-call | tf_op jit(solution)/shard_map/result/pallas_call | solution.py:493
  (9 shorter events, 0.1 us)
Async XLA Ops:
  2.6 4.7 %collective-permute-start = (bf16[2,64,512]{2,1,0:T(8,128)(2,1)S(1)}, bf16[2,64,512]{2,1,0:T(8,128)(2,1)S(1)}, u32[]{:S(2)}, u32[]{:S(2)}) collective-permute-start(bf16[2,64,512]{2,1,0:T(8,128)(2,1)S(1)} %get-tuple-element.58), channel_id=1, source_target_pairs={{0,4},{4,0},{8,12},{12,8},{16,20},{20,16},{24,28},{28,24},{1,5},{5... | collective-permute-start | bytes 393224 | tf_op jit(solution)/shard_map/ppermute | solution.py:507
  3.1 14.5 %collective-permute-start.1 = (bf16[2,128,512]{2,1,0:T(8,128)(2,1)S(1)}, bf16[2,128,512]{2,1,0:T(8,128)(2,1)S(1)}, u32[]{:S(2)}, u32[]{:S(2)}) collective-permute-start(bf16[2,128,512]{2,1,0:T(8,128)(2,1)S(1)} %get-tuple-element.63), channel_id=1, source_target_pairs={{0,24},{4,28},{8,16},{12,20},{16,8},{20,12},{24,0},{28,4},{1,25},{... | collective-permute-start | bytes 786440 | tf_op jit(solution)/shard_map/ppermute | solution.py:507
  6.6 12.5 %collective-permute-start.2 = (bf16[2,128,512]{2,1,0:T(8,128)(2,1)S(1)}, bf16[2,128,512]{2,1,0:T(8,128)(2,1)S(1)}, u32[]{:S(2)}, u32[]{:S(2)}) collective-permute-start(bf16[2,128,512]{2,1,0:T(8,128)(2,1)S(1)} %get-tuple-element.64), channel_id=1, source_target_pairs={{0,16},{4,20},{8,24},{12,28},{16,0},{20,4},{24,8},{28,12},{1,17},{... | collective-permute-start | bytes 786440 | tf_op jit(solution)/shard_map/ppermute | solution.py:507
  7.2 12.3 %collective-permute-start.3 = (bf16[2,128,512]{2,1,0:T(8,128)(2,1)S(1)}, bf16[2,128,512]{2,1,0:T(8,128)(2,1)S(1)}, u32[]{:S(2)}, u32[]{:S(2)}) collective-permute-start(bf16[2,128,512]{2,1,0:T(8,128)(2,1)S(1)} %get-tuple-element.65), channel_id=1, source_target_pairs={{0,8},{4,12},{8,0},{12,4},{16,24},{20,28},{24,16},{28,20},{1,9},{5... | collective-permute-start | bytes 786440 | tf_op jit(solution)/shard_map/ppermute | solution.py:507
  15.1 1.5 %collective-permute-start.4 = (bf16[4,64,384]{2,1,0:T(8,128)(2,1)S(1)}, bf16[4,64,384]{2,1,0:T(8,128)(2,1)S(1)}, u32[]{:S(2)}, u32[]{:S(2)}) collective-permute-start(bf16[4,64,384]{2,1,0:T(8,128)(2,1)S(1)} %get-tuple-element.68), channel_id=1, source_target_pairs={{0,4},{4,0},{8,12},{12,8},{16,20},{20,16},{24,28},{28,24},{1,5},{5... | collective-permute-start | bytes 589832 | tf_op jit(solution)/shard_map/ppermute | solution.py:507
  15.2 1.7 %collective-permute-start.5 = (bf16[4,64,384]{2,1,0:T(8,128)(2,1)S(1)}, bf16[4,64,384]{2,1,0:T(8,128)(2,1)S(1)}, u32[]{:S(2)}, u32[]{:S(2)}) collective-permute-start(bf16[4,64,384]{2,1,0:T(8,128)(2,1)S(1)} %get-tuple-element.69), channel_id=1, source_target_pairs={{0,4},{4,0},{8,12},{12,8},{16,20},{20,16},{24,28},{28,24},{1,5},{5... | collective-permute-start | bytes 589832 | tf_op jit(solution)/shard_map/ppermute | solution.py:507
  19.5 2.1 %collective-permute-start.6 = (bf16[2,128,512]{2,1,0:T(8,128)(2,1)S(1)}, bf16[2,128,512]{2,1,0:T(8,128)(2,1)S(1)}, u32[]{:S(2)}, u32[]{:S(2)}) collective-permute-start(bf16[2,128,512]{2,1,0:T(8,128)(2,1)S(1)} %collective-permute-done.1.near_1), channel_id=1, source_target_pairs={{0,4},{4,0},{8,12},{12,8},{16,20},{20,16},{24,28},{28,24},{1,5},{5... | collective-permute-start | bytes 786440 | tf_op jit(solution)/shard_map/ppermute | solution.py:507
  19.5 2.1 %collective-permute-start.7 = (bf16[2,128,512]{2,1,0:T(8,128)(2,1)S(1)}, bf16[2,128,512]{2,1,0:T(8,128)(2,1)S(1)}, u32[]{:S(2)}, u32[]{:S(2)}) collective-permute-start(bf16[2,128,512]{2,1,0:T(8,128)(2,1)S(1)} %collective-permute-done.2.near_2), channel_id=1, source_target_pairs={{0,4},{4,0},{8,12},{12,8},{16,20},{20,16},{24,28},{28,24},{1,5},{5... | collective-permute-start | bytes 786440 | tf_op jit(solution)/shard_map/ppermute | solution.py:507
  20.0 1.8 %collective-permute-start.8 = (bf16[2,128,512]{2,1,0:T(8,128)(2,1)S(1)}, bf16[2,128,512]{2,1,0:T(8,128)(2,1)S(1)}, u32[]{:S(2)}, u32[]{:S(2)}) collective-permute-start(bf16[2,128,512]{2,1,0:T(8,128)(2,1)S(1)} %collective-permute-done.3.near_3), channel_id=1, source_target_pairs={{0,4},{4,0},{8,12},{12,8},{16,20},{20,16},{24,28},{28,24},{1,5},{5... | collective-permute-start | bytes 786440 | tf_op jit(solution)/shard_map/ppermute | solution.py:507
  20.0 7.3 %collective-permute-start.10 = (bf16[4,32,768]{2,1,0:T(8,128)(2,1)S(1)}, bf16[4,32,768]{2,1,0:T(8,128)(2,1)S(1)}, u32[]{:S(2)}, u32[]{:S(2)}) collective-permute-start(bf16[4,32,768]{2,1,0:T(8,128)(2,1)S(1)} %get-tuple-element.87), channel_id=1, source_target_pairs={{0,1},{1,0},{2,3},{3,2},{4,5},{5,4},{6,7},{7,6},{8,9},{9,8},{10,11... | collective-permute-start | bytes 589832 | tf_op jit(solution)/shard_map/ppermute | solution.py:507
  27.3 2.1 %collective-permute-start.11 = (bf16[4,64,1280]{2,1,0:T(8,128)(2,1)S(1)}, bf16[4,64,1280]{2,1,0:T(8,128)(2,1)S(1)}, u32[]{:S(2)}, u32[]{:S(2)}) collective-permute-start(bf16[4,64,1280]{2,1,0:T(8,128)(2,1)S(1)} %get-tuple-element.88), channel_id=1, source_target_pairs={{0,4},{4,0},{8,12},{12,8},{16,20},{20,16},{24,28},{28,24},{1,5},{5... | collective-permute-start | bytes 1966088 | tf_op jit(solution)/shard_map/ppermute | solution.py:507
  28.5 5.2 %collective-permute-start.9 = (bf16[4,64,512]{2,1,0:T(8,128)(2,1)S(1)}, bf16[4,64,512]{2,1,0:T(8,128)(2,1)S(1)}, u32[]{:S(2)}, u32[]{:S(2)}) collective-permute-start(bf16[4,64,512]{2,1,0:T(8,128)(2,1)S(1)} %get-tuple-element.80), channel_id=1, source_target_pairs={{0,4},{4,0},{8,12},{12,8},{16,20},{20,16},{24,28},{28,24},{1,5},{5... | collective-permute-start | bytes 786440 | tf_op jit(solution)/shard_map/ppermute | solution.py:507
  30.1 28.6 %copy-start = (f32[512]{0:T(512)S(1)}, f32[512]{0:T(512)}, u32[]{:S(2)}) copy-start(f32[512]{0:T(512)} %param.6) | copy-start | bytes 6148
  30.1 9.1 %collective-permute-start.12 = (bf16[64,1664]{1,0:T(8,128)(2,1)S(1)}, bf16[64,1664]{1,0:T(8,128)(2,1)S(1)}, u32[]{:S(2)}, u32[]{:S(2)}) collective-permute-start(bf16[64,1664]{1,0:T(8,128)(2,1)S(1)} %get-tuple-element.97), channel_id=1, source_target_pairs={{0,24},{4,28},{8,16},{12,20},{16,8},{20,12},{24,0},{28,4},{1,25},{... | collective-permute-start | bytes 638984 | tf_op jit(solution)/shard_map/ppermute | solution.py:507
  31.7 11.3 %collective-permute-start.13 = (bf16[64,1664]{1,0:T(8,128)(2,1)S(1)}, bf16[64,1664]{1,0:T(8,128)(2,1)S(1)}, u32[]{:S(2)}, u32[]{:S(2)}) collective-permute-start(bf16[64,1664]{1,0:T(8,128)(2,1)S(1)} %get-tuple-element.98), channel_id=1, source_target_pairs={{0,16},{4,20},{8,24},{12,28},{16,0},{20,4},{24,8},{28,12},{1,17},{... | collective-permute-start | bytes 638984 | tf_op jit(solution)/shard_map/ppermute | solution.py:507
  33.2 9.8 %collective-permute-start.14 = (bf16[64,1664]{1,0:T(8,128)(2,1)S(1)}, bf16[64,1664]{1,0:T(8,128)(2,1)S(1)}, u32[]{:S(2)}, u32[]{:S(2)}) collective-permute-start(bf16[64,1664]{1,0:T(8,128)(2,1)S(1)} %get-tuple-element.99), channel_id=1, source_target_pairs={{0,8},{4,12},{8,0},{12,4},{16,24},{20,28},{24,16},{28,20},{1,9},{5... | collective-permute-start | bytes 638984 | tf_op jit(solution)/shard_map/ppermute | solution.py:507
  43.6 4.5 %collective-permute-start.15 = (bf16[32,1280]{1,0:T(8,128)(2,1)S(1)}, bf16[32,1280]{1,0:T(8,128)(2,1)S(1)}, u32[]{:S(2)}, u32[]{:S(2)}) collective-permute-start(bf16[32,1280]{1,0:T(8,128)(2,1)S(1)} %get-tuple-element.101), channel_id=1, source_target_pairs={{0,1},{1,0},{2,3},{3,2},{4,5},{5,4},{6,7},{7,6},{8,9},{9,8},{10,11... | collective-permute-start | bytes 245768 | tf_op jit(solution)/shard_map/ppermute | solution.py:507
  48.2 8.0 %collective-permute-start.19 = (bf16[32,2048]{1,0:T(8,128)(2,1)S(1)}, bf16[32,2048]{1,0:T(8,128)(2,1)S(1)}, u32[]{:S(2)}, u32[]{:S(2)}) collective-permute-start(bf16[32,2048]{1,0:T(8,128)(2,1)S(1)} %add_pair.1.kept_ref), channel_id=1, source_target_pairs={{0,2},{1,3},{2,0},{3,1},{4,6},{5,7},{6,4},{7,5},{8,10},{9,11},{10,... | collective-permute-start | bytes 393224 | tf_op jit(solution)/shard_map/ppermute | solution.py:507
  50.8 6.6 %collective-permute-start.16 = (bf16[128,512]{1,0:T(8,128)(2,1)S(1)}, bf16[128,512]{1,0:T(8,128)(2,1)S(1)}, u32[]{:S(2)}, u32[]{:S(2)}) collective-permute-start(bf16[128,512]{1,0:T(8,128)(2,1)S(1)} %get-tuple-element.104), channel_id=1, source_target_pairs={{0,24},{4,28},{8,16},{12,20},{16,8},{20,12},{24,0},{28,4},{1,25},{... | collective-permute-start | bytes 393224 | tf_op jit(solution)/shard_map/ppermute | solution.py:507
  52.5 6.0 %collective-permute-start.17 = (bf16[128,512]{1,0:T(8,128)(2,1)S(1)}, bf16[128,512]{1,0:T(8,128)(2,1)S(1)}, u32[]{:S(2)}, u32[]{:S(2)}) collective-permute-start(bf16[128,512]{1,0:T(8,128)(2,1)S(1)} %get-tuple-element.105), channel_id=1, source_target_pairs={{0,16},{4,20},{8,24},{12,28},{16,0},{20,4},{24,8},{28,12},{1,17},{... | collective-permute-start | bytes 393224 | tf_op jit(solution)/shard_map/ppermute | solution.py:507
  53.8 5.0 %collective-permute-start.18 = (bf16[128,512]{1,0:T(8,128)(2,1)S(1)}, bf16[128,512]{1,0:T(8,128)(2,1)S(1)}, u32[]{:S(2)}, u32[]{:S(2)}) collective-permute-start(bf16[128,512]{1,0:T(8,128)(2,1)S(1)} %get-tuple-element.106), channel_id=1, source_target_pairs={{0,8},{4,12},{8,0},{12,4},{16,24},{20,28},{24,16},{28,20},{1,9},{5... | collective-permute-start | bytes 393224 | tf_op jit(solution)/shard_map/ppermute | solution.py:507
  56.2 5.0 %collective-permute-start.20 = (bf16[32,2048]{1,0:T(8,128)(2,1)S(1)}, bf16[32,2048]{1,0:T(8,128)(2,1)S(1)}, u32[]{:S(2)}, u32[]{:S(2)}) collective-permute-start(bf16[32,2048]{1,0:T(8,128)(2,1)S(1)} %add_pairs.1.held_ref), channel_id=1, source_target_pairs={{0,1},{1,0},{2,3},{3,2},{4,5},{5,4},{6,7},{7,6},{8,9},{9,8},{10,11... | collective-permute-start | bytes 393224 | tf_op jit(solution)/shard_map/ppermute | solution.py:507

commit v9 on v8

v9 whole, which is shorter than its diff:
```python
import math

import jax
import jax.numpy as jnp
from jax import lax
from jax.experimental import pallas as pl
from jax.experimental.pallas import tpu as pltpu
from jax.sharding import PartitionSpec as P

H = 8
HD = 64
HH = H // 2
HW = HH * HD
SCALE = HD ** (-0.5)
F32 = jnp.float32
BF16 = jnp.bfloat16
QUERY_BLOCK = 128
BIG_VMEM = 20 * 1024 * 1024
SMALL_VMEM = 8 * 1024 * 1024
ANY = pl.BlockSpec(memory_space=pl.ANY)
VMEM = pl.BlockSpec(memory_space=pltpu.VMEM)
HBM = pl.BlockSpec(memory_space=pltpu.HBM)
CHIP_STEPS = (3, 2, 1)
PINNED = pl.BlockSpec(memory_space=pltpu.VMEM)
shaped = jax.ShapeDtypeStruct


def here():
    device = lax.axis_index("seq")
    return device >> 1, device & 1, lax.axis_index("dp")


def dot_nn(a, b):
    return lax.dot_general(a, b, (((1,), (0,)), ((), ())), preferred_element_type=F32)


def dot_nt(a, b):
    return lax.dot_general(a, b, (((1,), (1,)), ((), ())), preferred_element_type=F32)


def rms_parts(x):
    inverse_rms = lax.rsqrt(jnp.mean(x * x, -1, keepdims=True) + 1e-05)
    return inverse_rms, x * inverse_rms


def transposed(x):
    block = math.gcd(x.shape[1], 256)
    eye = (
        lax.broadcasted_iota(jnp.int32, (block, block), 0)
        == lax.broadcasted_iota(jnp.int32, (block, block), 1)
    ).astype(F32).astype(BF16)
    parts = [
        dot_nt(eye, x[:, at : at + block]).astype(BF16) for at in range(0, x.shape[1], block)
    ]
    return parts[0] if len(parts) == 1 else jnp.concatenate(parts, 0)


def head_pair(x):
    lane = lax.broadcasted_iota(jnp.int32, x.shape, 1)
    zero = jnp.zeros_like(x)
    return jnp.concatenate([jnp.where(lane < HD, x, zero), jnp.where(lane < HD, zero, x)], 0)


def both_heads(both, count):
    return jnp.concatenate([both[:HD, :count], both[HD:, count:]], 0)


def pair_steps(items, mask_rows, mask):
    count = items[0][2].shape[1]
    scores = [dot_nt(k, q2) for q2, _, _, k, _, _, _ in items]
    prob_grads = [dot_nt(v, g2) for _, g2, _, _, v, _, _ in items]
    probs = []
    for score in scores:
        first = score.shape[0] - mask_rows
        tail = jnp.where(mask, score[first:], -1e30)
        score = tail if first == 0 else jnp.concatenate([score[:first], tail], 0)
        exponent = jnp.exp(score - jnp.max(score, 0, keepdims=True))
        probs.append(exponent * (1.0 / jnp.sum(exponent, 0, keepdims=True)))
    weights = [prob.astype(BF16) for prob in probs]
    attended = [
        both_heads(dot_nn(item[6], weight), count).astype(BF16)
        for item, weight in zip(items, weights)
    ]
    score_grads = []
    for item, att, prob, prob_grad in zip(items, attended, probs, prob_grads):
        product = item[2].astype(F32) * att.astype(F32)
        delta = [jnp.sum(part, 0, keepdims=True) for part in (product[:HD], product[HD:])]
        score_grads.append((prob * (prob_grad - jnp.concatenate(delta, 1))).astype(BF16))
    grad_q = [
        (both_heads(dot_nn(item[5], score_grad), count) * SCALE).astype(BF16)
        for item, score_grad in zip(items, score_grads)
    ]
    grad_k = [dot_nn(score_grad, item[0]) for item, score_grad in zip(items, score_grads)]
    grad_v = [dot_nn(weight, item[1]) for item, weight in zip(items, weights)]
    return list(zip(attended, grad_q, grad_k, grad_v))


def split_cores(piece, send_ref, keep_ref, chips, lanes):
    rows = send_ref.shape[1]
    parts = piece.reshape(chips.stop - chips.start, 2, rows, piece.shape[1])
    even, odd = parts[:, 0], parts[:, 1]
    first = here()[1] == 0
    send_ref[chips, :, lanes] = jnp.where(first, odd, even)
    keep_ref[chips, :, lanes] = jnp.where(first, even, odd)


def qkv_copies(wqkv_ref, w_ref, sems, second):
    width = wqkv_ref.shape[0]
    return [
        pltpu.make_async_copy(
            wqkv_ref.at[:, pl.ds(i * width + second * HW, HW)],
            w_ref.at[:, pl.ds(i * HW, HW)],
            sems.at[i],
        )
        for i in range(3)
    ]


def weight_copies(wqkv_ref, wout_ref, w_ref, wo_ref, sems, second):
    out_rows = wout_ref.at[pl.ds(second * HW, HW), :]
    return [
        *qkv_copies(wqkv_ref, w_ref, sems, second),
        pltpu.make_async_copy(out_rows, wo_ref, sems.at[3]),
    ]


def started(*copies):
    for copy in copies:
        copy.start()
    return copies


def finished(*copies):
    for copy in copies:
        copy.wait()


def project(hidden, cot, w_ref, wo_ref):
    projected = dot_nn(hidden, w_ref[...]).astype(BF16)
    q, k, v = [projected[:, i * HW : (i + 1) * HW] for i in range(3)]
    g = dot_nt(cot, wo_ref[...]).astype(BF16)
    return q * jnp.asarray(SCALE, BF16), k, v, g


def row_part(
    x_any, cot_any, gain_any, wqkv_any, wout_any,
    out_ref, base_ref, normed_ref, inverse_ref, x_ref, cot_ref,
    gain_ref, w_ref, wo_ref, dk_ref, dv_ref, grads_ref, sems,
):
    first = started(
        pltpu.make_async_copy(x_any, x_ref, sems.at[4]),
        pltpu.make_async_copy(gain_any, gain_ref, sems.at[5]),
    )
    later = started(
        *weight_copies(wqkv_any, wout_any, w_ref, wo_ref, sems, 0),
        pltpu.make_async_copy(cot_any, cot_ref, sems.at[6]),
    )
    dk_ref[...] = jnp.zeros_like(dk_ref)
    dv_ref[...] = jnp.zeros_like(dv_ref)
    finished(*first)
    tokens = x_ref.shape[0]
    inverse_ref[...], normed_ref[...] = rms_parts(x_ref[...].astype(F32))
    hidden = (normed_ref[...] * gain_ref[...]).astype(BF16)
    hidden_t = transposed(hidden)
    finished(*later)
    cot = cot_ref[...]
    q, k, v, g = project(hidden, cot, w_ref, wo_ref)
    kt, vt, gt = transposed(k), transposed(v), transposed(g)
    step = math.gcd(tokens, QUERY_BLOCK)
    query = lax.broadcasted_iota(jnp.int32, (step, 2 * step), 1) % step
    mask = query >= lax.broadcasted_iota(jnp.int32, (step, 2 * step), 0)
    pairs = [slice(i * 2 * HD, (i + 1) * 2 * HD) for i in range(HH // 2)]
    att_blocks, dq_blocks = [], []
    for start in range(0, tokens, step):
        rows, keys = slice(start, start + step), slice(0, start + step)
        items = [
            (
                head_pair(q[rows, lanes]), head_pair(g[rows, lanes]), gt[lanes, rows],
                k[keys, lanes], v[keys, lanes], kt[lanes, keys], vt[lanes, keys],
            )
            for lanes in pairs
        ]
        results = pair_steps(items, step, mask)
        for lanes, (_, _, dk, dv) in zip(pairs, results):
            dk_ref[keys, lanes] += dk
            dv_ref[keys, lanes] += dv
        att_blocks.append(jnp.concatenate([result[0] for result in results], 0))
        dq_blocks.append(jnp.concatenate([result[1] for result in results], 0))
    grads_ref[:, :HW] = transposed(jnp.concatenate(dq_blocks, 1))
    grads_ref[:, HW : 2 * HW] = dk_ref[...].astype(BF16)
    grads_ref[:, 2 * HW :] = dv_ref[...].astype(BF16)
    term_qkv = dot_nn(hidden_t, grads_ref[...]).astype(BF16)
    out_ref[...] = dot_nn(jnp.concatenate(att_blocks, 1), cot).astype(BF16)
    grad_normed = dot_nt(grads_ref[...], w_ref[...]) * gain_ref[...]
    base_ref[...] = input_grad(
        cot_ref[...].astype(F32), normed_ref[...], inverse_ref[...], grad_normed
    )
    return term_qkv


def row_kernel(x_any, cot_any, gain_any, wqkv_any, wout_any, qkv_ref, *refs):
    qkv_ref[...] = row_part(x_any, cot_any, gain_any, wqkv_any, wout_any, *refs)


def row_chip_kernel(
    x_any, cot_any, gain_any, wqkv_any, wout_any,
    send_1, send_2, keep_1, keep_2, rows_ref, col_w_ref, col_wo_ref, *refs,
):
    chip, core, _ = here()
    sems, rows = refs[-1], rows_ref.shape[0]
    at = pl.multiple_of((chip * 2 + core) * rows, rows)
    handed = started(
        pltpu.make_async_copy(wqkv_any.at[pl.ds(at, rows), :], rows_ref, sems.at[7]),
        *weight_copies(wqkv_any, wout_any, col_w_ref, col_wo_ref, sems.at[pl.ds(8, 4)], 1),
    )
    term_qkv = row_part(x_any, cot_any, gain_any, wqkv_any, wout_any, *refs)
    chips, cut = send_1.shape[0], keep_1.shape[2]
    pieces = slice(0, chips), slice(0, cut)
    split_cores(term_qkv[:, :cut], send_1, keep_1, *pieces)
    split_cores(term_qkv[:, cut:], send_2, keep_2, *pieces)
    finished(*handed)


def column_part(x, cot, mask, gain, w_ref, wo_ref, weight_waits, grads_ref):
    tokens, block = x.shape[0], mask.shape[0]
    _, normed = rms_parts(x.astype(F32))
    hidden = (normed * gain).astype(BF16)
    hidden_t = transposed(hidden)
    finished(*weight_waits)
    q, k, v, g = project(hidden, cot, w_ref, wo_ref)
    kt, vt, gt = transposed(k), transposed(v), transposed(g)
    pairs = [slice(i * 2 * HD, (i + 1) * 2 * HD) for i in range(HH // 2)]
    blocks = [slice(at, at + block) for at in range(0, tokens, block)]
    items = [
        (
            head_pair(q[rows, lanes]), head_pair(g[rows, lanes]), gt[lanes, rows],
            k[rows, lanes], v[rows, lanes], kt[lanes, rows], vt[lanes, rows],
        )
        for lanes in pairs
        for rows in blocks
    ]
    results = pair_steps(items, block, mask)
    places = [(lanes, rows) for lanes in pairs for rows in blocks]
    for (lanes, rows), (_, _, dk, dv) in zip(places, results):
        grads_ref[rows, HW + lanes.start : HW + lanes.stop] = dk.astype(BF16)
        grads_ref[rows, 2 * HW + lanes.start : 2 * HW + lanes.stop] = dv.astype(BF16)
    by_pair = [results[i * len(blocks) : (i + 1) * len(blocks)] for i in range(len(pairs))]
    attended, grad_q = [
        jnp.concatenate([jnp.concatenate([r[i] for r in some], 1) for some in by_pair], 0)
        for i in range(2)
    ]
    grads_ref[:, :HW] = transposed(grad_q)
    term_qkv = dot_nn(hidden_t, grads_ref[...]).astype(BF16)
    term_out = dot_nn(attended, cot).astype(BF16)
    return term_qkv, term_out


def column_mask(all_rows, group, row_of):
    block = all_rows * group
    shape = (block, 2 * block)
    query = lax.broadcasted_iota(jnp.int32, shape, 1) % block
    key = lax.broadcasted_iota(jnp.int32, shape, 0)
    same_column = query % group == key % group
    return (row_of(query // group) >= row_of(key // group)) & same_column


def column_kernel(
    moved_any, gain_any, wqkv_any, wout_any, row_qkv_ref, row_out_ref,
    terms_ref, grads_ref, w_ref,
    moved_ref, gain_ref, wo_ref, sems,
):
    copies = started(
        pltpu.make_async_copy(moved_any, moved_ref, sems.at[4]),
        pltpu.make_async_copy(gain_any, gain_ref, sems.at[5]),
    )
    weights = started(*weight_copies(wqkv_any, wout_any, w_ref, wo_ref, sems, 1))
    finished(*copies)
    all_rows, _, share, width = moved_ref.shape
    group = math.gcd(share, 16)
    x, cot = [
        jnp.concatenate(
            [
                moved_ref[:, which, at : at + group, :].astype(F32).reshape(all_rows * group, width)
                for at in range(0, share, group)
            ],
            0,
        ).astype(BF16)
        for which in range(2)
    ]
    mask = column_mask(all_rows, group, lambda place: place)
    term_qkv, term_out = column_part(
        x, cot, mask, gain_ref[...], w_ref, wo_ref, weights, grads_ref
    )
    for i in range(3):
        at = i * width
        terms_ref[:, at : at + HW] = row_qkv_ref[:, i * HW : (i + 1) * HW]
        terms_ref[:, at + HW : at + 2 * HW] = term_qkv[:, i * HW : (i + 1) * HW]
    terms_ref[:HW, 3 * width :] = row_out_ref[...]
    terms_ref[HW:, 3 * width :] = term_out


def column_chip_kernel(
    x_ref, cot_ref, near_1, near_2, near_3, far_ref, gain_ref, w_ref, wo_ref, row_out_ref,
    send_ref, keep_ref, grads_ref,
):
    chip, core, _ = here()
    share = far_ref.shape[2]
    half = pl.ds(pl.multiple_of(core * share, share), share)
    at = pl.ds(pl.multiple_of((chip * 2 + core) * share, share), share)
    group = math.gcd(share, 16)

    def tokens(which, mine):
        pieces = [mine[at, :], far_ref[0, which]]
        for i, near in enumerate((near_1, near_2, near_3)):
            pieces += [near[which, half, :], far_ref[i + 1, which]]
        starts = range(0, share, group)
        return jnp.concatenate(
            [piece[start : start + group] for start in starts for piece in pieces], 0
        )

    def row_of(place):
        step = (4 - (place >> 1)) & 3
        return ((step ^ chip) << 1) + ((place & 1) ^ core)

    mask = column_mask(2 * (len(CHIP_STEPS) + 1), group, row_of)
    term_qkv, term_out = column_part(
        tokens(0, x_ref), tokens(1, cot_ref), mask, gain_ref[...], w_ref, wo_ref, (), grads_ref
    )
    chips = send_ref.shape[0]
    refs = send_ref, keep_ref
    out_lanes = slice(3 * HW, send_ref.shape[2])
    split_cores(term_qkv, *refs, slice(0, chips), slice(0, 3 * HW))
    split_cores(row_out_ref[...], *refs, slice(0, chips // 2), out_lanes)
    split_cores(term_out, *refs, slice(chips // 2, chips), out_lanes)


def far_kernel(x_ref, cot_ref, near_1, near_2, near_3, far_ref):
    chip, core, _ = here()
    share = far_ref.shape[2]
    at = pl.ds(pl.multiple_of((chip * 2 + 1 - core) * share, share), share)
    far_ref[0, 0], far_ref[0, 1] = x_ref[at, :], cot_ref[at, :]
    at = pl.ds(pl.multiple_of((1 - core) * share, share), share)
    for i, near in enumerate((near_1, near_2, near_3)):
        far_ref[i + 1] = near[:, at, :]


def back_kernel(grads_ref, w_ref, back_ref):
    grad_hidden = dot_nt(grads_ref[...], w_ref[...])
    all_rows, share, width = back_ref.shape
    group = math.gcd(share, 16)
    block = all_rows * group
    for i in range(share // group):
        piece = grad_hidden[i * block : (i + 1) * block].reshape(all_rows, group, width)
        back_ref[:, i * group : (i + 1) * group, :] = piece.astype(BF16)


def back_chip_kernel(grads_ref, w_ref, send_ref, keep_ref):
    grad_hidden = dot_nt(grads_ref[...], w_ref[...]).astype(BF16)
    chips, share, width = keep_ref.shape
    group = math.gcd(share, 16)
    block = 2 * chips * group
    for i in range(share // group):
        piece = grad_hidden[i * block : (i + 1) * block].reshape(chips, 2, group, width)
        at = slice(i * group, (i + 1) * group)
        keep_ref[:, at, :], send_ref[:, at, :] = piece[:, 0], piece[:, 1]


def back_pack_kernel(keep_ref, got_ref, *targets):
    share = keep_ref.shape[1]
    core = here()[1]
    kept_at = pl.ds(pl.multiple_of(core * share, share), share)
    got_at = pl.ds(pl.multiple_of((1 - core) * share, share), share)
    for i, target in enumerate(targets):
        target[kept_at, :] = keep_ref[i]
        target[got_at, :] = got_ref[i]


def input_kernel(base_ref, normed_ref, inverse_ref, gain_ref, back_ref, grad_ref):
    grad_ref[...] = input_grad(
        base_ref[...], normed_ref[...], inverse_ref[...], back_ref[...].astype(F32) * gain_ref[...]
    ).astype(BF16)


def input_grad(base, normed, inverse_rms, grad_normed):
    projected = jnp.mean(grad_normed * normed, -1, keepdims=True)
    return base + inverse_rms * (grad_normed - normed * projected)


def input_chip_kernel(
    base_ref, normed_ref, inverse_ref, gain_ref, own_ref, got_1, got_2, got_3,
    grad_any, grad_ref, sems,
):
    chip = here()[0]
    count = own_ref.shape[0]
    copies = []
    for i, (step, back_ref) in enumerate(zip((0, *CHIP_STEPS), (own_ref, got_1, got_2, got_3))):
        at = pl.ds(pl.multiple_of((chip ^ step) * count, count), count)
        grad_normed = back_ref[...].astype(F32) * gain_ref[...]
        grad = input_grad(base_ref[at, :], normed_ref[at, :], inverse_ref[at, :], grad_normed)
        grad_ref[i] = grad.astype(BF16)
        copies += started(pltpu.make_async_copy(grad_ref.at[i], grad_any.at[at, :], sems.at[i]))
    finished(*copies)


def pack_kernel(x_any, cot_any, off_1, off_2, off_3, sems):
    chip = here()[0]
    count = off_1.shape[1]
    copies = []
    for i, (step, target) in enumerate(zip(CHIP_STEPS, (off_1, off_2, off_3))):
        at = pl.ds(pl.multiple_of((chip ^ step) * count, count), count)
        for which, source in enumerate((x_any, cot_any)):
            copies.append(
                pltpu.make_async_copy(source.at[at, :], target.at[which], sems.at[2 * i + which])
            )
    finished(*started(*copies))


def chip_sum_kernel(*refs):
    chip = here()[0]
    pieces, targets = refs[:-4], refs[-4:]
    count = len(pieces) // 2
    for step, target in zip((0, *CHIP_STEPS), targets):
        there, at = chip ^ step, 0
        for kept_ref, got_ref in zip(pieces[:count], pieces[count:]):
            to = slice(at, at + kept_ref.shape[2])
            total = kept_ref[there].astype(F32) + got_ref[there].astype(F32)
            target[:, to] = total.astype(target.dtype)
            at = to.stop


def layer_sum_kernel(own_ref, got_1, got_2, got_3, send_ref, keep_ref):
    upper = (here()[2] & 1) == 1
    total = own_ref[...] + (
        (got_1[...].astype(F32) + got_2[...].astype(F32)) + got_3[...].astype(F32)
    )
    half = total.shape[0] // 2
    low, high = total[:half], total[half:]
    send_ref[...] = jnp.where(upper, low, high).astype(BF16)
    keep_ref[...] = jnp.where(upper, high, low)


def join_kernel(kept_ref, got_ref, row_kept, row_got, out_ref):
    cut = kept_ref.shape[1]
    out_ref[:, :cut] = (kept_ref[...] + got_ref[...].astype(F32)).astype(BF16)
    out_ref[:, cut:] = (row_kept[...] + row_got[...].astype(F32)).astype(BF16)


def add_kernel(kept_ref, got_ref, out_ref):
    out_ref[...] = (kept_ref[...].astype(F32) + got_ref[...].astype(F32)).astype(BF16)


def result_kernel(held_ref, got_ref, w_ref, gain_ref, qkv_ref, out_ref, grad_ref):
    rows = qkv_ref.shape[0]
    chip, core, layer = here()
    at = (chip * 2 + core) * rows
    upper = (layer & 1) == 1
    half = rows // 2
    width = out_ref.shape[1]

    def ordered(lanes):
        held, got = held_ref[:, lanes].astype(F32), got_ref[:, lanes].astype(F32)
        return (jnp.where(upper, got, held), jnp.where(upper, held, got))

    row_at = 3 * HW + width
    for i in range(3):
        for at_from, at_to in ((row_at + i * HW, i * width), (i * HW, i * width + HW)):
            to = slice(at_to, at_to + HW)
            qkv_ref[:half, to], qkv_ref[half:, to] = ordered(slice(at_from, at_from + HW))
    out_ref[:half], out_ref[half:] = ordered(slice(3 * HW, row_at))
    total = jnp.sum(qkv_ref[...] * w_ref[...].astype(F32), -1, keepdims=True)
    shape = (rows, gain_ref.shape[1])
    row = lax.broadcasted_iota(jnp.int32, shape, 0)
    feature = lax.broadcasted_iota(jnp.int32, shape, 1)
    gain = jnp.sum(jnp.where(feature == row + at, gain_ref[...], 0.0), -1, keepdims=True)
    shape = (rows, grad_ref.shape[1])
    same = lax.broadcasted_iota(jnp.int32, shape, 0) == lax.broadcasted_iota(jnp.int32, shape, 1)
    grad_ref[...] = jnp.sum(jnp.where(same, total / gain, 0.0), 0, keepdims=True)


def call(kernel, name, ins, outs, scratch=(), vmem=SMALL_VMEM, out_specs=None):
    out_specs = out_specs or [VMEM] * len(outs)
    places = [{id(HBM): pltpu.HBM, id(PINNED): pltpu.VMEM}.get(id(spec)) for spec in out_specs]
    outs = [place(*out) if place else shaped(*out) for place, out in zip(places, outs)]
    args = [
        pltpu.with_memory_space_constraint(array, pltpu.HBM) if spec is HBM else array
        for spec, array in ins
    ]
    return pl.pallas_call(
        kernel,
        out_shape=outs,
        in_specs=[spec for spec, _ in ins],
        out_specs=out_specs,
        scratch_shapes=scratch,
        name=name,
        cost_estimate=pl.CostEstimate(flops=0, bytes_accessed=0, transcendentals=0),
        compiler_params=pltpu.CompilerParams(vmem_limit_bytes=vmem),
    )(*args)


def swap(array, axis, bits):
    count = lax.axis_size(axis)
    return lax.ppermute(array, axis, [(i, i ^ bits) for i in range(count)])


def add_cores(keep, got, name):
    rows, wide = keep[0].shape[1], sum(one.shape[2] for one in keep)
    return call(
        chip_sum_kernel,
        name + "_add_cores",
        [(VMEM, one) for one in (*keep, *got)],
        [((rows, wide), F32)] + [((rows, wide), BF16)] * 3,
        out_specs=[PINNED, VMEM, VMEM, VMEM],
    )


def add_chips(owned, got, name):
    half, wide = owned.shape[0] // 2, owned.shape[1]
    return call(
        layer_sum_kernel,
        name + "_add_chips",
        [(VMEM, one) for one in (owned, *got)],
        [((half, wide), BF16), ((half, wide), F32)],
        out_specs=[VMEM, PINNED],
    )


def cross_chips(*offs):
    return [swap(off, "seq", 2 * step) for off, step in zip(offs, CHIP_STEPS)]


def add_two(kept, got, name):
    (total,) = call(add_kernel, name, [(VMEM, kept), (VMEM, got)], [(kept.shape, BF16)])
    return total


def body(inputs, norm_gain, qkv_weight, out_weight, out_cotan):
    columns, width = inputs.shape[2:]
    n = lax.axis_size("seq")
    m = lax.axis_size("dp")
    share = columns // n
    row_share = width // n
    row_width, col_width = 3 * HW, 3 * HW + width
    x = inputs.reshape(columns, width)
    cot = out_cotan.reshape(columns, width)
    gain = norm_gain.reshape(1, width)
    chips = 4
    layered = n == 2 * chips and m == 4 and row_share == share
    weight_scratch = [
        pltpu.VMEM((1, width), F32),
        pltpu.VMEM((width, 3 * HW), BF16),
        pltpu.VMEM((HW, width), BF16),
    ]
    weights = [(HBM, gain), (HBM, qkv_weight), (HBM, out_weight)]
    col_outs = [((columns, 3 * HW), BF16), ((width, 3 * HW), BF16)]

    if layered:
        packed = call(
            pack_kernel,
            "pack_columns",
            [(HBM, x), (HBM, cot)],
            [((2, 2 * share, width), BF16)] * 3,
            [pltpu.SemaphoreType.DMA((6,))],
            out_specs=[ANY] * 3,
        )
        near = cross_chips(*packed)
        x_first, _ = lax.optimization_barrier((x, packed[0]))
    else:
        outgoing = jnp.stack([x.reshape(n, share, width), cot.reshape(n, share, width)], 1)
        moved = lax.all_to_all(outgoing, "seq", split_axis=0, concat_axis=0, tiled=True)
        x_first = x

    row_outs = [
        ((HW, width), BF16),
        ((columns, width), F32), ((columns, width), F32), ((columns, 1), F32),
        ((columns, width), BF16), ((columns, width), BF16),
    ]
    if layered:
        cut = row_width // 2
        split_outs = [((chips, row_share, cut), BF16)] * 4
        handed_outs = [
            ((row_share, 3 * width), BF16), ((width, 3 * HW), BF16), ((HW, width), BF16),
        ]
        row_outs = [*split_outs, *handed_outs, *row_outs]
        specs = [VMEM] * 4 + [PINNED] * (len(row_outs) - 4)
    else:
        row_outs = [((width, row_width), BF16), *row_outs]
        specs = [VMEM] * len(row_outs)
    *row_terms, row_out, base, normed, inverse_rms, x_near, cot_near = call(
        row_chip_kernel if layered else row_kernel,
        "row_heads",
        [(HBM, x_first), (HBM, cot), *weights],
        row_outs,
        [
            *weight_scratch,
            pltpu.VMEM((columns, HW), F32),
            pltpu.VMEM((columns, HW), F32),
            pltpu.VMEM((columns, 3 * HW), BF16),
            pltpu.SemaphoreType.DMA((12,)),
        ],
        BIG_VMEM,
        specs,
    )
    if layered:
        *row_terms, weight_rows, col_weight, col_out_weight = row_terms
        row_sent = [swap(one, "seq", 1) for one in row_terms[:2]]
        row_owned, *row_off = add_cores(row_terms[2:], row_sent, "row")
        *near, row_owned = lax.optimization_barrier((*near, row_owned))
        (far,) = call(
            far_kernel,
            "pack_other_core",
            [(VMEM, one) for one in (x_near, cot_near, *near)],
            [((chips, 2, share, width), BF16)],
        )
        row_got = cross_chips(*row_off)
        send, keep, col_grads = call(
            column_chip_kernel,
            "column_heads",
            [
                (VMEM, one)
                for one in (
                    x_near, cot_near, *near, swap(far, "seq", 1),
                    gain, col_weight, col_out_weight, row_out,
                )
            ],
            [((chips, row_share, col_width), BF16)] * 2 + [col_outs[0]],
            vmem=BIG_VMEM,
            out_specs=[VMEM, VMEM, PINNED],
        )
        send, *row_got = lax.optimization_barrier((send, *row_got))
        row_next, row_kept = add_chips(row_owned, row_got, "row")
        back_send, back_keep = call(
            back_chip_kernel,
            "column_grad_hidden",
            [(VMEM, col_grads), (VMEM, col_weight)],
            [((chips, share, width), BF16)] * 2,
        )
        keep, row_kept, back_keep = lax.optimization_barrier((keep, row_kept, back_keep))
        owned, *off = add_cores([keep], [swap(send, "seq", 1)], "column")
        got = cross_chips(*off)
        back = call(
            back_pack_kernel,
            "pack_grad_hidden",
            [(VMEM, back_keep), (VMEM, swap(back_send, "seq", 1))],
            [((2 * share, width), BF16)] * 4,
        )
        row_next, _ = lax.optimization_barrier((row_next, owned))
        row_next = swap(row_next, "dp", 1)
        *back, owned, row_next = lax.optimization_barrier((*back, owned, row_next))
        to_next, kept = add_chips(owned, got, "column")
        (pair_sum,) = call(
            join_kernel,
            "add_pair",
            [
                (VMEM, kept), (VMEM, swap(to_next, "dp", 1)),
                (VMEM, row_kept), (VMEM, row_next),
            ],
            [((row_share // 2, col_width + row_width), BF16)],
        )
        *back, pair_sum = lax.optimization_barrier((*back, pair_sum))
        held = add_two(pair_sum, swap(pair_sum, "dp", 2), "add_pairs")
        other = swap(held, "dp", 1)
        (grad,) = call(
            input_chip_kernel,
            "input_grad",
            [
                (VMEM, one)
                for one in (base, normed, inverse_rms, gain, back[0], *cross_chips(*back[1:]))
            ],
            [((columns, width), BF16)],
            [pltpu.VMEM((chips, 2 * share, width), BF16), pltpu.SemaphoreType.DMA((chips,))],
            out_specs=[HBM],
        )
        sum_qkv, sum_out, sum_gain = call(
            result_kernel,
            "result",
            [(VMEM, held), (VMEM, other), (VMEM, weight_rows), (VMEM, gain)],
            [((row_share, 3 * width), F32), ((row_share, width), F32), ((1, row_share), F32)],
        )
        sum_gain = sum_gain.reshape(row_share)
    else:
        terms, *col_grads = call(
            column_kernel,
            "column_heads",
            [(ANY, moved), *weights, (VMEM, row_terms[0]), (VMEM, row_out)],
            [((width, 4 * width), BF16), *col_outs],
            [
                pltpu.VMEM((n, 2, share, width), BF16),
                weight_scratch[0],
                weight_scratch[2],
                pltpu.SemaphoreType.DMA((6,)),
            ],
            BIG_VMEM,
        )
        (back,) = call(
            back_kernel,
            "column_grad_hidden",
            [(VMEM, one) for one in col_grads],
            [((n, share, width), BF16)],
        )
        returned = lax.all_to_all(back, "seq", split_axis=0, concat_axis=0, tiled=True)
        (grad,) = call(
            input_kernel,
            "input_grad",
            [
                (VMEM, base), (VMEM, normed), (VMEM, inverse_rms), (VMEM, gain),
                (VMEM, returned.reshape(columns, width)),
            ],
            [((columns, width), BF16)],
        )
        terms = lax.all_to_all(
            terms.reshape(n, row_share, 4 * width), "seq", split_axis=0, concat_axis=0, tiled=True
        )
        total = jnp.sum(terms.astype(F32), 0)
        for step in range(m.bit_length() - 1):
            sent = total.astype(BF16)
            total = sent.astype(F32) + swap(sent, "dp", 1 << step).astype(F32)
        sum_qkv, sum_out = total[:, : 3 * width], total[:, 3 * width :]
        here_at = lax.axis_index("seq") * row_share
        own_gain = lax.dynamic_slice_in_dim(norm_gain, here_at, row_share, 0)
        own_weight = lax.dynamic_slice_in_dim(qkv_weight, here_at, row_share, 0)
        sum_gain = jnp.sum(sum_qkv * own_weight.astype(F32), -1) / own_gain
    return (grad.reshape(inputs.shape), sum_qkv, sum_out, sum_gain)


def solution(mesh):
    return jax.shard_map(
        body,
        mesh=mesh,
        in_specs=(P("dp", "seq", None, None), P(), P(), P(), P("dp", "seq", None, None)),
        out_specs=(P("dp", "seq", None, None), P("seq", None), P("seq", None), P("seq")),
        check_vma=False,
    )
```

time: 62.9 us -> 58.4 us (0.928)
  Pallas kernels: 21.9 us -> 15.2 us
  starting transfers between devices: 20 us -> 23 us
    pallas_call x12 -> x14, Pallas kernels: 21.9 us -> 15.2 us  [call(): pl.pallas_call(kernel, out_shape=outs, in_specs=[spec for spec, _ in ins]...]
    ppermute x21, starting transfers between devices: 20 us -> 23 us  [swap(): return lax.ppermute(array, axis, [(i, i ^ bits) for i in range(count)])]
  transfers between devices with their start and end apart: 21 -> 21, of which waited for: 15 -> 15; matrix products, arithmetic and copies ran while one was open for 0% -> 0% of each run, Pallas kernels for 29% -> 22%
where the time goes in v9:
time: 58.4 us; the launch traced here: 58.2 us
  starting transfers between devices  23 us (39%)
  waiting for transfers between devices  19.3 us (33%)
  Pallas kernels  15.2 us (26%)
  between operations  0.76 us (1%)
    ppermute x21, starting transfers between devices, swap(): return lax.ppermute(array, axis, [(i, i ^ bits) for i in range(count)])  23 us
    ppermute x21, waiting for transfers between devices, swap(): return lax.ppermute(array, axis, [(i, i ^ bits) for i in range(count)])  19.3 us
    pallas_call x14, Pallas kernels, call(): pl.pallas_call(kernel, out_shape=outs, in_specs=[spec for spec, _ in ins]...  15.2 us
  transfers between devices with their start and end apart: 21, of which 15 were waited for; matrix products, arithmetic and copies ran while one was open for 0% of the time, Pallas kernels for 22%

profile of v9, /device:TPU:0, one launch (start us, length us, event | category | flops | bytes accessed | tf_op | source)
XLA Modules:
  0.0 58.2 jit_solution(6144409246315293328)
XLA Ops:
  0.6 1.3 %pack_columns.1 = (bf16[2,128,512]{2,1,0:T(8,128)(2,1)S(1)}, bf16[2,128,512]{2,1,0:T(8,128)(2,1)S(1)}, bf16[2,128,512]{2,1,0:T(8,128)(2,1)S(1)}) custom-call(bf16[512,512]{1,0:T(8,128)(2,1)} %bitcast.9, bf16[512,512]{1,0:T(8,128)(2,1)} %bitcast.11), custom_call_target="tpu_custom_call" | custom-call | tf_op jit(solution)/shard_map/pack_columns/pallas_call | solution.py:488
  1.9 3.0 %collective-permute-start.1 = (bf16[2,128,512]{2,1,0:T(8,128)(2,1)S(1)}, bf16[2,128,512]{2,1,0:T(8,128)(2,1)S(1)}, u32[]{:S(2)}, u32[]{:S(2)}) collective-permute-start(bf16[2,128,512]{2,1,0:T(8,128)(2,1)S(1)} %get-tuple-element.75), channel_id=1, source_target_pairs={{0,16},{4,20},{8,24},{12,28},{16,0},{20,4},{24,8},{28,12},{1,17},{... | collective-permute-start | bytes 786440 | tf_op jit(solution)/shard_map/ppermute | solution.py:502
  4.9 1.5 %collective-permute-start.2 = (bf16[2,128,512]{2,1,0:T(8,128)(2,1)S(1)}, bf16[2,128,512]{2,1,0:T(8,128)(2,1)S(1)}, u32[]{:S(2)}, u32[]{:S(2)}) collective-permute-start(bf16[2,128,512]{2,1,0:T(8,128)(2,1)S(1)} %get-tuple-element.76), channel_id=1, source_target_pairs={{0,8},{4,12},{8,0},{12,4},{16,24},{20,28},{24,16},{28,20},{1,9},{5... | collective-permute-start | bytes 786440 | tf_op jit(solution)/shard_map/ppermute | solution.py:502
  6.4 0.0 collective-permute-start
  6.5 7.7 %row_heads.1 = (bf16[4,64,384]{2,1,0:T(8,128)(2,1)S(1)}, bf16[4,64,384]{2,1,0:T(8,128)(2,1)S(1)}, bf16[4,64,384]{2,1,0:T(8,128)(2,1)S(1)}, bf16[4,64,384]{2,1,0:...) custom-call(bf16[512,512]{1,0:T(8,128)(2,1)} %bitcast.10, ...), custom_call_target="tpu_custom_call" | custom-call | tf_op jit(solution)/shard_map/row_heads/pallas_call | solution.py:488
  14.1 0.1 collective-permute-start.3
  14.2 0.5 collective-permute-start.4
  14.7 0.9 %collective-permute-done.3.refs_2_ = bf16[4,64,384]{2,1,0:T(8,128)(2,1)S(1)} collective-permute-done((bf16[4,64,384]{2,1,0:T(8,128)(2,1)S(1)}, bf16[4,64,384]{2,1,0:T(8,128)(2,1)S(1)}, u32[]{:S(2)}, u32[]{:S(2)}) %collective-permute-start.3) | collective-permute-done | bytes 196640 | tf_op jit(solution)/shard_map/ppermute | solution.py:502
  15.6 0.3 collective-permute-done.4.refs_3_
  15.9 0.1 row_add_cores.1
  16.0 0.0 collective-permute-done.1.near_2
  16.0 0.0 collective-permute-done.2.near_3
  16.0 2.1 %collective-permute-done.near_1 = bf16[2,128,512]{2,1,0:T(8,128)(2,1)S(1)} collective-permute-done((bf16[2,128,512]{2,1,0:T(8,128)(2,1)S(1)}, bf16[2,128,512]{2,1,0:T(8,128)(2,1)S(1)}, u32[]{:S(2)}, u32[]{:S(2)}) %collective-permute-start) | collective-permute-done | bytes 262176 | tf_op jit(solution)/shard_map/ppermute | solution.py:502
  18.2 0.1 collective-permute-start.5
  18.2 2.7 %collective-permute-start.6 = (bf16[64,768]{1,0:T(8,128)(2,1)S(1)}, bf16[64,768]{1,0:T(8,128)(2,1)S(1)}, u32[]{:S(2)}, u32[]{:S(2)}) collective-permute-start(bf16[64,768]{1,0:T(8,128)(2,1)S(1)} %get-tuple-element.91), channel_id=1, source_target_pairs={{0,24},{4,28},{8,16},{12,20},{16,8},{20,12},{24,0},{28,4},{1,25},{... | collective-permute-start | bytes 294920 | tf_op jit(solution)/shard_map/ppermute | solution.py:502
  20.9 0.5 collective-permute-start.7
  21.4 0.4 collective-permute-start.8
  21.8 3.1 %column_heads.1 = (bf16[4,64,1280]{2,1,0:T(8,128)(2,1)S(1)}, bf16[4,64,1280]{2,1,0:T(8,128)(2,1)S(1)}, bf16[512,768]{1,0:T(8,128)(2,1)S(1)}) custom-call(bf16[512,512]{1,0:T(8,128)(2,1)S(1)} %get-tuple-element.73.x_ref, bf16[512,512]{1,0:T(8,128)(2,1)S(1)} %get-tuple-element.74.cot_ref, bf16[2,128,512]{2,1,0:T(8,128)(2,1)S(1)} %collective-permute-done.near_1, ...), custom_call_target="tpu_custom_call" | custom-call | tf_op jit(solution)/shard_map/column_heads/pallas_call | solution.py:488
  24.9 1.5 %collective-permute-done.7.got_2 = bf16[64,768]{1,0:T(8,128)(2,1)S(1)} collective-permute-done((bf16[64,768]{1,0:T(8,128)(2,1)S(1)}, bf16[64,768]{1,0:T(8,128)(2,1)S(1)}, u32[]{:S(2)}, u32[]{:S(2)}) %collective-permute-start.7) | collective-permute-done | bytes 98336 | tf_op jit(solution)/shard_map/ppermute | solution.py:502
  26.5 0.2 collective-permute-done.8.got_3
  26.7 0.6 %column_grad_hidden.1 = (bf16[4,64,512]{2,1,0:T(8,128)(2,1)S(1)}, bf16[4,64,512]{2,1,0:T(8,128)(2,1)S(1)}) custom-call(bf16[512,768]{1,0:T(8,128)(2,1)S(1)} %get-tuple-element.98.grads_ref, bf16[512,768]{1,0:T(8,128)(2,1)S(1)} %get-tuple-element.85.w_ref), custom_call_target="tpu_custom_call" | custom-call | tf_op jit(solution)/shard_map/column_grad_hidden/pallas_call | solution.py:488
  27.3 0.6 collective-permute-start.9
  27.8 0.1 row_add_chips.1
  27.9 0.9 %collective-permute-done.10.refs_1_ = bf16[4,64,1280]{2,1,0:T(8,128)(2,1)S(1)} collective-permute-done((bf16[4,64,1280]{2,1,0:T(8,128)(2,1)S(1)}, bf16[4,64,1280]{2,1,0:T(8,128)(2,1)S(1)}, u32[]{:S(2)}, u32[]{:S(2)}) %collective-permute-start.10) | collective-permute-done | bytes 655392 | tf_op jit(solution)/shard_map/ppermute | solution.py:502
  28.8 0.1 column_add_cores.1
  28.9 1.6 %collective-permute-start.12 = (bf16[64,1280]{1,0:T(8,128)(2,1)S(1)}, bf16[64,1280]{1,0:T(8,128)(2,1)S(1)}, u32[]{:S(2)}, u32[]{:S(2)}) collective-permute-start(bf16[64,1280]{1,0:T(8,128)(2,1)S(1)} %get-tuple-element.116), channel_id=1, source_target_pairs={{0,24},{4,28},{8,16},{12,20},{16,8},{20,12},{24,0},{28,4},{1,25},{... | collective-permute-start | bytes 491528 | tf_op jit(solution)/shard_map/ppermute | solution.py:502
  30.5 1.5 %collective-permute-start.13 = (bf16[64,1280]{1,0:T(8,128)(2,1)S(1)}, bf16[64,1280]{1,0:T(8,128)(2,1)S(1)}, u32[]{:S(2)}, u32[]{:S(2)}) collective-permute-start(bf16[64,1280]{1,0:T(8,128)(2,1)S(1)} %get-tuple-element.117), channel_id=1, source_target_pairs={{0,16},{4,20},{8,24},{12,28},{16,0},{20,4},{24,8},{28,12},{1,17},{... | collective-permute-start | bytes 491528 | tf_op jit(solution)/shard_map/ppermute | solution.py:502
  32.0 0.5 collective-permute-start.14
  32.5 1.6 %collective-permute-start.11 = (bf16[32,768]{1,0:T(8,128)(2,1)S(1)}, bf16[32,768]{1,0:T(8,128)(2,1)S(1)}, u32[]{:S(2)}, u32[]{:S(2)}) collective-permute-start(bf16[32,768]{1,0:T(8,128)(2,1)S(1)} %get-tuple-element.110), channel_id=1, source_target_pairs={{0,1},{1,0},{2,3},{3,2},{4,5},{5,4},{6,7},{7,6},{8,9},{9,8},{10,11... | collective-permute-start | bytes 147464 | tf_op jit(solution)/shard_map/ppermute | solution.py:502
  34.1 2.5 %collective-permute-done.11.row_got = bf16[32,768]{1,0:T(8,128)(2,1)S(1)} collective-permute-done((bf16[32,768]{1,0:T(8,128)(2,1)S(1)}, bf16[32,768]{1,0:T(8,128)(2,1)S(1)}, u32[]{:S(2)}, u32[]{:S(2)}) %collective-permute-start.11) | collective-permute-done | bytes 49184 | tf_op jit(solution)/shard_map/ppermute | solution.py:502
  36.5 0.4 collective-permute-done.12.got_1
  37.0 2.7 %collective-permute-done.13.got_2 = bf16[64,1280]{1,0:T(8,128)(2,1)S(1)} collective-permute-done((bf16[64,1280]{1,0:T(8,128)(2,1)S(1)}, bf16[64,1280]{1,0:T(8,128)(2,1)S(1)}, u32[]{:S(2)}, u32[]{:S(2)}) %collective-permute-start.13) | collective-permute-done | bytes 163872 | tf_op jit(solution)/shard_map/ppermute | solution.py:502
  39.6 0.0 collective-permute-done.14.got_3
  39.7 0.1 column_add_chips.1
  39.8 1.6 %collective-permute-start.15 = (bf16[32,1280]{1,0:T(8,128)(2,1)S(1)}, bf16[32,1280]{1,0:T(8,128)(2,1)S(1)}, u32[]{:S(2)}, u32[]{:S(2)}) collective-permute-start(bf16[32,1280]{1,0:T(8,128)(2,1)S(1)} %get-tuple-element.120), channel_id=1, source_target_pairs={{0,1},{1,0},{2,3},{3,2},{4,5},{5,4},{6,7},{7,6},{8,9},{9,8},{10,11... | collective-permute-start | bytes 245768 | tf_op jit(solution)/shard_map/ppermute | solution.py:502
  41.4 2.9 %collective-permute-done.15.got_ref = bf16[32,1280]{1,0:T(8,128)(2,1)S(1)} collective-permute-done((bf16[32,1280]{1,0:T(8,128)(2,1)S(1)}, bf16[32,1280]{1,0:T(8,128)(2,1)S(1)}, u32[]{:S(2)}, u32[]{:S(2)}) %collective-permute-start.15) | collective-permute-done | bytes 81952 | tf_op jit(solution)/shard_map/ppermute | solution.py:502
  44.3 2.7 %collective-permute-start.19 = (bf16[32,2048]{1,0:T(8,128)(2,1)S(1)}, bf16[32,2048]{1,0:T(8,128)(2,1)S(1)}, u32[]{:S(2)}, u32[]{:S(2)}) collective-permute-start(bf16[32,2048]{1,0:T(8,128)(2,1)S(1)} %add_pair.1.kept_ref), channel_id=1, source_target_pairs={{0,2},{1,3},{2,0},{3,1},{4,6},{5,7},{6,4},{7,5},{8,10},{9,11},{10,... | collective-permute-start | bytes 393224 | tf_op jit(solution)/shard_map/ppermute | solution.py:502
  47.0 1.7 %collective-permute-start.16 = (bf16[128,512]{1,0:T(8,128)(2,1)S(1)}, bf16[128,512]{1,0:T(8,128)(2,1)S(1)}, u32[]{:S(2)}, u32[]{:S(2)}) collective-permute-start(bf16[128,512]{1,0:T(8,128)(2,1)S(1)} %get-tuple-element.124), channel_id=1, source_target_pairs={{0,24},{4,28},{8,16},{12,20},{16,8},{20,12},{24,0},{28,4},{1,25},{... | collective-permute-start | bytes 393224 | tf_op jit(solution)/shard_map/ppermute | solution.py:502
  48.6 1.3 %collective-permute-start.17 = (bf16[128,512]{1,0:T(8,128)(2,1)S(1)}, bf16[128,512]{1,0:T(8,128)(2,1)S(1)}, u32[]{:S(2)}, u32[]{:S(2)}) collective-permute-start(bf16[128,512]{1,0:T(8,128)(2,1)S(1)} %get-tuple-element.125), channel_id=1, source_target_pairs={{0,16},{4,20},{8,24},{12,28},{16,0},{20,4},{24,8},{28,12},{1,17},{... | collective-permute-start | bytes 393224 | tf_op jit(solution)/shard_map/ppermute | solution.py:502
  49.9 0.5 collective-permute-start.18
  50.4 1.9 %collective-permute-done.19.got_ref = bf16[32,2048]{1,0:T(8,128)(2,1)S(1)} collective-permute-done((bf16[32,2048]{1,0:T(8,128)(2,1)S(1)}, bf16[32,2048]{1,0:T(8,128)(2,1)S(1)}, u32[]{:S(2)}, u32[]{:S(2)}) %collective-permute-start.19) | collective-permute-done | bytes 131104 | tf_op jit(solution)/shard_map/ppermute | solution.py:502
  52.3 0.7 %collective-permute-start.20 = (bf16[32,2048]{1,0:T(8,128)(2,1)S(1)}, bf16[32,2048]{1,0:T(8,128)(2,1)S(1)}, u32[]{:S(2)}, u32[]{:S(2)}) collective-permute-start(bf16[32,2048]{1,0:T(8,128)(2,1)S(1)} %add_pairs.1.held_ref), channel_id=1, source_target_pairs={{0,1},{1,0},{2,3},{3,2},{4,5},{5,4},{6,7},{7,6},{8,9},{9,8},{10,11... | collective-permute-start | bytes 393224 | tf_op jit(solution)/shard_map/ppermute | solution.py:502
  53.1 0.5 collective-permute-done.16.got_1
  53.6 1.1 %collective-permute-done.17.got_2 = bf16[128,512]{1,0:T(8,128)(2,1)S(1)} collective-permute-done((bf16[128,512]{1,0:T(8,128)(2,1)S(1)}, bf16[128,512]{1,0:T(8,128)(2,1)S(1)}, u32[]{:S(2)}, u32[]{:S(2)}) %collective-permute-start.17) | collective-permute-done | bytes 131104 | tf_op jit(solution)/shard_map/ppermute | solution.py:502
  54.6 0.3 collective-permute-done.18.got_3
  54.9 1.2 %input_grad.1 = bf16[512,512]{1,0:T(8,128)(2,1)} custom-call(f32[512,512]{1,0:T(8,128)S(1)} %get-tuple-element.70.base_ref, f32[512,512]{1,0:T(8,128)S(1)} %get-tuple-element.71.normed_ref, f32[512,1]{1,0:T(8,128)S(1)} %get-tuple-element.72.inverse_ref, f32[1,512]{1,0:T(1,128)S(1)} %bitcast.7, bf16[128,512]{1,0:T(8,128)(2,1)S(1)} %get-tuple-element.123.own_ref, ...), custom_call_target="tpu_custom_call" | custom-call | tf_op jit(solution)/shard_map/input_grad/pallas_call | solution.py:488
  56.1 1.3 %collective-permute-done.20.got_ref = bf16[32,2048]{1,0:T(8,128)(2,1)S(1)} collective-permute-done((bf16[32,2048]{1,0:T(8,128)(2,1)S(1)}, bf16[32,2048]{1,0:T(8,128)(2,1)S(1)}, u32[]{:S(2)}, u32[]{:S(2)}) %collective-permute-start.20) | collective-permute-done | bytes 131104 | tf_op jit(solution)/shard_map/ppermute | solution.py:502
  57.4 0.9 %result.1 = (f32[64,1536]{1,0:T(8,128)}, f32[64,512]{1,0:T(8,128)}, f32[1,64]{1,0:T(1,128)}) custom-call(bf16[32,2048]{1,0:T(8,128)(2,1)S(1)} %add_pairs.1.held_ref, bf16[32,2048]{1,0:T(8,128)(2,1)S(1)} %collective-permute-done.20.got_ref, bf16[64,1536]{1,0:T(8,128)(2,1)S(1)} %get-tuple-element.128.w_ref, f32[1,512]{1,0:T(1,128)S(1)} %bitcast.8), custom_call_target="tpu_custom_call" | custom-call | tf_op jit(solution)/shard_map/result/pallas_call | solution.py:488
  (10 shorter events, 0.2 us)
Async XLA Ops:
  1.9 14.1 %collective-permute-start.1 = (bf16[2,128,512]{2,1,0:T(8,128)(2,1)S(1)}, bf16[2,128,512]{2,1,0:T(8,128)(2,1)S(1)}, u32[]{:S(2)}, u32[]{:S(2)}) collective-permute-start(bf16[2,128,512]{2,1,0:T(8,128)(2,1)S(1)} %get-tuple-element.75), channel_id=1, source_target_pairs={{0,16},{4,20},{8,24},{12,28},{16,0},{20,4},{24,8},{28,12},{1,17},{... | collective-permute-start | bytes 786440 | tf_op jit(solution)/shard_map/ppermute | solution.py:502
  4.9 11.1 %collective-permute-start.2 = (bf16[2,128,512]{2,1,0:T(8,128)(2,1)S(1)}, bf16[2,128,512]{2,1,0:T(8,128)(2,1)S(1)}, u32[]{:S(2)}, u32[]{:S(2)}) collective-permute-start(bf16[2,128,512]{2,1,0:T(8,128)(2,1)S(1)} %get-tuple-element.76), channel_id=1, source_target_pairs={{0,8},{4,12},{8,0},{12,4},{16,24},{20,28},{24,16},{28,20},{1,9},{5... | collective-permute-start | bytes 786440 | tf_op jit(solution)/shard_map/ppermute | solution.py:502
  6.4 11.7 %collective-permute-start = (bf16[2,128,512]{2,1,0:T(8,128)(2,1)S(1)}, bf16[2,128,512]{2,1,0:T(8,128)(2,1)S(1)}, u32[]{:S(2)}, u32[]{:S(2)}) collective-permute-start(bf16[2,128,512]{2,1,0:T(8,128)(2,1)S(1)} %get-tuple-element.68), channel_id=1, source_target_pairs={{0,24},{4,28},{8,16},{12,20},{16,8},{20,12},{24,0},{28,4},{1,25},{... | collective-permute-start | bytes 786440 | tf_op jit(solution)/shard_map/ppermute | solution.py:502
  14.1 1.5 %collective-permute-start.3 = (bf16[4,64,384]{2,1,0:T(8,128)(2,1)S(1)}, bf16[4,64,384]{2,1,0:T(8,128)(2,1)S(1)}, u32[]{:S(2)}, u32[]{:S(2)}) collective-permute-start(bf16[4,64,384]{2,1,0:T(8,128)(2,1)S(1)} %get-tuple-element.79), channel_id=1, source_target_pairs={{0,4},{4,0},{8,12},{12,8},{16,20},{20,16},{24,28},{28,24},{1,5},{5... | collective-permute-start | bytes 589832 | tf_op jit(solution)/shard_map/ppermute | solution.py:502
  14.2 1.7 %collective-permute-start.4 = (bf16[4,64,384]{2,1,0:T(8,128)(2,1)S(1)}, bf16[4,64,384]{2,1,0:T(8,128)(2,1)S(1)}, u32[]{:S(2)}, u32[]{:S(2)}) collective-permute-start(bf16[4,64,384]{2,1,0:T(8,128)(2,1)S(1)} %get-tuple-element.80), channel_id=1, source_target_pairs={{0,4},{4,0},{8,12},{12,8},{16,20},{20,16},{24,28},{28,24},{1,5},{5... | collective-permute-start | bytes 589832 | tf_op jit(solution)/shard_map/ppermute | solution.py:502
  15.9 5.9 %copy-start = (f32[512]{0:T(512)S(1)}, f32[512]{0:T(512)}, u32[]{:S(2)}) copy-start(f32[512]{0:T(512)} %param.6) | copy-start | bytes 6148
  18.2 3.6 %collective-permute-start.5 = (bf16[4,2,64,512]{3,2,1,0:T(8,128)(2,1)S(1)}, bf16[4,2,64,512]{3,2,1,0:T(8,128)(2,1)S(1)}, u32[]{:S(2)}, u32[]{:S(2)}) collective-permute-start(bf16[4,2,64,512]{3,2,1,0:T(8,128)(2,1)S(1)} %pack_other_core.1), channel_id=1, source_target_pairs={{0,4},{4,0},{8,12},{12,8},{16,20},{20,16},{24,28},{28,24},{1,5},{5... | collective-permute-start | bytes 1572872 | tf_op jit(solution)/shard_map/ppermute | solution.py:502
  18.2 6.7 %collective-permute-start.6 = (bf16[64,768]{1,0:T(8,128)(2,1)S(1)}, bf16[64,768]{1,0:T(8,128)(2,1)S(1)}, u32[]{:S(2)}, u32[]{:S(2)}) collective-permute-start(bf16[64,768]{1,0:T(8,128)(2,1)S(1)} %get-tuple-element.91), channel_id=1, source_target_pairs={{0,24},{4,28},{8,16},{12,20},{16,8},{20,12},{24,0},{28,4},{1,25},{... | collective-permute-start | bytes 294920 | tf_op jit(solution)/shard_map/ppermute | solution.py:502
  20.9 5.6 %collective-permute-start.7 = (bf16[64,768]{1,0:T(8,128)(2,1)S(1)}, bf16[64,768]{1,0:T(8,128)(2,1)S(1)}, u32[]{:S(2)}, u32[]{:S(2)}) collective-permute-start(bf16[64,768]{1,0:T(8,128)(2,1)S(1)} %get-tuple-element.92), channel_id=1, source_target_pairs={{0,16},{4,20},{8,24},{12,28},{16,0},{20,4},{24,8},{28,12},{1,17},{... | collective-permute-start | bytes 294920 | tf_op jit(solution)/shard_map/ppermute | solution.py:502
  21.4 5.3 %collective-permute-start.8 = (bf16[64,768]{1,0:T(8,128)(2,1)S(1)}, bf16[64,768]{1,0:T(8,128)(2,1)S(1)}, u32[]{:S(2)}, u32[]{:S(2)}) collective-permute-start(bf16[64,768]{1,0:T(8,128)(2,1)S(1)} %get-tuple-element.93), channel_id=1, source_target_pairs={{0,8},{4,12},{8,0},{12,4},{16,24},{20,28},{24,16},{28,20},{1,9},{5... | collective-permute-start | bytes 294920 | tf_op jit(solution)/shard_map/ppermute | solution.py:502
  26.7 2.1 %collective-permute-start.10 = (bf16[4,64,1280]{2,1,0:T(8,128)(2,1)S(1)}, bf16[4,64,1280]{2,1,0:T(8,128)(2,1)S(1)}, u32[]{:S(2)}, u32[]{:S(2)}) collective-permute-start(bf16[4,64,1280]{2,1,0:T(8,128)(2,1)S(1)} %get-tuple-element.107), channel_id=1, source_target_pairs={{0,4},{4,0},{8,12},{12,8},{16,20},{20,16},{24,28},{28,24},{1,5},{5... | collective-permute-start | bytes 1966088 | tf_op jit(solution)/shard_map/ppermute | solution.py:502
  27.3 6.8 %collective-permute-start.9 = (bf16[4,64,512]{2,1,0:T(8,128)(2,1)S(1)}, bf16[4,64,512]{2,1,0:T(8,128)(2,1)S(1)}, u32[]{:S(2)}, u32[]{:S(2)}) collective-permute-start(bf16[4,64,512]{2,1,0:T(8,128)(2,1)S(1)} %get-tuple-element.101), channel_id=1, source_target_pairs={{0,4},{4,0},{8,12},{12,8},{16,20},{20,16},{24,28},{28,24},{1,5},{5... | collective-permute-start | bytes 786440 | tf_op jit(solution)/shard_map/ppermute | solution.py:502
  28.9 8.1 %collective-permute-start.12 = (bf16[64,1280]{1,0:T(8,128)(2,1)S(1)}, bf16[64,1280]{1,0:T(8,128)(2,1)S(1)}, u32[]{:S(2)}, u32[]{:S(2)}) collective-permute-start(bf16[64,1280]{1,0:T(8,128)(2,1)S(1)} %get-tuple-element.116), channel_id=1, source_target_pairs={{0,24},{4,28},{8,16},{12,20},{16,8},{20,12},{24,0},{28,4},{1,25},{... | collective-permute-start | bytes 491528 | tf_op jit(solution)/shard_map/ppermute | solution.py:502
  30.5 9.1 %collective-permute-start.13 = (bf16[64,1280]{1,0:T(8,128)(2,1)S(1)}, bf16[64,1280]{1,0:T(8,128)(2,1)S(1)}, u32[]{:S(2)}, u32[]{:S(2)}) collective-permute-start(bf16[64,1280]{1,0:T(8,128)(2,1)S(1)} %get-tuple-element.117), channel_id=1, source_target_pairs={{0,16},{4,20},{8,24},{12,28},{16,0},{20,4},{24,8},{28,12},{1,17},{... | collective-permute-start | bytes 491528 | tf_op jit(solution)/shard_map/ppermute | solution.py:502
  32.0 7.7 %collective-permute-start.14 = (bf16[64,1280]{1,0:T(8,128)(2,1)S(1)}, bf16[64,1280]{1,0:T(8,128)(2,1)S(1)}, u32[]{:S(2)}, u32[]{:S(2)}) collective-permute-start(bf16[64,1280]{1,0:T(8,128)(2,1)S(1)} %get-tuple-element.118), channel_id=1, source_target_pairs={{0,8},{4,12},{8,0},{12,4},{16,24},{20,28},{24,16},{28,20},{1,9},{5... | collective-permute-start | bytes 491528 | tf_op jit(solution)/shard_map/ppermute | solution.py:502
  32.5 4.1 %collective-permute-start.11 = (bf16[32,768]{1,0:T(8,128)(2,1)S(1)}, bf16[32,768]{1,0:T(8,128)(2,1)S(1)}, u32[]{:S(2)}, u32[]{:S(2)}) collective-permute-start(bf16[32,768]{1,0:T(8,128)(2,1)S(1)} %get-tuple-element.110), channel_id=1, source_target_pairs={{0,1},{1,0},{2,3},{3,2},{4,5},{5,4},{6,7},{7,6},{8,9},{9,8},{10,11... | collective-permute-start | bytes 147464 | tf_op jit(solution)/shard_map/ppermute | solution.py:502
  39.8 4.5 %collective-permute-start.15 = (bf16[32,1280]{1,0:T(8,128)(2,1)S(1)}, bf16[32,1280]{1,0:T(8,128)(2,1)S(1)}, u32[]{:S(2)}, u32[]{:S(2)}) collective-permute-start(bf16[32,1280]{1,0:T(8,128)(2,1)S(1)} %get-tuple-element.120), channel_id=1, source_target_pairs={{0,1},{1,0},{2,3},{3,2},{4,5},{5,4},{6,7},{7,6},{8,9},{9,8},{10,11... | collective-permute-start | bytes 245768 | tf_op jit(solution)/shard_map/ppermute | solution.py:502
  44.3 8.0 %collective-permute-start.19 = (bf16[32,2048]{1,0:T(8,128)(2,1)S(1)}, bf16[32,2048]{1,0:T(8,128)(2,1)S(1)}, u32[]{:S(2)}, u32[]{:S(2)}) collective-permute-start(bf16[32,2048]{1,0:T(8,128)(2,1)S(1)} %add_pair.1.kept_ref), channel_id=1, source_target_pairs={{0,2},{1,3},{2,0},{3,1},{4,6},{5,7},{6,4},{7,5},{8,10},{9,11},{10,... | collective-permute-start | bytes 393224 | tf_op jit(solution)/shard_map/ppermute | solution.py:502
  47.0 6.6 %collective-permute-start.16 = (bf16[128,512]{1,0:T(8,128)(2,1)S(1)}, bf16[128,512]{1,0:T(8,128)(2,1)S(1)}, u32[]{:S(2)}, u32[]{:S(2)}) collective-permute-start(bf16[128,512]{1,0:T(8,128)(2,1)S(1)} %get-tuple-element.124), channel_id=1, source_target_pairs={{0,24},{4,28},{8,16},{12,20},{16,8},{20,12},{24,0},{28,4},{1,25},{... | collective-permute-start | bytes 393224 | tf_op jit(solution)/shard_map/ppermute | solution.py:502
  48.6 6.0 %collective-permute-start.17 = (bf16[128,512]{1,0:T(8,128)(2,1)S(1)}, bf16[128,512]{1,0:T(8,128)(2,1)S(1)}, u32[]{:S(2)}, u32[]{:S(2)}) collective-permute-start(bf16[128,512]{1,0:T(8,128)(2,1)S(1)} %get-tuple-element.125), channel_id=1, source_target_pairs={{0,16},{4,20},{8,24},{12,28},{16,0},{20,4},{24,8},{28,12},{1,17},{... | collective-permute-start | bytes 393224 | tf_op jit(solution)/shard_map/ppermute | solution.py:502
  49.9 5.0 %collective-permute-start.18 = (bf16[128,512]{1,0:T(8,128)(2,1)S(1)}, bf16[128,512]{1,0:T(8,128)(2,1)S(1)}, u32[]{:S(2)}, u32[]{:S(2)}) collective-permute-start(bf16[128,512]{1,0:T(8,128)(2,1)S(1)} %get-tuple-element.126), channel_id=1, source_target_pairs={{0,8},{4,12},{8,0},{12,4},{16,24},{20,28},{24,16},{28,20},{1,9},{5... | collective-permute-start | bytes 393224 | tf_op jit(solution)/shard_map/ppermute | solution.py:502
  52.3 5.0 %collective-permute-start.20 = (bf16[32,2048]{1,0:T(8,128)(2,1)S(1)}, bf16[32,2048]{1,0:T(8,128)(2,1)S(1)}, u32[]{:S(2)}, u32[]{:S(2)}) collective-permute-start(bf16[32,2048]{1,0:T(8,128)(2,1)S(1)} %add_pairs.1.held_ref), channel_id=1, source_target_pairs={{0,1},{1,0},{2,3},{3,2},{4,5},{5,4},{6,7},{7,6},{8,9},{9,8},{10,11... | collective-permute-start | bytes 393224 | tf_op jit(solution)/shard_map/ppermute | solution.py:502

commit v10 on v9

--- a/solution.py
+++ b/solution.py
@@ -21,6 +21,7 @@
 VMEM = pl.BlockSpec(memory_space=pltpu.VMEM)
 HBM = pl.BlockSpec(memory_space=pltpu.HBM)
 CHIP_STEPS = (3, 2, 1)
+FIRST_PART = 640
 PINNED = pl.BlockSpec(memory_space=pltpu.VMEM)
 shaped = jax.ShapeDtypeStruct
 
@@ -415,34 +416,57 @@
     finished(*started(*copies))
 
 
-def chip_sum_kernel(*refs):
-    chip = here()[0]
-    pieces, targets = refs[:-4], refs[-4:]
-    count = len(pieces) // 2
+def split_rows(total, axis, send_ref, kept_ref):
+    upper = (here()[2] & 1) == 1
+    low, high = jnp.split(total, 2, axis)
+    send_ref[...] = jnp.where(upper, low, high).astype(BF16)
+    kept_ref[...] = jnp.where(upper, high, low)
+
+
+def row_cores_kernel(keep_1, keep_2, got_1, got_2, send_ref, kept_ref):
+    total = [
+        keep_ref[...].astype(F32) + got_ref[...].astype(F32)
+        for keep_ref, got_ref in ((keep_1, got_1), (keep_2, got_2))
+    ]
+    split_rows(jnp.concatenate(total, 2), 1, send_ref, kept_ref)
+
+
+def cores_kernel(keep_ref, got_ref, send_ref, kept_ref, *targets):
+    chip, cut = here()[0], kept_ref.shape[2]
+    first = keep_ref[:, :, :cut].astype(F32) + got_ref[:, :, :cut].astype(F32)
+    split_rows(first, 1, send_ref, kept_ref)
     for step, target in zip((0, *CHIP_STEPS), targets):
-        there, at = chip ^ step, 0
-        for kept_ref, got_ref in zip(pieces[:count], pieces[count:]):
-            to = slice(at, at + kept_ref.shape[2])
-            total = kept_ref[there].astype(F32) + got_ref[there].astype(F32)
-            target[:, to] = total.astype(target.dtype)
-            at = to.stop
-
-
-def layer_sum_kernel(own_ref, got_1, got_2, got_3, send_ref, keep_ref):
-    upper = (here()[2] & 1) == 1
-    total = own_ref[...] + (
+        there = chip ^ step
+        total = keep_ref[there, :, cut:].astype(F32) + got_ref[there, :, cut:].astype(F32)
+        target[...] = total.astype(target.dtype)
+
+
+def pair_kernel(kept_ref, got_ref, row_kept, row_got, *targets):
+    chip, cut = here()[0], kept_ref.shape[2]
+    for step, target in zip((0, *CHIP_STEPS), targets):
+        there = chip ^ step
+        total = kept_ref[there] + got_ref[there].astype(F32)
+        target[:, :cut] = total.astype(target.dtype)
+        total = row_kept[there] + row_got[there].astype(F32)
+        target[:, cut:] = total.astype(target.dtype)
+
+
+def layer_sum(own_ref, got_1, got_2, got_3):
+    return own_ref[...] + (
         (got_1[...].astype(F32) + got_2[...].astype(F32)) + got_3[...].astype(F32)
     )
-    half = total.shape[0] // 2
-    low, high = total[:half], total[half:]
-    send_ref[...] = jnp.where(upper, low, high).astype(BF16)
-    keep_ref[...] = jnp.where(upper, high, low)
-
-
-def join_kernel(kept_ref, got_ref, row_kept, row_got, out_ref):
-    cut = kept_ref.shape[1]
-    out_ref[:, :cut] = (kept_ref[...] + got_ref[...].astype(F32)).astype(BF16)
-    out_ref[:, cut:] = (row_kept[...] + row_got[...].astype(F32)).astype(BF16)
+
+
+def layer_kernel(own_ref, got_1, got_2, got_3, send_ref, kept_ref):
+    split_rows(layer_sum(own_ref, got_1, got_2, got_3), 0, send_ref, kept_ref)
+
+
+def join_kernel(own_ref, got_1, got_2, got_3, kept_ref, got_ref, out_ref):
+    total = layer_sum(own_ref, got_1, got_2, got_3).astype(BF16)
+    cut, width = FIRST_PART, kept_ref.shape[1]
+    out_ref[:, :cut] = total[:, :cut]
+    out_ref[:, cut : cut + width] = (kept_ref[...] + got_ref[...].astype(F32)).astype(BF16)
+    out_ref[:, cut + width :] = total[:, cut:]
 
 
 def add_kernel(kept_ref, got_ref, out_ref):
@@ -500,28 +524,6 @@
 def swap(array, axis, bits):
     count = lax.axis_size(axis)
     return lax.ppermute(array, axis, [(i, i ^ bits) for i in range(count)])
-
-
-def add_cores(keep, got, name):
-    rows, wide = keep[0].shape[1], sum(one.shape[2] for one in keep)
-    return call(
-        chip_sum_kernel,
-        name + "_add_cores",
-        [(VMEM, one) for one in (*keep, *got)],
-        [((rows, wide), F32)] + [((rows, wide), BF16)] * 3,
-        out_specs=[PINNED, VMEM, VMEM, VMEM],
-    )
-
-
-def add_chips(owned, got, name):
-    half, wide = owned.shape[0] // 2, owned.shape[1]
-    return call(
-        layer_sum_kernel,
-        name + "_add_chips",
-        [(VMEM, one) for one in (owned, *got)],
-        [((half, wide), BF16), ((half, wide), F32)],
-        out_specs=[VMEM, PINNED],
-    )
 
 
 def cross_chips(*offs):
@@ -603,15 +605,22 @@
     if layered:
         *row_terms, weight_rows, col_weight, col_out_weight = row_terms
         row_sent = [swap(one, "seq", 1) for one in row_terms[:2]]
-        row_owned, *row_off = add_cores(row_terms[2:], row_sent, "row")
-        *near, row_owned = lax.optimization_barrier((*near, row_owned))
+        half_block = (chips, row_share // 2, row_width)
+        row_next, row_kept = call(
+            row_cores_kernel,
+            "row_add_cores",
+            [(VMEM, one) for one in (*row_terms[2:], *row_sent)],
+            [(half_block, BF16), (half_block, F32)],
+            out_specs=[VMEM, PINNED],
+        )
+        *near, row_kept = lax.optimization_barrier((*near, row_kept))
         (far,) = call(
             far_kernel,
             "pack_other_core",
             [(VMEM, one) for one in (x_near, cot_near, *near)],
             [((chips, 2, share, width), BF16)],
         )
-        row_got = cross_chips(*row_off)
+        row_got = swap(row_next, "dp", 1)
         send, keep, col_grads = call(
             column_chip_kernel,
             "column_heads",
@@ -626,34 +635,51 @@
             vmem=BIG_VMEM,
             out_specs=[VMEM, VMEM, PINNED],
         )
-        send, *row_got = lax.optimization_barrier((send, *row_got))
-        row_next, row_kept = add_chips(row_owned, row_got, "row")
         back_send, back_keep = call(
             back_chip_kernel,
             "column_grad_hidden",
             [(VMEM, col_grads), (VMEM, col_weight)],
             [((chips, share, width), BF16)] * 2,
         )
-        keep, row_kept, back_keep = lax.optimization_barrier((keep, row_kept, back_keep))
-        owned, *off = add_cores([keep], [swap(send, "seq", 1)], "column")
-        got = cross_chips(*off)
+        send, row_got, back_keep = lax.optimization_barrier((send, row_got, back_keep))
+        first_half = (chips, row_share // 2, FIRST_PART)
+        second = (row_share, col_width - FIRST_PART)
+        to_next, kept, *parts = call(
+            cores_kernel,
+            "column_add_cores",
+            [(VMEM, keep), (VMEM, swap(send, "seq", 1))],
+            [(first_half, BF16), (first_half, F32), (second, F32)] + [(second, BF16)] * 3,
+            out_specs=[VMEM, PINNED, PINNED, VMEM, VMEM, VMEM],
+        )
+        layer_got = cross_chips(*parts[1:])
         back = call(
             back_pack_kernel,
             "pack_grad_hidden",
             [(VMEM, back_keep), (VMEM, swap(back_send, "seq", 1))],
             [((2 * share, width), BF16)] * 4,
         )
-        row_next, _ = lax.optimization_barrier((row_next, owned))
-        row_next = swap(row_next, "dp", 1)
-        *back, owned, row_next = lax.optimization_barrier((*back, owned, row_next))
-        to_next, kept = add_chips(owned, got, "column")
+        row_kept, *back = lax.optimization_barrier((row_kept, *back))
+        joint = (row_share // 2, FIRST_PART + row_width)
+        owned, *off = call(
+            pair_kernel,
+            "first_add_pair",
+            [(VMEM, one) for one in (kept, swap(to_next, "dp", 1), row_kept, row_got)],
+            [(joint, F32)] + [(joint, BF16)] * 3,
+            out_specs=[PINNED, VMEM, VMEM, VMEM],
+        )
+        got = cross_chips(*off)
+        half_second = (row_share // 2, second[1])
+        to_next, kept = call(
+            layer_kernel,
+            "second_add_chips",
+            [(VMEM, one) for one in (parts[0], *layer_got)],
+            [(half_second, BF16), (half_second, F32)],
+            out_specs=[VMEM, PINNED],
+        )
         (pair_sum,) = call(
             join_kernel,
-            "add_pair",
-            [
-                (VMEM, kept), (VMEM, swap(to_next, "dp", 1)),
-                (VMEM, row_kept), (VMEM, row_next),
-            ],
+            "join_terms",
+            [(VMEM, one) for one in (owned, *got, kept, swap(to_next, "dp", 1))],
             [((row_share // 2, col_width + row_width), BF16)],
         )
         *back, pair_sum = lax.optimization_barrier((*back, pair_sum))

time: 58.4 us -> 56.5 us (0.967)
  waiting for transfers between devices: 19.3 us -> 15.8 us
  starting transfers between devices: 23 us -> 24.5 us
    ppermute x21 -> x22, waiting for transfers between devices: 19.3 us -> 15.8 us  [swap(): return lax.ppermute(array, axis, [(i, i ^ bits) for i in range(count)])]
    ppermute x21 -> x22, starting transfers between devices: 23 us -> 24.5 us  [swap(): return lax.ppermute(array, axis, [(i, i ^ bits) for i in range(count)])]
  transfers between devices with their start and end apart: 21 -> 22, of which waited for: 15 -> 12; matrix products, arithmetic and copies ran while one was open for 0% -> 0% of each run, Pallas kernels for 22% -> 23%
where the time goes in v10:
time: 56.5 us; the launch traced here: 56.4 us
  starting transfers between devices  24.5 us (43%)
  waiting for transfers between devices  15.8 us (28%)
  Pallas kernels  15.3 us (27%)
  between operations  0.76 us (1%)
    ppermute x22, starting transfers between devices, swap(): return lax.ppermute(array, axis, [(i, i ^ bits) for i in range(count)])  24.5 us
    ppermute x22, waiting for transfers between devices, swap(): return lax.ppermute(array, axis, [(i, i ^ bits) for i in range(count)])  15.8 us
    pallas_call x14, Pallas kernels, call(): pl.pallas_call(kernel, out_shape=outs, in_specs=[spec for spec, _ in ins]...  15.3 us
  transfers between devices with their start and end apart: 22, of which 12 were waited for; matrix products, arithmetic and copies ran while one was open for 0% of the time, Pallas kernels for 23%

profile of v10, /device:TPU:0, one launch (start us, length us, event | category | flops | bytes accessed | tf_op | source)
XLA Modules:
  0.0 56.4 jit_solution(10104249968294480205)
XLA Ops:
  0.6 1.3 %pack_columns.1 = (bf16[2,128,512]{2,1,0:T(8,128)(2,1)S(1)}, bf16[2,128,512]{2,1,0:T(8,128)(2,1)S(1)}, bf16[2,128,512]{2,1,0:T(8,128)(2,1)S(1)}) custom-call(bf16[512,512]{1,0:T(8,128)(2,1)} %bitcast.9, bf16[512,512]{1,0:T(8,128)(2,1)} %bitcast.11), custom_call_target="tpu_custom_call" | custom-call | tf_op jit(solution)/shard_map/pack_columns/pallas_call | solution.py:512
  1.9 3.0 %collective-permute-start.1 = (bf16[2,128,512]{2,1,0:T(8,128)(2,1)S(1)}, bf16[2,128,512]{2,1,0:T(8,128)(2,1)S(1)}, u32[]{:S(2)}, u32[]{:S(2)}) collective-permute-start(bf16[2,128,512]{2,1,0:T(8,128)(2,1)S(1)} %get-tuple-element.69), channel_id=1, source_target_pairs={{0,16},{4,20},{8,24},{12,28},{16,0},{20,4},{24,8},{28,12},{1,17},{... | collective-permute-start | bytes 786440 | tf_op jit(solution)/shard_map/ppermute | solution.py:526
  4.9 1.5 %collective-permute-start.2 = (bf16[2,128,512]{2,1,0:T(8,128)(2,1)S(1)}, bf16[2,128,512]{2,1,0:T(8,128)(2,1)S(1)}, u32[]{:S(2)}, u32[]{:S(2)}) collective-permute-start(bf16[2,128,512]{2,1,0:T(8,128)(2,1)S(1)} %get-tuple-element.70), channel_id=1, source_target_pairs={{0,8},{4,12},{8,0},{12,4},{16,24},{20,28},{24,16},{28,20},{1,9},{5... | collective-permute-start | bytes 786440 | tf_op jit(solution)/shard_map/ppermute | solution.py:526
  6.4 0.0 collective-permute-start
  6.5 7.7 %row_heads.1 = (bf16[4,64,384]{2,1,0:T(8,128)(2,1)S(1)}, bf16[4,64,384]{2,1,0:T(8,128)(2,1)S(1)}, bf16[4,64,384]{2,1,0:T(8,128)(2,1)S(1)}, bf16[4,64,384]{2,1,0:...) custom-call(bf16[512,512]{1,0:T(8,128)(2,1)} %bitcast.10, ...), custom_call_target="tpu_custom_call" | custom-call | tf_op jit(solution)/shard_map/row_heads/pallas_call | solution.py:512
  14.1 0.1 collective-permute-start.3
  14.2 0.5 collective-permute-start.4
  14.7 0.9 %collective-permute-done.3.got_1 = bf16[4,64,384]{2,1,0:T(8,128)(2,1)S(1)} collective-permute-done((bf16[4,64,384]{2,1,0:T(8,128)(2,1)S(1)}, bf16[4,64,384]{2,1,0:T(8,128)(2,1)S(1)}, u32[]{:S(2)}, u32[]{:S(2)}) %collective-permute-start.3) | collective-permute-done | bytes 196640 | tf_op jit(solution)/shard_map/ppermute | solution.py:526
  15.6 0.3 collective-permute-done.4.got_2
  15.9 0.1 row_add_cores.1
  16.1 0.0 collective-permute-done.1.near_2
  16.1 2.0 %collective-permute-done.near_1 = bf16[2,128,512]{2,1,0:T(8,128)(2,1)S(1)} collective-permute-done((bf16[2,128,512]{2,1,0:T(8,128)(2,1)S(1)}, bf16[2,128,512]{2,1,0:T(8,128)(2,1)S(1)}, u32[]{:S(2)}, u32[]{:S(2)}) %collective-permute-start) | collective-permute-done | bytes 262176 | tf_op jit(solution)/shard_map/ppermute | solution.py:526
  18.2 0.1 collective-permute-start.5
  18.2 1.8 %collective-permute-start.6 = (bf16[4,32,768]{2,1,0:T(8,128)(2,1)S(1)}, bf16[4,32,768]{2,1,0:T(8,128)(2,1)S(1)}, u32[]{:S(2)}, u32[]{:S(2)}) collective-permute-start(bf16[4,32,768]{2,1,0:T(8,128)(2,1)S(1)} %get-tuple-element.86), channel_id=1, source_target_pairs={{0,1},{1,0},{2,3},{3,2},{4,5},{5,4},{6,7},{7,6},{8,9},{9,8},{10,11... | collective-permute-start | bytes 589832 | tf_op jit(solution)/shard_map/ppermute | solution.py:526
  20.0 0.1 collective-permute-done.5.far_ref
  20.1 3.1 %column_heads.1 = (bf16[4,64,1280]{2,1,0:T(8,128)(2,1)S(1)}, bf16[4,64,1280]{2,1,0:T(8,128)(2,1)S(1)}, bf16[512,768]{1,0:T(8,128)(2,1)S(1)}) custom-call(bf16[512,512]{1,0:T(8,128)(2,1)S(1)} %get-tuple-element.77.x_ref, bf16[512,512]{1,0:T(8,128)(2,1)S(1)} %get-tuple-element.78.cot_ref, bf16[2,128,512]{2,1,0:T(8,128)(2,1)S(1)} %collective-permute-done.near_1, ...), custom_call_target="tpu_custom_call" | custom-call | tf_op jit(solution)/shard_map/column_heads/pallas_call | solution.py:512
  23.2 0.6 %column_grad_hidden.1 = (bf16[4,64,512]{2,1,0:T(8,128)(2,1)S(1)}, bf16[4,64,512]{2,1,0:T(8,128)(2,1)S(1)}) custom-call(bf16[512,768]{1,0:T(8,128)(2,1)S(1)} %get-tuple-element.87.grads_ref, bf16[512,768]{1,0:T(8,128)(2,1)S(1)} %get-tuple-element.82.w_ref), custom_call_target="tpu_custom_call" | custom-call | tf_op jit(solution)/shard_map/column_grad_hidden/pallas_call | solution.py:512
  23.8 1.7 %collective-permute-done.6.row_got = bf16[4,32,768]{2,1,0:T(8,128)(2,1)S(1)} collective-permute-done((bf16[4,32,768]{2,1,0:T(8,128)(2,1)S(1)}, bf16[4,32,768]{2,1,0:T(8,128)(2,1)S(1)}, u32[]{:S(2)}, u32[]{:S(2)}) %collective-permute-start.6) | collective-permute-done | bytes 196640 | tf_op jit(solution)/shard_map/ppermute | solution.py:526
  25.6 0.5 collective-permute-start.7
  26.1 1.6 %collective-permute-done.8.got_ref = bf16[4,64,1280]{2,1,0:T(8,128)(2,1)S(1)} collective-permute-done((bf16[4,64,1280]{2,1,0:T(8,128)(2,1)S(1)}, bf16[4,64,1280]{2,1,0:T(8,128)(2,1)S(1)}, u32[]{:S(2)}, u32[]{:S(2)}) %collective-permute-start.8) | collective-permute-done | bytes 655392 | tf_op jit(solution)/shard_map/ppermute | solution.py:526
  27.7 0.2 column_add_cores.1
  27.9 1.8 %collective-permute-start.9 = (bf16[4,32,640]{2,1,0:T(8,128)(2,1)S(1)}, bf16[4,32,640]{2,1,0:T(8,128)(2,1)S(1)}, u32[]{:S(2)}, u32[]{:S(2)}) collective-permute-start(bf16[4,32,640]{2,1,0:T(8,128)(2,1)S(1)} %get-tuple-element.102), channel_id=1, source_target_pairs={{0,1},{1,0},{2,3},{3,2},{4,5},{5,4},{6,7},{7,6},{8,9},{9,8},{10,11... | collective-permute-start | bytes 491528 | tf_op jit(solution)/shard_map/ppermute | solution.py:526
  29.6 2.4 %collective-permute-start.13 = (bf16[64,640]{1,0:T(8,128)(2,1)S(1)}, bf16[64,640]{1,0:T(8,128)(2,1)S(1)}, u32[]{:S(2)}, u32[]{:S(2)}) collective-permute-start(bf16[64,640]{1,0:T(8,128)(2,1)S(1)} %get-tuple-element.110), channel_id=1, source_target_pairs={{0,24},{4,28},{8,16},{12,20},{16,8},{20,12},{24,0},{28,4},{1,25},{... | collective-permute-start | bytes 245768 | tf_op jit(solution)/shard_map/ppermute | solution.py:526
  32.1 0.5 collective-permute-start.14
  32.6 0.5 collective-permute-start.15
  33.2 1.0 %collective-permute-done.9.got_ref = bf16[4,32,640]{2,1,0:T(8,128)(2,1)S(1)} collective-permute-done((bf16[4,32,640]{2,1,0:T(8,128)(2,1)S(1)}, bf16[4,32,640]{2,1,0:T(8,128)(2,1)S(1)}, u32[]{:S(2)}, u32[]{:S(2)}) %collective-permute-start.9) | collective-permute-done | bytes 163872 | tf_op jit(solution)/shard_map/ppermute | solution.py:526
  34.2 0.1 first_add_pair.1
  34.2 2.7 %collective-permute-start.10 = (bf16[32,1408]{1,0:T(8,128)(2,1)S(1)}, bf16[32,1408]{1,0:T(8,128)(2,1)S(1)}, u32[]{:S(2)}, u32[]{:S(2)}) collective-permute-start(bf16[32,1408]{1,0:T(8,128)(2,1)S(1)} %get-tuple-element.106), channel_id=1, source_target_pairs={{0,24},{4,28},{8,16},{12,20},{16,8},{20,12},{24,0},{28,4},{1,25},{... | collective-permute-start | bytes 270344 | tf_op jit(solution)/shard_map/ppermute | solution.py:526
  36.9 0.5 collective-permute-start.11
  37.4 0.4 collective-permute-start.12
  37.8 0.0 collective-permute-done.14.got_2
  37.8 0.0 collective-permute-done.15.got_3
  37.8 1.8 %collective-permute-start.16 = (bf16[32,640]{1,0:T(8,128)(2,1)S(1)}, bf16[32,640]{1,0:T(8,128)(2,1)S(1)}, u32[]{:S(2)}, u32[]{:S(2)}) collective-permute-start(bf16[32,640]{1,0:T(8,128)(2,1)S(1)} %get-tuple-element.114), channel_id=1, source_target_pairs={{0,1},{1,0},{2,3},{3,2},{4,5},{5,4},{6,7},{7,6},{8,9},{9,8},{10,11... | collective-permute-start | bytes 122888 | tf_op jit(solution)/shard_map/ppermute | solution.py:526
  39.6 2.3 %collective-permute-done.16.got_ref = bf16[32,640]{1,0:T(8,128)(2,1)S(1)} collective-permute-done((bf16[32,640]{1,0:T(8,128)(2,1)S(1)}, bf16[32,640]{1,0:T(8,128)(2,1)S(1)}, u32[]{:S(2)}, u32[]{:S(2)}) %collective-permute-start.16) | collective-permute-done | bytes 40992 | tf_op jit(solution)/shard_map/ppermute | solution.py:526
  41.9 0.0 collective-permute-done.11.got_2
  41.9 0.0 collective-permute-done.12.got_3
  41.9 0.1 join_terms.1.kept_ref
  42.0 2.8 %collective-permute-start.20 = (bf16[32,2048]{1,0:T(8,128)(2,1)S(1)}, bf16[32,2048]{1,0:T(8,128)(2,1)S(1)}, u32[]{:S(2)}, u32[]{:S(2)}) collective-permute-start(bf16[32,2048]{1,0:T(8,128)(2,1)S(1)} %join_terms.1.kept_ref), channel_id=1, source_target_pairs={{0,2},{1,3},{2,0},{3,1},{4,6},{5,7},{6,4},{7,5},{8,10},{9,11},{10,... | collective-permute-start | bytes 393224 | tf_op jit(solution)/shard_map/ppermute | solution.py:526
  44.8 2.4 %collective-permute-start.17 = (bf16[128,512]{1,0:T(8,128)(2,1)S(1)}, bf16[128,512]{1,0:T(8,128)(2,1)S(1)}, u32[]{:S(2)}, u32[]{:S(2)}) collective-permute-start(bf16[128,512]{1,0:T(8,128)(2,1)S(1)} %get-tuple-element.116), channel_id=1, source_target_pairs={{0,24},{4,28},{8,16},{12,20},{16,8},{20,12},{24,0},{28,4},{1,25},{... | collective-permute-start | bytes 393224 | tf_op jit(solution)/shard_map/ppermute | solution.py:526
  47.2 0.5 collective-permute-start.18
  47.7 0.5 collective-permute-start.19
  48.3 2.1 %collective-permute-done.20.got_ref = bf16[32,2048]{1,0:T(8,128)(2,1)S(1)} collective-permute-done((bf16[32,2048]{1,0:T(8,128)(2,1)S(1)}, bf16[32,2048]{1,0:T(8,128)(2,1)S(1)}, u32[]{:S(2)}, u32[]{:S(2)}) %collective-permute-start.20) | collective-permute-done | bytes 131104 | tf_op jit(solution)/shard_map/ppermute | solution.py:526
  50.4 0.1 collective-permute-start.21
  50.4 0.9 %collective-permute-done.17.got_1 = bf16[128,512]{1,0:T(8,128)(2,1)S(1)} collective-permute-done((bf16[128,512]{1,0:T(8,128)(2,1)S(1)}, bf16[128,512]{1,0:T(8,128)(2,1)S(1)}, u32[]{:S(2)}, u32[]{:S(2)}) %collective-permute-start.17) | collective-permute-done | bytes 131104 | tf_op jit(solution)/shard_map/ppermute | solution.py:526
  51.4 1.3 %collective-permute-done.18.got_2 = bf16[128,512]{1,0:T(8,128)(2,1)S(1)} collective-permute-done((bf16[128,512]{1,0:T(8,128)(2,1)S(1)}, bf16[128,512]{1,0:T(8,128)(2,1)S(1)}, u32[]{:S(2)}, u32[]{:S(2)}) %collective-permute-start.18) | collective-permute-done | bytes 131104 | tf_op jit(solution)/shard_map/ppermute | solution.py:526
  52.7 1.2 %input_grad.1 = bf16[512,512]{1,0:T(8,128)(2,1)} custom-call(f32[512,512]{1,0:T(8,128)S(1)} %get-tuple-element.66.base_ref, f32[512,512]{1,0:T(8,128)S(1)} %get-tuple-element.67.normed_ref, f32[512,1]{1,0:T(8,128)S(1)} %get-tuple-element.68.inverse_ref, f32[1,512]{1,0:T(1,128)S(1)} %bitcast.7, bf16[128,512]{1,0:T(8,128)(2,1)S(1)} %get-tuple-element.115.own_ref, ...), custom_call_target="tpu_custom_call" | custom-call | tf_op jit(solution)/shard_map/input_grad/pallas_call | solution.py:512
  53.9 1.6 %collective-permute-done.21.got_ref = bf16[32,2048]{1,0:T(8,128)(2,1)S(1)} collective-permute-done((bf16[32,2048]{1,0:T(8,128)(2,1)S(1)}, bf16[32,2048]{1,0:T(8,128)(2,1)S(1)}, u32[]{:S(2)}, u32[]{:S(2)}) %collective-permute-start.21) | collective-permute-done | bytes 131104 | tf_op jit(solution)/shard_map/ppermute | solution.py:526
  55.5 0.9 %result.1 = (f32[64,1536]{1,0:T(8,128)}, f32[64,512]{1,0:T(8,128)}, f32[1,64]{1,0:T(1,128)}) custom-call(bf16[32,2048]{1,0:T(8,128)(2,1)S(1)} %add_pairs.1.held_ref, bf16[32,2048]{1,0:T(8,128)(2,1)S(1)} %collective-permute-done.21.got_ref, bf16[64,1536]{1,0:T(8,128)(2,1)S(1)} %get-tuple-element.120.w_ref, f32[1,512]{1,0:T(1,128)S(1)} %bitcast.8), custom_call_target="tpu_custom_call" | custom-call | tf_op jit(solution)/shard_map/result/pallas_call | solution.py:512
  (12 shorter events, 0.2 us)
Async XLA Ops:
  1.9 14.2 %collective-permute-start.1 = (bf16[2,128,512]{2,1,0:T(8,128)(2,1)S(1)}, bf16[2,128,512]{2,1,0:T(8,128)(2,1)S(1)}, u32[]{:S(2)}, u32[]{:S(2)}) collective-permute-start(bf16[2,128,512]{2,1,0:T(8,128)(2,1)S(1)} %get-tuple-element.69), channel_id=1, source_target_pairs={{0,16},{4,20},{8,24},{12,28},{16,0},{20,4},{24,8},{28,12},{1,17},{... | collective-permute-start | bytes 786440 | tf_op jit(solution)/shard_map/ppermute | solution.py:526
  4.9 11.1 %collective-permute-start.2 = (bf16[2,128,512]{2,1,0:T(8,128)(2,1)S(1)}, bf16[2,128,512]{2,1,0:T(8,128)(2,1)S(1)}, u32[]{:S(2)}, u32[]{:S(2)}) collective-permute-start(bf16[2,128,512]{2,1,0:T(8,128)(2,1)S(1)} %get-tuple-element.70), channel_id=1, source_target_pairs={{0,8},{4,12},{8,0},{12,4},{16,24},{20,28},{24,16},{28,20},{1,9},{5... | collective-permute-start | bytes 786440 | tf_op jit(solution)/shard_map/ppermute | solution.py:526
  6.4 11.7 %collective-permute-start = (bf16[2,128,512]{2,1,0:T(8,128)(2,1)S(1)}, bf16[2,128,512]{2,1,0:T(8,128)(2,1)S(1)}, u32[]{:S(2)}, u32[]{:S(2)}) collective-permute-start(bf16[2,128,512]{2,1,0:T(8,128)(2,1)S(1)} %get-tuple-element.64), channel_id=1, source_target_pairs={{0,24},{4,28},{8,16},{12,20},{16,8},{20,12},{24,0},{28,4},{1,25},{... | collective-permute-start | bytes 786440 | tf_op jit(solution)/shard_map/ppermute | solution.py:526
  14.1 1.5 %collective-permute-start.3 = (bf16[4,64,384]{2,1,0:T(8,128)(2,1)S(1)}, bf16[4,64,384]{2,1,0:T(8,128)(2,1)S(1)}, u32[]{:S(2)}, u32[]{:S(2)}) collective-permute-start(bf16[4,64,384]{2,1,0:T(8,128)(2,1)S(1)} %get-tuple-element.73), channel_id=1, source_target_pairs={{0,4},{4,0},{8,12},{12,8},{16,20},{20,16},{24,28},{28,24},{1,5},{5... | collective-permute-start | bytes 589832 | tf_op jit(solution)/shard_map/ppermute | solution.py:526
  14.2 1.7 %collective-permute-start.4 = (bf16[4,64,384]{2,1,0:T(8,128)(2,1)S(1)}, bf16[4,64,384]{2,1,0:T(8,128)(2,1)S(1)}, u32[]{:S(2)}, u32[]{:S(2)}) collective-permute-start(bf16[4,64,384]{2,1,0:T(8,128)(2,1)S(1)} %get-tuple-element.74), channel_id=1, source_target_pairs={{0,4},{4,0},{8,12},{12,8},{16,20},{20,16},{24,28},{28,24},{1,5},{5... | collective-permute-start | bytes 589832 | tf_op jit(solution)/shard_map/ppermute | solution.py:526
  15.9 4.2 %copy-start = (f32[512]{0:T(512)S(1)}, f32[512]{0:T(512)}, u32[]{:S(2)}) copy-start(f32[512]{0:T(512)} %param.6) | copy-start | bytes 6148
  18.2 2.0 %collective-permute-start.5 = (bf16[4,2,64,512]{3,2,1,0:T(8,128)(2,1)S(1)}, bf16[4,2,64,512]{3,2,1,0:T(8,128)(2,1)S(1)}, u32[]{:S(2)}, u32[]{:S(2)}) collective-permute-start(bf16[4,2,64,512]{3,2,1,0:T(8,128)(2,1)S(1)} %pack_other_core.1), channel_id=1, source_target_pairs={{0,4},{4,0},{8,12},{12,8},{16,20},{20,16},{24,28},{28,24},{1,5},{5... | collective-permute-start | bytes 1572872 | tf_op jit(solution)/shard_map/ppermute | solution.py:526
  18.2 7.3 %collective-permute-start.6 = (bf16[4,32,768]{2,1,0:T(8,128)(2,1)S(1)}, bf16[4,32,768]{2,1,0:T(8,128)(2,1)S(1)}, u32[]{:S(2)}, u32[]{:S(2)}) collective-permute-start(bf16[4,32,768]{2,1,0:T(8,128)(2,1)S(1)} %get-tuple-element.86), channel_id=1, source_target_pairs={{0,1},{1,0},{2,3},{3,2},{4,5},{5,4},{6,7},{7,6},{8,9},{9,8},{10,11... | collective-permute-start | bytes 589832 | tf_op jit(solution)/shard_map/ppermute | solution.py:526
  25.6 2.1 %collective-permute-start.8 = (bf16[4,64,1280]{2,1,0:T(8,128)(2,1)S(1)}, bf16[4,64,1280]{2,1,0:T(8,128)(2,1)S(1)}, u32[]{:S(2)}, u32[]{:S(2)}) collective-permute-start(bf16[4,64,1280]{2,1,0:T(8,128)(2,1)S(1)} %get-tuple-element.100), channel_id=1, source_target_pairs={{0,4},{4,0},{8,12},{12,8},{16,20},{20,16},{24,28},{28,24},{1,5},{5... | collective-permute-start | bytes 1966088 | tf_op jit(solution)/shard_map/ppermute | solution.py:526
  25.6 7.6 %collective-permute-start.7 = (bf16[4,64,512]{2,1,0:T(8,128)(2,1)S(1)}, bf16[4,64,512]{2,1,0:T(8,128)(2,1)S(1)}, u32[]{:S(2)}, u32[]{:S(2)}) collective-permute-start(bf16[4,64,512]{2,1,0:T(8,128)(2,1)S(1)} %get-tuple-element.90), channel_id=1, source_target_pairs={{0,4},{4,0},{8,12},{12,8},{16,20},{20,16},{24,28},{28,24},{1,5},{5... | collective-permute-start | bytes 786440 | tf_op jit(solution)/shard_map/ppermute | solution.py:526
  27.9 6.3 %collective-permute-start.9 = (bf16[4,32,640]{2,1,0:T(8,128)(2,1)S(1)}, bf16[4,32,640]{2,1,0:T(8,128)(2,1)S(1)}, u32[]{:S(2)}, u32[]{:S(2)}) collective-permute-start(bf16[4,32,640]{2,1,0:T(8,128)(2,1)S(1)} %get-tuple-element.102), channel_id=1, source_target_pairs={{0,1},{1,0},{2,3},{3,2},{4,5},{5,4},{6,7},{7,6},{8,9},{9,8},{10,11... | collective-permute-start | bytes 491528 | tf_op jit(solution)/shard_map/ppermute | solution.py:526
  29.6 7.8 %collective-permute-start.13 = (bf16[64,640]{1,0:T(8,128)(2,1)S(1)}, bf16[64,640]{1,0:T(8,128)(2,1)S(1)}, u32[]{:S(2)}, u32[]{:S(2)}) collective-permute-start(bf16[64,640]{1,0:T(8,128)(2,1)S(1)} %get-tuple-element.110), channel_id=1, source_target_pairs={{0,24},{4,28},{8,16},{12,20},{16,8},{20,12},{24,0},{28,4},{1,25},{... | collective-permute-start | bytes 245768 | tf_op jit(solution)/shard_map/ppermute | solution.py:526
  32.1 5.7 %collective-permute-start.14 = (bf16[64,640]{1,0:T(8,128)(2,1)S(1)}, bf16[64,640]{1,0:T(8,128)(2,1)S(1)}, u32[]{:S(2)}, u32[]{:S(2)}) collective-permute-start(bf16[64,640]{1,0:T(8,128)(2,1)S(1)} %get-tuple-element.111), channel_id=1, source_target_pairs={{0,16},{4,20},{8,24},{12,28},{16,0},{20,4},{24,8},{28,12},{1,17},{... | collective-permute-start | bytes 245768 | tf_op jit(solution)/shard_map/ppermute | solution.py:526
  32.6 5.2 %collective-permute-start.15 = (bf16[64,640]{1,0:T(8,128)(2,1)S(1)}, bf16[64,640]{1,0:T(8,128)(2,1)S(1)}, u32[]{:S(2)}, u32[]{:S(2)}) collective-permute-start(bf16[64,640]{1,0:T(8,128)(2,1)S(1)} %get-tuple-element.112), channel_id=1, source_target_pairs={{0,8},{4,12},{8,0},{12,4},{16,24},{20,28},{24,16},{28,20},{1,9},{5... | collective-permute-start | bytes 245768 | tf_op jit(solution)/shard_map/ppermute | solution.py:526
  34.2 7.7 %collective-permute-start.10 = (bf16[32,1408]{1,0:T(8,128)(2,1)S(1)}, bf16[32,1408]{1,0:T(8,128)(2,1)S(1)}, u32[]{:S(2)}, u32[]{:S(2)}) collective-permute-start(bf16[32,1408]{1,0:T(8,128)(2,1)S(1)} %get-tuple-element.106), channel_id=1, source_target_pairs={{0,24},{4,28},{8,16},{12,20},{16,8},{20,12},{24,0},{28,4},{1,25},{... | collective-permute-start | bytes 270344 | tf_op jit(solution)/shard_map/ppermute | solution.py:526
  36.9 5.0 %collective-permute-start.11 = (bf16[32,1408]{1,0:T(8,128)(2,1)S(1)}, bf16[32,1408]{1,0:T(8,128)(2,1)S(1)}, u32[]{:S(2)}, u32[]{:S(2)}) collective-permute-start(bf16[32,1408]{1,0:T(8,128)(2,1)S(1)} %get-tuple-element.107), channel_id=1, source_target_pairs={{0,16},{4,20},{8,24},{12,28},{16,0},{20,4},{24,8},{28,12},{1,17},{... | collective-permute-start | bytes 270344 | tf_op jit(solution)/shard_map/ppermute | solution.py:526
  37.4 4.5 %collective-permute-start.12 = (bf16[32,1408]{1,0:T(8,128)(2,1)S(1)}, bf16[32,1408]{1,0:T(8,128)(2,1)S(1)}, u32[]{:S(2)}, u32[]{:S(2)}) collective-permute-start(bf16[32,1408]{1,0:T(8,128)(2,1)S(1)} %get-tuple-element.108), channel_id=1, source_target_pairs={{0,8},{4,12},{8,0},{12,4},{16,24},{20,28},{24,16},{28,20},{1,9},{5... | collective-permute-start | bytes 270344 | tf_op jit(solution)/shard_map/ppermute | solution.py:526
  37.8 4.1 %collective-permute-start.16 = (bf16[32,640]{1,0:T(8,128)(2,1)S(1)}, bf16[32,640]{1,0:T(8,128)(2,1)S(1)}, u32[]{:S(2)}, u32[]{:S(2)}) collective-permute-start(bf16[32,640]{1,0:T(8,128)(2,1)S(1)} %get-tuple-element.114), channel_id=1, source_target_pairs={{0,1},{1,0},{2,3},{3,2},{4,5},{5,4},{6,7},{7,6},{8,9},{9,8},{10,11... | collective-permute-start | bytes 122888 | tf_op jit(solution)/shard_map/ppermute | solution.py:526
  42.0 8.3 %collective-permute-start.20 = (bf16[32,2048]{1,0:T(8,128)(2,1)S(1)}, bf16[32,2048]{1,0:T(8,128)(2,1)S(1)}, u32[]{:S(2)}, u32[]{:S(2)}) collective-permute-start(bf16[32,2048]{1,0:T(8,128)(2,1)S(1)} %join_terms.1.kept_ref), channel_id=1, source_target_pairs={{0,2},{1,3},{2,0},{3,1},{4,6},{5,7},{6,4},{7,5},{8,10},{9,11},{10,... | collective-permute-start | bytes 393224 | tf_op jit(solution)/shard_map/ppermute | solution.py:526
  44.8 6.6 %collective-permute-start.17 = (bf16[128,512]{1,0:T(8,128)(2,1)S(1)}, bf16[128,512]{1,0:T(8,128)(2,1)S(1)}, u32[]{:S(2)}, u32[]{:S(2)}) collective-permute-start(bf16[128,512]{1,0:T(8,128)(2,1)S(1)} %get-tuple-element.116), channel_id=1, source_target_pairs={{0,24},{4,28},{8,16},{12,20},{16,8},{20,12},{24,0},{28,4},{1,25},{... | collective-permute-start | bytes 393224 | tf_op jit(solution)/shard_map/ppermute | solution.py:526
  47.2 5.5 %collective-permute-start.18 = (bf16[128,512]{1,0:T(8,128)(2,1)S(1)}, bf16[128,512]{1,0:T(8,128)(2,1)S(1)}, u32[]{:S(2)}, u32[]{:S(2)}) collective-permute-start(bf16[128,512]{1,0:T(8,128)(2,1)S(1)} %get-tuple-element.117), channel_id=1, source_target_pairs={{0,16},{4,20},{8,24},{12,28},{16,0},{20,4},{24,8},{28,12},{1,17},{... | collective-permute-start | bytes 393224 | tf_op jit(solution)/shard_map/ppermute | solution.py:526
  47.7 5.0 %collective-permute-start.19 = (bf16[128,512]{1,0:T(8,128)(2,1)S(1)}, bf16[128,512]{1,0:T(8,128)(2,1)S(1)}, u32[]{:S(2)}, u32[]{:S(2)}) collective-permute-start(bf16[128,512]{1,0:T(8,128)(2,1)S(1)} %get-tuple-element.118), channel_id=1, source_target_pairs={{0,8},{4,12},{8,0},{12,4},{16,24},{20,28},{24,16},{28,20},{1,9},{5... | collective-permute-start | bytes 393224 | tf_op jit(solution)/shard_map/ppermute | solution.py:526
  50.4 5.1 %collective-permute-start.21 = (bf16[32,2048]{1,0:T(8,128)(2,1)S(1)}, bf16[32,2048]{1,0:T(8,128)(2,1)S(1)}, u32[]{:S(2)}, u32[]{:S(2)}) collective-permute-start(bf16[32,2048]{1,0:T(8,128)(2,1)S(1)} %add_pairs.1.held_ref), channel_id=1, source_target_pairs={{0,1},{1,0},{2,3},{3,2},{4,5},{5,4},{6,7},{7,6},{8,9},{9,8},{10,11... | collective-permute-start | bytes 393224 | tf_op jit(solution)/shard_map/ppermute | solution.py:526

commit v11 on v10

--- a/solution.py
+++ b/solution.py
@@ -21,7 +21,6 @@
 VMEM = pl.BlockSpec(memory_space=pltpu.VMEM)
 HBM = pl.BlockSpec(memory_space=pltpu.HBM)
 CHIP_STEPS = (3, 2, 1)
-FIRST_PART = 640
 PINNED = pl.BlockSpec(memory_space=pltpu.VMEM)
 shaped = jax.ShapeDtypeStruct
 
@@ -416,11 +415,10 @@
     finished(*started(*copies))
 
 
-def split_rows(total, axis, send_ref, kept_ref):
+def split_rows(total, axis):
     upper = (here()[2] & 1) == 1
     low, high = jnp.split(total, 2, axis)
-    send_ref[...] = jnp.where(upper, low, high).astype(BF16)
-    kept_ref[...] = jnp.where(upper, high, low)
+    return jnp.where(upper, low, high).astype(BF16), jnp.where(upper, high, low)
 
 
 def row_cores_kernel(keep_1, keep_2, got_1, got_2, send_ref, kept_ref):
@@ -428,27 +426,15 @@
         keep_ref[...].astype(F32) + got_ref[...].astype(F32)
         for keep_ref, got_ref in ((keep_1, got_1), (keep_2, got_2))
     ]
-    split_rows(jnp.concatenate(total, 2), 1, send_ref, kept_ref)
-
-
-def cores_kernel(keep_ref, got_ref, send_ref, kept_ref, *targets):
-    chip, cut = here()[0], kept_ref.shape[2]
-    first = keep_ref[:, :, :cut].astype(F32) + got_ref[:, :, :cut].astype(F32)
-    split_rows(first, 1, send_ref, kept_ref)
+    send_ref[...], kept_ref[...] = split_rows(jnp.concatenate(total, 2), 1)
+
+
+def cores_kernel(keep_ref, got_ref, *targets):
+    chip = here()[0]
     for step, target in zip((0, *CHIP_STEPS), targets):
         there = chip ^ step
-        total = keep_ref[there, :, cut:].astype(F32) + got_ref[there, :, cut:].astype(F32)
+        total = keep_ref[there].astype(F32) + got_ref[there].astype(F32)
         target[...] = total.astype(target.dtype)
-
-
-def pair_kernel(kept_ref, got_ref, row_kept, row_got, *targets):
-    chip, cut = here()[0], kept_ref.shape[2]
-    for step, target in zip((0, *CHIP_STEPS), targets):
-        there = chip ^ step
-        total = kept_ref[there] + got_ref[there].astype(F32)
-        target[:, :cut] = total.astype(target.dtype)
-        total = row_kept[there] + row_got[there].astype(F32)
-        target[:, cut:] = total.astype(target.dtype)
 
 
 def layer_sum(own_ref, got_1, got_2, got_3):
@@ -457,16 +443,17 @@
     )
 
 
-def layer_kernel(own_ref, got_1, got_2, got_3, send_ref, kept_ref):
-    split_rows(layer_sum(own_ref, got_1, got_2, got_3), 0, send_ref, kept_ref)
-
-
-def join_kernel(own_ref, got_1, got_2, got_3, kept_ref, got_ref, out_ref):
-    total = layer_sum(own_ref, got_1, got_2, got_3).astype(BF16)
-    cut, width = FIRST_PART, kept_ref.shape[1]
-    out_ref[:, :cut] = total[:, :cut]
-    out_ref[:, cut : cut + width] = (kept_ref[...] + got_ref[...].astype(F32)).astype(BF16)
-    out_ref[:, cut + width :] = total[:, cut:]
+def layer_kernel(own_ref, got_1, got_2, got_3, send_1, send_2, kept_ref):
+    sent, kept_ref[...] = split_rows(layer_sum(own_ref, got_1, got_2, got_3), 0)
+    cut = send_1.shape[1]
+    send_1[...], send_2[...] = sent[:, :cut], sent[:, cut:]
+
+
+def join_kernel(own_ref, got_1, got_2, got_3, kept_ref, pair_1, pair_2, out_ref):
+    cut = kept_ref.shape[1]
+    got = jnp.concatenate([pair_1[...], pair_2[...]], 1).astype(F32)
+    out_ref[:, :cut] = (kept_ref[...] + got).astype(BF16)
+    out_ref[:, cut:] = layer_sum(own_ref, got_1, got_2, got_3).astype(BF16)
 
 
 def add_kernel(kept_ref, got_ref, out_ref):
@@ -524,6 +511,17 @@
 def swap(array, axis, bits):
     count = lax.axis_size(axis)
     return lax.ppermute(array, axis, [(i, i ^ bits) for i in range(count)])
+
+
+def add_by_chip(keep, got, name):
+    shape = keep.shape[1:]
+    return call(
+        cores_kernel,
+        name,
+        [(VMEM, keep), (VMEM, got)],
+        [(shape, F32)] + [(shape, BF16)] * 3,
+        out_specs=[PINNED, VMEM, VMEM, VMEM],
+    )
 
 
 def cross_chips(*offs):
@@ -620,7 +618,6 @@
             [(VMEM, one) for one in (x_near, cot_near, *near)],
             [((chips, 2, share, width), BF16)],
         )
-        row_got = swap(row_next, "dp", 1)
         send, keep, col_grads = call(
             column_chip_kernel,
             "column_heads",
@@ -641,17 +638,10 @@
             [(VMEM, col_grads), (VMEM, col_weight)],
             [((chips, share, width), BF16)] * 2,
         )
-        send, row_got, back_keep = lax.optimization_barrier((send, row_got, back_keep))
-        first_half = (chips, row_share // 2, FIRST_PART)
-        second = (row_share, col_width - FIRST_PART)
-        to_next, kept, *parts = call(
-            cores_kernel,
-            "column_add_cores",
-            [(VMEM, keep), (VMEM, swap(send, "seq", 1))],
-            [(first_half, BF16), (first_half, F32), (second, F32)] + [(second, BF16)] * 3,
-            out_specs=[VMEM, PINNED, PINNED, VMEM, VMEM, VMEM],
-        )
-        layer_got = cross_chips(*parts[1:])
+        row_next, _ = lax.optimization_barrier((row_next, send))
+        keep, back_keep = lax.optimization_barrier((keep, back_keep))
+        owned, *off = add_by_chip(keep, swap(send, "seq", 1), "column_add_cores")
+        got = cross_chips(*off)
         back = call(
             back_pack_kernel,
             "pack_grad_hidden",
@@ -659,27 +649,21 @@
             [((2 * share, width), BF16)] * 4,
         )
         row_kept, *back = lax.optimization_barrier((row_kept, *back))
-        joint = (row_share // 2, FIRST_PART + row_width)
-        owned, *off = call(
-            pair_kernel,
-            "first_add_pair",
-            [(VMEM, one) for one in (kept, swap(to_next, "dp", 1), row_kept, row_got)],
-            [(joint, F32)] + [(joint, BF16)] * 3,
-            out_specs=[PINNED, VMEM, VMEM, VMEM],
-        )
-        got = cross_chips(*off)
-        half_second = (row_share // 2, second[1])
-        to_next, kept = call(
+        row_owned, *row_off = add_by_chip(row_kept, swap(row_next, "dp", 1), "row_add_pair")
+        row_got = cross_chips(*row_off)
+        half_rows = row_share // 2
+        *to_next, kept = call(
             layer_kernel,
-            "second_add_chips",
-            [(VMEM, one) for one in (parts[0], *layer_got)],
-            [(half_second, BF16), (half_second, F32)],
-            out_specs=[VMEM, PINNED],
-        )
+            "column_add_chips",
+            [(VMEM, one) for one in (owned, *got)],
+            [((half_rows, col_width // 2), BF16)] * 2 + [((half_rows, col_width), F32)],
+            out_specs=[VMEM, VMEM, PINNED],
+        )
+        pair_got = [swap(one, "dp", 1) for one in to_next]
         (pair_sum,) = call(
             join_kernel,
             "join_terms",
-            [(VMEM, one) for one in (owned, *got, kept, swap(to_next, "dp", 1))],
+            [(VMEM, one) for one in (row_owned, *row_got, kept, *pair_got)],
             [((row_share // 2, col_width + row_width), BF16)],
         )
         *back, pair_sum = lax.optimization_barrier((*back, pair_sum))

time: 56.5 us -> 56.6 us (level)
  waiting for transfers between devices: 15.8 us -> 16.4 us
  transfers between devices with their start and end apart: 22 -> 22, of which waited for: 12 -> 14; matrix products, arithmetic and copies ran while one was open for 0% -> 0% of each run, Pallas kernels for 23% -> 17%
where the time goes in v11:
time: 56.6 us; the launch traced here: 56.5 us
  starting transfers between devices  24.1 us (43%)
  waiting for transfers between devices  16.4 us (29%)
  Pallas kernels  15.2 us (27%)
  between operations  0.75 us (1%)
    ppermute x22, starting transfers between devices, swap(): return lax.ppermute(array, axis, [(i, i ^ bits) for i in range(count)])  24.1 us
    ppermute x22, waiting for transfers between devices, swap(): return lax.ppermute(array, axis, [(i, i ^ bits) for i in range(count)])  16.4 us
    pallas_call x14, Pallas kernels, call(): pl.pallas_call(kernel, out_shape=outs, in_specs=[spec for spec, _ in ins]...  15.2 us
  transfers between devices with their start and end apart: 22, of which 14 were waited for; matrix products, arithmetic and copies ran while one was open for 0% of the time, Pallas kernels for 17%

profile of v11, /device:TPU:0, one launch (start us, length us, event | category | flops | bytes accessed | tf_op | source)
XLA Modules:
  0.0 56.5 jit_solution(17900390052906532475)
XLA Ops:
  0.6 1.3 %pack_columns.1 = (bf16[2,128,512]{2,1,0:T(8,128)(2,1)S(1)}, bf16[2,128,512]{2,1,0:T(8,128)(2,1)S(1)}, bf16[2,128,512]{2,1,0:T(8,128)(2,1)S(1)}) custom-call(bf16[512,512]{1,0:T(8,128)(2,1)} %bitcast.9, bf16[512,512]{1,0:T(8,128)(2,1)} %bitcast.11), custom_call_target="tpu_custom_call" | custom-call | tf_op jit(solution)/shard_map/pack_columns/pallas_call | solution.py:499
  1.9 3.0 %collective-permute-start.1 = (bf16[2,128,512]{2,1,0:T(8,128)(2,1)S(1)}, bf16[2,128,512]{2,1,0:T(8,128)(2,1)S(1)}, u32[]{:S(2)}, u32[]{:S(2)}) collective-permute-start(bf16[2,128,512]{2,1,0:T(8,128)(2,1)S(1)} %get-tuple-element.68), channel_id=1, source_target_pairs={{0,16},{4,20},{8,24},{12,28},{16,0},{20,4},{24,8},{28,12},{1,17},{... | collective-permute-start | bytes 786440 | tf_op jit(solution)/shard_map/ppermute | solution.py:513
  4.9 1.5 %collective-permute-start.2 = (bf16[2,128,512]{2,1,0:T(8,128)(2,1)S(1)}, bf16[2,128,512]{2,1,0:T(8,128)(2,1)S(1)}, u32[]{:S(2)}, u32[]{:S(2)}) collective-permute-start(bf16[2,128,512]{2,1,0:T(8,128)(2,1)S(1)} %get-tuple-element.69), channel_id=1, source_target_pairs={{0,8},{4,12},{8,0},{12,4},{16,24},{20,28},{24,16},{28,20},{1,9},{5... | collective-permute-start | bytes 786440 | tf_op jit(solution)/shard_map/ppermute | solution.py:513
  6.4 0.0 collective-permute-start
  6.5 7.7 %row_heads.1 = (bf16[4,64,384]{2,1,0:T(8,128)(2,1)S(1)}, bf16[4,64,384]{2,1,0:T(8,128)(2,1)S(1)}, bf16[4,64,384]{2,1,0:T(8,128)(2,1)S(1)}, bf16[4,64,384]{2,1,0:...) custom-call(bf16[512,512]{1,0:T(8,128)(2,1)} %bitcast.10, ...), custom_call_target="tpu_custom_call" | custom-call | tf_op jit(solution)/shard_map/row_heads/pallas_call | solution.py:499
  14.1 0.1 collective-permute-start.3
  14.2 0.5 collective-permute-start.4
  14.7 0.9 %collective-permute-done.3.got_1 = bf16[4,64,384]{2,1,0:T(8,128)(2,1)S(1)} collective-permute-done((bf16[4,64,384]{2,1,0:T(8,128)(2,1)S(1)}, bf16[4,64,384]{2,1,0:T(8,128)(2,1)S(1)}, u32[]{:S(2)}, u32[]{:S(2)}) %collective-permute-start.3) | collective-permute-done | bytes 196640 | tf_op jit(solution)/shard_map/ppermute | solution.py:513
  15.6 0.3 collective-permute-done.4.got_2
  15.9 0.1 row_add_cores.1
  16.1 0.0 collective-permute-done.2.near_3
  16.1 2.0 %collective-permute-done.near_1 = bf16[2,128,512]{2,1,0:T(8,128)(2,1)S(1)} collective-permute-done((bf16[2,128,512]{2,1,0:T(8,128)(2,1)S(1)}, bf16[2,128,512]{2,1,0:T(8,128)(2,1)S(1)}, u32[]{:S(2)}, u32[]{:S(2)}) %collective-permute-start) | collective-permute-done | bytes 262176 | tf_op jit(solution)/shard_map/ppermute | solution.py:513
  18.2 0.1 collective-permute-start.5
  18.2 1.9 %collective-permute-done.5.far_ref = bf16[4,2,64,512]{3,2,1,0:T(8,128)(2,1)S(1)} collective-permute-done((bf16[4,2,64,512]{3,2,1,0:T(8,128)(2,1)S(1)}, bf16[4,2,64,512]{3,2,1,0:T(8,128)(2,1)S(1)}, u32[]{:S(2)}, u32[]{:S(2)}) %collective-permute-start.5) | collective-permute-done | bytes 524320 | tf_op jit(solution)/shard_map/ppermute | solution.py:513
  20.1 3.1 %column_heads.1 = (bf16[4,64,1280]{2,1,0:T(8,128)(2,1)S(1)}, bf16[4,64,1280]{2,1,0:T(8,128)(2,1)S(1)}, bf16[512,768]{1,0:T(8,128)(2,1)S(1)}) custom-call(bf16[512,512]{1,0:T(8,128)(2,1)S(1)} %get-tuple-element.76.x_ref, bf16[512,512]{1,0:T(8,128)(2,1)S(1)} %get-tuple-element.77.cot_ref, bf16[2,128,512]{2,1,0:T(8,128)(2,1)S(1)} %collective-permute-done.near_1, ...), custom_call_target="tpu_custom_call" | custom-call | tf_op jit(solution)/shard_map/column_heads/pallas_call | solution.py:499
  23.2 0.2 collective-permute-start.11
  23.4 0.6 %column_grad_hidden.1 = (bf16[4,64,512]{2,1,0:T(8,128)(2,1)S(1)}, bf16[4,64,512]{2,1,0:T(8,128)(2,1)S(1)}) custom-call(bf16[512,768]{1,0:T(8,128)(2,1)S(1)} %get-tuple-element.85.grads_ref, bf16[512,768]{1,0:T(8,128)(2,1)S(1)} %get-tuple-element.81.w_ref), custom_call_target="tpu_custom_call" | custom-call | tf_op jit(solution)/shard_map/column_grad_hidden/pallas_call | solution.py:499
  24.0 0.4 collective-permute-start.6
  24.5 1.7 %collective-permute-start.7 = (bf16[4,32,768]{2,1,0:T(8,128)(2,1)S(1)}, bf16[4,32,768]{2,1,0:T(8,128)(2,1)S(1)}, u32[]{:S(2)}, u32[]{:S(2)}) collective-permute-start(bf16[4,32,768]{2,1,0:T(8,128)(2,1)S(1)} %get-tuple-element.100), channel_id=1, source_target_pairs={{0,1},{1,0},{2,3},{3,2},{4,5},{5,4},{6,7},{7,6},{8,9},{9,8},{10,11... | collective-permute-start | bytes 589832 | tf_op jit(solution)/shard_map/ppermute | solution.py:513
  26.2 0.0 collective-permute-done.11.got_ref
  26.2 0.1 column_add_cores.1
  26.4 2.5 %collective-permute-start.12 = (bf16[64,1280]{1,0:T(8,128)(2,1)S(1)}, bf16[64,1280]{1,0:T(8,128)(2,1)S(1)}, u32[]{:S(2)}, u32[]{:S(2)}) collective-permute-start(bf16[64,1280]{1,0:T(8,128)(2,1)S(1)} %get-tuple-element.107), channel_id=1, source_target_pairs={{0,24},{4,28},{8,16},{12,20},{16,8},{20,12},{24,0},{28,4},{1,25},{... | collective-permute-start | bytes 491528 | tf_op jit(solution)/shard_map/ppermute | solution.py:513
  28.9 0.5 collective-permute-start.13
  29.4 0.5 collective-permute-start.14
  29.9 0.0 collective-permute-done.6.got_ref
  30.0 1.5 %collective-permute-done.7.got_ref = bf16[4,32,768]{2,1,0:T(8,128)(2,1)S(1)} collective-permute-done((bf16[4,32,768]{2,1,0:T(8,128)(2,1)S(1)}, bf16[4,32,768]{2,1,0:T(8,128)(2,1)S(1)}, u32[]{:S(2)}, u32[]{:S(2)}) %collective-permute-start.7) | collective-permute-done | bytes 196640 | tf_op jit(solution)/shard_map/ppermute | solution.py:513
  31.5 2.7 %collective-permute-start.8 = (bf16[32,768]{1,0:T(8,128)(2,1)S(1)}, bf16[32,768]{1,0:T(8,128)(2,1)S(1)}, u32[]{:S(2)}, u32[]{:S(2)}) collective-permute-start(bf16[32,768]{1,0:T(8,128)(2,1)S(1)} %get-tuple-element.102), channel_id=1, source_target_pairs={{0,24},{4,28},{8,16},{12,20},{16,8},{20,12},{24,0},{28,4},{1,25},{... | collective-permute-start | bytes 147464 | tf_op jit(solution)/shard_map/ppermute | solution.py:513
  34.1 0.5 collective-permute-start.9
  34.6 1.3 %collective-permute-start.10 = (bf16[32,768]{1,0:T(8,128)(2,1)S(1)}, bf16[32,768]{1,0:T(8,128)(2,1)S(1)}, u32[]{:S(2)}, u32[]{:S(2)}) collective-permute-start(bf16[32,768]{1,0:T(8,128)(2,1)S(1)} %get-tuple-element.104), channel_id=1, source_target_pairs={{0,8},{4,12},{8,0},{12,4},{16,24},{20,28},{24,16},{28,20},{1,9},{5... | collective-permute-start | bytes 147464 | tf_op jit(solution)/shard_map/ppermute | solution.py:513
  35.9 1.5 %collective-permute-done.13.got_2 = bf16[64,1280]{1,0:T(8,128)(2,1)S(1)} collective-permute-done((bf16[64,1280]{1,0:T(8,128)(2,1)S(1)}, bf16[64,1280]{1,0:T(8,128)(2,1)S(1)}, u32[]{:S(2)}, u32[]{:S(2)}) %collective-permute-start.13) | collective-permute-done | bytes 163872 | tf_op jit(solution)/shard_map/ppermute | solution.py:513
  37.4 0.5 collective-permute-done.14.got_3
  38.0 0.1 column_add_chips.1
  38.0 1.0 %collective-permute-start.15 = (bf16[32,640]{1,0:T(8,128)(2,1)S(1)}, bf16[32,640]{1,0:T(8,128)(2,1)S(1)}, u32[]{:S(2)}, u32[]{:S(2)}) collective-permute-start(bf16[32,640]{1,0:T(8,128)(2,1)S(1)} %get-tuple-element.111), channel_id=1, source_target_pairs={{0,1},{1,0},{2,3},{3,2},{4,5},{5,4},{6,7},{7,6},{8,9},{9,8},{10,11... | collective-permute-start | bytes 122888 | tf_op jit(solution)/shard_map/ppermute | solution.py:513
  39.0 1.1 %collective-permute-start.16 = (bf16[32,640]{1,0:T(8,128)(2,1)S(1)}, bf16[32,640]{1,0:T(8,128)(2,1)S(1)}, u32[]{:S(2)}, u32[]{:S(2)}) collective-permute-start(bf16[32,640]{1,0:T(8,128)(2,1)S(1)} %get-tuple-element.112), channel_id=1, source_target_pairs={{0,1},{1,0},{2,3},{3,2},{4,5},{5,4},{6,7},{7,6},{8,9},{9,8},{10,11... | collective-permute-start | bytes 122888 | tf_op jit(solution)/shard_map/ppermute | solution.py:513
  40.1 2.0 %collective-permute-done.15.pair_1 = bf16[32,640]{1,0:T(8,128)(2,1)S(1)} collective-permute-done((bf16[32,640]{1,0:T(8,128)(2,1)S(1)}, bf16[32,640]{1,0:T(8,128)(2,1)S(1)}, u32[]{:S(2)}, u32[]{:S(2)}) %collective-permute-start.15) | collective-permute-done | bytes 40992 | tf_op jit(solution)/shard_map/ppermute | solution.py:513
  42.1 0.9 %collective-permute-done.16.pair_2 = bf16[32,640]{1,0:T(8,128)(2,1)S(1)} collective-permute-done((bf16[32,640]{1,0:T(8,128)(2,1)S(1)}, bf16[32,640]{1,0:T(8,128)(2,1)S(1)}, u32[]{:S(2)}, u32[]{:S(2)}) %collective-permute-start.16) | collective-permute-done | bytes 40992 | tf_op jit(solution)/shard_map/ppermute | solution.py:513
  43.1 2.7 %collective-permute-start.20 = (bf16[32,2048]{1,0:T(8,128)(2,1)S(1)}, bf16[32,2048]{1,0:T(8,128)(2,1)S(1)}, u32[]{:S(2)}, u32[]{:S(2)}) collective-permute-start(bf16[32,2048]{1,0:T(8,128)(2,1)S(1)} %join_terms.1.kept_ref), channel_id=1, source_target_pairs={{0,2},{1,3},{2,0},{3,1},{4,6},{5,7},{6,4},{7,5},{8,10},{9,11},{10,... | collective-permute-start | bytes 393224 | tf_op jit(solution)/shard_map/ppermute | solution.py:513
  45.7 2.3 %collective-permute-start.17 = (bf16[128,512]{1,0:T(8,128)(2,1)S(1)}, bf16[128,512]{1,0:T(8,128)(2,1)S(1)}, u32[]{:S(2)}, u32[]{:S(2)}) collective-permute-start(bf16[128,512]{1,0:T(8,128)(2,1)S(1)} %get-tuple-element.114), channel_id=1, source_target_pairs={{0,24},{4,28},{8,16},{12,20},{16,8},{20,12},{24,0},{28,4},{1,25},{... | collective-permute-start | bytes 393224 | tf_op jit(solution)/shard_map/ppermute | solution.py:513
  48.1 0.6 %collective-permute-start.18 = (bf16[128,512]{1,0:T(8,128)(2,1)S(1)}, bf16[128,512]{1,0:T(8,128)(2,1)S(1)}, u32[]{:S(2)}, u32[]{:S(2)}) collective-permute-start(bf16[128,512]{1,0:T(8,128)(2,1)S(1)} %get-tuple-element.115), channel_id=1, source_target_pairs={{0,16},{4,20},{8,24},{12,28},{16,0},{20,4},{24,8},{28,12},{1,17},{... | collective-permute-start | bytes 393224 | tf_op jit(solution)/shard_map/ppermute | solution.py:513
  48.7 0.5 collective-permute-start.19
  49.2 1.3 %collective-permute-done.20.got_ref = bf16[32,2048]{1,0:T(8,128)(2,1)S(1)} collective-permute-done((bf16[32,2048]{1,0:T(8,128)(2,1)S(1)}, bf16[32,2048]{1,0:T(8,128)(2,1)S(1)}, u32[]{:S(2)}, u32[]{:S(2)}) %collective-permute-start.20) | collective-permute-done | bytes 131104 | tf_op jit(solution)/shard_map/ppermute | solution.py:513
  50.5 0.3 collective-permute-start.21
  50.8 1.0 %collective-permute-done.17.got_1 = bf16[128,512]{1,0:T(8,128)(2,1)S(1)} collective-permute-done((bf16[128,512]{1,0:T(8,128)(2,1)S(1)}, bf16[128,512]{1,0:T(8,128)(2,1)S(1)}, u32[]{:S(2)}, u32[]{:S(2)}) %collective-permute-start.17) | collective-permute-done | bytes 131104 | tf_op jit(solution)/shard_map/ppermute | solution.py:513
  51.8 1.4 %collective-permute-done.18.got_2 = bf16[128,512]{1,0:T(8,128)(2,1)S(1)} collective-permute-done((bf16[128,512]{1,0:T(8,128)(2,1)S(1)}, bf16[128,512]{1,0:T(8,128)(2,1)S(1)}, u32[]{:S(2)}, u32[]{:S(2)}) %collective-permute-start.18) | collective-permute-done | bytes 131104 | tf_op jit(solution)/shard_map/ppermute | solution.py:513
  53.2 0.4 collective-permute-done.19.got_3
  53.7 1.1 %input_grad.1 = bf16[512,512]{1,0:T(8,128)(2,1)} custom-call(f32[512,512]{1,0:T(8,128)S(1)} %get-tuple-element.65.base_ref, f32[512,512]{1,0:T(8,128)S(1)} %get-tuple-element.66.normed_ref, f32[512,1]{1,0:T(8,128)S(1)} %get-tuple-element.67.inverse_ref, f32[1,512]{1,0:T(1,128)S(1)} %bitcast.7, bf16[128,512]{1,0:T(8,128)(2,1)S(1)} %get-tuple-element.113.own_ref, ...), custom_call_target="tpu_custom_call" | custom-call | tf_op jit(solution)/shard_map/input_grad/pallas_call | solution.py:499
  54.8 0.8 %collective-permute-done.21.got_ref = bf16[32,2048]{1,0:T(8,128)(2,1)S(1)} collective-permute-done((bf16[32,2048]{1,0:T(8,128)(2,1)S(1)}, bf16[32,2048]{1,0:T(8,128)(2,1)S(1)}, u32[]{:S(2)}, u32[]{:S(2)}) %collective-permute-start.21) | collective-permute-done | bytes 131104 | tf_op jit(solution)/shard_map/ppermute | solution.py:513
  55.6 0.9 %result.1 = (f32[64,1536]{1,0:T(8,128)}, f32[64,512]{1,0:T(8,128)}, f32[1,64]{1,0:T(1,128)}) custom-call(bf16[32,2048]{1,0:T(8,128)(2,1)S(1)} %add_pairs.1.held_ref, bf16[32,2048]{1,0:T(8,128)(2,1)S(1)} %collective-permute-done.21.got_ref, bf16[64,1536]{1,0:T(8,128)(2,1)S(1)} %get-tuple-element.118.w_ref, f32[1,512]{1,0:T(1,128)S(1)} %bitcast.8), custom_call_target="tpu_custom_call" | custom-call | tf_op jit(solution)/shard_map/result/pallas_call | solution.py:499
  (12 shorter events, 0.2 us)
Async XLA Ops:
  1.9 14.2 %collective-permute-start.1 = (bf16[2,128,512]{2,1,0:T(8,128)(2,1)S(1)}, bf16[2,128,512]{2,1,0:T(8,128)(2,1)S(1)}, u32[]{:S(2)}, u32[]{:S(2)}) collective-permute-start(bf16[2,128,512]{2,1,0:T(8,128)(2,1)S(1)} %get-tuple-element.68), channel_id=1, source_target_pairs={{0,16},{4,20},{8,24},{12,28},{16,0},{20,4},{24,8},{28,12},{1,17},{... | collective-permute-start | bytes 786440 | tf_op jit(solution)/shard_map/ppermute | solution.py:513
  4.9 11.1 %collective-permute-start.2 = (bf16[2,128,512]{2,1,0:T(8,128)(2,1)S(1)}, bf16[2,128,512]{2,1,0:T(8,128)(2,1)S(1)}, u32[]{:S(2)}, u32[]{:S(2)}) collective-permute-start(bf16[2,128,512]{2,1,0:T(8,128)(2,1)S(1)} %get-tuple-element.69), channel_id=1, source_target_pairs={{0,8},{4,12},{8,0},{12,4},{16,24},{20,28},{24,16},{28,20},{1,9},{5... | collective-permute-start | bytes 786440 | tf_op jit(solution)/shard_map/ppermute | solution.py:513
  6.4 11.7 %collective-permute-start = (bf16[2,128,512]{2,1,0:T(8,128)(2,1)S(1)}, bf16[2,128,512]{2,1,0:T(8,128)(2,1)S(1)}, u32[]{:S(2)}, u32[]{:S(2)}) collective-permute-start(bf16[2,128,512]{2,1,0:T(8,128)(2,1)S(1)} %get-tuple-element.63), channel_id=1, source_target_pairs={{0,24},{4,28},{8,16},{12,20},{16,8},{20,12},{24,0},{28,4},{1,25},{... | collective-permute-start | bytes 786440 | tf_op jit(solution)/shard_map/ppermute | solution.py:513
  14.1 1.5 %collective-permute-start.3 = (bf16[4,64,384]{2,1,0:T(8,128)(2,1)S(1)}, bf16[4,64,384]{2,1,0:T(8,128)(2,1)S(1)}, u32[]{:S(2)}, u32[]{:S(2)}) collective-permute-start(bf16[4,64,384]{2,1,0:T(8,128)(2,1)S(1)} %get-tuple-element.72), channel_id=1, source_target_pairs={{0,4},{4,0},{8,12},{12,8},{16,20},{20,16},{24,28},{28,24},{1,5},{5... | collective-permute-start | bytes 589832 | tf_op jit(solution)/shard_map/ppermute | solution.py:513
  14.2 1.7 %collective-permute-start.4 = (bf16[4,64,384]{2,1,0:T(8,128)(2,1)S(1)}, bf16[4,64,384]{2,1,0:T(8,128)(2,1)S(1)}, u32[]{:S(2)}, u32[]{:S(2)}) collective-permute-start(bf16[4,64,384]{2,1,0:T(8,128)(2,1)S(1)} %get-tuple-element.73), channel_id=1, source_target_pairs={{0,4},{4,0},{8,12},{12,8},{16,20},{20,16},{24,28},{28,24},{1,5},{5... | collective-permute-start | bytes 589832 | tf_op jit(solution)/shard_map/ppermute | solution.py:513
  15.9 4.2 %copy-start = (f32[512]{0:T(512)S(1)}, f32[512]{0:T(512)}, u32[]{:S(2)}) copy-start(f32[512]{0:T(512)} %param.6) | copy-start | bytes 6148
  18.2 2.0 %collective-permute-start.5 = (bf16[4,2,64,512]{3,2,1,0:T(8,128)(2,1)S(1)}, bf16[4,2,64,512]{3,2,1,0:T(8,128)(2,1)S(1)}, u32[]{:S(2)}, u32[]{:S(2)}) collective-permute-start(bf16[4,2,64,512]{3,2,1,0:T(8,128)(2,1)S(1)} %pack_other_core.1), channel_id=1, source_target_pairs={{0,4},{4,0},{8,12},{12,8},{16,20},{20,16},{24,28},{28,24},{1,5},{5... | collective-permute-start | bytes 1572872 | tf_op jit(solution)/shard_map/ppermute | solution.py:513
  23.2 3.0 %collective-permute-start.11 = (bf16[4,64,1280]{2,1,0:T(8,128)(2,1)S(1)}, bf16[4,64,1280]{2,1,0:T(8,128)(2,1)S(1)}, u32[]{:S(2)}, u32[]{:S(2)}) collective-permute-start(bf16[4,64,1280]{2,1,0:T(8,128)(2,1)S(1)} %get-tuple-element.99), channel_id=1, source_target_pairs={{0,4},{4,0},{8,12},{12,8},{16,20},{20,16},{24,28},{28,24},{1,5},{5... | collective-permute-start | bytes 1966088 | tf_op jit(solution)/shard_map/ppermute | solution.py:513
  24.0 5.9 %collective-permute-start.6 = (bf16[4,64,512]{2,1,0:T(8,128)(2,1)S(1)}, bf16[4,64,512]{2,1,0:T(8,128)(2,1)S(1)}, u32[]{:S(2)}, u32[]{:S(2)}) collective-permute-start(bf16[4,64,512]{2,1,0:T(8,128)(2,1)S(1)} %get-tuple-element.88), channel_id=1, source_target_pairs={{0,4},{4,0},{8,12},{12,8},{16,20},{20,16},{24,28},{28,24},{1,5},{5... | collective-permute-start | bytes 786440 | tf_op jit(solution)/shard_map/ppermute | solution.py:513
  24.5 6.9 %collective-permute-start.7 = (bf16[4,32,768]{2,1,0:T(8,128)(2,1)S(1)}, bf16[4,32,768]{2,1,0:T(8,128)(2,1)S(1)}, u32[]{:S(2)}, u32[]{:S(2)}) collective-permute-start(bf16[4,32,768]{2,1,0:T(8,128)(2,1)S(1)} %get-tuple-element.100), channel_id=1, source_target_pairs={{0,1},{1,0},{2,3},{3,2},{4,5},{5,4},{6,7},{7,6},{8,9},{9,8},{10,11... | collective-permute-start | bytes 589832 | tf_op jit(solution)/shard_map/ppermute | solution.py:513
  26.4 8.3 %collective-permute-start.12 = (bf16[64,1280]{1,0:T(8,128)(2,1)S(1)}, bf16[64,1280]{1,0:T(8,128)(2,1)S(1)}, u32[]{:S(2)}, u32[]{:S(2)}) collective-permute-start(bf16[64,1280]{1,0:T(8,128)(2,1)S(1)} %get-tuple-element.107), channel_id=1, source_target_pairs={{0,24},{4,28},{8,16},{12,20},{16,8},{20,12},{24,0},{28,4},{1,25},{... | collective-permute-start | bytes 491528 | tf_op jit(solution)/shard_map/ppermute | solution.py:513
  28.9 8.5 %collective-permute-start.13 = (bf16[64,1280]{1,0:T(8,128)(2,1)S(1)}, bf16[64,1280]{1,0:T(8,128)(2,1)S(1)}, u32[]{:S(2)}, u32[]{:S(2)}) collective-permute-start(bf16[64,1280]{1,0:T(8,128)(2,1)S(1)} %get-tuple-element.108), channel_id=1, source_target_pairs={{0,16},{4,20},{8,24},{12,28},{16,0},{20,4},{24,8},{28,12},{1,17},{... | collective-permute-start | bytes 491528 | tf_op jit(solution)/shard_map/ppermute | solution.py:513
  29.4 8.6 %collective-permute-start.14 = (bf16[64,1280]{1,0:T(8,128)(2,1)S(1)}, bf16[64,1280]{1,0:T(8,128)(2,1)S(1)}, u32[]{:S(2)}, u32[]{:S(2)}) collective-permute-start(bf16[64,1280]{1,0:T(8,128)(2,1)S(1)} %get-tuple-element.109), channel_id=1, source_target_pairs={{0,8},{4,12},{8,0},{12,4},{16,24},{20,28},{24,16},{28,20},{1,9},{5... | collective-permute-start | bytes 491528 | tf_op jit(solution)/shard_map/ppermute | solution.py:513
  31.5 8.7 %collective-permute-start.8 = (bf16[32,768]{1,0:T(8,128)(2,1)S(1)}, bf16[32,768]{1,0:T(8,128)(2,1)S(1)}, u32[]{:S(2)}, u32[]{:S(2)}) collective-permute-start(bf16[32,768]{1,0:T(8,128)(2,1)S(1)} %get-tuple-element.102), channel_id=1, source_target_pairs={{0,24},{4,28},{8,16},{12,20},{16,8},{20,12},{24,0},{28,4},{1,25},{... | collective-permute-start | bytes 147464 | tf_op jit(solution)/shard_map/ppermute | solution.py:513
  34.1 6.0 %collective-permute-start.9 = (bf16[32,768]{1,0:T(8,128)(2,1)S(1)}, bf16[32,768]{1,0:T(8,128)(2,1)S(1)}, u32[]{:S(2)}, u32[]{:S(2)}) collective-permute-start(bf16[32,768]{1,0:T(8,128)(2,1)S(1)} %get-tuple-element.103), channel_id=1, source_target_pairs={{0,16},{4,20},{8,24},{12,28},{16,0},{20,4},{24,8},{28,12},{1,17},{... | collective-permute-start | bytes 147464 | tf_op jit(solution)/shard_map/ppermute | solution.py:513
  34.6 5.5 %collective-permute-start.10 = (bf16[32,768]{1,0:T(8,128)(2,1)S(1)}, bf16[32,768]{1,0:T(8,128)(2,1)S(1)}, u32[]{:S(2)}, u32[]{:S(2)}) collective-permute-start(bf16[32,768]{1,0:T(8,128)(2,1)S(1)} %get-tuple-element.104), channel_id=1, source_target_pairs={{0,8},{4,12},{8,0},{12,4},{16,24},{20,28},{24,16},{28,20},{1,9},{5... | collective-permute-start | bytes 147464 | tf_op jit(solution)/shard_map/ppermute | solution.py:513
  38.0 4.1 %collective-permute-start.15 = (bf16[32,640]{1,0:T(8,128)(2,1)S(1)}, bf16[32,640]{1,0:T(8,128)(2,1)S(1)}, u32[]{:S(2)}, u32[]{:S(2)}) collective-permute-start(bf16[32,640]{1,0:T(8,128)(2,1)S(1)} %get-tuple-element.111), channel_id=1, source_target_pairs={{0,1},{1,0},{2,3},{3,2},{4,5},{5,4},{6,7},{7,6},{8,9},{9,8},{10,11... | collective-permute-start | bytes 122888 | tf_op jit(solution)/shard_map/ppermute | solution.py:513
  39.0 4.0 %collective-permute-start.16 = (bf16[32,640]{1,0:T(8,128)(2,1)S(1)}, bf16[32,640]{1,0:T(8,128)(2,1)S(1)}, u32[]{:S(2)}, u32[]{:S(2)}) collective-permute-start(bf16[32,640]{1,0:T(8,128)(2,1)S(1)} %get-tuple-element.112), channel_id=1, source_target_pairs={{0,1},{1,0},{2,3},{3,2},{4,5},{5,4},{6,7},{7,6},{8,9},{9,8},{10,11... | collective-permute-start | bytes 122888 | tf_op jit(solution)/shard_map/ppermute | solution.py:513
  43.1 7.4 %collective-permute-start.20 = (bf16[32,2048]{1,0:T(8,128)(2,1)S(1)}, bf16[32,2048]{1,0:T(8,128)(2,1)S(1)}, u32[]{:S(2)}, u32[]{:S(2)}) collective-permute-start(bf16[32,2048]{1,0:T(8,128)(2,1)S(1)} %join_terms.1.kept_ref), channel_id=1, source_target_pairs={{0,2},{1,3},{2,0},{3,1},{4,6},{5,7},{6,4},{7,5},{8,10},{9,11},{10,... | collective-permute-start | bytes 393224 | tf_op jit(solution)/shard_map/ppermute | solution.py:513
  45.7 6.1 %collective-permute-start.17 = (bf16[128,512]{1,0:T(8,128)(2,1)S(1)}, bf16[128,512]{1,0:T(8,128)(2,1)S(1)}, u32[]{:S(2)}, u32[]{:S(2)}) collective-permute-start(bf16[128,512]{1,0:T(8,128)(2,1)S(1)} %get-tuple-element.114), channel_id=1, source_target_pairs={{0,24},{4,28},{8,16},{12,20},{16,8},{20,12},{24,0},{28,4},{1,25},{... | collective-permute-start | bytes 393224 | tf_op jit(solution)/shard_map/ppermute | solution.py:513
  48.1 5.2 %collective-permute-start.18 = (bf16[128,512]{1,0:T(8,128)(2,1)S(1)}, bf16[128,512]{1,0:T(8,128)(2,1)S(1)}, u32[]{:S(2)}, u32[]{:S(2)}) collective-permute-start(bf16[128,512]{1,0:T(8,128)(2,1)S(1)} %get-tuple-element.115), channel_id=1, source_target_pairs={{0,16},{4,20},{8,24},{12,28},{16,0},{20,4},{24,8},{28,12},{1,17},{... | collective-permute-start | bytes 393224 | tf_op jit(solution)/shard_map/ppermute | solution.py:513
  48.7 5.0 %collective-permute-start.19 = (bf16[128,512]{1,0:T(8,128)(2,1)S(1)}, bf16[128,512]{1,0:T(8,128)(2,1)S(1)}, u32[]{:S(2)}, u32[]{:S(2)}) collective-permute-start(bf16[128,512]{1,0:T(8,128)(2,1)S(1)} %get-tuple-element.116), channel_id=1, source_target_pairs={{0,8},{4,12},{8,0},{12,4},{16,24},{20,28},{24,16},{28,20},{1,9},{5... | collective-permute-start | bytes 393224 | tf_op jit(solution)/shard_map/ppermute | solution.py:513
  50.5 5.0 %collective-permute-start.21 = (bf16[32,2048]{1,0:T(8,128)(2,1)S(1)}, bf16[32,2048]{1,0:T(8,128)(2,1)S(1)}, u32[]{:S(2)}, u32[]{:S(2)}) collective-permute-start(bf16[32,2048]{1,0:T(8,128)(2,1)S(1)} %add_pairs.1.held_ref), channel_id=1, source_target_pairs={{0,1},{1,0},{2,3},{3,2},{4,5},{5,4},{6,7},{7,6},{8,9},{9,8},{10,11... | collective-permute-start | bytes 393224 | tf_op jit(solution)/shard_map/ppermute | solution.py:513

commit v12 on v10

--- a/solution.py
+++ b/solution.py
@@ -21,7 +21,7 @@
 VMEM = pl.BlockSpec(memory_space=pltpu.VMEM)
 HBM = pl.BlockSpec(memory_space=pltpu.HBM)
 CHIP_STEPS = (3, 2, 1)
-FIRST_PART = 640
+FIRST_PART = 384
 PINNED = pl.BlockSpec(memory_space=pltpu.VMEM)
 shaped = jax.ShapeDtypeStruct
 
@@ -416,11 +416,10 @@
     finished(*started(*copies))
 
 
-def split_rows(total, axis, send_ref, kept_ref):
+def split_rows(total, axis):
     upper = (here()[2] & 1) == 1
     low, high = jnp.split(total, 2, axis)
-    send_ref[...] = jnp.where(upper, low, high).astype(BF16)
-    kept_ref[...] = jnp.where(upper, high, low)
+    return jnp.where(upper, low, high).astype(BF16), jnp.where(upper, high, low)
 
 
 def row_cores_kernel(keep_1, keep_2, got_1, got_2, send_ref, kept_ref):
@@ -428,13 +427,13 @@
         keep_ref[...].astype(F32) + got_ref[...].astype(F32)
         for keep_ref, got_ref in ((keep_1, got_1), (keep_2, got_2))
     ]
-    split_rows(jnp.concatenate(total, 2), 1, send_ref, kept_ref)
+    send_ref[...], kept_ref[...] = split_rows(jnp.concatenate(total, 2), 1)
 
 
 def cores_kernel(keep_ref, got_ref, send_ref, kept_ref, *targets):
     chip, cut = here()[0], kept_ref.shape[2]
     first = keep_ref[:, :, :cut].astype(F32) + got_ref[:, :, :cut].astype(F32)
-    split_rows(first, 1, send_ref, kept_ref)
+    send_ref[...], kept_ref[...] = split_rows(first, 1)
     for step, target in zip((0, *CHIP_STEPS), targets):
         there = chip ^ step
         total = keep_ref[there, :, cut:].astype(F32) + got_ref[there, :, cut:].astype(F32)
@@ -458,7 +457,7 @@
 
 
 def layer_kernel(own_ref, got_1, got_2, got_3, send_ref, kept_ref):
-    split_rows(layer_sum(own_ref, got_1, got_2, got_3), 0, send_ref, kept_ref)
+    send_ref[...], kept_ref[...] = split_rows(layer_sum(own_ref, got_1, got_2, got_3), 0)
 
 
 def join_kernel(own_ref, got_1, got_2, got_3, kept_ref, got_ref, out_ref):
@@ -620,7 +619,6 @@
             [(VMEM, one) for one in (x_near, cot_near, *near)],
             [((chips, 2, share, width), BF16)],
         )
-        row_got = swap(row_next, "dp", 1)
         send, keep, col_grads = call(
             column_chip_kernel,
             "column_heads",
@@ -641,17 +639,18 @@
             [(VMEM, col_grads), (VMEM, col_weight)],
             [((chips, share, width), BF16)] * 2,
         )
-        send, row_got, back_keep = lax.optimization_barrier((send, row_got, back_keep))
+        row_next, _ = lax.optimization_barrier((row_next, send))
+        keep, back_keep = lax.optimization_barrier((keep, back_keep))
         first_half = (chips, row_share // 2, FIRST_PART)
         second = (row_share, col_width - FIRST_PART)
-        to_next, kept, *parts = call(
+        to_next, kept, owned, *off = call(
             cores_kernel,
             "column_add_cores",
             [(VMEM, keep), (VMEM, swap(send, "seq", 1))],
             [(first_half, BF16), (first_half, F32), (second, F32)] + [(second, BF16)] * 3,
             out_specs=[VMEM, PINNED, PINNED, VMEM, VMEM, VMEM],
         )
-        layer_got = cross_chips(*parts[1:])
+        got = cross_chips(*off)
         back = call(
             back_pack_kernel,
             "pack_grad_hidden",
@@ -660,26 +659,29 @@
         )
         row_kept, *back = lax.optimization_barrier((row_kept, *back))
         joint = (row_share // 2, FIRST_PART + row_width)
-        owned, *off = call(
+        first_owned, *off = call(
             pair_kernel,
             "first_add_pair",
-            [(VMEM, one) for one in (kept, swap(to_next, "dp", 1), row_kept, row_got)],
+            [
+                (VMEM, one)
+                for one in (kept, swap(to_next, "dp", 1), row_kept, swap(row_next, "dp", 1))
+            ],
             [(joint, F32)] + [(joint, BF16)] * 3,
             out_specs=[PINNED, VMEM, VMEM, VMEM],
         )
-        got = cross_chips(*off)
-        half_second = (row_share // 2, second[1])
+        first_got = cross_chips(*off)
+        second_half = (row_share // 2, second[1])
         to_next, kept = call(
             layer_kernel,
             "second_add_chips",
-            [(VMEM, one) for one in (parts[0], *layer_got)],
-            [(half_second, BF16), (half_second, F32)],
+            [(VMEM, one) for one in (owned, *got)],
+            [(second_half, BF16), (second_half, F32)],
             out_specs=[VMEM, PINNED],
         )
         (pair_sum,) = call(
             join_kernel,
             "join_terms",
-            [(VMEM, one) for one in (owned, *got, kept, swap(to_next, "dp", 1))],
+            [(VMEM, one) for one in (first_owned, *first_got, kept, swap(to_next, "dp", 1))],
             [((row_share // 2, col_width + row_width), BF16)],
         )
         *back, pair_sum = lax.optimization_barrier((*back, pair_sum))

time: 56.5 us -> 55.1 us (0.975)
  waiting for transfers between devices: 15.8 us -> 14.5 us
    ppermute x22, waiting for transfers between devices: 15.8 us -> 14.5 us  [swap(): return lax.ppermute(array, axis, [(i, i ^ bits) for i in range(count)])]
  transfers between devices with their start and end apart: 22 -> 22, of which waited for: 12 -> 12; matrix products, arithmetic and copies ran while one was open for 0% -> 0% of each run, Pallas kernels for 23% -> 18%
where the time goes in v12:
time: 55.1 us; the launch traced here: 54.9 us
  starting transfers between devices  24.4 us (44%)
  Pallas kernels  15.2 us (28%)
  waiting for transfers between devices  14.5 us (26%)
  between operations  0.75 us (1%)
    ppermute x22, starting transfers between devices, swap(): return lax.ppermute(array, axis, [(i, i ^ bits) for i in range(count)])  24.4 us
    pallas_call x14, Pallas kernels, call(): pl.pallas_call(kernel, out_shape=outs, in_specs=[spec for spec, _ in ins]...  15.2 us
    ppermute x22, waiting for transfers between devices, swap(): return lax.ppermute(array, axis, [(i, i ^ bits) for i in range(count)])  14.5 us
  transfers between devices with their start and end apart: 22, of which 12 were waited for; matrix products, arithmetic and copies ran while one was open for 0% of the time, Pallas kernels for 18%

profile of v12, /device:TPU:0, one launch (start us, length us, event | category | flops | bytes accessed | tf_op | source)
XLA Modules:
  0.0 54.9 jit_solution(3867589721392007110)
XLA Ops:
  0.6 1.3 %pack_columns.1 = (bf16[2,128,512]{2,1,0:T(8,128)(2,1)S(1)}, bf16[2,128,512]{2,1,0:T(8,128)(2,1)S(1)}, bf16[2,128,512]{2,1,0:T(8,128)(2,1)S(1)}) custom-call(bf16[512,512]{1,0:T(8,128)(2,1)} %bitcast.9, bf16[512,512]{1,0:T(8,128)(2,1)} %bitcast.11), custom_call_target="tpu_custom_call" | custom-call | tf_op jit(solution)/shard_map/pack_columns/pallas_call | solution.py:511
  1.9 3.0 %collective-permute-start.1 = (bf16[2,128,512]{2,1,0:T(8,128)(2,1)S(1)}, bf16[2,128,512]{2,1,0:T(8,128)(2,1)S(1)}, u32[]{:S(2)}, u32[]{:S(2)}) collective-permute-start(bf16[2,128,512]{2,1,0:T(8,128)(2,1)S(1)} %get-tuple-element.69), channel_id=1, source_target_pairs={{0,16},{4,20},{8,24},{12,28},{16,0},{20,4},{24,8},{28,12},{1,17},{... | collective-permute-start | bytes 786440 | tf_op jit(solution)/shard_map/ppermute | solution.py:525
  4.9 1.5 %collective-permute-start.2 = (bf16[2,128,512]{2,1,0:T(8,128)(2,1)S(1)}, bf16[2,128,512]{2,1,0:T(8,128)(2,1)S(1)}, u32[]{:S(2)}, u32[]{:S(2)}) collective-permute-start(bf16[2,128,512]{2,1,0:T(8,128)(2,1)S(1)} %get-tuple-element.70), channel_id=1, source_target_pairs={{0,8},{4,12},{8,0},{12,4},{16,24},{20,28},{24,16},{28,20},{1,9},{5... | collective-permute-start | bytes 786440 | tf_op jit(solution)/shard_map/ppermute | solution.py:525
  6.4 0.0 collective-permute-start
  6.5 7.7 %row_heads.1 = (bf16[4,64,384]{2,1,0:T(8,128)(2,1)S(1)}, bf16[4,64,384]{2,1,0:T(8,128)(2,1)S(1)}, bf16[4,64,384]{2,1,0:T(8,128)(2,1)S(1)}, bf16[4,64,384]{2,1,0:...) custom-call(bf16[512,512]{1,0:T(8,128)(2,1)} %bitcast.10, ...), custom_call_target="tpu_custom_call" | custom-call | tf_op jit(solution)/shard_map/row_heads/pallas_call | solution.py:511
  14.1 0.1 collective-permute-start.3
  14.2 0.5 collective-permute-start.4
  14.7 0.9 %collective-permute-done.3.got_1 = bf16[4,64,384]{2,1,0:T(8,128)(2,1)S(1)} collective-permute-done((bf16[4,64,384]{2,1,0:T(8,128)(2,1)S(1)}, bf16[4,64,384]{2,1,0:T(8,128)(2,1)S(1)}, u32[]{:S(2)}, u32[]{:S(2)}) %collective-permute-start.3) | collective-permute-done | bytes 196640 | tf_op jit(solution)/shard_map/ppermute | solution.py:525
  15.6 0.3 collective-permute-done.4.got_2
  15.9 0.1 row_add_cores.1
  16.1 0.0 collective-permute-done.2.near_3
  16.1 2.0 %collective-permute-done.near_1 = bf16[2,128,512]{2,1,0:T(8,128)(2,1)S(1)} collective-permute-done((bf16[2,128,512]{2,1,0:T(8,128)(2,1)S(1)}, bf16[2,128,512]{2,1,0:T(8,128)(2,1)S(1)}, u32[]{:S(2)}, u32[]{:S(2)}) %collective-permute-start) | collective-permute-done | bytes 262176 | tf_op jit(solution)/shard_map/ppermute | solution.py:525
  18.2 0.1 collective-permute-start.5
  18.2 1.9 %collective-permute-done.5.far_ref = bf16[4,2,64,512]{3,2,1,0:T(8,128)(2,1)S(1)} collective-permute-done((bf16[4,2,64,512]{3,2,1,0:T(8,128)(2,1)S(1)}, bf16[4,2,64,512]{3,2,1,0:T(8,128)(2,1)S(1)}, u32[]{:S(2)}, u32[]{:S(2)}) %collective-permute-start.5) | collective-permute-done | bytes 524320 | tf_op jit(solution)/shard_map/ppermute | solution.py:525
  20.1 3.1 %column_heads.1 = (bf16[4,64,1280]{2,1,0:T(8,128)(2,1)S(1)}, bf16[4,64,1280]{2,1,0:T(8,128)(2,1)S(1)}, bf16[512,768]{1,0:T(8,128)(2,1)S(1)}) custom-call(bf16[512,512]{1,0:T(8,128)(2,1)S(1)} %get-tuple-element.77.x_ref, bf16[512,512]{1,0:T(8,128)(2,1)S(1)} %get-tuple-element.78.cot_ref, bf16[2,128,512]{2,1,0:T(8,128)(2,1)S(1)} %collective-permute-done.near_1, ...), custom_call_target="tpu_custom_call" | custom-call | tf_op jit(solution)/shard_map/column_heads/pallas_call | solution.py:511
  23.2 0.2 collective-permute-start.7
  23.4 0.6 %column_grad_hidden.1 = (bf16[4,64,512]{2,1,0:T(8,128)(2,1)S(1)}, bf16[4,64,512]{2,1,0:T(8,128)(2,1)S(1)}) custom-call(bf16[512,768]{1,0:T(8,128)(2,1)S(1)} %get-tuple-element.86.grads_ref, bf16[512,768]{1,0:T(8,128)(2,1)S(1)} %get-tuple-element.82.w_ref), custom_call_target="tpu_custom_call" | custom-call | tf_op jit(solution)/shard_map/column_grad_hidden/pallas_call | solution.py:511
  24.0 0.4 collective-permute-start.6
  24.5 1.7 %collective-permute-start.9 = (bf16[4,32,768]{2,1,0:T(8,128)(2,1)S(1)}, bf16[4,32,768]{2,1,0:T(8,128)(2,1)S(1)}, u32[]{:S(2)}, u32[]{:S(2)}) collective-permute-start(bf16[4,32,768]{2,1,0:T(8,128)(2,1)S(1)} %get-tuple-element.104), channel_id=1, source_target_pairs={{0,1},{1,0},{2,3},{3,2},{4,5},{5,4},{6,7},{7,6},{8,9},{9,8},{10,11... | collective-permute-start | bytes 589832 | tf_op jit(solution)/shard_map/ppermute | solution.py:525
  26.2 0.2 column_add_cores.1
  26.4 2.5 %collective-permute-start.13 = (bf16[64,896]{1,0:T(8,128)(2,1)S(1)}, bf16[64,896]{1,0:T(8,128)(2,1)S(1)}, u32[]{:S(2)}, u32[]{:S(2)}) collective-permute-start(bf16[64,896]{1,0:T(8,128)(2,1)S(1)} %get-tuple-element.110), channel_id=1, source_target_pairs={{0,24},{4,28},{8,16},{12,20},{16,8},{20,12},{24,0},{28,4},{1,25},{... | collective-permute-start | bytes 344072 | tf_op jit(solution)/shard_map/ppermute | solution.py:525
  28.9 0.9 %collective-permute-start.8 = (bf16[4,32,384]{2,1,0:T(8,128)(2,1)S(1)}, bf16[4,32,384]{2,1,0:T(8,128)(2,1)S(1)}, u32[]{:S(2)}, u32[]{:S(2)}) collective-permute-start(bf16[4,32,384]{2,1,0:T(8,128)(2,1)S(1)} %get-tuple-element.101), channel_id=1, source_target_pairs={{0,1},{1,0},{2,3},{3,2},{4,5},{5,4},{6,7},{7,6},{8,9},{9,8},{10,11... | collective-permute-start | bytes 294920 | tf_op jit(solution)/shard_map/ppermute | solution.py:525
  29.8 0.5 collective-permute-start.14
  30.3 0.5 collective-permute-start.15
  30.9 0.8 %collective-permute-done.9.row_got = bf16[4,32,768]{2,1,0:T(8,128)(2,1)S(1)} collective-permute-done((bf16[4,32,768]{2,1,0:T(8,128)(2,1)S(1)}, bf16[4,32,768]{2,1,0:T(8,128)(2,1)S(1)}, u32[]{:S(2)}, u32[]{:S(2)}) %collective-permute-start.9) | collective-permute-done | bytes 196640 | tf_op jit(solution)/shard_map/ppermute | solution.py:525
  31.7 1.8 %collective-permute-done.8.got_ref = bf16[4,32,384]{2,1,0:T(8,128)(2,1)S(1)} collective-permute-done((bf16[4,32,384]{2,1,0:T(8,128)(2,1)S(1)}, bf16[4,32,384]{2,1,0:T(8,128)(2,1)S(1)}, u32[]{:S(2)}, u32[]{:S(2)}) %collective-permute-start.8) | collective-permute-done | bytes 98336 | tf_op jit(solution)/shard_map/ppermute | solution.py:525
  33.5 0.1 first_add_pair.1
  33.6 2.7 %collective-permute-start.10 = (bf16[32,1152]{1,0:T(8,128)(2,1)S(1)}, bf16[32,1152]{1,0:T(8,128)(2,1)S(1)}, u32[]{:S(2)}, u32[]{:S(2)}) collective-permute-start(bf16[32,1152]{1,0:T(8,128)(2,1)S(1)} %get-tuple-element.106), channel_id=1, source_target_pairs={{0,24},{4,28},{8,16},{12,20},{16,8},{20,12},{24,0},{28,4},{1,25},{... | collective-permute-start | bytes 221192 | tf_op jit(solution)/shard_map/ppermute | solution.py:525
  36.3 0.5 collective-permute-start.11
  36.8 0.0 collective-permute-done.13.got_1
  36.8 0.4 collective-permute-start.12
  37.2 0.0 collective-permute-done.14.got_2
  37.2 0.1 second_add_chips.1
  37.2 1.8 %collective-permute-start.16 = (bf16[32,896]{1,0:T(8,128)(2,1)S(1)}, bf16[32,896]{1,0:T(8,128)(2,1)S(1)}, u32[]{:S(2)}, u32[]{:S(2)}) collective-permute-start(bf16[32,896]{1,0:T(8,128)(2,1)S(1)} %get-tuple-element.114), channel_id=1, source_target_pairs={{0,1},{1,0},{2,3},{3,2},{4,5},{5,4},{6,7},{7,6},{8,9},{9,8},{10,11... | collective-permute-start | bytes 172040 | tf_op jit(solution)/shard_map/ppermute | solution.py:525
  39.0 2.5 %collective-permute-done.16.got_ref = bf16[32,896]{1,0:T(8,128)(2,1)S(1)} collective-permute-done((bf16[32,896]{1,0:T(8,128)(2,1)S(1)}, bf16[32,896]{1,0:T(8,128)(2,1)S(1)}, u32[]{:S(2)}, u32[]{:S(2)}) %collective-permute-start.16) | collective-permute-done | bytes 57376 | tf_op jit(solution)/shard_map/ppermute | solution.py:525
  41.5 0.1 join_terms.1.kept_ref
  41.5 2.8 %collective-permute-start.20 = (bf16[32,2048]{1,0:T(8,128)(2,1)S(1)}, bf16[32,2048]{1,0:T(8,128)(2,1)S(1)}, u32[]{:S(2)}, u32[]{:S(2)}) collective-permute-start(bf16[32,2048]{1,0:T(8,128)(2,1)S(1)} %join_terms.1.kept_ref), channel_id=1, source_target_pairs={{0,2},{1,3},{2,0},{3,1},{4,6},{5,7},{6,4},{7,5},{8,10},{9,11},{10,... | collective-permute-start | bytes 393224 | tf_op jit(solution)/shard_map/ppermute | solution.py:525
  44.3 2.5 %collective-permute-start.17 = (bf16[128,512]{1,0:T(8,128)(2,1)S(1)}, bf16[128,512]{1,0:T(8,128)(2,1)S(1)}, u32[]{:S(2)}, u32[]{:S(2)}) collective-permute-start(bf16[128,512]{1,0:T(8,128)(2,1)S(1)} %get-tuple-element.116), channel_id=1, source_target_pairs={{0,24},{4,28},{8,16},{12,20},{16,8},{20,12},{24,0},{28,4},{1,25},{... | collective-permute-start | bytes 393224 | tf_op jit(solution)/shard_map/ppermute | solution.py:525
  46.8 0.5 collective-permute-start.18
  47.3 0.5 collective-permute-start.19
  47.8 1.2 %collective-permute-done.20.got_ref = bf16[32,2048]{1,0:T(8,128)(2,1)S(1)} collective-permute-done((bf16[32,2048]{1,0:T(8,128)(2,1)S(1)}, bf16[32,2048]{1,0:T(8,128)(2,1)S(1)}, u32[]{:S(2)}, u32[]{:S(2)}) %collective-permute-start.20) | collective-permute-done | bytes 131104 | tf_op jit(solution)/shard_map/ppermute | solution.py:525
  49.0 0.8 %collective-permute-start.21 = (bf16[32,2048]{1,0:T(8,128)(2,1)S(1)}, bf16[32,2048]{1,0:T(8,128)(2,1)S(1)}, u32[]{:S(2)}, u32[]{:S(2)}) collective-permute-start(bf16[32,2048]{1,0:T(8,128)(2,1)S(1)} %add_pairs.1.held_ref), channel_id=1, source_target_pairs={{0,1},{1,0},{2,3},{3,2},{4,5},{5,4},{6,7},{7,6},{8,9},{9,8},{10,11... | collective-permute-start | bytes 393224 | tf_op jit(solution)/shard_map/ppermute | solution.py:525
  49.8 0.6 %collective-permute-done.17.got_1 = bf16[128,512]{1,0:T(8,128)(2,1)S(1)} collective-permute-done((bf16[128,512]{1,0:T(8,128)(2,1)S(1)}, bf16[128,512]{1,0:T(8,128)(2,1)S(1)}, u32[]{:S(2)}, u32[]{:S(2)}) %collective-permute-start.17) | collective-permute-done | bytes 131104 | tf_op jit(solution)/shard_map/ppermute | solution.py:525
  50.4 1.4 %collective-permute-done.18.got_2 = bf16[128,512]{1,0:T(8,128)(2,1)S(1)} collective-permute-done((bf16[128,512]{1,0:T(8,128)(2,1)S(1)}, bf16[128,512]{1,0:T(8,128)(2,1)S(1)}, u32[]{:S(2)}, u32[]{:S(2)}) %collective-permute-start.18) | collective-permute-done | bytes 131104 | tf_op jit(solution)/shard_map/ppermute | solution.py:525
  51.8 0.4 collective-permute-done.19.got_3
  52.3 1.2 %input_grad.1 = bf16[512,512]{1,0:T(8,128)(2,1)} custom-call(f32[512,512]{1,0:T(8,128)S(1)} %get-tuple-element.66.base_ref, f32[512,512]{1,0:T(8,128)S(1)} %get-tuple-element.67.normed_ref, f32[512,1]{1,0:T(8,128)S(1)} %get-tuple-element.68.inverse_ref, f32[1,512]{1,0:T(1,128)S(1)} %bitcast.7, bf16[128,512]{1,0:T(8,128)(2,1)S(1)} %get-tuple-element.115.own_ref, ...), custom_call_target="tpu_custom_call" | custom-call | tf_op jit(solution)/shard_map/input_grad/pallas_call | solution.py:511
  53.4 0.6 %collective-permute-done.21.got_ref = bf16[32,2048]{1,0:T(8,128)(2,1)S(1)} collective-permute-done((bf16[32,2048]{1,0:T(8,128)(2,1)S(1)}, bf16[32,2048]{1,0:T(8,128)(2,1)S(1)}, u32[]{:S(2)}, u32[]{:S(2)}) %collective-permute-start.21) | collective-permute-done | bytes 131104 | tf_op jit(solution)/shard_map/ppermute | solution.py:525
  54.1 0.9 %result.1 = (f32[64,1536]{1,0:T(8,128)}, f32[64,512]{1,0:T(8,128)}, f32[1,64]{1,0:T(1,128)}) custom-call(bf16[32,2048]{1,0:T(8,128)(2,1)S(1)} %add_pairs.1.held_ref, bf16[32,2048]{1,0:T(8,128)(2,1)S(1)} %collective-permute-done.21.got_ref, bf16[64,1536]{1,0:T(8,128)(2,1)S(1)} %get-tuple-element.120.w_ref, f32[1,512]{1,0:T(1,128)S(1)} %bitcast.8), custom_call_target="tpu_custom_call" | custom-call | tf_op jit(solution)/shard_map/result/pallas_call | solution.py:511
  (12 shorter events, 0.1 us)
Async XLA Ops:
  1.9 14.2 %collective-permute-start.1 = (bf16[2,128,512]{2,1,0:T(8,128)(2,1)S(1)}, bf16[2,128,512]{2,1,0:T(8,128)(2,1)S(1)}, u32[]{:S(2)}, u32[]{:S(2)}) collective-permute-start(bf16[2,128,512]{2,1,0:T(8,128)(2,1)S(1)} %get-tuple-element.69), channel_id=1, source_target_pairs={{0,16},{4,20},{8,24},{12,28},{16,0},{20,4},{24,8},{28,12},{1,17},{... | collective-permute-start | bytes 786440 | tf_op jit(solution)/shard_map/ppermute | solution.py:525
  4.9 11.1 %collective-permute-start.2 = (bf16[2,128,512]{2,1,0:T(8,128)(2,1)S(1)}, bf16[2,128,512]{2,1,0:T(8,128)(2,1)S(1)}, u32[]{:S(2)}, u32[]{:S(2)}) collective-permute-start(bf16[2,128,512]{2,1,0:T(8,128)(2,1)S(1)} %get-tuple-element.70), channel_id=1, source_target_pairs={{0,8},{4,12},{8,0},{12,4},{16,24},{20,28},{24,16},{28,20},{1,9},{5... | collective-permute-start | bytes 786440 | tf_op jit(solution)/shard_map/ppermute | solution.py:525
  6.4 11.7 %collective-permute-start = (bf16[2,128,512]{2,1,0:T(8,128)(2,1)S(1)}, bf16[2,128,512]{2,1,0:T(8,128)(2,1)S(1)}, u32[]{:S(2)}, u32[]{:S(2)}) collective-permute-start(bf16[2,128,512]{2,1,0:T(8,128)(2,1)S(1)} %get-tuple-element.64), channel_id=1, source_target_pairs={{0,24},{4,28},{8,16},{12,20},{16,8},{20,12},{24,0},{28,4},{1,25},{... | collective-permute-start | bytes 786440 | tf_op jit(solution)/shard_map/ppermute | solution.py:525
  14.1 1.5 %collective-permute-start.3 = (bf16[4,64,384]{2,1,0:T(8,128)(2,1)S(1)}, bf16[4,64,384]{2,1,0:T(8,128)(2,1)S(1)}, u32[]{:S(2)}, u32[]{:S(2)}) collective-permute-start(bf16[4,64,384]{2,1,0:T(8,128)(2,1)S(1)} %get-tuple-element.73), channel_id=1, source_target_pairs={{0,4},{4,0},{8,12},{12,8},{16,20},{20,16},{24,28},{28,24},{1,5},{5... | collective-permute-start | bytes 589832 | tf_op jit(solution)/shard_map/ppermute | solution.py:525
  14.2 1.7 %collective-permute-start.4 = (bf16[4,64,384]{2,1,0:T(8,128)(2,1)S(1)}, bf16[4,64,384]{2,1,0:T(8,128)(2,1)S(1)}, u32[]{:S(2)}, u32[]{:S(2)}) collective-permute-start(bf16[4,64,384]{2,1,0:T(8,128)(2,1)S(1)} %get-tuple-element.74), channel_id=1, source_target_pairs={{0,4},{4,0},{8,12},{12,8},{16,20},{20,16},{24,28},{28,24},{1,5},{5... | collective-permute-start | bytes 589832 | tf_op jit(solution)/shard_map/ppermute | solution.py:525
  15.9 4.2 %copy-start = (f32[512]{0:T(512)S(1)}, f32[512]{0:T(512)}, u32[]{:S(2)}) copy-start(f32[512]{0:T(512)} %param.6) | copy-start | bytes 6148
  18.2 2.0 %collective-permute-start.5 = (bf16[4,2,64,512]{3,2,1,0:T(8,128)(2,1)S(1)}, bf16[4,2,64,512]{3,2,1,0:T(8,128)(2,1)S(1)}, u32[]{:S(2)}, u32[]{:S(2)}) collective-permute-start(bf16[4,2,64,512]{3,2,1,0:T(8,128)(2,1)S(1)} %pack_other_core.1), channel_id=1, source_target_pairs={{0,4},{4,0},{8,12},{12,8},{16,20},{20,16},{24,28},{28,24},{1,5},{5... | collective-permute-start | bytes 1572872 | tf_op jit(solution)/shard_map/ppermute | solution.py:525
  23.2 3.0 %collective-permute-start.7 = (bf16[4,64,1280]{2,1,0:T(8,128)(2,1)S(1)}, bf16[4,64,1280]{2,1,0:T(8,128)(2,1)S(1)}, u32[]{:S(2)}, u32[]{:S(2)}) collective-permute-start(bf16[4,64,1280]{2,1,0:T(8,128)(2,1)S(1)} %get-tuple-element.99), channel_id=1, source_target_pairs={{0,4},{4,0},{8,12},{12,8},{16,20},{20,16},{24,28},{28,24},{1,5},{5... | collective-permute-start | bytes 1966088 | tf_op jit(solution)/shard_map/ppermute | solution.py:525
  24.0 6.3 %collective-permute-start.6 = (bf16[4,64,512]{2,1,0:T(8,128)(2,1)S(1)}, bf16[4,64,512]{2,1,0:T(8,128)(2,1)S(1)}, u32[]{:S(2)}, u32[]{:S(2)}) collective-permute-start(bf16[4,64,512]{2,1,0:T(8,128)(2,1)S(1)} %get-tuple-element.89), channel_id=1, source_target_pairs={{0,4},{4,0},{8,12},{12,8},{16,20},{20,16},{24,28},{28,24},{1,5},{5... | collective-permute-start | bytes 786440 | tf_op jit(solution)/shard_map/ppermute | solution.py:525
  24.5 7.2 %collective-permute-start.9 = (bf16[4,32,768]{2,1,0:T(8,128)(2,1)S(1)}, bf16[4,32,768]{2,1,0:T(8,128)(2,1)S(1)}, u32[]{:S(2)}, u32[]{:S(2)}) collective-permute-start(bf16[4,32,768]{2,1,0:T(8,128)(2,1)S(1)} %get-tuple-element.104), channel_id=1, source_target_pairs={{0,1},{1,0},{2,3},{3,2},{4,5},{5,4},{6,7},{7,6},{8,9},{9,8},{10,11... | collective-permute-start | bytes 589832 | tf_op jit(solution)/shard_map/ppermute | solution.py:525
  26.4 10.4 %collective-permute-start.13 = (bf16[64,896]{1,0:T(8,128)(2,1)S(1)}, bf16[64,896]{1,0:T(8,128)(2,1)S(1)}, u32[]{:S(2)}, u32[]{:S(2)}) collective-permute-start(bf16[64,896]{1,0:T(8,128)(2,1)S(1)} %get-tuple-element.110), channel_id=1, source_target_pairs={{0,24},{4,28},{8,16},{12,20},{16,8},{20,12},{24,0},{28,4},{1,25},{... | collective-permute-start | bytes 344072 | tf_op jit(solution)/shard_map/ppermute | solution.py:525
  28.9 4.6 %collective-permute-start.8 = (bf16[4,32,384]{2,1,0:T(8,128)(2,1)S(1)}, bf16[4,32,384]{2,1,0:T(8,128)(2,1)S(1)}, u32[]{:S(2)}, u32[]{:S(2)}) collective-permute-start(bf16[4,32,384]{2,1,0:T(8,128)(2,1)S(1)} %get-tuple-element.101), channel_id=1, source_target_pairs={{0,1},{1,0},{2,3},{3,2},{4,5},{5,4},{6,7},{7,6},{8,9},{9,8},{10,11... | collective-permute-start | bytes 294920 | tf_op jit(solution)/shard_map/ppermute | solution.py:525
  29.8 7.3 %collective-permute-start.14 = (bf16[64,896]{1,0:T(8,128)(2,1)S(1)}, bf16[64,896]{1,0:T(8,128)(2,1)S(1)}, u32[]{:S(2)}, u32[]{:S(2)}) collective-permute-start(bf16[64,896]{1,0:T(8,128)(2,1)S(1)} %get-tuple-element.111), channel_id=1, source_target_pairs={{0,16},{4,20},{8,24},{12,28},{16,0},{20,4},{24,8},{28,12},{1,17},{... | collective-permute-start | bytes 344072 | tf_op jit(solution)/shard_map/ppermute | solution.py:525
  30.3 6.8 %collective-permute-start.15 = (bf16[64,896]{1,0:T(8,128)(2,1)S(1)}, bf16[64,896]{1,0:T(8,128)(2,1)S(1)}, u32[]{:S(2)}, u32[]{:S(2)}) collective-permute-start(bf16[64,896]{1,0:T(8,128)(2,1)S(1)} %get-tuple-element.112), channel_id=1, source_target_pairs={{0,8},{4,12},{8,0},{12,4},{16,24},{20,28},{24,16},{28,20},{1,9},{5... | collective-permute-start | bytes 344072 | tf_op jit(solution)/shard_map/ppermute | solution.py:525
  33.6 7.9 %collective-permute-start.10 = (bf16[32,1152]{1,0:T(8,128)(2,1)S(1)}, bf16[32,1152]{1,0:T(8,128)(2,1)S(1)}, u32[]{:S(2)}, u32[]{:S(2)}) collective-permute-start(bf16[32,1152]{1,0:T(8,128)(2,1)S(1)} %get-tuple-element.106), channel_id=1, source_target_pairs={{0,24},{4,28},{8,16},{12,20},{16,8},{20,12},{24,0},{28,4},{1,25},{... | collective-permute-start | bytes 221192 | tf_op jit(solution)/shard_map/ppermute | solution.py:525
  36.3 5.2 %collective-permute-start.11 = (bf16[32,1152]{1,0:T(8,128)(2,1)S(1)}, bf16[32,1152]{1,0:T(8,128)(2,1)S(1)}, u32[]{:S(2)}, u32[]{:S(2)}) collective-permute-start(bf16[32,1152]{1,0:T(8,128)(2,1)S(1)} %get-tuple-element.107), channel_id=1, source_target_pairs={{0,16},{4,20},{8,24},{12,28},{16,0},{20,4},{24,8},{28,12},{1,17},{... | collective-permute-start | bytes 221192 | tf_op jit(solution)/shard_map/ppermute | solution.py:525
  36.8 4.7 %collective-permute-start.12 = (bf16[32,1152]{1,0:T(8,128)(2,1)S(1)}, bf16[32,1152]{1,0:T(8,128)(2,1)S(1)}, u32[]{:S(2)}, u32[]{:S(2)}) collective-permute-start(bf16[32,1152]{1,0:T(8,128)(2,1)S(1)} %get-tuple-element.108), channel_id=1, source_target_pairs={{0,8},{4,12},{8,0},{12,4},{16,24},{20,28},{24,16},{28,20},{1,9},{5... | collective-permute-start | bytes 221192 | tf_op jit(solution)/shard_map/ppermute | solution.py:525
  37.2 4.2 %collective-permute-start.16 = (bf16[32,896]{1,0:T(8,128)(2,1)S(1)}, bf16[32,896]{1,0:T(8,128)(2,1)S(1)}, u32[]{:S(2)}, u32[]{:S(2)}) collective-permute-start(bf16[32,896]{1,0:T(8,128)(2,1)S(1)} %get-tuple-element.114), channel_id=1, source_target_pairs={{0,1},{1,0},{2,3},{3,2},{4,5},{5,4},{6,7},{7,6},{8,9},{9,8},{10,11... | collective-permute-start | bytes 172040 | tf_op jit(solution)/shard_map/ppermute | solution.py:525
  41.5 7.4 %collective-permute-start.20 = (bf16[32,2048]{1,0:T(8,128)(2,1)S(1)}, bf16[32,2048]{1,0:T(8,128)(2,1)S(1)}, u32[]{:S(2)}, u32[]{:S(2)}) collective-permute-start(bf16[32,2048]{1,0:T(8,128)(2,1)S(1)} %join_terms.1.kept_ref), channel_id=1, source_target_pairs={{0,2},{1,3},{2,0},{3,1},{4,6},{5,7},{6,4},{7,5},{8,10},{9,11},{10,... | collective-permute-start | bytes 393224 | tf_op jit(solution)/shard_map/ppermute | solution.py:525
  44.3 6.1 %collective-permute-start.17 = (bf16[128,512]{1,0:T(8,128)(2,1)S(1)}, bf16[128,512]{1,0:T(8,128)(2,1)S(1)}, u32[]{:S(2)}, u32[]{:S(2)}) collective-permute-start(bf16[128,512]{1,0:T(8,128)(2,1)S(1)} %get-tuple-element.116), channel_id=1, source_target_pairs={{0,24},{4,28},{8,16},{12,20},{16,8},{20,12},{24,0},{28,4},{1,25},{... | collective-permute-start | bytes 393224 | tf_op jit(solution)/shard_map/ppermute | solution.py:525
  46.8 5.0 %collective-permute-start.18 = (bf16[128,512]{1,0:T(8,128)(2,1)S(1)}, bf16[128,512]{1,0:T(8,128)(2,1)S(1)}, u32[]{:S(2)}, u32[]{:S(2)}) collective-permute-start(bf16[128,512]{1,0:T(8,128)(2,1)S(1)} %get-tuple-element.117), channel_id=1, source_target_pairs={{0,16},{4,20},{8,24},{12,28},{16,0},{20,4},{24,8},{28,12},{1,17},{... | collective-permute-start | bytes 393224 | tf_op jit(solution)/shard_map/ppermute | solution.py:525
  47.3 5.0 %collective-permute-start.19 = (bf16[128,512]{1,0:T(8,128)(2,1)S(1)}, bf16[128,512]{1,0:T(8,128)(2,1)S(1)}, u32[]{:S(2)}, u32[]{:S(2)}) collective-permute-start(bf16[128,512]{1,0:T(8,128)(2,1)S(1)} %get-tuple-element.118), channel_id=1, source_target_pairs={{0,8},{4,12},{8,0},{12,4},{16,24},{20,28},{24,16},{28,20},{1,9},{5... | collective-permute-start | bytes 393224 | tf_op jit(solution)/shard_map/ppermute | solution.py:525
  49.0 5.0 %collective-permute-start.21 = (bf16[32,2048]{1,0:T(8,128)(2,1)S(1)}, bf16[32,2048]{1,0:T(8,128)(2,1)S(1)}, u32[]{:S(2)}, u32[]{:S(2)}) collective-permute-start(bf16[32,2048]{1,0:T(8,128)(2,1)S(1)} %add_pairs.1.held_ref), channel_id=1, source_target_pairs={{0,1},{1,0},{2,3},{3,2},{4,5},{5,4},{6,7},{7,6},{8,9},{9,8},{10,11... | collective-permute-start | bytes 393224 | tf_op jit(solution)/shard_map/ppermute | solution.py:525

commit v13 on v12

--- a/solution.py
+++ b/solution.py
@@ -22,6 +22,7 @@
 HBM = pl.BlockSpec(memory_space=pltpu.HBM)
 CHIP_STEPS = (3, 2, 1)
 FIRST_PART = 384
+SWAP_PIECES = (384, 384, 256, 256)
 PINNED = pl.BlockSpec(memory_space=pltpu.VMEM)
 shaped = jax.ShapeDtypeStruct
 
@@ -302,7 +303,7 @@
 
 def column_chip_kernel(
     x_ref, cot_ref, near_1, near_2, near_3, far_ref, gain_ref, w_ref, wo_ref, row_out_ref,
-    send_ref, keep_ref, grads_ref,
+    keep_ref, grads_ref, *refs,
 ):
     chip, core, _ = here()
     share = far_ref.shape[2]
@@ -327,12 +328,17 @@
     term_qkv, term_out = column_part(
         tokens(0, x_ref), tokens(1, cot_ref), mask, gain_ref[...], w_ref, wo_ref, (), grads_ref
     )
+    *pieces, send_ref = refs
     chips = send_ref.shape[0]
-    refs = send_ref, keep_ref
+    both = send_ref, keep_ref
     out_lanes = slice(3 * HW, send_ref.shape[2])
-    split_cores(term_qkv, *refs, slice(0, chips), slice(0, 3 * HW))
-    split_cores(row_out_ref[...], *refs, slice(0, chips // 2), out_lanes)
-    split_cores(term_out, *refs, slice(chips // 2, chips), out_lanes)
+    split_cores(term_qkv, *both, slice(0, chips), slice(0, 3 * HW))
+    split_cores(row_out_ref[...], *both, slice(0, chips // 2), out_lanes)
+    split_cores(term_out, *both, slice(chips // 2, chips), out_lanes)
+    at = 0
+    for piece in pieces:
+        piece[...] = send_ref[:, :, at : at + piece.shape[2]]
+        at += piece.shape[2]
 
 
 def far_kernel(x_ref, cot_ref, near_1, near_2, near_3, far_ref):
@@ -430,13 +436,14 @@
     send_ref[...], kept_ref[...] = split_rows(jnp.concatenate(total, 2), 1)
 
 
-def cores_kernel(keep_ref, got_ref, send_ref, kept_ref, *targets):
+def cores_kernel(keep_ref, got_1, got_2, got_3, got_4, send_ref, kept_ref, *targets):
     chip, cut = here()[0], kept_ref.shape[2]
-    first = keep_ref[:, :, :cut].astype(F32) + got_ref[:, :, :cut].astype(F32)
+    first = keep_ref[:, :, :cut].astype(F32) + got_1[...].astype(F32)
     send_ref[...], kept_ref[...] = split_rows(first, 1)
     for step, target in zip((0, *CHIP_STEPS), targets):
         there = chip ^ step
-        total = keep_ref[there, :, cut:].astype(F32) + got_ref[there, :, cut:].astype(F32)
+        got = jnp.concatenate([ref[there] for ref in (got_2, got_3, got_4)], 1)
+        total = keep_ref[there, :, cut:].astype(F32) + got.astype(F32)
         target[...] = total.astype(target.dtype)
 
 
@@ -619,7 +626,8 @@
             [(VMEM, one) for one in (x_near, cot_near, *near)],
             [((chips, 2, share, width), BF16)],
         )
-        send, keep, col_grads = call(
+        row_got = swap(row_next, "dp", 1)
+        keep, col_grads, *pieces = call(
             column_chip_kernel,
             "column_heads",
             [
@@ -629,9 +637,11 @@
                     gain, col_weight, col_out_weight, row_out,
                 )
             ],
-            [((chips, row_share, col_width), BF16)] * 2 + [col_outs[0]],
-            vmem=BIG_VMEM,
-            out_specs=[VMEM, VMEM, PINNED],
+            [((chips, row_share, col_width), BF16), col_outs[0]]
+            + [((chips, row_share, wide), BF16) for wide in SWAP_PIECES],
+            [pltpu.VMEM((chips, row_share, col_width), BF16)],
+            BIG_VMEM,
+            [VMEM, PINNED] + [VMEM] * len(SWAP_PIECES),
         )
         back_send, back_keep = call(
             back_chip_kernel,
@@ -639,14 +649,13 @@
             [(VMEM, col_grads), (VMEM, col_weight)],
             [((chips, share, width), BF16)] * 2,
         )
-        row_next, _ = lax.optimization_barrier((row_next, send))
-        keep, back_keep = lax.optimization_barrier((keep, back_keep))
+        keep, back_keep, row_got = lax.optimization_barrier((keep, back_keep, row_got))
         first_half = (chips, row_share // 2, FIRST_PART)
         second = (row_share, col_width - FIRST_PART)
         to_next, kept, owned, *off = call(
             cores_kernel,
             "column_add_cores",
-            [(VMEM, keep), (VMEM, swap(send, "seq", 1))],
+            [(VMEM, keep), *[(VMEM, swap(piece, "seq", 1)) for piece in pieces]],
             [(first_half, BF16), (first_half, F32), (second, F32)] + [(second, BF16)] * 3,
             out_specs=[VMEM, PINNED, PINNED, VMEM, VMEM, VMEM],
         )
@@ -664,7 +673,7 @@
             "first_add_pair",
             [
                 (VMEM, one)
-                for one in (kept, swap(to_next, "dp", 1), row_kept, swap(row_next, "dp", 1))
+                for one in (kept, swap(to_next, "dp", 1), row_kept, row_got)
             ],
             [(joint, F32)] + [(joint, BF16)] * 3,
             out_specs=[PINNED, VMEM, VMEM, VMEM],

time: 55.1 us -> 55.9 us (1.015)
  starting transfers between devices: 24.4 us -> 25.6 us
    ppermute x22 -> x25, starting transfers between devices: 24.4 us -> 25.6 us  [swap(): return lax.ppermute(array, axis, [(i, i ^ bits) for i in range(count)])]
    ppermute x22 -> x25, waiting for transfers between devices: 14.5 us -> 14.1 us  [swap(): return lax.ppermute(array, axis, [(i, i ^ bits) for i in range(count)])]
  transfers between devices with their start and end apart: 22 -> 25, of which waited for: 12 -> 13; matrix products, arithmetic and copies ran while one was open for 0% -> 0% of each run, Pallas kernels for 18% -> 23%
where the time goes in v13:
time: 55.9 us; the launch traced here: 55.8 us
  starting transfers between devices  25.6 us (46%)
  Pallas kernels  15.3 us (27%)
  waiting for transfers between devices  14.1 us (25%)
  between operations  0.75 us (1%)
    ppermute x25, starting transfers between devices, swap(): return lax.ppermute(array, axis, [(i, i ^ bits) for i in range(count)])  25.6 us
    pallas_call x14, Pallas kernels, call(): pl.pallas_call(kernel, out_shape=outs, in_specs=[spec for spec, _ in ins]...  15.3 us
    ppermute x25, waiting for transfers between devices, swap(): return lax.ppermute(array, axis, [(i, i ^ bits) for i in range(count)])  14.1 us
  transfers between devices with their start and end apart: 25, of which 13 were waited for; matrix products, arithmetic and copies ran while one was open for 0% of the time, Pallas kernels for 23%

profile of v13, /device:TPU:0, one launch (start us, length us, event | category | flops | bytes accessed | tf_op | source)
XLA Modules:
  0.0 55.8 jit_solution(9246206529576622139)
XLA Ops:
  0.6 1.3 %pack_columns.1 = (bf16[2,128,512]{2,1,0:T(8,128)(2,1)S(1)}, bf16[2,128,512]{2,1,0:T(8,128)(2,1)S(1)}, bf16[2,128,512]{2,1,0:T(8,128)(2,1)S(1)}) custom-call(bf16[512,512]{1,0:T(8,128)(2,1)} %bitcast.9, bf16[512,512]{1,0:T(8,128)(2,1)} %bitcast.11), custom_call_target="tpu_custom_call" | custom-call | tf_op jit(solution)/shard_map/pack_columns/pallas_call | solution.py:518
  1.9 3.0 %collective-permute-start.1 = (bf16[2,128,512]{2,1,0:T(8,128)(2,1)S(1)}, bf16[2,128,512]{2,1,0:T(8,128)(2,1)S(1)}, u32[]{:S(2)}, u32[]{:S(2)}) collective-permute-start(bf16[2,128,512]{2,1,0:T(8,128)(2,1)S(1)} %get-tuple-element.72), channel_id=1, source_target_pairs={{0,16},{4,20},{8,24},{12,28},{16,0},{20,4},{24,8},{28,12},{1,17},{... | collective-permute-start | bytes 786440 | tf_op jit(solution)/shard_map/ppermute | solution.py:532
  4.9 1.5 %collective-permute-start.2 = (bf16[2,128,512]{2,1,0:T(8,128)(2,1)S(1)}, bf16[2,128,512]{2,1,0:T(8,128)(2,1)S(1)}, u32[]{:S(2)}, u32[]{:S(2)}) collective-permute-start(bf16[2,128,512]{2,1,0:T(8,128)(2,1)S(1)} %get-tuple-element.73), channel_id=1, source_target_pairs={{0,8},{4,12},{8,0},{12,4},{16,24},{20,28},{24,16},{28,20},{1,9},{5... | collective-permute-start | bytes 786440 | tf_op jit(solution)/shard_map/ppermute | solution.py:532
  6.4 0.0 collective-permute-start
  6.5 7.7 %row_heads.1 = (bf16[4,64,384]{2,1,0:T(8,128)(2,1)S(1)}, bf16[4,64,384]{2,1,0:T(8,128)(2,1)S(1)}, bf16[4,64,384]{2,1,0:T(8,128)(2,1)S(1)}, bf16[4,64,384]{2,1,0:...) custom-call(bf16[512,512]{1,0:T(8,128)(2,1)} %bitcast.10, ...), custom_call_target="tpu_custom_call" | custom-call | tf_op jit(solution)/shard_map/row_heads/pallas_call | solution.py:518
  14.1 0.1 collective-permute-start.3
  14.2 0.5 collective-permute-start.4
  14.7 0.9 %collective-permute-done.3.got_1 = bf16[4,64,384]{2,1,0:T(8,128)(2,1)S(1)} collective-permute-done((bf16[4,64,384]{2,1,0:T(8,128)(2,1)S(1)}, bf16[4,64,384]{2,1,0:T(8,128)(2,1)S(1)}, u32[]{:S(2)}, u32[]{:S(2)}) %collective-permute-start.3) | collective-permute-done | bytes 196640 | tf_op jit(solution)/shard_map/ppermute | solution.py:532
  15.6 0.3 collective-permute-done.4.got_2
  15.9 0.1 row_add_cores.1
  16.1 2.0 %collective-permute-done.near_1 = bf16[2,128,512]{2,1,0:T(8,128)(2,1)S(1)} collective-permute-done((bf16[2,128,512]{2,1,0:T(8,128)(2,1)S(1)}, bf16[2,128,512]{2,1,0:T(8,128)(2,1)S(1)}, u32[]{:S(2)}, u32[]{:S(2)}) %collective-permute-start) | collective-permute-done | bytes 262176 | tf_op jit(solution)/shard_map/ppermute | solution.py:532
  18.2 0.1 collective-permute-start.5
  18.2 1.8 %collective-permute-start.6 = (bf16[4,32,768]{2,1,0:T(8,128)(2,1)S(1)}, bf16[4,32,768]{2,1,0:T(8,128)(2,1)S(1)}, u32[]{:S(2)}, u32[]{:S(2)}) collective-permute-start(bf16[4,32,768]{2,1,0:T(8,128)(2,1)S(1)} %get-tuple-element.91), channel_id=1, source_target_pairs={{0,1},{1,0},{2,3},{3,2},{4,5},{5,4},{6,7},{7,6},{8,9},{9,8},{10,11... | collective-permute-start | bytes 589832 | tf_op jit(solution)/shard_map/ppermute | solution.py:532
  20.0 0.1 collective-permute-done.5.far_ref
  20.1 3.1 %column_heads.1 = (bf16[4,64,1280]{2,1,0:T(8,128)(2,1)S(1)}, bf16[512,768]{1,0:T(8,128)(2,1)S(1)}, bf16[4,64,384]{2,1,0:T(8,128)(2,1)S(1)}, bf16[4,64,384]{2,1,0...) custom-call(bf16[512,512]{1,0:T(8,128)(2,1)S(1)} %get-tuple-element.80.x_ref, ...), custom_call_target="tpu_custom_call" | custom-call | tf_op jit(solution)/shard_map/column_heads/pallas_call | solution.py:518
  23.3 0.2 collective-permute-start.8
  23.5 0.4 collective-permute-start.9
  23.8 0.6 %column_grad_hidden.1 = (bf16[4,64,512]{2,1,0:T(8,128)(2,1)S(1)}, bf16[4,64,512]{2,1,0:T(8,128)(2,1)S(1)}) custom-call(bf16[512,768]{1,0:T(8,128)(2,1)S(1)} %get-tuple-element.89.grads_ref, bf16[512,768]{1,0:T(8,128)(2,1)S(1)} %get-tuple-element.85.w_ref), custom_call_target="tpu_custom_call" | custom-call | tf_op jit(solution)/shard_map/column_grad_hidden/pallas_call | solution.py:518
  24.5 0.2 collective-permute-start.7
  24.7 0.4 collective-permute-start.10
  25.0 0.5 collective-permute-done.6.row_got
  25.6 0.7 %collective-permute-done.10.got_3 = bf16[4,64,256]{2,1,0:T(8,128)(2,1)S(1)} collective-permute-done((bf16[4,64,256]{2,1,0:T(8,128)(2,1)S(1)}, bf16[4,64,256]{2,1,0:T(8,128)(2,1)S(1)}, u32[]{:S(2)}, u32[]{:S(2)}) %collective-permute-start.10) | collective-permute-done | bytes 131104 | tf_op jit(solution)/shard_map/ppermute | solution.py:532
  26.2 0.7 %collective-permute-done.11.got_4 = bf16[4,64,256]{2,1,0:T(8,128)(2,1)S(1)} collective-permute-done((bf16[4,64,256]{2,1,0:T(8,128)(2,1)S(1)}, bf16[4,64,256]{2,1,0:T(8,128)(2,1)S(1)}, u32[]{:S(2)}, u32[]{:S(2)}) %collective-permute-start.11) | collective-permute-done | bytes 131104 | tf_op jit(solution)/shard_map/ppermute | solution.py:532
  26.9 0.2 column_add_cores.1
  27.1 2.7 %collective-permute-start.16 = (bf16[64,896]{1,0:T(8,128)(2,1)S(1)}, bf16[64,896]{1,0:T(8,128)(2,1)S(1)}, u32[]{:S(2)}, u32[]{:S(2)}) collective-permute-start(bf16[64,896]{1,0:T(8,128)(2,1)S(1)} %get-tuple-element.116), channel_id=1, source_target_pairs={{0,24},{4,28},{8,16},{12,20},{16,8},{20,12},{24,0},{28,4},{1,25},{... | collective-permute-start | bytes 344072 | tf_op jit(solution)/shard_map/ppermute | solution.py:532
  29.8 1.6 %collective-permute-start.12 = (bf16[4,32,384]{2,1,0:T(8,128)(2,1)S(1)}, bf16[4,32,384]{2,1,0:T(8,128)(2,1)S(1)}, u32[]{:S(2)}, u32[]{:S(2)}) collective-permute-start(bf16[4,32,384]{2,1,0:T(8,128)(2,1)S(1)} %get-tuple-element.108), channel_id=1, source_target_pairs={{0,1},{1,0},{2,3},{3,2},{4,5},{5,4},{6,7},{7,6},{8,9},{9,8},{10,11... | collective-permute-start | bytes 294920 | tf_op jit(solution)/shard_map/ppermute | solution.py:532
  31.3 0.5 collective-permute-start.17
  31.8 0.5 collective-permute-start.18
  32.4 1.9 %collective-permute-done.12.got_ref = bf16[4,32,384]{2,1,0:T(8,128)(2,1)S(1)} collective-permute-done((bf16[4,32,384]{2,1,0:T(8,128)(2,1)S(1)}, bf16[4,32,384]{2,1,0:T(8,128)(2,1)S(1)}, u32[]{:S(2)}, u32[]{:S(2)}) %collective-permute-start.12) | collective-permute-done | bytes 98336 | tf_op jit(solution)/shard_map/ppermute | solution.py:532
  34.4 0.1 first_add_pair.1
  34.4 0.6 %collective-permute-start.13 = (bf16[32,1152]{1,0:T(8,128)(2,1)S(1)}, bf16[32,1152]{1,0:T(8,128)(2,1)S(1)}, u32[]{:S(2)}, u32[]{:S(2)}) collective-permute-start(bf16[32,1152]{1,0:T(8,128)(2,1)S(1)} %get-tuple-element.112), channel_id=1, source_target_pairs={{0,24},{4,28},{8,16},{12,20},{16,8},{20,12},{24,0},{28,4},{1,25},{... | collective-permute-start | bytes 221192 | tf_op jit(solution)/shard_map/ppermute | solution.py:532
  35.0 1.5 %collective-permute-start.14 = (bf16[32,1152]{1,0:T(8,128)(2,1)S(1)}, bf16[32,1152]{1,0:T(8,128)(2,1)S(1)}, u32[]{:S(2)}, u32[]{:S(2)}) collective-permute-start(bf16[32,1152]{1,0:T(8,128)(2,1)S(1)} %get-tuple-element.113), channel_id=1, source_target_pairs={{0,16},{4,20},{8,24},{12,28},{16,0},{20,4},{24,8},{28,12},{1,17},{... | collective-permute-start | bytes 221192 | tf_op jit(solution)/shard_map/ppermute | solution.py:532
  36.5 1.5 %collective-permute-start.15 = (bf16[32,1152]{1,0:T(8,128)(2,1)S(1)}, bf16[32,1152]{1,0:T(8,128)(2,1)S(1)}, u32[]{:S(2)}, u32[]{:S(2)}) collective-permute-start(bf16[32,1152]{1,0:T(8,128)(2,1)S(1)} %get-tuple-element.114), channel_id=1, source_target_pairs={{0,8},{4,12},{8,0},{12,4},{16,24},{20,28},{24,16},{28,20},{1,9},{5... | collective-permute-start | bytes 221192 | tf_op jit(solution)/shard_map/ppermute | solution.py:532
  38.0 0.1 second_add_chips.1
  38.1 1.6 %collective-permute-start.19 = (bf16[32,896]{1,0:T(8,128)(2,1)S(1)}, bf16[32,896]{1,0:T(8,128)(2,1)S(1)}, u32[]{:S(2)}, u32[]{:S(2)}) collective-permute-start(bf16[32,896]{1,0:T(8,128)(2,1)S(1)} %get-tuple-element.120), channel_id=1, source_target_pairs={{0,1},{1,0},{2,3},{3,2},{4,5},{5,4},{6,7},{7,6},{8,9},{9,8},{10,11... | collective-permute-start | bytes 172040 | tf_op jit(solution)/shard_map/ppermute | solution.py:532
  39.7 2.6 %collective-permute-done.19.got_ref = bf16[32,896]{1,0:T(8,128)(2,1)S(1)} collective-permute-done((bf16[32,896]{1,0:T(8,128)(2,1)S(1)}, bf16[32,896]{1,0:T(8,128)(2,1)S(1)}, u32[]{:S(2)}, u32[]{:S(2)}) %collective-permute-start.19) | collective-permute-done | bytes 57376 | tf_op jit(solution)/shard_map/ppermute | solution.py:532
  42.3 0.1 join_terms.1.kept_ref
  42.4 2.8 %collective-permute-start.23 = (bf16[32,2048]{1,0:T(8,128)(2,1)S(1)}, bf16[32,2048]{1,0:T(8,128)(2,1)S(1)}, u32[]{:S(2)}, u32[]{:S(2)}) collective-permute-start(bf16[32,2048]{1,0:T(8,128)(2,1)S(1)} %join_terms.1.kept_ref), channel_id=1, source_target_pairs={{0,2},{1,3},{2,0},{3,1},{4,6},{5,7},{6,4},{7,5},{8,10},{9,11},{10,... | collective-permute-start | bytes 393224 | tf_op jit(solution)/shard_map/ppermute | solution.py:532
  45.2 1.1 %collective-permute-start.20 = (bf16[128,512]{1,0:T(8,128)(2,1)S(1)}, bf16[128,512]{1,0:T(8,128)(2,1)S(1)}, u32[]{:S(2)}, u32[]{:S(2)}) collective-permute-start(bf16[128,512]{1,0:T(8,128)(2,1)S(1)} %get-tuple-element.122), channel_id=1, source_target_pairs={{0,24},{4,28},{8,16},{12,20},{16,8},{20,12},{24,0},{28,4},{1,25},{... | collective-permute-start | bytes 393224 | tf_op jit(solution)/shard_map/ppermute | solution.py:532
  46.2 0.8 %collective-permute-start.21 = (bf16[128,512]{1,0:T(8,128)(2,1)S(1)}, bf16[128,512]{1,0:T(8,128)(2,1)S(1)}, u32[]{:S(2)}, u32[]{:S(2)}) collective-permute-start(bf16[128,512]{1,0:T(8,128)(2,1)S(1)} %get-tuple-element.123), channel_id=1, source_target_pairs={{0,16},{4,20},{8,24},{12,28},{16,0},{20,4},{24,8},{28,12},{1,17},{... | collective-permute-start | bytes 393224 | tf_op jit(solution)/shard_map/ppermute | solution.py:532
  47.0 1.6 %collective-permute-start.22 = (bf16[128,512]{1,0:T(8,128)(2,1)S(1)}, bf16[128,512]{1,0:T(8,128)(2,1)S(1)}, u32[]{:S(2)}, u32[]{:S(2)}) collective-permute-start(bf16[128,512]{1,0:T(8,128)(2,1)S(1)} %get-tuple-element.124), channel_id=1, source_target_pairs={{0,8},{4,12},{8,0},{12,4},{16,24},{20,28},{24,16},{28,20},{1,9},{5... | collective-permute-start | bytes 393224 | tf_op jit(solution)/shard_map/ppermute | solution.py:532
  48.7 1.2 %collective-permute-done.23.got_ref = bf16[32,2048]{1,0:T(8,128)(2,1)S(1)} collective-permute-done((bf16[32,2048]{1,0:T(8,128)(2,1)S(1)}, bf16[32,2048]{1,0:T(8,128)(2,1)S(1)}, u32[]{:S(2)}, u32[]{:S(2)}) %collective-permute-start.23) | collective-permute-done | bytes 131104 | tf_op jit(solution)/shard_map/ppermute | solution.py:532
  49.9 0.7 %collective-permute-start.24 = (bf16[32,2048]{1,0:T(8,128)(2,1)S(1)}, bf16[32,2048]{1,0:T(8,128)(2,1)S(1)}, u32[]{:S(2)}, u32[]{:S(2)}) collective-permute-start(bf16[32,2048]{1,0:T(8,128)(2,1)S(1)} %add_pairs.1.held_ref), channel_id=1, source_target_pairs={{0,1},{1,0},{2,3},{3,2},{4,5},{5,4},{6,7},{7,6},{8,9},{9,8},{10,11... | collective-permute-start | bytes 393224 | tf_op jit(solution)/shard_map/ppermute | solution.py:532
  50.6 0.7 %collective-permute-done.20.got_1 = bf16[128,512]{1,0:T(8,128)(2,1)S(1)} collective-permute-done((bf16[128,512]{1,0:T(8,128)(2,1)S(1)}, bf16[128,512]{1,0:T(8,128)(2,1)S(1)}, u32[]{:S(2)}, u32[]{:S(2)}) %collective-permute-start.20) | collective-permute-done | bytes 131104 | tf_op jit(solution)/shard_map/ppermute | solution.py:532
  51.3 1.3 %collective-permute-done.21.got_2 = bf16[128,512]{1,0:T(8,128)(2,1)S(1)} collective-permute-done((bf16[128,512]{1,0:T(8,128)(2,1)S(1)}, bf16[128,512]{1,0:T(8,128)(2,1)S(1)}, u32[]{:S(2)}, u32[]{:S(2)}) %collective-permute-start.21) | collective-permute-done | bytes 131104 | tf_op jit(solution)/shard_map/ppermute | solution.py:532
  52.5 1.2 %input_grad.1 = bf16[512,512]{1,0:T(8,128)(2,1)} custom-call(f32[512,512]{1,0:T(8,128)S(1)} %get-tuple-element.69.base_ref, f32[512,512]{1,0:T(8,128)S(1)} %get-tuple-element.70.normed_ref, f32[512,1]{1,0:T(8,128)S(1)} %get-tuple-element.71.inverse_ref, f32[1,512]{1,0:T(1,128)S(1)} %bitcast.7, bf16[128,512]{1,0:T(8,128)(2,1)S(1)} %get-tuple-element.121.own_ref, ...), custom_call_target="tpu_custom_call" | custom-call | tf_op jit(solution)/shard_map/input_grad/pallas_call | solution.py:518
  53.7 1.2 %collective-permute-done.24.got_ref = bf16[32,2048]{1,0:T(8,128)(2,1)S(1)} collective-permute-done((bf16[32,2048]{1,0:T(8,128)(2,1)S(1)}, bf16[32,2048]{1,0:T(8,128)(2,1)S(1)}, u32[]{:S(2)}, u32[]{:S(2)}) %collective-permute-start.24) | collective-permute-done | bytes 131104 | tf_op jit(solution)/shard_map/ppermute | solution.py:532
  54.9 0.9 %result.1 = (f32[64,1536]{1,0:T(8,128)}, f32[64,512]{1,0:T(8,128)}, f32[1,64]{1,0:T(1,128)}) custom-call(bf16[32,2048]{1,0:T(8,128)(2,1)S(1)} %add_pairs.1.held_ref, bf16[32,2048]{1,0:T(8,128)(2,1)S(1)} %collective-permute-done.24.got_ref, bf16[64,1536]{1,0:T(8,128)(2,1)S(1)} %get-tuple-element.126.w_ref, f32[1,512]{1,0:T(1,128)S(1)} %bitcast.8), custom_call_target="tpu_custom_call" | custom-call | tf_op jit(solution)/shard_map/result/pallas_call | solution.py:518
  (18 shorter events, 0.2 us)
Async XLA Ops:
  1.9 14.2 %collective-permute-start.1 = (bf16[2,128,512]{2,1,0:T(8,128)(2,1)S(1)}, bf16[2,128,512]{2,1,0:T(8,128)(2,1)S(1)}, u32[]{:S(2)}, u32[]{:S(2)}) collective-permute-start(bf16[2,128,512]{2,1,0:T(8,128)(2,1)S(1)} %get-tuple-element.72), channel_id=1, source_target_pairs={{0,16},{4,20},{8,24},{12,28},{16,0},{20,4},{24,8},{28,12},{1,17},{... | collective-permute-start | bytes 786440 | tf_op jit(solution)/shard_map/ppermute | solution.py:532
  4.9 11.1 %collective-permute-start.2 = (bf16[2,128,512]{2,1,0:T(8,128)(2,1)S(1)}, bf16[2,128,512]{2,1,0:T(8,128)(2,1)S(1)}, u32[]{:S(2)}, u32[]{:S(2)}) collective-permute-start(bf16[2,128,512]{2,1,0:T(8,128)(2,1)S(1)} %get-tuple-element.73), channel_id=1, source_target_pairs={{0,8},{4,12},{8,0},{12,4},{16,24},{20,28},{24,16},{28,20},{1,9},{5... | collective-permute-start | bytes 786440 | tf_op jit(solution)/shard_map/ppermute | solution.py:532
  6.4 11.7 %collective-permute-start = (bf16[2,128,512]{2,1,0:T(8,128)(2,1)S(1)}, bf16[2,128,512]{2,1,0:T(8,128)(2,1)S(1)}, u32[]{:S(2)}, u32[]{:S(2)}) collective-permute-start(bf16[2,128,512]{2,1,0:T(8,128)(2,1)S(1)} %get-tuple-element.67), channel_id=1, source_target_pairs={{0,24},{4,28},{8,16},{12,20},{16,8},{20,12},{24,0},{28,4},{1,25},{... | collective-permute-start | bytes 786440 | tf_op jit(solution)/shard_map/ppermute | solution.py:532
  14.1 1.5 %collective-permute-start.3 = (bf16[4,64,384]{2,1,0:T(8,128)(2,1)S(1)}, bf16[4,64,384]{2,1,0:T(8,128)(2,1)S(1)}, u32[]{:S(2)}, u32[]{:S(2)}) collective-permute-start(bf16[4,64,384]{2,1,0:T(8,128)(2,1)S(1)} %get-tuple-element.76), channel_id=1, source_target_pairs={{0,4},{4,0},{8,12},{12,8},{16,20},{20,16},{24,28},{28,24},{1,5},{5... | collective-permute-start | bytes 589832 | tf_op jit(solution)/shard_map/ppermute | solution.py:532
  14.2 1.7 %collective-permute-start.4 = (bf16[4,64,384]{2,1,0:T(8,128)(2,1)S(1)}, bf16[4,64,384]{2,1,0:T(8,128)(2,1)S(1)}, u32[]{:S(2)}, u32[]{:S(2)}) collective-permute-start(bf16[4,64,384]{2,1,0:T(8,128)(2,1)S(1)} %get-tuple-element.77), channel_id=1, source_target_pairs={{0,4},{4,0},{8,12},{12,8},{16,20},{20,16},{24,28},{28,24},{1,5},{5... | collective-permute-start | bytes 589832 | tf_op jit(solution)/shard_map/ppermute | solution.py:532
  15.9 4.2 %copy-start = (f32[512]{0:T(512)S(1)}, f32[512]{0:T(512)}, u32[]{:S(2)}) copy-start(f32[512]{0:T(512)} %param.6) | copy-start | bytes 6148
  18.2 2.0 %collective-permute-start.5 = (bf16[4,2,64,512]{3,2,1,0:T(8,128)(2,1)S(1)}, bf16[4,2,64,512]{3,2,1,0:T(8,128)(2,1)S(1)}, u32[]{:S(2)}, u32[]{:S(2)}) collective-permute-start(bf16[4,2,64,512]{3,2,1,0:T(8,128)(2,1)S(1)} %pack_other_core.1), channel_id=1, source_target_pairs={{0,4},{4,0},{8,12},{12,8},{16,20},{20,16},{24,28},{28,24},{1,5},{5... | collective-permute-start | bytes 1572872 | tf_op jit(solution)/shard_map/ppermute | solution.py:532
  18.2 7.3 %collective-permute-start.6 = (bf16[4,32,768]{2,1,0:T(8,128)(2,1)S(1)}, bf16[4,32,768]{2,1,0:T(8,128)(2,1)S(1)}, u32[]{:S(2)}, u32[]{:S(2)}) collective-permute-start(bf16[4,32,768]{2,1,0:T(8,128)(2,1)S(1)} %get-tuple-element.91), channel_id=1, source_target_pairs={{0,1},{1,0},{2,3},{3,2},{4,5},{5,4},{6,7},{7,6},{8,9},{9,8},{10,11... | collective-permute-start | bytes 589832 | tf_op jit(solution)/shard_map/ppermute | solution.py:532
  23.3 3.6 %collective-permute-start.8 = (bf16[4,64,384]{2,1,0:T(8,128)(2,1)S(1)}, bf16[4,64,384]{2,1,0:T(8,128)(2,1)S(1)}, u32[]{:S(2)}, u32[]{:S(2)}) collective-permute-start(bf16[4,64,384]{2,1,0:T(8,128)(2,1)S(1)} %get-tuple-element.103), channel_id=1, source_target_pairs={{0,4},{4,0},{8,12},{12,8},{16,20},{20,16},{24,28},{28,24},{1,5},{5... | collective-permute-start | bytes 589832 | tf_op jit(solution)/shard_map/ppermute | solution.py:532
  23.5 3.4 %collective-permute-start.9 = (bf16[4,64,384]{2,1,0:T(8,128)(2,1)S(1)}, bf16[4,64,384]{2,1,0:T(8,128)(2,1)S(1)}, u32[]{:S(2)}, u32[]{:S(2)}) collective-permute-start(bf16[4,64,384]{2,1,0:T(8,128)(2,1)S(1)} %get-tuple-element.104), channel_id=1, source_target_pairs={{0,4},{4,0},{8,12},{12,8},{16,20},{20,16},{24,28},{28,24},{1,5},{5... | collective-permute-start | bytes 589832 | tf_op jit(solution)/shard_map/ppermute | solution.py:532
  24.5 7.9 %collective-permute-start.7 = (bf16[4,64,512]{2,1,0:T(8,128)(2,1)S(1)}, bf16[4,64,512]{2,1,0:T(8,128)(2,1)S(1)}, u32[]{:S(2)}, u32[]{:S(2)}) collective-permute-start(bf16[4,64,512]{2,1,0:T(8,128)(2,1)S(1)} %get-tuple-element.93), channel_id=1, source_target_pairs={{0,4},{4,0},{8,12},{12,8},{16,20},{20,16},{24,28},{28,24},{1,5},{5... | collective-permute-start | bytes 786440 | tf_op jit(solution)/shard_map/ppermute | solution.py:532
  24.7 1.6 %collective-permute-start.10 = (bf16[4,64,256]{2,1,0:T(8,128)(2,1)S(1)}, bf16[4,64,256]{2,1,0:T(8,128)(2,1)S(1)}, u32[]{:S(2)}, u32[]{:S(2)}) collective-permute-start(bf16[4,64,256]{2,1,0:T(8,128)(2,1)S(1)} %get-tuple-element.105), channel_id=1, source_target_pairs={{0,4},{4,0},{8,12},{12,8},{16,20},{20,16},{24,28},{28,24},{1,5},{5... | collective-permute-start | bytes 393224 | tf_op jit(solution)/shard_map/ppermute | solution.py:532
  25.6 1.3 %collective-permute-start.11 = (bf16[4,64,256]{2,1,0:T(8,128)(2,1)S(1)}, bf16[4,64,256]{2,1,0:T(8,128)(2,1)S(1)}, u32[]{:S(2)}, u32[]{:S(2)}) collective-permute-start(bf16[4,64,256]{2,1,0:T(8,128)(2,1)S(1)} %get-tuple-element.106), channel_id=1, source_target_pairs={{0,4},{4,0},{8,12},{12,8},{16,20},{20,16},{24,28},{28,24},{1,5},{5... | collective-permute-start | bytes 393224 | tf_op jit(solution)/shard_map/ppermute | solution.py:532
  27.1 9.4 %collective-permute-start.16 = (bf16[64,896]{1,0:T(8,128)(2,1)S(1)}, bf16[64,896]{1,0:T(8,128)(2,1)S(1)}, u32[]{:S(2)}, u32[]{:S(2)}) collective-permute-start(bf16[64,896]{1,0:T(8,128)(2,1)S(1)} %get-tuple-element.116), channel_id=1, source_target_pairs={{0,24},{4,28},{8,16},{12,20},{16,8},{20,12},{24,0},{28,4},{1,25},{... | collective-permute-start | bytes 344072 | tf_op jit(solution)/shard_map/ppermute | solution.py:532
  29.8 4.6 %collective-permute-start.12 = (bf16[4,32,384]{2,1,0:T(8,128)(2,1)S(1)}, bf16[4,32,384]{2,1,0:T(8,128)(2,1)S(1)}, u32[]{:S(2)}, u32[]{:S(2)}) collective-permute-start(bf16[4,32,384]{2,1,0:T(8,128)(2,1)S(1)} %get-tuple-element.108), channel_id=1, source_target_pairs={{0,1},{1,0},{2,3},{3,2},{4,5},{5,4},{6,7},{7,6},{8,9},{9,8},{10,11... | collective-permute-start | bytes 294920 | tf_op jit(solution)/shard_map/ppermute | solution.py:532
  31.3 6.7 %collective-permute-start.17 = (bf16[64,896]{1,0:T(8,128)(2,1)S(1)}, bf16[64,896]{1,0:T(8,128)(2,1)S(1)}, u32[]{:S(2)}, u32[]{:S(2)}) collective-permute-start(bf16[64,896]{1,0:T(8,128)(2,1)S(1)} %get-tuple-element.117), channel_id=1, source_target_pairs={{0,16},{4,20},{8,24},{12,28},{16,0},{20,4},{24,8},{28,12},{1,17},{... | collective-permute-start | bytes 344072 | tf_op jit(solution)/shard_map/ppermute | solution.py:532
  31.8 6.2 %collective-permute-start.18 = (bf16[64,896]{1,0:T(8,128)(2,1)S(1)}, bf16[64,896]{1,0:T(8,128)(2,1)S(1)}, u32[]{:S(2)}, u32[]{:S(2)}) collective-permute-start(bf16[64,896]{1,0:T(8,128)(2,1)S(1)} %get-tuple-element.118), channel_id=1, source_target_pairs={{0,8},{4,12},{8,0},{12,4},{16,24},{20,28},{24,16},{28,20},{1,9},{5... | collective-permute-start | bytes 344072 | tf_op jit(solution)/shard_map/ppermute | solution.py:532
  34.4 7.9 %collective-permute-start.13 = (bf16[32,1152]{1,0:T(8,128)(2,1)S(1)}, bf16[32,1152]{1,0:T(8,128)(2,1)S(1)}, u32[]{:S(2)}, u32[]{:S(2)}) collective-permute-start(bf16[32,1152]{1,0:T(8,128)(2,1)S(1)} %get-tuple-element.112), channel_id=1, source_target_pairs={{0,24},{4,28},{8,16},{12,20},{16,8},{20,12},{24,0},{28,4},{1,25},{... | collective-permute-start | bytes 221192 | tf_op jit(solution)/shard_map/ppermute | solution.py:532
  35.0 7.3 %collective-permute-start.14 = (bf16[32,1152]{1,0:T(8,128)(2,1)S(1)}, bf16[32,1152]{1,0:T(8,128)(2,1)S(1)}, u32[]{:S(2)}, u32[]{:S(2)}) collective-permute-start(bf16[32,1152]{1,0:T(8,128)(2,1)S(1)} %get-tuple-element.113), channel_id=1, source_target_pairs={{0,16},{4,20},{8,24},{12,28},{16,0},{20,4},{24,8},{28,12},{1,17},{... | collective-permute-start | bytes 221192 | tf_op jit(solution)/shard_map/ppermute | solution.py:532
  36.5 5.8 %collective-permute-start.15 = (bf16[32,1152]{1,0:T(8,128)(2,1)S(1)}, bf16[32,1152]{1,0:T(8,128)(2,1)S(1)}, u32[]{:S(2)}, u32[]{:S(2)}) collective-permute-start(bf16[32,1152]{1,0:T(8,128)(2,1)S(1)} %get-tuple-element.114), channel_id=1, source_target_pairs={{0,8},{4,12},{8,0},{12,4},{16,24},{20,28},{24,16},{28,20},{1,9},{5... | collective-permute-start | bytes 221192 | tf_op jit(solution)/shard_map/ppermute | solution.py:532
  38.1 4.2 %collective-permute-start.19 = (bf16[32,896]{1,0:T(8,128)(2,1)S(1)}, bf16[32,896]{1,0:T(8,128)(2,1)S(1)}, u32[]{:S(2)}, u32[]{:S(2)}) collective-permute-start(bf16[32,896]{1,0:T(8,128)(2,1)S(1)} %get-tuple-element.120), channel_id=1, source_target_pairs={{0,1},{1,0},{2,3},{3,2},{4,5},{5,4},{6,7},{7,6},{8,9},{9,8},{10,11... | collective-permute-start | bytes 172040 | tf_op jit(solution)/shard_map/ppermute | solution.py:532
  42.4 7.4 %collective-permute-start.23 = (bf16[32,2048]{1,0:T(8,128)(2,1)S(1)}, bf16[32,2048]{1,0:T(8,128)(2,1)S(1)}, u32[]{:S(2)}, u32[]{:S(2)}) collective-permute-start(bf16[32,2048]{1,0:T(8,128)(2,1)S(1)} %join_terms.1.kept_ref), channel_id=1, source_target_pairs={{0,2},{1,3},{2,0},{3,1},{4,6},{5,7},{6,4},{7,5},{8,10},{9,11},{10,... | collective-permute-start | bytes 393224 | tf_op jit(solution)/shard_map/ppermute | solution.py:532
  45.2 6.1 %collective-permute-start.20 = (bf16[128,512]{1,0:T(8,128)(2,1)S(1)}, bf16[128,512]{1,0:T(8,128)(2,1)S(1)}, u32[]{:S(2)}, u32[]{:S(2)}) collective-permute-start(bf16[128,512]{1,0:T(8,128)(2,1)S(1)} %get-tuple-element.122), channel_id=1, source_target_pairs={{0,24},{4,28},{8,16},{12,20},{16,8},{20,12},{24,0},{28,4},{1,25},{... | collective-permute-start | bytes 393224 | tf_op jit(solution)/shard_map/ppermute | solution.py:532
  46.2 6.3 %collective-permute-start.21 = (bf16[128,512]{1,0:T(8,128)(2,1)S(1)}, bf16[128,512]{1,0:T(8,128)(2,1)S(1)}, u32[]{:S(2)}, u32[]{:S(2)}) collective-permute-start(bf16[128,512]{1,0:T(8,128)(2,1)S(1)} %get-tuple-element.123), channel_id=1, source_target_pairs={{0,16},{4,20},{8,24},{12,28},{16,0},{20,4},{24,8},{28,12},{1,17},{... | collective-permute-start | bytes 393224 | tf_op jit(solution)/shard_map/ppermute | solution.py:532
  47.0 5.5 %collective-permute-start.22 = (bf16[128,512]{1,0:T(8,128)(2,1)S(1)}, bf16[128,512]{1,0:T(8,128)(2,1)S(1)}, u32[]{:S(2)}, u32[]{:S(2)}) collective-permute-start(bf16[128,512]{1,0:T(8,128)(2,1)S(1)} %get-tuple-element.124), channel_id=1, source_target_pairs={{0,8},{4,12},{8,0},{12,4},{16,24},{20,28},{24,16},{28,20},{1,9},{5... | collective-permute-start | bytes 393224 | tf_op jit(solution)/shard_map/ppermute | solution.py:532
  49.9 5.0 %collective-permute-start.24 = (bf16[32,2048]{1,0:T(8,128)(2,1)S(1)}, bf16[32,2048]{1,0:T(8,128)(2,1)S(1)}, u32[]{:S(2)}, u32[]{:S(2)}) collective-permute-start(bf16[32,2048]{1,0:T(8,128)(2,1)S(1)} %add_pairs.1.held_ref), channel_id=1, source_target_pairs={{0,1},{1,0},{2,3},{3,2},{4,5},{5,4},{6,7},{7,6},{8,9},{9,8},{10,11... | collective-permute-start | bytes 393224 | tf_op jit(solution)/shard_map/ppermute | solution.py:532

commit v14 on v12

--- a/solution.py
+++ b/solution.py
@@ -460,19 +460,17 @@
     send_ref[...], kept_ref[...] = split_rows(layer_sum(own_ref, got_1, got_2, got_3), 0)
 
 
-def join_kernel(own_ref, got_1, got_2, got_3, kept_ref, got_ref, out_ref):
-    total = layer_sum(own_ref, got_1, got_2, got_3).astype(BF16)
-    cut, width = FIRST_PART, kept_ref.shape[1]
-    out_ref[:, :cut] = total[:, :cut]
-    out_ref[:, cut : cut + width] = (kept_ref[...] + got_ref[...].astype(F32)).astype(BF16)
-    out_ref[:, cut + width :] = total[:, cut:]
+def layer_total_kernel(own_ref, got_1, got_2, got_3, out_ref):
+    out_ref[...] = layer_sum(own_ref, got_1, got_2, got_3).astype(BF16)
 
 
 def add_kernel(kept_ref, got_ref, out_ref):
     out_ref[...] = (kept_ref[...].astype(F32) + got_ref[...].astype(F32)).astype(BF16)
 
 
-def result_kernel(held_ref, got_ref, w_ref, gain_ref, qkv_ref, out_ref, grad_ref):
+def result_kernel(
+    first_held, first_got, held_ref, got_ref, w_ref, gain_ref, qkv_ref, out_ref, grad_ref
+):
     rows = qkv_ref.shape[0]
     chip, core, layer = here()
     at = (chip * 2 + core) * rows
@@ -480,16 +478,25 @@
     half = rows // 2
     width = out_ref.shape[1]
 
-    def ordered(lanes):
-        held, got = held_ref[:, lanes].astype(F32), got_ref[:, lanes].astype(F32)
-        return (jnp.where(upper, got, held), jnp.where(upper, held, got))
-
-    row_at = 3 * HW + width
+    def place(target, to, first, lanes):
+        held, got = (first_held, first_got) if first else (held_ref, got_ref)
+        held, got = held[:, lanes].astype(F32), got[:, lanes].astype(F32)
+        to = slice(to, to + held.shape[1])
+        target[:half, to], target[half:, to] = jnp.where(upper, got, held), jnp.where(upper, held, got)
+
+    def place_column(target, to, at, count):
+        in_first = max(0, min(count, FIRST_PART - at))
+        if in_first:
+            place(target, to, True, slice(at, at + in_first))
+        if in_first < count:
+            at -= FIRST_PART
+            place(target, to + in_first, False, slice(at + in_first, at + count))
+
     for i in range(3):
-        for at_from, at_to in ((row_at + i * HW, i * width), (i * HW, i * width + HW)):
-            to = slice(at_to, at_to + HW)
-            qkv_ref[:half, to], qkv_ref[half:, to] = ordered(slice(at_from, at_from + HW))
-    out_ref[:half], out_ref[half:] = ordered(slice(3 * HW, row_at))
+        row_at = FIRST_PART + i * HW
+        place(qkv_ref, i * width, True, slice(row_at, row_at + HW))
+        place_column(qkv_ref, i * width + HW, i * HW, HW)
+    place_column(out_ref, 0, 3 * HW, width)
     total = jnp.sum(qkv_ref[...] * w_ref[...].astype(F32), -1, keepdims=True)
     shape = (rows, gain_ref.shape[1])
     row = lax.broadcasted_iota(jnp.int32, shape, 0)
@@ -678,14 +685,17 @@
             [(second_half, BF16), (second_half, F32)],
             out_specs=[VMEM, PINNED],
         )
-        (pair_sum,) = call(
-            join_kernel,
-            "join_terms",
-            [(VMEM, one) for one in (first_owned, *first_got, kept, swap(to_next, "dp", 1))],
-            [((row_share // 2, col_width + row_width), BF16)],
-        )
+        (first_sum,) = call(
+            layer_total_kernel,
+            "first_add_chips",
+            [(VMEM, one) for one in (first_owned, *first_got)],
+            [(joint, BF16)],
+        )
+        first_held = add_two(first_sum, swap(first_sum, "dp", 2), "first_add_pairs")
+        first_other = swap(first_held, "dp", 1)
+        pair_sum = add_two(kept, swap(to_next, "dp", 1), "second_add_pair")
         *back, pair_sum = lax.optimization_barrier((*back, pair_sum))
-        held = add_two(pair_sum, swap(pair_sum, "dp", 2), "add_pairs")
+        held = add_two(pair_sum, swap(pair_sum, "dp", 2), "second_add_pairs")
         other = swap(held, "dp", 1)
         (grad,) = call(
             input_chip_kernel,
@@ -701,7 +711,10 @@
         sum_qkv, sum_out, sum_gain = call(
             result_kernel,
             "result",
-            [(VMEM, held), (VMEM, other), (VMEM, weight_rows), (VMEM, gain)],
+            [
+                (VMEM, one)
+                for one in (first_held, first_other, held, other, weight_rows, gain)
+            ],
             [((row_share, 3 * width), F32), ((row_share, width), F32), ((1, row_share), F32)],
         )
         sum_gain = sum_gain.reshape(row_share)

time: 55.1 us -> 57.9 us (1.051)
  starting transfers between devices: 24.4 us -> 27.7 us
    ppermute x22 -> x24, starting transfers between devices: 24.4 us -> 27.7 us  [swap(): return lax.ppermute(array, axis, [(i, i ^ bits) for i in range(count)])]
    ppermute x22 -> x24, waiting for transfers between devices: 14.5 us -> 14 us  [swap(): return lax.ppermute(array, axis, [(i, i ^ bits) for i in range(count)])]
    pallas_call x14 -> x16, Pallas kernels: 15.2 us -> 15.3 us  [call(): pl.pallas_call(kernel, out_shape=outs, in_specs=[spec for spec, _ in ins]...]
  transfers between devices with their start and end apart: 22 -> 24, of which waited for: 12 -> 10; matrix products, arithmetic and copies ran while one was open for 0% -> 0% of each run, Pallas kernels for 18% -> 17%
where the time goes in v14:
time: 57.9 us; the launch traced here: 57.8 us
  starting transfers between devices  27.7 us (48%)
  Pallas kernels  15.3 us (26%)
  waiting for transfers between devices  14 us (24%)
  between operations  0.76 us (1%)
    ppermute x24, starting transfers between devices, swap(): return lax.ppermute(array, axis, [(i, i ^ bits) for i in range(count)])  27.7 us
    pallas_call x16, Pallas kernels, call(): pl.pallas_call(kernel, out_shape=outs, in_specs=[spec for spec, _ in ins]...  15.3 us
    ppermute x24, waiting for transfers between devices, swap(): return lax.ppermute(array, axis, [(i, i ^ bits) for i in range(count)])  14 us
  transfers between devices with their start and end apart: 24, of which 10 were waited for; matrix products, arithmetic and copies ran while one was open for 0% of the time, Pallas kernels for 17%

profile of v14, /device:TPU:0, one launch (start us, length us, event | category | flops | bytes accessed | tf_op | source)
XLA Modules:
  0.0 57.8 jit_solution(13321753729009660038)
XLA Ops:
  0.6 1.3 %pack_columns.1 = (bf16[2,128,512]{2,1,0:T(8,128)(2,1)S(1)}, bf16[2,128,512]{2,1,0:T(8,128)(2,1)S(1)}, bf16[2,128,512]{2,1,0:T(8,128)(2,1)S(1)}) custom-call(bf16[512,512]{1,0:T(8,128)(2,1)} %bitcast.9, bf16[512,512]{1,0:T(8,128)(2,1)} %bitcast.11), custom_call_target="tpu_custom_call" | custom-call | tf_op jit(solution)/shard_map/pack_columns/pallas_call | solution.py:518
  1.9 3.0 %collective-permute-start.1 = (bf16[2,128,512]{2,1,0:T(8,128)(2,1)S(1)}, bf16[2,128,512]{2,1,0:T(8,128)(2,1)S(1)}, u32[]{:S(2)}, u32[]{:S(2)}) collective-permute-start(bf16[2,128,512]{2,1,0:T(8,128)(2,1)S(1)} %get-tuple-element.69), channel_id=1, source_target_pairs={{0,16},{4,20},{8,24},{12,28},{16,0},{20,4},{24,8},{28,12},{1,17},{... | collective-permute-start | bytes 786440 | tf_op jit(solution)/shard_map/ppermute | solution.py:532
  4.9 1.5 %collective-permute-start.2 = (bf16[2,128,512]{2,1,0:T(8,128)(2,1)S(1)}, bf16[2,128,512]{2,1,0:T(8,128)(2,1)S(1)}, u32[]{:S(2)}, u32[]{:S(2)}) collective-permute-start(bf16[2,128,512]{2,1,0:T(8,128)(2,1)S(1)} %get-tuple-element.70), channel_id=1, source_target_pairs={{0,8},{4,12},{8,0},{12,4},{16,24},{20,28},{24,16},{28,20},{1,9},{5... | collective-permute-start | bytes 786440 | tf_op jit(solution)/shard_map/ppermute | solution.py:532
  6.4 0.0 collective-permute-start
  6.5 7.7 %row_heads.1 = (bf16[4,64,384]{2,1,0:T(8,128)(2,1)S(1)}, bf16[4,64,384]{2,1,0:T(8,128)(2,1)S(1)}, bf16[4,64,384]{2,1,0:T(8,128)(2,1)S(1)}, bf16[4,64,384]{2,1,0:...) custom-call(bf16[512,512]{1,0:T(8,128)(2,1)} %bitcast.10, ...), custom_call_target="tpu_custom_call" | custom-call | tf_op jit(solution)/shard_map/row_heads/pallas_call | solution.py:518
  14.1 0.1 collective-permute-start.3
  14.2 0.5 collective-permute-start.4
  14.7 0.9 %collective-permute-done.3.got_1 = bf16[4,64,384]{2,1,0:T(8,128)(2,1)S(1)} collective-permute-done((bf16[4,64,384]{2,1,0:T(8,128)(2,1)S(1)}, bf16[4,64,384]{2,1,0:T(8,128)(2,1)S(1)}, u32[]{:S(2)}, u32[]{:S(2)}) %collective-permute-start.3) | collective-permute-done | bytes 196640 | tf_op jit(solution)/shard_map/ppermute | solution.py:532
  15.6 0.3 collective-permute-done.4.got_2
  15.9 0.1 row_add_cores.1
  16.1 0.0 collective-permute-done.2.near_3
  16.1 2.0 %collective-permute-done.near_1 = bf16[2,128,512]{2,1,0:T(8,128)(2,1)S(1)} collective-permute-done((bf16[2,128,512]{2,1,0:T(8,128)(2,1)S(1)}, bf16[2,128,512]{2,1,0:T(8,128)(2,1)S(1)}, u32[]{:S(2)}, u32[]{:S(2)}) %collective-permute-start) | collective-permute-done | bytes 262176 | tf_op jit(solution)/shard_map/ppermute | solution.py:532
  18.2 0.1 collective-permute-start.5
  18.2 1.9 %collective-permute-done.5.far_ref = bf16[4,2,64,512]{3,2,1,0:T(8,128)(2,1)S(1)} collective-permute-done((bf16[4,2,64,512]{3,2,1,0:T(8,128)(2,1)S(1)}, bf16[4,2,64,512]{3,2,1,0:T(8,128)(2,1)S(1)}, u32[]{:S(2)}, u32[]{:S(2)}) %collective-permute-start.5) | collective-permute-done | bytes 524320 | tf_op jit(solution)/shard_map/ppermute | solution.py:532
  20.1 3.1 %column_heads.1 = (bf16[4,64,1280]{2,1,0:T(8,128)(2,1)S(1)}, bf16[4,64,1280]{2,1,0:T(8,128)(2,1)S(1)}, bf16[512,768]{1,0:T(8,128)(2,1)S(1)}) custom-call(bf16[512,512]{1,0:T(8,128)(2,1)S(1)} %get-tuple-element.77.x_ref, bf16[512,512]{1,0:T(8,128)(2,1)S(1)} %get-tuple-element.78.cot_ref, bf16[2,128,512]{2,1,0:T(8,128)(2,1)S(1)} %collective-permute-done.near_1, ...), custom_call_target="tpu_custom_call" | custom-call | tf_op jit(solution)/shard_map/column_heads/pallas_call | solution.py:518
  23.2 0.2 collective-permute-start.7
  23.4 0.6 %column_grad_hidden.1 = (bf16[4,64,512]{2,1,0:T(8,128)(2,1)S(1)}, bf16[4,64,512]{2,1,0:T(8,128)(2,1)S(1)}) custom-call(bf16[512,768]{1,0:T(8,128)(2,1)S(1)} %get-tuple-element.86.grads_ref, bf16[512,768]{1,0:T(8,128)(2,1)S(1)} %get-tuple-element.82.w_ref), custom_call_target="tpu_custom_call" | custom-call | tf_op jit(solution)/shard_map/column_grad_hidden/pallas_call | solution.py:518
  24.0 0.4 collective-permute-start.6
  24.5 1.7 %collective-permute-start.16 = (bf16[4,32,768]{2,1,0:T(8,128)(2,1)S(1)}, bf16[4,32,768]{2,1,0:T(8,128)(2,1)S(1)}, u32[]{:S(2)}, u32[]{:S(2)}) collective-permute-start(bf16[4,32,768]{2,1,0:T(8,128)(2,1)S(1)} %get-tuple-element.114), channel_id=1, source_target_pairs={{0,1},{1,0},{2,3},{3,2},{4,5},{5,4},{6,7},{7,6},{8,9},{9,8},{10,11... | collective-permute-start | bytes 589832 | tf_op jit(solution)/shard_map/ppermute | solution.py:532
  26.2 0.2 column_add_cores.1
  26.4 2.5 %collective-permute-start.8 = (bf16[64,896]{1,0:T(8,128)(2,1)S(1)}, bf16[64,896]{1,0:T(8,128)(2,1)S(1)}, u32[]{:S(2)}, u32[]{:S(2)}) collective-permute-start(bf16[64,896]{1,0:T(8,128)(2,1)S(1)} %get-tuple-element.101), channel_id=1, source_target_pairs={{0,24},{4,28},{8,16},{12,20},{16,8},{20,12},{24,0},{28,4},{1,25},{... | collective-permute-start | bytes 344072 | tf_op jit(solution)/shard_map/ppermute | solution.py:532
  28.9 0.9 %collective-permute-start.15 = (bf16[4,32,384]{2,1,0:T(8,128)(2,1)S(1)}, bf16[4,32,384]{2,1,0:T(8,128)(2,1)S(1)}, u32[]{:S(2)}, u32[]{:S(2)}) collective-permute-start(bf16[4,32,384]{2,1,0:T(8,128)(2,1)S(1)} %get-tuple-element.111), channel_id=1, source_target_pairs={{0,1},{1,0},{2,3},{3,2},{4,5},{5,4},{6,7},{7,6},{8,9},{9,8},{10,11... | collective-permute-start | bytes 294920 | tf_op jit(solution)/shard_map/ppermute | solution.py:532
  29.8 0.5 collective-permute-start.9
  30.3 0.5 collective-permute-start.10
  30.9 0.8 %collective-permute-done.16.row_got = bf16[4,32,768]{2,1,0:T(8,128)(2,1)S(1)} collective-permute-done((bf16[4,32,768]{2,1,0:T(8,128)(2,1)S(1)}, bf16[4,32,768]{2,1,0:T(8,128)(2,1)S(1)}, u32[]{:S(2)}, u32[]{:S(2)}) %collective-permute-start.16) | collective-permute-done | bytes 196640 | tf_op jit(solution)/shard_map/ppermute | solution.py:532
  31.7 1.8 %collective-permute-done.15.got_ref = bf16[4,32,384]{2,1,0:T(8,128)(2,1)S(1)} collective-permute-done((bf16[4,32,384]{2,1,0:T(8,128)(2,1)S(1)}, bf16[4,32,384]{2,1,0:T(8,128)(2,1)S(1)}, u32[]{:S(2)}, u32[]{:S(2)}) %collective-permute-start.15) | collective-permute-done | bytes 98336 | tf_op jit(solution)/shard_map/ppermute | solution.py:532
  33.5 0.1 first_add_pair.1
  33.6 2.7 %collective-permute-start.17 = (bf16[32,1152]{1,0:T(8,128)(2,1)S(1)}, bf16[32,1152]{1,0:T(8,128)(2,1)S(1)}, u32[]{:S(2)}, u32[]{:S(2)}) collective-permute-start(bf16[32,1152]{1,0:T(8,128)(2,1)S(1)} %get-tuple-element.116), channel_id=1, source_target_pairs={{0,24},{4,28},{8,16},{12,20},{16,8},{20,12},{24,0},{28,4},{1,25},{... | collective-permute-start | bytes 221192 | tf_op jit(solution)/shard_map/ppermute | solution.py:532
  36.3 0.5 collective-permute-start.18
  36.8 0.0 collective-permute-done.8.got_1
  36.8 0.4 collective-permute-start.19
  37.2 0.0 collective-permute-done.9.got_2
  37.2 0.0 collective-permute-done.10.got_3
  37.2 0.1 second_add_chips.1
  37.2 1.8 %collective-permute-start.11 = (bf16[32,896]{1,0:T(8,128)(2,1)S(1)}, bf16[32,896]{1,0:T(8,128)(2,1)S(1)}, u32[]{:S(2)}, u32[]{:S(2)}) collective-permute-start(bf16[32,896]{1,0:T(8,128)(2,1)S(1)} %get-tuple-element.105), channel_id=1, source_target_pairs={{0,1},{1,0},{2,3},{3,2},{4,5},{5,4},{6,7},{7,6},{8,9},{9,8},{10,11... | collective-permute-start | bytes 172040 | tf_op jit(solution)/shard_map/ppermute | solution.py:532
  39.0 1.6 %collective-permute-done.18.got_2 = bf16[32,1152]{1,0:T(8,128)(2,1)S(1)} collective-permute-done((bf16[32,1152]{1,0:T(8,128)(2,1)S(1)}, bf16[32,1152]{1,0:T(8,128)(2,1)S(1)}, u32[]{:S(2)}, u32[]{:S(2)}) %collective-permute-start.18) | collective-permute-done | bytes 73760 | tf_op jit(solution)/shard_map/ppermute | solution.py:532
  40.6 0.5 collective-permute-done.19.got_3
  41.2 2.7 %collective-permute-start.20 = (bf16[32,1152]{1,0:T(8,128)(2,1)S(1)}, bf16[32,1152]{1,0:T(8,128)(2,1)S(1)}, u32[]{:S(2)}, u32[]{:S(2)}) collective-permute-start(bf16[32,1152]{1,0:T(8,128)(2,1)S(1)} %first_add_chips.1.kept_ref), channel_id=1, source_target_pairs={{0,2},{1,3},{2,0},{3,1},{4,6},{5,7},{6,4},{7,5},{8,10},{9,11},{10,... | collective-permute-start | bytes 221192 | tf_op jit(solution)/shard_map/ppermute | solution.py:532
  43.8 1.6 %collective-permute-start.12 = (bf16[128,512]{1,0:T(8,128)(2,1)S(1)}, bf16[128,512]{1,0:T(8,128)(2,1)S(1)}, u32[]{:S(2)}, u32[]{:S(2)}) collective-permute-start(bf16[128,512]{1,0:T(8,128)(2,1)S(1)} %get-tuple-element.107), channel_id=1, source_target_pairs={{0,24},{4,28},{8,16},{12,20},{16,8},{20,12},{24,0},{28,4},{1,25},{... | collective-permute-start | bytes 393224 | tf_op jit(solution)/shard_map/ppermute | solution.py:532
  45.4 0.5 collective-permute-start.13
  45.9 1.5 %collective-permute-start.14 = (bf16[128,512]{1,0:T(8,128)(2,1)S(1)}, bf16[128,512]{1,0:T(8,128)(2,1)S(1)}, u32[]{:S(2)}, u32[]{:S(2)}) collective-permute-start(bf16[128,512]{1,0:T(8,128)(2,1)S(1)} %get-tuple-element.109), channel_id=1, source_target_pairs={{0,8},{4,12},{8,0},{12,4},{16,24},{20,28},{24,16},{28,20},{1,9},{5... | collective-permute-start | bytes 393224 | tf_op jit(solution)/shard_map/ppermute | solution.py:532
  47.4 0.4 collective-permute-start.22
  47.8 1.6 %collective-permute-start.21 = (bf16[32,1152]{1,0:T(8,128)(2,1)S(1)}, bf16[32,1152]{1,0:T(8,128)(2,1)S(1)}, u32[]{:S(2)}, u32[]{:S(2)}) collective-permute-start(bf16[32,1152]{1,0:T(8,128)(2,1)S(1)} %first_add_pairs.1.first_held), channel_id=1, source_target_pairs={{0,1},{1,0},{2,3},{3,2},{4,5},{5,4},{6,7},{7,6},{8,9},{9,8},{10,11... | collective-permute-start | bytes 221192 | tf_op jit(solution)/shard_map/ppermute | solution.py:532
  49.4 3.1 %collective-permute-done.22.got_ref = bf16[32,896]{1,0:T(8,128)(2,1)S(1)} collective-permute-done((bf16[32,896]{1,0:T(8,128)(2,1)S(1)}, bf16[32,896]{1,0:T(8,128)(2,1)S(1)}, u32[]{:S(2)}, u32[]{:S(2)}) %collective-permute-start.22) | collective-permute-done | bytes 57376 | tf_op jit(solution)/shard_map/ppermute | solution.py:532
  52.6 2.1 %collective-permute-start.23 = (bf16[32,896]{1,0:T(8,128)(2,1)S(1)}, bf16[32,896]{1,0:T(8,128)(2,1)S(1)}, u32[]{:S(2)}, u32[]{:S(2)}) collective-permute-start(bf16[32,896]{1,0:T(8,128)(2,1)S(1)} %second_add_pairs.1.held_ref), channel_id=1, source_target_pairs={{0,1},{1,0},{2,3},{3,2},{4,5},{5,4},{6,7},{7,6},{8,9},{9,8},{10,11... | collective-permute-start | bytes 172040 | tf_op jit(solution)/shard_map/ppermute | solution.py:532
  54.7 1.2 %input_grad.1 = bf16[512,512]{1,0:T(8,128)(2,1)} custom-call(f32[512,512]{1,0:T(8,128)S(1)} %get-tuple-element.66.base_ref, f32[512,512]{1,0:T(8,128)S(1)} %get-tuple-element.67.normed_ref, f32[512,1]{1,0:T(8,128)S(1)} %get-tuple-element.68.inverse_ref, f32[1,512]{1,0:T(1,128)S(1)} %bitcast.7, bf16[128,512]{1,0:T(8,128)(2,1)S(1)} %get-tuple-element.106.own_ref, ...), custom_call_target="tpu_custom_call" | custom-call | tf_op jit(solution)/shard_map/input_grad/pallas_call | solution.py:518
  55.9 1.0 %collective-permute-done.23.got_ref = bf16[32,896]{1,0:T(8,128)(2,1)S(1)} collective-permute-done((bf16[32,896]{1,0:T(8,128)(2,1)S(1)}, bf16[32,896]{1,0:T(8,128)(2,1)S(1)}, u32[]{:S(2)}, u32[]{:S(2)}) %collective-permute-start.23) | collective-permute-done | bytes 57376 | tf_op jit(solution)/shard_map/ppermute | solution.py:532
  56.9 0.9 %result.1 = (f32[64,1536]{1,0:T(8,128)}, f32[64,512]{1,0:T(8,128)}, f32[1,64]{1,0:T(1,128)}) custom-call(bf16[32,1152]{1,0:T(8,128)(2,1)S(1)} %first_add_pairs.1.first_held, bf16[32,1152]{1,0:T(8,128)(2,1)S(1)} %collective-permute-done.21.first_got, bf16[32,896]{1,0:T(8,128)(2,1)S(1)} %second_add_pairs.1.held_ref, ...), custom_call_target="tpu_custom_call" | custom-call | tf_op jit(solution)/shard_map/result/pallas_call | solution.py:518
  (18 shorter events, 0.2 us)
Async XLA Ops:
  1.9 14.2 %collective-permute-start.1 = (bf16[2,128,512]{2,1,0:T(8,128)(2,1)S(1)}, bf16[2,128,512]{2,1,0:T(8,128)(2,1)S(1)}, u32[]{:S(2)}, u32[]{:S(2)}) collective-permute-start(bf16[2,128,512]{2,1,0:T(8,128)(2,1)S(1)} %get-tuple-element.69), channel_id=1, source_target_pairs={{0,16},{4,20},{8,24},{12,28},{16,0},{20,4},{24,8},{28,12},{1,17},{... | collective-permute-start | bytes 786440 | tf_op jit(solution)/shard_map/ppermute | solution.py:532
  4.9 11.1 %collective-permute-start.2 = (bf16[2,128,512]{2,1,0:T(8,128)(2,1)S(1)}, bf16[2,128,512]{2,1,0:T(8,128)(2,1)S(1)}, u32[]{:S(2)}, u32[]{:S(2)}) collective-permute-start(bf16[2,128,512]{2,1,0:T(8,128)(2,1)S(1)} %get-tuple-element.70), channel_id=1, source_target_pairs={{0,8},{4,12},{8,0},{12,4},{16,24},{20,28},{24,16},{28,20},{1,9},{5... | collective-permute-start | bytes 786440 | tf_op jit(solution)/shard_map/ppermute | solution.py:532
  6.4 11.7 %collective-permute-start = (bf16[2,128,512]{2,1,0:T(8,128)(2,1)S(1)}, bf16[2,128,512]{2,1,0:T(8,128)(2,1)S(1)}, u32[]{:S(2)}, u32[]{:S(2)}) collective-permute-start(bf16[2,128,512]{2,1,0:T(8,128)(2,1)S(1)} %get-tuple-element.64), channel_id=1, source_target_pairs={{0,24},{4,28},{8,16},{12,20},{16,8},{20,12},{24,0},{28,4},{1,25},{... | collective-permute-start | bytes 786440 | tf_op jit(solution)/shard_map/ppermute | solution.py:532
  14.1 1.5 %collective-permute-start.3 = (bf16[4,64,384]{2,1,0:T(8,128)(2,1)S(1)}, bf16[4,64,384]{2,1,0:T(8,128)(2,1)S(1)}, u32[]{:S(2)}, u32[]{:S(2)}) collective-permute-start(bf16[4,64,384]{2,1,0:T(8,128)(2,1)S(1)} %get-tuple-element.73), channel_id=1, source_target_pairs={{0,4},{4,0},{8,12},{12,8},{16,20},{20,16},{24,28},{28,24},{1,5},{5... | collective-permute-start | bytes 589832 | tf_op jit(solution)/shard_map/ppermute | solution.py:532
  14.2 1.7 %collective-permute-start.4 = (bf16[4,64,384]{2,1,0:T(8,128)(2,1)S(1)}, bf16[4,64,384]{2,1,0:T(8,128)(2,1)S(1)}, u32[]{:S(2)}, u32[]{:S(2)}) collective-permute-start(bf16[4,64,384]{2,1,0:T(8,128)(2,1)S(1)} %get-tuple-element.74), channel_id=1, source_target_pairs={{0,4},{4,0},{8,12},{12,8},{16,20},{20,16},{24,28},{28,24},{1,5},{5... | collective-permute-start | bytes 589832 | tf_op jit(solution)/shard_map/ppermute | solution.py:532
  15.9 4.2 %copy-start = (f32[512]{0:T(512)S(1)}, f32[512]{0:T(512)}, u32[]{:S(2)}) copy-start(f32[512]{0:T(512)} %param.6) | copy-start | bytes 6148
  18.2 2.0 %collective-permute-start.5 = (bf16[4,2,64,512]{3,2,1,0:T(8,128)(2,1)S(1)}, bf16[4,2,64,512]{3,2,1,0:T(8,128)(2,1)S(1)}, u32[]{:S(2)}, u32[]{:S(2)}) collective-permute-start(bf16[4,2,64,512]{3,2,1,0:T(8,128)(2,1)S(1)} %pack_other_core.1), channel_id=1, source_target_pairs={{0,4},{4,0},{8,12},{12,8},{16,20},{20,16},{24,28},{28,24},{1,5},{5... | collective-permute-start | bytes 1572872 | tf_op jit(solution)/shard_map/ppermute | solution.py:532
  23.2 3.0 %collective-permute-start.7 = (bf16[4,64,1280]{2,1,0:T(8,128)(2,1)S(1)}, bf16[4,64,1280]{2,1,0:T(8,128)(2,1)S(1)}, u32[]{:S(2)}, u32[]{:S(2)}) collective-permute-start(bf16[4,64,1280]{2,1,0:T(8,128)(2,1)S(1)} %get-tuple-element.99), channel_id=1, source_target_pairs={{0,4},{4,0},{8,12},{12,8},{16,20},{20,16},{24,28},{28,24},{1,5},{5... | collective-permute-start | bytes 1966088 | tf_op jit(solution)/shard_map/ppermute | solution.py:532
  24.0 6.3 %collective-permute-start.6 = (bf16[4,64,512]{2,1,0:T(8,128)(2,1)S(1)}, bf16[4,64,512]{2,1,0:T(8,128)(2,1)S(1)}, u32[]{:S(2)}, u32[]{:S(2)}) collective-permute-start(bf16[4,64,512]{2,1,0:T(8,128)(2,1)S(1)} %get-tuple-element.89), channel_id=1, source_target_pairs={{0,4},{4,0},{8,12},{12,8},{16,20},{20,16},{24,28},{28,24},{1,5},{5... | collective-permute-start | bytes 786440 | tf_op jit(solution)/shard_map/ppermute | solution.py:532
  24.5 7.2 %collective-permute-start.16 = (bf16[4,32,768]{2,1,0:T(8,128)(2,1)S(1)}, bf16[4,32,768]{2,1,0:T(8,128)(2,1)S(1)}, u32[]{:S(2)}, u32[]{:S(2)}) collective-permute-start(bf16[4,32,768]{2,1,0:T(8,128)(2,1)S(1)} %get-tuple-element.114), channel_id=1, source_target_pairs={{0,1},{1,0},{2,3},{3,2},{4,5},{5,4},{6,7},{7,6},{8,9},{9,8},{10,11... | collective-permute-start | bytes 589832 | tf_op jit(solution)/shard_map/ppermute | solution.py:532
  26.4 10.4 %collective-permute-start.8 = (bf16[64,896]{1,0:T(8,128)(2,1)S(1)}, bf16[64,896]{1,0:T(8,128)(2,1)S(1)}, u32[]{:S(2)}, u32[]{:S(2)}) collective-permute-start(bf16[64,896]{1,0:T(8,128)(2,1)S(1)} %get-tuple-element.101), channel_id=1, source_target_pairs={{0,24},{4,28},{8,16},{12,20},{16,8},{20,12},{24,0},{28,4},{1,25},{... | collective-permute-start | bytes 344072 | tf_op jit(solution)/shard_map/ppermute | solution.py:532
  28.9 4.6 %collective-permute-start.15 = (bf16[4,32,384]{2,1,0:T(8,128)(2,1)S(1)}, bf16[4,32,384]{2,1,0:T(8,128)(2,1)S(1)}, u32[]{:S(2)}, u32[]{:S(2)}) collective-permute-start(bf16[4,32,384]{2,1,0:T(8,128)(2,1)S(1)} %get-tuple-element.111), channel_id=1, source_target_pairs={{0,1},{1,0},{2,3},{3,2},{4,5},{5,4},{6,7},{7,6},{8,9},{9,8},{10,11... | collective-permute-start | bytes 294920 | tf_op jit(solution)/shard_map/ppermute | solution.py:532
  29.8 7.3 %collective-permute-start.9 = (bf16[64,896]{1,0:T(8,128)(2,1)S(1)}, bf16[64,896]{1,0:T(8,128)(2,1)S(1)}, u32[]{:S(2)}, u32[]{:S(2)}) collective-permute-start(bf16[64,896]{1,0:T(8,128)(2,1)S(1)} %get-tuple-element.102), channel_id=1, source_target_pairs={{0,16},{4,20},{8,24},{12,28},{16,0},{20,4},{24,8},{28,12},{1,17},{... | collective-permute-start | bytes 344072 | tf_op jit(solution)/shard_map/ppermute | solution.py:532
  30.3 6.8 %collective-permute-start.10 = (bf16[64,896]{1,0:T(8,128)(2,1)S(1)}, bf16[64,896]{1,0:T(8,128)(2,1)S(1)}, u32[]{:S(2)}, u32[]{:S(2)}) collective-permute-start(bf16[64,896]{1,0:T(8,128)(2,1)S(1)} %get-tuple-element.103), channel_id=1, source_target_pairs={{0,8},{4,12},{8,0},{12,4},{16,24},{20,28},{24,16},{28,20},{1,9},{5... | collective-permute-start | bytes 344072 | tf_op jit(solution)/shard_map/ppermute | solution.py:532
  33.6 5.4 %collective-permute-start.17 = (bf16[32,1152]{1,0:T(8,128)(2,1)S(1)}, bf16[32,1152]{1,0:T(8,128)(2,1)S(1)}, u32[]{:S(2)}, u32[]{:S(2)}) collective-permute-start(bf16[32,1152]{1,0:T(8,128)(2,1)S(1)} %get-tuple-element.116), channel_id=1, source_target_pairs={{0,24},{4,28},{8,16},{12,20},{16,8},{20,12},{24,0},{28,4},{1,25},{... | collective-permute-start | bytes 221192 | tf_op jit(solution)/shard_map/ppermute | solution.py:532
  36.3 4.4 %collective-permute-start.18 = (bf16[32,1152]{1,0:T(8,128)(2,1)S(1)}, bf16[32,1152]{1,0:T(8,128)(2,1)S(1)}, u32[]{:S(2)}, u32[]{:S(2)}) collective-permute-start(bf16[32,1152]{1,0:T(8,128)(2,1)S(1)} %get-tuple-element.117), channel_id=1, source_target_pairs={{0,16},{4,20},{8,24},{12,28},{16,0},{20,4},{24,8},{28,12},{1,17},{... | collective-permute-start | bytes 221192 | tf_op jit(solution)/shard_map/ppermute | solution.py:532
  36.8 4.4 %collective-permute-start.19 = (bf16[32,1152]{1,0:T(8,128)(2,1)S(1)}, bf16[32,1152]{1,0:T(8,128)(2,1)S(1)}, u32[]{:S(2)}, u32[]{:S(2)}) collective-permute-start(bf16[32,1152]{1,0:T(8,128)(2,1)S(1)} %get-tuple-element.118), channel_id=1, source_target_pairs={{0,8},{4,12},{8,0},{12,4},{16,24},{20,28},{24,16},{28,20},{1,9},{5... | collective-permute-start | bytes 221192 | tf_op jit(solution)/shard_map/ppermute | solution.py:532
  37.2 6.6 %collective-permute-start.11 = (bf16[32,896]{1,0:T(8,128)(2,1)S(1)}, bf16[32,896]{1,0:T(8,128)(2,1)S(1)}, u32[]{:S(2)}, u32[]{:S(2)}) collective-permute-start(bf16[32,896]{1,0:T(8,128)(2,1)S(1)} %get-tuple-element.105), channel_id=1, source_target_pairs={{0,1},{1,0},{2,3},{3,2},{4,5},{5,4},{6,7},{7,6},{8,9},{9,8},{10,11... | collective-permute-start | bytes 172040 | tf_op jit(solution)/shard_map/ppermute | solution.py:532
  41.2 6.6 %collective-permute-start.20 = (bf16[32,1152]{1,0:T(8,128)(2,1)S(1)}, bf16[32,1152]{1,0:T(8,128)(2,1)S(1)}, u32[]{:S(2)}, u32[]{:S(2)}) collective-permute-start(bf16[32,1152]{1,0:T(8,128)(2,1)S(1)} %first_add_chips.1.kept_ref), channel_id=1, source_target_pairs={{0,2},{1,3},{2,0},{3,1},{4,6},{5,7},{6,4},{7,5},{8,10},{9,11},{10,... | collective-permute-start | bytes 221192 | tf_op jit(solution)/shard_map/ppermute | solution.py:532
  43.8 10.9 %collective-permute-start.12 = (bf16[128,512]{1,0:T(8,128)(2,1)S(1)}, bf16[128,512]{1,0:T(8,128)(2,1)S(1)}, u32[]{:S(2)}, u32[]{:S(2)}) collective-permute-start(bf16[128,512]{1,0:T(8,128)(2,1)S(1)} %get-tuple-element.107), channel_id=1, source_target_pairs={{0,24},{4,28},{8,16},{12,20},{16,8},{20,12},{24,0},{28,4},{1,25},{... | collective-permute-start | bytes 393224 | tf_op jit(solution)/shard_map/ppermute | solution.py:532
  45.4 9.3 %collective-permute-start.13 = (bf16[128,512]{1,0:T(8,128)(2,1)S(1)}, bf16[128,512]{1,0:T(8,128)(2,1)S(1)}, u32[]{:S(2)}, u32[]{:S(2)}) collective-permute-start(bf16[128,512]{1,0:T(8,128)(2,1)S(1)} %get-tuple-element.108), channel_id=1, source_target_pairs={{0,16},{4,20},{8,24},{12,28},{16,0},{20,4},{24,8},{28,12},{1,17},{... | collective-permute-start | bytes 393224 | tf_op jit(solution)/shard_map/ppermute | solution.py:532
  45.9 8.8 %collective-permute-start.14 = (bf16[128,512]{1,0:T(8,128)(2,1)S(1)}, bf16[128,512]{1,0:T(8,128)(2,1)S(1)}, u32[]{:S(2)}, u32[]{:S(2)}) collective-permute-start(bf16[128,512]{1,0:T(8,128)(2,1)S(1)} %get-tuple-element.109), channel_id=1, source_target_pairs={{0,8},{4,12},{8,0},{12,4},{16,24},{20,28},{24,16},{28,20},{1,9},{5... | collective-permute-start | bytes 393224 | tf_op jit(solution)/shard_map/ppermute | solution.py:532
  47.4 5.2 %collective-permute-start.22 = (bf16[32,896]{1,0:T(8,128)(2,1)S(1)}, bf16[32,896]{1,0:T(8,128)(2,1)S(1)}, u32[]{:S(2)}, u32[]{:S(2)}) collective-permute-start(bf16[32,896]{1,0:T(8,128)(2,1)S(1)} %second_add_pair.1.kept_ref), channel_id=1, source_target_pairs={{0,2},{1,3},{2,0},{3,1},{4,6},{5,7},{6,4},{7,5},{8,10},{9,11},{10,... | collective-permute-start | bytes 172040 | tf_op jit(solution)/shard_map/ppermute | solution.py:532
  47.8 9.1 %collective-permute-start.21 = (bf16[32,1152]{1,0:T(8,128)(2,1)S(1)}, bf16[32,1152]{1,0:T(8,128)(2,1)S(1)}, u32[]{:S(2)}, u32[]{:S(2)}) collective-permute-start(bf16[32,1152]{1,0:T(8,128)(2,1)S(1)} %first_add_pairs.1.first_held), channel_id=1, source_target_pairs={{0,1},{1,0},{2,3},{3,2},{4,5},{5,4},{6,7},{7,6},{8,9},{9,8},{10,11... | collective-permute-start | bytes 221192 | tf_op jit(solution)/shard_map/ppermute | solution.py:532
  52.6 4.3 %collective-permute-start.23 = (bf16[32,896]{1,0:T(8,128)(2,1)S(1)}, bf16[32,896]{1,0:T(8,128)(2,1)S(1)}, u32[]{:S(2)}, u32[]{:S(2)}) collective-permute-start(bf16[32,896]{1,0:T(8,128)(2,1)S(1)} %second_add_pairs.1.held_ref), channel_id=1, source_target_pairs={{0,1},{1,0},{2,3},{3,2},{4,5},{5,4},{6,7},{7,6},{8,9},{9,8},{10,11... | collective-permute-start | bytes 172040 | tf_op jit(solution)/shard_map/ppermute | solution.py:532

commit v15 on v12

--- a/solution.py
+++ b/solution.py
@@ -301,7 +301,7 @@
 
 
 def column_chip_kernel(
-    x_ref, cot_ref, near_1, near_2, near_3, far_ref, gain_ref, w_ref, wo_ref, row_out_ref,
+    x_ref, cot_ref, near_1, near_2, near_3, far_ref, last_ref, gain_ref, w_ref, wo_ref, row_out_ref,
     send_ref, keep_ref, grads_ref,
 ):
     chip, core, _ = here()
@@ -312,8 +312,9 @@
 
     def tokens(which, mine):
         pieces = [mine[at, :], far_ref[0, which]]
-        for i, near in enumerate((near_1, near_2, near_3)):
-            pieces += [near[which, half, :], far_ref[i + 1, which]]
+        fars = last_ref[which], far_ref[1, which], far_ref[2, which]
+        for near, far in zip((near_1, near_2, near_3), fars):
+            pieces += [near[which, half, :], far]
         starts = range(0, share, group)
         return jnp.concatenate(
             [piece[start : start + group] for start in starts for piece in pieces], 0
@@ -335,14 +336,22 @@
     split_cores(term_out, *refs, slice(chips // 2, chips), out_lanes)
 
 
-def far_kernel(x_ref, cot_ref, near_1, near_2, near_3, far_ref):
+def other_core(near, share):
+    at = pl.ds(pl.multiple_of((1 - here()[1]) * share, share), share)
+    return near[:, at, :]
+
+
+def far_kernel(x_ref, cot_ref, near_2, near_3, far_ref):
     chip, core, _ = here()
     share = far_ref.shape[2]
     at = pl.ds(pl.multiple_of((chip * 2 + 1 - core) * share, share), share)
     far_ref[0, 0], far_ref[0, 1] = x_ref[at, :], cot_ref[at, :]
-    at = pl.ds(pl.multiple_of((1 - core) * share, share), share)
-    for i, near in enumerate((near_1, near_2, near_3)):
-        far_ref[i + 1] = near[:, at, :]
+    for i, near in enumerate((near_2, near_3)):
+        far_ref[i + 1] = other_core(near, share)
+
+
+def last_far_kernel(near_1, far_ref):
+    far_ref[...] = other_core(near_1, far_ref.shape[1])
 
 
 def back_kernel(grads_ref, w_ref, back_ref):
@@ -612,12 +621,19 @@
             [(half_block, BF16), (half_block, F32)],
             out_specs=[VMEM, PINNED],
         )
-        *near, row_kept = lax.optimization_barrier((*near, row_kept))
+        col_weight, row_kept = lax.optimization_barrier((col_weight, row_kept))
         (far,) = call(
             far_kernel,
             "pack_other_core",
-            [(VMEM, one) for one in (x_near, cot_near, *near)],
-            [((chips, 2, share, width), BF16)],
+            [(VMEM, one) for one in (x_near, cot_near, *near[1:])],
+            [((3, 2, share, width), BF16)],
+        )
+        near[0], _ = lax.optimization_barrier((near[0], far))
+        (last,) = call(
+            last_far_kernel,
+            "pack_other_core_last",
+            [(VMEM, near[0])],
+            [((2, share, width), BF16)],
         )
         send, keep, col_grads = call(
             column_chip_kernel,
@@ -625,7 +641,7 @@
             [
                 (VMEM, one)
                 for one in (
-                    x_near, cot_near, *near, swap(far, "seq", 1),
+                    x_near, cot_near, *near, swap(far, "seq", 1), swap(last, "seq", 1),
                     gain, col_weight, col_out_weight, row_out,
                 )
             ],

time: 55.1 us -> 54.5 us (0.989)
  waiting for transfers between devices: 14.5 us -> 13.8 us
    ppermute x22 -> x23, waiting for transfers between devices: 14.5 us -> 13.8 us  [swap(): return lax.ppermute(array, axis, [(i, i ^ bits) for i in range(count)])]
    ppermute x22 -> x23, starting transfers between devices: 24.4 us -> 24.5 us  [swap(): return lax.ppermute(array, axis, [(i, i ^ bits) for i in range(count)])]
    pallas_call x14 -> x15, Pallas kernels: 15.2 us -> 15.2 us  [call(): pl.pallas_call(kernel, out_shape=outs, in_specs=[spec for spec, _ in ins]...]
  transfers between devices with their start and end apart: 22 -> 23, of which waited for: 12 -> 12; matrix products, arithmetic and copies ran while one was open for 0% -> 0% of each run, Pallas kernels for 18% -> 18%
where the time goes in v15:
time: 54.5 us; the launch traced here: 54.3 us
  starting transfers between devices  24.5 us (45%)
  Pallas kernels  15.2 us (28%)
  waiting for transfers between devices  13.8 us (25%)
  between operations  0.77 us (1%)
    ppermute x23, starting transfers between devices, swap(): return lax.ppermute(array, axis, [(i, i ^ bits) for i in range(count)])  24.5 us
    pallas_call x15, Pallas kernels, call(): pl.pallas_call(kernel, out_shape=outs, in_specs=[spec for spec, _ in ins]...  15.2 us
    ppermute x23, waiting for transfers between devices, swap(): return lax.ppermute(array, axis, [(i, i ^ bits) for i in range(count)])  13.8 us
  transfers between devices with their start and end apart: 23, of which 12 were waited for; matrix products, arithmetic and copies ran while one was open for 0% of the time, Pallas kernels for 18%

profile of v15, /device:TPU:0, one launch (start us, length us, event | category | flops | bytes accessed | tf_op | source)
XLA Modules:
  0.0 54.3 jit_solution(9154900109968347911)
XLA Ops:
  0.6 1.3 %pack_columns.1 = (bf16[2,128,512]{2,1,0:T(8,128)(2,1)S(1)}, bf16[2,128,512]{2,1,0:T(8,128)(2,1)S(1)}, bf16[2,128,512]{2,1,0:T(8,128)(2,1)S(1)}) custom-call(bf16[512,512]{1,0:T(8,128)(2,1)} %bitcast.9, bf16[512,512]{1,0:T(8,128)(2,1)} %bitcast.11), custom_call_target="tpu_custom_call" | custom-call | tf_op jit(solution)/shard_map/pack_columns/pallas_call | solution.py:520
  1.9 3.0 %collective-permute-start.3 = (bf16[2,128,512]{2,1,0:T(8,128)(2,1)S(1)}, bf16[2,128,512]{2,1,0:T(8,128)(2,1)S(1)}, u32[]{:S(2)}, u32[]{:S(2)}) collective-permute-start(bf16[2,128,512]{2,1,0:T(8,128)(2,1)S(1)} %get-tuple-element.77), channel_id=1, source_target_pairs={{0,16},{4,20},{8,24},{12,28},{16,0},{20,4},{24,8},{28,12},{1,17},{... | collective-permute-start | bytes 786440 | tf_op jit(solution)/shard_map/ppermute | solution.py:534
  4.9 1.5 %collective-permute-start.4 = (bf16[2,128,512]{2,1,0:T(8,128)(2,1)S(1)}, bf16[2,128,512]{2,1,0:T(8,128)(2,1)S(1)}, u32[]{:S(2)}, u32[]{:S(2)}) collective-permute-start(bf16[2,128,512]{2,1,0:T(8,128)(2,1)S(1)} %get-tuple-element.78), channel_id=1, source_target_pairs={{0,8},{4,12},{8,0},{12,4},{16,24},{20,28},{24,16},{28,20},{1,9},{5... | collective-permute-start | bytes 786440 | tf_op jit(solution)/shard_map/ppermute | solution.py:534
  6.4 0.0 collective-permute-start.2
  6.5 7.7 %row_heads.1 = (bf16[4,64,384]{2,1,0:T(8,128)(2,1)S(1)}, bf16[4,64,384]{2,1,0:T(8,128)(2,1)S(1)}, bf16[4,64,384]{2,1,0:T(8,128)(2,1)S(1)}, bf16[4,64,384]{2,1,0:...) custom-call(bf16[512,512]{1,0:T(8,128)(2,1)} %bitcast.10, ...), custom_call_target="tpu_custom_call" | custom-call | tf_op jit(solution)/shard_map/row_heads/pallas_call | solution.py:520
  14.1 0.0 collective-permute-done.3.near_2
  14.1 0.0 collective-permute-done.4.near_3
  14.2 0.1 collective-permute-start.5
  14.3 0.5 collective-permute-start
  14.8 0.1 collective-permute-start.1
  14.9 3.2 %collective-permute-done.2.near_1 = bf16[2,128,512]{2,1,0:T(8,128)(2,1)S(1)} collective-permute-done((bf16[2,128,512]{2,1,0:T(8,128)(2,1)S(1)}, bf16[2,128,512]{2,1,0:T(8,128)(2,1)S(1)}, u32[]{:S(2)}, u32[]{:S(2)}) %collective-permute-start.2) | collective-permute-done | bytes 262176 | tf_op jit(solution)/shard_map/ppermute | solution.py:534
  18.1 0.1 collective-permute-start.6
  18.2 0.1 row_add_cores.1
  18.4 1.2 %collective-permute-done.6.last_ref = bf16[2,64,512]{2,1,0:T(8,128)(2,1)S(1)} collective-permute-done((bf16[2,64,512]{2,1,0:T(8,128)(2,1)S(1)}, bf16[2,64,512]{2,1,0:T(8,128)(2,1)S(1)}, u32[]{:S(2)}, u32[]{:S(2)}) %collective-permute-start.6) | collective-permute-done | bytes 131104 | tf_op jit(solution)/shard_map/ppermute | solution.py:534
  19.6 3.1 %column_heads.1 = (bf16[4,64,1280]{2,1,0:T(8,128)(2,1)S(1)}, bf16[4,64,1280]{2,1,0:T(8,128)(2,1)S(1)}, bf16[512,768]{1,0:T(8,128)(2,1)S(1)}) custom-call(bf16[512,512]{1,0:T(8,128)(2,1)S(1)} %get-tuple-element.75.x_ref, bf16[512,512]{1,0:T(8,128)(2,1)S(1)} %get-tuple-element.76.cot_ref, bf16[2,128,512]{2,1,0:T(8,128)(2,1)S(1)} %collective-permute-done.2.near_1, ...), custom_call_target="tpu_custom_call" | custom-call | tf_op jit(solution)/shard_map/column_heads/pallas_call | solution.py:520
  22.6 0.2 collective-permute-start.8
  22.9 0.6 %column_grad_hidden.1 = (bf16[4,64,512]{2,1,0:T(8,128)(2,1)S(1)}, bf16[4,64,512]{2,1,0:T(8,128)(2,1)S(1)}) custom-call(bf16[512,768]{1,0:T(8,128)(2,1)S(1)} %get-tuple-element.84.grads_ref, bf16[512,768]{1,0:T(8,128)(2,1)S(1)} %get-tuple-element.80.w_ref), custom_call_target="tpu_custom_call" | custom-call | tf_op jit(solution)/shard_map/column_grad_hidden/pallas_call | solution.py:520
  23.5 0.4 collective-permute-start.7
  23.9 1.7 %collective-permute-start.10 = (bf16[4,32,768]{2,1,0:T(8,128)(2,1)S(1)}, bf16[4,32,768]{2,1,0:T(8,128)(2,1)S(1)}, u32[]{:S(2)}, u32[]{:S(2)}) collective-permute-start(bf16[4,32,768]{2,1,0:T(8,128)(2,1)S(1)} %get-tuple-element.102), channel_id=1, source_target_pairs={{0,1},{1,0},{2,3},{3,2},{4,5},{5,4},{6,7},{7,6},{8,9},{9,8},{10,11... | collective-permute-start | bytes 589832 | tf_op jit(solution)/shard_map/ppermute | solution.py:534
  25.6 0.2 column_add_cores.1
  25.8 2.5 %collective-permute-start.14 = (bf16[64,896]{1,0:T(8,128)(2,1)S(1)}, bf16[64,896]{1,0:T(8,128)(2,1)S(1)}, u32[]{:S(2)}, u32[]{:S(2)}) collective-permute-start(bf16[64,896]{1,0:T(8,128)(2,1)S(1)} %get-tuple-element.108), channel_id=1, source_target_pairs={{0,24},{4,28},{8,16},{12,20},{16,8},{20,12},{24,0},{28,4},{1,25},{... | collective-permute-start | bytes 344072 | tf_op jit(solution)/shard_map/ppermute | solution.py:534
  28.3 0.9 %collective-permute-start.9 = (bf16[4,32,384]{2,1,0:T(8,128)(2,1)S(1)}, bf16[4,32,384]{2,1,0:T(8,128)(2,1)S(1)}, u32[]{:S(2)}, u32[]{:S(2)}) collective-permute-start(bf16[4,32,384]{2,1,0:T(8,128)(2,1)S(1)} %get-tuple-element.99), channel_id=1, source_target_pairs={{0,1},{1,0},{2,3},{3,2},{4,5},{5,4},{6,7},{7,6},{8,9},{9,8},{10,11... | collective-permute-start | bytes 294920 | tf_op jit(solution)/shard_map/ppermute | solution.py:534
  29.2 0.5 collective-permute-start.15
  29.7 0.5 collective-permute-start.16
  30.3 0.8 %collective-permute-done.10.row_got = bf16[4,32,768]{2,1,0:T(8,128)(2,1)S(1)} collective-permute-done((bf16[4,32,768]{2,1,0:T(8,128)(2,1)S(1)}, bf16[4,32,768]{2,1,0:T(8,128)(2,1)S(1)}, u32[]{:S(2)}, u32[]{:S(2)}) %collective-permute-start.10) | collective-permute-done | bytes 196640 | tf_op jit(solution)/shard_map/ppermute | solution.py:534
  31.1 1.8 %collective-permute-done.9.got_ref = bf16[4,32,384]{2,1,0:T(8,128)(2,1)S(1)} collective-permute-done((bf16[4,32,384]{2,1,0:T(8,128)(2,1)S(1)}, bf16[4,32,384]{2,1,0:T(8,128)(2,1)S(1)}, u32[]{:S(2)}, u32[]{:S(2)}) %collective-permute-start.9) | collective-permute-done | bytes 98336 | tf_op jit(solution)/shard_map/ppermute | solution.py:534
  33.0 0.1 first_add_pair.1
  33.0 2.7 %collective-permute-start.11 = (bf16[32,1152]{1,0:T(8,128)(2,1)S(1)}, bf16[32,1152]{1,0:T(8,128)(2,1)S(1)}, u32[]{:S(2)}, u32[]{:S(2)}) collective-permute-start(bf16[32,1152]{1,0:T(8,128)(2,1)S(1)} %get-tuple-element.104), channel_id=1, source_target_pairs={{0,24},{4,28},{8,16},{12,20},{16,8},{20,12},{24,0},{28,4},{1,25},{... | collective-permute-start | bytes 221192 | tf_op jit(solution)/shard_map/ppermute | solution.py:534
  35.7 0.5 collective-permute-start.12
  36.2 0.4 collective-permute-start.13
  36.6 0.1 second_add_chips.1
  36.7 1.8 %collective-permute-start.17 = (bf16[32,896]{1,0:T(8,128)(2,1)S(1)}, bf16[32,896]{1,0:T(8,128)(2,1)S(1)}, u32[]{:S(2)}, u32[]{:S(2)}) collective-permute-start(bf16[32,896]{1,0:T(8,128)(2,1)S(1)} %get-tuple-element.112), channel_id=1, source_target_pairs={{0,1},{1,0},{2,3},{3,2},{4,5},{5,4},{6,7},{7,6},{8,9},{9,8},{10,11... | collective-permute-start | bytes 172040 | tf_op jit(solution)/shard_map/ppermute | solution.py:534
  38.4 1.6 %collective-permute-done.12.got_2 = bf16[32,1152]{1,0:T(8,128)(2,1)S(1)} collective-permute-done((bf16[32,1152]{1,0:T(8,128)(2,1)S(1)}, bf16[32,1152]{1,0:T(8,128)(2,1)S(1)}, u32[]{:S(2)}, u32[]{:S(2)}) %collective-permute-start.12) | collective-permute-done | bytes 73760 | tf_op jit(solution)/shard_map/ppermute | solution.py:534
  40.0 0.5 collective-permute-done.13.got_3
  40.5 0.4 collective-permute-done.17.got_ref
  40.9 0.1 join_terms.1.kept_ref
  41.0 2.8 %collective-permute-start.21 = (bf16[32,2048]{1,0:T(8,128)(2,1)S(1)}, bf16[32,2048]{1,0:T(8,128)(2,1)S(1)}, u32[]{:S(2)}, u32[]{:S(2)}) collective-permute-start(bf16[32,2048]{1,0:T(8,128)(2,1)S(1)} %join_terms.1.kept_ref), channel_id=1, source_target_pairs={{0,2},{1,3},{2,0},{3,1},{4,6},{5,7},{6,4},{7,5},{8,10},{9,11},{10,... | collective-permute-start | bytes 393224 | tf_op jit(solution)/shard_map/ppermute | solution.py:534
  43.8 2.4 %collective-permute-start.18 = (bf16[128,512]{1,0:T(8,128)(2,1)S(1)}, bf16[128,512]{1,0:T(8,128)(2,1)S(1)}, u32[]{:S(2)}, u32[]{:S(2)}) collective-permute-start(bf16[128,512]{1,0:T(8,128)(2,1)S(1)} %get-tuple-element.114), channel_id=1, source_target_pairs={{0,24},{4,28},{8,16},{12,20},{16,8},{20,12},{24,0},{28,4},{1,25},{... | collective-permute-start | bytes 393224 | tf_op jit(solution)/shard_map/ppermute | solution.py:534
  46.2 0.5 collective-permute-start.19
  46.7 0.5 collective-permute-start.20
  47.2 1.2 %collective-permute-done.21.got_ref = bf16[32,2048]{1,0:T(8,128)(2,1)S(1)} collective-permute-done((bf16[32,2048]{1,0:T(8,128)(2,1)S(1)}, bf16[32,2048]{1,0:T(8,128)(2,1)S(1)}, u32[]{:S(2)}, u32[]{:S(2)}) %collective-permute-start.21) | collective-permute-done | bytes 131104 | tf_op jit(solution)/shard_map/ppermute | solution.py:534
  48.4 0.8 %collective-permute-start.22 = (bf16[32,2048]{1,0:T(8,128)(2,1)S(1)}, bf16[32,2048]{1,0:T(8,128)(2,1)S(1)}, u32[]{:S(2)}, u32[]{:S(2)}) collective-permute-start(bf16[32,2048]{1,0:T(8,128)(2,1)S(1)} %add_pairs.1.held_ref), channel_id=1, source_target_pairs={{0,1},{1,0},{2,3},{3,2},{4,5},{5,4},{6,7},{7,6},{8,9},{9,8},{10,11... | collective-permute-start | bytes 393224 | tf_op jit(solution)/shard_map/ppermute | solution.py:534
  49.2 0.7 %collective-permute-done.18.got_1 = bf16[128,512]{1,0:T(8,128)(2,1)S(1)} collective-permute-done((bf16[128,512]{1,0:T(8,128)(2,1)S(1)}, bf16[128,512]{1,0:T(8,128)(2,1)S(1)}, u32[]{:S(2)}, u32[]{:S(2)}) %collective-permute-start.18) | collective-permute-done | bytes 131104 | tf_op jit(solution)/shard_map/ppermute | solution.py:534
  49.9 1.4 %collective-permute-done.19.got_2 = bf16[128,512]{1,0:T(8,128)(2,1)S(1)} collective-permute-done((bf16[128,512]{1,0:T(8,128)(2,1)S(1)}, bf16[128,512]{1,0:T(8,128)(2,1)S(1)}, u32[]{:S(2)}, u32[]{:S(2)}) %collective-permute-start.19) | collective-permute-done | bytes 131104 | tf_op jit(solution)/shard_map/ppermute | solution.py:534
  51.3 0.4 collective-permute-done.20.got_3
  51.7 1.1 %input_grad.1 = bf16[512,512]{1,0:T(8,128)(2,1)} custom-call(f32[512,512]{1,0:T(8,128)S(1)} %get-tuple-element.65.base_ref, f32[512,512]{1,0:T(8,128)S(1)} %get-tuple-element.66.normed_ref, f32[512,1]{1,0:T(8,128)S(1)} %get-tuple-element.67.inverse_ref, f32[1,512]{1,0:T(1,128)S(1)} %bitcast.7, bf16[128,512]{1,0:T(8,128)(2,1)S(1)} %get-tuple-element.113.own_ref, ...), custom_call_target="tpu_custom_call" | custom-call | tf_op jit(solution)/shard_map/input_grad/pallas_call | solution.py:520
  52.8 0.6 %collective-permute-done.22.got_ref = bf16[32,2048]{1,0:T(8,128)(2,1)S(1)} collective-permute-done((bf16[32,2048]{1,0:T(8,128)(2,1)S(1)}, bf16[32,2048]{1,0:T(8,128)(2,1)S(1)}, u32[]{:S(2)}, u32[]{:S(2)}) %collective-permute-start.22) | collective-permute-done | bytes 131104 | tf_op jit(solution)/shard_map/ppermute | solution.py:534
  53.5 0.9 %result.1 = (f32[64,1536]{1,0:T(8,128)}, f32[64,512]{1,0:T(8,128)}, f32[1,64]{1,0:T(1,128)}) custom-call(bf16[32,2048]{1,0:T(8,128)(2,1)S(1)} %add_pairs.1.held_ref, bf16[32,2048]{1,0:T(8,128)(2,1)S(1)} %collective-permute-done.22.got_ref, bf16[64,1536]{1,0:T(8,128)(2,1)S(1)} %get-tuple-element.118.w_ref, f32[1,512]{1,0:T(1,128)S(1)} %bitcast.8), custom_call_target="tpu_custom_call" | custom-call | tf_op jit(solution)/shard_map/result/pallas_call | solution.py:520
  (15 shorter events, 0.2 us)
Async XLA Ops:
  1.9 12.2 %collective-permute-start.3 = (bf16[2,128,512]{2,1,0:T(8,128)(2,1)S(1)}, bf16[2,128,512]{2,1,0:T(8,128)(2,1)S(1)}, u32[]{:S(2)}, u32[]{:S(2)}) collective-permute-start(bf16[2,128,512]{2,1,0:T(8,128)(2,1)S(1)} %get-tuple-element.77), channel_id=1, source_target_pairs={{0,16},{4,20},{8,24},{12,28},{16,0},{20,4},{24,8},{28,12},{1,17},{... | collective-permute-start | bytes 786440 | tf_op jit(solution)/shard_map/ppermute | solution.py:534
  4.9 9.2 %collective-permute-start.4 = (bf16[2,128,512]{2,1,0:T(8,128)(2,1)S(1)}, bf16[2,128,512]{2,1,0:T(8,128)(2,1)S(1)}, u32[]{:S(2)}, u32[]{:S(2)}) collective-permute-start(bf16[2,128,512]{2,1,0:T(8,128)(2,1)S(1)} %get-tuple-element.78), channel_id=1, source_target_pairs={{0,8},{4,12},{8,0},{12,4},{16,24},{20,28},{24,16},{28,20},{1,9},{5... | collective-permute-start | bytes 786440 | tf_op jit(solution)/shard_map/ppermute | solution.py:534
  6.4 11.7 %collective-permute-start.2 = (bf16[2,128,512]{2,1,0:T(8,128)(2,1)S(1)}, bf16[2,128,512]{2,1,0:T(8,128)(2,1)S(1)}, u32[]{:S(2)}, u32[]{:S(2)}) collective-permute-start(bf16[2,128,512]{2,1,0:T(8,128)(2,1)S(1)} %get-tuple-element.63), channel_id=1, source_target_pairs={{0,24},{4,28},{8,16},{12,20},{16,8},{20,12},{24,0},{28,4},{1,25},{... | collective-permute-start | bytes 786440 | tf_op jit(solution)/shard_map/ppermute | solution.py:534
  14.2 5.4 %copy-start = (f32[512]{0:T(512)S(1)}, f32[512]{0:T(512)}, u32[]{:S(2)}) copy-start(f32[512]{0:T(512)} %param.6) | copy-start | bytes 6148
  14.2 5.3 %collective-permute-start.5 = (bf16[3,2,64,512]{3,2,1,0:T(8,128)(2,1)S(1)}, bf16[3,2,64,512]{3,2,1,0:T(8,128)(2,1)S(1)}, u32[]{:S(2)}, u32[]{:S(2)}) collective-permute-start(bf16[3,2,64,512]{3,2,1,0:T(8,128)(2,1)S(1)} %pack_other_core.1), channel_id=1, source_target_pairs={{0,4},{4,0},{8,12},{12,8},{16,20},{20,16},{24,28},{28,24},{1,5},{5... | collective-permute-start | bytes 1179656 | tf_op jit(solution)/shard_map/ppermute | solution.py:534
  14.3 3.9 %collective-permute-start = (bf16[4,64,384]{2,1,0:T(8,128)(2,1)S(1)}, bf16[4,64,384]{2,1,0:T(8,128)(2,1)S(1)}, u32[]{:S(2)}, u32[]{:S(2)}) collective-permute-start(bf16[4,64,384]{2,1,0:T(8,128)(2,1)S(1)} %get-tuple-element.71), channel_id=1, source_target_pairs={{0,4},{4,0},{8,12},{12,8},{16,20},{20,16},{24,28},{28,24},{1,5},{5... | collective-permute-start | bytes 589832 | tf_op jit(solution)/shard_map/ppermute | solution.py:534
  14.8 3.4 %collective-permute-start.1 = (bf16[4,64,384]{2,1,0:T(8,128)(2,1)S(1)}, bf16[4,64,384]{2,1,0:T(8,128)(2,1)S(1)}, u32[]{:S(2)}, u32[]{:S(2)}) collective-permute-start(bf16[4,64,384]{2,1,0:T(8,128)(2,1)S(1)} %get-tuple-element.72), channel_id=1, source_target_pairs={{0,4},{4,0},{8,12},{12,8},{16,20},{20,16},{24,28},{28,24},{1,5},{5... | collective-permute-start | bytes 589832 | tf_op jit(solution)/shard_map/ppermute | solution.py:534
  18.1 1.4 %collective-permute-start.6 = (bf16[2,64,512]{2,1,0:T(8,128)(2,1)S(1)}, bf16[2,64,512]{2,1,0:T(8,128)(2,1)S(1)}, u32[]{:S(2)}, u32[]{:S(2)}) collective-permute-start(bf16[2,64,512]{2,1,0:T(8,128)(2,1)S(1)} %pack_other_core_last.1), channel_id=1, source_target_pairs={{0,4},{4,0},{8,12},{12,8},{16,20},{20,16},{24,28},{28,24},{1,5},{5... | collective-permute-start | bytes 393224 | tf_op jit(solution)/shard_map/ppermute | solution.py:534
  22.6 3.0 %collective-permute-start.8 = (bf16[4,64,1280]{2,1,0:T(8,128)(2,1)S(1)}, bf16[4,64,1280]{2,1,0:T(8,128)(2,1)S(1)}, u32[]{:S(2)}, u32[]{:S(2)}) collective-permute-start(bf16[4,64,1280]{2,1,0:T(8,128)(2,1)S(1)} %get-tuple-element.97), channel_id=1, source_target_pairs={{0,4},{4,0},{8,12},{12,8},{16,20},{20,16},{24,28},{28,24},{1,5},{5... | collective-permute-start | bytes 1966088 | tf_op jit(solution)/shard_map/ppermute | solution.py:534
  23.5 6.3 %collective-permute-start.7 = (bf16[4,64,512]{2,1,0:T(8,128)(2,1)S(1)}, bf16[4,64,512]{2,1,0:T(8,128)(2,1)S(1)}, u32[]{:S(2)}, u32[]{:S(2)}) collective-permute-start(bf16[4,64,512]{2,1,0:T(8,128)(2,1)S(1)} %get-tuple-element.87), channel_id=1, source_target_pairs={{0,4},{4,0},{8,12},{12,8},{16,20},{20,16},{24,28},{28,24},{1,5},{5... | collective-permute-start | bytes 786440 | tf_op jit(solution)/shard_map/ppermute | solution.py:534
  23.9 7.2 %collective-permute-start.10 = (bf16[4,32,768]{2,1,0:T(8,128)(2,1)S(1)}, bf16[4,32,768]{2,1,0:T(8,128)(2,1)S(1)}, u32[]{:S(2)}, u32[]{:S(2)}) collective-permute-start(bf16[4,32,768]{2,1,0:T(8,128)(2,1)S(1)} %get-tuple-element.102), channel_id=1, source_target_pairs={{0,1},{1,0},{2,3},{3,2},{4,5},{5,4},{6,7},{7,6},{8,9},{9,8},{10,11... | collective-permute-start | bytes 589832 | tf_op jit(solution)/shard_map/ppermute | solution.py:534
  25.8 10.4 %collective-permute-start.14 = (bf16[64,896]{1,0:T(8,128)(2,1)S(1)}, bf16[64,896]{1,0:T(8,128)(2,1)S(1)}, u32[]{:S(2)}, u32[]{:S(2)}) collective-permute-start(bf16[64,896]{1,0:T(8,128)(2,1)S(1)} %get-tuple-element.108), channel_id=1, source_target_pairs={{0,24},{4,28},{8,16},{12,20},{16,8},{20,12},{24,0},{28,4},{1,25},{... | collective-permute-start | bytes 344072 | tf_op jit(solution)/shard_map/ppermute | solution.py:534
  28.3 4.6 %collective-permute-start.9 = (bf16[4,32,384]{2,1,0:T(8,128)(2,1)S(1)}, bf16[4,32,384]{2,1,0:T(8,128)(2,1)S(1)}, u32[]{:S(2)}, u32[]{:S(2)}) collective-permute-start(bf16[4,32,384]{2,1,0:T(8,128)(2,1)S(1)} %get-tuple-element.99), channel_id=1, source_target_pairs={{0,1},{1,0},{2,3},{3,2},{4,5},{5,4},{6,7},{7,6},{8,9},{9,8},{10,11... | collective-permute-start | bytes 294920 | tf_op jit(solution)/shard_map/ppermute | solution.py:534
  29.2 7.4 %collective-permute-start.15 = (bf16[64,896]{1,0:T(8,128)(2,1)S(1)}, bf16[64,896]{1,0:T(8,128)(2,1)S(1)}, u32[]{:S(2)}, u32[]{:S(2)}) collective-permute-start(bf16[64,896]{1,0:T(8,128)(2,1)S(1)} %get-tuple-element.109), channel_id=1, source_target_pairs={{0,16},{4,20},{8,24},{12,28},{16,0},{20,4},{24,8},{28,12},{1,17},{... | collective-permute-start | bytes 344072 | tf_op jit(solution)/shard_map/ppermute | solution.py:534
  29.7 6.8 %collective-permute-start.16 = (bf16[64,896]{1,0:T(8,128)(2,1)S(1)}, bf16[64,896]{1,0:T(8,128)(2,1)S(1)}, u32[]{:S(2)}, u32[]{:S(2)}) collective-permute-start(bf16[64,896]{1,0:T(8,128)(2,1)S(1)} %get-tuple-element.110), channel_id=1, source_target_pairs={{0,8},{4,12},{8,0},{12,4},{16,24},{20,28},{24,16},{28,20},{1,9},{5... | collective-permute-start | bytes 344072 | tf_op jit(solution)/shard_map/ppermute | solution.py:534
  33.0 5.4 %collective-permute-start.11 = (bf16[32,1152]{1,0:T(8,128)(2,1)S(1)}, bf16[32,1152]{1,0:T(8,128)(2,1)S(1)}, u32[]{:S(2)}, u32[]{:S(2)}) collective-permute-start(bf16[32,1152]{1,0:T(8,128)(2,1)S(1)} %get-tuple-element.104), channel_id=1, source_target_pairs={{0,24},{4,28},{8,16},{12,20},{16,8},{20,12},{24,0},{28,4},{1,25},{... | collective-permute-start | bytes 221192 | tf_op jit(solution)/shard_map/ppermute | solution.py:534
  35.7 4.4 %collective-permute-start.12 = (bf16[32,1152]{1,0:T(8,128)(2,1)S(1)}, bf16[32,1152]{1,0:T(8,128)(2,1)S(1)}, u32[]{:S(2)}, u32[]{:S(2)}) collective-permute-start(bf16[32,1152]{1,0:T(8,128)(2,1)S(1)} %get-tuple-element.105), channel_id=1, source_target_pairs={{0,16},{4,20},{8,24},{12,28},{16,0},{20,4},{24,8},{28,12},{1,17},{... | collective-permute-start | bytes 221192 | tf_op jit(solution)/shard_map/ppermute | solution.py:534
  36.2 4.4 %collective-permute-start.13 = (bf16[32,1152]{1,0:T(8,128)(2,1)S(1)}, bf16[32,1152]{1,0:T(8,128)(2,1)S(1)}, u32[]{:S(2)}, u32[]{:S(2)}) collective-permute-start(bf16[32,1152]{1,0:T(8,128)(2,1)S(1)} %get-tuple-element.106), channel_id=1, source_target_pairs={{0,8},{4,12},{8,0},{12,4},{16,24},{20,28},{24,16},{28,20},{1,9},{5... | collective-permute-start | bytes 221192 | tf_op jit(solution)/shard_map/ppermute | solution.py:534
  36.7 4.2 %collective-permute-start.17 = (bf16[32,896]{1,0:T(8,128)(2,1)S(1)}, bf16[32,896]{1,0:T(8,128)(2,1)S(1)}, u32[]{:S(2)}, u32[]{:S(2)}) collective-permute-start(bf16[32,896]{1,0:T(8,128)(2,1)S(1)} %get-tuple-element.112), channel_id=1, source_target_pairs={{0,1},{1,0},{2,3},{3,2},{4,5},{5,4},{6,7},{7,6},{8,9},{9,8},{10,11... | collective-permute-start | bytes 172040 | tf_op jit(solution)/shard_map/ppermute | solution.py:534
  41.0 7.4 %collective-permute-start.21 = (bf16[32,2048]{1,0:T(8,128)(2,1)S(1)}, bf16[32,2048]{1,0:T(8,128)(2,1)S(1)}, u32[]{:S(2)}, u32[]{:S(2)}) collective-permute-start(bf16[32,2048]{1,0:T(8,128)(2,1)S(1)} %join_terms.1.kept_ref), channel_id=1, source_target_pairs={{0,2},{1,3},{2,0},{3,1},{4,6},{5,7},{6,4},{7,5},{8,10},{9,11},{10,... | collective-permute-start | bytes 393224 | tf_op jit(solution)/shard_map/ppermute | solution.py:534
  43.8 6.1 %collective-permute-start.18 = (bf16[128,512]{1,0:T(8,128)(2,1)S(1)}, bf16[128,512]{1,0:T(8,128)(2,1)S(1)}, u32[]{:S(2)}, u32[]{:S(2)}) collective-permute-start(bf16[128,512]{1,0:T(8,128)(2,1)S(1)} %get-tuple-element.114), channel_id=1, source_target_pairs={{0,24},{4,28},{8,16},{12,20},{16,8},{20,12},{24,0},{28,4},{1,25},{... | collective-permute-start | bytes 393224 | tf_op jit(solution)/shard_map/ppermute | solution.py:534
  46.2 5.1 %collective-permute-start.19 = (bf16[128,512]{1,0:T(8,128)(2,1)S(1)}, bf16[128,512]{1,0:T(8,128)(2,1)S(1)}, u32[]{:S(2)}, u32[]{:S(2)}) collective-permute-start(bf16[128,512]{1,0:T(8,128)(2,1)S(1)} %get-tuple-element.115), channel_id=1, source_target_pairs={{0,16},{4,20},{8,24},{12,28},{16,0},{20,4},{24,8},{28,12},{1,17},{... | collective-permute-start | bytes 393224 | tf_op jit(solution)/shard_map/ppermute | solution.py:534
  46.7 5.0 %collective-permute-start.20 = (bf16[128,512]{1,0:T(8,128)(2,1)S(1)}, bf16[128,512]{1,0:T(8,128)(2,1)S(1)}, u32[]{:S(2)}, u32[]{:S(2)}) collective-permute-start(bf16[128,512]{1,0:T(8,128)(2,1)S(1)} %get-tuple-element.116), channel_id=1, source_target_pairs={{0,8},{4,12},{8,0},{12,4},{16,24},{20,28},{24,16},{28,20},{1,9},{5... | collective-permute-start | bytes 393224 | tf_op jit(solution)/shard_map/ppermute | solution.py:534
  48.4 5.0 %collective-permute-start.22 = (bf16[32,2048]{1,0:T(8,128)(2,1)S(1)}, bf16[32,2048]{1,0:T(8,128)(2,1)S(1)}, u32[]{:S(2)}, u32[]{:S(2)}) collective-permute-start(bf16[32,2048]{1,0:T(8,128)(2,1)S(1)} %add_pairs.1.held_ref), channel_id=1, source_target_pairs={{0,1},{1,0},{2,3},{3,2},{4,5},{5,4},{6,7},{7,6},{8,9},{9,8},{10,11... | collective-permute-start | bytes 393224 | tf_op jit(solution)/shard_map/ppermute | solution.py:534

commit v16 on v15

--- a/solution.py
+++ b/solution.py
@@ -21,7 +21,7 @@
 VMEM = pl.BlockSpec(memory_space=pltpu.VMEM)
 HBM = pl.BlockSpec(memory_space=pltpu.HBM)
 CHIP_STEPS = (3, 2, 1)
-FIRST_PART = 384
+FIRST_PART = 256
 PINNED = pl.BlockSpec(memory_space=pltpu.VMEM)
 shaped = jax.ShapeDtypeStruct
 

time: 54.5 us -> 55.6 us (1.020)
  waiting for transfers between devices: 13.8 us -> 15.8 us
  starting transfers between devices: 24.5 us -> 23.6 us
    ppermute x23, waiting for transfers between devices: 13.8 us -> 15.8 us  [swap(): return lax.ppermute(array, axis, [(i, i ^ bits) for i in range(count)])]
    ppermute x23, starting transfers between devices: 24.5 us -> 23.6 us  [swap(): return lax.ppermute(array, axis, [(i, i ^ bits) for i in range(count)])]
  transfers between devices with their start and end apart: 23 -> 23, of which waited for: 12 -> 13; matrix products, arithmetic and copies ran while one was open for 0% -> 0% of each run, Pallas kernels for 18% -> 18%
where the time goes in v16:
time: 55.6 us; the launch traced here: 55.4 us
  starting transfers between devices  23.6 us (42%)
  waiting for transfers between devices  15.8 us (28%)
  Pallas kernels  15.2 us (27%)
  between operations  0.78 us (1%)
    ppermute x23, starting transfers between devices, swap(): return lax.ppermute(array, axis, [(i, i ^ bits) for i in range(count)])  23.6 us
    ppermute x23, waiting for transfers between devices, swap(): return lax.ppermute(array, axis, [(i, i ^ bits) for i in range(count)])  15.8 us
    pallas_call x15, Pallas kernels, call(): pl.pallas_call(kernel, out_shape=outs, in_specs=[spec for spec, _ in ins]...  15.2 us
  transfers between devices with their start and end apart: 23, of which 13 were waited for; matrix products, arithmetic and copies ran while one was open for 0% of the time, Pallas kernels for 18%

profile of v16, /device:TPU:0, one launch (start us, length us, event | category | flops | bytes accessed | tf_op | source)
XLA Modules:
  0.0 55.4 jit_solution(9135975853561143723)
XLA Ops:
  0.6 1.3 %pack_columns.1 = (bf16[2,128,512]{2,1,0:T(8,128)(2,1)S(1)}, bf16[2,128,512]{2,1,0:T(8,128)(2,1)S(1)}, bf16[2,128,512]{2,1,0:T(8,128)(2,1)S(1)}) custom-call(bf16[512,512]{1,0:T(8,128)(2,1)} %bitcast.9, bf16[512,512]{1,0:T(8,128)(2,1)} %bitcast.11), custom_call_target="tpu_custom_call" | custom-call | tf_op jit(solution)/shard_map/pack_columns/pallas_call | solution.py:520
  1.9 3.0 %collective-permute-start.3 = (bf16[2,128,512]{2,1,0:T(8,128)(2,1)S(1)}, bf16[2,128,512]{2,1,0:T(8,128)(2,1)S(1)}, u32[]{:S(2)}, u32[]{:S(2)}) collective-permute-start(bf16[2,128,512]{2,1,0:T(8,128)(2,1)S(1)} %get-tuple-element.77), channel_id=1, source_target_pairs={{0,16},{4,20},{8,24},{12,28},{16,0},{20,4},{24,8},{28,12},{1,17},{... | collective-permute-start | bytes 786440 | tf_op jit(solution)/shard_map/ppermute | solution.py:534
  4.9 1.5 %collective-permute-start.4 = (bf16[2,128,512]{2,1,0:T(8,128)(2,1)S(1)}, bf16[2,128,512]{2,1,0:T(8,128)(2,1)S(1)}, u32[]{:S(2)}, u32[]{:S(2)}) collective-permute-start(bf16[2,128,512]{2,1,0:T(8,128)(2,1)S(1)} %get-tuple-element.78), channel_id=1, source_target_pairs={{0,8},{4,12},{8,0},{12,4},{16,24},{20,28},{24,16},{28,20},{1,9},{5... | collective-permute-start | bytes 786440 | tf_op jit(solution)/shard_map/ppermute | solution.py:534
  6.4 0.0 collective-permute-start.2
  6.5 7.7 %row_heads.1 = (bf16[4,64,384]{2,1,0:T(8,128)(2,1)S(1)}, bf16[4,64,384]{2,1,0:T(8,128)(2,1)S(1)}, bf16[4,64,384]{2,1,0:T(8,128)(2,1)S(1)}, bf16[4,64,384]{2,1,0:...) custom-call(bf16[512,512]{1,0:T(8,128)(2,1)} %bitcast.10, ...), custom_call_target="tpu_custom_call" | custom-call | tf_op jit(solution)/shard_map/row_heads/pallas_call | solution.py:520
  14.1 0.0 collective-permute-done.4.near_3
  14.2 0.1 collective-permute-start.5
  14.3 0.5 collective-permute-start
  14.8 0.1 collective-permute-start.1
  14.9 3.2 %collective-permute-done.2.near_1 = bf16[2,128,512]{2,1,0:T(8,128)(2,1)S(1)} collective-permute-done((bf16[2,128,512]{2,1,0:T(8,128)(2,1)S(1)}, bf16[2,128,512]{2,1,0:T(8,128)(2,1)S(1)}, u32[]{:S(2)}, u32[]{:S(2)}) %collective-permute-start.2) | collective-permute-done | bytes 262176 | tf_op jit(solution)/shard_map/ppermute | solution.py:534
  18.1 0.1 collective-permute-start.6
  18.2 0.0 collective-permute-done.got_1
  18.2 0.1 row_add_cores.1
  18.4 1.2 %collective-permute-done.6.last_ref = bf16[2,64,512]{2,1,0:T(8,128)(2,1)S(1)} collective-permute-done((bf16[2,64,512]{2,1,0:T(8,128)(2,1)S(1)}, bf16[2,64,512]{2,1,0:T(8,128)(2,1)S(1)}, u32[]{:S(2)}, u32[]{:S(2)}) %collective-permute-start.6) | collective-permute-done | bytes 131104 | tf_op jit(solution)/shard_map/ppermute | solution.py:534
  19.6 3.1 %column_heads.1 = (bf16[4,64,1280]{2,1,0:T(8,128)(2,1)S(1)}, bf16[4,64,1280]{2,1,0:T(8,128)(2,1)S(1)}, bf16[512,768]{1,0:T(8,128)(2,1)S(1)}) custom-call(bf16[512,512]{1,0:T(8,128)(2,1)S(1)} %get-tuple-element.75.x_ref, bf16[512,512]{1,0:T(8,128)(2,1)S(1)} %get-tuple-element.76.cot_ref, bf16[2,128,512]{2,1,0:T(8,128)(2,1)S(1)} %collective-permute-done.2.near_1, ...), custom_call_target="tpu_custom_call" | custom-call | tf_op jit(solution)/shard_map/column_heads/pallas_call | solution.py:520
  22.7 0.2 collective-permute-start.8
  22.9 0.6 %column_grad_hidden.1 = (bf16[4,64,512]{2,1,0:T(8,128)(2,1)S(1)}, bf16[4,64,512]{2,1,0:T(8,128)(2,1)S(1)}) custom-call(bf16[512,768]{1,0:T(8,128)(2,1)S(1)} %get-tuple-element.84.grads_ref, bf16[512,768]{1,0:T(8,128)(2,1)S(1)} %get-tuple-element.80.w_ref), custom_call_target="tpu_custom_call" | custom-call | tf_op jit(solution)/shard_map/column_grad_hidden/pallas_call | solution.py:520
  23.5 0.4 collective-permute-start.7
  23.9 1.7 %collective-permute-start.10 = (bf16[4,32,768]{2,1,0:T(8,128)(2,1)S(1)}, bf16[4,32,768]{2,1,0:T(8,128)(2,1)S(1)}, u32[]{:S(2)}, u32[]{:S(2)}) collective-permute-start(bf16[4,32,768]{2,1,0:T(8,128)(2,1)S(1)} %get-tuple-element.102), channel_id=1, source_target_pairs={{0,1},{1,0},{2,3},{3,2},{4,5},{5,4},{6,7},{7,6},{8,9},{9,8},{10,11... | collective-permute-start | bytes 589832 | tf_op jit(solution)/shard_map/ppermute | solution.py:534
  25.6 0.2 column_add_cores.1
  25.8 2.5 %collective-permute-start.14 = (bf16[64,1024]{1,0:T(8,128)(2,1)S(1)}, bf16[64,1024]{1,0:T(8,128)(2,1)S(1)}, u32[]{:S(2)}, u32[]{:S(2)}) collective-permute-start(bf16[64,1024]{1,0:T(8,128)(2,1)S(1)} %get-tuple-element.108), channel_id=1, source_target_pairs={{0,24},{4,28},{8,16},{12,20},{16,8},{20,12},{24,0},{28,4},{1,25},{... | collective-permute-start | bytes 393224 | tf_op jit(solution)/shard_map/ppermute | solution.py:534
  28.3 0.5 collective-permute-start.15
  28.8 0.5 collective-permute-start.16
  29.3 0.9 %collective-permute-start.9 = (bf16[4,32,256]{2,1,0:T(8,128)(2,1)S(1)}, bf16[4,32,256]{2,1,0:T(8,128)(2,1)S(1)}, u32[]{:S(2)}, u32[]{:S(2)}) collective-permute-start(bf16[4,32,256]{2,1,0:T(8,128)(2,1)S(1)} %get-tuple-element.99), channel_id=1, source_target_pairs={{0,1},{1,0},{2,3},{3,2},{4,5},{5,4},{6,7},{7,6},{8,9},{9,8},{10,11... | collective-permute-start | bytes 196616 | tf_op jit(solution)/shard_map/ppermute | solution.py:534
  30.3 0.5 collective-permute-done.10.row_got
  30.9 2.8 %collective-permute-done.9.got_ref = bf16[4,32,256]{2,1,0:T(8,128)(2,1)S(1)} collective-permute-done((bf16[4,32,256]{2,1,0:T(8,128)(2,1)S(1)}, bf16[4,32,256]{2,1,0:T(8,128)(2,1)S(1)}, u32[]{:S(2)}, u32[]{:S(2)}) %collective-permute-start.9) | collective-permute-done | bytes 65568 | tf_op jit(solution)/shard_map/ppermute | solution.py:534
  33.6 0.1 first_add_pair.1
  33.7 2.5 %collective-permute-start.11 = (bf16[32,1024]{1,0:T(8,128)(2,1)S(1)}, bf16[32,1024]{1,0:T(8,128)(2,1)S(1)}, u32[]{:S(2)}, u32[]{:S(2)}) collective-permute-start(bf16[32,1024]{1,0:T(8,128)(2,1)S(1)} %get-tuple-element.104), channel_id=1, source_target_pairs={{0,24},{4,28},{8,16},{12,20},{16,8},{20,12},{24,0},{28,4},{1,25},{... | collective-permute-start | bytes 196616 | tf_op jit(solution)/shard_map/ppermute | solution.py:534
  36.2 0.5 collective-permute-start.12
  36.7 0.5 collective-permute-start.13
  37.2 0.1 second_add_chips.1
  37.3 1.0 %collective-permute-start.17 = (bf16[32,1024]{1,0:T(8,128)(2,1)S(1)}, bf16[32,1024]{1,0:T(8,128)(2,1)S(1)}, u32[]{:S(2)}, u32[]{:S(2)}) collective-permute-start(bf16[32,1024]{1,0:T(8,128)(2,1)S(1)} %get-tuple-element.112), channel_id=1, source_target_pairs={{0,1},{1,0},{2,3},{3,2},{4,5},{5,4},{6,7},{7,6},{8,9},{9,8},{10,11... | collective-permute-start | bytes 196616 | tf_op jit(solution)/shard_map/ppermute | solution.py:534
  38.3 1.0 %collective-permute-done.11.got_1 = bf16[32,1024]{1,0:T(8,128)(2,1)S(1)} collective-permute-done((bf16[32,1024]{1,0:T(8,128)(2,1)S(1)}, bf16[32,1024]{1,0:T(8,128)(2,1)S(1)}, u32[]{:S(2)}, u32[]{:S(2)}) %collective-permute-start.11) | collective-permute-done | bytes 65568 | tf_op jit(solution)/shard_map/ppermute | solution.py:534
  39.3 1.2 %collective-permute-done.12.got_2 = bf16[32,1024]{1,0:T(8,128)(2,1)S(1)} collective-permute-done((bf16[32,1024]{1,0:T(8,128)(2,1)S(1)}, bf16[32,1024]{1,0:T(8,128)(2,1)S(1)}, u32[]{:S(2)}, u32[]{:S(2)}) %collective-permute-start.12) | collective-permute-done | bytes 65568 | tf_op jit(solution)/shard_map/ppermute | solution.py:534
  40.5 0.5 collective-permute-done.13.got_3
  41.0 0.7 %collective-permute-done.17.got_ref = bf16[32,1024]{1,0:T(8,128)(2,1)S(1)} collective-permute-done((bf16[32,1024]{1,0:T(8,128)(2,1)S(1)}, bf16[32,1024]{1,0:T(8,128)(2,1)S(1)}, u32[]{:S(2)}, u32[]{:S(2)}) %collective-permute-start.17) | collective-permute-done | bytes 65568 | tf_op jit(solution)/shard_map/ppermute | solution.py:534
  41.7 3.4 %collective-permute-start.21 = (bf16[32,2048]{1,0:T(8,128)(2,1)S(1)}, bf16[32,2048]{1,0:T(8,128)(2,1)S(1)}, u32[]{:S(2)}, u32[]{:S(2)}) collective-permute-start(bf16[32,2048]{1,0:T(8,128)(2,1)S(1)} %join_terms.1.kept_ref), channel_id=1, source_target_pairs={{0,2},{1,3},{2,0},{3,1},{4,6},{5,7},{6,4},{7,5},{8,10},{9,11},{10,... | collective-permute-start | bytes 393224 | tf_op jit(solution)/shard_map/ppermute | solution.py:534
  45.0 2.4 %collective-permute-start.18 = (bf16[128,512]{1,0:T(8,128)(2,1)S(1)}, bf16[128,512]{1,0:T(8,128)(2,1)S(1)}, u32[]{:S(2)}, u32[]{:S(2)}) collective-permute-start(bf16[128,512]{1,0:T(8,128)(2,1)S(1)} %get-tuple-element.114), channel_id=1, source_target_pairs={{0,24},{4,28},{8,16},{12,20},{16,8},{20,12},{24,0},{28,4},{1,25},{... | collective-permute-start | bytes 393224 | tf_op jit(solution)/shard_map/ppermute | solution.py:534
  47.5 0.5 collective-permute-start.19
  48.0 0.5 collective-permute-start.20
  48.5 0.9 %collective-permute-done.21.got_ref = bf16[32,2048]{1,0:T(8,128)(2,1)S(1)} collective-permute-done((bf16[32,2048]{1,0:T(8,128)(2,1)S(1)}, bf16[32,2048]{1,0:T(8,128)(2,1)S(1)}, u32[]{:S(2)}, u32[]{:S(2)}) %collective-permute-start.21) | collective-permute-done | bytes 131104 | tf_op jit(solution)/shard_map/ppermute | solution.py:534
  49.5 0.1 collective-permute-start.22
  49.6 1.3 %collective-permute-done.18.got_1 = bf16[128,512]{1,0:T(8,128)(2,1)S(1)} collective-permute-done((bf16[128,512]{1,0:T(8,128)(2,1)S(1)}, bf16[128,512]{1,0:T(8,128)(2,1)S(1)}, u32[]{:S(2)}, u32[]{:S(2)}) %collective-permute-start.18) | collective-permute-done | bytes 131104 | tf_op jit(solution)/shard_map/ppermute | solution.py:534
  50.9 1.5 %collective-permute-done.19.got_2 = bf16[128,512]{1,0:T(8,128)(2,1)S(1)} collective-permute-done((bf16[128,512]{1,0:T(8,128)(2,1)S(1)}, bf16[128,512]{1,0:T(8,128)(2,1)S(1)}, u32[]{:S(2)}, u32[]{:S(2)}) %collective-permute-start.19) | collective-permute-done | bytes 131104 | tf_op jit(solution)/shard_map/ppermute | solution.py:534
  52.5 0.5 collective-permute-done.20.got_3
  53.0 1.2 %input_grad.1 = bf16[512,512]{1,0:T(8,128)(2,1)} custom-call(f32[512,512]{1,0:T(8,128)S(1)} %get-tuple-element.65.base_ref, f32[512,512]{1,0:T(8,128)S(1)} %get-tuple-element.66.normed_ref, f32[512,1]{1,0:T(8,128)S(1)} %get-tuple-element.67.inverse_ref, f32[1,512]{1,0:T(1,128)S(1)} %bitcast.7, bf16[128,512]{1,0:T(8,128)(2,1)S(1)} %get-tuple-element.113.own_ref, ...), custom_call_target="tpu_custom_call" | custom-call | tf_op jit(solution)/shard_map/input_grad/pallas_call | solution.py:520
  54.1 0.4 collective-permute-done.22.got_ref
  54.5 0.9 %result.1 = (f32[64,1536]{1,0:T(8,128)}, f32[64,512]{1,0:T(8,128)}, f32[1,64]{1,0:T(1,128)}) custom-call(bf16[32,2048]{1,0:T(8,128)(2,1)S(1)} %add_pairs.1.held_ref, bf16[32,2048]{1,0:T(8,128)(2,1)S(1)} %collective-permute-done.22.got_ref, bf16[64,1536]{1,0:T(8,128)(2,1)S(1)} %get-tuple-element.118.w_ref, f32[1,512]{1,0:T(1,128)S(1)} %bitcast.8), custom_call_target="tpu_custom_call" | custom-call | tf_op jit(solution)/shard_map/result/pallas_call | solution.py:520
  (15 shorter events, 0.2 us)
Async XLA Ops:
  1.9 12.2 %collective-permute-start.3 = (bf16[2,128,512]{2,1,0:T(8,128)(2,1)S(1)}, bf16[2,128,512]{2,1,0:T(8,128)(2,1)S(1)}, u32[]{:S(2)}, u32[]{:S(2)}) collective-permute-start(bf16[2,128,512]{2,1,0:T(8,128)(2,1)S(1)} %get-tuple-element.77), channel_id=1, source_target_pairs={{0,16},{4,20},{8,24},{12,28},{16,0},{20,4},{24,8},{28,12},{1,17},{... | collective-permute-start | bytes 786440 | tf_op jit(solution)/shard_map/ppermute | solution.py:534
  4.9 9.2 %collective-permute-start.4 = (bf16[2,128,512]{2,1,0:T(8,128)(2,1)S(1)}, bf16[2,128,512]{2,1,0:T(8,128)(2,1)S(1)}, u32[]{:S(2)}, u32[]{:S(2)}) collective-permute-start(bf16[2,128,512]{2,1,0:T(8,128)(2,1)S(1)} %get-tuple-element.78), channel_id=1, source_target_pairs={{0,8},{4,12},{8,0},{12,4},{16,24},{20,28},{24,16},{28,20},{1,9},{5... | collective-permute-start | bytes 786440 | tf_op jit(solution)/shard_map/ppermute | solution.py:534
  6.4 11.7 %collective-permute-start.2 = (bf16[2,128,512]{2,1,0:T(8,128)(2,1)S(1)}, bf16[2,128,512]{2,1,0:T(8,128)(2,1)S(1)}, u32[]{:S(2)}, u32[]{:S(2)}) collective-permute-start(bf16[2,128,512]{2,1,0:T(8,128)(2,1)S(1)} %get-tuple-element.63), channel_id=1, source_target_pairs={{0,24},{4,28},{8,16},{12,20},{16,8},{20,12},{24,0},{28,4},{1,25},{... | collective-permute-start | bytes 786440 | tf_op jit(solution)/shard_map/ppermute | solution.py:534
  14.2 5.4 %copy-start = (f32[512]{0:T(512)S(1)}, f32[512]{0:T(512)}, u32[]{:S(2)}) copy-start(f32[512]{0:T(512)} %param.6) | copy-start | bytes 6148
  14.2 5.3 %collective-permute-start.5 = (bf16[3,2,64,512]{3,2,1,0:T(8,128)(2,1)S(1)}, bf16[3,2,64,512]{3,2,1,0:T(8,128)(2,1)S(1)}, u32[]{:S(2)}, u32[]{:S(2)}) collective-permute-start(bf16[3,2,64,512]{3,2,1,0:T(8,128)(2,1)S(1)} %pack_other_core.1), channel_id=1, source_target_pairs={{0,4},{4,0},{8,12},{12,8},{16,20},{20,16},{24,28},{28,24},{1,5},{5... | collective-permute-start | bytes 1179656 | tf_op jit(solution)/shard_map/ppermute | solution.py:534
  14.3 3.9 %collective-permute-start = (bf16[4,64,384]{2,1,0:T(8,128)(2,1)S(1)}, bf16[4,64,384]{2,1,0:T(8,128)(2,1)S(1)}, u32[]{:S(2)}, u32[]{:S(2)}) collective-permute-start(bf16[4,64,384]{2,1,0:T(8,128)(2,1)S(1)} %get-tuple-element.71), channel_id=1, source_target_pairs={{0,4},{4,0},{8,12},{12,8},{16,20},{20,16},{24,28},{28,24},{1,5},{5... | collective-permute-start | bytes 589832 | tf_op jit(solution)/shard_map/ppermute | solution.py:534
  14.8 3.4 %collective-permute-start.1 = (bf16[4,64,384]{2,1,0:T(8,128)(2,1)S(1)}, bf16[4,64,384]{2,1,0:T(8,128)(2,1)S(1)}, u32[]{:S(2)}, u32[]{:S(2)}) collective-permute-start(bf16[4,64,384]{2,1,0:T(8,128)(2,1)S(1)} %get-tuple-element.72), channel_id=1, source_target_pairs={{0,4},{4,0},{8,12},{12,8},{16,20},{20,16},{24,28},{28,24},{1,5},{5... | collective-permute-start | bytes 589832 | tf_op jit(solution)/shard_map/ppermute | solution.py:534
  18.1 1.4 %collective-permute-start.6 = (bf16[2,64,512]{2,1,0:T(8,128)(2,1)S(1)}, bf16[2,64,512]{2,1,0:T(8,128)(2,1)S(1)}, u32[]{:S(2)}, u32[]{:S(2)}) collective-permute-start(bf16[2,64,512]{2,1,0:T(8,128)(2,1)S(1)} %pack_other_core_last.1), channel_id=1, source_target_pairs={{0,4},{4,0},{8,12},{12,8},{16,20},{20,16},{24,28},{28,24},{1,5},{5... | collective-permute-start | bytes 393224 | tf_op jit(solution)/shard_map/ppermute | solution.py:534
  22.7 3.0 %collective-permute-start.8 = (bf16[4,64,1280]{2,1,0:T(8,128)(2,1)S(1)}, bf16[4,64,1280]{2,1,0:T(8,128)(2,1)S(1)}, u32[]{:S(2)}, u32[]{:S(2)}) collective-permute-start(bf16[4,64,1280]{2,1,0:T(8,128)(2,1)S(1)} %get-tuple-element.97), channel_id=1, source_target_pairs={{0,4},{4,0},{8,12},{12,8},{16,20},{20,16},{24,28},{28,24},{1,5},{5... | collective-permute-start | bytes 1966088 | tf_op jit(solution)/shard_map/ppermute | solution.py:534
  23.5 5.9 %collective-permute-start.7 = (bf16[4,64,512]{2,1,0:T(8,128)(2,1)S(1)}, bf16[4,64,512]{2,1,0:T(8,128)(2,1)S(1)}, u32[]{:S(2)}, u32[]{:S(2)}) collective-permute-start(bf16[4,64,512]{2,1,0:T(8,128)(2,1)S(1)} %get-tuple-element.87), channel_id=1, source_target_pairs={{0,4},{4,0},{8,12},{12,8},{16,20},{20,16},{24,28},{28,24},{1,5},{5... | collective-permute-start | bytes 786440 | tf_op jit(solution)/shard_map/ppermute | solution.py:534
  23.9 7.0 %collective-permute-start.10 = (bf16[4,32,768]{2,1,0:T(8,128)(2,1)S(1)}, bf16[4,32,768]{2,1,0:T(8,128)(2,1)S(1)}, u32[]{:S(2)}, u32[]{:S(2)}) collective-permute-start(bf16[4,32,768]{2,1,0:T(8,128)(2,1)S(1)} %get-tuple-element.102), channel_id=1, source_target_pairs={{0,1},{1,0},{2,3},{3,2},{4,5},{5,4},{6,7},{7,6},{8,9},{9,8},{10,11... | collective-permute-start | bytes 589832 | tf_op jit(solution)/shard_map/ppermute | solution.py:534
  25.8 10.9 %collective-permute-start.14 = (bf16[64,1024]{1,0:T(8,128)(2,1)S(1)}, bf16[64,1024]{1,0:T(8,128)(2,1)S(1)}, u32[]{:S(2)}, u32[]{:S(2)}) collective-permute-start(bf16[64,1024]{1,0:T(8,128)(2,1)S(1)} %get-tuple-element.108), channel_id=1, source_target_pairs={{0,24},{4,28},{8,16},{12,20},{16,8},{20,12},{24,0},{28,4},{1,25},{... | collective-permute-start | bytes 393224 | tf_op jit(solution)/shard_map/ppermute | solution.py:534
  28.3 8.9 %collective-permute-start.15 = (bf16[64,1024]{1,0:T(8,128)(2,1)S(1)}, bf16[64,1024]{1,0:T(8,128)(2,1)S(1)}, u32[]{:S(2)}, u32[]{:S(2)}) collective-permute-start(bf16[64,1024]{1,0:T(8,128)(2,1)S(1)} %get-tuple-element.109), channel_id=1, source_target_pairs={{0,16},{4,20},{8,24},{12,28},{16,0},{20,4},{24,8},{28,12},{1,17},{... | collective-permute-start | bytes 393224 | tf_op jit(solution)/shard_map/ppermute | solution.py:534
  28.8 8.4 %collective-permute-start.16 = (bf16[64,1024]{1,0:T(8,128)(2,1)S(1)}, bf16[64,1024]{1,0:T(8,128)(2,1)S(1)}, u32[]{:S(2)}, u32[]{:S(2)}) collective-permute-start(bf16[64,1024]{1,0:T(8,128)(2,1)S(1)} %get-tuple-element.110), channel_id=1, source_target_pairs={{0,8},{4,12},{8,0},{12,4},{16,24},{20,28},{24,16},{28,20},{1,9},{5... | collective-permute-start | bytes 393224 | tf_op jit(solution)/shard_map/ppermute | solution.py:534
  29.3 4.3 %collective-permute-start.9 = (bf16[4,32,256]{2,1,0:T(8,128)(2,1)S(1)}, bf16[4,32,256]{2,1,0:T(8,128)(2,1)S(1)}, u32[]{:S(2)}, u32[]{:S(2)}) collective-permute-start(bf16[4,32,256]{2,1,0:T(8,128)(2,1)S(1)} %get-tuple-element.99), channel_id=1, source_target_pairs={{0,1},{1,0},{2,3},{3,2},{4,5},{5,4},{6,7},{7,6},{8,9},{9,8},{10,11... | collective-permute-start | bytes 196616 | tf_op jit(solution)/shard_map/ppermute | solution.py:534
  33.7 5.6 %collective-permute-start.11 = (bf16[32,1024]{1,0:T(8,128)(2,1)S(1)}, bf16[32,1024]{1,0:T(8,128)(2,1)S(1)}, u32[]{:S(2)}, u32[]{:S(2)}) collective-permute-start(bf16[32,1024]{1,0:T(8,128)(2,1)S(1)} %get-tuple-element.104), channel_id=1, source_target_pairs={{0,24},{4,28},{8,16},{12,20},{16,8},{20,12},{24,0},{28,4},{1,25},{... | collective-permute-start | bytes 196616 | tf_op jit(solution)/shard_map/ppermute | solution.py:534
  36.2 4.3 %collective-permute-start.12 = (bf16[32,1024]{1,0:T(8,128)(2,1)S(1)}, bf16[32,1024]{1,0:T(8,128)(2,1)S(1)}, u32[]{:S(2)}, u32[]{:S(2)}) collective-permute-start(bf16[32,1024]{1,0:T(8,128)(2,1)S(1)} %get-tuple-element.105), channel_id=1, source_target_pairs={{0,16},{4,20},{8,24},{12,28},{16,0},{20,4},{24,8},{28,12},{1,17},{... | collective-permute-start | bytes 196616 | tf_op jit(solution)/shard_map/ppermute | solution.py:534
  36.7 4.3 %collective-permute-start.13 = (bf16[32,1024]{1,0:T(8,128)(2,1)S(1)}, bf16[32,1024]{1,0:T(8,128)(2,1)S(1)}, u32[]{:S(2)}, u32[]{:S(2)}) collective-permute-start(bf16[32,1024]{1,0:T(8,128)(2,1)S(1)} %get-tuple-element.106), channel_id=1, source_target_pairs={{0,8},{4,12},{8,0},{12,4},{16,24},{20,28},{24,16},{28,20},{1,9},{5... | collective-permute-start | bytes 196616 | tf_op jit(solution)/shard_map/ppermute | solution.py:534
  37.3 4.3 %collective-permute-start.17 = (bf16[32,1024]{1,0:T(8,128)(2,1)S(1)}, bf16[32,1024]{1,0:T(8,128)(2,1)S(1)}, u32[]{:S(2)}, u32[]{:S(2)}) collective-permute-start(bf16[32,1024]{1,0:T(8,128)(2,1)S(1)} %get-tuple-element.112), channel_id=1, source_target_pairs={{0,1},{1,0},{2,3},{3,2},{4,5},{5,4},{6,7},{7,6},{8,9},{9,8},{10,11... | collective-permute-start | bytes 196616 | tf_op jit(solution)/shard_map/ppermute | solution.py:534
  41.7 7.8 %collective-permute-start.21 = (bf16[32,2048]{1,0:T(8,128)(2,1)S(1)}, bf16[32,2048]{1,0:T(8,128)(2,1)S(1)}, u32[]{:S(2)}, u32[]{:S(2)}) collective-permute-start(bf16[32,2048]{1,0:T(8,128)(2,1)S(1)} %join_terms.1.kept_ref), channel_id=1, source_target_pairs={{0,2},{1,3},{2,0},{3,1},{4,6},{5,7},{6,4},{7,5},{8,10},{9,11},{10,... | collective-permute-start | bytes 393224 | tf_op jit(solution)/shard_map/ppermute | solution.py:534
  45.0 5.9 %collective-permute-start.18 = (bf16[128,512]{1,0:T(8,128)(2,1)S(1)}, bf16[128,512]{1,0:T(8,128)(2,1)S(1)}, u32[]{:S(2)}, u32[]{:S(2)}) collective-permute-start(bf16[128,512]{1,0:T(8,128)(2,1)S(1)} %get-tuple-element.114), channel_id=1, source_target_pairs={{0,24},{4,28},{8,16},{12,20},{16,8},{20,12},{24,0},{28,4},{1,25},{... | collective-permute-start | bytes 393224 | tf_op jit(solution)/shard_map/ppermute | solution.py:534
  47.5 5.0 %collective-permute-start.19 = (bf16[128,512]{1,0:T(8,128)(2,1)S(1)}, bf16[128,512]{1,0:T(8,128)(2,1)S(1)}, u32[]{:S(2)}, u32[]{:S(2)}) collective-permute-start(bf16[128,512]{1,0:T(8,128)(2,1)S(1)} %get-tuple-element.115), channel_id=1, source_target_pairs={{0,16},{4,20},{8,24},{12,28},{16,0},{20,4},{24,8},{28,12},{1,17},{... | collective-permute-start | bytes 393224 | tf_op jit(solution)/shard_map/ppermute | solution.py:534
  48.0 5.0 %collective-permute-start.20 = (bf16[128,512]{1,0:T(8,128)(2,1)S(1)}, bf16[128,512]{1,0:T(8,128)(2,1)S(1)}, u32[]{:S(2)}, u32[]{:S(2)}) collective-permute-start(bf16[128,512]{1,0:T(8,128)(2,1)S(1)} %get-tuple-element.116), channel_id=1, source_target_pairs={{0,8},{4,12},{8,0},{12,4},{16,24},{20,28},{24,16},{28,20},{1,9},{5... | collective-permute-start | bytes 393224 | tf_op jit(solution)/shard_map/ppermute | solution.py:534
  49.5 5.0 %collective-permute-start.22 = (bf16[32,2048]{1,0:T(8,128)(2,1)S(1)}, bf16[32,2048]{1,0:T(8,128)(2,1)S(1)}, u32[]{:S(2)}, u32[]{:S(2)}) collective-permute-start(bf16[32,2048]{1,0:T(8,128)(2,1)S(1)} %add_pairs.1.held_ref), channel_id=1, source_target_pairs={{0,1},{1,0},{2,3},{3,2},{4,5},{5,4},{6,7},{7,6},{8,9},{9,8},{10,11... | collective-permute-start | bytes 393224 | tf_op jit(solution)/shard_map/ppermute | solution.py:534

commit v17 on v13

--- a/solution.py
+++ b/solution.py
@@ -21,7 +21,7 @@
 VMEM = pl.BlockSpec(memory_space=pltpu.VMEM)
 HBM = pl.BlockSpec(memory_space=pltpu.HBM)
 CHIP_STEPS = (3, 2, 1)
-FIRST_PART = 384
+FIRST_PART = 512
 SWAP_PIECES = (384, 384, 256, 256)
 PINNED = pl.BlockSpec(memory_space=pltpu.VMEM)
 shaped = jax.ShapeDtypeStruct
@@ -302,7 +302,7 @@
 
 
 def column_chip_kernel(
-    x_ref, cot_ref, near_1, near_2, near_3, far_ref, gain_ref, w_ref, wo_ref, row_out_ref,
+    x_ref, cot_ref, near_1, near_2, near_3, far_ref, last_ref, gain_ref, w_ref, wo_ref, row_out_ref,
     keep_ref, grads_ref, *refs,
 ):
     chip, core, _ = here()
@@ -313,8 +313,9 @@
 
     def tokens(which, mine):
         pieces = [mine[at, :], far_ref[0, which]]
-        for i, near in enumerate((near_1, near_2, near_3)):
-            pieces += [near[which, half, :], far_ref[i + 1, which]]
+        fars = last_ref[which], far_ref[1, which], far_ref[2, which]
+        for near, far in zip((near_1, near_2, near_3), fars):
+            pieces += [near[which, half, :], far]
         starts = range(0, share, group)
         return jnp.concatenate(
             [piece[start : start + group] for start in starts for piece in pieces], 0
@@ -341,14 +342,22 @@
         at += piece.shape[2]
 
 
-def far_kernel(x_ref, cot_ref, near_1, near_2, near_3, far_ref):
+def other_core(near, share):
+    at = pl.ds(pl.multiple_of((1 - here()[1]) * share, share), share)
+    return near[:, at, :]
+
+
+def far_kernel(x_ref, cot_ref, near_2, near_3, far_ref):
     chip, core, _ = here()
     share = far_ref.shape[2]
     at = pl.ds(pl.multiple_of((chip * 2 + 1 - core) * share, share), share)
     far_ref[0, 0], far_ref[0, 1] = x_ref[at, :], cot_ref[at, :]
-    at = pl.ds(pl.multiple_of((1 - core) * share, share), share)
-    for i, near in enumerate((near_1, near_2, near_3)):
-        far_ref[i + 1] = near[:, at, :]
+    for i, near in enumerate((near_2, near_3)):
+        far_ref[i + 1] = other_core(near, share)
+
+
+def last_far_kernel(near_1, far_ref):
+    far_ref[...] = other_core(near_1, far_ref.shape[1])
 
 
 def back_kernel(grads_ref, w_ref, back_ref):
@@ -438,12 +447,13 @@
 
 def cores_kernel(keep_ref, got_1, got_2, got_3, got_4, send_ref, kept_ref, *targets):
     chip, cut = here()[0], kept_ref.shape[2]
-    first = keep_ref[:, :, :cut].astype(F32) + got_1[...].astype(F32)
+    got = jnp.concatenate([ref[...] for ref in (got_1, got_2)], 2)
+    first = keep_ref[:, :, :cut].astype(F32) + got[:, :, :cut].astype(F32)
     send_ref[...], kept_ref[...] = split_rows(first, 1)
     for step, target in zip((0, *CHIP_STEPS), targets):
         there = chip ^ step
-        got = jnp.concatenate([ref[there] for ref in (got_2, got_3, got_4)], 1)
-        total = keep_ref[there, :, cut:].astype(F32) + got.astype(F32)
+        got = jnp.concatenate([ref[there] for ref in (got_1, got_2, got_3, got_4)], 1)
+        total = keep_ref[there, :, cut:].astype(F32) + got[:, cut:].astype(F32)
         target[...] = total.astype(target.dtype)
 
 
@@ -619,12 +629,19 @@
             [(half_block, BF16), (half_block, F32)],
             out_specs=[VMEM, PINNED],
         )
-        *near, row_kept = lax.optimization_barrier((*near, row_kept))
+        col_weight, row_kept = lax.optimization_barrier((col_weight, row_kept))
         (far,) = call(
             far_kernel,
             "pack_other_core",
-            [(VMEM, one) for one in (x_near, cot_near, *near)],
-            [((chips, 2, share, width), BF16)],
+            [(VMEM, one) for one in (x_near, cot_near, *near[1:])],
+            [((3, 2, share, width), BF16)],
+        )
+        near[0], _ = lax.optimization_barrier((near[0], far))
+        (last,) = call(
+            last_far_kernel,
+            "pack_other_core_last",
+            [(VMEM, near[0])],
+            [((2, share, width), BF16)],
         )
         row_got = swap(row_next, "dp", 1)
         keep, col_grads, *pieces = call(
@@ -633,7 +650,7 @@
             [
                 (VMEM, one)
                 for one in (
-                    x_near, cot_near, *near, swap(far, "seq", 1),
+                    x_near, cot_near, *near, swap(far, "seq", 1), swap(last, "seq", 1),
                     gain, col_weight, col_out_weight, row_out,
                 )
             ],

time: 55.9 us -> 55.5 us (level)
  starting transfers between devices: 25.6 us -> 24.6 us
  waiting for transfers between devices: 14.1 us -> 14.7 us
    ppermute x25 -> x26, starting transfers between devices: 25.6 us -> 24.6 us  [swap(): return lax.ppermute(array, axis, [(i, i ^ bits) for i in range(count)])]
    ppermute x25 -> x26, waiting for transfers between devices: 14.1 us -> 14.7 us  [swap(): return lax.ppermute(array, axis, [(i, i ^ bits) for i in range(count)])]
    pallas_call x14 -> x15, Pallas kernels: 15.3 us -> 15.3 us  [call(): pl.pallas_call(kernel, out_shape=outs, in_specs=[spec for spec, _ in ins]...]
  transfers between devices with their start and end apart: 25 -> 26, of which waited for: 13 -> 12; matrix products, arithmetic and copies ran while one was open for 0% -> 0% of each run, Pallas kernels for 23% -> 24%
where the time goes in v17:
time: 55.5 us; the launch traced here: 55.4 us
  starting transfers between devices  24.6 us (44%)
  Pallas kernels  15.3 us (28%)
  waiting for transfers between devices  14.7 us (26%)
  between operations  0.79 us (1%)
    ppermute x26, starting transfers between devices, swap(): return lax.ppermute(array, axis, [(i, i ^ bits) for i in range(count)])  24.6 us
    pallas_call x15, Pallas kernels, call(): pl.pallas_call(kernel, out_shape=outs, in_specs=[spec for spec, _ in ins]...  15.3 us
    ppermute x26, waiting for transfers between devices, swap(): return lax.ppermute(array, axis, [(i, i ^ bits) for i in range(count)])  14.7 us
  transfers between devices with their start and end apart: 26, of which 12 were waited for; matrix products, arithmetic and copies ran while one was open for 0% of the time, Pallas kernels for 24%

profile of v17, /device:TPU:0, one launch (start us, length us, event | category | flops | bytes accessed | tf_op | source)
XLA Modules:
  0.0 55.4 jit_solution(13884046972458906828)
XLA Ops:
  0.6 1.3 %pack_columns.1 = (bf16[2,128,512]{2,1,0:T(8,128)(2,1)S(1)}, bf16[2,128,512]{2,1,0:T(8,128)(2,1)S(1)}, bf16[2,128,512]{2,1,0:T(8,128)(2,1)S(1)}) custom-call(bf16[512,512]{1,0:T(8,128)(2,1)} %bitcast.9, bf16[512,512]{1,0:T(8,128)(2,1)} %bitcast.11), custom_call_target="tpu_custom_call" | custom-call | tf_op jit(solution)/shard_map/pack_columns/pallas_call | solution.py:528
  1.9 3.0 %collective-permute-start.3 = (bf16[2,128,512]{2,1,0:T(8,128)(2,1)S(1)}, bf16[2,128,512]{2,1,0:T(8,128)(2,1)S(1)}, u32[]{:S(2)}, u32[]{:S(2)}) collective-permute-start(bf16[2,128,512]{2,1,0:T(8,128)(2,1)S(1)} %get-tuple-element.80), channel_id=1, source_target_pairs={{0,16},{4,20},{8,24},{12,28},{16,0},{20,4},{24,8},{28,12},{1,17},{... | collective-permute-start | bytes 786440 | tf_op jit(solution)/shard_map/ppermute | solution.py:542
  4.9 1.5 %collective-permute-start.4 = (bf16[2,128,512]{2,1,0:T(8,128)(2,1)S(1)}, bf16[2,128,512]{2,1,0:T(8,128)(2,1)S(1)}, u32[]{:S(2)}, u32[]{:S(2)}) collective-permute-start(bf16[2,128,512]{2,1,0:T(8,128)(2,1)S(1)} %get-tuple-element.81), channel_id=1, source_target_pairs={{0,8},{4,12},{8,0},{12,4},{16,24},{20,28},{24,16},{28,20},{1,9},{5... | collective-permute-start | bytes 786440 | tf_op jit(solution)/shard_map/ppermute | solution.py:542
  6.4 0.0 collective-permute-start.2
  6.5 7.7 %row_heads.1 = (bf16[4,64,384]{2,1,0:T(8,128)(2,1)S(1)}, bf16[4,64,384]{2,1,0:T(8,128)(2,1)S(1)}, bf16[4,64,384]{2,1,0:T(8,128)(2,1)S(1)}, bf16[4,64,384]{2,1,0:...) custom-call(bf16[512,512]{1,0:T(8,128)(2,1)} %bitcast.10, ...), custom_call_target="tpu_custom_call" | custom-call | tf_op jit(solution)/shard_map/row_heads/pallas_call | solution.py:528
  14.1 0.0 collective-permute-done.4.near_3
  14.2 0.1 collective-permute-start.5
  14.3 0.5 collective-permute-start
  14.8 0.1 collective-permute-start.1
  14.9 3.2 %collective-permute-done.2.near_1 = bf16[2,128,512]{2,1,0:T(8,128)(2,1)S(1)} collective-permute-done((bf16[2,128,512]{2,1,0:T(8,128)(2,1)S(1)}, bf16[2,128,512]{2,1,0:T(8,128)(2,1)S(1)}, u32[]{:S(2)}, u32[]{:S(2)}) %collective-permute-start.2) | collective-permute-done | bytes 262176 | tf_op jit(solution)/shard_map/ppermute | solution.py:542
  18.1 0.1 collective-permute-start.6
  18.2 0.1 row_add_cores.1
  18.4 1.8 %collective-permute-start.7 = (bf16[4,32,768]{2,1,0:T(8,128)(2,1)S(1)}, bf16[4,32,768]{2,1,0:T(8,128)(2,1)S(1)}, u32[]{:S(2)}, u32[]{:S(2)}) collective-permute-start(bf16[4,32,768]{2,1,0:T(8,128)(2,1)S(1)} %get-tuple-element.89), channel_id=1, source_target_pairs={{0,1},{1,0},{2,3},{3,2},{4,5},{5,4},{6,7},{7,6},{8,9},{9,8},{10,11... | collective-permute-start | bytes 589832 | tf_op jit(solution)/shard_map/ppermute | solution.py:542
  20.2 3.1 %column_heads.1 = (bf16[4,64,1280]{2,1,0:T(8,128)(2,1)S(1)}, bf16[512,768]{1,0:T(8,128)(2,1)S(1)}, bf16[4,64,384]{2,1,0:T(8,128)(2,1)S(1)}, bf16[4,64,384]{2,1,0...) custom-call(bf16[512,512]{1,0:T(8,128)(2,1)S(1)} %get-tuple-element.78.x_ref, ...), custom_call_target="tpu_custom_call" | custom-call | tf_op jit(solution)/shard_map/column_heads/pallas_call | solution.py:528
  23.3 0.3 collective-permute-start.9
  23.6 0.3 collective-permute-start.10
  23.9 0.6 %column_grad_hidden.1 = (bf16[4,64,512]{2,1,0:T(8,128)(2,1)S(1)}, bf16[4,64,512]{2,1,0:T(8,128)(2,1)S(1)}) custom-call(bf16[512,768]{1,0:T(8,128)(2,1)S(1)} %get-tuple-element.87.grads_ref, bf16[512,768]{1,0:T(8,128)(2,1)S(1)} %get-tuple-element.83.w_ref), custom_call_target="tpu_custom_call" | custom-call | tf_op jit(solution)/shard_map/column_grad_hidden/pallas_call | solution.py:528
  24.5 0.3 collective-permute-start.8
  24.8 0.3 collective-permute-start.11
  25.1 0.6 %collective-permute-done.7.row_got = bf16[4,32,768]{2,1,0:T(8,128)(2,1)S(1)} collective-permute-done((bf16[4,32,768]{2,1,0:T(8,128)(2,1)S(1)}, bf16[4,32,768]{2,1,0:T(8,128)(2,1)S(1)}, u32[]{:S(2)}, u32[]{:S(2)}) %collective-permute-start.7) | collective-permute-done | bytes 196640 | tf_op jit(solution)/shard_map/ppermute | solution.py:542
  25.7 0.6 %collective-permute-done.11.got_3 = bf16[4,64,256]{2,1,0:T(8,128)(2,1)S(1)} collective-permute-done((bf16[4,64,256]{2,1,0:T(8,128)(2,1)S(1)}, bf16[4,64,256]{2,1,0:T(8,128)(2,1)S(1)}, u32[]{:S(2)}, u32[]{:S(2)}) %collective-permute-start.11) | collective-permute-done | bytes 131104 | tf_op jit(solution)/shard_map/ppermute | solution.py:542
  26.3 0.8 %collective-permute-done.12.got_4 = bf16[4,64,256]{2,1,0:T(8,128)(2,1)S(1)} collective-permute-done((bf16[4,64,256]{2,1,0:T(8,128)(2,1)S(1)}, bf16[4,64,256]{2,1,0:T(8,128)(2,1)S(1)}, u32[]{:S(2)}, u32[]{:S(2)}) %collective-permute-start.12) | collective-permute-done | bytes 131104 | tf_op jit(solution)/shard_map/ppermute | solution.py:542
  27.1 0.2 column_add_cores.1
  27.3 1.8 %collective-permute-start.13 = (bf16[4,32,512]{2,1,0:T(8,128)(2,1)S(1)}, bf16[4,32,512]{2,1,0:T(8,128)(2,1)S(1)}, u32[]{:S(2)}, u32[]{:S(2)}) collective-permute-start(bf16[4,32,512]{2,1,0:T(8,128)(2,1)S(1)} %get-tuple-element.106), channel_id=1, source_target_pairs={{0,1},{1,0},{2,3},{3,2},{4,5},{5,4},{6,7},{7,6},{8,9},{9,8},{10,11... | collective-permute-start | bytes 393224 | tf_op jit(solution)/shard_map/ppermute | solution.py:542
  29.0 2.4 %collective-permute-start.17 = (bf16[64,768]{1,0:T(8,128)(2,1)S(1)}, bf16[64,768]{1,0:T(8,128)(2,1)S(1)}, u32[]{:S(2)}, u32[]{:S(2)}) collective-permute-start(bf16[64,768]{1,0:T(8,128)(2,1)S(1)} %get-tuple-element.114), channel_id=1, source_target_pairs={{0,24},{4,28},{8,16},{12,20},{16,8},{20,12},{24,0},{28,4},{1,25},{... | collective-permute-start | bytes 294920 | tf_op jit(solution)/shard_map/ppermute | solution.py:542
  31.5 0.5 collective-permute-start.18
  32.0 0.5 collective-permute-start.19
  32.6 0.3 collective-permute-done.13.got_ref
  32.9 0.1 first_add_pair.1
  32.9 2.7 %collective-permute-start.14 = (bf16[32,1280]{1,0:T(8,128)(2,1)S(1)}, bf16[32,1280]{1,0:T(8,128)(2,1)S(1)}, u32[]{:S(2)}, u32[]{:S(2)}) collective-permute-start(bf16[32,1280]{1,0:T(8,128)(2,1)S(1)} %get-tuple-element.110), channel_id=1, source_target_pairs={{0,24},{4,28},{8,16},{12,20},{16,8},{20,12},{24,0},{28,4},{1,25},{... | collective-permute-start | bytes 245768 | tf_op jit(solution)/shard_map/ppermute | solution.py:542
  35.6 0.5 collective-permute-start.15
  36.1 0.7 %collective-permute-start.16 = (bf16[32,1280]{1,0:T(8,128)(2,1)S(1)}, bf16[32,1280]{1,0:T(8,128)(2,1)S(1)}, u32[]{:S(2)}, u32[]{:S(2)}) collective-permute-start(bf16[32,1280]{1,0:T(8,128)(2,1)S(1)} %get-tuple-element.112), channel_id=1, source_target_pairs={{0,8},{4,12},{8,0},{12,4},{16,24},{20,28},{24,16},{28,20},{1,9},{5... | collective-permute-start | bytes 245768 | tf_op jit(solution)/shard_map/ppermute | solution.py:542
  36.8 1.0 %collective-permute-done.18.got_2 = bf16[64,768]{1,0:T(8,128)(2,1)S(1)} collective-permute-done((bf16[64,768]{1,0:T(8,128)(2,1)S(1)}, bf16[64,768]{1,0:T(8,128)(2,1)S(1)}, u32[]{:S(2)}, u32[]{:S(2)}) %collective-permute-start.18) | collective-permute-done | bytes 98336 | tf_op jit(solution)/shard_map/ppermute | solution.py:542
  37.8 0.1 second_add_chips.1
  37.9 0.5 collective-permute-start.20
  38.4 3.6 %collective-permute-done.20.got_ref = bf16[32,768]{1,0:T(8,128)(2,1)S(1)} collective-permute-done((bf16[32,768]{1,0:T(8,128)(2,1)S(1)}, bf16[32,768]{1,0:T(8,128)(2,1)S(1)}, u32[]{:S(2)}, u32[]{:S(2)}) %collective-permute-start.20) | collective-permute-done | bytes 49184 | tf_op jit(solution)/shard_map/ppermute | solution.py:542
  42.1 3.2 %collective-permute-start.24 = (bf16[32,2048]{1,0:T(8,128)(2,1)S(1)}, bf16[32,2048]{1,0:T(8,128)(2,1)S(1)}, u32[]{:S(2)}, u32[]{:S(2)}) collective-permute-start(bf16[32,2048]{1,0:T(8,128)(2,1)S(1)} %join_terms.1.kept_ref), channel_id=1, source_target_pairs={{0,2},{1,3},{2,0},{3,1},{4,6},{5,7},{6,4},{7,5},{8,10},{9,11},{10,... | collective-permute-start | bytes 393224 | tf_op jit(solution)/shard_map/ppermute | solution.py:542
  45.2 0.8 %collective-permute-start.21 = (bf16[128,512]{1,0:T(8,128)(2,1)S(1)}, bf16[128,512]{1,0:T(8,128)(2,1)S(1)}, u32[]{:S(2)}, u32[]{:S(2)}) collective-permute-start(bf16[128,512]{1,0:T(8,128)(2,1)S(1)} %get-tuple-element.120), channel_id=1, source_target_pairs={{0,24},{4,28},{8,16},{12,20},{16,8},{20,12},{24,0},{28,4},{1,25},{... | collective-permute-start | bytes 393224 | tf_op jit(solution)/shard_map/ppermute | solution.py:542
  46.0 1.8 %collective-permute-start.22 = (bf16[128,512]{1,0:T(8,128)(2,1)S(1)}, bf16[128,512]{1,0:T(8,128)(2,1)S(1)}, u32[]{:S(2)}, u32[]{:S(2)}) collective-permute-start(bf16[128,512]{1,0:T(8,128)(2,1)S(1)} %get-tuple-element.121), channel_id=1, source_target_pairs={{0,16},{4,20},{8,24},{12,28},{16,0},{20,4},{24,8},{28,12},{1,17},{... | collective-permute-start | bytes 393224 | tf_op jit(solution)/shard_map/ppermute | solution.py:542
  47.8 0.9 %collective-permute-start.23 = (bf16[128,512]{1,0:T(8,128)(2,1)S(1)}, bf16[128,512]{1,0:T(8,128)(2,1)S(1)}, u32[]{:S(2)}, u32[]{:S(2)}) collective-permute-start(bf16[128,512]{1,0:T(8,128)(2,1)S(1)} %get-tuple-element.122), channel_id=1, source_target_pairs={{0,8},{4,12},{8,0},{12,4},{16,24},{20,28},{24,16},{28,20},{1,9},{5... | collective-permute-start | bytes 393224 | tf_op jit(solution)/shard_map/ppermute | solution.py:542
  48.7 0.7 %collective-permute-done.24.got_ref = bf16[32,2048]{1,0:T(8,128)(2,1)S(1)} collective-permute-done((bf16[32,2048]{1,0:T(8,128)(2,1)S(1)}, bf16[32,2048]{1,0:T(8,128)(2,1)S(1)}, u32[]{:S(2)}, u32[]{:S(2)}) %collective-permute-start.24) | collective-permute-done | bytes 131104 | tf_op jit(solution)/shard_map/ppermute | solution.py:542
  49.5 0.1 collective-permute-start.25
  49.6 1.7 %collective-permute-done.21.got_1 = bf16[128,512]{1,0:T(8,128)(2,1)S(1)} collective-permute-done((bf16[128,512]{1,0:T(8,128)(2,1)S(1)}, bf16[128,512]{1,0:T(8,128)(2,1)S(1)}, u32[]{:S(2)}, u32[]{:S(2)}) %collective-permute-start.21) | collective-permute-done | bytes 131104 | tf_op jit(solution)/shard_map/ppermute | solution.py:542
  51.2 1.2 %collective-permute-done.22.got_2 = bf16[128,512]{1,0:T(8,128)(2,1)S(1)} collective-permute-done((bf16[128,512]{1,0:T(8,128)(2,1)S(1)}, bf16[128,512]{1,0:T(8,128)(2,1)S(1)}, u32[]{:S(2)}, u32[]{:S(2)}) %collective-permute-start.22) | collective-permute-done | bytes 131104 | tf_op jit(solution)/shard_map/ppermute | solution.py:542
  52.4 0.3 collective-permute-done.23.got_3
  52.8 1.1 %input_grad.1 = bf16[512,512]{1,0:T(8,128)(2,1)} custom-call(f32[512,512]{1,0:T(8,128)S(1)} %get-tuple-element.68.base_ref, f32[512,512]{1,0:T(8,128)S(1)} %get-tuple-element.69.normed_ref, f32[512,1]{1,0:T(8,128)S(1)} %get-tuple-element.70.inverse_ref, f32[1,512]{1,0:T(1,128)S(1)} %bitcast.7, bf16[128,512]{1,0:T(8,128)(2,1)S(1)} %get-tuple-element.119.own_ref, ...), custom_call_target="tpu_custom_call" | custom-call | tf_op jit(solution)/shard_map/input_grad/pallas_call | solution.py:528
  53.9 0.6 %collective-permute-done.25.got_ref = bf16[32,2048]{1,0:T(8,128)(2,1)S(1)} collective-permute-done((bf16[32,2048]{1,0:T(8,128)(2,1)S(1)}, bf16[32,2048]{1,0:T(8,128)(2,1)S(1)}, u32[]{:S(2)}, u32[]{:S(2)}) %collective-permute-start.25) | collective-permute-done | bytes 131104 | tf_op jit(solution)/shard_map/ppermute | solution.py:542
  54.5 0.9 %result.1 = (f32[64,1536]{1,0:T(8,128)}, f32[64,512]{1,0:T(8,128)}, f32[1,64]{1,0:T(1,128)}) custom-call(bf16[32,2048]{1,0:T(8,128)(2,1)S(1)} %add_pairs.1.held_ref, bf16[32,2048]{1,0:T(8,128)(2,1)S(1)} %collective-permute-done.25.got_ref, bf16[64,1536]{1,0:T(8,128)(2,1)S(1)} %get-tuple-element.124.w_ref, f32[1,512]{1,0:T(1,128)S(1)} %bitcast.8), custom_call_target="tpu_custom_call" | custom-call | tf_op jit(solution)/shard_map/result/pallas_call | solution.py:528
  (21 shorter events, 0.2 us)
Async XLA Ops:
  1.9 12.2 %collective-permute-start.3 = (bf16[2,128,512]{2,1,0:T(8,128)(2,1)S(1)}, bf16[2,128,512]{2,1,0:T(8,128)(2,1)S(1)}, u32[]{:S(2)}, u32[]{:S(2)}) collective-permute-start(bf16[2,128,512]{2,1,0:T(8,128)(2,1)S(1)} %get-tuple-element.80), channel_id=1, source_target_pairs={{0,16},{4,20},{8,24},{12,28},{16,0},{20,4},{24,8},{28,12},{1,17},{... | collective-permute-start | bytes 786440 | tf_op jit(solution)/shard_map/ppermute | solution.py:542
  4.9 9.2 %collective-permute-start.4 = (bf16[2,128,512]{2,1,0:T(8,128)(2,1)S(1)}, bf16[2,128,512]{2,1,0:T(8,128)(2,1)S(1)}, u32[]{:S(2)}, u32[]{:S(2)}) collective-permute-start(bf16[2,128,512]{2,1,0:T(8,128)(2,1)S(1)} %get-tuple-element.81), channel_id=1, source_target_pairs={{0,8},{4,12},{8,0},{12,4},{16,24},{20,28},{24,16},{28,20},{1,9},{5... | collective-permute-start | bytes 786440 | tf_op jit(solution)/shard_map/ppermute | solution.py:542
  6.4 11.7 %collective-permute-start.2 = (bf16[2,128,512]{2,1,0:T(8,128)(2,1)S(1)}, bf16[2,128,512]{2,1,0:T(8,128)(2,1)S(1)}, u32[]{:S(2)}, u32[]{:S(2)}) collective-permute-start(bf16[2,128,512]{2,1,0:T(8,128)(2,1)S(1)} %get-tuple-element.66), channel_id=1, source_target_pairs={{0,24},{4,28},{8,16},{12,20},{16,8},{20,12},{24,0},{28,4},{1,25},{... | collective-permute-start | bytes 786440 | tf_op jit(solution)/shard_map/ppermute | solution.py:542
  14.2 6.0 %copy-start = (f32[512]{0:T(512)S(1)}, f32[512]{0:T(512)}, u32[]{:S(2)}) copy-start(f32[512]{0:T(512)} %param.6) | copy-start | bytes 6148
  14.2 5.9 %collective-permute-start.5 = (bf16[3,2,64,512]{3,2,1,0:T(8,128)(2,1)S(1)}, bf16[3,2,64,512]{3,2,1,0:T(8,128)(2,1)S(1)}, u32[]{:S(2)}, u32[]{:S(2)}) collective-permute-start(bf16[3,2,64,512]{3,2,1,0:T(8,128)(2,1)S(1)} %pack_other_core.1), channel_id=1, source_target_pairs={{0,4},{4,0},{8,12},{12,8},{16,20},{20,16},{24,28},{28,24},{1,5},{5... | collective-permute-start | bytes 1179656 | tf_op jit(solution)/shard_map/ppermute | solution.py:542
  14.3 3.9 %collective-permute-start = (bf16[4,64,384]{2,1,0:T(8,128)(2,1)S(1)}, bf16[4,64,384]{2,1,0:T(8,128)(2,1)S(1)}, u32[]{:S(2)}, u32[]{:S(2)}) collective-permute-start(bf16[4,64,384]{2,1,0:T(8,128)(2,1)S(1)} %get-tuple-element.74), channel_id=1, source_target_pairs={{0,4},{4,0},{8,12},{12,8},{16,20},{20,16},{24,28},{28,24},{1,5},{5... | collective-permute-start | bytes 589832 | tf_op jit(solution)/shard_map/ppermute | solution.py:542
  14.8 3.4 %collective-permute-start.1 = (bf16[4,64,384]{2,1,0:T(8,128)(2,1)S(1)}, bf16[4,64,384]{2,1,0:T(8,128)(2,1)S(1)}, u32[]{:S(2)}, u32[]{:S(2)}) collective-permute-start(bf16[4,64,384]{2,1,0:T(8,128)(2,1)S(1)} %get-tuple-element.75), channel_id=1, source_target_pairs={{0,4},{4,0},{8,12},{12,8},{16,20},{20,16},{24,28},{28,24},{1,5},{5... | collective-permute-start | bytes 589832 | tf_op jit(solution)/shard_map/ppermute | solution.py:542
  18.1 2.0 %collective-permute-start.6 = (bf16[2,64,512]{2,1,0:T(8,128)(2,1)S(1)}, bf16[2,64,512]{2,1,0:T(8,128)(2,1)S(1)}, u32[]{:S(2)}, u32[]{:S(2)}) collective-permute-start(bf16[2,64,512]{2,1,0:T(8,128)(2,1)S(1)} %pack_other_core_last.1), channel_id=1, source_target_pairs={{0,4},{4,0},{8,12},{12,8},{16,20},{20,16},{24,28},{28,24},{1,5},{5... | collective-permute-start | bytes 393224 | tf_op jit(solution)/shard_map/ppermute | solution.py:542
  18.4 7.3 %collective-permute-start.7 = (bf16[4,32,768]{2,1,0:T(8,128)(2,1)S(1)}, bf16[4,32,768]{2,1,0:T(8,128)(2,1)S(1)}, u32[]{:S(2)}, u32[]{:S(2)}) collective-permute-start(bf16[4,32,768]{2,1,0:T(8,128)(2,1)S(1)} %get-tuple-element.89), channel_id=1, source_target_pairs={{0,1},{1,0},{2,3},{3,2},{4,5},{5,4},{6,7},{7,6},{8,9},{9,8},{10,11... | collective-permute-start | bytes 589832 | tf_op jit(solution)/shard_map/ppermute | solution.py:542
  23.3 3.8 %collective-permute-start.9 = (bf16[4,64,384]{2,1,0:T(8,128)(2,1)S(1)}, bf16[4,64,384]{2,1,0:T(8,128)(2,1)S(1)}, u32[]{:S(2)}, u32[]{:S(2)}) collective-permute-start(bf16[4,64,384]{2,1,0:T(8,128)(2,1)S(1)} %get-tuple-element.101), channel_id=1, source_target_pairs={{0,4},{4,0},{8,12},{12,8},{16,20},{20,16},{24,28},{28,24},{1,5},{5... | collective-permute-start | bytes 589832 | tf_op jit(solution)/shard_map/ppermute | solution.py:542
  23.6 3.5 %collective-permute-start.10 = (bf16[4,64,384]{2,1,0:T(8,128)(2,1)S(1)}, bf16[4,64,384]{2,1,0:T(8,128)(2,1)S(1)}, u32[]{:S(2)}, u32[]{:S(2)}) collective-permute-start(bf16[4,64,384]{2,1,0:T(8,128)(2,1)S(1)} %get-tuple-element.102), channel_id=1, source_target_pairs={{0,4},{4,0},{8,12},{12,8},{16,20},{20,16},{24,28},{28,24},{1,5},{5... | collective-permute-start | bytes 589832 | tf_op jit(solution)/shard_map/ppermute | solution.py:542
  24.5 8.0 %collective-permute-start.8 = (bf16[4,64,512]{2,1,0:T(8,128)(2,1)S(1)}, bf16[4,64,512]{2,1,0:T(8,128)(2,1)S(1)}, u32[]{:S(2)}, u32[]{:S(2)}) collective-permute-start(bf16[4,64,512]{2,1,0:T(8,128)(2,1)S(1)} %get-tuple-element.91), channel_id=1, source_target_pairs={{0,4},{4,0},{8,12},{12,8},{16,20},{20,16},{24,28},{28,24},{1,5},{5... | collective-permute-start | bytes 786440 | tf_op jit(solution)/shard_map/ppermute | solution.py:542
  24.8 1.5 %collective-permute-start.11 = (bf16[4,64,256]{2,1,0:T(8,128)(2,1)S(1)}, bf16[4,64,256]{2,1,0:T(8,128)(2,1)S(1)}, u32[]{:S(2)}, u32[]{:S(2)}) collective-permute-start(bf16[4,64,256]{2,1,0:T(8,128)(2,1)S(1)} %get-tuple-element.103), channel_id=1, source_target_pairs={{0,4},{4,0},{8,12},{12,8},{16,20},{20,16},{24,28},{28,24},{1,5},{5... | collective-permute-start | bytes 393224 | tf_op jit(solution)/shard_map/ppermute | solution.py:542
  25.7 1.3 %collective-permute-start.12 = (bf16[4,64,256]{2,1,0:T(8,128)(2,1)S(1)}, bf16[4,64,256]{2,1,0:T(8,128)(2,1)S(1)}, u32[]{:S(2)}, u32[]{:S(2)}) collective-permute-start(bf16[4,64,256]{2,1,0:T(8,128)(2,1)S(1)} %get-tuple-element.104), channel_id=1, source_target_pairs={{0,4},{4,0},{8,12},{12,8},{16,20},{20,16},{24,28},{28,24},{1,5},{5... | collective-permute-start | bytes 393224 | tf_op jit(solution)/shard_map/ppermute | solution.py:542
  27.3 5.6 %collective-permute-start.13 = (bf16[4,32,512]{2,1,0:T(8,128)(2,1)S(1)}, bf16[4,32,512]{2,1,0:T(8,128)(2,1)S(1)}, u32[]{:S(2)}, u32[]{:S(2)}) collective-permute-start(bf16[4,32,512]{2,1,0:T(8,128)(2,1)S(1)} %get-tuple-element.106), channel_id=1, source_target_pairs={{0,1},{1,0},{2,3},{3,2},{4,5},{5,4},{6,7},{7,6},{8,9},{9,8},{10,11... | collective-permute-start | bytes 393224 | tf_op jit(solution)/shard_map/ppermute | solution.py:542
  29.0 7.1 %collective-permute-start.17 = (bf16[64,768]{1,0:T(8,128)(2,1)S(1)}, bf16[64,768]{1,0:T(8,128)(2,1)S(1)}, u32[]{:S(2)}, u32[]{:S(2)}) collective-permute-start(bf16[64,768]{1,0:T(8,128)(2,1)S(1)} %get-tuple-element.114), channel_id=1, source_target_pairs={{0,24},{4,28},{8,16},{12,20},{16,8},{20,12},{24,0},{28,4},{1,25},{... | collective-permute-start | bytes 294920 | tf_op jit(solution)/shard_map/ppermute | solution.py:542
  31.5 6.3 %collective-permute-start.18 = (bf16[64,768]{1,0:T(8,128)(2,1)S(1)}, bf16[64,768]{1,0:T(8,128)(2,1)S(1)}, u32[]{:S(2)}, u32[]{:S(2)}) collective-permute-start(bf16[64,768]{1,0:T(8,128)(2,1)S(1)} %get-tuple-element.115), channel_id=1, source_target_pairs={{0,16},{4,20},{8,24},{12,28},{16,0},{20,4},{24,8},{28,12},{1,17},{... | collective-permute-start | bytes 294920 | tf_op jit(solution)/shard_map/ppermute | solution.py:542
  32.0 5.8 %collective-permute-start.19 = (bf16[64,768]{1,0:T(8,128)(2,1)S(1)}, bf16[64,768]{1,0:T(8,128)(2,1)S(1)}, u32[]{:S(2)}, u32[]{:S(2)}) collective-permute-start(bf16[64,768]{1,0:T(8,128)(2,1)S(1)} %get-tuple-element.116), channel_id=1, source_target_pairs={{0,8},{4,12},{8,0},{12,4},{16,24},{20,28},{24,16},{28,20},{1,9},{5... | collective-permute-start | bytes 294920 | tf_op jit(solution)/shard_map/ppermute | solution.py:542
  32.9 9.1 %collective-permute-start.14 = (bf16[32,1280]{1,0:T(8,128)(2,1)S(1)}, bf16[32,1280]{1,0:T(8,128)(2,1)S(1)}, u32[]{:S(2)}, u32[]{:S(2)}) collective-permute-start(bf16[32,1280]{1,0:T(8,128)(2,1)S(1)} %get-tuple-element.110), channel_id=1, source_target_pairs={{0,24},{4,28},{8,16},{12,20},{16,8},{20,12},{24,0},{28,4},{1,25},{... | collective-permute-start | bytes 245768 | tf_op jit(solution)/shard_map/ppermute | solution.py:542
  35.6 6.4 %collective-permute-start.15 = (bf16[32,1280]{1,0:T(8,128)(2,1)S(1)}, bf16[32,1280]{1,0:T(8,128)(2,1)S(1)}, u32[]{:S(2)}, u32[]{:S(2)}) collective-permute-start(bf16[32,1280]{1,0:T(8,128)(2,1)S(1)} %get-tuple-element.111), channel_id=1, source_target_pairs={{0,16},{4,20},{8,24},{12,28},{16,0},{20,4},{24,8},{28,12},{1,17},{... | collective-permute-start | bytes 245768 | tf_op jit(solution)/shard_map/ppermute | solution.py:542
  36.1 5.9 %collective-permute-start.16 = (bf16[32,1280]{1,0:T(8,128)(2,1)S(1)}, bf16[32,1280]{1,0:T(8,128)(2,1)S(1)}, u32[]{:S(2)}, u32[]{:S(2)}) collective-permute-start(bf16[32,1280]{1,0:T(8,128)(2,1)S(1)} %get-tuple-element.112), channel_id=1, source_target_pairs={{0,8},{4,12},{8,0},{12,4},{16,24},{20,28},{24,16},{28,20},{1,9},{5... | collective-permute-start | bytes 245768 | tf_op jit(solution)/shard_map/ppermute | solution.py:542
  37.9 4.2 %collective-permute-start.20 = (bf16[32,768]{1,0:T(8,128)(2,1)S(1)}, bf16[32,768]{1,0:T(8,128)(2,1)S(1)}, u32[]{:S(2)}, u32[]{:S(2)}) collective-permute-start(bf16[32,768]{1,0:T(8,128)(2,1)S(1)} %get-tuple-element.118), channel_id=1, source_target_pairs={{0,1},{1,0},{2,3},{3,2},{4,5},{5,4},{6,7},{7,6},{8,9},{9,8},{10,11... | collective-permute-start | bytes 147464 | tf_op jit(solution)/shard_map/ppermute | solution.py:542
  42.1 7.4 %collective-permute-start.24 = (bf16[32,2048]{1,0:T(8,128)(2,1)S(1)}, bf16[32,2048]{1,0:T(8,128)(2,1)S(1)}, u32[]{:S(2)}, u32[]{:S(2)}) collective-permute-start(bf16[32,2048]{1,0:T(8,128)(2,1)S(1)} %join_terms.1.kept_ref), channel_id=1, source_target_pairs={{0,2},{1,3},{2,0},{3,1},{4,6},{5,7},{6,4},{7,5},{8,10},{9,11},{10,... | collective-permute-start | bytes 393224 | tf_op jit(solution)/shard_map/ppermute | solution.py:542
  45.2 6.0 %collective-permute-start.21 = (bf16[128,512]{1,0:T(8,128)(2,1)S(1)}, bf16[128,512]{1,0:T(8,128)(2,1)S(1)}, u32[]{:S(2)}, u32[]{:S(2)}) collective-permute-start(bf16[128,512]{1,0:T(8,128)(2,1)S(1)} %get-tuple-element.120), channel_id=1, source_target_pairs={{0,24},{4,28},{8,16},{12,20},{16,8},{20,12},{24,0},{28,4},{1,25},{... | collective-permute-start | bytes 393224 | tf_op jit(solution)/shard_map/ppermute | solution.py:542
  46.0 6.4 %collective-permute-start.22 = (bf16[128,512]{1,0:T(8,128)(2,1)S(1)}, bf16[128,512]{1,0:T(8,128)(2,1)S(1)}, u32[]{:S(2)}, u32[]{:S(2)}) collective-permute-start(bf16[128,512]{1,0:T(8,128)(2,1)S(1)} %get-tuple-element.121), channel_id=1, source_target_pairs={{0,16},{4,20},{8,24},{12,28},{16,0},{20,4},{24,8},{28,12},{1,17},{... | collective-permute-start | bytes 393224 | tf_op jit(solution)/shard_map/ppermute | solution.py:542
  47.8 5.0 %collective-permute-start.23 = (bf16[128,512]{1,0:T(8,128)(2,1)S(1)}, bf16[128,512]{1,0:T(8,128)(2,1)S(1)}, u32[]{:S(2)}, u32[]{:S(2)}) collective-permute-start(bf16[128,512]{1,0:T(8,128)(2,1)S(1)} %get-tuple-element.122), channel_id=1, source_target_pairs={{0,8},{4,12},{8,0},{12,4},{16,24},{20,28},{24,16},{28,20},{1,9},{5... | collective-permute-start | bytes 393224 | tf_op jit(solution)/shard_map/ppermute | solution.py:542
  49.5 5.0 %collective-permute-start.25 = (bf16[32,2048]{1,0:T(8,128)(2,1)S(1)}, bf16[32,2048]{1,0:T(8,128)(2,1)S(1)}, u32[]{:S(2)}, u32[]{:S(2)}) collective-permute-start(bf16[32,2048]{1,0:T(8,128)(2,1)S(1)} %add_pairs.1.held_ref), channel_id=1, source_target_pairs={{0,1},{1,0},{2,3},{3,2},{4,5},{5,4},{6,7},{7,6},{8,9},{9,8},{10,11... | collective-permute-start | bytes 393224 | tf_op jit(solution)/shard_map/ppermute | solution.py:542

commit v18 on v15

--- a/solution.py
+++ b/solution.py
@@ -20,7 +20,7 @@
 ANY = pl.BlockSpec(memory_space=pl.ANY)
 VMEM = pl.BlockSpec(memory_space=pltpu.VMEM)
 HBM = pl.BlockSpec(memory_space=pltpu.HBM)
-CHIP_STEPS = (3, 2, 1)
+CHIP_STEPS = ((3, 2, 1), (3, 1, 2))
 FIRST_PART = 384
 PINNED = pl.BlockSpec(memory_space=pltpu.VMEM)
 shaped = jax.ShapeDtypeStruct
@@ -29,6 +29,11 @@
 def here():
     device = lax.axis_index("seq")
     return device >> 1, device & 1, lax.axis_index("dp")
+
+
+def chip_steps():
+    core = here()[1]
+    return [0] + [jnp.where(core == 0, even, odd) for even, odd in zip(*CHIP_STEPS)]
 
 
 def dot_nn(a, b):
@@ -321,10 +326,12 @@
         )
 
     def row_of(place):
-        step = (4 - (place >> 1)) & 3
-        return ((step ^ chip) << 1) + ((place & 1) ^ core)
-
-    mask = column_mask(2 * (len(CHIP_STEPS) + 1), group, row_of)
+        owner, step = (place & 1) ^ core, 0
+        for i, (even, odd) in enumerate(zip(*CHIP_STEPS)):
+            step = jnp.where(place >> 1 == i + 1, jnp.where(owner == 0, even, odd), step)
+        return ((step ^ chip) << 1) + owner
+
+    mask = column_mask(2 * (len(CHIP_STEPS[0]) + 1), group, row_of)
     term_qkv, term_out = column_part(
         tokens(0, x_ref), tokens(1, cot_ref), mask, gain_ref[...], w_ref, wo_ref, (), grads_ref
     )
@@ -403,7 +410,7 @@
     chip = here()[0]
     count = own_ref.shape[0]
     copies = []
-    for i, (step, back_ref) in enumerate(zip((0, *CHIP_STEPS), (own_ref, got_1, got_2, got_3))):
+    for i, (step, back_ref) in enumerate(zip(chip_steps(), (own_ref, got_1, got_2, got_3))):
         at = pl.ds(pl.multiple_of((chip ^ step) * count, count), count)
         grad_normed = back_ref[...].astype(F32) * gain_ref[...]
         grad = input_grad(base_ref[at, :], normed_ref[at, :], inverse_ref[at, :], grad_normed)
@@ -416,7 +423,7 @@
     chip = here()[0]
     count = off_1.shape[1]
     copies = []
-    for i, (step, target) in enumerate(zip(CHIP_STEPS, (off_1, off_2, off_3))):
+    for i, (step, target) in enumerate(zip(chip_steps()[1:], (off_1, off_2, off_3))):
         at = pl.ds(pl.multiple_of((chip ^ step) * count, count), count)
         for which, source in enumerate((x_any, cot_any)):
             copies.append(
@@ -443,7 +450,7 @@
     chip, cut = here()[0], kept_ref.shape[2]
     first = keep_ref[:, :, :cut].astype(F32) + got_ref[:, :, :cut].astype(F32)
     send_ref[...], kept_ref[...] = split_rows(first, 1)
-    for step, target in zip((0, *CHIP_STEPS), targets):
+    for step, target in zip(chip_steps(), targets):
         there = chip ^ step
         total = keep_ref[there, :, cut:].astype(F32) + got_ref[there, :, cut:].astype(F32)
         target[...] = total.astype(target.dtype)
@@ -451,7 +458,7 @@
 
 def pair_kernel(kept_ref, got_ref, row_kept, row_got, *targets):
     chip, cut = here()[0], kept_ref.shape[2]
-    for step, target in zip((0, *CHIP_STEPS), targets):
+    for step, target in zip(chip_steps(), targets):
         there = chip ^ step
         total = kept_ref[there] + got_ref[there].astype(F32)
         target[:, :cut] = total.astype(target.dtype)
@@ -535,7 +542,11 @@
 
 
 def cross_chips(*offs):
-    return [swap(off, "seq", 2 * step) for off, step in zip(offs, CHIP_STEPS)]
+    count = lax.axis_size("seq")
+    return [
+        lax.ppermute(off, "seq", [(d, d ^ 2 * steps[d & 1]) for d in range(count)])
+        for off, steps in zip(offs, zip(*CHIP_STEPS))
+    ]
 
 
 def add_two(kept, got, name):

time: 54.5 us -> 56 us (1.028)
  starting transfers between devices: 24.5 us -> 25.5 us
  waiting for transfers between devices: 13.8 us -> 14.4 us
    ppermute x0 -> x12, starting transfers between devices: none -> 15.2 us  [cross_chips(): lax.ppermute(off, 'seq', [(d, d ^ 2 * steps[d & 1]) for d in range(count)])]
    ppermute x23 -> x11, starting transfers between devices: 24.5 us -> 10.3 us  [swap(): return lax.ppermute(array, axis, [(i, i ^ bits) for i in range(count)])]
    ppermute x0 -> x12, waiting for transfers between devices: none -> 6.12 us  [cross_chips(): lax.ppermute(off, 'seq', [(d, d ^ 2 * steps[d & 1]) for d in range(count)])]
    ppermute x23 -> x11, waiting for transfers between devices: 13.8 us -> 8.3 us  [swap(): return lax.ppermute(array, axis, [(i, i ^ bits) for i in range(count)])]
  transfers between devices with their start and end apart: 23 -> 23, of which waited for: 12 -> 13; matrix products, arithmetic and copies ran while one was open for 0% -> 0% of each run, Pallas kernels for 18% -> 18%
where the time goes in v18:
time: 56 us; the launch traced here: 55.9 us
  starting transfers between devices  25.5 us (46%)
  Pallas kernels  15.2 us (27%)
  waiting for transfers between devices  14.4 us (26%)
  between operations  0.73 us (1%)
    pallas_call x15, Pallas kernels, call(): pl.pallas_call(kernel, out_shape=outs, in_specs=[spec for spec, _ in ins]...  15.2 us
    ppermute x12, starting transfers between devices, cross_chips(): lax.ppermute(off, 'seq', [(d, d ^ 2 * steps[d & 1]) for d in range(count)])  15.2 us
    ppermute x11, starting transfers between devices, swap(): return lax.ppermute(array, axis, [(i, i ^ bits) for i in range(count)])  10.3 us
    ppermute x11, waiting for transfers between devices, swap(): return lax.ppermute(array, axis, [(i, i ^ bits) for i in range(count)])  8.3 us
    ppermute x12, waiting for transfers between devices, cross_chips(): lax.ppermute(off, 'seq', [(d, d ^ 2 * steps[d & 1]) for d in range(count)])  6.12 us
  transfers between devices with their start and end apart: 23, of which 13 were waited for; matrix products, arithmetic and copies ran while one was open for 0% of the time, Pallas kernels for 18%

profile of v18, /device:TPU:0, one launch (start us, length us, event | category | flops | bytes accessed | tf_op | source)
XLA Modules:
  0.0 55.9 jit_solution(14341527559786221307)
XLA Ops:
  0.6 1.3 %pack_columns.1 = (bf16[2,128,512]{2,1,0:T(8,128)(2,1)S(1)}, bf16[2,128,512]{2,1,0:T(8,128)(2,1)S(1)}, bf16[2,128,512]{2,1,0:T(8,128)(2,1)S(1)}) custom-call(bf16[512,512]{1,0:T(8,128)(2,1)} %bitcast.9, bf16[512,512]{1,0:T(8,128)(2,1)} %bitcast.11), custom_call_target="tpu_custom_call" | custom-call | tf_op jit(solution)/shard_map/pack_columns/pallas_call | solution.py:527
  1.9 3.0 %collective-permute-start.3 = (bf16[2,128,512]{2,1,0:T(8,128)(2,1)S(1)}, bf16[2,128,512]{2,1,0:T(8,128)(2,1)S(1)}, u32[]{:S(2)}, u32[]{:S(2)}) collective-permute-start(bf16[2,128,512]{2,1,0:T(8,128)(2,1)S(1)} %get-tuple-element.77), channel_id=1, source_target_pairs={{0,16},{4,12},{8,24},{12,4},{16,0},{20,28},{24,8},{28,20},{1,17},{... | collective-permute-start | bytes 786440 | tf_op jit(solution)/shard_map/ppermute | solution.py:547
  4.9 1.5 %collective-permute-start.4 = (bf16[2,128,512]{2,1,0:T(8,128)(2,1)S(1)}, bf16[2,128,512]{2,1,0:T(8,128)(2,1)S(1)}, u32[]{:S(2)}, u32[]{:S(2)}) collective-permute-start(bf16[2,128,512]{2,1,0:T(8,128)(2,1)S(1)} %get-tuple-element.78), channel_id=1, source_target_pairs={{0,8},{4,20},{8,0},{12,28},{16,24},{20,4},{24,16},{28,12},{1,9},{5... | collective-permute-start | bytes 786440 | tf_op jit(solution)/shard_map/ppermute | solution.py:547
  6.4 0.0 collective-permute-start.2
  6.5 7.7 %row_heads.1 = (bf16[4,64,384]{2,1,0:T(8,128)(2,1)S(1)}, bf16[4,64,384]{2,1,0:T(8,128)(2,1)S(1)}, bf16[4,64,384]{2,1,0:T(8,128)(2,1)S(1)}, bf16[4,64,384]{2,1,0:...) custom-call(bf16[512,512]{1,0:T(8,128)(2,1)} %bitcast.10, ...), custom_call_target="tpu_custom_call" | custom-call | tf_op jit(solution)/shard_map/row_heads/pallas_call | solution.py:527
  14.1 3.0 %collective-permute-done.3.near_2 = bf16[2,128,512]{2,1,0:T(8,128)(2,1)S(1)} collective-permute-done((bf16[2,128,512]{2,1,0:T(8,128)(2,1)S(1)}, bf16[2,128,512]{2,1,0:T(8,128)(2,1)S(1)}, u32[]{:S(2)}, u32[]{:S(2)}) %collective-permute-start.3) | collective-permute-done | bytes 262176 | tf_op jit(solution)/shard_map/ppermute | solution.py:547
  17.2 0.3 collective-permute-start.5
  17.5 0.2 collective-permute-start
  17.8 0.3 collective-permute-start.1
  18.1 0.3 collective-permute-start.6
  18.4 0.9 %collective-permute-done.got_1 = bf16[4,64,384]{2,1,0:T(8,128)(2,1)S(1)} collective-permute-done((bf16[4,64,384]{2,1,0:T(8,128)(2,1)S(1)}, bf16[4,64,384]{2,1,0:T(8,128)(2,1)S(1)}, u32[]{:S(2)}, u32[]{:S(2)}) %collective-permute-start) | collective-permute-done | bytes 196640 | tf_op jit(solution)/shard_map/ppermute | solution.py:541
  19.3 0.3 collective-permute-done.1.got_2
  19.6 0.1 row_add_cores.1
  19.7 0.1 collective-permute-done.6.last_ref
  19.8 0.0 collective-permute-done.5.far_ref
  19.8 3.1 %column_heads.1 = (bf16[4,64,1280]{2,1,0:T(8,128)(2,1)S(1)}, bf16[4,64,1280]{2,1,0:T(8,128)(2,1)S(1)}, bf16[512,768]{1,0:T(8,128)(2,1)S(1)}) custom-call(bf16[512,512]{1,0:T(8,128)(2,1)S(1)} %get-tuple-element.75.x_ref, bf16[512,512]{1,0:T(8,128)(2,1)S(1)} %get-tuple-element.76.cot_ref, bf16[2,128,512]{2,1,0:T(8,128)(2,1)S(1)} %collective-permute-done.2.near_1, ...), custom_call_target="tpu_custom_call" | custom-call | tf_op jit(solution)/shard_map/column_heads/pallas_call | solution.py:527
  22.9 0.3 collective-permute-start.8
  23.2 0.6 %column_grad_hidden.1 = (bf16[4,64,512]{2,1,0:T(8,128)(2,1)S(1)}, bf16[4,64,512]{2,1,0:T(8,128)(2,1)S(1)}) custom-call(bf16[512,768]{1,0:T(8,128)(2,1)S(1)} %get-tuple-element.84.grads_ref, bf16[512,768]{1,0:T(8,128)(2,1)S(1)} %get-tuple-element.80.w_ref), custom_call_target="tpu_custom_call" | custom-call | tf_op jit(solution)/shard_map/column_grad_hidden/pallas_call | solution.py:527
  23.8 0.3 collective-permute-start.7
  24.1 2.2 %collective-permute-start.10 = (bf16[4,32,768]{2,1,0:T(8,128)(2,1)S(1)}, bf16[4,32,768]{2,1,0:T(8,128)(2,1)S(1)}, u32[]{:S(2)}, u32[]{:S(2)}) collective-permute-start(bf16[4,32,768]{2,1,0:T(8,128)(2,1)S(1)} %get-tuple-element.102), channel_id=1, source_target_pairs={{0,1},{1,0},{2,3},{3,2},{4,5},{5,4},{6,7},{7,6},{8,9},{9,8},{10,11... | collective-permute-start | bytes 589832 | tf_op jit(solution)/shard_map/ppermute | solution.py:541
  26.4 0.2 column_add_cores.1
  26.5 2.0 %collective-permute-start.14 = (bf16[64,896]{1,0:T(8,128)(2,1)S(1)}, bf16[64,896]{1,0:T(8,128)(2,1)S(1)}, u32[]{:S(2)}, u32[]{:S(2)}) collective-permute-start(bf16[64,896]{1,0:T(8,128)(2,1)S(1)} %get-tuple-element.108), channel_id=1, source_target_pairs={{0,24},{4,28},{8,16},{12,20},{16,8},{20,12},{24,0},{28,4},{1,25},{... | collective-permute-start | bytes 344072 | tf_op jit(solution)/shard_map/ppermute | solution.py:547
  28.5 0.9 %collective-permute-start.9 = (bf16[4,32,384]{2,1,0:T(8,128)(2,1)S(1)}, bf16[4,32,384]{2,1,0:T(8,128)(2,1)S(1)}, u32[]{:S(2)}, u32[]{:S(2)}) collective-permute-start(bf16[4,32,384]{2,1,0:T(8,128)(2,1)S(1)} %get-tuple-element.99), channel_id=1, source_target_pairs={{0,1},{1,0},{2,3},{3,2},{4,5},{5,4},{6,7},{7,6},{8,9},{9,8},{10,11... | collective-permute-start | bytes 294920 | tf_op jit(solution)/shard_map/ppermute | solution.py:541
  29.5 0.1 collective-permute-start.15
  29.5 1.5 %collective-permute-start.16 = (bf16[64,896]{1,0:T(8,128)(2,1)S(1)}, bf16[64,896]{1,0:T(8,128)(2,1)S(1)}, u32[]{:S(2)}, u32[]{:S(2)}) collective-permute-start(bf16[64,896]{1,0:T(8,128)(2,1)S(1)} %get-tuple-element.110), channel_id=1, source_target_pairs={{0,8},{4,20},{8,0},{12,28},{16,24},{20,4},{24,16},{28,12},{1,9},{5... | collective-permute-start | bytes 344072 | tf_op jit(solution)/shard_map/ppermute | solution.py:547
  31.1 1.0 %collective-permute-done.10.row_got = bf16[4,32,768]{2,1,0:T(8,128)(2,1)S(1)} collective-permute-done((bf16[4,32,768]{2,1,0:T(8,128)(2,1)S(1)}, bf16[4,32,768]{2,1,0:T(8,128)(2,1)S(1)}, u32[]{:S(2)}, u32[]{:S(2)}) %collective-permute-start.10) | collective-permute-done | bytes 196640 | tf_op jit(solution)/shard_map/ppermute | solution.py:541
  32.1 1.8 %collective-permute-done.9.got_ref = bf16[4,32,384]{2,1,0:T(8,128)(2,1)S(1)} collective-permute-done((bf16[4,32,384]{2,1,0:T(8,128)(2,1)S(1)}, bf16[4,32,384]{2,1,0:T(8,128)(2,1)S(1)}, u32[]{:S(2)}, u32[]{:S(2)}) %collective-permute-start.9) | collective-permute-done | bytes 98336 | tf_op jit(solution)/shard_map/ppermute | solution.py:541
  33.9 0.1 first_add_pair.1
  33.9 2.0 %collective-permute-start.11 = (bf16[32,1152]{1,0:T(8,128)(2,1)S(1)}, bf16[32,1152]{1,0:T(8,128)(2,1)S(1)}, u32[]{:S(2)}, u32[]{:S(2)}) collective-permute-start(bf16[32,1152]{1,0:T(8,128)(2,1)S(1)} %get-tuple-element.104), channel_id=1, source_target_pairs={{0,24},{4,28},{8,16},{12,20},{16,8},{20,12},{24,0},{28,4},{1,25},{... | collective-permute-start | bytes 221192 | tf_op jit(solution)/shard_map/ppermute | solution.py:547
  35.9 0.2 collective-permute-start.12
  36.1 1.4 %collective-permute-start.13 = (bf16[32,1152]{1,0:T(8,128)(2,1)S(1)}, bf16[32,1152]{1,0:T(8,128)(2,1)S(1)}, u32[]{:S(2)}, u32[]{:S(2)}) collective-permute-start(bf16[32,1152]{1,0:T(8,128)(2,1)S(1)} %get-tuple-element.106), channel_id=1, source_target_pairs={{0,8},{4,20},{8,0},{12,28},{16,24},{20,4},{24,16},{28,12},{1,9},{5... | collective-permute-start | bytes 221192 | tf_op jit(solution)/shard_map/ppermute | solution.py:547
  37.5 0.1 second_add_chips.1
  37.6 1.8 %collective-permute-start.17 = (bf16[32,896]{1,0:T(8,128)(2,1)S(1)}, bf16[32,896]{1,0:T(8,128)(2,1)S(1)}, u32[]{:S(2)}, u32[]{:S(2)}) collective-permute-start(bf16[32,896]{1,0:T(8,128)(2,1)S(1)} %get-tuple-element.112), channel_id=1, source_target_pairs={{0,1},{1,0},{2,3},{3,2},{4,5},{5,4},{6,7},{7,6},{8,9},{9,8},{10,11... | collective-permute-start | bytes 172040 | tf_op jit(solution)/shard_map/ppermute | solution.py:541
  39.4 0.3 collective-permute-done.11.got_1
  39.7 1.2 %collective-permute-done.12.got_2 = bf16[32,1152]{1,0:T(8,128)(2,1)S(1)} collective-permute-done((bf16[32,1152]{1,0:T(8,128)(2,1)S(1)}, bf16[32,1152]{1,0:T(8,128)(2,1)S(1)}, u32[]{:S(2)}, u32[]{:S(2)}) %collective-permute-start.12) | collective-permute-done | bytes 73760 | tf_op jit(solution)/shard_map/ppermute | solution.py:547
  40.9 0.9 %collective-permute-done.17.got_ref = bf16[32,896]{1,0:T(8,128)(2,1)S(1)} collective-permute-done((bf16[32,896]{1,0:T(8,128)(2,1)S(1)}, bf16[32,896]{1,0:T(8,128)(2,1)S(1)}, u32[]{:S(2)}, u32[]{:S(2)}) %collective-permute-start.17) | collective-permute-done | bytes 57376 | tf_op jit(solution)/shard_map/ppermute | solution.py:541
  41.8 0.1 join_terms.1.kept_ref
  41.9 2.8 %collective-permute-start.21 = (bf16[32,2048]{1,0:T(8,128)(2,1)S(1)}, bf16[32,2048]{1,0:T(8,128)(2,1)S(1)}, u32[]{:S(2)}, u32[]{:S(2)}) collective-permute-start(bf16[32,2048]{1,0:T(8,128)(2,1)S(1)} %join_terms.1.kept_ref), channel_id=1, source_target_pairs={{0,2},{1,3},{2,0},{3,1},{4,6},{5,7},{6,4},{7,5},{8,10},{9,11},{10,... | collective-permute-start | bytes 393224 | tf_op jit(solution)/shard_map/ppermute | solution.py:541
  44.7 1.7 %collective-permute-start.18 = (bf16[128,512]{1,0:T(8,128)(2,1)S(1)}, bf16[128,512]{1,0:T(8,128)(2,1)S(1)}, u32[]{:S(2)}, u32[]{:S(2)}) collective-permute-start(bf16[128,512]{1,0:T(8,128)(2,1)S(1)} %get-tuple-element.114), channel_id=1, source_target_pairs={{0,24},{4,28},{8,16},{12,20},{16,8},{20,12},{24,0},{28,4},{1,25},{... | collective-permute-start | bytes 393224 | tf_op jit(solution)/shard_map/ppermute | solution.py:547
  46.4 0.2 collective-permute-start.19
  46.6 1.6 %collective-permute-start.20 = (bf16[128,512]{1,0:T(8,128)(2,1)S(1)}, bf16[128,512]{1,0:T(8,128)(2,1)S(1)}, u32[]{:S(2)}, u32[]{:S(2)}) collective-permute-start(bf16[128,512]{1,0:T(8,128)(2,1)S(1)} %get-tuple-element.116), channel_id=1, source_target_pairs={{0,8},{4,20},{8,0},{12,28},{16,24},{20,4},{24,16},{28,12},{1,9},{5... | collective-permute-start | bytes 393224 | tf_op jit(solution)/shard_map/ppermute | solution.py:547
  48.2 1.7 %collective-permute-done.21.got_ref = bf16[32,2048]{1,0:T(8,128)(2,1)S(1)} collective-permute-done((bf16[32,2048]{1,0:T(8,128)(2,1)S(1)}, bf16[32,2048]{1,0:T(8,128)(2,1)S(1)}, u32[]{:S(2)}, u32[]{:S(2)}) %collective-permute-start.21) | collective-permute-done | bytes 131104 | tf_op jit(solution)/shard_map/ppermute | solution.py:541
  50.0 0.8 %collective-permute-start.22 = (bf16[32,2048]{1,0:T(8,128)(2,1)S(1)}, bf16[32,2048]{1,0:T(8,128)(2,1)S(1)}, u32[]{:S(2)}, u32[]{:S(2)}) collective-permute-start(bf16[32,2048]{1,0:T(8,128)(2,1)S(1)} %add_pairs.1.held_ref), channel_id=1, source_target_pairs={{0,1},{1,0},{2,3},{3,2},{4,5},{5,4},{6,7},{7,6},{8,9},{9,8},{10,11... | collective-permute-start | bytes 393224 | tf_op jit(solution)/shard_map/ppermute | solution.py:541
  50.7 0.2 collective-permute-done.18.got_1
  51.0 1.3 %collective-permute-done.19.got_2 = bf16[128,512]{1,0:T(8,128)(2,1)S(1)} collective-permute-done((bf16[128,512]{1,0:T(8,128)(2,1)S(1)}, bf16[128,512]{1,0:T(8,128)(2,1)S(1)}, u32[]{:S(2)}, u32[]{:S(2)}) %collective-permute-start.19) | collective-permute-done | bytes 131104 | tf_op jit(solution)/shard_map/ppermute | solution.py:547
  52.3 1.1 %input_grad.1 = bf16[512,512]{1,0:T(8,128)(2,1)} custom-call(f32[512,512]{1,0:T(8,128)S(1)} %get-tuple-element.65.base_ref, f32[512,512]{1,0:T(8,128)S(1)} %get-tuple-element.66.normed_ref, f32[512,1]{1,0:T(8,128)S(1)} %get-tuple-element.67.inverse_ref, f32[1,512]{1,0:T(1,128)S(1)} %bitcast.7, bf16[128,512]{1,0:T(8,128)(2,1)S(1)} %get-tuple-element.113.own_ref, ...), custom_call_target="tpu_custom_call" | custom-call | tf_op jit(solution)/shard_map/input_grad/pallas_call | solution.py:527
  53.4 1.6 %collective-permute-done.22.got_ref = bf16[32,2048]{1,0:T(8,128)(2,1)S(1)} collective-permute-done((bf16[32,2048]{1,0:T(8,128)(2,1)S(1)}, bf16[32,2048]{1,0:T(8,128)(2,1)S(1)}, u32[]{:S(2)}, u32[]{:S(2)}) %collective-permute-start.22) | collective-permute-done | bytes 131104 | tf_op jit(solution)/shard_map/ppermute | solution.py:541
  55.0 0.9 %result.1 = (f32[64,1536]{1,0:T(8,128)}, f32[64,512]{1,0:T(8,128)}, f32[1,64]{1,0:T(1,128)}) custom-call(bf16[32,2048]{1,0:T(8,128)(2,1)S(1)} %add_pairs.1.held_ref, bf16[32,2048]{1,0:T(8,128)(2,1)S(1)} %collective-permute-done.22.got_ref, bf16[64,1536]{1,0:T(8,128)(2,1)S(1)} %get-tuple-element.118.w_ref, f32[1,512]{1,0:T(1,128)S(1)} %bitcast.8), custom_call_target="tpu_custom_call" | custom-call | tf_op jit(solution)/shard_map/result/pallas_call | solution.py:527
  (15 shorter events, 0.1 us)
Async XLA Ops:
  1.9 15.3 %collective-permute-start.3 = (bf16[2,128,512]{2,1,0:T(8,128)(2,1)S(1)}, bf16[2,128,512]{2,1,0:T(8,128)(2,1)S(1)}, u32[]{:S(2)}, u32[]{:S(2)}) collective-permute-start(bf16[2,128,512]{2,1,0:T(8,128)(2,1)S(1)} %get-tuple-element.77), channel_id=1, source_target_pairs={{0,16},{4,12},{8,24},{12,4},{16,0},{20,28},{24,8},{28,20},{1,17},{... | collective-permute-start | bytes 786440 | tf_op jit(solution)/shard_map/ppermute | solution.py:547
  4.9 12.2 %collective-permute-start.4 = (bf16[2,128,512]{2,1,0:T(8,128)(2,1)S(1)}, bf16[2,128,512]{2,1,0:T(8,128)(2,1)S(1)}, u32[]{:S(2)}, u32[]{:S(2)}) collective-permute-start(bf16[2,128,512]{2,1,0:T(8,128)(2,1)S(1)} %get-tuple-element.78), channel_id=1, source_target_pairs={{0,8},{4,20},{8,0},{12,28},{16,24},{20,4},{24,16},{28,12},{1,9},{5... | collective-permute-start | bytes 786440 | tf_op jit(solution)/shard_map/ppermute | solution.py:547
  6.4 11.6 %collective-permute-start.2 = (bf16[2,128,512]{2,1,0:T(8,128)(2,1)S(1)}, bf16[2,128,512]{2,1,0:T(8,128)(2,1)S(1)}, u32[]{:S(2)}, u32[]{:S(2)}) collective-permute-start(bf16[2,128,512]{2,1,0:T(8,128)(2,1)S(1)} %get-tuple-element.63), channel_id=1, source_target_pairs={{0,24},{4,28},{8,16},{12,20},{16,8},{20,12},{24,0},{28,4},{1,25},{... | collective-permute-start | bytes 786440 | tf_op jit(solution)/shard_map/ppermute | solution.py:547
  17.2 2.6 %copy-start = (f32[512]{0:T(512)S(1)}, f32[512]{0:T(512)}, u32[]{:S(2)}) copy-start(f32[512]{0:T(512)} %param.6) | copy-start | bytes 6148
  17.2 2.5 %collective-permute-start.5 = (bf16[3,2,64,512]{3,2,1,0:T(8,128)(2,1)S(1)}, bf16[3,2,64,512]{3,2,1,0:T(8,128)(2,1)S(1)}, u32[]{:S(2)}, u32[]{:S(2)}) collective-permute-start(bf16[3,2,64,512]{3,2,1,0:T(8,128)(2,1)S(1)} %pack_other_core.1), channel_id=1, source_target_pairs={{0,4},{4,0},{8,12},{12,8},{16,20},{20,16},{24,28},{28,24},{1,5},{5... | collective-permute-start | bytes 1179656 | tf_op jit(solution)/shard_map/ppermute | solution.py:541
  17.5 1.7 %collective-permute-start = (bf16[4,64,384]{2,1,0:T(8,128)(2,1)S(1)}, bf16[4,64,384]{2,1,0:T(8,128)(2,1)S(1)}, u32[]{:S(2)}, u32[]{:S(2)}) collective-permute-start(bf16[4,64,384]{2,1,0:T(8,128)(2,1)S(1)} %get-tuple-element.71), channel_id=1, source_target_pairs={{0,4},{4,0},{8,12},{12,8},{16,20},{20,16},{24,28},{28,24},{1,5},{5... | collective-permute-start | bytes 589832 | tf_op jit(solution)/shard_map/ppermute | solution.py:541
  17.8 1.8 %collective-permute-start.1 = (bf16[4,64,384]{2,1,0:T(8,128)(2,1)S(1)}, bf16[4,64,384]{2,1,0:T(8,128)(2,1)S(1)}, u32[]{:S(2)}, u32[]{:S(2)}) collective-permute-start(bf16[4,64,384]{2,1,0:T(8,128)(2,1)S(1)} %get-tuple-element.72), channel_id=1, source_target_pairs={{0,4},{4,0},{8,12},{12,8},{16,20},{20,16},{24,28},{28,24},{1,5},{5... | collective-permute-start | bytes 589832 | tf_op jit(solution)/shard_map/ppermute | solution.py:541
  18.1 1.7 %collective-permute-start.6 = (bf16[2,64,512]{2,1,0:T(8,128)(2,1)S(1)}, bf16[2,64,512]{2,1,0:T(8,128)(2,1)S(1)}, u32[]{:S(2)}, u32[]{:S(2)}) collective-permute-start(bf16[2,64,512]{2,1,0:T(8,128)(2,1)S(1)} %pack_other_core_last.1), channel_id=1, source_target_pairs={{0,4},{4,0},{8,12},{12,8},{16,20},{20,16},{24,28},{28,24},{1,5},{5... | collective-permute-start | bytes 393224 | tf_op jit(solution)/shard_map/ppermute | solution.py:541
  22.9 3.5 %collective-permute-start.8 = (bf16[4,64,1280]{2,1,0:T(8,128)(2,1)S(1)}, bf16[4,64,1280]{2,1,0:T(8,128)(2,1)S(1)}, u32[]{:S(2)}, u32[]{:S(2)}) collective-permute-start(bf16[4,64,1280]{2,1,0:T(8,128)(2,1)S(1)} %get-tuple-element.97), channel_id=1, source_target_pairs={{0,4},{4,0},{8,12},{12,8},{16,20},{20,16},{24,28},{28,24},{1,5},{5... | collective-permute-start | bytes 1966088 | tf_op jit(solution)/shard_map/ppermute | solution.py:541
  23.8 5.7 %collective-permute-start.7 = (bf16[4,64,512]{2,1,0:T(8,128)(2,1)S(1)}, bf16[4,64,512]{2,1,0:T(8,128)(2,1)S(1)}, u32[]{:S(2)}, u32[]{:S(2)}) collective-permute-start(bf16[4,64,512]{2,1,0:T(8,128)(2,1)S(1)} %get-tuple-element.87), channel_id=1, source_target_pairs={{0,4},{4,0},{8,12},{12,8},{16,20},{20,16},{24,28},{28,24},{1,5},{5... | collective-permute-start | bytes 786440 | tf_op jit(solution)/shard_map/ppermute | solution.py:541
  24.1 8.0 %collective-permute-start.10 = (bf16[4,32,768]{2,1,0:T(8,128)(2,1)S(1)}, bf16[4,32,768]{2,1,0:T(8,128)(2,1)S(1)}, u32[]{:S(2)}, u32[]{:S(2)}) collective-permute-start(bf16[4,32,768]{2,1,0:T(8,128)(2,1)S(1)} %get-tuple-element.102), channel_id=1, source_target_pairs={{0,1},{1,0},{2,3},{3,2},{4,5},{5,4},{6,7},{7,6},{8,9},{9,8},{10,11... | collective-permute-start | bytes 589832 | tf_op jit(solution)/shard_map/ppermute | solution.py:541
  26.5 9.6 %collective-permute-start.14 = (bf16[64,896]{1,0:T(8,128)(2,1)S(1)}, bf16[64,896]{1,0:T(8,128)(2,1)S(1)}, u32[]{:S(2)}, u32[]{:S(2)}) collective-permute-start(bf16[64,896]{1,0:T(8,128)(2,1)S(1)} %get-tuple-element.108), channel_id=1, source_target_pairs={{0,24},{4,28},{8,16},{12,20},{16,8},{20,12},{24,0},{28,4},{1,25},{... | collective-permute-start | bytes 344072 | tf_op jit(solution)/shard_map/ppermute | solution.py:547
  28.5 5.3 %collective-permute-start.9 = (bf16[4,32,384]{2,1,0:T(8,128)(2,1)S(1)}, bf16[4,32,384]{2,1,0:T(8,128)(2,1)S(1)}, u32[]{:S(2)}, u32[]{:S(2)}) collective-permute-start(bf16[4,32,384]{2,1,0:T(8,128)(2,1)S(1)} %get-tuple-element.99), channel_id=1, source_target_pairs={{0,1},{1,0},{2,3},{3,2},{4,5},{5,4},{6,7},{7,6},{8,9},{9,8},{10,11... | collective-permute-start | bytes 294920 | tf_op jit(solution)/shard_map/ppermute | solution.py:541
  29.5 8.0 %collective-permute-start.15 = (bf16[64,896]{1,0:T(8,128)(2,1)S(1)}, bf16[64,896]{1,0:T(8,128)(2,1)S(1)}, u32[]{:S(2)}, u32[]{:S(2)}) collective-permute-start(bf16[64,896]{1,0:T(8,128)(2,1)S(1)} %get-tuple-element.109), channel_id=1, source_target_pairs={{0,16},{4,12},{8,24},{12,4},{16,0},{20,28},{24,8},{28,20},{1,17},{... | collective-permute-start | bytes 344072 | tf_op jit(solution)/shard_map/ppermute | solution.py:547
  29.5 8.0 %collective-permute-start.16 = (bf16[64,896]{1,0:T(8,128)(2,1)S(1)}, bf16[64,896]{1,0:T(8,128)(2,1)S(1)}, u32[]{:S(2)}, u32[]{:S(2)}) collective-permute-start(bf16[64,896]{1,0:T(8,128)(2,1)S(1)} %get-tuple-element.110), channel_id=1, source_target_pairs={{0,8},{4,20},{8,0},{12,28},{16,24},{20,4},{24,16},{28,12},{1,9},{5... | collective-permute-start | bytes 344072 | tf_op jit(solution)/shard_map/ppermute | solution.py:547
  33.9 5.7 %collective-permute-start.11 = (bf16[32,1152]{1,0:T(8,128)(2,1)S(1)}, bf16[32,1152]{1,0:T(8,128)(2,1)S(1)}, u32[]{:S(2)}, u32[]{:S(2)}) collective-permute-start(bf16[32,1152]{1,0:T(8,128)(2,1)S(1)} %get-tuple-element.104), channel_id=1, source_target_pairs={{0,24},{4,28},{8,16},{12,20},{16,8},{20,12},{24,0},{28,4},{1,25},{... | collective-permute-start | bytes 221192 | tf_op jit(solution)/shard_map/ppermute | solution.py:547
  35.9 5.0 %collective-permute-start.12 = (bf16[32,1152]{1,0:T(8,128)(2,1)S(1)}, bf16[32,1152]{1,0:T(8,128)(2,1)S(1)}, u32[]{:S(2)}, u32[]{:S(2)}) collective-permute-start(bf16[32,1152]{1,0:T(8,128)(2,1)S(1)} %get-tuple-element.105), channel_id=1, source_target_pairs={{0,16},{4,12},{8,24},{12,4},{16,0},{20,28},{24,8},{28,20},{1,17},{... | collective-permute-start | bytes 221192 | tf_op jit(solution)/shard_map/ppermute | solution.py:547
  36.1 4.8 %collective-permute-start.13 = (bf16[32,1152]{1,0:T(8,128)(2,1)S(1)}, bf16[32,1152]{1,0:T(8,128)(2,1)S(1)}, u32[]{:S(2)}, u32[]{:S(2)}) collective-permute-start(bf16[32,1152]{1,0:T(8,128)(2,1)S(1)} %get-tuple-element.106), channel_id=1, source_target_pairs={{0,8},{4,20},{8,0},{12,28},{16,24},{20,4},{24,16},{28,12},{1,9},{5... | collective-permute-start | bytes 221192 | tf_op jit(solution)/shard_map/ppermute | solution.py:547
  37.6 4.2 %collective-permute-start.17 = (bf16[32,896]{1,0:T(8,128)(2,1)S(1)}, bf16[32,896]{1,0:T(8,128)(2,1)S(1)}, u32[]{:S(2)}, u32[]{:S(2)}) collective-permute-start(bf16[32,896]{1,0:T(8,128)(2,1)S(1)} %get-tuple-element.112), channel_id=1, source_target_pairs={{0,1},{1,0},{2,3},{3,2},{4,5},{5,4},{6,7},{7,6},{8,9},{9,8},{10,11... | collective-permute-start | bytes 172040 | tf_op jit(solution)/shard_map/ppermute | solution.py:541
  41.9 8.1 %collective-permute-start.21 = (bf16[32,2048]{1,0:T(8,128)(2,1)S(1)}, bf16[32,2048]{1,0:T(8,128)(2,1)S(1)}, u32[]{:S(2)}, u32[]{:S(2)}) collective-permute-start(bf16[32,2048]{1,0:T(8,128)(2,1)S(1)} %join_terms.1.kept_ref), channel_id=1, source_target_pairs={{0,2},{1,3},{2,0},{3,1},{4,6},{5,7},{6,4},{7,5},{8,10},{9,11},{10,... | collective-permute-start | bytes 393224 | tf_op jit(solution)/shard_map/ppermute | solution.py:541
  44.7 6.3 %collective-permute-start.18 = (bf16[128,512]{1,0:T(8,128)(2,1)S(1)}, bf16[128,512]{1,0:T(8,128)(2,1)S(1)}, u32[]{:S(2)}, u32[]{:S(2)}) collective-permute-start(bf16[128,512]{1,0:T(8,128)(2,1)S(1)} %get-tuple-element.114), channel_id=1, source_target_pairs={{0,24},{4,28},{8,16},{12,20},{16,8},{20,12},{24,0},{28,4},{1,25},{... | collective-permute-start | bytes 393224 | tf_op jit(solution)/shard_map/ppermute | solution.py:547
  46.4 5.8 %collective-permute-start.19 = (bf16[128,512]{1,0:T(8,128)(2,1)S(1)}, bf16[128,512]{1,0:T(8,128)(2,1)S(1)}, u32[]{:S(2)}, u32[]{:S(2)}) collective-permute-start(bf16[128,512]{1,0:T(8,128)(2,1)S(1)} %get-tuple-element.115), channel_id=1, source_target_pairs={{0,16},{4,12},{8,24},{12,4},{16,0},{20,28},{24,8},{28,20},{1,17},{... | collective-permute-start | bytes 393224 | tf_op jit(solution)/shard_map/ppermute | solution.py:547
  46.6 5.7 %collective-permute-start.20 = (bf16[128,512]{1,0:T(8,128)(2,1)S(1)}, bf16[128,512]{1,0:T(8,128)(2,1)S(1)}, u32[]{:S(2)}, u32[]{:S(2)}) collective-permute-start(bf16[128,512]{1,0:T(8,128)(2,1)S(1)} %get-tuple-element.116), channel_id=1, source_target_pairs={{0,8},{4,20},{8,0},{12,28},{16,24},{20,4},{24,16},{28,12},{1,9},{5... | collective-permute-start | bytes 393224 | tf_op jit(solution)/shard_map/ppermute | solution.py:547
  50.0 5.0 %collective-permute-start.22 = (bf16[32,2048]{1,0:T(8,128)(2,1)S(1)}, bf16[32,2048]{1,0:T(8,128)(2,1)S(1)}, u32[]{:S(2)}, u32[]{:S(2)}) collective-permute-start(bf16[32,2048]{1,0:T(8,128)(2,1)S(1)} %add_pairs.1.held_ref), channel_id=1, source_target_pairs={{0,1},{1,0},{2,3},{3,2},{4,5},{5,4},{6,7},{7,6},{8,9},{9,8},{10,11... | collective-permute-start | bytes 393224 | tf_op jit(solution)/shard_map/ppermute | solution.py:541

commit v19 on v12

--- a/solution.py
+++ b/solution.py
@@ -20,7 +20,8 @@
 ANY = pl.BlockSpec(memory_space=pl.ANY)
 VMEM = pl.BlockSpec(memory_space=pltpu.VMEM)
 HBM = pl.BlockSpec(memory_space=pltpu.HBM)
-CHIP_STEPS = (3, 2, 1)
+CHIP_STEPS = ((3, 2, 1), (3, 1, 2))
+TERM_STEPS = (3, 2, 1)
 FIRST_PART = 384
 PINNED = pl.BlockSpec(memory_space=pltpu.VMEM)
 shaped = jax.ShapeDtypeStruct
@@ -29,6 +30,11 @@
 def here():
     device = lax.axis_index("seq")
     return device >> 1, device & 1, lax.axis_index("dp")
+
+
+def chip_steps():
+    core = here()[1]
+    return [0] + [jnp.where(core == 0, even, odd) for even, odd in zip(*CHIP_STEPS)]
 
 
 def dot_nn(a, b):
@@ -320,10 +326,12 @@
         )
 
     def row_of(place):
-        step = (4 - (place >> 1)) & 3
-        return ((step ^ chip) << 1) + ((place & 1) ^ core)
-
-    mask = column_mask(2 * (len(CHIP_STEPS) + 1), group, row_of)
+        owner, step = (place & 1) ^ core, 0
+        for i, (even, odd) in enumerate(zip(*CHIP_STEPS)):
+            step = jnp.where(place >> 1 == i + 1, jnp.where(owner == 0, even, odd), step)
+        return ((step ^ chip) << 1) + owner
+
+    mask = column_mask(2 * (len(CHIP_STEPS[0]) + 1), group, row_of)
     term_qkv, term_out = column_part(
         tokens(0, x_ref), tokens(1, cot_ref), mask, gain_ref[...], w_ref, wo_ref, (), grads_ref
     )
@@ -394,7 +402,7 @@
     chip = here()[0]
     count = own_ref.shape[0]
     copies = []
-    for i, (step, back_ref) in enumerate(zip((0, *CHIP_STEPS), (own_ref, got_1, got_2, got_3))):
+    for i, (step, back_ref) in enumerate(zip(chip_steps(), (own_ref, got_1, got_2, got_3))):
         at = pl.ds(pl.multiple_of((chip ^ step) * count, count), count)
         grad_normed = back_ref[...].astype(F32) * gain_ref[...]
         grad = input_grad(base_ref[at, :], normed_ref[at, :], inverse_ref[at, :], grad_normed)
@@ -407,7 +415,7 @@
     chip = here()[0]
     count = off_1.shape[1]
     copies = []
-    for i, (step, target) in enumerate(zip(CHIP_STEPS, (off_1, off_2, off_3))):
+    for i, (step, target) in enumerate(zip(chip_steps()[1:], (off_1, off_2, off_3))):
         at = pl.ds(pl.multiple_of((chip ^ step) * count, count), count)
         for which, source in enumerate((x_any, cot_any)):
             copies.append(
@@ -434,7 +442,7 @@
     chip, cut = here()[0], kept_ref.shape[2]
     first = keep_ref[:, :, :cut].astype(F32) + got_ref[:, :, :cut].astype(F32)
     send_ref[...], kept_ref[...] = split_rows(first, 1)
-    for step, target in zip((0, *CHIP_STEPS), targets):
+    for step, target in zip((0, *TERM_STEPS), targets):
         there = chip ^ step
         total = keep_ref[there, :, cut:].astype(F32) + got_ref[there, :, cut:].astype(F32)
         target[...] = total.astype(target.dtype)
@@ -442,7 +450,7 @@
 
 def pair_kernel(kept_ref, got_ref, row_kept, row_got, *targets):
     chip, cut = here()[0], kept_ref.shape[2]
-    for step, target in zip((0, *CHIP_STEPS), targets):
+    for step, target in zip((0, *TERM_STEPS), targets):
         there = chip ^ step
         total = kept_ref[there] + got_ref[there].astype(F32)
         target[:, :cut] = total.astype(target.dtype)
@@ -525,8 +533,12 @@
     return lax.ppermute(array, axis, [(i, i ^ bits) for i in range(count)])
 
 
-def cross_chips(*offs):
-    return [swap(off, "seq", 2 * step) for off, step in zip(offs, CHIP_STEPS)]
+def cross_chips(offs, by_core=CHIP_STEPS):
+    count = lax.axis_size("seq")
+    return [
+        lax.ppermute(off, "seq", [(d, d ^ 2 * steps[d & 1]) for d in range(count)])
+        for off, steps in zip(offs, zip(*by_core))
+    ]
 
 
 def add_two(kept, got, name):
@@ -563,7 +575,7 @@
             [pltpu.SemaphoreType.DMA((6,))],
             out_specs=[ANY] * 3,
         )
-        near = cross_chips(*packed)
+        near = cross_chips(packed)
         x_first, _ = lax.optimization_barrier((x, packed[0]))
     else:
         outgoing = jnp.stack([x.reshape(n, share, width), cot.reshape(n, share, width)], 1)
@@ -650,7 +662,7 @@
             [(first_half, BF16), (first_half, F32), (second, F32)] + [(second, BF16)] * 3,
             out_specs=[VMEM, PINNED, PINNED, VMEM, VMEM, VMEM],
         )
-        got = cross_chips(*off)
+        got = cross_chips(off, (TERM_STEPS, TERM_STEPS))
         back = call(
             back_pack_kernel,
             "pack_grad_hidden",
@@ -669,7 +681,7 @@
             [(joint, F32)] + [(joint, BF16)] * 3,
             out_specs=[PINNED, VMEM, VMEM, VMEM],
         )
-        first_got = cross_chips(*off)
+        first_got = cross_chips(off, (TERM_STEPS, TERM_STEPS))
         second_half = (row_share // 2, second[1])
         to_next, kept = call(
             layer_kernel,
@@ -692,7 +704,7 @@
             "input_grad",
             [
                 (VMEM, one)
-                for one in (base, normed, inverse_rms, gain, back[0], *cross_chips(*back[1:]))
+                for one in (base, normed, inverse_rms, gain, back[0], *cross_chips(back[1:]))
             ],
             [((columns, width), BF16)],
             [pltpu.VMEM((chips, 2 * share, width), BF16), pltpu.SemaphoreType.DMA((chips,))],

time: 55.1 us -> 55 us (level)
    ppermute x22 -> x10, starting transfers between devices: 24.4 us -> 9.12 us  [swap(): return lax.ppermute(array, axis, [(i, i ^ bits) for i in range(count)])]
    ppermute x0 -> x12, starting transfers between devices: none -> 15.2 us  [cross_chips(): lax.ppermute(off, 'seq', [(d, d ^ 2 * steps[d & 1]) for d in range(count)])]
    ppermute x0 -> x12, waiting for transfers between devices: none -> 4.35 us  [cross_chips(): lax.ppermute(off, 'seq', [(d, d ^ 2 * steps[d & 1]) for d in range(count)])]
    ppermute x22 -> x10, waiting for transfers between devices: 14.5 us -> 10.2 us  [swap(): return lax.ppermute(array, axis, [(i, i ^ bits) for i in range(count)])]
  transfers between devices with their start and end apart: 22 -> 22, of which waited for: 12 -> 13; matrix products, arithmetic and copies ran while one was open for 0% -> 0% of each run, Pallas kernels for 18% -> 18%
where the time goes in v19:
time: 55 us; the launch traced here: 54.9 us
  starting transfers between devices  24.3 us (44%)
  Pallas kernels  15.3 us (28%)
  waiting for transfers between devices  14.6 us (27%)
  between operations  0.74 us (1%)
    pallas_call x14, Pallas kernels, call(): pl.pallas_call(kernel, out_shape=outs, in_specs=[spec for spec, _ in ins]...  15.3 us
    ppermute x12, starting transfers between devices, cross_chips(): lax.ppermute(off, 'seq', [(d, d ^ 2 * steps[d & 1]) for d in range(count)])  15.2 us
    ppermute x10, waiting for transfers between devices, swap(): return lax.ppermute(array, axis, [(i, i ^ bits) for i in range(count)])  10.2 us
    ppermute x10, starting transfers between devices, swap(): return lax.ppermute(array, axis, [(i, i ^ bits) for i in range(count)])  9.12 us
    ppermute x12, waiting for transfers between devices, cross_chips(): lax.ppermute(off, 'seq', [(d, d ^ 2 * steps[d & 1]) for d in range(count)])  4.35 us
  transfers between devices with their start and end apart: 22, of which 13 were waited for; matrix products, arithmetic and copies ran while one was open for 0% of the time, Pallas kernels for 18%

profile of v19, /device:TPU:0, one launch (start us, length us, event | category | flops | bytes accessed | tf_op | source)
XLA Modules:
  0.0 54.9 jit_solution(7830036793329245359)
XLA Ops:
  0.6 1.3 %pack_columns.1 = (bf16[2,128,512]{2,1,0:T(8,128)(2,1)S(1)}, bf16[2,128,512]{2,1,0:T(8,128)(2,1)S(1)}, bf16[2,128,512]{2,1,0:T(8,128)(2,1)S(1)}) custom-call(bf16[512,512]{1,0:T(8,128)(2,1)} %bitcast.9, bf16[512,512]{1,0:T(8,128)(2,1)} %bitcast.11), custom_call_target="tpu_custom_call" | custom-call | tf_op jit(solution)/shard_map/pack_columns/pallas_call | solution.py:519
  1.9 3.0 %collective-permute-start.1 = (bf16[2,128,512]{2,1,0:T(8,128)(2,1)S(1)}, bf16[2,128,512]{2,1,0:T(8,128)(2,1)S(1)}, u32[]{:S(2)}, u32[]{:S(2)}) collective-permute-start(bf16[2,128,512]{2,1,0:T(8,128)(2,1)S(1)} %get-tuple-element.69), channel_id=1, source_target_pairs={{0,16},{4,12},{8,24},{12,4},{16,0},{20,28},{24,8},{28,20},{1,17},{... | collective-permute-start | bytes 786440 | tf_op jit(solution)/shard_map/ppermute | solution.py:539
  4.9 1.5 %collective-permute-start.2 = (bf16[2,128,512]{2,1,0:T(8,128)(2,1)S(1)}, bf16[2,128,512]{2,1,0:T(8,128)(2,1)S(1)}, u32[]{:S(2)}, u32[]{:S(2)}) collective-permute-start(bf16[2,128,512]{2,1,0:T(8,128)(2,1)S(1)} %get-tuple-element.70), channel_id=1, source_target_pairs={{0,8},{4,20},{8,0},{12,28},{16,24},{20,4},{24,16},{28,12},{1,9},{5... | collective-permute-start | bytes 786440 | tf_op jit(solution)/shard_map/ppermute | solution.py:539
  6.4 0.0 collective-permute-start
  6.5 7.7 %row_heads.1 = (bf16[4,64,384]{2,1,0:T(8,128)(2,1)S(1)}, bf16[4,64,384]{2,1,0:T(8,128)(2,1)S(1)}, bf16[4,64,384]{2,1,0:T(8,128)(2,1)S(1)}, bf16[4,64,384]{2,1,0:...) custom-call(bf16[512,512]{1,0:T(8,128)(2,1)} %bitcast.10, ...), custom_call_target="tpu_custom_call" | custom-call | tf_op jit(solution)/shard_map/row_heads/pallas_call | solution.py:519
  14.1 0.1 collective-permute-start.3
  14.2 0.5 collective-permute-start.4
  14.7 0.9 %collective-permute-done.3.got_1 = bf16[4,64,384]{2,1,0:T(8,128)(2,1)S(1)} collective-permute-done((bf16[4,64,384]{2,1,0:T(8,128)(2,1)S(1)}, bf16[4,64,384]{2,1,0:T(8,128)(2,1)S(1)}, u32[]{:S(2)}, u32[]{:S(2)}) %collective-permute-start.3) | collective-permute-done | bytes 196640 | tf_op jit(solution)/shard_map/ppermute | solution.py:533
  15.6 0.3 collective-permute-done.4.got_2
  15.9 0.1 row_add_cores.1
  16.1 1.1 %collective-permute-done.1.near_2 = bf16[2,128,512]{2,1,0:T(8,128)(2,1)S(1)} collective-permute-done((bf16[2,128,512]{2,1,0:T(8,128)(2,1)S(1)}, bf16[2,128,512]{2,1,0:T(8,128)(2,1)S(1)}, u32[]{:S(2)}, u32[]{:S(2)}) %collective-permute-start.1) | collective-permute-done | bytes 262176 | tf_op jit(solution)/shard_map/ppermute | solution.py:539
  17.2 0.0 collective-permute-done.2.near_3
  17.2 0.9 %collective-permute-done.near_1 = bf16[2,128,512]{2,1,0:T(8,128)(2,1)S(1)} collective-permute-done((bf16[2,128,512]{2,1,0:T(8,128)(2,1)S(1)}, bf16[2,128,512]{2,1,0:T(8,128)(2,1)S(1)}, u32[]{:S(2)}, u32[]{:S(2)}) %collective-permute-start) | collective-permute-done | bytes 262176 | tf_op jit(solution)/shard_map/ppermute | solution.py:539
  18.1 0.1 collective-permute-start.5
  18.2 1.9 %collective-permute-done.5.far_ref = bf16[4,2,64,512]{3,2,1,0:T(8,128)(2,1)S(1)} collective-permute-done((bf16[4,2,64,512]{3,2,1,0:T(8,128)(2,1)S(1)}, bf16[4,2,64,512]{3,2,1,0:T(8,128)(2,1)S(1)}, u32[]{:S(2)}, u32[]{:S(2)}) %collective-permute-start.5) | collective-permute-done | bytes 524320 | tf_op jit(solution)/shard_map/ppermute | solution.py:533
  20.1 3.1 %column_heads.1 = (bf16[4,64,1280]{2,1,0:T(8,128)(2,1)S(1)}, bf16[4,64,1280]{2,1,0:T(8,128)(2,1)S(1)}, bf16[512,768]{1,0:T(8,128)(2,1)S(1)}) custom-call(bf16[512,512]{1,0:T(8,128)(2,1)S(1)} %get-tuple-element.77.x_ref, bf16[512,512]{1,0:T(8,128)(2,1)S(1)} %get-tuple-element.78.cot_ref, bf16[2,128,512]{2,1,0:T(8,128)(2,1)S(1)} %collective-permute-done.near_1, ...), custom_call_target="tpu_custom_call" | custom-call | tf_op jit(solution)/shard_map/column_heads/pallas_call | solution.py:519
  23.2 0.2 collective-permute-start.7
  23.4 0.6 %column_grad_hidden.1 = (bf16[4,64,512]{2,1,0:T(8,128)(2,1)S(1)}, bf16[4,64,512]{2,1,0:T(8,128)(2,1)S(1)}) custom-call(bf16[512,768]{1,0:T(8,128)(2,1)S(1)} %get-tuple-element.86.grads_ref, bf16[512,768]{1,0:T(8,128)(2,1)S(1)} %get-tuple-element.82.w_ref), custom_call_target="tpu_custom_call" | custom-call | tf_op jit(solution)/shard_map/column_grad_hidden/pallas_call | solution.py:519
  24.0 0.4 collective-permute-start.6
  24.4 1.7 %collective-permute-start.9 = (bf16[4,32,768]{2,1,0:T(8,128)(2,1)S(1)}, bf16[4,32,768]{2,1,0:T(8,128)(2,1)S(1)}, u32[]{:S(2)}, u32[]{:S(2)}) collective-permute-start(bf16[4,32,768]{2,1,0:T(8,128)(2,1)S(1)} %get-tuple-element.104), channel_id=1, source_target_pairs={{0,1},{1,0},{2,3},{3,2},{4,5},{5,4},{6,7},{7,6},{8,9},{9,8},{10,11... | collective-permute-start | bytes 589832 | tf_op jit(solution)/shard_map/ppermute | solution.py:533
  26.1 0.2 column_add_cores.1
  26.3 1.7 %collective-permute-start.13 = (bf16[64,896]{1,0:T(8,128)(2,1)S(1)}, bf16[64,896]{1,0:T(8,128)(2,1)S(1)}, u32[]{:S(2)}, u32[]{:S(2)}) collective-permute-start(bf16[64,896]{1,0:T(8,128)(2,1)S(1)} %get-tuple-element.110), channel_id=1, source_target_pairs={{0,24},{4,28},{8,16},{12,20},{16,8},{20,12},{24,0},{28,4},{1,25},{... | collective-permute-start | bytes 344072 | tf_op jit(solution)/shard_map/ppermute | solution.py:539
  28.0 0.9 %collective-permute-start.8 = (bf16[4,32,384]{2,1,0:T(8,128)(2,1)S(1)}, bf16[4,32,384]{2,1,0:T(8,128)(2,1)S(1)}, u32[]{:S(2)}, u32[]{:S(2)}) collective-permute-start(bf16[4,32,384]{2,1,0:T(8,128)(2,1)S(1)} %get-tuple-element.101), channel_id=1, source_target_pairs={{0,1},{1,0},{2,3},{3,2},{4,5},{5,4},{6,7},{7,6},{8,9},{9,8},{10,11... | collective-permute-start | bytes 294920 | tf_op jit(solution)/shard_map/ppermute | solution.py:533
  28.9 1.2 %collective-permute-start.14 = (bf16[64,896]{1,0:T(8,128)(2,1)S(1)}, bf16[64,896]{1,0:T(8,128)(2,1)S(1)}, u32[]{:S(2)}, u32[]{:S(2)}) collective-permute-start(bf16[64,896]{1,0:T(8,128)(2,1)S(1)} %get-tuple-element.111), channel_id=1, source_target_pairs={{0,16},{4,20},{8,24},{12,28},{16,0},{20,4},{24,8},{28,12},{1,17},{... | collective-permute-start | bytes 344072 | tf_op jit(solution)/shard_map/ppermute | solution.py:539
  30.1 0.0 collective-permute-done.6.got_ref
  30.1 0.6 %collective-permute-start.15 = (bf16[64,896]{1,0:T(8,128)(2,1)S(1)}, bf16[64,896]{1,0:T(8,128)(2,1)S(1)}, u32[]{:S(2)}, u32[]{:S(2)}) collective-permute-start(bf16[64,896]{1,0:T(8,128)(2,1)S(1)} %get-tuple-element.112), channel_id=1, source_target_pairs={{0,8},{4,12},{8,0},{12,4},{16,24},{20,28},{24,16},{28,20},{1,9},{5... | collective-permute-start | bytes 344072 | tf_op jit(solution)/shard_map/ppermute | solution.py:539
  30.8 1.4 %collective-permute-done.9.row_got = bf16[4,32,768]{2,1,0:T(8,128)(2,1)S(1)} collective-permute-done((bf16[4,32,768]{2,1,0:T(8,128)(2,1)S(1)}, bf16[4,32,768]{2,1,0:T(8,128)(2,1)S(1)}, u32[]{:S(2)}, u32[]{:S(2)}) %collective-permute-start.9) | collective-permute-done | bytes 196640 | tf_op jit(solution)/shard_map/ppermute | solution.py:533
  32.2 1.3 %collective-permute-done.8.got_ref = bf16[4,32,384]{2,1,0:T(8,128)(2,1)S(1)} collective-permute-done((bf16[4,32,384]{2,1,0:T(8,128)(2,1)S(1)}, bf16[4,32,384]{2,1,0:T(8,128)(2,1)S(1)}, u32[]{:S(2)}, u32[]{:S(2)}) %collective-permute-start.8) | collective-permute-done | bytes 98336 | tf_op jit(solution)/shard_map/ppermute | solution.py:533
  33.5 0.1 first_add_pair.1
  33.5 1.8 %collective-permute-start.10 = (bf16[32,1152]{1,0:T(8,128)(2,1)S(1)}, bf16[32,1152]{1,0:T(8,128)(2,1)S(1)}, u32[]{:S(2)}, u32[]{:S(2)}) collective-permute-start(bf16[32,1152]{1,0:T(8,128)(2,1)S(1)} %get-tuple-element.106), channel_id=1, source_target_pairs={{0,24},{4,28},{8,16},{12,20},{16,8},{20,12},{24,0},{28,4},{1,25},{... | collective-permute-start | bytes 221192 | tf_op jit(solution)/shard_map/ppermute | solution.py:539
  35.3 1.2 %collective-permute-start.11 = (bf16[32,1152]{1,0:T(8,128)(2,1)S(1)}, bf16[32,1152]{1,0:T(8,128)(2,1)S(1)}, u32[]{:S(2)}, u32[]{:S(2)}) collective-permute-start(bf16[32,1152]{1,0:T(8,128)(2,1)S(1)} %get-tuple-element.107), channel_id=1, source_target_pairs={{0,16},{4,20},{8,24},{12,28},{16,0},{20,4},{24,8},{28,12},{1,17},{... | collective-permute-start | bytes 221192 | tf_op jit(solution)/shard_map/ppermute | solution.py:539
  36.5 0.5 collective-permute-start.12
  37.1 0.1 second_add_chips.1
  37.2 1.7 %collective-permute-start.16 = (bf16[32,896]{1,0:T(8,128)(2,1)S(1)}, bf16[32,896]{1,0:T(8,128)(2,1)S(1)}, u32[]{:S(2)}, u32[]{:S(2)}) collective-permute-start(bf16[32,896]{1,0:T(8,128)(2,1)S(1)} %get-tuple-element.114), channel_id=1, source_target_pairs={{0,1},{1,0},{2,3},{3,2},{4,5},{5,4},{6,7},{7,6},{8,9},{9,8},{10,11... | collective-permute-start | bytes 172040 | tf_op jit(solution)/shard_map/ppermute | solution.py:533
  38.9 2.5 %collective-permute-done.16.got_ref = bf16[32,896]{1,0:T(8,128)(2,1)S(1)} collective-permute-done((bf16[32,896]{1,0:T(8,128)(2,1)S(1)}, bf16[32,896]{1,0:T(8,128)(2,1)S(1)}, u32[]{:S(2)}, u32[]{:S(2)}) %collective-permute-start.16) | collective-permute-done | bytes 57376 | tf_op jit(solution)/shard_map/ppermute | solution.py:533
  41.4 0.1 join_terms.1.kept_ref
  41.5 2.8 %collective-permute-start.20 = (bf16[32,2048]{1,0:T(8,128)(2,1)S(1)}, bf16[32,2048]{1,0:T(8,128)(2,1)S(1)}, u32[]{:S(2)}, u32[]{:S(2)}) collective-permute-start(bf16[32,2048]{1,0:T(8,128)(2,1)S(1)} %join_terms.1.kept_ref), channel_id=1, source_target_pairs={{0,2},{1,3},{2,0},{3,1},{4,6},{5,7},{6,4},{7,5},{8,10},{9,11},{10,... | collective-permute-start | bytes 393224 | tf_op jit(solution)/shard_map/ppermute | solution.py:533
  44.2 1.6 %collective-permute-start.17 = (bf16[128,512]{1,0:T(8,128)(2,1)S(1)}, bf16[128,512]{1,0:T(8,128)(2,1)S(1)}, u32[]{:S(2)}, u32[]{:S(2)}) collective-permute-start(bf16[128,512]{1,0:T(8,128)(2,1)S(1)} %get-tuple-element.116), channel_id=1, source_target_pairs={{0,24},{4,28},{8,16},{12,20},{16,8},{20,12},{24,0},{28,4},{1,25},{... | collective-permute-start | bytes 393224 | tf_op jit(solution)/shard_map/ppermute | solution.py:539
  45.9 1.2 %collective-permute-start.18 = (bf16[128,512]{1,0:T(8,128)(2,1)S(1)}, bf16[128,512]{1,0:T(8,128)(2,1)S(1)}, u32[]{:S(2)}, u32[]{:S(2)}) collective-permute-start(bf16[128,512]{1,0:T(8,128)(2,1)S(1)} %get-tuple-element.117), channel_id=1, source_target_pairs={{0,16},{4,12},{8,24},{12,4},{16,0},{20,28},{24,8},{28,20},{1,17},{... | collective-permute-start | bytes 393224 | tf_op jit(solution)/shard_map/ppermute | solution.py:539
  47.1 0.6 %collective-permute-start.19 = (bf16[128,512]{1,0:T(8,128)(2,1)S(1)}, bf16[128,512]{1,0:T(8,128)(2,1)S(1)}, u32[]{:S(2)}, u32[]{:S(2)}) collective-permute-start(bf16[128,512]{1,0:T(8,128)(2,1)S(1)} %get-tuple-element.118), channel_id=1, source_target_pairs={{0,8},{4,20},{8,0},{12,28},{16,24},{20,4},{24,16},{28,12},{1,9},{5... | collective-permute-start | bytes 393224 | tf_op jit(solution)/shard_map/ppermute | solution.py:539
  47.7 1.2 %collective-permute-done.20.got_ref = bf16[32,2048]{1,0:T(8,128)(2,1)S(1)} collective-permute-done((bf16[32,2048]{1,0:T(8,128)(2,1)S(1)}, bf16[32,2048]{1,0:T(8,128)(2,1)S(1)}, u32[]{:S(2)}, u32[]{:S(2)}) %collective-permute-start.20) | collective-permute-done | bytes 131104 | tf_op jit(solution)/shard_map/ppermute | solution.py:533
  49.0 0.7 %collective-permute-start.21 = (bf16[32,2048]{1,0:T(8,128)(2,1)S(1)}, bf16[32,2048]{1,0:T(8,128)(2,1)S(1)}, u32[]{:S(2)}, u32[]{:S(2)}) collective-permute-start(bf16[32,2048]{1,0:T(8,128)(2,1)S(1)} %add_pairs.1.held_ref), channel_id=1, source_target_pairs={{0,1},{1,0},{2,3},{3,2},{4,5},{5,4},{6,7},{7,6},{8,9},{9,8},{10,11... | collective-permute-start | bytes 393224 | tf_op jit(solution)/shard_map/ppermute | solution.py:533
  49.7 0.5 collective-permute-done.17.got_1
  50.2 1.3 %collective-permute-done.18.got_2 = bf16[128,512]{1,0:T(8,128)(2,1)S(1)} collective-permute-done((bf16[128,512]{1,0:T(8,128)(2,1)S(1)}, bf16[128,512]{1,0:T(8,128)(2,1)S(1)}, u32[]{:S(2)}, u32[]{:S(2)}) %collective-permute-start.18) | collective-permute-done | bytes 131104 | tf_op jit(solution)/shard_map/ppermute | solution.py:539
  51.5 0.5 collective-permute-done.19.got_3
  52.1 1.2 %input_grad.1 = bf16[512,512]{1,0:T(8,128)(2,1)} custom-call(f32[512,512]{1,0:T(8,128)S(1)} %get-tuple-element.66.base_ref, f32[512,512]{1,0:T(8,128)S(1)} %get-tuple-element.67.normed_ref, f32[512,1]{1,0:T(8,128)S(1)} %get-tuple-element.68.inverse_ref, f32[1,512]{1,0:T(1,128)S(1)} %bitcast.7, bf16[128,512]{1,0:T(8,128)(2,1)S(1)} %get-tuple-element.115.own_ref, ...), custom_call_target="tpu_custom_call" | custom-call | tf_op jit(solution)/shard_map/input_grad/pallas_call | solution.py:519
  53.2 0.8 %collective-permute-done.21.got_ref = bf16[32,2048]{1,0:T(8,128)(2,1)S(1)} collective-permute-done((bf16[32,2048]{1,0:T(8,128)(2,1)S(1)}, bf16[32,2048]{1,0:T(8,128)(2,1)S(1)}, u32[]{:S(2)}, u32[]{:S(2)}) %collective-permute-start.21) | collective-permute-done | bytes 131104 | tf_op jit(solution)/shard_map/ppermute | solution.py:533
  54.0 0.9 %result.1 = (f32[64,1536]{1,0:T(8,128)}, f32[64,512]{1,0:T(8,128)}, f32[1,64]{1,0:T(1,128)}) custom-call(bf16[32,2048]{1,0:T(8,128)(2,1)S(1)} %add_pairs.1.held_ref, bf16[32,2048]{1,0:T(8,128)(2,1)S(1)} %collective-permute-done.21.got_ref, bf16[64,1536]{1,0:T(8,128)(2,1)S(1)} %get-tuple-element.120.w_ref, f32[1,512]{1,0:T(1,128)S(1)} %bitcast.8), custom_call_target="tpu_custom_call" | custom-call | tf_op jit(solution)/shard_map/result/pallas_call | solution.py:519
  (12 shorter events, 0.1 us)
Async XLA Ops:
  1.9 15.3 %collective-permute-start.1 = (bf16[2,128,512]{2,1,0:T(8,128)(2,1)S(1)}, bf16[2,128,512]{2,1,0:T(8,128)(2,1)S(1)}, u32[]{:S(2)}, u32[]{:S(2)}) collective-permute-start(bf16[2,128,512]{2,1,0:T(8,128)(2,1)S(1)} %get-tuple-element.69), channel_id=1, source_target_pairs={{0,16},{4,12},{8,24},{12,4},{16,0},{20,28},{24,8},{28,20},{1,17},{... | collective-permute-start | bytes 786440 | tf_op jit(solution)/shard_map/ppermute | solution.py:539
  4.9 12.2 %collective-permute-start.2 = (bf16[2,128,512]{2,1,0:T(8,128)(2,1)S(1)}, bf16[2,128,512]{2,1,0:T(8,128)(2,1)S(1)}, u32[]{:S(2)}, u32[]{:S(2)}) collective-permute-start(bf16[2,128,512]{2,1,0:T(8,128)(2,1)S(1)} %get-tuple-element.70), channel_id=1, source_target_pairs={{0,8},{4,20},{8,0},{12,28},{16,24},{20,4},{24,16},{28,12},{1,9},{5... | collective-permute-start | bytes 786440 | tf_op jit(solution)/shard_map/ppermute | solution.py:539
  6.4 11.6 %collective-permute-start = (bf16[2,128,512]{2,1,0:T(8,128)(2,1)S(1)}, bf16[2,128,512]{2,1,0:T(8,128)(2,1)S(1)}, u32[]{:S(2)}, u32[]{:S(2)}) collective-permute-start(bf16[2,128,512]{2,1,0:T(8,128)(2,1)S(1)} %get-tuple-element.64), channel_id=1, source_target_pairs={{0,24},{4,28},{8,16},{12,20},{16,8},{20,12},{24,0},{28,4},{1,25},{... | collective-permute-start | bytes 786440 | tf_op jit(solution)/shard_map/ppermute | solution.py:539
  14.1 1.5 %collective-permute-start.3 = (bf16[4,64,384]{2,1,0:T(8,128)(2,1)S(1)}, bf16[4,64,384]{2,1,0:T(8,128)(2,1)S(1)}, u32[]{:S(2)}, u32[]{:S(2)}) collective-permute-start(bf16[4,64,384]{2,1,0:T(8,128)(2,1)S(1)} %get-tuple-element.73), channel_id=1, source_target_pairs={{0,4},{4,0},{8,12},{12,8},{16,20},{20,16},{24,28},{28,24},{1,5},{5... | collective-permute-start | bytes 589832 | tf_op jit(solution)/shard_map/ppermute | solution.py:533
  14.2 1.7 %collective-permute-start.4 = (bf16[4,64,384]{2,1,0:T(8,128)(2,1)S(1)}, bf16[4,64,384]{2,1,0:T(8,128)(2,1)S(1)}, u32[]{:S(2)}, u32[]{:S(2)}) collective-permute-start(bf16[4,64,384]{2,1,0:T(8,128)(2,1)S(1)} %get-tuple-element.74), channel_id=1, source_target_pairs={{0,4},{4,0},{8,12},{12,8},{16,20},{20,16},{24,28},{28,24},{1,5},{5... | collective-permute-start | bytes 589832 | tf_op jit(solution)/shard_map/ppermute | solution.py:533
  15.9 4.1 %copy-start = (f32[512]{0:T(512)S(1)}, f32[512]{0:T(512)}, u32[]{:S(2)}) copy-start(f32[512]{0:T(512)} %param.6) | copy-start | bytes 6148
  18.1 2.0 %collective-permute-start.5 = (bf16[4,2,64,512]{3,2,1,0:T(8,128)(2,1)S(1)}, bf16[4,2,64,512]{3,2,1,0:T(8,128)(2,1)S(1)}, u32[]{:S(2)}, u32[]{:S(2)}) collective-permute-start(bf16[4,2,64,512]{3,2,1,0:T(8,128)(2,1)S(1)} %pack_other_core.1), channel_id=1, source_target_pairs={{0,4},{4,0},{8,12},{12,8},{16,20},{20,16},{24,28},{28,24},{1,5},{5... | collective-permute-start | bytes 1572872 | tf_op jit(solution)/shard_map/ppermute | solution.py:533
  23.2 2.9 %collective-permute-start.7 = (bf16[4,64,1280]{2,1,0:T(8,128)(2,1)S(1)}, bf16[4,64,1280]{2,1,0:T(8,128)(2,1)S(1)}, u32[]{:S(2)}, u32[]{:S(2)}) collective-permute-start(bf16[4,64,1280]{2,1,0:T(8,128)(2,1)S(1)} %get-tuple-element.99), channel_id=1, source_target_pairs={{0,4},{4,0},{8,12},{12,8},{16,20},{20,16},{24,28},{28,24},{1,5},{5... | collective-permute-start | bytes 1966088 | tf_op jit(solution)/shard_map/ppermute | solution.py:533
  24.0 6.1 %collective-permute-start.6 = (bf16[4,64,512]{2,1,0:T(8,128)(2,1)S(1)}, bf16[4,64,512]{2,1,0:T(8,128)(2,1)S(1)}, u32[]{:S(2)}, u32[]{:S(2)}) collective-permute-start(bf16[4,64,512]{2,1,0:T(8,128)(2,1)S(1)} %get-tuple-element.89), channel_id=1, source_target_pairs={{0,4},{4,0},{8,12},{12,8},{16,20},{20,16},{24,28},{28,24},{1,5},{5... | collective-permute-start | bytes 786440 | tf_op jit(solution)/shard_map/ppermute | solution.py:533
  24.4 7.7 %collective-permute-start.9 = (bf16[4,32,768]{2,1,0:T(8,128)(2,1)S(1)}, bf16[4,32,768]{2,1,0:T(8,128)(2,1)S(1)}, u32[]{:S(2)}, u32[]{:S(2)}) collective-permute-start(bf16[4,32,768]{2,1,0:T(8,128)(2,1)S(1)} %get-tuple-element.104), channel_id=1, source_target_pairs={{0,1},{1,0},{2,3},{3,2},{4,5},{5,4},{6,7},{7,6},{8,9},{9,8},{10,11... | collective-permute-start | bytes 589832 | tf_op jit(solution)/shard_map/ppermute | solution.py:533
  26.3 10.3 %collective-permute-start.13 = (bf16[64,896]{1,0:T(8,128)(2,1)S(1)}, bf16[64,896]{1,0:T(8,128)(2,1)S(1)}, u32[]{:S(2)}, u32[]{:S(2)}) collective-permute-start(bf16[64,896]{1,0:T(8,128)(2,1)S(1)} %get-tuple-element.110), channel_id=1, source_target_pairs={{0,24},{4,28},{8,16},{12,20},{16,8},{20,12},{24,0},{28,4},{1,25},{... | collective-permute-start | bytes 344072 | tf_op jit(solution)/shard_map/ppermute | solution.py:539
  28.0 5.5 %collective-permute-start.8 = (bf16[4,32,384]{2,1,0:T(8,128)(2,1)S(1)}, bf16[4,32,384]{2,1,0:T(8,128)(2,1)S(1)}, u32[]{:S(2)}, u32[]{:S(2)}) collective-permute-start(bf16[4,32,384]{2,1,0:T(8,128)(2,1)S(1)} %get-tuple-element.101), channel_id=1, source_target_pairs={{0,1},{1,0},{2,3},{3,2},{4,5},{5,4},{6,7},{7,6},{8,9},{9,8},{10,11... | collective-permute-start | bytes 294920 | tf_op jit(solution)/shard_map/ppermute | solution.py:533
  28.9 8.2 %collective-permute-start.14 = (bf16[64,896]{1,0:T(8,128)(2,1)S(1)}, bf16[64,896]{1,0:T(8,128)(2,1)S(1)}, u32[]{:S(2)}, u32[]{:S(2)}) collective-permute-start(bf16[64,896]{1,0:T(8,128)(2,1)S(1)} %get-tuple-element.111), channel_id=1, source_target_pairs={{0,16},{4,20},{8,24},{12,28},{16,0},{20,4},{24,8},{28,12},{1,17},{... | collective-permute-start | bytes 344072 | tf_op jit(solution)/shard_map/ppermute | solution.py:539
  30.1 7.0 %collective-permute-start.15 = (bf16[64,896]{1,0:T(8,128)(2,1)S(1)}, bf16[64,896]{1,0:T(8,128)(2,1)S(1)}, u32[]{:S(2)}, u32[]{:S(2)}) collective-permute-start(bf16[64,896]{1,0:T(8,128)(2,1)S(1)} %get-tuple-element.112), channel_id=1, source_target_pairs={{0,8},{4,12},{8,0},{12,4},{16,24},{20,28},{24,16},{28,20},{1,9},{5... | collective-permute-start | bytes 344072 | tf_op jit(solution)/shard_map/ppermute | solution.py:539
  33.5 7.9 %collective-permute-start.10 = (bf16[32,1152]{1,0:T(8,128)(2,1)S(1)}, bf16[32,1152]{1,0:T(8,128)(2,1)S(1)}, u32[]{:S(2)}, u32[]{:S(2)}) collective-permute-start(bf16[32,1152]{1,0:T(8,128)(2,1)S(1)} %get-tuple-element.106), channel_id=1, source_target_pairs={{0,24},{4,28},{8,16},{12,20},{16,8},{20,12},{24,0},{28,4},{1,25},{... | collective-permute-start | bytes 221192 | tf_op jit(solution)/shard_map/ppermute | solution.py:539
  35.3 6.1 %collective-permute-start.11 = (bf16[32,1152]{1,0:T(8,128)(2,1)S(1)}, bf16[32,1152]{1,0:T(8,128)(2,1)S(1)}, u32[]{:S(2)}, u32[]{:S(2)}) collective-permute-start(bf16[32,1152]{1,0:T(8,128)(2,1)S(1)} %get-tuple-element.107), channel_id=1, source_target_pairs={{0,16},{4,20},{8,24},{12,28},{16,0},{20,4},{24,8},{28,12},{1,17},{... | collective-permute-start | bytes 221192 | tf_op jit(solution)/shard_map/ppermute | solution.py:539
  36.5 4.9 %collective-permute-start.12 = (bf16[32,1152]{1,0:T(8,128)(2,1)S(1)}, bf16[32,1152]{1,0:T(8,128)(2,1)S(1)}, u32[]{:S(2)}, u32[]{:S(2)}) collective-permute-start(bf16[32,1152]{1,0:T(8,128)(2,1)S(1)} %get-tuple-element.108), channel_id=1, source_target_pairs={{0,8},{4,12},{8,0},{12,4},{16,24},{20,28},{24,16},{28,20},{1,9},{5... | collective-permute-start | bytes 221192 | tf_op jit(solution)/shard_map/ppermute | solution.py:539
  37.2 4.2 %collective-permute-start.16 = (bf16[32,896]{1,0:T(8,128)(2,1)S(1)}, bf16[32,896]{1,0:T(8,128)(2,1)S(1)}, u32[]{:S(2)}, u32[]{:S(2)}) collective-permute-start(bf16[32,896]{1,0:T(8,128)(2,1)S(1)} %get-tuple-element.114), channel_id=1, source_target_pairs={{0,1},{1,0},{2,3},{3,2},{4,5},{5,4},{6,7},{7,6},{8,9},{9,8},{10,11... | collective-permute-start | bytes 172040 | tf_op jit(solution)/shard_map/ppermute | solution.py:533
  41.5 7.4 %collective-permute-start.20 = (bf16[32,2048]{1,0:T(8,128)(2,1)S(1)}, bf16[32,2048]{1,0:T(8,128)(2,1)S(1)}, u32[]{:S(2)}, u32[]{:S(2)}) collective-permute-start(bf16[32,2048]{1,0:T(8,128)(2,1)S(1)} %join_terms.1.kept_ref), channel_id=1, source_target_pairs={{0,2},{1,3},{2,0},{3,1},{4,6},{5,7},{6,4},{7,5},{8,10},{9,11},{10,... | collective-permute-start | bytes 393224 | tf_op jit(solution)/shard_map/ppermute | solution.py:533
  44.2 5.9 %collective-permute-start.17 = (bf16[128,512]{1,0:T(8,128)(2,1)S(1)}, bf16[128,512]{1,0:T(8,128)(2,1)S(1)}, u32[]{:S(2)}, u32[]{:S(2)}) collective-permute-start(bf16[128,512]{1,0:T(8,128)(2,1)S(1)} %get-tuple-element.116), channel_id=1, source_target_pairs={{0,24},{4,28},{8,16},{12,20},{16,8},{20,12},{24,0},{28,4},{1,25},{... | collective-permute-start | bytes 393224 | tf_op jit(solution)/shard_map/ppermute | solution.py:539
  45.9 5.6 %collective-permute-start.18 = (bf16[128,512]{1,0:T(8,128)(2,1)S(1)}, bf16[128,512]{1,0:T(8,128)(2,1)S(1)}, u32[]{:S(2)}, u32[]{:S(2)}) collective-permute-start(bf16[128,512]{1,0:T(8,128)(2,1)S(1)} %get-tuple-element.117), channel_id=1, source_target_pairs={{0,16},{4,12},{8,24},{12,4},{16,0},{20,28},{24,8},{28,20},{1,17},{... | collective-permute-start | bytes 393224 | tf_op jit(solution)/shard_map/ppermute | solution.py:539
  47.1 5.0 %collective-permute-start.19 = (bf16[128,512]{1,0:T(8,128)(2,1)S(1)}, bf16[128,512]{1,0:T(8,128)(2,1)S(1)}, u32[]{:S(2)}, u32[]{:S(2)}) collective-permute-start(bf16[128,512]{1,0:T(8,128)(2,1)S(1)} %get-tuple-element.118), channel_id=1, source_target_pairs={{0,8},{4,20},{8,0},{12,28},{16,24},{20,4},{24,16},{28,12},{1,9},{5... | collective-permute-start | bytes 393224 | tf_op jit(solution)/shard_map/ppermute | solution.py:539
  49.0 5.0 %collective-permute-start.21 = (bf16[32,2048]{1,0:T(8,128)(2,1)S(1)}, bf16[32,2048]{1,0:T(8,128)(2,1)S(1)}, u32[]{:S(2)}, u32[]{:S(2)}) collective-permute-start(bf16[32,2048]{1,0:T(8,128)(2,1)S(1)} %add_pairs.1.held_ref), channel_id=1, source_target_pairs={{0,1},{1,0},{2,3},{3,2},{4,5},{5,4},{6,7},{7,6},{8,9},{9,8},{10,11... | collective-permute-start | bytes 393224 | tf_op jit(solution)/shard_map/ppermute | solution.py:533

commit v20 on v12

--- a/solution.py
+++ b/solution.py
@@ -301,7 +301,7 @@
 
 
 def column_chip_kernel(
-    x_ref, cot_ref, near_1, near_2, near_3, far_ref, gain_ref, w_ref, wo_ref, row_out_ref,
+    x_ref, cot_ref, swapped_ref, corner_ref, near_2, near_3, far_ref, gain_ref, w_ref, wo_ref, row_out_ref,
     send_ref, keep_ref, grads_ref,
 ):
     chip, core, _ = here()
@@ -311,9 +311,11 @@
     group = math.gcd(share, 16)
 
     def tokens(which, mine):
-        pieces = [mine[at, :], far_ref[0, which]]
-        for i, near in enumerate((near_1, near_2, near_3)):
-            pieces += [near[which, half, :], far_ref[i + 1, which]]
+        pieces = [
+            mine[at, :], swapped_ref[0, which], corner_ref[0, which], corner_ref[1, which],
+        ]
+        for i, near in enumerate((near_2, near_3)):
+            pieces += [near[which, half, :], far_ref[i, which]]
         starts = range(0, share, group)
         return jnp.concatenate(
             [piece[start : start + group] for start in starts for piece in pieces], 0
@@ -335,14 +337,11 @@
     split_cores(term_out, *refs, slice(chips // 2, chips), out_lanes)
 
 
-def far_kernel(x_ref, cot_ref, near_1, near_2, near_3, far_ref):
-    chip, core, _ = here()
+def far_kernel(near_2, near_3, far_ref):
     share = far_ref.shape[2]
-    at = pl.ds(pl.multiple_of((chip * 2 + 1 - core) * share, share), share)
-    far_ref[0, 0], far_ref[0, 1] = x_ref[at, :], cot_ref[at, :]
-    at = pl.ds(pl.multiple_of((1 - core) * share, share), share)
-    for i, near in enumerate((near_1, near_2, near_3)):
-        far_ref[i + 1] = near[:, at, :]
+    at = pl.ds(pl.multiple_of((1 - here()[1]) * share, share), share)
+    for i, near in enumerate((near_2, near_3)):
+        far_ref[i] = near[:, at, :]
 
 
 def back_kernel(grads_ref, w_ref, back_ref):
@@ -403,17 +402,34 @@
     finished(*copies)
 
 
-def pack_kernel(x_any, cot_any, off_1, off_2, off_3, sems):
-    chip = here()[0]
-    count = off_1.shape[1]
+def pack_kernel(x_any, cot_any, swap_ref, corner_ref, off_2, off_3, sems):
+    chip, core, _ = here()
+    share = corner_ref.shape[1]
+
+    def columns(step, of_core):
+        return pl.multiple_of(((chip ^ step) * 2 + of_core) * share, share)
+
+    corner = CHIP_STEPS[0]
     copies = []
-    for i, (step, target) in enumerate(zip(CHIP_STEPS, (off_1, off_2, off_3))):
-        at = pl.ds(pl.multiple_of((chip ^ step) * count, count), count)
-        for which, source in enumerate((x_any, cot_any)):
+    for which, source in enumerate((x_any, cot_any)):
+        pieces = [
+            (columns(0, 1 - core), share, swap_ref.at[0, which]),
+            (columns(corner, 1 - core), share, swap_ref.at[1, which]),
+            (columns(corner, core), share, corner_ref.at[which]),
+            (columns(CHIP_STEPS[1], 0), 2 * share, off_2.at[which]),
+            (columns(CHIP_STEPS[2], 0), 2 * share, off_3.at[which]),
+        ]
+        for i, (at, count, target) in enumerate(pieces):
             copies.append(
-                pltpu.make_async_copy(source.at[at, :], target.at[which], sems.at[2 * i + which])
+                pltpu.make_async_copy(
+                    source.at[pl.ds(at, count), :], target, sems.at[5 * which + i]
+                )
             )
     finished(*started(*copies))
+
+
+def corner_kernel(corner_ref, swapped_ref, out_ref):
+    out_ref[0], out_ref[1] = corner_ref[...], swapped_ref[1]
 
 
 def split_rows(total, axis):
@@ -559,12 +575,21 @@
             pack_kernel,
             "pack_columns",
             [(HBM, x), (HBM, cot)],
-            [((2, 2 * share, width), BF16)] * 3,
-            [pltpu.SemaphoreType.DMA((6,))],
-            out_specs=[ANY] * 3,
-        )
-        near = cross_chips(*packed)
-        x_first, _ = lax.optimization_barrier((x, packed[0]))
+            [((2, 2, share, width), BF16), ((2, share, width), BF16)]
+            + [((2, 2 * share, width), BF16)] * 2,
+            [pltpu.SemaphoreType.DMA((10,))],
+            out_specs=[ANY] * 4,
+        )
+        near = [swap(one, "seq", 2 * step) for one, step in zip(packed[2:], CHIP_STEPS[1:])]
+        swapped = swap(packed[0], "seq", 1)
+        (corner,) = call(
+            corner_kernel,
+            "pack_corner",
+            [(VMEM, packed[1]), (VMEM, swapped)],
+            [((2, 2, share, width), BF16)],
+        )
+        x_first, _ = lax.optimization_barrier((x, corner))
+        corner = swap(corner, "seq", 2 * CHIP_STEPS[0])
     else:
         outgoing = jnp.stack([x.reshape(n, share, width), cot.reshape(n, share, width)], 1)
         moved = lax.all_to_all(outgoing, "seq", split_axis=0, concat_axis=0, tiled=True)
@@ -612,12 +637,13 @@
             [(half_block, BF16), (half_block, F32)],
             out_specs=[VMEM, PINNED],
         )
-        *near, row_kept = lax.optimization_barrier((*near, row_kept))
+        col_weight, row_kept = lax.optimization_barrier((col_weight, row_kept))
+        *near, base = lax.optimization_barrier((*near, base))
         (far,) = call(
             far_kernel,
             "pack_other_core",
-            [(VMEM, one) for one in (x_near, cot_near, *near)],
-            [((chips, 2, share, width), BF16)],
+            [(VMEM, one) for one in near],
+            [((2, 2, share, width), BF16)],
         )
         send, keep, col_grads = call(
             column_chip_kernel,
@@ -625,7 +651,7 @@
             [
                 (VMEM, one)
                 for one in (
-                    x_near, cot_near, *near, swap(far, "seq", 1),
+                    x_near, cot_near, swapped, corner, *near, swap(far, "seq", 1),
                     gain, col_weight, col_out_weight, row_out,
                 )
             ],

time: 55.1 us -> 53.8 us (0.976)
  waiting for transfers between devices: 14.5 us -> 12.2 us
  starting transfers between devices: 24.4 us -> 25.4 us
    ppermute x22 -> x23, waiting for transfers between devices: 14.5 us -> 12.2 us  [swap(): return lax.ppermute(array, axis, [(i, i ^ bits) for i in range(count)])]
    ppermute x22 -> x23, starting transfers between devices: 24.4 us -> 25.4 us  [swap(): return lax.ppermute(array, axis, [(i, i ^ bits) for i in range(count)])]
    pallas_call x14 -> x15, Pallas kernels: 15.2 us -> 15.3 us  [call(): pl.pallas_call(kernel, out_shape=outs, in_specs=[spec for spec, _ in ins]...]
  transfers between devices with their start and end apart: 22 -> 23, of which waited for: 12 -> 13; matrix products, arithmetic and copies ran while one was open for 0% -> 0% of each run, Pallas kernels for 18% -> 19%
where the time goes in v20:
time: 53.8 us; the launch traced here: 53.7 us
  starting transfers between devices  25.4 us (47%)
  Pallas kernels  15.3 us (28%)
  waiting for transfers between devices  12.2 us (23%)
  between operations  0.77 us (1%)
    ppermute x23, starting transfers between devices, swap(): return lax.ppermute(array, axis, [(i, i ^ bits) for i in range(count)])  25.4 us
    pallas_call x15, Pallas kernels, call(): pl.pallas_call(kernel, out_shape=outs, in_specs=[spec for spec, _ in ins]...  15.3 us
    ppermute x23, waiting for transfers between devices, swap(): return lax.ppermute(array, axis, [(i, i ^ bits) for i in range(count)])  12.2 us
  transfers between devices with their start and end apart: 23, of which 13 were waited for; matrix products, arithmetic and copies ran while one was open for 0% of the time, Pallas kernels for 19%

profile of v20, /device:TPU:0, one launch (start us, length us, event | category | flops | bytes accessed | tf_op | source)
XLA Modules:
  0.0 53.7 jit_solution(7972873157399846729)
XLA Ops:
  0.6 1.4 %pack_columns.1 = (bf16[2,2,64,512]{3,2,1,0:T(8,128)(2,1)S(1)}, bf16[2,64,512]{2,1,0:T(8,128)(2,1)S(1)}, bf16[2,128,512]{2,1,0:T(8,128)(2,1)S(1)}, bf16[2,128,512]{2,1,0:T(8,128)(2,1)S(1)}) custom-call(bf16[512,512]{1,0:T(8,128)(2,1)} %bitcast.9, bf16[512,512]{1,0:T(8,128)(2,1)} %bitcast.11), custom_call_target="tpu_custom_call" | custom-call | tf_op jit(solution)/shard_map/pack_columns/pallas_call | solution.py:527
  2.0 0.5 collective-permute-start.2
  2.5 2.6 %collective-permute-start = (bf16[2,128,512]{2,1,0:T(8,128)(2,1)S(1)}, bf16[2,128,512]{2,1,0:T(8,128)(2,1)S(1)}, u32[]{:S(2)}, u32[]{:S(2)}) collective-permute-start(bf16[2,128,512]{2,1,0:T(8,128)(2,1)S(1)} %get-tuple-element.66), channel_id=1, source_target_pairs={{0,16},{4,20},{8,24},{12,28},{16,0},{20,4},{24,8},{28,12},{1,17},{... | collective-permute-start | bytes 786440 | tf_op jit(solution)/shard_map/ppermute | solution.py:541
  5.1 1.5 %collective-permute-start.1 = (bf16[2,128,512]{2,1,0:T(8,128)(2,1)S(1)}, bf16[2,128,512]{2,1,0:T(8,128)(2,1)S(1)}, u32[]{:S(2)}, u32[]{:S(2)}) collective-permute-start(bf16[2,128,512]{2,1,0:T(8,128)(2,1)S(1)} %get-tuple-element.67), channel_id=1, source_target_pairs={{0,8},{4,12},{8,0},{12,4},{16,24},{20,28},{24,16},{28,20},{1,9},{5... | collective-permute-start | bytes 786440 | tf_op jit(solution)/shard_map/ppermute | solution.py:541
  6.6 1.0 %collective-permute-start.5 = (bf16[2,2,64,512]{3,2,1,0:T(8,128)(2,1)S(1)}, bf16[2,2,64,512]{3,2,1,0:T(8,128)(2,1)S(1)}, u32[]{:S(2)}, u32[]{:S(2)}) collective-permute-start(bf16[2,2,64,512]{3,2,1,0:T(8,128)(2,1)S(1)} %pack_corner.1), channel_id=1, source_target_pairs={{0,24},{4,28},{8,16},{12,20},{16,8},{20,12},{24,0},{28,4},{1,25},{... | collective-permute-start | bytes 786440 | tf_op jit(solution)/shard_map/ppermute | solution.py:541
  7.6 7.6 %row_heads.1 = (bf16[4,64,384]{2,1,0:T(8,128)(2,1)S(1)}, bf16[4,64,384]{2,1,0:T(8,128)(2,1)S(1)}, bf16[4,64,384]{2,1,0:T(8,128)(2,1)S(1)}, bf16[4,64,384]{2,1,0:...) custom-call(bf16[512,512]{1,0:T(8,128)(2,1)} %bitcast.10, ...), custom_call_target="tpu_custom_call" | custom-call | tf_op jit(solution)/shard_map/row_heads/pallas_call | solution.py:527
  15.3 0.1 collective-permute-start.6
  15.4 0.5 collective-permute-start.3
  15.9 0.1 collective-permute-start.4
  16.0 1.2 %collective-permute-done.3.got_1 = bf16[4,64,384]{2,1,0:T(8,128)(2,1)S(1)} collective-permute-done((bf16[4,64,384]{2,1,0:T(8,128)(2,1)S(1)}, bf16[4,64,384]{2,1,0:T(8,128)(2,1)S(1)}, u32[]{:S(2)}, u32[]{:S(2)}) %collective-permute-start.3) | collective-permute-done | bytes 196640 | tf_op jit(solution)/shard_map/ppermute | solution.py:541
  17.2 0.3 collective-permute-done.4.got_2
  17.5 0.1 row_add_cores.1
  17.6 1.2 %collective-permute-done.5.corner_ref = bf16[2,2,64,512]{3,2,1,0:T(8,128)(2,1)S(1)} collective-permute-done((bf16[2,2,64,512]{3,2,1,0:T(8,128)(2,1)S(1)}, bf16[2,2,64,512]{3,2,1,0:T(8,128)(2,1)S(1)}, u32[]{:S(2)}, u32[]{:S(2)}) %collective-permute-start.5) | collective-permute-done | bytes 262176 | tf_op jit(solution)/shard_map/ppermute | solution.py:541
  18.8 3.1 %column_heads.1 = (bf16[4,64,1280]{2,1,0:T(8,128)(2,1)S(1)}, bf16[4,64,1280]{2,1,0:T(8,128)(2,1)S(1)}, bf16[512,768]{1,0:T(8,128)(2,1)S(1)}) custom-call(bf16[512,512]{1,0:T(8,128)(2,1)S(1)} %get-tuple-element.82.x_ref, bf16[512,512]{1,0:T(8,128)(2,1)S(1)} %get-tuple-element.83.cot_ref, bf16[2,2,64,512]{3,2,1,0:T(8,128)(2,1)S(1)} %collective-permute-done.2.swapped_ref, ...), custom_call_target="tpu_custom_call" | custom-call | tf_op jit(solution)/shard_map/column_heads/pallas_call | solution.py:527
  21.9 0.1 collective-permute-start.8
  22.0 0.6 %column_grad_hidden.1 = (bf16[4,64,512]{2,1,0:T(8,128)(2,1)S(1)}, bf16[4,64,512]{2,1,0:T(8,128)(2,1)S(1)}) custom-call(bf16[512,768]{1,0:T(8,128)(2,1)S(1)} %get-tuple-element.90.grads_ref, bf16[512,768]{1,0:T(8,128)(2,1)S(1)} %get-tuple-element.86.w_ref), custom_call_target="tpu_custom_call" | custom-call | tf_op jit(solution)/shard_map/column_grad_hidden/pallas_call | solution.py:527
  22.6 0.6 %collective-permute-start.7 = (bf16[4,64,512]{2,1,0:T(8,128)(2,1)S(1)}, bf16[4,64,512]{2,1,0:T(8,128)(2,1)S(1)}, u32[]{:S(2)}, u32[]{:S(2)}) collective-permute-start(bf16[4,64,512]{2,1,0:T(8,128)(2,1)S(1)} %get-tuple-element.93), channel_id=1, source_target_pairs={{0,4},{4,0},{8,12},{12,8},{16,20},{20,16},{24,28},{28,24},{1,5},{5... | collective-permute-start | bytes 786440 | tf_op jit(solution)/shard_map/ppermute | solution.py:541
  23.2 1.8 %collective-permute-start.10 = (bf16[4,32,768]{2,1,0:T(8,128)(2,1)S(1)}, bf16[4,32,768]{2,1,0:T(8,128)(2,1)S(1)}, u32[]{:S(2)}, u32[]{:S(2)}) collective-permute-start(bf16[4,32,768]{2,1,0:T(8,128)(2,1)S(1)} %get-tuple-element.108), channel_id=1, source_target_pairs={{0,1},{1,0},{2,3},{3,2},{4,5},{5,4},{6,7},{7,6},{8,9},{9,8},{10,11... | collective-permute-start | bytes 589832 | tf_op jit(solution)/shard_map/ppermute | solution.py:541
  25.0 0.2 column_add_cores.1
  25.1 2.5 %collective-permute-start.14 = (bf16[64,896]{1,0:T(8,128)(2,1)S(1)}, bf16[64,896]{1,0:T(8,128)(2,1)S(1)}, u32[]{:S(2)}, u32[]{:S(2)}) collective-permute-start(bf16[64,896]{1,0:T(8,128)(2,1)S(1)} %get-tuple-element.114), channel_id=1, source_target_pairs={{0,24},{4,28},{8,16},{12,20},{16,8},{20,12},{24,0},{28,4},{1,25},{... | collective-permute-start | bytes 344072 | tf_op jit(solution)/shard_map/ppermute | solution.py:541
  27.7 0.9 %collective-permute-start.9 = (bf16[4,32,384]{2,1,0:T(8,128)(2,1)S(1)}, bf16[4,32,384]{2,1,0:T(8,128)(2,1)S(1)}, u32[]{:S(2)}, u32[]{:S(2)}) collective-permute-start(bf16[4,32,384]{2,1,0:T(8,128)(2,1)S(1)} %get-tuple-element.105), channel_id=1, source_target_pairs={{0,1},{1,0},{2,3},{3,2},{4,5},{5,4},{6,7},{7,6},{8,9},{9,8},{10,11... | collective-permute-start | bytes 294920 | tf_op jit(solution)/shard_map/ppermute | solution.py:541
  28.6 0.5 collective-permute-start.15
  29.1 0.5 collective-permute-start.16
  29.7 0.7 %collective-permute-done.10.row_got = bf16[4,32,768]{2,1,0:T(8,128)(2,1)S(1)} collective-permute-done((bf16[4,32,768]{2,1,0:T(8,128)(2,1)S(1)}, bf16[4,32,768]{2,1,0:T(8,128)(2,1)S(1)}, u32[]{:S(2)}, u32[]{:S(2)}) %collective-permute-start.10) | collective-permute-done | bytes 196640 | tf_op jit(solution)/shard_map/ppermute | solution.py:541
  30.4 1.9 %collective-permute-done.9.got_ref = bf16[4,32,384]{2,1,0:T(8,128)(2,1)S(1)} collective-permute-done((bf16[4,32,384]{2,1,0:T(8,128)(2,1)S(1)}, bf16[4,32,384]{2,1,0:T(8,128)(2,1)S(1)}, u32[]{:S(2)}, u32[]{:S(2)}) %collective-permute-start.9) | collective-permute-done | bytes 98336 | tf_op jit(solution)/shard_map/ppermute | solution.py:541
  32.3 0.1 first_add_pair.1
  32.3 2.6 %collective-permute-start.11 = (bf16[32,1152]{1,0:T(8,128)(2,1)S(1)}, bf16[32,1152]{1,0:T(8,128)(2,1)S(1)}, u32[]{:S(2)}, u32[]{:S(2)}) collective-permute-start(bf16[32,1152]{1,0:T(8,128)(2,1)S(1)} %get-tuple-element.110), channel_id=1, source_target_pairs={{0,24},{4,28},{8,16},{12,20},{16,8},{20,12},{24,0},{28,4},{1,25},{... | collective-permute-start | bytes 221192 | tf_op jit(solution)/shard_map/ppermute | solution.py:541
  35.0 0.5 collective-permute-start.12
  35.5 0.4 collective-permute-start.13
  35.9 0.1 second_add_chips.1
  36.0 1.7 %collective-permute-start.17 = (bf16[32,896]{1,0:T(8,128)(2,1)S(1)}, bf16[32,896]{1,0:T(8,128)(2,1)S(1)}, u32[]{:S(2)}, u32[]{:S(2)}) collective-permute-start(bf16[32,896]{1,0:T(8,128)(2,1)S(1)} %get-tuple-element.118), channel_id=1, source_target_pairs={{0,1},{1,0},{2,3},{3,2},{4,5},{5,4},{6,7},{7,6},{8,9},{9,8},{10,11... | collective-permute-start | bytes 172040 | tf_op jit(solution)/shard_map/ppermute | solution.py:541
  37.7 0.0 collective-permute-done.11.got_1
  37.8 1.6 %collective-permute-done.12.got_2 = bf16[32,1152]{1,0:T(8,128)(2,1)S(1)} collective-permute-done((bf16[32,1152]{1,0:T(8,128)(2,1)S(1)}, bf16[32,1152]{1,0:T(8,128)(2,1)S(1)}, u32[]{:S(2)}, u32[]{:S(2)}) %collective-permute-start.12) | collective-permute-done | bytes 73760 | tf_op jit(solution)/shard_map/ppermute | solution.py:541
  39.3 0.5 collective-permute-done.13.got_3
  39.8 0.4 collective-permute-done.17.got_ref
  40.2 0.1 join_terms.1.kept_ref
  40.3 2.8 %collective-permute-start.21 = (bf16[32,2048]{1,0:T(8,128)(2,1)S(1)}, bf16[32,2048]{1,0:T(8,128)(2,1)S(1)}, u32[]{:S(2)}, u32[]{:S(2)}) collective-permute-start(bf16[32,2048]{1,0:T(8,128)(2,1)S(1)} %join_terms.1.kept_ref), channel_id=1, source_target_pairs={{0,2},{1,3},{2,0},{3,1},{4,6},{5,7},{6,4},{7,5},{8,10},{9,11},{10,... | collective-permute-start | bytes 393224 | tf_op jit(solution)/shard_map/ppermute | solution.py:541
  43.0 2.4 %collective-permute-start.18 = (bf16[128,512]{1,0:T(8,128)(2,1)S(1)}, bf16[128,512]{1,0:T(8,128)(2,1)S(1)}, u32[]{:S(2)}, u32[]{:S(2)}) collective-permute-start(bf16[128,512]{1,0:T(8,128)(2,1)S(1)} %get-tuple-element.120), channel_id=1, source_target_pairs={{0,24},{4,28},{8,16},{12,20},{16,8},{20,12},{24,0},{28,4},{1,25},{... | collective-permute-start | bytes 393224 | tf_op jit(solution)/shard_map/ppermute | solution.py:541
  45.5 0.5 collective-permute-start.19
  46.0 0.5 %collective-permute-start.20 = (bf16[128,512]{1,0:T(8,128)(2,1)S(1)}, bf16[128,512]{1,0:T(8,128)(2,1)S(1)}, u32[]{:S(2)}, u32[]{:S(2)}) collective-permute-start(bf16[128,512]{1,0:T(8,128)(2,1)S(1)} %get-tuple-element.122), channel_id=1, source_target_pairs={{0,8},{4,12},{8,0},{12,4},{16,24},{20,28},{24,16},{28,20},{1,9},{5... | collective-permute-start | bytes 393224 | tf_op jit(solution)/shard_map/ppermute | solution.py:541
  46.5 1.2 %collective-permute-done.21.got_ref = bf16[32,2048]{1,0:T(8,128)(2,1)S(1)} collective-permute-done((bf16[32,2048]{1,0:T(8,128)(2,1)S(1)}, bf16[32,2048]{1,0:T(8,128)(2,1)S(1)}, u32[]{:S(2)}, u32[]{:S(2)}) %collective-permute-start.21) | collective-permute-done | bytes 131104 | tf_op jit(solution)/shard_map/ppermute | solution.py:541
  47.8 0.7 %collective-permute-start.22 = (bf16[32,2048]{1,0:T(8,128)(2,1)S(1)}, bf16[32,2048]{1,0:T(8,128)(2,1)S(1)}, u32[]{:S(2)}, u32[]{:S(2)}) collective-permute-start(bf16[32,2048]{1,0:T(8,128)(2,1)S(1)} %add_pairs.1.held_ref), channel_id=1, source_target_pairs={{0,1},{1,0},{2,3},{3,2},{4,5},{5,4},{6,7},{7,6},{8,9},{9,8},{10,11... | collective-permute-start | bytes 393224 | tf_op jit(solution)/shard_map/ppermute | solution.py:541
  48.5 0.6 %collective-permute-done.18.got_1 = bf16[128,512]{1,0:T(8,128)(2,1)S(1)} collective-permute-done((bf16[128,512]{1,0:T(8,128)(2,1)S(1)}, bf16[128,512]{1,0:T(8,128)(2,1)S(1)}, u32[]{:S(2)}, u32[]{:S(2)}) %collective-permute-start.18) | collective-permute-done | bytes 131104 | tf_op jit(solution)/shard_map/ppermute | solution.py:541
  49.0 1.4 %collective-permute-done.19.got_2 = bf16[128,512]{1,0:T(8,128)(2,1)S(1)} collective-permute-done((bf16[128,512]{1,0:T(8,128)(2,1)S(1)}, bf16[128,512]{1,0:T(8,128)(2,1)S(1)}, u32[]{:S(2)}, u32[]{:S(2)}) %collective-permute-start.19) | collective-permute-done | bytes 131104 | tf_op jit(solution)/shard_map/ppermute | solution.py:541
  50.4 0.5 collective-permute-done.20.got_3
  51.0 1.2 %input_grad.1 = bf16[512,512]{1,0:T(8,128)(2,1)} custom-call(f32[512,512]{1,0:T(8,128)S(1)} %get-tuple-element.72.base_ref, f32[512,512]{1,0:T(8,128)S(1)} %get-tuple-element.73.normed_ref, f32[512,1]{1,0:T(8,128)S(1)} %get-tuple-element.74.inverse_ref, f32[1,512]{1,0:T(1,128)S(1)} %bitcast.7, bf16[128,512]{1,0:T(8,128)(2,1)S(1)} %get-tuple-element.119.own_ref, ...), custom_call_target="tpu_custom_call" | custom-call | tf_op jit(solution)/shard_map/input_grad/pallas_call | solution.py:527
  52.1 0.7 %collective-permute-done.22.got_ref = bf16[32,2048]{1,0:T(8,128)(2,1)S(1)} collective-permute-done((bf16[32,2048]{1,0:T(8,128)(2,1)S(1)}, bf16[32,2048]{1,0:T(8,128)(2,1)S(1)}, u32[]{:S(2)}, u32[]{:S(2)}) %collective-permute-start.22) | collective-permute-done | bytes 131104 | tf_op jit(solution)/shard_map/ppermute | solution.py:541
  52.8 0.9 %result.1 = (f32[64,1536]{1,0:T(8,128)}, f32[64,512]{1,0:T(8,128)}, f32[1,64]{1,0:T(1,128)}) custom-call(bf16[32,2048]{1,0:T(8,128)(2,1)S(1)} %add_pairs.1.held_ref, bf16[32,2048]{1,0:T(8,128)(2,1)S(1)} %collective-permute-done.22.got_ref, bf16[64,1536]{1,0:T(8,128)(2,1)S(1)} %get-tuple-element.124.w_ref, f32[1,512]{1,0:T(1,128)S(1)} %bitcast.8), custom_call_target="tpu_custom_call" | custom-call | tf_op jit(solution)/shard_map/result/pallas_call | solution.py:527
  (15 shorter events, 0.2 us)
Async XLA Ops:
  2.0 4.6 %collective-permute-start.2 = (bf16[2,2,64,512]{3,2,1,0:T(8,128)(2,1)S(1)}, bf16[2,2,64,512]{3,2,1,0:T(8,128)(2,1)S(1)}, u32[]{:S(2)}, u32[]{:S(2)}) collective-permute-start(bf16[2,2,64,512]{3,2,1,0:T(8,128)(2,1)S(1)} %get-tuple-element.69), channel_id=1, source_target_pairs={{0,4},{4,0},{8,12},{12,8},{16,20},{20,16},{24,28},{28,24},{1,5},{5... | collective-permute-start | bytes 786440 | tf_op jit(solution)/shard_map/ppermute | solution.py:541
  2.5 12.7 %collective-permute-start = (bf16[2,128,512]{2,1,0:T(8,128)(2,1)S(1)}, bf16[2,128,512]{2,1,0:T(8,128)(2,1)S(1)}, u32[]{:S(2)}, u32[]{:S(2)}) collective-permute-start(bf16[2,128,512]{2,1,0:T(8,128)(2,1)S(1)} %get-tuple-element.66), channel_id=1, source_target_pairs={{0,16},{4,20},{8,24},{12,28},{16,0},{20,4},{24,8},{28,12},{1,17},{... | collective-permute-start | bytes 786440 | tf_op jit(solution)/shard_map/ppermute | solution.py:541
  5.1 10.2 %collective-permute-start.1 = (bf16[2,128,512]{2,1,0:T(8,128)(2,1)S(1)}, bf16[2,128,512]{2,1,0:T(8,128)(2,1)S(1)}, u32[]{:S(2)}, u32[]{:S(2)}) collective-permute-start(bf16[2,128,512]{2,1,0:T(8,128)(2,1)S(1)} %get-tuple-element.67), channel_id=1, source_target_pairs={{0,8},{4,12},{8,0},{12,4},{16,24},{20,28},{24,16},{28,20},{1,9},{5... | collective-permute-start | bytes 786440 | tf_op jit(solution)/shard_map/ppermute | solution.py:541
  6.6 12.2 %collective-permute-start.5 = (bf16[2,2,64,512]{3,2,1,0:T(8,128)(2,1)S(1)}, bf16[2,2,64,512]{3,2,1,0:T(8,128)(2,1)S(1)}, u32[]{:S(2)}, u32[]{:S(2)}) collective-permute-start(bf16[2,2,64,512]{3,2,1,0:T(8,128)(2,1)S(1)} %pack_corner.1), channel_id=1, source_target_pairs={{0,24},{4,28},{8,16},{12,20},{16,8},{20,12},{24,0},{28,4},{1,25},{... | collective-permute-start | bytes 786440 | tf_op jit(solution)/shard_map/ppermute | solution.py:541
  15.2 3.6 %copy-start = (f32[512]{0:T(512)S(1)}, f32[512]{0:T(512)}, u32[]{:S(2)}) copy-start(f32[512]{0:T(512)} %param.6) | copy-start | bytes 6148
  15.3 3.5 %collective-permute-start.6 = (bf16[2,2,64,512]{3,2,1,0:T(8,128)(2,1)S(1)}, bf16[2,2,64,512]{3,2,1,0:T(8,128)(2,1)S(1)}, u32[]{:S(2)}, u32[]{:S(2)}) collective-permute-start(bf16[2,2,64,512]{3,2,1,0:T(8,128)(2,1)S(1)} %pack_other_core.1), channel_id=1, source_target_pairs={{0,4},{4,0},{8,12},{12,8},{16,20},{20,16},{24,28},{28,24},{1,5},{5... | collective-permute-start | bytes 786440 | tf_op jit(solution)/shard_map/ppermute | solution.py:541
  15.4 1.8 %collective-permute-start.3 = (bf16[4,64,384]{2,1,0:T(8,128)(2,1)S(1)}, bf16[4,64,384]{2,1,0:T(8,128)(2,1)S(1)}, u32[]{:S(2)}, u32[]{:S(2)}) collective-permute-start(bf16[4,64,384]{2,1,0:T(8,128)(2,1)S(1)} %get-tuple-element.78), channel_id=1, source_target_pairs={{0,4},{4,0},{8,12},{12,8},{16,20},{20,16},{24,28},{28,24},{1,5},{5... | collective-permute-start | bytes 589832 | tf_op jit(solution)/shard_map/ppermute | solution.py:541
  15.9 1.6 %collective-permute-start.4 = (bf16[4,64,384]{2,1,0:T(8,128)(2,1)S(1)}, bf16[4,64,384]{2,1,0:T(8,128)(2,1)S(1)}, u32[]{:S(2)}, u32[]{:S(2)}) collective-permute-start(bf16[4,64,384]{2,1,0:T(8,128)(2,1)S(1)} %get-tuple-element.79), channel_id=1, source_target_pairs={{0,4},{4,0},{8,12},{12,8},{16,20},{20,16},{24,28},{28,24},{1,5},{5... | collective-permute-start | bytes 589832 | tf_op jit(solution)/shard_map/ppermute | solution.py:541
  21.9 3.1 %collective-permute-start.8 = (bf16[4,64,1280]{2,1,0:T(8,128)(2,1)S(1)}, bf16[4,64,1280]{2,1,0:T(8,128)(2,1)S(1)}, u32[]{:S(2)}, u32[]{:S(2)}) collective-permute-start(bf16[4,64,1280]{2,1,0:T(8,128)(2,1)S(1)} %get-tuple-element.103), channel_id=1, source_target_pairs={{0,4},{4,0},{8,12},{12,8},{16,20},{20,16},{24,28},{28,24},{1,5},{5... | collective-permute-start | bytes 1966088 | tf_op jit(solution)/shard_map/ppermute | solution.py:541
  22.6 6.5 %collective-permute-start.7 = (bf16[4,64,512]{2,1,0:T(8,128)(2,1)S(1)}, bf16[4,64,512]{2,1,0:T(8,128)(2,1)S(1)}, u32[]{:S(2)}, u32[]{:S(2)}) collective-permute-start(bf16[4,64,512]{2,1,0:T(8,128)(2,1)S(1)} %get-tuple-element.93), channel_id=1, source_target_pairs={{0,4},{4,0},{8,12},{12,8},{16,20},{20,16},{24,28},{28,24},{1,5},{5... | collective-permute-start | bytes 786440 | tf_op jit(solution)/shard_map/ppermute | solution.py:541
  23.2 7.2 %collective-permute-start.10 = (bf16[4,32,768]{2,1,0:T(8,128)(2,1)S(1)}, bf16[4,32,768]{2,1,0:T(8,128)(2,1)S(1)}, u32[]{:S(2)}, u32[]{:S(2)}) collective-permute-start(bf16[4,32,768]{2,1,0:T(8,128)(2,1)S(1)} %get-tuple-element.108), channel_id=1, source_target_pairs={{0,1},{1,0},{2,3},{3,2},{4,5},{5,4},{6,7},{7,6},{8,9},{9,8},{10,11... | collective-permute-start | bytes 589832 | tf_op jit(solution)/shard_map/ppermute | solution.py:541
  25.1 10.3 %collective-permute-start.14 = (bf16[64,896]{1,0:T(8,128)(2,1)S(1)}, bf16[64,896]{1,0:T(8,128)(2,1)S(1)}, u32[]{:S(2)}, u32[]{:S(2)}) collective-permute-start(bf16[64,896]{1,0:T(8,128)(2,1)S(1)} %get-tuple-element.114), channel_id=1, source_target_pairs={{0,24},{4,28},{8,16},{12,20},{16,8},{20,12},{24,0},{28,4},{1,25},{... | collective-permute-start | bytes 344072 | tf_op jit(solution)/shard_map/ppermute | solution.py:541
  27.7 4.6 %collective-permute-start.9 = (bf16[4,32,384]{2,1,0:T(8,128)(2,1)S(1)}, bf16[4,32,384]{2,1,0:T(8,128)(2,1)S(1)}, u32[]{:S(2)}, u32[]{:S(2)}) collective-permute-start(bf16[4,32,384]{2,1,0:T(8,128)(2,1)S(1)} %get-tuple-element.105), channel_id=1, source_target_pairs={{0,1},{1,0},{2,3},{3,2},{4,5},{5,4},{6,7},{7,6},{8,9},{9,8},{10,11... | collective-permute-start | bytes 294920 | tf_op jit(solution)/shard_map/ppermute | solution.py:541
  28.6 7.3 %collective-permute-start.15 = (bf16[64,896]{1,0:T(8,128)(2,1)S(1)}, bf16[64,896]{1,0:T(8,128)(2,1)S(1)}, u32[]{:S(2)}, u32[]{:S(2)}) collective-permute-start(bf16[64,896]{1,0:T(8,128)(2,1)S(1)} %get-tuple-element.115), channel_id=1, source_target_pairs={{0,16},{4,20},{8,24},{12,28},{16,0},{20,4},{24,8},{28,12},{1,17},{... | collective-permute-start | bytes 344072 | tf_op jit(solution)/shard_map/ppermute | solution.py:541
  29.1 6.8 %collective-permute-start.16 = (bf16[64,896]{1,0:T(8,128)(2,1)S(1)}, bf16[64,896]{1,0:T(8,128)(2,1)S(1)}, u32[]{:S(2)}, u32[]{:S(2)}) collective-permute-start(bf16[64,896]{1,0:T(8,128)(2,1)S(1)} %get-tuple-element.116), channel_id=1, source_target_pairs={{0,8},{4,12},{8,0},{12,4},{16,24},{20,28},{24,16},{28,20},{1,9},{5... | collective-permute-start | bytes 344072 | tf_op jit(solution)/shard_map/ppermute | solution.py:541
  32.3 5.4 %collective-permute-start.11 = (bf16[32,1152]{1,0:T(8,128)(2,1)S(1)}, bf16[32,1152]{1,0:T(8,128)(2,1)S(1)}, u32[]{:S(2)}, u32[]{:S(2)}) collective-permute-start(bf16[32,1152]{1,0:T(8,128)(2,1)S(1)} %get-tuple-element.110), channel_id=1, source_target_pairs={{0,24},{4,28},{8,16},{12,20},{16,8},{20,12},{24,0},{28,4},{1,25},{... | collective-permute-start | bytes 221192 | tf_op jit(solution)/shard_map/ppermute | solution.py:541
  35.0 4.4 %collective-permute-start.12 = (bf16[32,1152]{1,0:T(8,128)(2,1)S(1)}, bf16[32,1152]{1,0:T(8,128)(2,1)S(1)}, u32[]{:S(2)}, u32[]{:S(2)}) collective-permute-start(bf16[32,1152]{1,0:T(8,128)(2,1)S(1)} %get-tuple-element.111), channel_id=1, source_target_pairs={{0,16},{4,20},{8,24},{12,28},{16,0},{20,4},{24,8},{28,12},{1,17},{... | collective-permute-start | bytes 221192 | tf_op jit(solution)/shard_map/ppermute | solution.py:541
  35.5 4.4 %collective-permute-start.13 = (bf16[32,1152]{1,0:T(8,128)(2,1)S(1)}, bf16[32,1152]{1,0:T(8,128)(2,1)S(1)}, u32[]{:S(2)}, u32[]{:S(2)}) collective-permute-start(bf16[32,1152]{1,0:T(8,128)(2,1)S(1)} %get-tuple-element.112), channel_id=1, source_target_pairs={{0,8},{4,12},{8,0},{12,4},{16,24},{20,28},{24,16},{28,20},{1,9},{5... | collective-permute-start | bytes 221192 | tf_op jit(solution)/shard_map/ppermute | solution.py:541
  36.0 4.2 %collective-permute-start.17 = (bf16[32,896]{1,0:T(8,128)(2,1)S(1)}, bf16[32,896]{1,0:T(8,128)(2,1)S(1)}, u32[]{:S(2)}, u32[]{:S(2)}) collective-permute-start(bf16[32,896]{1,0:T(8,128)(2,1)S(1)} %get-tuple-element.118), channel_id=1, source_target_pairs={{0,1},{1,0},{2,3},{3,2},{4,5},{5,4},{6,7},{7,6},{8,9},{9,8},{10,11... | collective-permute-start | bytes 172040 | tf_op jit(solution)/shard_map/ppermute | solution.py:541
  40.3 7.4 %collective-permute-start.21 = (bf16[32,2048]{1,0:T(8,128)(2,1)S(1)}, bf16[32,2048]{1,0:T(8,128)(2,1)S(1)}, u32[]{:S(2)}, u32[]{:S(2)}) collective-permute-start(bf16[32,2048]{1,0:T(8,128)(2,1)S(1)} %join_terms.1.kept_ref), channel_id=1, source_target_pairs={{0,2},{1,3},{2,0},{3,1},{4,6},{5,7},{6,4},{7,5},{8,10},{9,11},{10,... | collective-permute-start | bytes 393224 | tf_op jit(solution)/shard_map/ppermute | solution.py:541
  43.0 6.0 %collective-permute-start.18 = (bf16[128,512]{1,0:T(8,128)(2,1)S(1)}, bf16[128,512]{1,0:T(8,128)(2,1)S(1)}, u32[]{:S(2)}, u32[]{:S(2)}) collective-permute-start(bf16[128,512]{1,0:T(8,128)(2,1)S(1)} %get-tuple-element.120), channel_id=1, source_target_pairs={{0,24},{4,28},{8,16},{12,20},{16,8},{20,12},{24,0},{28,4},{1,25},{... | collective-permute-start | bytes 393224 | tf_op jit(solution)/shard_map/ppermute | solution.py:541
  45.5 5.0 %collective-permute-start.19 = (bf16[128,512]{1,0:T(8,128)(2,1)S(1)}, bf16[128,512]{1,0:T(8,128)(2,1)S(1)}, u32[]{:S(2)}, u32[]{:S(2)}) collective-permute-start(bf16[128,512]{1,0:T(8,128)(2,1)S(1)} %get-tuple-element.121), channel_id=1, source_target_pairs={{0,16},{4,20},{8,24},{12,28},{16,0},{20,4},{24,8},{28,12},{1,17},{... | collective-permute-start | bytes 393224 | tf_op jit(solution)/shard_map/ppermute | solution.py:541
  46.0 5.0 %collective-permute-start.20 = (bf16[128,512]{1,0:T(8,128)(2,1)S(1)}, bf16[128,512]{1,0:T(8,128)(2,1)S(1)}, u32[]{:S(2)}, u32[]{:S(2)}) collective-permute-start(bf16[128,512]{1,0:T(8,128)(2,1)S(1)} %get-tuple-element.122), channel_id=1, source_target_pairs={{0,8},{4,12},{8,0},{12,4},{16,24},{20,28},{24,16},{28,20},{1,9},{5... | collective-permute-start | bytes 393224 | tf_op jit(solution)/shard_map/ppermute | solution.py:541
  47.8 5.0 %collective-permute-start.22 = (bf16[32,2048]{1,0:T(8,128)(2,1)S(1)}, bf16[32,2048]{1,0:T(8,128)(2,1)S(1)}, u32[]{:S(2)}, u32[]{:S(2)}) collective-permute-start(bf16[32,2048]{1,0:T(8,128)(2,1)S(1)} %add_pairs.1.held_ref), channel_id=1, source_target_pairs={{0,1},{1,0},{2,3},{3,2},{4,5},{5,4},{6,7},{7,6},{8,9},{9,8},{10,11... | collective-permute-start | bytes 393224 | tf_op jit(solution)/shard_map/ppermute | solution.py:541

commit v21 on v20

--- a/solution.py
+++ b/solution.py
@@ -1,3 +1,4 @@
+import functools
 import math
 
 import jax
@@ -488,35 +489,37 @@
     out_ref[...] = (kept_ref[...].astype(F32) + got_ref[...].astype(F32)).astype(BF16)
 
 
-def result_kernel(held_ref, got_ref, w_ref, gain_ref, qkv_ref, out_ref, grad_ref):
-    rows = qkv_ref.shape[0]
+def result_kernel(mine, *refs):
+    half_ref, w_ref, gain_ref = refs[:3]
+    qkv_any, out_any, grad_ref, qkv_ref, out_ref, sems = refs[-6:]
     chip, core, layer = here()
-    at = (chip * 2 + core) * rows
-    upper = (layer & 1) == 1
-    half = rows // 2
-    width = out_ref.shape[1]
-
-    def ordered(lanes):
-        held, got = held_ref[:, lanes].astype(F32), got_ref[:, lanes].astype(F32)
-        return (jnp.where(upper, got, held), jnp.where(upper, held, got))
-
+    half, width = out_ref.shape
+    rows = 2 * half
+    upper = layer & 1 if mine else 1 - (layer & 1)
+    first = pl.multiple_of(upper * half, half)
     row_at = 3 * HW + width
+    out_ref[...] = half_ref[:, 3 * HW : row_at].astype(F32)
+    here_rows = pl.ds(first, half)
+    copies = started(pltpu.make_async_copy(out_ref, out_any.at[here_rows, :], sems.at[0]))
     for i in range(3):
-        for at_from, at_to in ((row_at + i * HW, i * width), (i * HW, i * width + HW)):
-            to = slice(at_to, at_to + HW)
-            qkv_ref[:half, to], qkv_ref[half:, to] = ordered(slice(at_from, at_from + HW))
-    out_ref[:half], out_ref[half:] = ordered(slice(3 * HW, row_at))
-    total = jnp.sum(qkv_ref[...] * w_ref[...].astype(F32), -1, keepdims=True)
-    shape = (rows, gain_ref.shape[1])
-    row = lax.broadcasted_iota(jnp.int32, shape, 0)
+        at = i * width
+        qkv_ref[:, at : at + HW] = half_ref[:, row_at + i * HW : row_at + (i + 1) * HW].astype(F32)
+        qkv_ref[:, at + HW : at + 2 * HW] = half_ref[:, i * HW : (i + 1) * HW].astype(F32)
+    copies += started(pltpu.make_async_copy(qkv_ref, qkv_any.at[here_rows, :], sems.at[1]))
+    weight = w_ref[here_rows, :].astype(F32)
+    total = jnp.sum(qkv_ref[...] * weight, -1, keepdims=True)
+    shape = (half, width)
+    row = lax.broadcasted_iota(jnp.int32, shape, 0) + (chip * 2 + core) * rows + first
     feature = lax.broadcasted_iota(jnp.int32, shape, 1)
-    gain = jnp.sum(jnp.where(feature == row + at, gain_ref[...], 0.0), -1, keepdims=True)
-    shape = (rows, grad_ref.shape[1])
-    same = lax.broadcasted_iota(jnp.int32, shape, 0) == lax.broadcasted_iota(jnp.int32, shape, 1)
-    grad_ref[...] = jnp.sum(jnp.where(same, total / gain, 0.0), 0, keepdims=True)
-
-
-def call(kernel, name, ins, outs, scratch=(), vmem=SMALL_VMEM, out_specs=None):
+    gain = jnp.sum(jnp.where(feature == row, gain_ref[...], 0.0), -1, keepdims=True)
+    shape = (half, rows)
+    same = lax.broadcasted_iota(jnp.int32, shape, 0) + first == lax.broadcasted_iota(jnp.int32, shape, 1)
+    grad = jnp.sum(jnp.where(same, total / gain, 0.0), 0, keepdims=True)
+    grad_ref[...] = grad if mine else refs[5][...] + grad
+    finished(*copies)
+
+
+def call(kernel, name, ins, outs, scratch=(), vmem=SMALL_VMEM, out_specs=None, aliases=None):
     out_specs = out_specs or [VMEM] * len(outs)
     places = [{id(HBM): pltpu.HBM, id(PINNED): pltpu.VMEM}.get(id(spec)) for spec in out_specs]
     outs = [place(*out) if place else shaped(*out) for place, out in zip(places, outs)]
@@ -530,6 +533,7 @@
         in_specs=[spec for spec, _ in ins],
         out_specs=out_specs,
         scratch_shapes=scratch,
+        input_output_aliases=aliases or {},
         name=name,
         cost_estimate=pl.CostEstimate(flops=0, bytes_accessed=0, transcendentals=0),
         compiler_params=pltpu.CompilerParams(vmem_limit_bytes=vmem),
@@ -724,12 +728,24 @@
             [pltpu.VMEM((chips, 2 * share, width), BF16), pltpu.SemaphoreType.DMA((chips,))],
             out_specs=[HBM],
         )
-        sum_qkv, sum_out, sum_gain = call(
-            result_kernel,
-            "result",
-            [(VMEM, held), (VMEM, other), (VMEM, weight_rows), (VMEM, gain)],
-            [((row_share, 3 * width), F32), ((row_share, width), F32), ((1, row_share), F32)],
-        )
+        half = row_share // 2
+        results = []
+        for mine, part in ((True, held), (False, other)):
+            aliased = [(HBM, one) for one in results[:2]] + [(VMEM, one) for one in results[2:]]
+            results = call(
+                functools.partial(result_kernel, mine),
+                "result_first" if mine else "result",
+                [(VMEM, part), (VMEM, weight_rows), (VMEM, gain), *aliased],
+                [((row_share, 3 * width), F32), ((row_share, width), F32), ((1, row_share), F32)],
+                [
+                    pltpu.VMEM((half, 3 * width), F32),
+                    pltpu.VMEM((half, width), F32),
+                    pltpu.SemaphoreType.DMA((2,)),
+                ],
+                out_specs=[HBM, HBM, VMEM],
+                aliases={} if mine else {3: 0, 4: 1},
+            )
+        sum_qkv, sum_out, sum_gain = results
         sum_gain = sum_gain.reshape(row_share)
     else:
         terms, *col_grads = call(

time: 53.8 us -> 54.2 us (level)
  Pallas kernels: 15.3 us -> 16.5 us
  waiting for transfers between devices: 12.2 us -> 11.4 us
    pallas_call x15 -> x16, Pallas kernels: 15.3 us -> 16.5 us  [call(): pl.pallas_call(kernel, out_shape=outs, in_specs=[spec for spec, _ in ins]...]
    ppermute x23, waiting for transfers between devices: 12.2 us -> 11.4 us  [swap(): return lax.ppermute(array, axis, [(i, i ^ bits) for i in range(count)])]
  transfers between devices with their start and end apart: 23 -> 23, of which waited for: 13 -> 12; matrix products, arithmetic and copies ran while one was open for 0% -> 0% of each run, Pallas kernels for 19% -> 20%
where the time goes in v21:
time: 54.2 us; the launch traced here: 54.1 us
  starting transfers between devices  25.4 us (47%)
  Pallas kernels  16.5 us (30%)
  waiting for transfers between devices  11.4 us (21%)
  between operations  0.78 us (1%)
    ppermute x23, starting transfers between devices, swap(): return lax.ppermute(array, axis, [(i, i ^ bits) for i in range(count)])  25.4 us
    pallas_call x16, Pallas kernels, call(): pl.pallas_call(kernel, out_shape=outs, in_specs=[spec for spec, _ in ins]...  16.5 us
    ppermute x23, waiting for transfers between devices, swap(): return lax.ppermute(array, axis, [(i, i ^ bits) for i in range(count)])  11.4 us
  transfers between devices with their start and end apart: 23, of which 12 were waited for; matrix products, arithmetic and copies ran while one was open for 0% of the time, Pallas kernels for 20%

profile of v21, /device:TPU:0, one launch (start us, length us, event | category | flops | bytes accessed | tf_op | source)
XLA Modules:
  0.0 54.1 jit_solution(16799084188884011132)
XLA Ops:
  0.6 1.4 %pack_columns.1 = (bf16[2,2,64,512]{3,2,1,0:T(8,128)(2,1)S(1)}, bf16[2,64,512]{2,1,0:T(8,128)(2,1)S(1)}, bf16[2,128,512]{2,1,0:T(8,128)(2,1)S(1)}, bf16[2,128,512]{2,1,0:T(8,128)(2,1)S(1)}) custom-call(bf16[512,512]{1,0:T(8,128)(2,1)} %bitcast.10, bf16[512,512]{1,0:T(8,128)(2,1)} %bitcast.12), custom_call_target="tpu_custom_call" | custom-call | tf_op jit(solution)/shard_map/pack_columns/pallas_call | solution.py:530
  2.0 0.5 collective-permute-start.2
  2.5 2.6 %collective-permute-start = (bf16[2,128,512]{2,1,0:T(8,128)(2,1)S(1)}, bf16[2,128,512]{2,1,0:T(8,128)(2,1)S(1)}, u32[]{:S(2)}, u32[]{:S(2)}) collective-permute-start(bf16[2,128,512]{2,1,0:T(8,128)(2,1)S(1)} %get-tuple-element.69), channel_id=1, source_target_pairs={{0,16},{4,20},{8,24},{12,28},{16,0},{20,4},{24,8},{28,12},{1,17},{... | collective-permute-start | bytes 786440 | tf_op jit(solution)/shard_map/ppermute | solution.py:545
  5.1 1.5 %collective-permute-start.1 = (bf16[2,128,512]{2,1,0:T(8,128)(2,1)S(1)}, bf16[2,128,512]{2,1,0:T(8,128)(2,1)S(1)}, u32[]{:S(2)}, u32[]{:S(2)}) collective-permute-start(bf16[2,128,512]{2,1,0:T(8,128)(2,1)S(1)} %get-tuple-element.70), channel_id=1, source_target_pairs={{0,8},{4,12},{8,0},{12,4},{16,24},{20,28},{24,16},{28,20},{1,9},{5... | collective-permute-start | bytes 786440 | tf_op jit(solution)/shard_map/ppermute | solution.py:545
  6.6 1.0 %collective-permute-start.5 = (bf16[2,2,64,512]{3,2,1,0:T(8,128)(2,1)S(1)}, bf16[2,2,64,512]{3,2,1,0:T(8,128)(2,1)S(1)}, u32[]{:S(2)}, u32[]{:S(2)}) collective-permute-start(bf16[2,2,64,512]{3,2,1,0:T(8,128)(2,1)S(1)} %pack_corner.1), channel_id=1, source_target_pairs={{0,24},{4,28},{8,16},{12,20},{16,8},{20,12},{24,0},{28,4},{1,25},{... | collective-permute-start | bytes 786440 | tf_op jit(solution)/shard_map/ppermute | solution.py:545
  7.6 7.6 %row_heads.1 = (bf16[4,64,384]{2,1,0:T(8,128)(2,1)S(1)}, bf16[4,64,384]{2,1,0:T(8,128)(2,1)S(1)}, bf16[4,64,384]{2,1,0:T(8,128)(2,1)S(1)}, bf16[4,64,384]{2,1,0:...) custom-call(bf16[512,512]{1,0:T(8,128)(2,1)} %bitcast.11, ...), custom_call_target="tpu_custom_call" | custom-call | tf_op jit(solution)/shard_map/row_heads/pallas_call | solution.py:530
  15.3 0.1 collective-permute-start.6
  15.4 0.5 collective-permute-start.3
  15.9 0.1 collective-permute-start.4
  16.0 1.2 %collective-permute-done.3.got_1 = bf16[4,64,384]{2,1,0:T(8,128)(2,1)S(1)} collective-permute-done((bf16[4,64,384]{2,1,0:T(8,128)(2,1)S(1)}, bf16[4,64,384]{2,1,0:T(8,128)(2,1)S(1)}, u32[]{:S(2)}, u32[]{:S(2)}) %collective-permute-start.3) | collective-permute-done | bytes 196640 | tf_op jit(solution)/shard_map/ppermute | solution.py:545
  17.2 0.3 collective-permute-done.4.got_2
  17.5 0.1 row_add_cores.1
  17.6 1.2 %collective-permute-done.5.corner_ref = bf16[2,2,64,512]{3,2,1,0:T(8,128)(2,1)S(1)} collective-permute-done((bf16[2,2,64,512]{3,2,1,0:T(8,128)(2,1)S(1)}, bf16[2,2,64,512]{3,2,1,0:T(8,128)(2,1)S(1)}, u32[]{:S(2)}, u32[]{:S(2)}) %collective-permute-start.5) | collective-permute-done | bytes 262176 | tf_op jit(solution)/shard_map/ppermute | solution.py:545
  18.8 3.1 %column_heads.1 = (bf16[4,64,1280]{2,1,0:T(8,128)(2,1)S(1)}, bf16[4,64,1280]{2,1,0:T(8,128)(2,1)S(1)}, bf16[512,768]{1,0:T(8,128)(2,1)S(1)}) custom-call(bf16[512,512]{1,0:T(8,128)(2,1)S(1)} %get-tuple-element.85.x_ref, bf16[512,512]{1,0:T(8,128)(2,1)S(1)} %get-tuple-element.86.cot_ref, bf16[2,2,64,512]{3,2,1,0:T(8,128)(2,1)S(1)} %collective-permute-done.2.swapped_ref, ...), custom_call_target="tpu_custom_call" | custom-call | tf_op jit(solution)/shard_map/column_heads/pallas_call | solution.py:530
  21.9 0.1 collective-permute-start.8
  22.0 0.6 %column_grad_hidden.1 = (bf16[4,64,512]{2,1,0:T(8,128)(2,1)S(1)}, bf16[4,64,512]{2,1,0:T(8,128)(2,1)S(1)}) custom-call(bf16[512,768]{1,0:T(8,128)(2,1)S(1)} %get-tuple-element.93.grads_ref, bf16[512,768]{1,0:T(8,128)(2,1)S(1)} %get-tuple-element.89.w_ref), custom_call_target="tpu_custom_call" | custom-call | tf_op jit(solution)/shard_map/column_grad_hidden/pallas_call | solution.py:530
  22.6 0.6 %collective-permute-start.7 = (bf16[4,64,512]{2,1,0:T(8,128)(2,1)S(1)}, bf16[4,64,512]{2,1,0:T(8,128)(2,1)S(1)}, u32[]{:S(2)}, u32[]{:S(2)}) collective-permute-start(bf16[4,64,512]{2,1,0:T(8,128)(2,1)S(1)} %get-tuple-element.96), channel_id=1, source_target_pairs={{0,4},{4,0},{8,12},{12,8},{16,20},{20,16},{24,28},{28,24},{1,5},{5... | collective-permute-start | bytes 786440 | tf_op jit(solution)/shard_map/ppermute | solution.py:545
  23.2 1.8 %collective-permute-start.10 = (bf16[4,32,768]{2,1,0:T(8,128)(2,1)S(1)}, bf16[4,32,768]{2,1,0:T(8,128)(2,1)S(1)}, u32[]{:S(2)}, u32[]{:S(2)}) collective-permute-start(bf16[4,32,768]{2,1,0:T(8,128)(2,1)S(1)} %get-tuple-element.111), channel_id=1, source_target_pairs={{0,1},{1,0},{2,3},{3,2},{4,5},{5,4},{6,7},{7,6},{8,9},{9,8},{10,11... | collective-permute-start | bytes 589832 | tf_op jit(solution)/shard_map/ppermute | solution.py:545
  25.0 0.2 column_add_cores.1
  25.1 2.5 %collective-permute-start.14 = (bf16[64,896]{1,0:T(8,128)(2,1)S(1)}, bf16[64,896]{1,0:T(8,128)(2,1)S(1)}, u32[]{:S(2)}, u32[]{:S(2)}) collective-permute-start(bf16[64,896]{1,0:T(8,128)(2,1)S(1)} %get-tuple-element.117), channel_id=1, source_target_pairs={{0,24},{4,28},{8,16},{12,20},{16,8},{20,12},{24,0},{28,4},{1,25},{... | collective-permute-start | bytes 344072 | tf_op jit(solution)/shard_map/ppermute | solution.py:545
  27.7 0.9 %collective-permute-start.9 = (bf16[4,32,384]{2,1,0:T(8,128)(2,1)S(1)}, bf16[4,32,384]{2,1,0:T(8,128)(2,1)S(1)}, u32[]{:S(2)}, u32[]{:S(2)}) collective-permute-start(bf16[4,32,384]{2,1,0:T(8,128)(2,1)S(1)} %get-tuple-element.108), channel_id=1, source_target_pairs={{0,1},{1,0},{2,3},{3,2},{4,5},{5,4},{6,7},{7,6},{8,9},{9,8},{10,11... | collective-permute-start | bytes 294920 | tf_op jit(solution)/shard_map/ppermute | solution.py:545
  28.6 0.5 collective-permute-start.15
  29.1 0.5 collective-permute-start.16
  29.7 0.7 %collective-permute-done.10.row_got = bf16[4,32,768]{2,1,0:T(8,128)(2,1)S(1)} collective-permute-done((bf16[4,32,768]{2,1,0:T(8,128)(2,1)S(1)}, bf16[4,32,768]{2,1,0:T(8,128)(2,1)S(1)}, u32[]{:S(2)}, u32[]{:S(2)}) %collective-permute-start.10) | collective-permute-done | bytes 196640 | tf_op jit(solution)/shard_map/ppermute | solution.py:545
  30.4 1.9 %collective-permute-done.9.got_ref = bf16[4,32,384]{2,1,0:T(8,128)(2,1)S(1)} collective-permute-done((bf16[4,32,384]{2,1,0:T(8,128)(2,1)S(1)}, bf16[4,32,384]{2,1,0:T(8,128)(2,1)S(1)}, u32[]{:S(2)}, u32[]{:S(2)}) %collective-permute-start.9) | collective-permute-done | bytes 98336 | tf_op jit(solution)/shard_map/ppermute | solution.py:545
  32.3 0.1 first_add_pair.1
  32.3 2.6 %collective-permute-start.11 = (bf16[32,1152]{1,0:T(8,128)(2,1)S(1)}, bf16[32,1152]{1,0:T(8,128)(2,1)S(1)}, u32[]{:S(2)}, u32[]{:S(2)}) collective-permute-start(bf16[32,1152]{1,0:T(8,128)(2,1)S(1)} %get-tuple-element.113), channel_id=1, source_target_pairs={{0,24},{4,28},{8,16},{12,20},{16,8},{20,12},{24,0},{28,4},{1,25},{... | collective-permute-start | bytes 221192 | tf_op jit(solution)/shard_map/ppermute | solution.py:545
  35.0 0.5 collective-permute-start.12
  35.5 0.4 collective-permute-start.13
  35.9 0.1 second_add_chips.1
  36.0 1.7 %collective-permute-start.17 = (bf16[32,896]{1,0:T(8,128)(2,1)S(1)}, bf16[32,896]{1,0:T(8,128)(2,1)S(1)}, u32[]{:S(2)}, u32[]{:S(2)}) collective-permute-start(bf16[32,896]{1,0:T(8,128)(2,1)S(1)} %get-tuple-element.121), channel_id=1, source_target_pairs={{0,1},{1,0},{2,3},{3,2},{4,5},{5,4},{6,7},{7,6},{8,9},{9,8},{10,11... | collective-permute-start | bytes 172040 | tf_op jit(solution)/shard_map/ppermute | solution.py:545
  37.7 0.0 collective-permute-done.11.got_1
  37.8 1.5 %collective-permute-done.12.got_2 = bf16[32,1152]{1,0:T(8,128)(2,1)S(1)} collective-permute-done((bf16[32,1152]{1,0:T(8,128)(2,1)S(1)}, bf16[32,1152]{1,0:T(8,128)(2,1)S(1)}, u32[]{:S(2)}, u32[]{:S(2)}) %collective-permute-start.12) | collective-permute-done | bytes 73760 | tf_op jit(solution)/shard_map/ppermute | solution.py:545
  39.3 0.5 collective-permute-done.13.got_3
  39.8 0.4 collective-permute-done.17.got_ref
  40.2 0.1 join_terms.1.kept_ref
  40.3 2.8 %collective-permute-start.21 = (bf16[32,2048]{1,0:T(8,128)(2,1)S(1)}, bf16[32,2048]{1,0:T(8,128)(2,1)S(1)}, u32[]{:S(2)}, u32[]{:S(2)}) collective-permute-start(bf16[32,2048]{1,0:T(8,128)(2,1)S(1)} %join_terms.1.kept_ref), channel_id=1, source_target_pairs={{0,2},{1,3},{2,0},{3,1},{4,6},{5,7},{6,4},{7,5},{8,10},{9,11},{10,... | collective-permute-start | bytes 393224 | tf_op jit(solution)/shard_map/ppermute | solution.py:545
  43.0 2.4 %collective-permute-start.18 = (bf16[128,512]{1,0:T(8,128)(2,1)S(1)}, bf16[128,512]{1,0:T(8,128)(2,1)S(1)}, u32[]{:S(2)}, u32[]{:S(2)}) collective-permute-start(bf16[128,512]{1,0:T(8,128)(2,1)S(1)} %get-tuple-element.123), channel_id=1, source_target_pairs={{0,24},{4,28},{8,16},{12,20},{16,8},{20,12},{24,0},{28,4},{1,25},{... | collective-permute-start | bytes 393224 | tf_op jit(solution)/shard_map/ppermute | solution.py:545
  45.5 0.5 collective-permute-start.19
  46.0 0.5 collective-permute-start.20
  46.5 1.2 %collective-permute-done.21.got_ref = bf16[32,2048]{1,0:T(8,128)(2,1)S(1)} collective-permute-done((bf16[32,2048]{1,0:T(8,128)(2,1)S(1)}, bf16[32,2048]{1,0:T(8,128)(2,1)S(1)}, u32[]{:S(2)}, u32[]{:S(2)}) %collective-permute-start.21) | collective-permute-done | bytes 131104 | tf_op jit(solution)/shard_map/ppermute | solution.py:545
  47.8 0.7 %collective-permute-start.22 = (bf16[32,2048]{1,0:T(8,128)(2,1)S(1)}, bf16[32,2048]{1,0:T(8,128)(2,1)S(1)}, u32[]{:S(2)}, u32[]{:S(2)}) collective-permute-start(bf16[32,2048]{1,0:T(8,128)(2,1)S(1)} %add_pairs.1.refs_0_), channel_id=1, source_target_pairs={{0,1},{1,0},{2,3},{3,2},{4,5},{5,4},{6,7},{7,6},{8,9},{9,8},{10,11... | collective-permute-start | bytes 393224 | tf_op jit(solution)/shard_map/ppermute | solution.py:545
  48.5 0.8 %result_first.1 = (f32[64,1536]{1,0:T(8,128)}, f32[64,512]{1,0:T(8,128)}, f32[1,64]{1,0:T(1,128)S(1)}) custom-call(bf16[32,2048]{1,0:T(8,128)(2,1)S(1)} %add_pairs.1.refs_0_, bf16[64,1536]{1,0:T(8,128)(2,1)S(1)} %get-tuple-element.127.refs_1_, f32[1,512]{1,0:T(1,128)S(1)} %bitcast.7), custom_call_target="tpu_custom_call" | custom-call | tf_op jit(solution)/shard_map/result_first/pallas_call | solution.py:530
  49.3 1.2 %collective-permute-done.19.got_2 = bf16[128,512]{1,0:T(8,128)(2,1)S(1)} collective-permute-done((bf16[128,512]{1,0:T(8,128)(2,1)S(1)}, bf16[128,512]{1,0:T(8,128)(2,1)S(1)}, u32[]{:S(2)}, u32[]{:S(2)}) %collective-permute-start.19) | collective-permute-done | bytes 131104 | tf_op jit(solution)/shard_map/ppermute | solution.py:545
  50.5 0.5 collective-permute-done.20.got_3
  51.0 1.1 %input_grad.1 = bf16[512,512]{1,0:T(8,128)(2,1)} custom-call(f32[512,512]{1,0:T(8,128)S(1)} %get-tuple-element.75.base_ref, f32[512,512]{1,0:T(8,128)S(1)} %get-tuple-element.76.normed_ref, f32[512,1]{1,0:T(8,128)S(1)} %get-tuple-element.77.inverse_ref, f32[1,512]{1,0:T(1,128)S(1)} %bitcast.8, bf16[128,512]{1,0:T(8,128)(2,1)S(1)} %get-tuple-element.122.own_ref, ...), custom_call_target="tpu_custom_call" | custom-call | tf_op jit(solution)/shard_map/input_grad/pallas_call | solution.py:530
  52.1 0.7 %collective-permute-done.22.refs_0_ = bf16[32,2048]{1,0:T(8,128)(2,1)S(1)} collective-permute-done((bf16[32,2048]{1,0:T(8,128)(2,1)S(1)}, bf16[32,2048]{1,0:T(8,128)(2,1)S(1)}, u32[]{:S(2)}, u32[]{:S(2)}) %collective-permute-start.22) | collective-permute-done | bytes 131104 | tf_op jit(solution)/shard_map/ppermute | solution.py:545
  52.8 1.3 %result.1 = (f32[64,1536]{1,0:T(8,128)}, f32[64,512]{1,0:T(8,128)}, f32[1,64]{1,0:T(1,128)}) custom-call(bf16[32,2048]{1,0:T(8,128)(2,1)S(1)} %collective-permute-done.22.refs_0_, bf16[64,1536]{1,0:T(8,128)(2,1)S(1)} %get-tuple-element.127.refs_1_, f32[1,512]{1,0:T(1,128)S(1)} %bitcast.9, ...), custom_call_target="tpu_custom_call", output_to_operand_aliasing={{0}: (3, {}), {1}: (4, {})} | custom-call | tf_op jit(solution)/shard_map/result/pallas_call | solution.py:530
  (16 shorter events, 0.2 us)
Async XLA Ops:
  2.0 4.6 %collective-permute-start.2 = (bf16[2,2,64,512]{3,2,1,0:T(8,128)(2,1)S(1)}, bf16[2,2,64,512]{3,2,1,0:T(8,128)(2,1)S(1)}, u32[]{:S(2)}, u32[]{:S(2)}) collective-permute-start(bf16[2,2,64,512]{3,2,1,0:T(8,128)(2,1)S(1)} %get-tuple-element.72), channel_id=1, source_target_pairs={{0,4},{4,0},{8,12},{12,8},{16,20},{20,16},{24,28},{28,24},{1,5},{5... | collective-permute-start | bytes 786440 | tf_op jit(solution)/shard_map/ppermute | solution.py:545
  2.5 12.7 %collective-permute-start = (bf16[2,128,512]{2,1,0:T(8,128)(2,1)S(1)}, bf16[2,128,512]{2,1,0:T(8,128)(2,1)S(1)}, u32[]{:S(2)}, u32[]{:S(2)}) collective-permute-start(bf16[2,128,512]{2,1,0:T(8,128)(2,1)S(1)} %get-tuple-element.69), channel_id=1, source_target_pairs={{0,16},{4,20},{8,24},{12,28},{16,0},{20,4},{24,8},{28,12},{1,17},{... | collective-permute-start | bytes 786440 | tf_op jit(solution)/shard_map/ppermute | solution.py:545
  5.1 10.2 %collective-permute-start.1 = (bf16[2,128,512]{2,1,0:T(8,128)(2,1)S(1)}, bf16[2,128,512]{2,1,0:T(8,128)(2,1)S(1)}, u32[]{:S(2)}, u32[]{:S(2)}) collective-permute-start(bf16[2,128,512]{2,1,0:T(8,128)(2,1)S(1)} %get-tuple-element.70), channel_id=1, source_target_pairs={{0,8},{4,12},{8,0},{12,4},{16,24},{20,28},{24,16},{28,20},{1,9},{5... | collective-permute-start | bytes 786440 | tf_op jit(solution)/shard_map/ppermute | solution.py:545
  6.6 12.2 %collective-permute-start.5 = (bf16[2,2,64,512]{3,2,1,0:T(8,128)(2,1)S(1)}, bf16[2,2,64,512]{3,2,1,0:T(8,128)(2,1)S(1)}, u32[]{:S(2)}, u32[]{:S(2)}) collective-permute-start(bf16[2,2,64,512]{3,2,1,0:T(8,128)(2,1)S(1)} %pack_corner.1), channel_id=1, source_target_pairs={{0,24},{4,28},{8,16},{12,20},{16,8},{20,12},{24,0},{28,4},{1,25},{... | collective-permute-start | bytes 786440 | tf_op jit(solution)/shard_map/ppermute | solution.py:545
  15.2 3.6 %copy-start = (f32[512]{0:T(512)S(1)}, f32[512]{0:T(512)}, u32[]{:S(2)}) copy-start(f32[512]{0:T(512)} %param.6) | copy-start | bytes 6148
  15.3 3.5 %collective-permute-start.6 = (bf16[2,2,64,512]{3,2,1,0:T(8,128)(2,1)S(1)}, bf16[2,2,64,512]{3,2,1,0:T(8,128)(2,1)S(1)}, u32[]{:S(2)}, u32[]{:S(2)}) collective-permute-start(bf16[2,2,64,512]{3,2,1,0:T(8,128)(2,1)S(1)} %pack_other_core.1), channel_id=1, source_target_pairs={{0,4},{4,0},{8,12},{12,8},{16,20},{20,16},{24,28},{28,24},{1,5},{5... | collective-permute-start | bytes 786440 | tf_op jit(solution)/shard_map/ppermute | solution.py:545
  15.4 1.8 %collective-permute-start.3 = (bf16[4,64,384]{2,1,0:T(8,128)(2,1)S(1)}, bf16[4,64,384]{2,1,0:T(8,128)(2,1)S(1)}, u32[]{:S(2)}, u32[]{:S(2)}) collective-permute-start(bf16[4,64,384]{2,1,0:T(8,128)(2,1)S(1)} %get-tuple-element.81), channel_id=1, source_target_pairs={{0,4},{4,0},{8,12},{12,8},{16,20},{20,16},{24,28},{28,24},{1,5},{5... | collective-permute-start | bytes 589832 | tf_op jit(solution)/shard_map/ppermute | solution.py:545
  15.9 1.6 %collective-permute-start.4 = (bf16[4,64,384]{2,1,0:T(8,128)(2,1)S(1)}, bf16[4,64,384]{2,1,0:T(8,128)(2,1)S(1)}, u32[]{:S(2)}, u32[]{:S(2)}) collective-permute-start(bf16[4,64,384]{2,1,0:T(8,128)(2,1)S(1)} %get-tuple-element.82), channel_id=1, source_target_pairs={{0,4},{4,0},{8,12},{12,8},{16,20},{20,16},{24,28},{28,24},{1,5},{5... | collective-permute-start | bytes 589832 | tf_op jit(solution)/shard_map/ppermute | solution.py:545
  21.9 3.1 %collective-permute-start.8 = (bf16[4,64,1280]{2,1,0:T(8,128)(2,1)S(1)}, bf16[4,64,1280]{2,1,0:T(8,128)(2,1)S(1)}, u32[]{:S(2)}, u32[]{:S(2)}) collective-permute-start(bf16[4,64,1280]{2,1,0:T(8,128)(2,1)S(1)} %get-tuple-element.106), channel_id=1, source_target_pairs={{0,4},{4,0},{8,12},{12,8},{16,20},{20,16},{24,28},{28,24},{1,5},{5... | collective-permute-start | bytes 1966088 | tf_op jit(solution)/shard_map/ppermute | solution.py:545
  22.6 6.5 %collective-permute-start.7 = (bf16[4,64,512]{2,1,0:T(8,128)(2,1)S(1)}, bf16[4,64,512]{2,1,0:T(8,128)(2,1)S(1)}, u32[]{:S(2)}, u32[]{:S(2)}) collective-permute-start(bf16[4,64,512]{2,1,0:T(8,128)(2,1)S(1)} %get-tuple-element.96), channel_id=1, source_target_pairs={{0,4},{4,0},{8,12},{12,8},{16,20},{20,16},{24,28},{28,24},{1,5},{5... | collective-permute-start | bytes 786440 | tf_op jit(solution)/shard_map/ppermute | solution.py:545
  23.2 7.2 %collective-permute-start.10 = (bf16[4,32,768]{2,1,0:T(8,128)(2,1)S(1)}, bf16[4,32,768]{2,1,0:T(8,128)(2,1)S(1)}, u32[]{:S(2)}, u32[]{:S(2)}) collective-permute-start(bf16[4,32,768]{2,1,0:T(8,128)(2,1)S(1)} %get-tuple-element.111), channel_id=1, source_target_pairs={{0,1},{1,0},{2,3},{3,2},{4,5},{5,4},{6,7},{7,6},{8,9},{9,8},{10,11... | collective-permute-start | bytes 589832 | tf_op jit(solution)/shard_map/ppermute | solution.py:545
  25.1 10.3 %collective-permute-start.14 = (bf16[64,896]{1,0:T(8,128)(2,1)S(1)}, bf16[64,896]{1,0:T(8,128)(2,1)S(1)}, u32[]{:S(2)}, u32[]{:S(2)}) collective-permute-start(bf16[64,896]{1,0:T(8,128)(2,1)S(1)} %get-tuple-element.117), channel_id=1, source_target_pairs={{0,24},{4,28},{8,16},{12,20},{16,8},{20,12},{24,0},{28,4},{1,25},{... | collective-permute-start | bytes 344072 | tf_op jit(solution)/shard_map/ppermute | solution.py:545
  27.7 4.6 %collective-permute-start.9 = (bf16[4,32,384]{2,1,0:T(8,128)(2,1)S(1)}, bf16[4,32,384]{2,1,0:T(8,128)(2,1)S(1)}, u32[]{:S(2)}, u32[]{:S(2)}) collective-permute-start(bf16[4,32,384]{2,1,0:T(8,128)(2,1)S(1)} %get-tuple-element.108), channel_id=1, source_target_pairs={{0,1},{1,0},{2,3},{3,2},{4,5},{5,4},{6,7},{7,6},{8,9},{9,8},{10,11... | collective-permute-start | bytes 294920 | tf_op jit(solution)/shard_map/ppermute | solution.py:545
  28.6 7.3 %collective-permute-start.15 = (bf16[64,896]{1,0:T(8,128)(2,1)S(1)}, bf16[64,896]{1,0:T(8,128)(2,1)S(1)}, u32[]{:S(2)}, u32[]{:S(2)}) collective-permute-start(bf16[64,896]{1,0:T(8,128)(2,1)S(1)} %get-tuple-element.118), channel_id=1, source_target_pairs={{0,16},{4,20},{8,24},{12,28},{16,0},{20,4},{24,8},{28,12},{1,17},{... | collective-permute-start | bytes 344072 | tf_op jit(solution)/shard_map/ppermute | solution.py:545
  29.1 6.8 %collective-permute-start.16 = (bf16[64,896]{1,0:T(8,128)(2,1)S(1)}, bf16[64,896]{1,0:T(8,128)(2,1)S(1)}, u32[]{:S(2)}, u32[]{:S(2)}) collective-permute-start(bf16[64,896]{1,0:T(8,128)(2,1)S(1)} %get-tuple-element.119), channel_id=1, source_target_pairs={{0,8},{4,12},{8,0},{12,4},{16,24},{20,28},{24,16},{28,20},{1,9},{5... | collective-permute-start | bytes 344072 | tf_op jit(solution)/shard_map/ppermute | solution.py:545
  32.3 5.4 %collective-permute-start.11 = (bf16[32,1152]{1,0:T(8,128)(2,1)S(1)}, bf16[32,1152]{1,0:T(8,128)(2,1)S(1)}, u32[]{:S(2)}, u32[]{:S(2)}) collective-permute-start(bf16[32,1152]{1,0:T(8,128)(2,1)S(1)} %get-tuple-element.113), channel_id=1, source_target_pairs={{0,24},{4,28},{8,16},{12,20},{16,8},{20,12},{24,0},{28,4},{1,25},{... | collective-permute-start | bytes 221192 | tf_op jit(solution)/shard_map/ppermute | solution.py:545
  35.0 4.4 %collective-permute-start.12 = (bf16[32,1152]{1,0:T(8,128)(2,1)S(1)}, bf16[32,1152]{1,0:T(8,128)(2,1)S(1)}, u32[]{:S(2)}, u32[]{:S(2)}) collective-permute-start(bf16[32,1152]{1,0:T(8,128)(2,1)S(1)} %get-tuple-element.114), channel_id=1, source_target_pairs={{0,16},{4,20},{8,24},{12,28},{16,0},{20,4},{24,8},{28,12},{1,17},{... | collective-permute-start | bytes 221192 | tf_op jit(solution)/shard_map/ppermute | solution.py:545
  35.5 4.4 %collective-permute-start.13 = (bf16[32,1152]{1,0:T(8,128)(2,1)S(1)}, bf16[32,1152]{1,0:T(8,128)(2,1)S(1)}, u32[]{:S(2)}, u32[]{:S(2)}) collective-permute-start(bf16[32,1152]{1,0:T(8,128)(2,1)S(1)} %get-tuple-element.115), channel_id=1, source_target_pairs={{0,8},{4,12},{8,0},{12,4},{16,24},{20,28},{24,16},{28,20},{1,9},{5... | collective-permute-start | bytes 221192 | tf_op jit(solution)/shard_map/ppermute | solution.py:545
  36.0 4.2 %collective-permute-start.17 = (bf16[32,896]{1,0:T(8,128)(2,1)S(1)}, bf16[32,896]{1,0:T(8,128)(2,1)S(1)}, u32[]{:S(2)}, u32[]{:S(2)}) collective-permute-start(bf16[32,896]{1,0:T(8,128)(2,1)S(1)} %get-tuple-element.121), channel_id=1, source_target_pairs={{0,1},{1,0},{2,3},{3,2},{4,5},{5,4},{6,7},{7,6},{8,9},{9,8},{10,11... | collective-permute-start | bytes 172040 | tf_op jit(solution)/shard_map/ppermute | solution.py:545
  40.3 7.4 %collective-permute-start.21 = (bf16[32,2048]{1,0:T(8,128)(2,1)S(1)}, bf16[32,2048]{1,0:T(8,128)(2,1)S(1)}, u32[]{:S(2)}, u32[]{:S(2)}) collective-permute-start(bf16[32,2048]{1,0:T(8,128)(2,1)S(1)} %join_terms.1.kept_ref), channel_id=1, source_target_pairs={{0,2},{1,3},{2,0},{3,1},{4,6},{5,7},{6,4},{7,5},{8,10},{9,11},{10,... | collective-permute-start | bytes 393224 | tf_op jit(solution)/shard_map/ppermute | solution.py:545
  43.0 6.2 %collective-permute-start.18 = (bf16[128,512]{1,0:T(8,128)(2,1)S(1)}, bf16[128,512]{1,0:T(8,128)(2,1)S(1)}, u32[]{:S(2)}, u32[]{:S(2)}) collective-permute-start(bf16[128,512]{1,0:T(8,128)(2,1)S(1)} %get-tuple-element.123), channel_id=1, source_target_pairs={{0,24},{4,28},{8,16},{12,20},{16,8},{20,12},{24,0},{28,4},{1,25},{... | collective-permute-start | bytes 393224 | tf_op jit(solution)/shard_map/ppermute | solution.py:545
  45.5 5.0 %collective-permute-start.19 = (bf16[128,512]{1,0:T(8,128)(2,1)S(1)}, bf16[128,512]{1,0:T(8,128)(2,1)S(1)}, u32[]{:S(2)}, u32[]{:S(2)}) collective-permute-start(bf16[128,512]{1,0:T(8,128)(2,1)S(1)} %get-tuple-element.124), channel_id=1, source_target_pairs={{0,16},{4,20},{8,24},{12,28},{16,0},{20,4},{24,8},{28,12},{1,17},{... | collective-permute-start | bytes 393224 | tf_op jit(solution)/shard_map/ppermute | solution.py:545
  46.0 5.0 %collective-permute-start.20 = (bf16[128,512]{1,0:T(8,128)(2,1)S(1)}, bf16[128,512]{1,0:T(8,128)(2,1)S(1)}, u32[]{:S(2)}, u32[]{:S(2)}) collective-permute-start(bf16[128,512]{1,0:T(8,128)(2,1)S(1)} %get-tuple-element.125), channel_id=1, source_target_pairs={{0,8},{4,12},{8,0},{12,4},{16,24},{20,28},{24,16},{28,20},{1,9},{5... | collective-permute-start | bytes 393224 | tf_op jit(solution)/shard_map/ppermute | solution.py:545
  47.8 5.0 %collective-permute-start.22 = (bf16[32,2048]{1,0:T(8,128)(2,1)S(1)}, bf16[32,2048]{1,0:T(8,128)(2,1)S(1)}, u32[]{:S(2)}, u32[]{:S(2)}) collective-permute-start(bf16[32,2048]{1,0:T(8,128)(2,1)S(1)} %add_pairs.1.refs_0_), channel_id=1, source_target_pairs={{0,1},{1,0},{2,3},{3,2},{4,5},{5,4},{6,7},{7,6},{8,9},{9,8},{10,11... | collective-permute-start | bytes 393224 | tf_op jit(solution)/shard_map/ppermute | solution.py:545

commit v22 on v20

--- a/solution.py
+++ b/solution.py
@@ -21,7 +21,7 @@
 VMEM = pl.BlockSpec(memory_space=pltpu.VMEM)
 HBM = pl.BlockSpec(memory_space=pltpu.HBM)
 CHIP_STEPS = (3, 2, 1)
-FIRST_PART = 384
+FIRST_PART = 512
 PINNED = pl.BlockSpec(memory_space=pltpu.VMEM)
 shaped = jax.ShapeDtypeStruct
 

time: 53.8 us -> 54.4 us (1.011)
  transfers between devices with their start and end apart: 23 -> 23, of which waited for: 13 -> 11; matrix products, arithmetic and copies ran while one was open for 0% -> 0% of each run, Pallas kernels for 19% -> 18%
where the time goes in v22:
time: 54.4 us; the launch traced here: 54.2 us
  starting transfers between devices  25.6 us (47%)
  Pallas kernels  15.3 us (28%)
  waiting for transfers between devices  12.6 us (23%)
  between operations  0.77 us (1%)
    ppermute x23, starting transfers between devices, swap(): return lax.ppermute(array, axis, [(i, i ^ bits) for i in range(count)])  25.6 us
    pallas_call x15, Pallas kernels, call(): pl.pallas_call(kernel, out_shape=outs, in_specs=[spec for spec, _ in ins]...  15.3 us
    ppermute x23, waiting for transfers between devices, swap(): return lax.ppermute(array, axis, [(i, i ^ bits) for i in range(count)])  12.6 us
  transfers between devices with their start and end apart: 23, of which 11 were waited for; matrix products, arithmetic and copies ran while one was open for 0% of the time, Pallas kernels for 18%

profile of v22, /device:TPU:0, one launch (start us, length us, event | category | flops | bytes accessed | tf_op | source)
XLA Modules:
  0.0 54.2 jit_solution(6422058840612890368)
XLA Ops:
  0.6 1.4 %pack_columns.1 = (bf16[2,2,64,512]{3,2,1,0:T(8,128)(2,1)S(1)}, bf16[2,64,512]{2,1,0:T(8,128)(2,1)S(1)}, bf16[2,128,512]{2,1,0:T(8,128)(2,1)S(1)}, bf16[2,128,512]{2,1,0:T(8,128)(2,1)S(1)}) custom-call(bf16[512,512]{1,0:T(8,128)(2,1)} %bitcast.9, bf16[512,512]{1,0:T(8,128)(2,1)} %bitcast.11), custom_call_target="tpu_custom_call" | custom-call | tf_op jit(solution)/shard_map/pack_columns/pallas_call | solution.py:527
  2.0 0.5 collective-permute-start.2
  2.5 2.6 %collective-permute-start = (bf16[2,128,512]{2,1,0:T(8,128)(2,1)S(1)}, bf16[2,128,512]{2,1,0:T(8,128)(2,1)S(1)}, u32[]{:S(2)}, u32[]{:S(2)}) collective-permute-start(bf16[2,128,512]{2,1,0:T(8,128)(2,1)S(1)} %get-tuple-element.66), channel_id=1, source_target_pairs={{0,16},{4,20},{8,24},{12,28},{16,0},{20,4},{24,8},{28,12},{1,17},{... | collective-permute-start | bytes 786440 | tf_op jit(solution)/shard_map/ppermute | solution.py:541
  5.1 1.5 %collective-permute-start.1 = (bf16[2,128,512]{2,1,0:T(8,128)(2,1)S(1)}, bf16[2,128,512]{2,1,0:T(8,128)(2,1)S(1)}, u32[]{:S(2)}, u32[]{:S(2)}) collective-permute-start(bf16[2,128,512]{2,1,0:T(8,128)(2,1)S(1)} %get-tuple-element.67), channel_id=1, source_target_pairs={{0,8},{4,12},{8,0},{12,4},{16,24},{20,28},{24,16},{28,20},{1,9},{5... | collective-permute-start | bytes 786440 | tf_op jit(solution)/shard_map/ppermute | solution.py:541
  6.6 0.0 collective-permute-done.2.swapped_ref
  6.6 1.0 %collective-permute-start.5 = (bf16[2,2,64,512]{3,2,1,0:T(8,128)(2,1)S(1)}, bf16[2,2,64,512]{3,2,1,0:T(8,128)(2,1)S(1)}, u32[]{:S(2)}, u32[]{:S(2)}) collective-permute-start(bf16[2,2,64,512]{3,2,1,0:T(8,128)(2,1)S(1)} %pack_corner.1), channel_id=1, source_target_pairs={{0,24},{4,28},{8,16},{12,20},{16,8},{20,12},{24,0},{28,4},{1,25},{... | collective-permute-start | bytes 786440 | tf_op jit(solution)/shard_map/ppermute | solution.py:541
  7.6 7.6 %row_heads.1 = (bf16[4,64,384]{2,1,0:T(8,128)(2,1)S(1)}, bf16[4,64,384]{2,1,0:T(8,128)(2,1)S(1)}, bf16[4,64,384]{2,1,0:T(8,128)(2,1)S(1)}, bf16[4,64,384]{2,1,0:...) custom-call(bf16[512,512]{1,0:T(8,128)(2,1)} %bitcast.10, ...), custom_call_target="tpu_custom_call" | custom-call | tf_op jit(solution)/shard_map/row_heads/pallas_call | solution.py:527
  15.2 0.0 copy-start
  15.3 0.1 collective-permute-start.6
  15.4 0.5 collective-permute-start.3
  15.9 0.1 collective-permute-start.4
  16.0 1.2 %collective-permute-done.3.got_1 = bf16[4,64,384]{2,1,0:T(8,128)(2,1)S(1)} collective-permute-done((bf16[4,64,384]{2,1,0:T(8,128)(2,1)S(1)}, bf16[4,64,384]{2,1,0:T(8,128)(2,1)S(1)}, u32[]{:S(2)}, u32[]{:S(2)}) %collective-permute-start.3) | collective-permute-done | bytes 196640 | tf_op jit(solution)/shard_map/ppermute | solution.py:541
  17.2 0.3 collective-permute-done.4.got_2
  17.5 0.1 row_add_cores.1
  17.6 1.2 %collective-permute-done.5.corner_ref = bf16[2,2,64,512]{3,2,1,0:T(8,128)(2,1)S(1)} collective-permute-done((bf16[2,2,64,512]{3,2,1,0:T(8,128)(2,1)S(1)}, bf16[2,2,64,512]{3,2,1,0:T(8,128)(2,1)S(1)}, u32[]{:S(2)}, u32[]{:S(2)}) %collective-permute-start.5) | collective-permute-done | bytes 262176 | tf_op jit(solution)/shard_map/ppermute | solution.py:541
  18.8 0.0 collective-permute-done.6.far_ref
  18.8 3.1 %column_heads.1 = (bf16[4,64,1280]{2,1,0:T(8,128)(2,1)S(1)}, bf16[4,64,1280]{2,1,0:T(8,128)(2,1)S(1)}, bf16[512,768]{1,0:T(8,128)(2,1)S(1)}) custom-call(bf16[512,512]{1,0:T(8,128)(2,1)S(1)} %get-tuple-element.82.x_ref, bf16[512,512]{1,0:T(8,128)(2,1)S(1)} %get-tuple-element.83.cot_ref, bf16[2,2,64,512]{3,2,1,0:T(8,128)(2,1)S(1)} %collective-permute-done.2.swapped_ref, ...), custom_call_target="tpu_custom_call" | custom-call | tf_op jit(solution)/shard_map/column_heads/pallas_call | solution.py:527
  21.9 0.1 collective-permute-start.8
  22.0 0.6 %column_grad_hidden.1 = (bf16[4,64,512]{2,1,0:T(8,128)(2,1)S(1)}, bf16[4,64,512]{2,1,0:T(8,128)(2,1)S(1)}) custom-call(bf16[512,768]{1,0:T(8,128)(2,1)S(1)} %get-tuple-element.90.grads_ref, bf16[512,768]{1,0:T(8,128)(2,1)S(1)} %get-tuple-element.86.w_ref), custom_call_target="tpu_custom_call" | custom-call | tf_op jit(solution)/shard_map/column_grad_hidden/pallas_call | solution.py:527
  22.6 0.6 %collective-permute-start.7 = (bf16[4,64,512]{2,1,0:T(8,128)(2,1)S(1)}, bf16[4,64,512]{2,1,0:T(8,128)(2,1)S(1)}, u32[]{:S(2)}, u32[]{:S(2)}) collective-permute-start(bf16[4,64,512]{2,1,0:T(8,128)(2,1)S(1)} %get-tuple-element.93), channel_id=1, source_target_pairs={{0,4},{4,0},{8,12},{12,8},{16,20},{20,16},{24,28},{28,24},{1,5},{5... | collective-permute-start | bytes 786440 | tf_op jit(solution)/shard_map/ppermute | solution.py:541
  23.2 1.8 %collective-permute-start.10 = (bf16[4,32,768]{2,1,0:T(8,128)(2,1)S(1)}, bf16[4,32,768]{2,1,0:T(8,128)(2,1)S(1)}, u32[]{:S(2)}, u32[]{:S(2)}) collective-permute-start(bf16[4,32,768]{2,1,0:T(8,128)(2,1)S(1)} %get-tuple-element.108), channel_id=1, source_target_pairs={{0,1},{1,0},{2,3},{3,2},{4,5},{5,4},{6,7},{7,6},{8,9},{9,8},{10,11... | collective-permute-start | bytes 589832 | tf_op jit(solution)/shard_map/ppermute | solution.py:541
  25.0 0.2 column_add_cores.1
  25.2 1.0 %collective-permute-start.9 = (bf16[4,32,512]{2,1,0:T(8,128)(2,1)S(1)}, bf16[4,32,512]{2,1,0:T(8,128)(2,1)S(1)}, u32[]{:S(2)}, u32[]{:S(2)}) collective-permute-start(bf16[4,32,512]{2,1,0:T(8,128)(2,1)S(1)} %get-tuple-element.105), channel_id=1, source_target_pairs={{0,1},{1,0},{2,3},{3,2},{4,5},{5,4},{6,7},{7,6},{8,9},{9,8},{10,11... | collective-permute-start | bytes 393224 | tf_op jit(solution)/shard_map/ppermute | solution.py:541
  26.1 2.4 %collective-permute-start.14 = (bf16[64,768]{1,0:T(8,128)(2,1)S(1)}, bf16[64,768]{1,0:T(8,128)(2,1)S(1)}, u32[]{:S(2)}, u32[]{:S(2)}) collective-permute-start(bf16[64,768]{1,0:T(8,128)(2,1)S(1)} %get-tuple-element.114), channel_id=1, source_target_pairs={{0,24},{4,28},{8,16},{12,20},{16,8},{20,12},{24,0},{28,4},{1,25},{... | collective-permute-start | bytes 294920 | tf_op jit(solution)/shard_map/ppermute | solution.py:541
  28.6 0.5 collective-permute-start.15
  29.1 0.5 collective-permute-start.16
  29.7 1.2 %collective-permute-done.10.row_got = bf16[4,32,768]{2,1,0:T(8,128)(2,1)S(1)} collective-permute-done((bf16[4,32,768]{2,1,0:T(8,128)(2,1)S(1)}, bf16[4,32,768]{2,1,0:T(8,128)(2,1)S(1)}, u32[]{:S(2)}, u32[]{:S(2)}) %collective-permute-start.10) | collective-permute-done | bytes 196640 | tf_op jit(solution)/shard_map/ppermute | solution.py:541
  30.9 2.0 %collective-permute-done.9.got_ref = bf16[4,32,512]{2,1,0:T(8,128)(2,1)S(1)} collective-permute-done((bf16[4,32,512]{2,1,0:T(8,128)(2,1)S(1)}, bf16[4,32,512]{2,1,0:T(8,128)(2,1)S(1)}, u32[]{:S(2)}, u32[]{:S(2)}) %collective-permute-start.9) | collective-permute-done | bytes 131104 | tf_op jit(solution)/shard_map/ppermute | solution.py:541
  32.9 0.1 first_add_pair.1
  33.0 2.7 %collective-permute-start.11 = (bf16[32,1280]{1,0:T(8,128)(2,1)S(1)}, bf16[32,1280]{1,0:T(8,128)(2,1)S(1)}, u32[]{:S(2)}, u32[]{:S(2)}) collective-permute-start(bf16[32,1280]{1,0:T(8,128)(2,1)S(1)} %get-tuple-element.110), channel_id=1, source_target_pairs={{0,24},{4,28},{8,16},{12,20},{16,8},{20,12},{24,0},{28,4},{1,25},{... | collective-permute-start | bytes 245768 | tf_op jit(solution)/shard_map/ppermute | solution.py:541
  35.7 0.5 collective-permute-start.12
  36.2 0.4 collective-permute-start.13
  36.6 0.1 second_add_chips.1
  36.6 1.8 %collective-permute-start.17 = (bf16[32,768]{1,0:T(8,128)(2,1)S(1)}, bf16[32,768]{1,0:T(8,128)(2,1)S(1)}, u32[]{:S(2)}, u32[]{:S(2)}) collective-permute-start(bf16[32,768]{1,0:T(8,128)(2,1)S(1)} %get-tuple-element.118), channel_id=1, source_target_pairs={{0,1},{1,0},{2,3},{3,2},{4,5},{5,4},{6,7},{7,6},{8,9},{9,8},{10,11... | collective-permute-start | bytes 147464 | tf_op jit(solution)/shard_map/ppermute | solution.py:541
  38.4 2.3 %collective-permute-done.17.got_ref = bf16[32,768]{1,0:T(8,128)(2,1)S(1)} collective-permute-done((bf16[32,768]{1,0:T(8,128)(2,1)S(1)}, bf16[32,768]{1,0:T(8,128)(2,1)S(1)}, u32[]{:S(2)}, u32[]{:S(2)}) %collective-permute-start.17) | collective-permute-done | bytes 49184 | tf_op jit(solution)/shard_map/ppermute | solution.py:541
  40.8 0.1 join_terms.1.kept_ref
  40.8 2.8 %collective-permute-start.21 = (bf16[32,2048]{1,0:T(8,128)(2,1)S(1)}, bf16[32,2048]{1,0:T(8,128)(2,1)S(1)}, u32[]{:S(2)}, u32[]{:S(2)}) collective-permute-start(bf16[32,2048]{1,0:T(8,128)(2,1)S(1)} %join_terms.1.kept_ref), channel_id=1, source_target_pairs={{0,2},{1,3},{2,0},{3,1},{4,6},{5,7},{6,4},{7,5},{8,10},{9,11},{10,... | collective-permute-start | bytes 393224 | tf_op jit(solution)/shard_map/ppermute | solution.py:541
  43.7 2.4 %collective-permute-start.18 = (bf16[128,512]{1,0:T(8,128)(2,1)S(1)}, bf16[128,512]{1,0:T(8,128)(2,1)S(1)}, u32[]{:S(2)}, u32[]{:S(2)}) collective-permute-start(bf16[128,512]{1,0:T(8,128)(2,1)S(1)} %get-tuple-element.120), channel_id=1, source_target_pairs={{0,24},{4,28},{8,16},{12,20},{16,8},{20,12},{24,0},{28,4},{1,25},{... | collective-permute-start | bytes 393224 | tf_op jit(solution)/shard_map/ppermute | solution.py:541
  46.1 0.5 collective-permute-start.19
  46.6 0.5 collective-permute-start.20
  47.1 1.1 %collective-permute-done.21.got_ref = bf16[32,2048]{1,0:T(8,128)(2,1)S(1)} collective-permute-done((bf16[32,2048]{1,0:T(8,128)(2,1)S(1)}, bf16[32,2048]{1,0:T(8,128)(2,1)S(1)}, u32[]{:S(2)}, u32[]{:S(2)}) %collective-permute-start.21) | collective-permute-done | bytes 131104 | tf_op jit(solution)/shard_map/ppermute | solution.py:541
  48.3 0.8 %collective-permute-start.22 = (bf16[32,2048]{1,0:T(8,128)(2,1)S(1)}, bf16[32,2048]{1,0:T(8,128)(2,1)S(1)}, u32[]{:S(2)}, u32[]{:S(2)}) collective-permute-start(bf16[32,2048]{1,0:T(8,128)(2,1)S(1)} %add_pairs.1.held_ref), channel_id=1, source_target_pairs={{0,1},{1,0},{2,3},{3,2},{4,5},{5,4},{6,7},{7,6},{8,9},{9,8},{10,11... | collective-permute-start | bytes 393224 | tf_op jit(solution)/shard_map/ppermute | solution.py:541
  49.1 0.6 %collective-permute-done.18.got_1 = bf16[128,512]{1,0:T(8,128)(2,1)S(1)} collective-permute-done((bf16[128,512]{1,0:T(8,128)(2,1)S(1)}, bf16[128,512]{1,0:T(8,128)(2,1)S(1)}, u32[]{:S(2)}, u32[]{:S(2)}) %collective-permute-start.18) | collective-permute-done | bytes 131104 | tf_op jit(solution)/shard_map/ppermute | solution.py:541
  49.7 1.4 %collective-permute-done.19.got_2 = bf16[128,512]{1,0:T(8,128)(2,1)S(1)} collective-permute-done((bf16[128,512]{1,0:T(8,128)(2,1)S(1)}, bf16[128,512]{1,0:T(8,128)(2,1)S(1)}, u32[]{:S(2)}, u32[]{:S(2)}) %collective-permute-start.19) | collective-permute-done | bytes 131104 | tf_op jit(solution)/shard_map/ppermute | solution.py:541
  51.1 0.5 collective-permute-done.20.got_3
  51.6 1.2 %input_grad.1 = bf16[512,512]{1,0:T(8,128)(2,1)} custom-call(f32[512,512]{1,0:T(8,128)S(1)} %get-tuple-element.72.base_ref, f32[512,512]{1,0:T(8,128)S(1)} %get-tuple-element.73.normed_ref, f32[512,1]{1,0:T(8,128)S(1)} %get-tuple-element.74.inverse_ref, f32[1,512]{1,0:T(1,128)S(1)} %bitcast.7, bf16[128,512]{1,0:T(8,128)(2,1)S(1)} %get-tuple-element.119.own_ref, ...), custom_call_target="tpu_custom_call" | custom-call | tf_op jit(solution)/shard_map/input_grad/pallas_call | solution.py:527
  52.7 0.6 %collective-permute-done.22.got_ref = bf16[32,2048]{1,0:T(8,128)(2,1)S(1)} collective-permute-done((bf16[32,2048]{1,0:T(8,128)(2,1)S(1)}, bf16[32,2048]{1,0:T(8,128)(2,1)S(1)}, u32[]{:S(2)}, u32[]{:S(2)}) %collective-permute-start.22) | collective-permute-done | bytes 131104 | tf_op jit(solution)/shard_map/ppermute | solution.py:541
  53.4 0.9 %result.1 = (f32[64,1536]{1,0:T(8,128)}, f32[64,512]{1,0:T(8,128)}, f32[1,64]{1,0:T(1,128)}) custom-call(bf16[32,2048]{1,0:T(8,128)(2,1)S(1)} %add_pairs.1.held_ref, bf16[32,2048]{1,0:T(8,128)(2,1)S(1)} %collective-permute-done.22.got_ref, bf16[64,1536]{1,0:T(8,128)(2,1)S(1)} %get-tuple-element.124.w_ref, f32[1,512]{1,0:T(1,128)S(1)} %bitcast.8), custom_call_target="tpu_custom_call" | custom-call | tf_op jit(solution)/shard_map/result/pallas_call | solution.py:527
  (15 shorter events, 0.2 us)
Async XLA Ops:
  2.0 4.6 %collective-permute-start.2 = (bf16[2,2,64,512]{3,2,1,0:T(8,128)(2,1)S(1)}, bf16[2,2,64,512]{3,2,1,0:T(8,128)(2,1)S(1)}, u32[]{:S(2)}, u32[]{:S(2)}) collective-permute-start(bf16[2,2,64,512]{3,2,1,0:T(8,128)(2,1)S(1)} %get-tuple-element.69), channel_id=1, source_target_pairs={{0,4},{4,0},{8,12},{12,8},{16,20},{20,16},{24,28},{28,24},{1,5},{5... | collective-permute-start | bytes 786440 | tf_op jit(solution)/shard_map/ppermute | solution.py:541
  2.5 12.7 %collective-permute-start = (bf16[2,128,512]{2,1,0:T(8,128)(2,1)S(1)}, bf16[2,128,512]{2,1,0:T(8,128)(2,1)S(1)}, u32[]{:S(2)}, u32[]{:S(2)}) collective-permute-start(bf16[2,128,512]{2,1,0:T(8,128)(2,1)S(1)} %get-tuple-element.66), channel_id=1, source_target_pairs={{0,16},{4,20},{8,24},{12,28},{16,0},{20,4},{24,8},{28,12},{1,17},{... | collective-permute-start | bytes 786440 | tf_op jit(solution)/shard_map/ppermute | solution.py:541
  5.1 10.2 %collective-permute-start.1 = (bf16[2,128,512]{2,1,0:T(8,128)(2,1)S(1)}, bf16[2,128,512]{2,1,0:T(8,128)(2,1)S(1)}, u32[]{:S(2)}, u32[]{:S(2)}) collective-permute-start(bf16[2,128,512]{2,1,0:T(8,128)(2,1)S(1)} %get-tuple-element.67), channel_id=1, source_target_pairs={{0,8},{4,12},{8,0},{12,4},{16,24},{20,28},{24,16},{28,20},{1,9},{5... | collective-permute-start | bytes 786440 | tf_op jit(solution)/shard_map/ppermute | solution.py:541
  6.6 12.2 %collective-permute-start.5 = (bf16[2,2,64,512]{3,2,1,0:T(8,128)(2,1)S(1)}, bf16[2,2,64,512]{3,2,1,0:T(8,128)(2,1)S(1)}, u32[]{:S(2)}, u32[]{:S(2)}) collective-permute-start(bf16[2,2,64,512]{3,2,1,0:T(8,128)(2,1)S(1)} %pack_corner.1), channel_id=1, source_target_pairs={{0,24},{4,28},{8,16},{12,20},{16,8},{20,12},{24,0},{28,4},{1,25},{... | collective-permute-start | bytes 786440 | tf_op jit(solution)/shard_map/ppermute | solution.py:541
  15.2 3.6 %copy-start = (f32[512]{0:T(512)S(1)}, f32[512]{0:T(512)}, u32[]{:S(2)}) copy-start(f32[512]{0:T(512)} %param.6) | copy-start | bytes 6148
  15.3 3.5 %collective-permute-start.6 = (bf16[2,2,64,512]{3,2,1,0:T(8,128)(2,1)S(1)}, bf16[2,2,64,512]{3,2,1,0:T(8,128)(2,1)S(1)}, u32[]{:S(2)}, u32[]{:S(2)}) collective-permute-start(bf16[2,2,64,512]{3,2,1,0:T(8,128)(2,1)S(1)} %pack_other_core.1), channel_id=1, source_target_pairs={{0,4},{4,0},{8,12},{12,8},{16,20},{20,16},{24,28},{28,24},{1,5},{5... | collective-permute-start | bytes 786440 | tf_op jit(solution)/shard_map/ppermute | solution.py:541
  15.4 1.8 %collective-permute-start.3 = (bf16[4,64,384]{2,1,0:T(8,128)(2,1)S(1)}, bf16[4,64,384]{2,1,0:T(8,128)(2,1)S(1)}, u32[]{:S(2)}, u32[]{:S(2)}) collective-permute-start(bf16[4,64,384]{2,1,0:T(8,128)(2,1)S(1)} %get-tuple-element.78), channel_id=1, source_target_pairs={{0,4},{4,0},{8,12},{12,8},{16,20},{20,16},{24,28},{28,24},{1,5},{5... | collective-permute-start | bytes 589832 | tf_op jit(solution)/shard_map/ppermute | solution.py:541
  15.9 1.6 %collective-permute-start.4 = (bf16[4,64,384]{2,1,0:T(8,128)(2,1)S(1)}, bf16[4,64,384]{2,1,0:T(8,128)(2,1)S(1)}, u32[]{:S(2)}, u32[]{:S(2)}) collective-permute-start(bf16[4,64,384]{2,1,0:T(8,128)(2,1)S(1)} %get-tuple-element.79), channel_id=1, source_target_pairs={{0,4},{4,0},{8,12},{12,8},{16,20},{20,16},{24,28},{28,24},{1,5},{5... | collective-permute-start | bytes 589832 | tf_op jit(solution)/shard_map/ppermute | solution.py:541
  21.9 3.1 %collective-permute-start.8 = (bf16[4,64,1280]{2,1,0:T(8,128)(2,1)S(1)}, bf16[4,64,1280]{2,1,0:T(8,128)(2,1)S(1)}, u32[]{:S(2)}, u32[]{:S(2)}) collective-permute-start(bf16[4,64,1280]{2,1,0:T(8,128)(2,1)S(1)} %get-tuple-element.103), channel_id=1, source_target_pairs={{0,4},{4,0},{8,12},{12,8},{16,20},{20,16},{24,28},{28,24},{1,5},{5... | collective-permute-start | bytes 1966088 | tf_op jit(solution)/shard_map/ppermute | solution.py:541
  22.6 6.5 %collective-permute-start.7 = (bf16[4,64,512]{2,1,0:T(8,128)(2,1)S(1)}, bf16[4,64,512]{2,1,0:T(8,128)(2,1)S(1)}, u32[]{:S(2)}, u32[]{:S(2)}) collective-permute-start(bf16[4,64,512]{2,1,0:T(8,128)(2,1)S(1)} %get-tuple-element.93), channel_id=1, source_target_pairs={{0,4},{4,0},{8,12},{12,8},{16,20},{20,16},{24,28},{28,24},{1,5},{5... | collective-permute-start | bytes 786440 | tf_op jit(solution)/shard_map/ppermute | solution.py:541
  23.2 7.7 %collective-permute-start.10 = (bf16[4,32,768]{2,1,0:T(8,128)(2,1)S(1)}, bf16[4,32,768]{2,1,0:T(8,128)(2,1)S(1)}, u32[]{:S(2)}, u32[]{:S(2)}) collective-permute-start(bf16[4,32,768]{2,1,0:T(8,128)(2,1)S(1)} %get-tuple-element.108), channel_id=1, source_target_pairs={{0,1},{1,0},{2,3},{3,2},{4,5},{5,4},{6,7},{7,6},{8,9},{9,8},{10,11... | collective-permute-start | bytes 589832 | tf_op jit(solution)/shard_map/ppermute | solution.py:541
  25.2 7.8 %collective-permute-start.9 = (bf16[4,32,512]{2,1,0:T(8,128)(2,1)S(1)}, bf16[4,32,512]{2,1,0:T(8,128)(2,1)S(1)}, u32[]{:S(2)}, u32[]{:S(2)}) collective-permute-start(bf16[4,32,512]{2,1,0:T(8,128)(2,1)S(1)} %get-tuple-element.105), channel_id=1, source_target_pairs={{0,1},{1,0},{2,3},{3,2},{4,5},{5,4},{6,7},{7,6},{8,9},{9,8},{10,11... | collective-permute-start | bytes 393224 | tf_op jit(solution)/shard_map/ppermute | solution.py:541
  26.1 10.0 %collective-permute-start.14 = (bf16[64,768]{1,0:T(8,128)(2,1)S(1)}, bf16[64,768]{1,0:T(8,128)(2,1)S(1)}, u32[]{:S(2)}, u32[]{:S(2)}) collective-permute-start(bf16[64,768]{1,0:T(8,128)(2,1)S(1)} %get-tuple-element.114), channel_id=1, source_target_pairs={{0,24},{4,28},{8,16},{12,20},{16,8},{20,12},{24,0},{28,4},{1,25},{... | collective-permute-start | bytes 294920 | tf_op jit(solution)/shard_map/ppermute | solution.py:541
  28.6 8.0 %collective-permute-start.15 = (bf16[64,768]{1,0:T(8,128)(2,1)S(1)}, bf16[64,768]{1,0:T(8,128)(2,1)S(1)}, u32[]{:S(2)}, u32[]{:S(2)}) collective-permute-start(bf16[64,768]{1,0:T(8,128)(2,1)S(1)} %get-tuple-element.115), channel_id=1, source_target_pairs={{0,16},{4,20},{8,24},{12,28},{16,0},{20,4},{24,8},{28,12},{1,17},{... | collective-permute-start | bytes 294920 | tf_op jit(solution)/shard_map/ppermute | solution.py:541
  29.1 7.5 %collective-permute-start.16 = (bf16[64,768]{1,0:T(8,128)(2,1)S(1)}, bf16[64,768]{1,0:T(8,128)(2,1)S(1)}, u32[]{:S(2)}, u32[]{:S(2)}) collective-permute-start(bf16[64,768]{1,0:T(8,128)(2,1)S(1)} %get-tuple-element.116), channel_id=1, source_target_pairs={{0,8},{4,12},{8,0},{12,4},{16,24},{20,28},{24,16},{28,20},{1,9},{5... | collective-permute-start | bytes 294920 | tf_op jit(solution)/shard_map/ppermute | solution.py:541
  33.0 7.8 %collective-permute-start.11 = (bf16[32,1280]{1,0:T(8,128)(2,1)S(1)}, bf16[32,1280]{1,0:T(8,128)(2,1)S(1)}, u32[]{:S(2)}, u32[]{:S(2)}) collective-permute-start(bf16[32,1280]{1,0:T(8,128)(2,1)S(1)} %get-tuple-element.110), channel_id=1, source_target_pairs={{0,24},{4,28},{8,16},{12,20},{16,8},{20,12},{24,0},{28,4},{1,25},{... | collective-permute-start | bytes 245768 | tf_op jit(solution)/shard_map/ppermute | solution.py:541
  35.7 5.1 %collective-permute-start.12 = (bf16[32,1280]{1,0:T(8,128)(2,1)S(1)}, bf16[32,1280]{1,0:T(8,128)(2,1)S(1)}, u32[]{:S(2)}, u32[]{:S(2)}) collective-permute-start(bf16[32,1280]{1,0:T(8,128)(2,1)S(1)} %get-tuple-element.111), channel_id=1, source_target_pairs={{0,16},{4,20},{8,24},{12,28},{16,0},{20,4},{24,8},{28,12},{1,17},{... | collective-permute-start | bytes 245768 | tf_op jit(solution)/shard_map/ppermute | solution.py:541
  36.2 4.6 %collective-permute-start.13 = (bf16[32,1280]{1,0:T(8,128)(2,1)S(1)}, bf16[32,1280]{1,0:T(8,128)(2,1)S(1)}, u32[]{:S(2)}, u32[]{:S(2)}) collective-permute-start(bf16[32,1280]{1,0:T(8,128)(2,1)S(1)} %get-tuple-element.112), channel_id=1, source_target_pairs={{0,8},{4,12},{8,0},{12,4},{16,24},{20,28},{24,16},{28,20},{1,9},{5... | collective-permute-start | bytes 245768 | tf_op jit(solution)/shard_map/ppermute | solution.py:541
  36.6 4.2 %collective-permute-start.17 = (bf16[32,768]{1,0:T(8,128)(2,1)S(1)}, bf16[32,768]{1,0:T(8,128)(2,1)S(1)}, u32[]{:S(2)}, u32[]{:S(2)}) collective-permute-start(bf16[32,768]{1,0:T(8,128)(2,1)S(1)} %get-tuple-element.118), channel_id=1, source_target_pairs={{0,1},{1,0},{2,3},{3,2},{4,5},{5,4},{6,7},{7,6},{8,9},{9,8},{10,11... | collective-permute-start | bytes 147464 | tf_op jit(solution)/shard_map/ppermute | solution.py:541
  40.8 7.4 %collective-permute-start.21 = (bf16[32,2048]{1,0:T(8,128)(2,1)S(1)}, bf16[32,2048]{1,0:T(8,128)(2,1)S(1)}, u32[]{:S(2)}, u32[]{:S(2)}) collective-permute-start(bf16[32,2048]{1,0:T(8,128)(2,1)S(1)} %join_terms.1.kept_ref), channel_id=1, source_target_pairs={{0,2},{1,3},{2,0},{3,1},{4,6},{5,7},{6,4},{7,5},{8,10},{9,11},{10,... | collective-permute-start | bytes 393224 | tf_op jit(solution)/shard_map/ppermute | solution.py:541
  43.7 6.0 %collective-permute-start.18 = (bf16[128,512]{1,0:T(8,128)(2,1)S(1)}, bf16[128,512]{1,0:T(8,128)(2,1)S(1)}, u32[]{:S(2)}, u32[]{:S(2)}) collective-permute-start(bf16[128,512]{1,0:T(8,128)(2,1)S(1)} %get-tuple-element.120), channel_id=1, source_target_pairs={{0,24},{4,28},{8,16},{12,20},{16,8},{20,12},{24,0},{28,4},{1,25},{... | collective-permute-start | bytes 393224 | tf_op jit(solution)/shard_map/ppermute | solution.py:541
  46.1 5.0 %collective-permute-start.19 = (bf16[128,512]{1,0:T(8,128)(2,1)S(1)}, bf16[128,512]{1,0:T(8,128)(2,1)S(1)}, u32[]{:S(2)}, u32[]{:S(2)}) collective-permute-start(bf16[128,512]{1,0:T(8,128)(2,1)S(1)} %get-tuple-element.121), channel_id=1, source_target_pairs={{0,16},{4,20},{8,24},{12,28},{16,0},{20,4},{24,8},{28,12},{1,17},{... | collective-permute-start | bytes 393224 | tf_op jit(solution)/shard_map/ppermute | solution.py:541
  46.6 5.0 %collective-permute-start.20 = (bf16[128,512]{1,0:T(8,128)(2,1)S(1)}, bf16[128,512]{1,0:T(8,128)(2,1)S(1)}, u32[]{:S(2)}, u32[]{:S(2)}) collective-permute-start(bf16[128,512]{1,0:T(8,128)(2,1)S(1)} %get-tuple-element.122), channel_id=1, source_target_pairs={{0,8},{4,12},{8,0},{12,4},{16,24},{20,28},{24,16},{28,20},{1,9},{5... | collective-permute-start | bytes 393224 | tf_op jit(solution)/shard_map/ppermute | solution.py:541
  48.3 5.0 %collective-permute-start.22 = (bf16[32,2048]{1,0:T(8,128)(2,1)S(1)}, bf16[32,2048]{1,0:T(8,128)(2,1)S(1)}, u32[]{:S(2)}, u32[]{:S(2)}) collective-permute-start(bf16[32,2048]{1,0:T(8,128)(2,1)S(1)} %add_pairs.1.held_ref), channel_id=1, source_target_pairs={{0,1},{1,0},{2,3},{3,2},{4,5},{5,4},{6,7},{7,6},{8,9},{9,8},{10,11... | collective-permute-start | bytes 393224 | tf_op jit(solution)/shard_map/ppermute | solution.py:541

commit v23 on v20

--- a/solution.py
+++ b/solution.py
@@ -683,7 +683,6 @@
             [(VMEM, back_keep), (VMEM, swap(back_send, "seq", 1))],
             [((2 * share, width), BF16)] * 4,
         )
-        row_kept, *back = lax.optimization_barrier((row_kept, *back))
         joint = (row_share // 2, FIRST_PART + row_width)
         first_owned, *off = call(
             pair_kernel,

time: 53.8 us -> 54 us (level)
  transfers between devices with their start and end apart: 23 -> 23, of which waited for: 13 -> 14; matrix products, arithmetic and copies ran while one was open for 0% -> 0% of each run, Pallas kernels for 19% -> 18%
where the time goes in v23:
time: 54 us; the launch traced here: 53.8 us
  starting transfers between devices  25.9 us (48%)
  Pallas kernels  15.3 us (28%)
  waiting for transfers between devices  11.9 us (22%)
  between operations  0.77 us (1%)
    ppermute x23, starting transfers between devices, swap(): return lax.ppermute(array, axis, [(i, i ^ bits) for i in range(count)])  25.9 us
    pallas_call x15, Pallas kernels, call(): pl.pallas_call(kernel, out_shape=outs, in_specs=[spec for spec, _ in ins]...  15.3 us
    ppermute x23, waiting for transfers between devices, swap(): return lax.ppermute(array, axis, [(i, i ^ bits) for i in range(count)])  11.9 us
  transfers between devices with their start and end apart: 23, of which 14 were waited for; matrix products, arithmetic and copies ran while one was open for 0% of the time, Pallas kernels for 18%

profile of v23, /device:TPU:0, one launch (start us, length us, event | category | flops | bytes accessed | tf_op | source)
XLA Modules:
  0.0 53.8 jit_solution(17057285389302154414)
XLA Ops:
  0.6 1.4 %pack_columns.1 = (bf16[2,2,64,512]{3,2,1,0:T(8,128)(2,1)S(1)}, bf16[2,64,512]{2,1,0:T(8,128)(2,1)S(1)}, bf16[2,128,512]{2,1,0:T(8,128)(2,1)S(1)}, bf16[2,128,512]{2,1,0:T(8,128)(2,1)S(1)}) custom-call(bf16[512,512]{1,0:T(8,128)(2,1)} %bitcast.9, bf16[512,512]{1,0:T(8,128)(2,1)} %bitcast.11), custom_call_target="tpu_custom_call" | custom-call | tf_op jit(solution)/shard_map/pack_columns/pallas_call | solution.py:527
  2.0 0.5 collective-permute-start.2
  2.5 2.6 %collective-permute-start = (bf16[2,128,512]{2,1,0:T(8,128)(2,1)S(1)}, bf16[2,128,512]{2,1,0:T(8,128)(2,1)S(1)}, u32[]{:S(2)}, u32[]{:S(2)}) collective-permute-start(bf16[2,128,512]{2,1,0:T(8,128)(2,1)S(1)} %get-tuple-element.61), channel_id=1, source_target_pairs={{0,16},{4,20},{8,24},{12,28},{16,0},{20,4},{24,8},{28,12},{1,17},{... | collective-permute-start | bytes 786440 | tf_op jit(solution)/shard_map/ppermute | solution.py:541
  5.1 1.5 %collective-permute-start.1 = (bf16[2,128,512]{2,1,0:T(8,128)(2,1)S(1)}, bf16[2,128,512]{2,1,0:T(8,128)(2,1)S(1)}, u32[]{:S(2)}, u32[]{:S(2)}) collective-permute-start(bf16[2,128,512]{2,1,0:T(8,128)(2,1)S(1)} %get-tuple-element.62), channel_id=1, source_target_pairs={{0,8},{4,12},{8,0},{12,4},{16,24},{20,28},{24,16},{28,20},{1,9},{5... | collective-permute-start | bytes 786440 | tf_op jit(solution)/shard_map/ppermute | solution.py:541
  6.6 1.0 %collective-permute-start.3 = (bf16[2,2,64,512]{3,2,1,0:T(8,128)(2,1)S(1)}, bf16[2,2,64,512]{3,2,1,0:T(8,128)(2,1)S(1)}, u32[]{:S(2)}, u32[]{:S(2)}) collective-permute-start(bf16[2,2,64,512]{3,2,1,0:T(8,128)(2,1)S(1)} %pack_corner.1), channel_id=1, source_target_pairs={{0,24},{4,28},{8,16},{12,20},{16,8},{20,12},{24,0},{28,4},{1,25},{... | collective-permute-start | bytes 786440 | tf_op jit(solution)/shard_map/ppermute | solution.py:541
  7.6 7.6 %row_heads.1 = (bf16[4,64,384]{2,1,0:T(8,128)(2,1)S(1)}, bf16[4,64,384]{2,1,0:T(8,128)(2,1)S(1)}, bf16[4,64,384]{2,1,0:T(8,128)(2,1)S(1)}, bf16[4,64,384]{2,1,0:...) custom-call(bf16[512,512]{1,0:T(8,128)(2,1)} %bitcast.10, ...), custom_call_target="tpu_custom_call" | custom-call | tf_op jit(solution)/shard_map/row_heads/pallas_call | solution.py:527
  15.2 0.0 copy-start
  15.3 0.1 collective-permute-start.4
  15.4 0.5 collective-permute-start.5
  15.9 0.1 collective-permute-start.6
  16.0 1.2 %collective-permute-done.5.got_1 = bf16[4,64,384]{2,1,0:T(8,128)(2,1)S(1)} collective-permute-done((bf16[4,64,384]{2,1,0:T(8,128)(2,1)S(1)}, bf16[4,64,384]{2,1,0:T(8,128)(2,1)S(1)}, u32[]{:S(2)}, u32[]{:S(2)}) %collective-permute-start.5) | collective-permute-done | bytes 196640 | tf_op jit(solution)/shard_map/ppermute | solution.py:541
  17.2 0.3 collective-permute-done.6.got_2
  17.5 0.1 row_add_cores.1
  17.6 1.2 %collective-permute-done.3.corner_ref = bf16[2,2,64,512]{3,2,1,0:T(8,128)(2,1)S(1)} collective-permute-done((bf16[2,2,64,512]{3,2,1,0:T(8,128)(2,1)S(1)}, bf16[2,2,64,512]{3,2,1,0:T(8,128)(2,1)S(1)}, u32[]{:S(2)}, u32[]{:S(2)}) %collective-permute-start.3) | collective-permute-done | bytes 262176 | tf_op jit(solution)/shard_map/ppermute | solution.py:541
  18.8 3.1 %column_heads.1 = (bf16[4,64,1280]{2,1,0:T(8,128)(2,1)S(1)}, bf16[4,64,1280]{2,1,0:T(8,128)(2,1)S(1)}, bf16[512,768]{1,0:T(8,128)(2,1)S(1)}) custom-call(bf16[512,512]{1,0:T(8,128)(2,1)S(1)} %get-tuple-element.70.x_ref, bf16[512,512]{1,0:T(8,128)(2,1)S(1)} %get-tuple-element.71.cot_ref, bf16[2,2,64,512]{3,2,1,0:T(8,128)(2,1)S(1)} %collective-permute-done.2.swapped_ref, ...), custom_call_target="tpu_custom_call" | custom-call | tf_op jit(solution)/shard_map/column_heads/pallas_call | solution.py:527
  21.9 0.1 collective-permute-start.8
  22.0 1.9 %collective-permute-start.10 = (bf16[4,32,768]{2,1,0:T(8,128)(2,1)S(1)}, bf16[4,32,768]{2,1,0:T(8,128)(2,1)S(1)}, u32[]{:S(2)}, u32[]{:S(2)}) collective-permute-start(bf16[4,32,768]{2,1,0:T(8,128)(2,1)S(1)} %get-tuple-element.98), channel_id=1, source_target_pairs={{0,1},{1,0},{2,3},{3,2},{4,5},{5,4},{6,7},{7,6},{8,9},{9,8},{10,11... | collective-permute-start | bytes 589832 | tf_op jit(solution)/shard_map/ppermute | solution.py:541
  23.9 0.6 %column_grad_hidden.1 = (bf16[4,64,512]{2,1,0:T(8,128)(2,1)S(1)}, bf16[4,64,512]{2,1,0:T(8,128)(2,1)S(1)}) custom-call(bf16[512,768]{1,0:T(8,128)(2,1)S(1)} %get-tuple-element.84.grads_ref, bf16[512,768]{1,0:T(8,128)(2,1)S(1)} %get-tuple-element.80.w_ref), custom_call_target="tpu_custom_call" | custom-call | tf_op jit(solution)/shard_map/column_grad_hidden/pallas_call | solution.py:527
  24.5 0.2 collective-permute-start.7
  24.7 0.2 column_add_cores.1
  24.9 2.5 %collective-permute-start.14 = (bf16[64,896]{1,0:T(8,128)(2,1)S(1)}, bf16[64,896]{1,0:T(8,128)(2,1)S(1)}, u32[]{:S(2)}, u32[]{:S(2)}) collective-permute-start(bf16[64,896]{1,0:T(8,128)(2,1)S(1)} %get-tuple-element.104), channel_id=1, source_target_pairs={{0,24},{4,28},{8,16},{12,20},{16,8},{20,12},{24,0},{28,4},{1,25},{... | collective-permute-start | bytes 344072 | tf_op jit(solution)/shard_map/ppermute | solution.py:541
  27.4 0.5 collective-permute-start.15
  27.9 1.2 %collective-permute-start.9 = (bf16[4,32,384]{2,1,0:T(8,128)(2,1)S(1)}, bf16[4,32,384]{2,1,0:T(8,128)(2,1)S(1)}, u32[]{:S(2)}, u32[]{:S(2)}) collective-permute-start(bf16[4,32,384]{2,1,0:T(8,128)(2,1)S(1)} %get-tuple-element.95), channel_id=1, source_target_pairs={{0,1},{1,0},{2,3},{3,2},{4,5},{5,4},{6,7},{7,6},{8,9},{9,8},{10,11... | collective-permute-start | bytes 294920 | tf_op jit(solution)/shard_map/ppermute | solution.py:541
  29.1 0.3 collective-permute-done.10.row_got
  29.4 1.8 %collective-permute-start.16 = (bf16[64,896]{1,0:T(8,128)(2,1)S(1)}, bf16[64,896]{1,0:T(8,128)(2,1)S(1)}, u32[]{:S(2)}, u32[]{:S(2)}) collective-permute-start(bf16[64,896]{1,0:T(8,128)(2,1)S(1)} %get-tuple-element.106), channel_id=1, source_target_pairs={{0,8},{4,12},{8,0},{12,4},{16,24},{20,28},{24,16},{28,20},{1,9},{5... | collective-permute-start | bytes 344072 | tf_op jit(solution)/shard_map/ppermute | solution.py:541
  31.2 1.3 %collective-permute-done.9.got_ref = bf16[4,32,384]{2,1,0:T(8,128)(2,1)S(1)} collective-permute-done((bf16[4,32,384]{2,1,0:T(8,128)(2,1)S(1)}, bf16[4,32,384]{2,1,0:T(8,128)(2,1)S(1)}, u32[]{:S(2)}, u32[]{:S(2)}) %collective-permute-start.9) | collective-permute-done | bytes 98336 | tf_op jit(solution)/shard_map/ppermute | solution.py:541
  32.5 0.1 first_add_pair.1
  32.6 1.6 %collective-permute-start.11 = (bf16[32,1152]{1,0:T(8,128)(2,1)S(1)}, bf16[32,1152]{1,0:T(8,128)(2,1)S(1)}, u32[]{:S(2)}, u32[]{:S(2)}) collective-permute-start(bf16[32,1152]{1,0:T(8,128)(2,1)S(1)} %get-tuple-element.100), channel_id=1, source_target_pairs={{0,24},{4,28},{8,16},{12,20},{16,8},{20,12},{24,0},{28,4},{1,25},{... | collective-permute-start | bytes 221192 | tf_op jit(solution)/shard_map/ppermute | solution.py:541
  34.2 0.5 collective-permute-start.12
  34.7 1.4 %collective-permute-start.13 = (bf16[32,1152]{1,0:T(8,128)(2,1)S(1)}, bf16[32,1152]{1,0:T(8,128)(2,1)S(1)}, u32[]{:S(2)}, u32[]{:S(2)}) collective-permute-start(bf16[32,1152]{1,0:T(8,128)(2,1)S(1)} %get-tuple-element.102), channel_id=1, source_target_pairs={{0,8},{4,12},{8,0},{12,4},{16,24},{20,28},{24,16},{28,20},{1,9},{5... | collective-permute-start | bytes 221192 | tf_op jit(solution)/shard_map/ppermute | solution.py:541
  36.1 0.1 second_add_chips.1
  36.2 1.2 %collective-permute-start.17 = (bf16[32,896]{1,0:T(8,128)(2,1)S(1)}, bf16[32,896]{1,0:T(8,128)(2,1)S(1)}, u32[]{:S(2)}, u32[]{:S(2)}) collective-permute-start(bf16[32,896]{1,0:T(8,128)(2,1)S(1)} %get-tuple-element.108), channel_id=1, source_target_pairs={{0,1},{1,0},{2,3},{3,2},{4,5},{5,4},{6,7},{7,6},{8,9},{9,8},{10,11... | collective-permute-start | bytes 172040 | tf_op jit(solution)/shard_map/ppermute | solution.py:541
  37.5 1.0 %collective-permute-done.11.got_1 = bf16[32,1152]{1,0:T(8,128)(2,1)S(1)} collective-permute-done((bf16[32,1152]{1,0:T(8,128)(2,1)S(1)}, bf16[32,1152]{1,0:T(8,128)(2,1)S(1)}, u32[]{:S(2)}, u32[]{:S(2)}) %collective-permute-start.11) | collective-permute-done | bytes 73760 | tf_op jit(solution)/shard_map/ppermute | solution.py:541
  38.5 0.4 collective-permute-done.12.got_2
  38.9 0.1 collective-permute-done.13.got_3
  39.1 1.4 %collective-permute-done.17.got_ref = bf16[32,896]{1,0:T(8,128)(2,1)S(1)} collective-permute-done((bf16[32,896]{1,0:T(8,128)(2,1)S(1)}, bf16[32,896]{1,0:T(8,128)(2,1)S(1)}, u32[]{:S(2)}, u32[]{:S(2)}) %collective-permute-start.17) | collective-permute-done | bytes 57376 | tf_op jit(solution)/shard_map/ppermute | solution.py:541
  40.5 2.8 %collective-permute-start.21 = (bf16[32,2048]{1,0:T(8,128)(2,1)S(1)}, bf16[32,2048]{1,0:T(8,128)(2,1)S(1)}, u32[]{:S(2)}, u32[]{:S(2)}) collective-permute-start(bf16[32,2048]{1,0:T(8,128)(2,1)S(1)} %join_terms.1.kept_ref), channel_id=1, source_target_pairs={{0,2},{1,3},{2,0},{3,1},{4,6},{5,7},{6,4},{7,5},{8,10},{9,11},{10,... | collective-permute-start | bytes 393224 | tf_op jit(solution)/shard_map/ppermute | solution.py:541
  43.3 1.5 %collective-permute-start.18 = (bf16[128,512]{1,0:T(8,128)(2,1)S(1)}, bf16[128,512]{1,0:T(8,128)(2,1)S(1)}, u32[]{:S(2)}, u32[]{:S(2)}) collective-permute-start(bf16[128,512]{1,0:T(8,128)(2,1)S(1)} %get-tuple-element.110), channel_id=1, source_target_pairs={{0,24},{4,28},{8,16},{12,20},{16,8},{20,12},{24,0},{28,4},{1,25},{... | collective-permute-start | bytes 393224 | tf_op jit(solution)/shard_map/ppermute | solution.py:541
  44.8 0.4 collective-permute-start.19
  45.2 1.6 %collective-permute-start.20 = (bf16[128,512]{1,0:T(8,128)(2,1)S(1)}, bf16[128,512]{1,0:T(8,128)(2,1)S(1)}, u32[]{:S(2)}, u32[]{:S(2)}) collective-permute-start(bf16[128,512]{1,0:T(8,128)(2,1)S(1)} %get-tuple-element.112), channel_id=1, source_target_pairs={{0,8},{4,12},{8,0},{12,4},{16,24},{20,28},{24,16},{28,20},{1,9},{5... | collective-permute-start | bytes 393224 | tf_op jit(solution)/shard_map/ppermute | solution.py:541
  46.8 1.1 %collective-permute-done.21.got_ref = bf16[32,2048]{1,0:T(8,128)(2,1)S(1)} collective-permute-done((bf16[32,2048]{1,0:T(8,128)(2,1)S(1)}, bf16[32,2048]{1,0:T(8,128)(2,1)S(1)}, u32[]{:S(2)}, u32[]{:S(2)}) %collective-permute-start.21) | collective-permute-done | bytes 131104 | tf_op jit(solution)/shard_map/ppermute | solution.py:541
  47.9 0.4 collective-permute-start.22
  48.4 0.9 %collective-permute-done.18.got_1 = bf16[128,512]{1,0:T(8,128)(2,1)S(1)} collective-permute-done((bf16[128,512]{1,0:T(8,128)(2,1)S(1)}, bf16[128,512]{1,0:T(8,128)(2,1)S(1)}, u32[]{:S(2)}, u32[]{:S(2)}) %collective-permute-start.18) | collective-permute-done | bytes 131104 | tf_op jit(solution)/shard_map/ppermute | solution.py:541
  49.3 1.3 %collective-permute-done.19.got_2 = bf16[128,512]{1,0:T(8,128)(2,1)S(1)} collective-permute-done((bf16[128,512]{1,0:T(8,128)(2,1)S(1)}, bf16[128,512]{1,0:T(8,128)(2,1)S(1)}, u32[]{:S(2)}, u32[]{:S(2)}) %collective-permute-start.19) | collective-permute-done | bytes 131104 | tf_op jit(solution)/shard_map/ppermute | solution.py:541
  50.6 0.4 collective-permute-done.20.got_3
  50.9 1.1 %input_grad.1 = bf16[512,512]{1,0:T(8,128)(2,1)} custom-call(f32[512,512]{1,0:T(8,128)S(1)} %get-tuple-element.67.base_ref, f32[512,512]{1,0:T(8,128)S(1)} %get-tuple-element.68.normed_ref, f32[512,1]{1,0:T(8,128)S(1)} %get-tuple-element.69.inverse_ref, f32[1,512]{1,0:T(1,128)S(1)} %bitcast.7, bf16[128,512]{1,0:T(8,128)(2,1)S(1)} %get-tuple-element.109.own_ref, ...), custom_call_target="tpu_custom_call" | custom-call | tf_op jit(solution)/shard_map/input_grad/pallas_call | solution.py:527
  52.1 0.9 %collective-permute-done.22.got_ref = bf16[32,2048]{1,0:T(8,128)(2,1)S(1)} collective-permute-done((bf16[32,2048]{1,0:T(8,128)(2,1)S(1)}, bf16[32,2048]{1,0:T(8,128)(2,1)S(1)}, u32[]{:S(2)}, u32[]{:S(2)}) %collective-permute-start.22) | collective-permute-done | bytes 131104 | tf_op jit(solution)/shard_map/ppermute | solution.py:541
  53.0 0.9 %result.1 = (f32[64,1536]{1,0:T(8,128)}, f32[64,512]{1,0:T(8,128)}, f32[1,64]{1,0:T(1,128)}) custom-call(bf16[32,2048]{1,0:T(8,128)(2,1)S(1)} %add_pairs.1.held_ref, bf16[32,2048]{1,0:T(8,128)(2,1)S(1)} %collective-permute-done.22.got_ref, bf16[64,1536]{1,0:T(8,128)(2,1)S(1)} %get-tuple-element.114.w_ref, f32[1,512]{1,0:T(1,128)S(1)} %bitcast.8), custom_call_target="tpu_custom_call" | custom-call | tf_op jit(solution)/shard_map/result/pallas_call | solution.py:527
  (15 shorter events, 0.2 us)
Async XLA Ops:
  2.0 4.6 %collective-permute-start.2 = (bf16[2,2,64,512]{3,2,1,0:T(8,128)(2,1)S(1)}, bf16[2,2,64,512]{3,2,1,0:T(8,128)(2,1)S(1)}, u32[]{:S(2)}, u32[]{:S(2)}) collective-permute-start(bf16[2,2,64,512]{3,2,1,0:T(8,128)(2,1)S(1)} %get-tuple-element.64), channel_id=1, source_target_pairs={{0,4},{4,0},{8,12},{12,8},{16,20},{20,16},{24,28},{28,24},{1,5},{5... | collective-permute-start | bytes 786440 | tf_op jit(solution)/shard_map/ppermute | solution.py:541
  2.5 12.7 %collective-permute-start = (bf16[2,128,512]{2,1,0:T(8,128)(2,1)S(1)}, bf16[2,128,512]{2,1,0:T(8,128)(2,1)S(1)}, u32[]{:S(2)}, u32[]{:S(2)}) collective-permute-start(bf16[2,128,512]{2,1,0:T(8,128)(2,1)S(1)} %get-tuple-element.61), channel_id=1, source_target_pairs={{0,16},{4,20},{8,24},{12,28},{16,0},{20,4},{24,8},{28,12},{1,17},{... | collective-permute-start | bytes 786440 | tf_op jit(solution)/shard_map/ppermute | solution.py:541
  5.1 10.2 %collective-permute-start.1 = (bf16[2,128,512]{2,1,0:T(8,128)(2,1)S(1)}, bf16[2,128,512]{2,1,0:T(8,128)(2,1)S(1)}, u32[]{:S(2)}, u32[]{:S(2)}) collective-permute-start(bf16[2,128,512]{2,1,0:T(8,128)(2,1)S(1)} %get-tuple-element.62), channel_id=1, source_target_pairs={{0,8},{4,12},{8,0},{12,4},{16,24},{20,28},{24,16},{28,20},{1,9},{5... | collective-permute-start | bytes 786440 | tf_op jit(solution)/shard_map/ppermute | solution.py:541
  6.6 12.2 %collective-permute-start.3 = (bf16[2,2,64,512]{3,2,1,0:T(8,128)(2,1)S(1)}, bf16[2,2,64,512]{3,2,1,0:T(8,128)(2,1)S(1)}, u32[]{:S(2)}, u32[]{:S(2)}) collective-permute-start(bf16[2,2,64,512]{3,2,1,0:T(8,128)(2,1)S(1)} %pack_corner.1), channel_id=1, source_target_pairs={{0,24},{4,28},{8,16},{12,20},{16,8},{20,12},{24,0},{28,4},{1,25},{... | collective-permute-start | bytes 786440 | tf_op jit(solution)/shard_map/ppermute | solution.py:541
  15.2 3.6 %copy-start = (f32[512]{0:T(512)S(1)}, f32[512]{0:T(512)}, u32[]{:S(2)}) copy-start(f32[512]{0:T(512)} %param.6) | copy-start | bytes 6148
  15.3 3.5 %collective-permute-start.4 = (bf16[2,2,64,512]{3,2,1,0:T(8,128)(2,1)S(1)}, bf16[2,2,64,512]{3,2,1,0:T(8,128)(2,1)S(1)}, u32[]{:S(2)}, u32[]{:S(2)}) collective-permute-start(bf16[2,2,64,512]{3,2,1,0:T(8,128)(2,1)S(1)} %pack_other_core.1), channel_id=1, source_target_pairs={{0,4},{4,0},{8,12},{12,8},{16,20},{20,16},{24,28},{28,24},{1,5},{5... | collective-permute-start | bytes 786440 | tf_op jit(solution)/shard_map/ppermute | solution.py:541
  15.4 1.8 %collective-permute-start.5 = (bf16[4,64,384]{2,1,0:T(8,128)(2,1)S(1)}, bf16[4,64,384]{2,1,0:T(8,128)(2,1)S(1)}, u32[]{:S(2)}, u32[]{:S(2)}) collective-permute-start(bf16[4,64,384]{2,1,0:T(8,128)(2,1)S(1)} %get-tuple-element.77), channel_id=1, source_target_pairs={{0,4},{4,0},{8,12},{12,8},{16,20},{20,16},{24,28},{28,24},{1,5},{5... | collective-permute-start | bytes 589832 | tf_op jit(solution)/shard_map/ppermute | solution.py:541
  15.9 1.6 %collective-permute-start.6 = (bf16[4,64,384]{2,1,0:T(8,128)(2,1)S(1)}, bf16[4,64,384]{2,1,0:T(8,128)(2,1)S(1)}, u32[]{:S(2)}, u32[]{:S(2)}) collective-permute-start(bf16[4,64,384]{2,1,0:T(8,128)(2,1)S(1)} %get-tuple-element.78), channel_id=1, source_target_pairs={{0,4},{4,0},{8,12},{12,8},{16,20},{20,16},{24,28},{28,24},{1,5},{5... | collective-permute-start | bytes 589832 | tf_op jit(solution)/shard_map/ppermute | solution.py:541
  21.9 2.8 %collective-permute-start.8 = (bf16[4,64,1280]{2,1,0:T(8,128)(2,1)S(1)}, bf16[4,64,1280]{2,1,0:T(8,128)(2,1)S(1)}, u32[]{:S(2)}, u32[]{:S(2)}) collective-permute-start(bf16[4,64,1280]{2,1,0:T(8,128)(2,1)S(1)} %get-tuple-element.93), channel_id=1, source_target_pairs={{0,4},{4,0},{8,12},{12,8},{16,20},{20,16},{24,28},{28,24},{1,5},{5... | collective-permute-start | bytes 1966088 | tf_op jit(solution)/shard_map/ppermute | solution.py:541
  22.0 7.4 %collective-permute-start.10 = (bf16[4,32,768]{2,1,0:T(8,128)(2,1)S(1)}, bf16[4,32,768]{2,1,0:T(8,128)(2,1)S(1)}, u32[]{:S(2)}, u32[]{:S(2)}) collective-permute-start(bf16[4,32,768]{2,1,0:T(8,128)(2,1)S(1)} %get-tuple-element.98), channel_id=1, source_target_pairs={{0,1},{1,0},{2,3},{3,2},{4,5},{5,4},{6,7},{7,6},{8,9},{9,8},{10,11... | collective-permute-start | bytes 589832 | tf_op jit(solution)/shard_map/ppermute | solution.py:541
  24.5 13.0 %collective-permute-start.7 = (bf16[4,64,512]{2,1,0:T(8,128)(2,1)S(1)}, bf16[4,64,512]{2,1,0:T(8,128)(2,1)S(1)}, u32[]{:S(2)}, u32[]{:S(2)}) collective-permute-start(bf16[4,64,512]{2,1,0:T(8,128)(2,1)S(1)} %get-tuple-element.87), channel_id=1, source_target_pairs={{0,4},{4,0},{8,12},{12,8},{16,20},{20,16},{24,28},{28,24},{1,5},{5... | collective-permute-start | bytes 786440 | tf_op jit(solution)/shard_map/ppermute | solution.py:541
  24.9 9.3 %collective-permute-start.14 = (bf16[64,896]{1,0:T(8,128)(2,1)S(1)}, bf16[64,896]{1,0:T(8,128)(2,1)S(1)}, u32[]{:S(2)}, u32[]{:S(2)}) collective-permute-start(bf16[64,896]{1,0:T(8,128)(2,1)S(1)} %get-tuple-element.104), channel_id=1, source_target_pairs={{0,24},{4,28},{8,16},{12,20},{16,8},{20,12},{24,0},{28,4},{1,25},{... | collective-permute-start | bytes 344072 | tf_op jit(solution)/shard_map/ppermute | solution.py:541
  27.4 7.3 %collective-permute-start.15 = (bf16[64,896]{1,0:T(8,128)(2,1)S(1)}, bf16[64,896]{1,0:T(8,128)(2,1)S(1)}, u32[]{:S(2)}, u32[]{:S(2)}) collective-permute-start(bf16[64,896]{1,0:T(8,128)(2,1)S(1)} %get-tuple-element.105), channel_id=1, source_target_pairs={{0,16},{4,20},{8,24},{12,28},{16,0},{20,4},{24,8},{28,12},{1,17},{... | collective-permute-start | bytes 344072 | tf_op jit(solution)/shard_map/ppermute | solution.py:541
  27.9 4.6 %collective-permute-start.9 = (bf16[4,32,384]{2,1,0:T(8,128)(2,1)S(1)}, bf16[4,32,384]{2,1,0:T(8,128)(2,1)S(1)}, u32[]{:S(2)}, u32[]{:S(2)}) collective-permute-start(bf16[4,32,384]{2,1,0:T(8,128)(2,1)S(1)} %get-tuple-element.95), channel_id=1, source_target_pairs={{0,1},{1,0},{2,3},{3,2},{4,5},{5,4},{6,7},{7,6},{8,9},{9,8},{10,11... | collective-permute-start | bytes 294920 | tf_op jit(solution)/shard_map/ppermute | solution.py:541
  29.4 6.8 %collective-permute-start.16 = (bf16[64,896]{1,0:T(8,128)(2,1)S(1)}, bf16[64,896]{1,0:T(8,128)(2,1)S(1)}, u32[]{:S(2)}, u32[]{:S(2)}) collective-permute-start(bf16[64,896]{1,0:T(8,128)(2,1)S(1)} %get-tuple-element.106), channel_id=1, source_target_pairs={{0,8},{4,12},{8,0},{12,4},{16,24},{20,28},{24,16},{28,20},{1,9},{5... | collective-permute-start | bytes 344072 | tf_op jit(solution)/shard_map/ppermute | solution.py:541
  32.6 5.9 %collective-permute-start.11 = (bf16[32,1152]{1,0:T(8,128)(2,1)S(1)}, bf16[32,1152]{1,0:T(8,128)(2,1)S(1)}, u32[]{:S(2)}, u32[]{:S(2)}) collective-permute-start(bf16[32,1152]{1,0:T(8,128)(2,1)S(1)} %get-tuple-element.100), channel_id=1, source_target_pairs={{0,24},{4,28},{8,16},{12,20},{16,8},{20,12},{24,0},{28,4},{1,25},{... | collective-permute-start | bytes 221192 | tf_op jit(solution)/shard_map/ppermute | solution.py:541
  34.2 4.7 %collective-permute-start.12 = (bf16[32,1152]{1,0:T(8,128)(2,1)S(1)}, bf16[32,1152]{1,0:T(8,128)(2,1)S(1)}, u32[]{:S(2)}, u32[]{:S(2)}) collective-permute-start(bf16[32,1152]{1,0:T(8,128)(2,1)S(1)} %get-tuple-element.101), channel_id=1, source_target_pairs={{0,16},{4,20},{8,24},{12,28},{16,0},{20,4},{24,8},{28,12},{1,17},{... | collective-permute-start | bytes 221192 | tf_op jit(solution)/shard_map/ppermute | solution.py:541
  34.7 4.4 %collective-permute-start.13 = (bf16[32,1152]{1,0:T(8,128)(2,1)S(1)}, bf16[32,1152]{1,0:T(8,128)(2,1)S(1)}, u32[]{:S(2)}, u32[]{:S(2)}) collective-permute-start(bf16[32,1152]{1,0:T(8,128)(2,1)S(1)} %get-tuple-element.102), channel_id=1, source_target_pairs={{0,8},{4,12},{8,0},{12,4},{16,24},{20,28},{24,16},{28,20},{1,9},{5... | collective-permute-start | bytes 221192 | tf_op jit(solution)/shard_map/ppermute | solution.py:541
  36.2 4.2 %collective-permute-start.17 = (bf16[32,896]{1,0:T(8,128)(2,1)S(1)}, bf16[32,896]{1,0:T(8,128)(2,1)S(1)}, u32[]{:S(2)}, u32[]{:S(2)}) collective-permute-start(bf16[32,896]{1,0:T(8,128)(2,1)S(1)} %get-tuple-element.108), channel_id=1, source_target_pairs={{0,1},{1,0},{2,3},{3,2},{4,5},{5,4},{6,7},{7,6},{8,9},{9,8},{10,11... | collective-permute-start | bytes 172040 | tf_op jit(solution)/shard_map/ppermute | solution.py:541
  40.5 7.4 %collective-permute-start.21 = (bf16[32,2048]{1,0:T(8,128)(2,1)S(1)}, bf16[32,2048]{1,0:T(8,128)(2,1)S(1)}, u32[]{:S(2)}, u32[]{:S(2)}) collective-permute-start(bf16[32,2048]{1,0:T(8,128)(2,1)S(1)} %join_terms.1.kept_ref), channel_id=1, source_target_pairs={{0,2},{1,3},{2,0},{3,1},{4,6},{5,7},{6,4},{7,5},{8,10},{9,11},{10,... | collective-permute-start | bytes 393224 | tf_op jit(solution)/shard_map/ppermute | solution.py:541
  43.3 6.0 %collective-permute-start.18 = (bf16[128,512]{1,0:T(8,128)(2,1)S(1)}, bf16[128,512]{1,0:T(8,128)(2,1)S(1)}, u32[]{:S(2)}, u32[]{:S(2)}) collective-permute-start(bf16[128,512]{1,0:T(8,128)(2,1)S(1)} %get-tuple-element.110), channel_id=1, source_target_pairs={{0,24},{4,28},{8,16},{12,20},{16,8},{20,12},{24,0},{28,4},{1,25},{... | collective-permute-start | bytes 393224 | tf_op jit(solution)/shard_map/ppermute | solution.py:541
  44.8 5.8 %collective-permute-start.19 = (bf16[128,512]{1,0:T(8,128)(2,1)S(1)}, bf16[128,512]{1,0:T(8,128)(2,1)S(1)}, u32[]{:S(2)}, u32[]{:S(2)}) collective-permute-start(bf16[128,512]{1,0:T(8,128)(2,1)S(1)} %get-tuple-element.111), channel_id=1, source_target_pairs={{0,16},{4,20},{8,24},{12,28},{16,0},{20,4},{24,8},{28,12},{1,17},{... | collective-permute-start | bytes 393224 | tf_op jit(solution)/shard_map/ppermute | solution.py:541
  45.2 5.7 %collective-permute-start.20 = (bf16[128,512]{1,0:T(8,128)(2,1)S(1)}, bf16[128,512]{1,0:T(8,128)(2,1)S(1)}, u32[]{:S(2)}, u32[]{:S(2)}) collective-permute-start(bf16[128,512]{1,0:T(8,128)(2,1)S(1)} %get-tuple-element.112), channel_id=1, source_target_pairs={{0,8},{4,12},{8,0},{12,4},{16,24},{20,28},{24,16},{28,20},{1,9},{5... | collective-permute-start | bytes 393224 | tf_op jit(solution)/shard_map/ppermute | solution.py:541
  47.9 5.0 %collective-permute-start.22 = (bf16[32,2048]{1,0:T(8,128)(2,1)S(1)}, bf16[32,2048]{1,0:T(8,128)(2,1)S(1)}, u32[]{:S(2)}, u32[]{:S(2)}) collective-permute-start(bf16[32,2048]{1,0:T(8,128)(2,1)S(1)} %add_pairs.1.held_ref), channel_id=1, source_target_pairs={{0,1},{1,0},{2,3},{3,2},{4,5},{5,4},{6,7},{7,6},{8,9},{9,8},{10,11... | collective-permute-start | bytes 393224 | tf_op jit(solution)/shard_map/ppermute | solution.py:541

commit v24 on v22

--- a/solution.py
+++ b/solution.py
@@ -683,7 +683,6 @@
             [(VMEM, back_keep), (VMEM, swap(back_send, "seq", 1))],
             [((2 * share, width), BF16)] * 4,
         )
-        row_kept, *back = lax.optimization_barrier((row_kept, *back))
         joint = (row_share // 2, FIRST_PART + row_width)
         first_owned, *off = call(
             pair_kernel,

time: 54.4 us -> 54.2 us (level)
  waiting for transfers between devices: 12.6 us -> 11.2 us
  starting transfers between devices: 25.6 us -> 26.8 us
    ppermute x23, waiting for transfers between devices: 12.6 us -> 11.2 us  [swap(): return lax.ppermute(array, axis, [(i, i ^ bits) for i in range(count)])]
    ppermute x23, starting transfers between devices: 25.6 us -> 26.8 us  [swap(): return lax.ppermute(array, axis, [(i, i ^ bits) for i in range(count)])]
where the time goes in v24:
time: 54.2 us; the launch traced here: 54 us
  starting transfers between devices  26.8 us (49%)
  Pallas kernels  15.3 us (28%)
  waiting for transfers between devices  11.2 us (21%)
  between operations  0.77 us (1%)
    ppermute x23, starting transfers between devices, swap(): return lax.ppermute(array, axis, [(i, i ^ bits) for i in range(count)])  26.8 us
    pallas_call x15, Pallas kernels, call(): pl.pallas_call(kernel, out_shape=outs, in_specs=[spec for spec, _ in ins]...  15.3 us
    ppermute x23, waiting for transfers between devices, swap(): return lax.ppermute(array, axis, [(i, i ^ bits) for i in range(count)])  11.2 us
  transfers between devices with their start and end apart: 23, of which 11 were waited for; matrix products, arithmetic and copies ran while one was open for 0% of the time, Pallas kernels for 18%

profile of v24, /device:TPU:0, one launch (start us, length us, event | category | flops | bytes accessed | tf_op | source)
XLA Modules:
  0.0 54.0 jit_solution(11470850092505856477)
XLA Ops:
  0.6 1.4 %pack_columns.1 = (bf16[2,2,64,512]{3,2,1,0:T(8,128)(2,1)S(1)}, bf16[2,64,512]{2,1,0:T(8,128)(2,1)S(1)}, bf16[2,128,512]{2,1,0:T(8,128)(2,1)S(1)}, bf16[2,128,512]{2,1,0:T(8,128)(2,1)S(1)}) custom-call(bf16[512,512]{1,0:T(8,128)(2,1)} %bitcast.9, bf16[512,512]{1,0:T(8,128)(2,1)} %bitcast.11), custom_call_target="tpu_custom_call" | custom-call | tf_op jit(solution)/shard_map/pack_columns/pallas_call | solution.py:527
  2.0 0.5 collective-permute-start.2
  2.5 2.6 %collective-permute-start = (bf16[2,128,512]{2,1,0:T(8,128)(2,1)S(1)}, bf16[2,128,512]{2,1,0:T(8,128)(2,1)S(1)}, u32[]{:S(2)}, u32[]{:S(2)}) collective-permute-start(bf16[2,128,512]{2,1,0:T(8,128)(2,1)S(1)} %get-tuple-element.61), channel_id=1, source_target_pairs={{0,16},{4,20},{8,24},{12,28},{16,0},{20,4},{24,8},{28,12},{1,17},{... | collective-permute-start | bytes 786440 | tf_op jit(solution)/shard_map/ppermute | solution.py:541
  5.1 1.5 %collective-permute-start.1 = (bf16[2,128,512]{2,1,0:T(8,128)(2,1)S(1)}, bf16[2,128,512]{2,1,0:T(8,128)(2,1)S(1)}, u32[]{:S(2)}, u32[]{:S(2)}) collective-permute-start(bf16[2,128,512]{2,1,0:T(8,128)(2,1)S(1)} %get-tuple-element.62), channel_id=1, source_target_pairs={{0,8},{4,12},{8,0},{12,4},{16,24},{20,28},{24,16},{28,20},{1,9},{5... | collective-permute-start | bytes 786440 | tf_op jit(solution)/shard_map/ppermute | solution.py:541
  6.6 0.0 collective-permute-done.2.swapped_ref
  6.6 1.0 %collective-permute-start.3 = (bf16[2,2,64,512]{3,2,1,0:T(8,128)(2,1)S(1)}, bf16[2,2,64,512]{3,2,1,0:T(8,128)(2,1)S(1)}, u32[]{:S(2)}, u32[]{:S(2)}) collective-permute-start(bf16[2,2,64,512]{3,2,1,0:T(8,128)(2,1)S(1)} %pack_corner.1), channel_id=1, source_target_pairs={{0,24},{4,28},{8,16},{12,20},{16,8},{20,12},{24,0},{28,4},{1,25},{... | collective-permute-start | bytes 786440 | tf_op jit(solution)/shard_map/ppermute | solution.py:541
  7.6 7.6 %row_heads.1 = (bf16[4,64,384]{2,1,0:T(8,128)(2,1)S(1)}, bf16[4,64,384]{2,1,0:T(8,128)(2,1)S(1)}, bf16[4,64,384]{2,1,0:T(8,128)(2,1)S(1)}, bf16[4,64,384]{2,1,0:...) custom-call(bf16[512,512]{1,0:T(8,128)(2,1)} %bitcast.10, ...), custom_call_target="tpu_custom_call" | custom-call | tf_op jit(solution)/shard_map/row_heads/pallas_call | solution.py:527
  15.2 0.0 copy-start
  15.2 0.0 collective-permute-done.near_2
  15.3 0.1 collective-permute-start.4
  15.4 0.5 collective-permute-start.5
  15.9 0.1 collective-permute-start.6
  16.0 1.2 %collective-permute-done.5.got_1 = bf16[4,64,384]{2,1,0:T(8,128)(2,1)S(1)} collective-permute-done((bf16[4,64,384]{2,1,0:T(8,128)(2,1)S(1)}, bf16[4,64,384]{2,1,0:T(8,128)(2,1)S(1)}, u32[]{:S(2)}, u32[]{:S(2)}) %collective-permute-start.5) | collective-permute-done | bytes 196640 | tf_op jit(solution)/shard_map/ppermute | solution.py:541
  17.2 0.3 collective-permute-done.6.got_2
  17.5 0.1 row_add_cores.1
  17.6 1.2 %collective-permute-done.3.corner_ref = bf16[2,2,64,512]{3,2,1,0:T(8,128)(2,1)S(1)} collective-permute-done((bf16[2,2,64,512]{3,2,1,0:T(8,128)(2,1)S(1)}, bf16[2,2,64,512]{3,2,1,0:T(8,128)(2,1)S(1)}, u32[]{:S(2)}, u32[]{:S(2)}) %collective-permute-start.3) | collective-permute-done | bytes 262176 | tf_op jit(solution)/shard_map/ppermute | solution.py:541
  18.8 0.0 collective-permute-done.4.far_ref
  18.8 3.1 %column_heads.1 = (bf16[4,64,1280]{2,1,0:T(8,128)(2,1)S(1)}, bf16[4,64,1280]{2,1,0:T(8,128)(2,1)S(1)}, bf16[512,768]{1,0:T(8,128)(2,1)S(1)}) custom-call(bf16[512,512]{1,0:T(8,128)(2,1)S(1)} %get-tuple-element.70.x_ref, bf16[512,512]{1,0:T(8,128)(2,1)S(1)} %get-tuple-element.71.cot_ref, bf16[2,2,64,512]{3,2,1,0:T(8,128)(2,1)S(1)} %collective-permute-done.2.swapped_ref, ...), custom_call_target="tpu_custom_call" | custom-call | tf_op jit(solution)/shard_map/column_heads/pallas_call | solution.py:527
  21.9 0.1 collective-permute-start.8
  22.0 1.9 %collective-permute-start.10 = (bf16[4,32,768]{2,1,0:T(8,128)(2,1)S(1)}, bf16[4,32,768]{2,1,0:T(8,128)(2,1)S(1)}, u32[]{:S(2)}, u32[]{:S(2)}) collective-permute-start(bf16[4,32,768]{2,1,0:T(8,128)(2,1)S(1)} %get-tuple-element.98), channel_id=1, source_target_pairs={{0,1},{1,0},{2,3},{3,2},{4,5},{5,4},{6,7},{7,6},{8,9},{9,8},{10,11... | collective-permute-start | bytes 589832 | tf_op jit(solution)/shard_map/ppermute | solution.py:541
  23.9 0.6 %column_grad_hidden.1 = (bf16[4,64,512]{2,1,0:T(8,128)(2,1)S(1)}, bf16[4,64,512]{2,1,0:T(8,128)(2,1)S(1)}) custom-call(bf16[512,768]{1,0:T(8,128)(2,1)S(1)} %get-tuple-element.84.grads_ref, bf16[512,768]{1,0:T(8,128)(2,1)S(1)} %get-tuple-element.80.w_ref), custom_call_target="tpu_custom_call" | custom-call | tf_op jit(solution)/shard_map/column_grad_hidden/pallas_call | solution.py:527
  24.5 0.2 collective-permute-start.7
  24.7 0.2 column_add_cores.1
  24.9 1.2 %collective-permute-start.9 = (bf16[4,32,512]{2,1,0:T(8,128)(2,1)S(1)}, bf16[4,32,512]{2,1,0:T(8,128)(2,1)S(1)}, u32[]{:S(2)}, u32[]{:S(2)}) collective-permute-start(bf16[4,32,512]{2,1,0:T(8,128)(2,1)S(1)} %get-tuple-element.95), channel_id=1, source_target_pairs={{0,1},{1,0},{2,3},{3,2},{4,5},{5,4},{6,7},{7,6},{8,9},{9,8},{10,11... | collective-permute-start | bytes 393224 | tf_op jit(solution)/shard_map/ppermute | solution.py:541
  26.1 2.4 %collective-permute-start.14 = (bf16[64,768]{1,0:T(8,128)(2,1)S(1)}, bf16[64,768]{1,0:T(8,128)(2,1)S(1)}, u32[]{:S(2)}, u32[]{:S(2)}) collective-permute-start(bf16[64,768]{1,0:T(8,128)(2,1)S(1)} %get-tuple-element.104), channel_id=1, source_target_pairs={{0,24},{4,28},{8,16},{12,20},{16,8},{20,12},{24,0},{28,4},{1,25},{... | collective-permute-start | bytes 294920 | tf_op jit(solution)/shard_map/ppermute | solution.py:541
  28.6 0.5 collective-permute-start.15
  29.1 0.7 %collective-permute-done.10.row_got = bf16[4,32,768]{2,1,0:T(8,128)(2,1)S(1)} collective-permute-done((bf16[4,32,768]{2,1,0:T(8,128)(2,1)S(1)}, bf16[4,32,768]{2,1,0:T(8,128)(2,1)S(1)}, u32[]{:S(2)}, u32[]{:S(2)}) %collective-permute-start.10) | collective-permute-done | bytes 196640 | tf_op jit(solution)/shard_map/ppermute | solution.py:541
  29.7 1.7 %collective-permute-start.16 = (bf16[64,768]{1,0:T(8,128)(2,1)S(1)}, bf16[64,768]{1,0:T(8,128)(2,1)S(1)}, u32[]{:S(2)}, u32[]{:S(2)}) collective-permute-start(bf16[64,768]{1,0:T(8,128)(2,1)S(1)} %get-tuple-element.106), channel_id=1, source_target_pairs={{0,8},{4,12},{8,0},{12,4},{16,24},{20,28},{24,16},{28,20},{1,9},{5... | collective-permute-start | bytes 294920 | tf_op jit(solution)/shard_map/ppermute | solution.py:541
  31.5 0.7 %collective-permute-done.9.got_ref = bf16[4,32,512]{2,1,0:T(8,128)(2,1)S(1)} collective-permute-done((bf16[4,32,512]{2,1,0:T(8,128)(2,1)S(1)}, bf16[4,32,512]{2,1,0:T(8,128)(2,1)S(1)}, u32[]{:S(2)}, u32[]{:S(2)}) %collective-permute-start.9) | collective-permute-done | bytes 131104 | tf_op jit(solution)/shard_map/ppermute | solution.py:541
  32.2 0.1 first_add_pair.1
  32.2 2.7 %collective-permute-start.11 = (bf16[32,1280]{1,0:T(8,128)(2,1)S(1)}, bf16[32,1280]{1,0:T(8,128)(2,1)S(1)}, u32[]{:S(2)}, u32[]{:S(2)}) collective-permute-start(bf16[32,1280]{1,0:T(8,128)(2,1)S(1)} %get-tuple-element.100), channel_id=1, source_target_pairs={{0,24},{4,28},{8,16},{12,20},{16,8},{20,12},{24,0},{28,4},{1,25},{... | collective-permute-start | bytes 245768 | tf_op jit(solution)/shard_map/ppermute | solution.py:541
  34.9 0.5 collective-permute-start.12
  35.4 0.4 collective-permute-start.13
  35.8 0.1 second_add_chips.1
  35.9 1.8 %collective-permute-start.17 = (bf16[32,768]{1,0:T(8,128)(2,1)S(1)}, bf16[32,768]{1,0:T(8,128)(2,1)S(1)}, u32[]{:S(2)}, u32[]{:S(2)}) collective-permute-start(bf16[32,768]{1,0:T(8,128)(2,1)S(1)} %get-tuple-element.108), channel_id=1, source_target_pairs={{0,1},{1,0},{2,3},{3,2},{4,5},{5,4},{6,7},{7,6},{8,9},{9,8},{10,11... | collective-permute-start | bytes 147464 | tf_op jit(solution)/shard_map/ppermute | solution.py:541
  37.7 2.3 %collective-permute-done.17.got_ref = bf16[32,768]{1,0:T(8,128)(2,1)S(1)} collective-permute-done((bf16[32,768]{1,0:T(8,128)(2,1)S(1)}, bf16[32,768]{1,0:T(8,128)(2,1)S(1)}, u32[]{:S(2)}, u32[]{:S(2)}) %collective-permute-start.17) | collective-permute-done | bytes 49184 | tf_op jit(solution)/shard_map/ppermute | solution.py:541
  40.1 2.8 %collective-permute-start.21 = (bf16[32,2048]{1,0:T(8,128)(2,1)S(1)}, bf16[32,2048]{1,0:T(8,128)(2,1)S(1)}, u32[]{:S(2)}, u32[]{:S(2)}) collective-permute-start(bf16[32,2048]{1,0:T(8,128)(2,1)S(1)} %join_terms.1.kept_ref), channel_id=1, source_target_pairs={{0,2},{1,3},{2,0},{3,1},{4,6},{5,7},{6,4},{7,5},{8,10},{9,11},{10,... | collective-permute-start | bytes 393224 | tf_op jit(solution)/shard_map/ppermute | solution.py:541
  42.9 2.4 %collective-permute-start.18 = (bf16[128,512]{1,0:T(8,128)(2,1)S(1)}, bf16[128,512]{1,0:T(8,128)(2,1)S(1)}, u32[]{:S(2)}, u32[]{:S(2)}) collective-permute-start(bf16[128,512]{1,0:T(8,128)(2,1)S(1)} %get-tuple-element.110), channel_id=1, source_target_pairs={{0,24},{4,28},{8,16},{12,20},{16,8},{20,12},{24,0},{28,4},{1,25},{... | collective-permute-start | bytes 393224 | tf_op jit(solution)/shard_map/ppermute | solution.py:541
  45.4 0.5 collective-permute-start.19
  45.9 0.5 collective-permute-start.20
  46.4 1.7 %collective-permute-done.21.got_ref = bf16[32,2048]{1,0:T(8,128)(2,1)S(1)} collective-permute-done((bf16[32,2048]{1,0:T(8,128)(2,1)S(1)}, bf16[32,2048]{1,0:T(8,128)(2,1)S(1)}, u32[]{:S(2)}, u32[]{:S(2)}) %collective-permute-start.21) | collective-permute-done | bytes 131104 | tf_op jit(solution)/shard_map/ppermute | solution.py:541
  48.1 0.7 %collective-permute-start.22 = (bf16[32,2048]{1,0:T(8,128)(2,1)S(1)}, bf16[32,2048]{1,0:T(8,128)(2,1)S(1)}, u32[]{:S(2)}, u32[]{:S(2)}) collective-permute-start(bf16[32,2048]{1,0:T(8,128)(2,1)S(1)} %add_pairs.1.held_ref), channel_id=1, source_target_pairs={{0,1},{1,0},{2,3},{3,2},{4,5},{5,4},{6,7},{7,6},{8,9},{9,8},{10,11... | collective-permute-start | bytes 393224 | tf_op jit(solution)/shard_map/ppermute | solution.py:541
  48.9 0.5 collective-permute-done.18.got_1
  49.4 1.4 %collective-permute-done.19.got_2 = bf16[128,512]{1,0:T(8,128)(2,1)S(1)} collective-permute-done((bf16[128,512]{1,0:T(8,128)(2,1)S(1)}, bf16[128,512]{1,0:T(8,128)(2,1)S(1)}, u32[]{:S(2)}, u32[]{:S(2)}) %collective-permute-start.19) | collective-permute-done | bytes 131104 | tf_op jit(solution)/shard_map/ppermute | solution.py:541
  50.8 0.1 collective-permute-done.20.got_3
  50.8 1.1 %input_grad.1 = bf16[512,512]{1,0:T(8,128)(2,1)} custom-call(f32[512,512]{1,0:T(8,128)S(1)} %get-tuple-element.67.base_ref, f32[512,512]{1,0:T(8,128)S(1)} %get-tuple-element.68.normed_ref, f32[512,1]{1,0:T(8,128)S(1)} %get-tuple-element.69.inverse_ref, f32[1,512]{1,0:T(1,128)S(1)} %bitcast.7, bf16[128,512]{1,0:T(8,128)(2,1)S(1)} %get-tuple-element.109.own_ref, ...), custom_call_target="tpu_custom_call" | custom-call | tf_op jit(solution)/shard_map/input_grad/pallas_call | solution.py:527
  52.0 1.2 %collective-permute-done.22.got_ref = bf16[32,2048]{1,0:T(8,128)(2,1)S(1)} collective-permute-done((bf16[32,2048]{1,0:T(8,128)(2,1)S(1)}, bf16[32,2048]{1,0:T(8,128)(2,1)S(1)}, u32[]{:S(2)}, u32[]{:S(2)}) %collective-permute-start.22) | collective-permute-done | bytes 131104 | tf_op jit(solution)/shard_map/ppermute | solution.py:541
  53.2 0.9 %result.1 = (f32[64,1536]{1,0:T(8,128)}, f32[64,512]{1,0:T(8,128)}, f32[1,64]{1,0:T(1,128)}) custom-call(bf16[32,2048]{1,0:T(8,128)(2,1)S(1)} %add_pairs.1.held_ref, bf16[32,2048]{1,0:T(8,128)(2,1)S(1)} %collective-permute-done.22.got_ref, bf16[64,1536]{1,0:T(8,128)(2,1)S(1)} %get-tuple-element.114.w_ref, f32[1,512]{1,0:T(1,128)S(1)} %bitcast.8), custom_call_target="tpu_custom_call" | custom-call | tf_op jit(solution)/shard_map/result/pallas_call | solution.py:527
  (15 shorter events, 0.2 us)
Async XLA Ops:
  2.0 4.6 %collective-permute-start.2 = (bf16[2,2,64,512]{3,2,1,0:T(8,128)(2,1)S(1)}, bf16[2,2,64,512]{3,2,1,0:T(8,128)(2,1)S(1)}, u32[]{:S(2)}, u32[]{:S(2)}) collective-permute-start(bf16[2,2,64,512]{3,2,1,0:T(8,128)(2,1)S(1)} %get-tuple-element.64), channel_id=1, source_target_pairs={{0,4},{4,0},{8,12},{12,8},{16,20},{20,16},{24,28},{28,24},{1,5},{5... | collective-permute-start | bytes 786440 | tf_op jit(solution)/shard_map/ppermute | solution.py:541
  2.5 12.7 %collective-permute-start = (bf16[2,128,512]{2,1,0:T(8,128)(2,1)S(1)}, bf16[2,128,512]{2,1,0:T(8,128)(2,1)S(1)}, u32[]{:S(2)}, u32[]{:S(2)}) collective-permute-start(bf16[2,128,512]{2,1,0:T(8,128)(2,1)S(1)} %get-tuple-element.61), channel_id=1, source_target_pairs={{0,16},{4,20},{8,24},{12,28},{16,0},{20,4},{24,8},{28,12},{1,17},{... | collective-permute-start | bytes 786440 | tf_op jit(solution)/shard_map/ppermute | solution.py:541
  5.1 10.2 %collective-permute-start.1 = (bf16[2,128,512]{2,1,0:T(8,128)(2,1)S(1)}, bf16[2,128,512]{2,1,0:T(8,128)(2,1)S(1)}, u32[]{:S(2)}, u32[]{:S(2)}) collective-permute-start(bf16[2,128,512]{2,1,0:T(8,128)(2,1)S(1)} %get-tuple-element.62), channel_id=1, source_target_pairs={{0,8},{4,12},{8,0},{12,4},{16,24},{20,28},{24,16},{28,20},{1,9},{5... | collective-permute-start | bytes 786440 | tf_op jit(solution)/shard_map/ppermute | solution.py:541
  6.6 12.2 %collective-permute-start.3 = (bf16[2,2,64,512]{3,2,1,0:T(8,128)(2,1)S(1)}, bf16[2,2,64,512]{3,2,1,0:T(8,128)(2,1)S(1)}, u32[]{:S(2)}, u32[]{:S(2)}) collective-permute-start(bf16[2,2,64,512]{3,2,1,0:T(8,128)(2,1)S(1)} %pack_corner.1), channel_id=1, source_target_pairs={{0,24},{4,28},{8,16},{12,20},{16,8},{20,12},{24,0},{28,4},{1,25},{... | collective-permute-start | bytes 786440 | tf_op jit(solution)/shard_map/ppermute | solution.py:541
  15.2 3.6 %copy-start = (f32[512]{0:T(512)S(1)}, f32[512]{0:T(512)}, u32[]{:S(2)}) copy-start(f32[512]{0:T(512)} %param.6) | copy-start | bytes 6148
  15.3 3.5 %collective-permute-start.4 = (bf16[2,2,64,512]{3,2,1,0:T(8,128)(2,1)S(1)}, bf16[2,2,64,512]{3,2,1,0:T(8,128)(2,1)S(1)}, u32[]{:S(2)}, u32[]{:S(2)}) collective-permute-start(bf16[2,2,64,512]{3,2,1,0:T(8,128)(2,1)S(1)} %pack_other_core.1), channel_id=1, source_target_pairs={{0,4},{4,0},{8,12},{12,8},{16,20},{20,16},{24,28},{28,24},{1,5},{5... | collective-permute-start | bytes 786440 | tf_op jit(solution)/shard_map/ppermute | solution.py:541
  15.4 1.8 %collective-permute-start.5 = (bf16[4,64,384]{2,1,0:T(8,128)(2,1)S(1)}, bf16[4,64,384]{2,1,0:T(8,128)(2,1)S(1)}, u32[]{:S(2)}, u32[]{:S(2)}) collective-permute-start(bf16[4,64,384]{2,1,0:T(8,128)(2,1)S(1)} %get-tuple-element.77), channel_id=1, source_target_pairs={{0,4},{4,0},{8,12},{12,8},{16,20},{20,16},{24,28},{28,24},{1,5},{5... | collective-permute-start | bytes 589832 | tf_op jit(solution)/shard_map/ppermute | solution.py:541
  15.9 1.6 %collective-permute-start.6 = (bf16[4,64,384]{2,1,0:T(8,128)(2,1)S(1)}, bf16[4,64,384]{2,1,0:T(8,128)(2,1)S(1)}, u32[]{:S(2)}, u32[]{:S(2)}) collective-permute-start(bf16[4,64,384]{2,1,0:T(8,128)(2,1)S(1)} %get-tuple-element.78), channel_id=1, source_target_pairs={{0,4},{4,0},{8,12},{12,8},{16,20},{20,16},{24,28},{28,24},{1,5},{5... | collective-permute-start | bytes 589832 | tf_op jit(solution)/shard_map/ppermute | solution.py:541
  21.9 2.8 %collective-permute-start.8 = (bf16[4,64,1280]{2,1,0:T(8,128)(2,1)S(1)}, bf16[4,64,1280]{2,1,0:T(8,128)(2,1)S(1)}, u32[]{:S(2)}, u32[]{:S(2)}) collective-permute-start(bf16[4,64,1280]{2,1,0:T(8,128)(2,1)S(1)} %get-tuple-element.93), channel_id=1, source_target_pairs={{0,4},{4,0},{8,12},{12,8},{16,20},{20,16},{24,28},{28,24},{1,5},{5... | collective-permute-start | bytes 1966088 | tf_op jit(solution)/shard_map/ppermute | solution.py:541
  22.0 7.8 %collective-permute-start.10 = (bf16[4,32,768]{2,1,0:T(8,128)(2,1)S(1)}, bf16[4,32,768]{2,1,0:T(8,128)(2,1)S(1)}, u32[]{:S(2)}, u32[]{:S(2)}) collective-permute-start(bf16[4,32,768]{2,1,0:T(8,128)(2,1)S(1)} %get-tuple-element.98), channel_id=1, source_target_pairs={{0,1},{1,0},{2,3},{3,2},{4,5},{5,4},{6,7},{7,6},{8,9},{9,8},{10,11... | collective-permute-start | bytes 589832 | tf_op jit(solution)/shard_map/ppermute | solution.py:541
  24.5 13.2 %collective-permute-start.7 = (bf16[4,64,512]{2,1,0:T(8,128)(2,1)S(1)}, bf16[4,64,512]{2,1,0:T(8,128)(2,1)S(1)}, u32[]{:S(2)}, u32[]{:S(2)}) collective-permute-start(bf16[4,64,512]{2,1,0:T(8,128)(2,1)S(1)} %get-tuple-element.87), channel_id=1, source_target_pairs={{0,4},{4,0},{8,12},{12,8},{16,20},{20,16},{24,28},{28,24},{1,5},{5... | collective-permute-start | bytes 786440 | tf_op jit(solution)/shard_map/ppermute | solution.py:541
  24.9 7.3 %collective-permute-start.9 = (bf16[4,32,512]{2,1,0:T(8,128)(2,1)S(1)}, bf16[4,32,512]{2,1,0:T(8,128)(2,1)S(1)}, u32[]{:S(2)}, u32[]{:S(2)}) collective-permute-start(bf16[4,32,512]{2,1,0:T(8,128)(2,1)S(1)} %get-tuple-element.95), channel_id=1, source_target_pairs={{0,1},{1,0},{2,3},{3,2},{4,5},{5,4},{6,7},{7,6},{8,9},{9,8},{10,11... | collective-permute-start | bytes 393224 | tf_op jit(solution)/shard_map/ppermute | solution.py:541
  26.1 8.8 %collective-permute-start.14 = (bf16[64,768]{1,0:T(8,128)(2,1)S(1)}, bf16[64,768]{1,0:T(8,128)(2,1)S(1)}, u32[]{:S(2)}, u32[]{:S(2)}) collective-permute-start(bf16[64,768]{1,0:T(8,128)(2,1)S(1)} %get-tuple-element.104), channel_id=1, source_target_pairs={{0,24},{4,28},{8,16},{12,20},{16,8},{20,12},{24,0},{28,4},{1,25},{... | collective-permute-start | bytes 294920 | tf_op jit(solution)/shard_map/ppermute | solution.py:541
  28.6 6.9 %collective-permute-start.15 = (bf16[64,768]{1,0:T(8,128)(2,1)S(1)}, bf16[64,768]{1,0:T(8,128)(2,1)S(1)}, u32[]{:S(2)}, u32[]{:S(2)}) collective-permute-start(bf16[64,768]{1,0:T(8,128)(2,1)S(1)} %get-tuple-element.105), channel_id=1, source_target_pairs={{0,16},{4,20},{8,24},{12,28},{16,0},{20,4},{24,8},{28,12},{1,17},{... | collective-permute-start | bytes 294920 | tf_op jit(solution)/shard_map/ppermute | solution.py:541
  29.7 6.1 %collective-permute-start.16 = (bf16[64,768]{1,0:T(8,128)(2,1)S(1)}, bf16[64,768]{1,0:T(8,128)(2,1)S(1)}, u32[]{:S(2)}, u32[]{:S(2)}) collective-permute-start(bf16[64,768]{1,0:T(8,128)(2,1)S(1)} %get-tuple-element.106), channel_id=1, source_target_pairs={{0,8},{4,12},{8,0},{12,4},{16,24},{20,28},{24,16},{28,20},{1,9},{5... | collective-permute-start | bytes 294920 | tf_op jit(solution)/shard_map/ppermute | solution.py:541
  32.2 7.8 %collective-permute-start.11 = (bf16[32,1280]{1,0:T(8,128)(2,1)S(1)}, bf16[32,1280]{1,0:T(8,128)(2,1)S(1)}, u32[]{:S(2)}, u32[]{:S(2)}) collective-permute-start(bf16[32,1280]{1,0:T(8,128)(2,1)S(1)} %get-tuple-element.100), channel_id=1, source_target_pairs={{0,24},{4,28},{8,16},{12,20},{16,8},{20,12},{24,0},{28,4},{1,25},{... | collective-permute-start | bytes 245768 | tf_op jit(solution)/shard_map/ppermute | solution.py:541
  34.9 5.1 %collective-permute-start.12 = (bf16[32,1280]{1,0:T(8,128)(2,1)S(1)}, bf16[32,1280]{1,0:T(8,128)(2,1)S(1)}, u32[]{:S(2)}, u32[]{:S(2)}) collective-permute-start(bf16[32,1280]{1,0:T(8,128)(2,1)S(1)} %get-tuple-element.101), channel_id=1, source_target_pairs={{0,16},{4,20},{8,24},{12,28},{16,0},{20,4},{24,8},{28,12},{1,17},{... | collective-permute-start | bytes 245768 | tf_op jit(solution)/shard_map/ppermute | solution.py:541
  35.4 4.6 %collective-permute-start.13 = (bf16[32,1280]{1,0:T(8,128)(2,1)S(1)}, bf16[32,1280]{1,0:T(8,128)(2,1)S(1)}, u32[]{:S(2)}, u32[]{:S(2)}) collective-permute-start(bf16[32,1280]{1,0:T(8,128)(2,1)S(1)} %get-tuple-element.102), channel_id=1, source_target_pairs={{0,8},{4,12},{8,0},{12,4},{16,24},{20,28},{24,16},{28,20},{1,9},{5... | collective-permute-start | bytes 245768 | tf_op jit(solution)/shard_map/ppermute | solution.py:541
  35.9 4.2 %collective-permute-start.17 = (bf16[32,768]{1,0:T(8,128)(2,1)S(1)}, bf16[32,768]{1,0:T(8,128)(2,1)S(1)}, u32[]{:S(2)}, u32[]{:S(2)}) collective-permute-start(bf16[32,768]{1,0:T(8,128)(2,1)S(1)} %get-tuple-element.108), channel_id=1, source_target_pairs={{0,1},{1,0},{2,3},{3,2},{4,5},{5,4},{6,7},{7,6},{8,9},{9,8},{10,11... | collective-permute-start | bytes 147464 | tf_op jit(solution)/shard_map/ppermute | solution.py:541
  40.1 8.0 %collective-permute-start.21 = (bf16[32,2048]{1,0:T(8,128)(2,1)S(1)}, bf16[32,2048]{1,0:T(8,128)(2,1)S(1)}, u32[]{:S(2)}, u32[]{:S(2)}) collective-permute-start(bf16[32,2048]{1,0:T(8,128)(2,1)S(1)} %join_terms.1.kept_ref), channel_id=1, source_target_pairs={{0,2},{1,3},{2,0},{3,1},{4,6},{5,7},{6,4},{7,5},{8,10},{9,11},{10,... | collective-permute-start | bytes 393224 | tf_op jit(solution)/shard_map/ppermute | solution.py:541
  42.9 6.5 %collective-permute-start.18 = (bf16[128,512]{1,0:T(8,128)(2,1)S(1)}, bf16[128,512]{1,0:T(8,128)(2,1)S(1)}, u32[]{:S(2)}, u32[]{:S(2)}) collective-permute-start(bf16[128,512]{1,0:T(8,128)(2,1)S(1)} %get-tuple-element.110), channel_id=1, source_target_pairs={{0,24},{4,28},{8,16},{12,20},{16,8},{20,12},{24,0},{28,4},{1,25},{... | collective-permute-start | bytes 393224 | tf_op jit(solution)/shard_map/ppermute | solution.py:541
  45.4 5.4 %collective-permute-start.19 = (bf16[128,512]{1,0:T(8,128)(2,1)S(1)}, bf16[128,512]{1,0:T(8,128)(2,1)S(1)}, u32[]{:S(2)}, u32[]{:S(2)}) collective-permute-start(bf16[128,512]{1,0:T(8,128)(2,1)S(1)} %get-tuple-element.111), channel_id=1, source_target_pairs={{0,16},{4,20},{8,24},{12,28},{16,0},{20,4},{24,8},{28,12},{1,17},{... | collective-permute-start | bytes 393224 | tf_op jit(solution)/shard_map/ppermute | solution.py:541
  45.9 5.0 %collective-permute-start.20 = (bf16[128,512]{1,0:T(8,128)(2,1)S(1)}, bf16[128,512]{1,0:T(8,128)(2,1)S(1)}, u32[]{:S(2)}, u32[]{:S(2)}) collective-permute-start(bf16[128,512]{1,0:T(8,128)(2,1)S(1)} %get-tuple-element.112), channel_id=1, source_target_pairs={{0,8},{4,12},{8,0},{12,4},{16,24},{20,28},{24,16},{28,20},{1,9},{5... | collective-permute-start | bytes 393224 | tf_op jit(solution)/shard_map/ppermute | solution.py:541
  48.1 5.0 %collective-permute-start.22 = (bf16[32,2048]{1,0:T(8,128)(2,1)S(1)}, bf16[32,2048]{1,0:T(8,128)(2,1)S(1)}, u32[]{:S(2)}, u32[]{:S(2)}) collective-permute-start(bf16[32,2048]{1,0:T(8,128)(2,1)S(1)} %add_pairs.1.held_ref), channel_id=1, source_target_pairs={{0,1},{1,0},{2,3},{3,2},{4,5},{5,4},{6,7},{7,6},{8,9},{9,8},{10,11... | collective-permute-start | bytes 393224 | tf_op jit(solution)/shard_map/ppermute | solution.py:541

commit v25 on v20

--- a/solution.py
+++ b/solution.py
@@ -226,7 +226,6 @@
     tokens, block = x.shape[0], mask.shape[0]
     _, normed = rms_parts(x.astype(F32))
     hidden = (normed * gain).astype(BF16)
-    hidden_t = transposed(hidden)
     finished(*weight_waits)
     q, k, v, g = project(hidden, cot, w_ref, wo_ref)
     kt, vt, gt = transposed(k), transposed(v), transposed(g)
@@ -251,7 +250,7 @@
         for i in range(2)
     ]
     grads_ref[:, :HW] = transposed(grad_q)
-    term_qkv = dot_nn(hidden_t, grads_ref[...]).astype(BF16)
+    term_qkv = dot_nn(transposed(hidden), grads_ref[...]).astype(BF16)
     term_out = dot_nn(attended, cot).astype(BF16)
     return term_qkv, term_out
 

time: 53.8 us -> 53.7 us (level)
  no operation moved by 1% of the time
where the time goes in v25:
time: 53.7 us; the launch traced here: 53.5 us
  starting transfers between devices  25.4 us (47%)
  Pallas kernels  15.2 us (28%)
  waiting for transfers between devices  12.2 us (23%)
  between operations  0.77 us (1%)
    ppermute x23, starting transfers between devices, swap(): return lax.ppermute(array, axis, [(i, i ^ bits) for i in range(count)])  25.4 us
    pallas_call x15, Pallas kernels, call(): pl.pallas_call(kernel, out_shape=outs, in_specs=[spec for spec, _ in ins]...  15.2 us
    ppermute x23, waiting for transfers between devices, swap(): return lax.ppermute(array, axis, [(i, i ^ bits) for i in range(count)])  12.2 us
  transfers between devices with their start and end apart: 23, of which 13 were waited for; matrix products, arithmetic and copies ran while one was open for 0% of the time, Pallas kernels for 19%

profile of v25, /device:TPU:0, one launch (start us, length us, event | category | flops | bytes accessed | tf_op | source)
XLA Modules:
  0.0 53.5 jit_solution(558588095520715354)
XLA Ops:
  0.6 1.4 %pack_columns.1 = (bf16[2,2,64,512]{3,2,1,0:T(8,128)(2,1)S(1)}, bf16[2,64,512]{2,1,0:T(8,128)(2,1)S(1)}, bf16[2,128,512]{2,1,0:T(8,128)(2,1)S(1)}, bf16[2,128,512]{2,1,0:T(8,128)(2,1)S(1)}) custom-call(bf16[512,512]{1,0:T(8,128)(2,1)} %bitcast.9, bf16[512,512]{1,0:T(8,128)(2,1)} %bitcast.11), custom_call_target="tpu_custom_call" | custom-call | tf_op jit(solution)/shard_map/pack_columns/pallas_call | solution.py:526
  2.0 0.5 collective-permute-start.2
  2.5 2.6 %collective-permute-start = (bf16[2,128,512]{2,1,0:T(8,128)(2,1)S(1)}, bf16[2,128,512]{2,1,0:T(8,128)(2,1)S(1)}, u32[]{:S(2)}, u32[]{:S(2)}) collective-permute-start(bf16[2,128,512]{2,1,0:T(8,128)(2,1)S(1)} %get-tuple-element.66), channel_id=1, source_target_pairs={{0,16},{4,20},{8,24},{12,28},{16,0},{20,4},{24,8},{28,12},{1,17},{... | collective-permute-start | bytes 786440 | tf_op jit(solution)/shard_map/ppermute | solution.py:540
  5.1 1.5 %collective-permute-start.1 = (bf16[2,128,512]{2,1,0:T(8,128)(2,1)S(1)}, bf16[2,128,512]{2,1,0:T(8,128)(2,1)S(1)}, u32[]{:S(2)}, u32[]{:S(2)}) collective-permute-start(bf16[2,128,512]{2,1,0:T(8,128)(2,1)S(1)} %get-tuple-element.67), channel_id=1, source_target_pairs={{0,8},{4,12},{8,0},{12,4},{16,24},{20,28},{24,16},{28,20},{1,9},{5... | collective-permute-start | bytes 786440 | tf_op jit(solution)/shard_map/ppermute | solution.py:540
  6.6 1.0 %collective-permute-start.5 = (bf16[2,2,64,512]{3,2,1,0:T(8,128)(2,1)S(1)}, bf16[2,2,64,512]{3,2,1,0:T(8,128)(2,1)S(1)}, u32[]{:S(2)}, u32[]{:S(2)}) collective-permute-start(bf16[2,2,64,512]{3,2,1,0:T(8,128)(2,1)S(1)} %pack_corner.1), channel_id=1, source_target_pairs={{0,24},{4,28},{8,16},{12,20},{16,8},{20,12},{24,0},{28,4},{1,25},{... | collective-permute-start | bytes 786440 | tf_op jit(solution)/shard_map/ppermute | solution.py:540
  7.6 7.6 %row_heads.1 = (bf16[4,64,384]{2,1,0:T(8,128)(2,1)S(1)}, bf16[4,64,384]{2,1,0:T(8,128)(2,1)S(1)}, bf16[4,64,384]{2,1,0:T(8,128)(2,1)S(1)}, bf16[4,64,384]{2,1,0:...) custom-call(bf16[512,512]{1,0:T(8,128)(2,1)} %bitcast.10, ...), custom_call_target="tpu_custom_call" | custom-call | tf_op jit(solution)/shard_map/row_heads/pallas_call | solution.py:526
  15.3 0.1 collective-permute-start.6
  15.4 0.5 collective-permute-start.3
  15.9 0.1 collective-permute-start.4
  16.0 1.2 %collective-permute-done.3.got_1 = bf16[4,64,384]{2,1,0:T(8,128)(2,1)S(1)} collective-permute-done((bf16[4,64,384]{2,1,0:T(8,128)(2,1)S(1)}, bf16[4,64,384]{2,1,0:T(8,128)(2,1)S(1)}, u32[]{:S(2)}, u32[]{:S(2)}) %collective-permute-start.3) | collective-permute-done | bytes 196640 | tf_op jit(solution)/shard_map/ppermute | solution.py:540
  17.2 0.3 collective-permute-done.4.got_2
  17.5 0.1 row_add_cores.1
  17.6 1.2 %collective-permute-done.5.corner_ref = bf16[2,2,64,512]{3,2,1,0:T(8,128)(2,1)S(1)} collective-permute-done((bf16[2,2,64,512]{3,2,1,0:T(8,128)(2,1)S(1)}, bf16[2,2,64,512]{3,2,1,0:T(8,128)(2,1)S(1)}, u32[]{:S(2)}, u32[]{:S(2)}) %collective-permute-start.5) | collective-permute-done | bytes 262176 | tf_op jit(solution)/shard_map/ppermute | solution.py:540
  18.8 3.0 %column_heads.1 = (bf16[4,64,1280]{2,1,0:T(8,128)(2,1)S(1)}, bf16[4,64,1280]{2,1,0:T(8,128)(2,1)S(1)}, bf16[512,768]{1,0:T(8,128)(2,1)S(1)}) custom-call(bf16[512,512]{1,0:T(8,128)(2,1)S(1)} %get-tuple-element.82.x_ref, bf16[512,512]{1,0:T(8,128)(2,1)S(1)} %get-tuple-element.83.cot_ref, bf16[2,2,64,512]{3,2,1,0:T(8,128)(2,1)S(1)} %collective-permute-done.2.swapped_ref, ...), custom_call_target="tpu_custom_call" | custom-call | tf_op jit(solution)/shard_map/column_heads/pallas_call | solution.py:526
  21.8 0.1 collective-permute-start.8
  21.9 0.6 %column_grad_hidden.1 = (bf16[4,64,512]{2,1,0:T(8,128)(2,1)S(1)}, bf16[4,64,512]{2,1,0:T(8,128)(2,1)S(1)}) custom-call(bf16[512,768]{1,0:T(8,128)(2,1)S(1)} %get-tuple-element.90.grads_ref, bf16[512,768]{1,0:T(8,128)(2,1)S(1)} %get-tuple-element.86.w_ref), custom_call_target="tpu_custom_call" | custom-call | tf_op jit(solution)/shard_map/column_grad_hidden/pallas_call | solution.py:526
  22.5 0.6 %collective-permute-start.7 = (bf16[4,64,512]{2,1,0:T(8,128)(2,1)S(1)}, bf16[4,64,512]{2,1,0:T(8,128)(2,1)S(1)}, u32[]{:S(2)}, u32[]{:S(2)}) collective-permute-start(bf16[4,64,512]{2,1,0:T(8,128)(2,1)S(1)} %get-tuple-element.93), channel_id=1, source_target_pairs={{0,4},{4,0},{8,12},{12,8},{16,20},{20,16},{24,28},{28,24},{1,5},{5... | collective-permute-start | bytes 786440 | tf_op jit(solution)/shard_map/ppermute | solution.py:540
  23.0 1.8 %collective-permute-start.10 = (bf16[4,32,768]{2,1,0:T(8,128)(2,1)S(1)}, bf16[4,32,768]{2,1,0:T(8,128)(2,1)S(1)}, u32[]{:S(2)}, u32[]{:S(2)}) collective-permute-start(bf16[4,32,768]{2,1,0:T(8,128)(2,1)S(1)} %get-tuple-element.108), channel_id=1, source_target_pairs={{0,1},{1,0},{2,3},{3,2},{4,5},{5,4},{6,7},{7,6},{8,9},{9,8},{10,11... | collective-permute-start | bytes 589832 | tf_op jit(solution)/shard_map/ppermute | solution.py:540
  24.8 0.2 column_add_cores.1
  25.0 2.5 %collective-permute-start.14 = (bf16[64,896]{1,0:T(8,128)(2,1)S(1)}, bf16[64,896]{1,0:T(8,128)(2,1)S(1)}, u32[]{:S(2)}, u32[]{:S(2)}) collective-permute-start(bf16[64,896]{1,0:T(8,128)(2,1)S(1)} %get-tuple-element.114), channel_id=1, source_target_pairs={{0,24},{4,28},{8,16},{12,20},{16,8},{20,12},{24,0},{28,4},{1,25},{... | collective-permute-start | bytes 344072 | tf_op jit(solution)/shard_map/ppermute | solution.py:540
  27.5 0.9 %collective-permute-start.9 = (bf16[4,32,384]{2,1,0:T(8,128)(2,1)S(1)}, bf16[4,32,384]{2,1,0:T(8,128)(2,1)S(1)}, u32[]{:S(2)}, u32[]{:S(2)}) collective-permute-start(bf16[4,32,384]{2,1,0:T(8,128)(2,1)S(1)} %get-tuple-element.105), channel_id=1, source_target_pairs={{0,1},{1,0},{2,3},{3,2},{4,5},{5,4},{6,7},{7,6},{8,9},{9,8},{10,11... | collective-permute-start | bytes 294920 | tf_op jit(solution)/shard_map/ppermute | solution.py:540
  28.4 0.5 collective-permute-start.15
  29.0 0.5 %collective-permute-start.16 = (bf16[64,896]{1,0:T(8,128)(2,1)S(1)}, bf16[64,896]{1,0:T(8,128)(2,1)S(1)}, u32[]{:S(2)}, u32[]{:S(2)}) collective-permute-start(bf16[64,896]{1,0:T(8,128)(2,1)S(1)} %get-tuple-element.116), channel_id=1, source_target_pairs={{0,8},{4,12},{8,0},{12,4},{16,24},{20,28},{24,16},{28,20},{1,9},{5... | collective-permute-start | bytes 344072 | tf_op jit(solution)/shard_map/ppermute | solution.py:540
  29.5 0.7 %collective-permute-done.10.row_got = bf16[4,32,768]{2,1,0:T(8,128)(2,1)S(1)} collective-permute-done((bf16[4,32,768]{2,1,0:T(8,128)(2,1)S(1)}, bf16[4,32,768]{2,1,0:T(8,128)(2,1)S(1)}, u32[]{:S(2)}, u32[]{:S(2)}) %collective-permute-start.10) | collective-permute-done | bytes 196640 | tf_op jit(solution)/shard_map/ppermute | solution.py:540
  30.3 1.9 %collective-permute-done.9.got_ref = bf16[4,32,384]{2,1,0:T(8,128)(2,1)S(1)} collective-permute-done((bf16[4,32,384]{2,1,0:T(8,128)(2,1)S(1)}, bf16[4,32,384]{2,1,0:T(8,128)(2,1)S(1)}, u32[]{:S(2)}, u32[]{:S(2)}) %collective-permute-start.9) | collective-permute-done | bytes 98336 | tf_op jit(solution)/shard_map/ppermute | solution.py:540
  32.1 0.1 first_add_pair.1
  32.2 2.6 %collective-permute-start.11 = (bf16[32,1152]{1,0:T(8,128)(2,1)S(1)}, bf16[32,1152]{1,0:T(8,128)(2,1)S(1)}, u32[]{:S(2)}, u32[]{:S(2)}) collective-permute-start(bf16[32,1152]{1,0:T(8,128)(2,1)S(1)} %get-tuple-element.110), channel_id=1, source_target_pairs={{0,24},{4,28},{8,16},{12,20},{16,8},{20,12},{24,0},{28,4},{1,25},{... | collective-permute-start | bytes 221192 | tf_op jit(solution)/shard_map/ppermute | solution.py:540
  34.8 0.5 collective-permute-start.12
  35.3 0.4 collective-permute-start.13
  35.8 0.1 second_add_chips.1
  35.8 1.7 %collective-permute-start.17 = (bf16[32,896]{1,0:T(8,128)(2,1)S(1)}, bf16[32,896]{1,0:T(8,128)(2,1)S(1)}, u32[]{:S(2)}, u32[]{:S(2)}) collective-permute-start(bf16[32,896]{1,0:T(8,128)(2,1)S(1)} %get-tuple-element.118), channel_id=1, source_target_pairs={{0,1},{1,0},{2,3},{3,2},{4,5},{5,4},{6,7},{7,6},{8,9},{9,8},{10,11... | collective-permute-start | bytes 172040 | tf_op jit(solution)/shard_map/ppermute | solution.py:540
  37.6 0.0 collective-permute-done.11.got_1
  37.6 1.6 %collective-permute-done.12.got_2 = bf16[32,1152]{1,0:T(8,128)(2,1)S(1)} collective-permute-done((bf16[32,1152]{1,0:T(8,128)(2,1)S(1)}, bf16[32,1152]{1,0:T(8,128)(2,1)S(1)}, u32[]{:S(2)}, u32[]{:S(2)}) %collective-permute-start.12) | collective-permute-done | bytes 73760 | tf_op jit(solution)/shard_map/ppermute | solution.py:540
  39.2 0.5 collective-permute-done.13.got_3
  39.7 0.4 collective-permute-done.17.got_ref
  40.1 0.1 join_terms.1.kept_ref
  40.1 2.8 %collective-permute-start.21 = (bf16[32,2048]{1,0:T(8,128)(2,1)S(1)}, bf16[32,2048]{1,0:T(8,128)(2,1)S(1)}, u32[]{:S(2)}, u32[]{:S(2)}) collective-permute-start(bf16[32,2048]{1,0:T(8,128)(2,1)S(1)} %join_terms.1.kept_ref), channel_id=1, source_target_pairs={{0,2},{1,3},{2,0},{3,1},{4,6},{5,7},{6,4},{7,5},{8,10},{9,11},{10,... | collective-permute-start | bytes 393224 | tf_op jit(solution)/shard_map/ppermute | solution.py:540
  42.9 2.4 %collective-permute-start.18 = (bf16[128,512]{1,0:T(8,128)(2,1)S(1)}, bf16[128,512]{1,0:T(8,128)(2,1)S(1)}, u32[]{:S(2)}, u32[]{:S(2)}) collective-permute-start(bf16[128,512]{1,0:T(8,128)(2,1)S(1)} %get-tuple-element.120), channel_id=1, source_target_pairs={{0,24},{4,28},{8,16},{12,20},{16,8},{20,12},{24,0},{28,4},{1,25},{... | collective-permute-start | bytes 393224 | tf_op jit(solution)/shard_map/ppermute | solution.py:540
  45.3 0.5 collective-permute-start.19
  45.9 0.5 %collective-permute-start.20 = (bf16[128,512]{1,0:T(8,128)(2,1)S(1)}, bf16[128,512]{1,0:T(8,128)(2,1)S(1)}, u32[]{:S(2)}, u32[]{:S(2)}) collective-permute-start(bf16[128,512]{1,0:T(8,128)(2,1)S(1)} %get-tuple-element.122), channel_id=1, source_target_pairs={{0,8},{4,12},{8,0},{12,4},{16,24},{20,28},{24,16},{28,20},{1,9},{5... | collective-permute-start | bytes 393224 | tf_op jit(solution)/shard_map/ppermute | solution.py:540
  46.4 1.2 %collective-permute-done.21.got_ref = bf16[32,2048]{1,0:T(8,128)(2,1)S(1)} collective-permute-done((bf16[32,2048]{1,0:T(8,128)(2,1)S(1)}, bf16[32,2048]{1,0:T(8,128)(2,1)S(1)}, u32[]{:S(2)}, u32[]{:S(2)}) %collective-permute-start.21) | collective-permute-done | bytes 131104 | tf_op jit(solution)/shard_map/ppermute | solution.py:540
  47.6 0.7 %collective-permute-start.22 = (bf16[32,2048]{1,0:T(8,128)(2,1)S(1)}, bf16[32,2048]{1,0:T(8,128)(2,1)S(1)}, u32[]{:S(2)}, u32[]{:S(2)}) collective-permute-start(bf16[32,2048]{1,0:T(8,128)(2,1)S(1)} %add_pairs.1.held_ref), channel_id=1, source_target_pairs={{0,1},{1,0},{2,3},{3,2},{4,5},{5,4},{6,7},{7,6},{8,9},{9,8},{10,11... | collective-permute-start | bytes 393224 | tf_op jit(solution)/shard_map/ppermute | solution.py:540
  48.4 0.6 %collective-permute-done.18.got_1 = bf16[128,512]{1,0:T(8,128)(2,1)S(1)} collective-permute-done((bf16[128,512]{1,0:T(8,128)(2,1)S(1)}, bf16[128,512]{1,0:T(8,128)(2,1)S(1)}, u32[]{:S(2)}, u32[]{:S(2)}) %collective-permute-start.18) | collective-permute-done | bytes 131104 | tf_op jit(solution)/shard_map/ppermute | solution.py:540
  48.9 1.4 %collective-permute-done.19.got_2 = bf16[128,512]{1,0:T(8,128)(2,1)S(1)} collective-permute-done((bf16[128,512]{1,0:T(8,128)(2,1)S(1)}, bf16[128,512]{1,0:T(8,128)(2,1)S(1)}, u32[]{:S(2)}, u32[]{:S(2)}) %collective-permute-start.19) | collective-permute-done | bytes 131104 | tf_op jit(solution)/shard_map/ppermute | solution.py:540
  50.3 0.5 collective-permute-done.20.got_3
  50.8 1.2 %input_grad.1 = bf16[512,512]{1,0:T(8,128)(2,1)} custom-call(f32[512,512]{1,0:T(8,128)S(1)} %get-tuple-element.72.base_ref, f32[512,512]{1,0:T(8,128)S(1)} %get-tuple-element.73.normed_ref, f32[512,1]{1,0:T(8,128)S(1)} %get-tuple-element.74.inverse_ref, f32[1,512]{1,0:T(1,128)S(1)} %bitcast.7, bf16[128,512]{1,0:T(8,128)(2,1)S(1)} %get-tuple-element.119.own_ref, ...), custom_call_target="tpu_custom_call" | custom-call | tf_op jit(solution)/shard_map/input_grad/pallas_call | solution.py:526
  52.0 0.7 %collective-permute-done.22.got_ref = bf16[32,2048]{1,0:T(8,128)(2,1)S(1)} collective-permute-done((bf16[32,2048]{1,0:T(8,128)(2,1)S(1)}, bf16[32,2048]{1,0:T(8,128)(2,1)S(1)}, u32[]{:S(2)}, u32[]{:S(2)}) %collective-permute-start.22) | collective-permute-done | bytes 131104 | tf_op jit(solution)/shard_map/ppermute | solution.py:540
  52.7 0.9 %result.1 = (f32[64,1536]{1,0:T(8,128)}, f32[64,512]{1,0:T(8,128)}, f32[1,64]{1,0:T(1,128)}) custom-call(bf16[32,2048]{1,0:T(8,128)(2,1)S(1)} %add_pairs.1.held_ref, bf16[32,2048]{1,0:T(8,128)(2,1)S(1)} %collective-permute-done.22.got_ref, bf16[64,1536]{1,0:T(8,128)(2,1)S(1)} %get-tuple-element.124.w_ref, f32[1,512]{1,0:T(1,128)S(1)} %bitcast.8), custom_call_target="tpu_custom_call" | custom-call | tf_op jit(solution)/shard_map/result/pallas_call | solution.py:526
  (15 shorter events, 0.2 us)
Async XLA Ops:
  2.0 4.6 %collective-permute-start.2 = (bf16[2,2,64,512]{3,2,1,0:T(8,128)(2,1)S(1)}, bf16[2,2,64,512]{3,2,1,0:T(8,128)(2,1)S(1)}, u32[]{:S(2)}, u32[]{:S(2)}) collective-permute-start(bf16[2,2,64,512]{3,2,1,0:T(8,128)(2,1)S(1)} %get-tuple-element.69), channel_id=1, source_target_pairs={{0,4},{4,0},{8,12},{12,8},{16,20},{20,16},{24,28},{28,24},{1,5},{5... | collective-permute-start | bytes 786440 | tf_op jit(solution)/shard_map/ppermute | solution.py:540
  2.5 12.7 %collective-permute-start = (bf16[2,128,512]{2,1,0:T(8,128)(2,1)S(1)}, bf16[2,128,512]{2,1,0:T(8,128)(2,1)S(1)}, u32[]{:S(2)}, u32[]{:S(2)}) collective-permute-start(bf16[2,128,512]{2,1,0:T(8,128)(2,1)S(1)} %get-tuple-element.66), channel_id=1, source_target_pairs={{0,16},{4,20},{8,24},{12,28},{16,0},{20,4},{24,8},{28,12},{1,17},{... | collective-permute-start | bytes 786440 | tf_op jit(solution)/shard_map/ppermute | solution.py:540
  5.1 10.2 %collective-permute-start.1 = (bf16[2,128,512]{2,1,0:T(8,128)(2,1)S(1)}, bf16[2,128,512]{2,1,0:T(8,128)(2,1)S(1)}, u32[]{:S(2)}, u32[]{:S(2)}) collective-permute-start(bf16[2,128,512]{2,1,0:T(8,128)(2,1)S(1)} %get-tuple-element.67), channel_id=1, source_target_pairs={{0,8},{4,12},{8,0},{12,4},{16,24},{20,28},{24,16},{28,20},{1,9},{5... | collective-permute-start | bytes 786440 | tf_op jit(solution)/shard_map/ppermute | solution.py:540
  6.6 12.2 %collective-permute-start.5 = (bf16[2,2,64,512]{3,2,1,0:T(8,128)(2,1)S(1)}, bf16[2,2,64,512]{3,2,1,0:T(8,128)(2,1)S(1)}, u32[]{:S(2)}, u32[]{:S(2)}) collective-permute-start(bf16[2,2,64,512]{3,2,1,0:T(8,128)(2,1)S(1)} %pack_corner.1), channel_id=1, source_target_pairs={{0,24},{4,28},{8,16},{12,20},{16,8},{20,12},{24,0},{28,4},{1,25},{... | collective-permute-start | bytes 786440 | tf_op jit(solution)/shard_map/ppermute | solution.py:540
  15.2 3.6 %copy-start = (f32[512]{0:T(512)S(1)}, f32[512]{0:T(512)}, u32[]{:S(2)}) copy-start(f32[512]{0:T(512)} %param.6) | copy-start | bytes 6148
  15.3 3.5 %collective-permute-start.6 = (bf16[2,2,64,512]{3,2,1,0:T(8,128)(2,1)S(1)}, bf16[2,2,64,512]{3,2,1,0:T(8,128)(2,1)S(1)}, u32[]{:S(2)}, u32[]{:S(2)}) collective-permute-start(bf16[2,2,64,512]{3,2,1,0:T(8,128)(2,1)S(1)} %pack_other_core.1), channel_id=1, source_target_pairs={{0,4},{4,0},{8,12},{12,8},{16,20},{20,16},{24,28},{28,24},{1,5},{5... | collective-permute-start | bytes 786440 | tf_op jit(solution)/shard_map/ppermute | solution.py:540
  15.4 1.8 %collective-permute-start.3 = (bf16[4,64,384]{2,1,0:T(8,128)(2,1)S(1)}, bf16[4,64,384]{2,1,0:T(8,128)(2,1)S(1)}, u32[]{:S(2)}, u32[]{:S(2)}) collective-permute-start(bf16[4,64,384]{2,1,0:T(8,128)(2,1)S(1)} %get-tuple-element.78), channel_id=1, source_target_pairs={{0,4},{4,0},{8,12},{12,8},{16,20},{20,16},{24,28},{28,24},{1,5},{5... | collective-permute-start | bytes 589832 | tf_op jit(solution)/shard_map/ppermute | solution.py:540
  15.9 1.6 %collective-permute-start.4 = (bf16[4,64,384]{2,1,0:T(8,128)(2,1)S(1)}, bf16[4,64,384]{2,1,0:T(8,128)(2,1)S(1)}, u32[]{:S(2)}, u32[]{:S(2)}) collective-permute-start(bf16[4,64,384]{2,1,0:T(8,128)(2,1)S(1)} %get-tuple-element.79), channel_id=1, source_target_pairs={{0,4},{4,0},{8,12},{12,8},{16,20},{20,16},{24,28},{28,24},{1,5},{5... | collective-permute-start | bytes 589832 | tf_op jit(solution)/shard_map/ppermute | solution.py:540
  21.8 3.1 %collective-permute-start.8 = (bf16[4,64,1280]{2,1,0:T(8,128)(2,1)S(1)}, bf16[4,64,1280]{2,1,0:T(8,128)(2,1)S(1)}, u32[]{:S(2)}, u32[]{:S(2)}) collective-permute-start(bf16[4,64,1280]{2,1,0:T(8,128)(2,1)S(1)} %get-tuple-element.103), channel_id=1, source_target_pairs={{0,4},{4,0},{8,12},{12,8},{16,20},{20,16},{24,28},{28,24},{1,5},{5... | collective-permute-start | bytes 1966088 | tf_op jit(solution)/shard_map/ppermute | solution.py:540
  22.5 6.5 %collective-permute-start.7 = (bf16[4,64,512]{2,1,0:T(8,128)(2,1)S(1)}, bf16[4,64,512]{2,1,0:T(8,128)(2,1)S(1)}, u32[]{:S(2)}, u32[]{:S(2)}) collective-permute-start(bf16[4,64,512]{2,1,0:T(8,128)(2,1)S(1)} %get-tuple-element.93), channel_id=1, source_target_pairs={{0,4},{4,0},{8,12},{12,8},{16,20},{20,16},{24,28},{28,24},{1,5},{5... | collective-permute-start | bytes 786440 | tf_op jit(solution)/shard_map/ppermute | solution.py:540
  23.0 7.2 %collective-permute-start.10 = (bf16[4,32,768]{2,1,0:T(8,128)(2,1)S(1)}, bf16[4,32,768]{2,1,0:T(8,128)(2,1)S(1)}, u32[]{:S(2)}, u32[]{:S(2)}) collective-permute-start(bf16[4,32,768]{2,1,0:T(8,128)(2,1)S(1)} %get-tuple-element.108), channel_id=1, source_target_pairs={{0,1},{1,0},{2,3},{3,2},{4,5},{5,4},{6,7},{7,6},{8,9},{9,8},{10,11... | collective-permute-start | bytes 589832 | tf_op jit(solution)/shard_map/ppermute | solution.py:540
  25.0 10.3 %collective-permute-start.14 = (bf16[64,896]{1,0:T(8,128)(2,1)S(1)}, bf16[64,896]{1,0:T(8,128)(2,1)S(1)}, u32[]{:S(2)}, u32[]{:S(2)}) collective-permute-start(bf16[64,896]{1,0:T(8,128)(2,1)S(1)} %get-tuple-element.114), channel_id=1, source_target_pairs={{0,24},{4,28},{8,16},{12,20},{16,8},{20,12},{24,0},{28,4},{1,25},{... | collective-permute-start | bytes 344072 | tf_op jit(solution)/shard_map/ppermute | solution.py:540
  27.5 4.6 %collective-permute-start.9 = (bf16[4,32,384]{2,1,0:T(8,128)(2,1)S(1)}, bf16[4,32,384]{2,1,0:T(8,128)(2,1)S(1)}, u32[]{:S(2)}, u32[]{:S(2)}) collective-permute-start(bf16[4,32,384]{2,1,0:T(8,128)(2,1)S(1)} %get-tuple-element.105), channel_id=1, source_target_pairs={{0,1},{1,0},{2,3},{3,2},{4,5},{5,4},{6,7},{7,6},{8,9},{9,8},{10,11... | collective-permute-start | bytes 294920 | tf_op jit(solution)/shard_map/ppermute | solution.py:540
  28.4 7.3 %collective-permute-start.15 = (bf16[64,896]{1,0:T(8,128)(2,1)S(1)}, bf16[64,896]{1,0:T(8,128)(2,1)S(1)}, u32[]{:S(2)}, u32[]{:S(2)}) collective-permute-start(bf16[64,896]{1,0:T(8,128)(2,1)S(1)} %get-tuple-element.115), channel_id=1, source_target_pairs={{0,16},{4,20},{8,24},{12,28},{16,0},{20,4},{24,8},{28,12},{1,17},{... | collective-permute-start | bytes 344072 | tf_op jit(solution)/shard_map/ppermute | solution.py:540
  29.0 6.8 %collective-permute-start.16 = (bf16[64,896]{1,0:T(8,128)(2,1)S(1)}, bf16[64,896]{1,0:T(8,128)(2,1)S(1)}, u32[]{:S(2)}, u32[]{:S(2)}) collective-permute-start(bf16[64,896]{1,0:T(8,128)(2,1)S(1)} %get-tuple-element.116), channel_id=1, source_target_pairs={{0,8},{4,12},{8,0},{12,4},{16,24},{20,28},{24,16},{28,20},{1,9},{5... | collective-permute-start | bytes 344072 | tf_op jit(solution)/shard_map/ppermute | solution.py:540
  32.2 5.4 %collective-permute-start.11 = (bf16[32,1152]{1,0:T(8,128)(2,1)S(1)}, bf16[32,1152]{1,0:T(8,128)(2,1)S(1)}, u32[]{:S(2)}, u32[]{:S(2)}) collective-permute-start(bf16[32,1152]{1,0:T(8,128)(2,1)S(1)} %get-tuple-element.110), channel_id=1, source_target_pairs={{0,24},{4,28},{8,16},{12,20},{16,8},{20,12},{24,0},{28,4},{1,25},{... | collective-permute-start | bytes 221192 | tf_op jit(solution)/shard_map/ppermute | solution.py:540
  34.8 4.4 %collective-permute-start.12 = (bf16[32,1152]{1,0:T(8,128)(2,1)S(1)}, bf16[32,1152]{1,0:T(8,128)(2,1)S(1)}, u32[]{:S(2)}, u32[]{:S(2)}) collective-permute-start(bf16[32,1152]{1,0:T(8,128)(2,1)S(1)} %get-tuple-element.111), channel_id=1, source_target_pairs={{0,16},{4,20},{8,24},{12,28},{16,0},{20,4},{24,8},{28,12},{1,17},{... | collective-permute-start | bytes 221192 | tf_op jit(solution)/shard_map/ppermute | solution.py:540
  35.3 4.4 %collective-permute-start.13 = (bf16[32,1152]{1,0:T(8,128)(2,1)S(1)}, bf16[32,1152]{1,0:T(8,128)(2,1)S(1)}, u32[]{:S(2)}, u32[]{:S(2)}) collective-permute-start(bf16[32,1152]{1,0:T(8,128)(2,1)S(1)} %get-tuple-element.112), channel_id=1, source_target_pairs={{0,8},{4,12},{8,0},{12,4},{16,24},{20,28},{24,16},{28,20},{1,9},{5... | collective-permute-start | bytes 221192 | tf_op jit(solution)/shard_map/ppermute | solution.py:540
  35.8 4.2 %collective-permute-start.17 = (bf16[32,896]{1,0:T(8,128)(2,1)S(1)}, bf16[32,896]{1,0:T(8,128)(2,1)S(1)}, u32[]{:S(2)}, u32[]{:S(2)}) collective-permute-start(bf16[32,896]{1,0:T(8,128)(2,1)S(1)} %get-tuple-element.118), channel_id=1, source_target_pairs={{0,1},{1,0},{2,3},{3,2},{4,5},{5,4},{6,7},{7,6},{8,9},{9,8},{10,11... | collective-permute-start | bytes 172040 | tf_op jit(solution)/shard_map/ppermute | solution.py:540
  40.1 7.4 %collective-permute-start.21 = (bf16[32,2048]{1,0:T(8,128)(2,1)S(1)}, bf16[32,2048]{1,0:T(8,128)(2,1)S(1)}, u32[]{:S(2)}, u32[]{:S(2)}) collective-permute-start(bf16[32,2048]{1,0:T(8,128)(2,1)S(1)} %join_terms.1.kept_ref), channel_id=1, source_target_pairs={{0,2},{1,3},{2,0},{3,1},{4,6},{5,7},{6,4},{7,5},{8,10},{9,11},{10,... | collective-permute-start | bytes 393224 | tf_op jit(solution)/shard_map/ppermute | solution.py:540
  42.9 6.0 %collective-permute-start.18 = (bf16[128,512]{1,0:T(8,128)(2,1)S(1)}, bf16[128,512]{1,0:T(8,128)(2,1)S(1)}, u32[]{:S(2)}, u32[]{:S(2)}) collective-permute-start(bf16[128,512]{1,0:T(8,128)(2,1)S(1)} %get-tuple-element.120), channel_id=1, source_target_pairs={{0,24},{4,28},{8,16},{12,20},{16,8},{20,12},{24,0},{28,4},{1,25},{... | collective-permute-start | bytes 393224 | tf_op jit(solution)/shard_map/ppermute | solution.py:540
  45.3 5.0 %collective-permute-start.19 = (bf16[128,512]{1,0:T(8,128)(2,1)S(1)}, bf16[128,512]{1,0:T(8,128)(2,1)S(1)}, u32[]{:S(2)}, u32[]{:S(2)}) collective-permute-start(bf16[128,512]{1,0:T(8,128)(2,1)S(1)} %get-tuple-element.121), channel_id=1, source_target_pairs={{0,16},{4,20},{8,24},{12,28},{16,0},{20,4},{24,8},{28,12},{1,17},{... | collective-permute-start | bytes 393224 | tf_op jit(solution)/shard_map/ppermute | solution.py:540
  45.9 5.0 %collective-permute-start.20 = (bf16[128,512]{1,0:T(8,128)(2,1)S(1)}, bf16[128,512]{1,0:T(8,128)(2,1)S(1)}, u32[]{:S(2)}, u32[]{:S(2)}) collective-permute-start(bf16[128,512]{1,0:T(8,128)(2,1)S(1)} %get-tuple-element.122), channel_id=1, source_target_pairs={{0,8},{4,12},{8,0},{12,4},{16,24},{20,28},{24,16},{28,20},{1,9},{5... | collective-permute-start | bytes 393224 | tf_op jit(solution)/shard_map/ppermute | solution.py:540
  47.6 5.0 %collective-permute-start.22 = (bf16[32,2048]{1,0:T(8,128)(2,1)S(1)}, bf16[32,2048]{1,0:T(8,128)(2,1)S(1)}, u32[]{:S(2)}, u32[]{:S(2)}) collective-permute-start(bf16[32,2048]{1,0:T(8,128)(2,1)S(1)} %add_pairs.1.held_ref), channel_id=1, source_target_pairs={{0,1},{1,0},{2,3},{3,2},{4,5},{5,4},{6,7},{7,6},{8,9},{9,8},{10,11... | collective-permute-start | bytes 393224 | tf_op jit(solution)/shard_map/ppermute | solution.py:540
